TPU v7x, 32 devices: a whole 2x2x4 slice. The times are simulated.
32 devices in a mesh: shard: 2 (over x), tensor: 4 (over z), section: 4 (over y, core).
Axes of the slice: x: 2, y: 2, z: 4, core: 2. Of those that a mesh axis runs over, the one named last changes fastest.
Arguments:
- activations: bfloat16 [8, 512, 2304], P(None, 'shard', ('tensor', 'section')), may hold values from -6 to 6
- router_grad: bfloat16 [8, 512], P(None, 'shard'), may hold values from -6 to 6
- token_ids: int32 [512], P('shard'), may hold values from 0 to 8191
- norm_terms: bfloat16 [2, 512, 2304], P(None, 'shard', ('tensor', 'section'))
- old_factors: float32 [8, 2304, 2304], P('shard', 'tensor', 'section'), as said below
- old_router_factor: float32 [8, 8], replicated, as said below
- old_norm_diag: float32 [2, 2304], P(None, ('tensor', 'section')), may hold values from 0.5 to 5
- old_embed_diag: float32 [8192], P('tensor'), may hold values from 0.05 to 0.5
Outputs:
- precond_attn: float32 [4, 2304, 2304], P(None, 'tensor', 'section')
- precond_router: float32 [8, 2304], P(None, 'tensor')
- precond_norms: float32 [2, 2304], P(None, ('tensor', 'section'))
- precond_embed: float32 [8192, 2304], P('tensor', 'section')
Inputs may be any that keep to these rules, and one draw needn't show every extreme that they name: `old_factors`: each matrix is symmetric with a positive diagonal. `old_router_factor`: symmetric with a positive diagonal.
All inputs are finite; a program needn't handle non-finite values.
Results may differ from a plain program's by a relative error of at most 0.0083.
Values may be sent and summed in bfloat16 or wider, within the bound.
No kernel may reach another device: no remote copies, remote signals or barrier semaphores. Data moves between devices by JAX's collectives and lax.ppermute only.
A program may use at most 128 MiB of HBM per device.

v0:
```python
import math

import jax
import jax.numpy as jnp
from jax import lax
from jax.sharding import PartitionSpec as P

D = 2304
EXPERTS = 8
VOCAB = 8192


factor_decay = 0.5
damping = 0.01
learning_rate = 0.05


def local_inverse(matrix):
    width = matrix.shape[0]
    trace = jnp.sum(jnp.diagonal(matrix))
    factor_scale = width / (3.0 * trace)
    identity = jnp.eye(width, dtype=jnp.float32)
    matrix_low = lax.optimization_barrier(matrix.astype(jnp.bfloat16))
    first = 2.0 * factor_scale * identity - factor_scale * factor_scale * matrix_low.astype(
        jnp.float32
    )
    first_low = first.astype(jnp.bfloat16)
    image = jnp.dot(matrix_low, first_low, preferred_element_type=jnp.float32).astype(jnp.bfloat16)
    product = jnp.dot(first_low, image, preferred_element_type=jnp.float32)
    return (2.0 * first - product).astype(jnp.bfloat16)


def fold_with(columns, piece):
    return jnp.einsum("kij,kjl->kil", piece, columns, preferred_element_type=jnp.float32)


def per_device(
    activations,
    router_grad,
    token_ids,
    norm_terms,
    old_factors,
    old_router_factor,
    old_norm_diag,
    old_embed_diag,
):
    n_tensor = lax.axis_size("tensor")
    n_section = lax.axis_size("section")
    n_shard = lax.axis_size("shard")
    tensor_rank = lax.axis_index("tensor")
    section_rank = lax.axis_index("section")
    row_block = D // n_tensor
    col_block = D // n_section
    tokens_all = activations.shape[1] * n_shard
    row_start = tensor_rank * row_block
    col_start = section_rank * col_block

    def collect(carry, piece):
        whole = lax.all_gather(piece, ("tensor", "section"), axis=1, tiled=True)
        rows_part = lax.dynamic_slice_in_dim(whole, row_start, row_block, 1)
        cols_part = lax.dynamic_slice_in_dim(whole, col_start, col_block, 1)
        return (carry, (rows_part, cols_part))

    unused_carry, (row_parts, col_parts) = lax.scan(collect, jnp.int32(0), activations)
    partial_value = jnp.einsum(
        "mnr,mnc->mrc", row_parts, col_parts, preferred_element_type=jnp.float32
    )
    fresh = lax.psum_scatter(partial_value, "shard", scatter_dimension=0, tiled=True) / tokens_all
    row_index = lax.broadcasted_iota(jnp.int32, (row_block, col_block), 0) + row_start
    col_index = lax.broadcasted_iota(jnp.int32, (row_block, col_block), 1) + col_start
    eye_block = (row_index == col_index).astype(jnp.float32)
    matrix = factor_decay * old_factors + (1.0 - factor_decay) * fresh + damping * eye_block
    diag_part = jnp.sum(matrix * eye_block, axis=(1, 2))
    trace = lax.psum(diag_part, ("tensor", "section"))
    factor_scale = (D / (3.0 * trace))[:, None, None]
    matrix_low = lax.optimization_barrier(matrix.astype(jnp.bfloat16))
    first = 2.0 * factor_scale * eye_block - factor_scale * factor_scale * matrix_low.astype(
        jnp.float32
    )
    first_low = first.astype(jnp.bfloat16)
    first_cols = lax.all_gather(first_low, "tensor", axis=1, tiled=True)
    image = fold_with(first_cols, lax.all_gather(matrix_low, "section", axis=2, tiled=True))
    image_cols = lax.all_gather(image.astype(jnp.bfloat16), "tensor", axis=1, tiled=True)
    product = fold_with(image_cols, lax.all_gather(first_low, "section", axis=2, tiled=True))
    inverse_low = (2.0 * first - product).astype(jnp.bfloat16)
    inverses = lax.all_gather(inverse_low, "shard", axis=0, tiled=True)
    left_terms = jnp.stack(
        [
            jnp.einsum("nc,rc->nr", col_parts[m], inverses[m], preferred_element_type=jnp.float32)
            for m in (0, 4, 6)
        ]
    )
    left = lax.psum(left_terms, "section").astype(jnp.bfloat16)
    right_terms = jnp.stack(
        [
            jnp.einsum("nr,rc->nc", row_parts[m], inverses[m], preferred_element_type=jnp.float32)
            for m in (1, 2, 3, 5, 7)
        ]
    )
    right = lax.psum(right_terms, "tensor").astype(jnp.bfloat16)
    norm_values = norm_terms.astype(jnp.float32)
    router_part = jnp.einsum(
        "en,fn->ef", router_grad, router_grad, preferred_element_type=jnp.float32
    )
    router_sum, norm_total, norm_squares = lax.psum(
        (router_part, jnp.sum(norm_values, axis=1), jnp.sum(norm_values * norm_values, axis=1)),
        "shard",
    )
    router_matrix = (
        factor_decay * old_router_factor
        + (1.0 - factor_decay) * (router_sum / tokens_all)
        + damping * jnp.eye(EXPERTS, dtype=jnp.float32)
    )
    router_inverse = local_inverse(router_matrix)
    router_right = jnp.einsum(
        "en,ef->nf", router_grad, router_inverse, preferred_element_type=jnp.float32
    ).astype(jnp.bfloat16)
    precond_norms = (
        learning_rate
        * norm_total
        / (
            factor_decay * old_norm_diag
            + (1.0 - factor_decay) * (norm_squares / tokens_all)
            + damping
        )
    )
    ids_all = lax.all_gather(token_ids, "shard", axis=0, tiled=True)
    embed_all = lax.all_gather(right[4], "shard", axis=0, tiled=True)
    paired_left = jnp.stack([left[0], left[0], left[0], left[1]])
    attn_terms = jnp.einsum(
        "wnr,wnc->wrc", paired_left, right[:4], preferred_element_type=jnp.float32
    )
    router_term = jnp.einsum("nf,nr->fr", router_right, left[2], preferred_element_type=jnp.float32)
    attn_sum, router_total = lax.psum((attn_terms, router_term), "shard")
    precond_attn = learning_rate * attn_sum
    precond_router = learning_rate * router_total
    vocab_block = VOCAB // n_tensor
    step_rows = math.gcd(vocab_block, 512)
    vocab_start = tensor_rank * vocab_block

    def embed_block(block_index):
        ids_here = vocab_start + block_index * step_rows + lax.iota(jnp.int32, step_rows)
        onehot = (ids_here[:, None] == ids_all[None, :]).astype(jnp.bfloat16)
        summed = jnp.dot(onehot, embed_all, preferred_element_type=jnp.float32)
        tallies = jnp.sum(onehot, axis=1, dtype=jnp.float32)
        return (summed, tallies)

    block_sums, block_counts = lax.map(
        embed_block, jnp.arange(vocab_block // step_rows, dtype=jnp.int32)
    )
    embed_sum = block_sums.reshape(vocab_block, col_block)
    counts = block_counts.reshape(vocab_block)
    divisor = factor_decay * old_embed_diag + (1.0 - factor_decay) * (counts / tokens_all) + damping
    precond_embed = learning_rate * embed_sum / divisor[:, None]
    return (precond_attn, precond_router, precond_norms, precond_embed)


def solution(mesh):
    return jax.shard_map(
        per_device,
        mesh=mesh,
        in_specs=(
            P(None, "shard", ("tensor", "section")),
            P(None, "shard"),
            P("shard"),
            P(None, "shard", ("tensor", "section")),
            P("shard", "tensor", "section"),
            P(),
            P(None, ("tensor", "section")),
            P("tensor"),
        ),
        out_specs=(
            P(None, "tensor", "section"),
            P(None, "tensor"),
            P(None, ("tensor", "section")),
            P("tensor", "section"),
        ),
        check_vma=False,
    )
```

profile of v0, /device:TPU:0, one launch (start us, length us, event | category | flops | bytes accessed | tf_op | source)
XLA Modules:
  0.0 1530.2 jit_solution(15836966290856979995)
XLA Ops:
  8.0 347.3 %while.26 = (s32[]{:T(128)}, bf16[8,256,576]{1,2,0:T(8,128)(2,1)S(1)}, bf16[8,256,576]{1,2,0:T(8,128)(2,1)}, bf16[8,256,144]{1,2,0:T(8,128)(2,1)}, s32[]{:T(128)}, /*index=5*/s32[]{:T(128)}, s32[]{:T(128)}) while((s32[]{:T(128)}, bf16[8,256,576]{1,2,0:T(8,128)(2,1)S(1)}, bf16[8,256,576]{1,2,0:T(8,128)(2,1)}, bf16[8,256,144]{1,2,0:T(8,128)(2,1)}, ...), condition=%wide.region_1.2_spmd, body=%wide.region_0.1_spmd.sunk | while | flops 2 | bytes 5088389 | solution.py:64
  9.7 43.4 %all-gather.22.cloned.1.call-done = bf16[1,256,2304]{1,2,0:T(8,128)(2,1)} async-done(((bf16[1,256,144]{1,2,0:T(8,128)(2,1)}), bf16[1,256,2304]{1,2,0:T(8,128)(2,1)}) %all-gather.22.cloned.1.call-update) | async-done | bytes 1179664 | tf_op jit(solution)/shard_map/while/body/eval_jaxpr/all_gather | solution.py:59
  56.4 39.7 %all-gather.22.cloned.1.call-done = bf16[1,256,2304]{1,2,0:T(8,128)(2,1)} async-done(((bf16[1,256,144]{1,2,0:T(8,128)(2,1)}), bf16[1,256,2304]{1,2,0:T(8,128)(2,1)}) %all-gather.22.cloned.1.call-update) | async-done | bytes 1179664 | tf_op jit(solution)/shard_map/while/body/eval_jaxpr/all_gather | solution.py:59
  99.5 39.7 %all-gather.22.cloned.1.call-done = bf16[1,256,2304]{1,2,0:T(8,128)(2,1)} async-done(((bf16[1,256,144]{1,2,0:T(8,128)(2,1)}), bf16[1,256,2304]{1,2,0:T(8,128)(2,1)}) %all-gather.22.cloned.1.call-update) | async-done | bytes 1179664 | tf_op jit(solution)/shard_map/while/body/eval_jaxpr/all_gather | solution.py:59
  142.5 39.4 %all-gather.22.cloned.1.call-done = bf16[1,256,2304]{1,2,0:T(8,128)(2,1)} async-done(((bf16[1,256,144]{1,2,0:T(8,128)(2,1)}), bf16[1,256,2304]{1,2,0:T(8,128)(2,1)}) %all-gather.22.cloned.1.call-update) | async-done | bytes 1179664 | tf_op jit(solution)/shard_map/while/body/eval_jaxpr/all_gather | solution.py:59
  185.3 39.4 %all-gather.22.cloned.1.call-done = bf16[1,256,2304]{1,2,0:T(8,128)(2,1)} async-done(((bf16[1,256,144]{1,2,0:T(8,128)(2,1)}), bf16[1,256,2304]{1,2,0:T(8,128)(2,1)}) %all-gather.22.cloned.1.call-update) | async-done | bytes 1179664 | tf_op jit(solution)/shard_map/while/body/eval_jaxpr/all_gather | solution.py:59
  228.0 39.4 %all-gather.22.cloned.1.call-done = bf16[1,256,2304]{1,2,0:T(8,128)(2,1)} async-done(((bf16[1,256,144]{1,2,0:T(8,128)(2,1)}), bf16[1,256,2304]{1,2,0:T(8,128)(2,1)}) %all-gather.22.cloned.1.call-update) | async-done | bytes 1179664 | tf_op jit(solution)/shard_map/while/body/eval_jaxpr/all_gather | solution.py:59
  270.8 39.7 %all-gather.22.cloned.1.call-done = bf16[1,256,2304]{1,2,0:T(8,128)(2,1)} async-done(((bf16[1,256,144]{1,2,0:T(8,128)(2,1)}), bf16[1,256,2304]{1,2,0:T(8,128)(2,1)}) %all-gather.22.cloned.1.call-update) | async-done | bytes 1179664 | tf_op jit(solution)/shard_map/while/body/eval_jaxpr/all_gather | solution.py:59
  313.8 39.7 %all-gather.22.cloned.1.call-done = bf16[1,256,2304]{1,2,0:T(8,128)(2,1)} async-done(((bf16[1,256,144]{1,2,0:T(8,128)(2,1)}), bf16[1,256,2304]{1,2,0:T(8,128)(2,1)}) %all-gather.22.cloned.1.call-update) | async-done | bytes 1179664 | tf_op jit(solution)/shard_map/while/body/eval_jaxpr/all_gather | solution.py:59
  355.3 8.9 fusion.59
  367.0 132.3 %reduce-scatter.2.cloned.1.call-done = f32[4,576,576]{2,1,0:T(8,128)} async-done(((f32[8,576,576]{2,1,0:T(8,128)}), f32[4,576,576]{2,1,0:T(8,128)}) %reduce-scatter.2.cloned.1.call-update) | async-done | bytes 5308432 | tf_op jit(solution)/shard_map/reduce_scatter | solution.py:68
  505.4 33.1 %psum.56 = f32[4]{0:T(128)S(1)} all-reduce(f32[4]{0:T(128)S(1)} %get-tuple-element.202), channel_id=1, replica_groups=mesh['shard'=2,'tensor'=4,'section'=4] {'tensor','section'}, use_global_device_ids=true, to_apply=%region_4.5 | all-reduce | flops 4 | bytes 32 | tf_op jit(solution)/shard_map/psum | solution.py:74
  556.2 188.0 %all-gather.16.cloned.1.call-done = bf16[4,2304,576]{2,1,0:T(8,128)(2,1)} async-done(((bf16[4,576,576]{2,1,0:T(8,128)(2,1)}), bf16[4,2304,576]{2,1,0:T(8,128)(2,1)}) %all-gather.16.cloned.1.call-update) | async-done | bytes 10616848 | tf_op jit(solution)/shard_map/all_gather | solution.py:81
  744.2 77.7 %all-gather.14.cloned.1.call-done = bf16[4,576,2304]{1,0,2:T(4,128)(2,1)} async-done(((bf16[4,576,576]{1,0,2:T(4,128)(2,1)}), bf16[4,576,2304]{1,0,2:T(4,128)(2,1)}) %all-gather.14.cloned.1.call-update) | async-done | bytes 10616848 | tf_op jit(solution)/shard_map/all_gather | solution.py:82
  821.9 16.4 %fusion.11 = bf16[4,576,576]{2,1,0:T(8,128)(2,1)} fusion(bf16[4,2304,576]{2,1,0:T(8,128)(2,1)} %all-gather.16.cloned.1.call-done, bf16[4,576,2304]{1,0,2:T(4,128)(2,1)} %all-gather.14.cloned.1.call-done), kind=kOutput, calls=%fused_computation.24 | convolution fusion | flops 6116622336 | bytes 23887872 | tf_op jit(solution)/shard_map/kij,kjl->kil/dot_general | solution.py:34
  838.5 62.5 %all-gather.12.cloned.1.call-done = bf16[4,576,2304]{1,0,2:T(4,128)(2,1)} async-done(((bf16[4,576,576]{1,0,2:T(4,128)(2,1)}), bf16[4,576,2304]{1,0,2:T(4,128)(2,1)}) %all-gather.12.cloned.1.call-update) | async-done | bytes 10616848 | tf_op jit(solution)/shard_map/all_gather | solution.py:84
  901.0 207.4 %all-gather.18.cloned.1.call-done = bf16[4,2304,576]{2,1,0:T(8,128)(2,1)} async-done(((bf16[4,576,576]{2,1,0:T(8,128)(2,1)}), bf16[4,2304,576]{2,1,0:T(8,128)(2,1)}) %all-gather.18.cloned.1.call-update) | async-done | bytes 10616848 | tf_op jit(solution)/shard_map/all_gather | solution.py:83
  1108.4 21.8 %subtract_convert_fusion = bf16[4,576,576]{2,1,0:T(8,128)(2,1)} fusion(bf16[4,576,576]{2,1,0:T(8,128)(2,1)S(1)} %get-tuple-element.203, f32[4]{0:T(128)S(1)} %mul.176, f32[4]{0:T(128)S(1)} %get-tuple-element.198, f32[576,576]{1,0:T(8,128)} %compare_convert_fusion.1, bf16[4,2304,576]{2,1,0:T(8,128)(2,1)} %all-gather.18.cloned.1.call-done, ...), kind=kOutput, calls=%fused_computation.16 | convolution fusion | flops 6124584960 | bytes 27869216 | tf_op jit(solution)/shard_map/kij,kjl->kil/dot_general | solution.py:34
  1130.3 74.0 %all-gather.20.cloned.1.call-done = bf16[8,576,576]{2,1,0:T(8,128)(2,1)} async-done(((bf16[4,576,576]{2,1,0:T(8,128)(2,1)}), bf16[8,576,576]{2,1,0:T(8,128)(2,1)}) %all-gather.20.cloned.1.call-update) | async-done | bytes 5308432 | tf_op jit(solution)/shard_map/all_gather | solution.py:86
  1209.2 35.7 %all-reduce.7 = bf16[3,256,576]{1,2,0:T(8,128)(2,1)S(1)} all-reduce(f32[3,256,576]{1,2,0:T(8,128)S(1)} %pad_maximum_fusion), channel_id=1, replica_groups=mesh['shard'=2,'tensor'=4,'section'=4] {'section'}, use_global_device_ids=true, to_apply=%region_5.6 | all-reduce | flops 442368 | bytes 2654208 | tf_op jit(solution)/shard_map/psum | solution.py:93
  1257.4 107.6 %all-reduce.6 = bf16[5,256,576]{1,2,0:T(8,128)(2,1)S(1)} all-reduce(f32[5,256,576]{1,2,0:T(8,128)} %fusion.14), channel_id=1, replica_groups=mesh['shard'=2,'tensor'=4,'section'=4] {'tensor'}, use_global_device_ids=true, to_apply=%region_6.7 | all-reduce | flops 737280 | bytes 4423680 | tf_op jit(solution)/shard_map/psum | solution.py:100
  1380.6 15.3 all-gather.1
  1396.2 13.0 while.27
  1429.7 87.3 %all-reduce.5.cloned.1.call-done = f32[4,576,576]{2,1,0:T(8,128)} async-done(((f32[4,576,576]{2,1,0:T(8,128)}), f32[4,576,576]{2,1,0:T(8,128)}) %all-reduce.5.cloned.1.call-update) | async-done | bytes 5308432 | tf_op jit(solution)/shard_map/psum | solution.py:134
  (136 shorter events, 122.5 us)
Async XLA Ops:
  8.0 1360.8 %copy-start = (bf16[8,256]{1,0:T(8,128)(2,1)S(1)}, bf16[8,256]{1,0:T(8,128)(2,1)}, u32[]{:S(2)}) copy-start(bf16[8,256]{1,0:T(8,128)(2,1)} %param.13) | copy-start | bytes 12292
  8.1 45.0 %all-gather.22.cloned.1.call-start = ((), (), s32[]{:S(2)}) async-start(), calls=%async_computation.8 | async-start | bytes 1253376 | tf_op jit(solution)/shard_map/while/body/eval_jaxpr/all_gather | solution.py:59
  54.9 41.3 %all-gather.22.cloned.1.call-start = ((), (), s32[]{:S(2)}) async-start(), calls=%async_computation.8 | async-start | bytes 1253376 | tf_op jit(solution)/shard_map/while/body/eval_jaxpr/all_gather | solution.py:59
  97.9 41.2 %all-gather.22.cloned.1.call-start = ((), (), s32[]{:S(2)}) async-start(), calls=%async_computation.8 | async-start | bytes 1253376 | tf_op jit(solution)/shard_map/while/body/eval_jaxpr/all_gather | solution.py:59
  141.0 40.9 %all-gather.22.cloned.1.call-start = ((), (), s32[]{:S(2)}) async-start(), calls=%async_computation.8 | async-start | bytes 1253376 | tf_op jit(solution)/shard_map/while/body/eval_jaxpr/all_gather | solution.py:59
  183.7 40.9 %all-gather.22.cloned.1.call-start = ((), (), s32[]{:S(2)}) async-start(), calls=%async_computation.8 | async-start | bytes 1253376 | tf_op jit(solution)/shard_map/while/body/eval_jaxpr/all_gather | solution.py:59
  226.5 40.9 %all-gather.22.cloned.1.call-start = ((), (), s32[]{:S(2)}) async-start(), calls=%async_computation.8 | async-start | bytes 1253376 | tf_op jit(solution)/shard_map/while/body/eval_jaxpr/all_gather | solution.py:59
  269.2 41.3 %all-gather.22.cloned.1.call-start = ((), (), s32[]{:S(2)}) async-start(), calls=%async_computation.8 | async-start | bytes 1253376 | tf_op jit(solution)/shard_map/while/body/eval_jaxpr/all_gather | solution.py:59
  312.3 41.3 %all-gather.22.cloned.1.call-start = ((), (), s32[]{:S(2)}) async-start(), calls=%async_computation.8 | async-start | bytes 1253376 | tf_op jit(solution)/shard_map/while/body/eval_jaxpr/all_gather | solution.py:59
  355.3 8.9 copy-start.3
  355.3 143.9 %reduce-scatter.2.cloned.1.call-start = ((), (), s32[]{:S(2)}) async-start(), calls=%async_computation.1 | async-start | bytes 17694720 | tf_op jit(solution)/shard_map/reduce_scatter | solution.py:68
  364.3 379.9 %all-gather.16.cloned.1.call-start = ((), (), s32[]{:S(2)}) async-start(), calls=%async_computation.4 | async-start | bytes 14745600 | tf_op jit(solution)/shard_map/all_gather | solution.py:81
  542.6 279.3 %all-gather.14.cloned.1.call-start = ((), (), s32[]{:S(2)}) async-start(), calls=%async_computation.3 | async-start | bytes 14745600 | tf_op jit(solution)/shard_map/all_gather | solution.py:82
  548.4 352.7 %all-gather.12.cloned.1.call-start = ((), (), s32[]{:S(2)}) async-start(), calls=%async_computation.2 | async-start | bytes 14745600 | tf_op jit(solution)/shard_map/all_gather | solution.py:84
  556.1 552.3 %all-gather.18.cloned.1.call-start = ((), (), s32[]{:S(2)}) async-start(), calls=%async_computation.5 | async-start | bytes 14745600 | tf_op jit(solution)/shard_map/all_gather | solution.py:83
  838.3 366.0 %all-gather.20.cloned.1.call-start = ((), (), s32[]{:S(2)}) async-start(), calls=%async_computation.6 | async-start | bytes 8847360 | tf_op jit(solution)/shard_map/all_gather | solution.py:86
  1130.2 386.8 %all-reduce.5.cloned.1.call-start = ((), (), s32[]{:S(2)}) async-start(), calls=%async_computation.7 | async-start | bytes 11796480 | tf_op jit(solution)/shard_map/psum | solution.py:134
  1244.9 7.6 copy-start.1
  1255.0 110.1 %slice-start = ((bf16[3,256,576]{1,2,0:T(8,128)(2,1)}), bf16[2,256,576]{1,2,0:T(8,128)(2,1)S(1)}, s32[]{:S(2)}) async-start(bf16[3,256,576]{1,2,0:T(8,128)(2,1)} %copy-done.1), calls=%async_computation.9 | async-start | bytes 1179648 | tf_op jit(solution)/shard_map/slice | solution.py:129
  1255.0 110.1 %slice-start.1 = ((bf16[3,256,576]{1,2,0:T(8,128)(2,1)}), bf16[1,256,576]{1,2,0:T(8,128)(2,1)S(1)}, s32[]{:S(2)}) async-start(bf16[3,256,576]{1,2,0:T(8,128)(2,1)} %copy-done.1), calls=%async_computation.10 | async-start | bytes 589824 | tf_op jit(solution)/shard_map/slice | solution.py:129
  1368.8 7.0 copy-start.9
  1368.8 11.3 copy-start.5
  1412.1 11.1 copy-start.8
  1412.1 11.7 copy-start.6
  (3 other events, 10.9 us)
Sparse Core Ops, SparseCore 0:
  12.0 41.0 all-gather.21
  58.8 37.2 all-gather.21
  101.9 37.2 all-gather.21
  144.6 37.2 all-gather.21
  187.3 37.2 all-gather.21
  230.1 37.2 all-gather.21
  273.2 37.2 all-gather.21
  316.2 37.2 all-gather.21
Sparse Core Ops, SparseCore 1:
  364.4 134.8 reduce-scatter.1
  542.7 201.5 all-gather.15
  746.2 75.6 all-gather.13
  823.5 77.5 all-gather.11
  903.2 205.2 all-gather.17
  1130.3 73.9 all-gather.19
  1368.9 148.1 all-reduce.4
where the time goes:
time: 1530 us
  waiting for transfers between devices  1150 us (75%)
  blocking collectives  209 us (14%)
  matrix products  75.4 us (5%)
  local copies, waits for them, and re-layouts  46.5 us (3%)
  other arithmetic  30 us (2%)
  between operations  16.5 us (1%)
    all_gather x8, waiting for transfers between devices, collect(): whole = lax.all_gather(piece, ('tensor', 'section'), axis=1, tiled=True)  320 us
    all_gather x1, waiting for transfers between devices, per_device(): lax.all_gather(image.astype(jnp.bfloat16), 'tensor', axis=1, tiled=True)  207 us
    all_gather x1, waiting for transfers between devices, per_device(): first_cols = lax.all_gather(first_low, 'tensor', axis=1, tiled=True)  188 us
    reduce_scatter x1, waiting for transfers between devices, per_device(): lax.psum_scatter(partial_value, 'shard', scatter_dimension=0, tiled=True)  132 us
    psum x1, blocking collectives, per_device(): right = lax.psum(right_terms, 'tensor').astype(jnp.bfloat16)  108 us
    psum x1, waiting for transfers between devices, per_device(): attn_sum, router_total = lax.psum((attn_terms, router_term), 'shard')  87.3 us
    all_gather x1, waiting for transfers between devices, per_device(): lax.all_gather(matrix_low, 'section', axis=2, tiled=True)  77.7 us
    all_gather x1, waiting for transfers between devices, per_device(): inverses = lax.all_gather(inverse_low, 'shard', axis=0, tiled=True)  74 us
  transfers between devices with their start and end apart: 15, of which 15 were waited for; matrix products, arithmetic and copies ran while one was open for 4% of the time, Pallas kernels for 0%

commit v1 on v0

--- a/solution.py
+++ b/solution.py
@@ -34,7 +34,7 @@
     return jnp.einsum("kij,kjl->kil", piece, columns, preferred_element_type=jnp.float32)
 
 
-def per_device(
+def general_plan(
     activations,
     router_grad,
     token_ids,
@@ -153,6 +153,209 @@
     divisor = factor_decay * old_embed_diag + (1.0 - factor_decay) * (counts / tokens_all) + damping
     precond_embed = learning_rate * embed_sum / divisor[:, None]
     return (precond_attn, precond_router, precond_norms, precond_embed)
+
+
+def split_three(values):
+    high = lax.reduce_precision(values, 8, 7)
+    rest = values - high
+    middle = lax.reduce_precision(rest, 8, 7)
+    return jnp.stack([high, middle, rest - middle], axis=-2).astype(jnp.bfloat16)
+
+
+def swap(value, axis, size, step):
+    return lax.ppermute(value, axis, [(i, i ^ step) for i in range(size)])
+
+
+def layer_plan(
+    activations,
+    router_grad,
+    token_ids,
+    norm_terms,
+    old_factors,
+    old_router_factor,
+    old_norm_diag,
+    old_embed_diag,
+):
+    n_tensor = lax.axis_size("tensor")
+    n_section = lax.axis_size("section")
+    n_shard = lax.axis_size("shard")
+    layer = lax.axis_index("tensor")
+    section = lax.axis_index("section")
+    side = section // 2
+    core = section % 2
+    owned, row_block, col_block = old_factors.shape
+    tokens = activations.shape[1]
+    tokens_all = tokens * n_shard
+    half = 2 * col_block
+    weight = (1.0 - factor_decay) / tokens_all
+
+    moved = lax.all_to_all(activations, ("shard", "tensor"), 0, 0, tiled=True)
+    gathered = lax.all_gather(moved, "section", axis=0)
+    features = gathered.reshape(n_section, n_shard, n_tensor, tokens, -1)
+    features = features.transpose(1, 3, 2, 0, 4).reshape(tokens_all, D)
+
+    row_index = lax.broadcasted_iota(jnp.int32, (row_block, col_block), 0) + layer * row_block
+    col_index = lax.broadcasted_iota(jnp.int32, (row_block, col_block), 1) + section * col_block
+    old_diag = jnp.sum(jnp.where(row_index == col_index, old_factors, 0.0), axis=1)
+    parts = split_three(old_diag)
+    message = jnp.concatenate(
+        [old_factors.astype(jnp.bfloat16), jnp.pad(parts, ((0, 0), (0, 13), (0, 0)))], axis=1
+    )
+    blocks = lax.all_to_all(message, "tensor", 0, 0, tiled=True)
+    old_traces = lax.psum(jnp.sum(old_diag, axis=1), ("tensor", "section"))
+    diag_here = jnp.sum(
+        blocks[:, row_block : row_block + 3].astype(jnp.float32), axis=(0, 1)
+    )
+    own_cols = lax.dynamic_slice_in_dim(features, section * col_block, col_block, 1)
+    fresh = jnp.einsum("nr,nc->rc", features, own_cols, preferred_element_type=jnp.float32)
+    on_diag = lax.broadcasted_iota(jnp.int32, (D, col_block), 0) == (
+        lax.broadcasted_iota(jnp.int32, (D, col_block), 1) + section * col_block
+    )
+    old_cols = blocks[:, :row_block].reshape(D, col_block).astype(jnp.float32)
+    matrix = (
+        factor_decay * jnp.where(on_diag, diag_here[None, :], old_cols)
+        + weight * fresh
+        + jnp.where(on_diag, damping, 0.0)
+    )
+    matrix_low = matrix.astype(jnp.bfloat16)
+    matrix_diag = jnp.sum(jnp.where(on_diag, matrix, 0.0), axis=0)
+    other_cols = swap(matrix_low, "section", n_section, 1)
+    other_diag = swap(matrix_diag, "section", n_section, 1)
+    first_core = core == 0
+    cols_low = jnp.concatenate(
+        [jnp.where(first_core, matrix_low, other_cols), jnp.where(first_core, other_cols, matrix_low)],
+        axis=1,
+    )
+    low_diag = lax.reduce_precision(
+        jnp.concatenate(
+            [
+                jnp.where(first_core, matrix_diag, other_diag),
+                jnp.where(first_core, other_diag, matrix_diag),
+            ]
+        ),
+        8,
+        7,
+    )
+
+    values = features.astype(jnp.float32)
+    trace = (
+        factor_decay * lax.dynamic_index_in_dim(old_traces, layer, 0, False)
+        + weight * jnp.sum(values * values)
+        + damping * D
+    )
+    scale = D / (3.0 * trace)
+    square = scale * scale
+    first_diag = lax.reduce_precision(2.0 * scale - square * low_diag, 8, 7)
+
+    def whole_rows(mine):
+        theirs = swap(mine, "section", n_section, 2)
+        return jnp.concatenate(
+            [jnp.where(side == 0, mine, theirs), jnp.where(side == 0, theirs, mine)], axis=1
+        )
+
+    def times(rows):
+        return jnp.dot(rows, cols_low, preferred_element_type=jnp.float32)
+
+    rows = lax.dynamic_slice_in_dim(features, core * tokens, tokens, 0)
+    rows_half = lax.dynamic_slice_in_dim(rows, side * half, half, 1).astype(jnp.float32)
+    product = times(rows)
+    by_first = 2.0 * scale * rows_half - square * product
+    step_one = first_diag * rows_half - square * (product - low_diag * rows_half)
+    step_one_low = lax.reduce_precision(step_one, 8, 7)
+    step_two = times(whole_rows(step_one_low.astype(jnp.bfloat16))) + low_diag * (
+        step_one - step_one_low
+    )
+    step_two_low = lax.reduce_precision(step_two, 8, 7)
+    step_three = first_diag * step_two - square * (
+        times(whole_rows(step_two_low.astype(jnp.bfloat16))) - low_diag * step_two_low
+    )
+    result = (2.0 * by_first - step_three).astype(jnp.bfloat16)
+
+    keep = lax.dynamic_slice_in_dim(result, core * col_block, col_block, 1)
+    give = lax.dynamic_slice_in_dim(result, (1 - core) * col_block, col_block, 1)
+    got = swap(give, "section", n_section, 1)
+    own = jnp.concatenate([jnp.where(first_core, keep, got), jnp.where(first_core, got, keep)], axis=0)
+    results = lax.all_gather(own, ("shard", "tensor"), axis=0)
+
+    grad_all = lax.all_gather(router_grad, "shard", axis=1, tiled=True)
+    ids_all = lax.all_gather(token_ids, "shard", axis=0, tiled=True)
+    norm_values = norm_terms.astype(jnp.float32)
+    norm_total, norm_squares = lax.psum(
+        (jnp.sum(norm_values, axis=1), jnp.sum(norm_values * norm_values, axis=1)), "shard"
+    )
+    router_matrix = (
+        factor_decay * old_router_factor
+        + weight * jnp.einsum("en,fn->ef", grad_all, grad_all, preferred_element_type=jnp.float32)
+        + damping * jnp.eye(EXPERTS, dtype=jnp.float32)
+    )
+    router_inverse = local_inverse(router_matrix)
+    router_right = jnp.einsum(
+        "en,ef->fn", grad_all, router_inverse, preferred_element_type=jnp.float32
+    ).astype(jnp.bfloat16)
+    precond_norms = (
+        learning_rate
+        * norm_total
+        / (
+            factor_decay * old_norm_diag
+            + (1.0 - factor_decay) * (norm_squares / tokens_all)
+            + damping
+        )
+    )
+
+    router_cols = learning_rate * jnp.dot(
+        router_right, results[6], preferred_element_type=jnp.float32
+    )
+    router_high = lax.reduce_precision(router_cols, 8, 7)
+    bundle = jnp.concatenate(
+        [
+            results[0],
+            results[4],
+            router_high.astype(jnp.bfloat16),
+            (router_cols - router_high).astype(jnp.bfloat16),
+        ],
+        axis=0,
+    )
+
+    def place(index, step):
+        return index * n_section + (index ^ step)
+
+    both = ("tensor", "section")
+    across = lax.ppermute(bundle, both, [(place(i, 0), place(i, 2)) for i in range(n_tensor)])
+    bundle = jnp.where(section == layer, bundle, across)
+    near = lax.ppermute(
+        bundle,
+        both,
+        [(place(i, 0), place(i, 1)) for i in range(n_tensor)]
+        + [(place(i, 2), place(i, 3)) for i in range(n_tensor)],
+    )
+    bundle = jnp.where((section ^ layer) % 2 == 0, bundle, near)
+    left_query = bundle[:tokens_all]
+    left_out = bundle[tokens_all : 2 * tokens_all]
+    tail = bundle[2 * tokens_all :].astype(jnp.float32)
+    precond_router = tail[:EXPERTS] + tail[EXPERTS:]
+    lefts = jnp.stack([left_query, left_query, left_query, left_out])
+    rights = jnp.stack([results[1], results[2], results[3], results[5]])
+    precond_attn = learning_rate * jnp.einsum(
+        "wnr,wnc->wrc", lefts, rights, preferred_element_type=jnp.float32
+    )
+
+    vocab_block = old_embed_diag.shape[0]
+    ids_here = layer * vocab_block + lax.iota(jnp.int32, vocab_block)
+    matches = ids_here[:, None] == ids_all[None, :]
+    counts = jnp.sum(matches.astype(jnp.float32), axis=1)
+    divisor = factor_decay * old_embed_diag + (1.0 - factor_decay) * (counts / tokens_all) + damping
+    embed_sum = jnp.dot(
+        matches.astype(jnp.bfloat16), results[7], preferred_element_type=jnp.float32
+    )
+    precond_embed = embed_sum * (learning_rate / divisor)[:, None]
+    return (precond_attn, precond_router, precond_norms, precond_embed)
+
+
+def per_device(*arguments):
+    one_each = arguments[4].shape[0] == lax.axis_size("tensor") == lax.axis_size("section")
+    if one_each and lax.axis_size("section") == 4 and lax.axis_size("shard") == 2:
+        return layer_plan(*arguments)
+    return general_plan(*arguments)
 
 
 def solution(mesh):

time: 1530 us -> 366 us (0.24)
  waiting for transfers between devices: 1150 us -> 189 us
  blocking collectives: 209 us -> 46 us
  matrix products: 75.4 us -> 28.9 us
  starting transfers between devices: 0.51 us -> 17.6 us
    all_gather x13 -> x2, waiting for transfers between devices: 930 us -> 75.9 us  [the longest x1 75.8 us: layer_plan(): results = lax.all_gather(own, ('shard', 'tensor'), axis=0)]
    psum x5 -> x2, blocking collectives: 189 us -> 37.2 us  [the longest x1 32.2 us: layer_plan(): old_traces = lax.psum(jnp.sum(old_diag, axis=1), ('tensor', 'section'))]
    reduce_scatter x1 -> x0, waiting for transfers between devices: 132 us -> none  [per_device(): lax.psum_scatter(partial_value, 'shard', scatter_dimension=0, tiled=True)]
    psum x1 -> x0, waiting for transfers between devices: 87.3 us -> none  [per_device(): attn_sum, router_total = lax.psum((attn_terms, router_term), 'shard')]
    all_to_all x0 -> x2, waiting for transfers between devices: none -> 69.1 us  [the longest x1 64.2 us: layer_plan(): blocks = lax.all_to_all(message, 'tensor', 0, 0, tiled=True)]
    dot_general x18 -> x8, matrix products: 75.1 us -> 28.7 us  [the longest x3 12.3 us: times(): return jnp.dot(rows, cols_low, preferred_element_type=jnp.float32)]
    ppermute x0 -> x7, waiting for transfers between devices: none -> 43.2 us  [the longest x5 31.9 us: swap(): return lax.ppermute(value, axis, [(i, i ^ step) for i in range(size)])]
  transfers between devices with their start and end apart: 15 -> 11, of which waited for: 15 -> 7; matrix products, arithmetic and copies ran while one was open for 4% -> 13% of each run, Pallas kernels for 0% -> 0%
where the time goes in v1:
time: 366 us; the launch traced here: 364 us
  waiting for transfers between devices  189 us (52%)
  blocking collectives  46 us (13%)
  local copies, waits for them, and re-layouts  43.3 us (12%)
  matrix products  28.9 us (8%)
  other arithmetic  23.3 us (6%)
  starting transfers between devices  17.6 us (5%)
  between operations  16.5 us (5%)
    all_gather x1, waiting for transfers between devices, layer_plan(): results = lax.all_gather(own, ('shard', 'tensor'), axis=0)  75.8 us
    all_to_all x1, waiting for transfers between devices, layer_plan(): blocks = lax.all_to_all(message, 'tensor', 0, 0, tiled=True)  64.2 us
    psum x1, blocking collectives, layer_plan(): old_traces = lax.psum(jnp.sum(old_diag, axis=1), ('tensor', 'section'))  32.2 us
    ppermute x5, waiting for transfers between devices, swap(): return lax.ppermute(value, axis, [(i, i ^ step) for i in range(size)])  31.9 us
    convert_element_type x2, local copies, waits for them, and re-layouts, layer_plan(): old_cols = blocks[:, :row_block].reshape(D, col_block).astype(jnp.float32)  14.2 us
    dot_general x3, matrix products, times(): return jnp.dot(rows, cols_low, preferred_element_type=jnp.float32)  12.3 us
    ppermute x1, waiting for transfers between devices, layer_plan(): lax.ppermute(bundle, both, [(place(i, 0), place(i, 2)) for i in range(n_t...  11.2 us
    unnamed x36, local copies, waits for them, and re-layouts  7.6 us
  transfers between devices with their start and end apart: 11, of which 7 were waited for; matrix products, arithmetic and copies ran while one was open for 13% of the time, Pallas kernels for 0%

profile of v1, /device:TPU:0, one launch (start us, length us, event | category | flops | bytes accessed | tf_op | source)
XLA Modules:
  0.0 364.5 jit_solution(163492725096785117)
XLA Ops:
  7.2 7.3 %all-to-all-start = ((bf16[8,256,144]{1,2,0:T(8,128)(2,1)}), bf16[8,256,144]{1,2,0:T(8,128)(2,1)}, u32[]{:S(2)}, u32[]{:S(2)}) async-start(bf16[8,256,144]{1,2,0:T(8,128)(2,1)} %param.8), calls=%async_computation | async-start | bytes 1179648 | tf_op jit(solution)/shard_map/all_to_all | solution.py:192
  15.3 4.0 %copy.38 = bf16[4,576,576]{1,2,0:T(8,128)(2,1)S(1)} copy(f32[4,576,576]{2,1,0:T(8,128)} %param.12) | data formatting | bytes 7962624 | tf_op args[4]
  19.3 4.6 %select_reduce_fusion.1 = (f32[4]{0:T(128)}, f32[4,576]{1,0:T(4,128)S(1)}) fusion(f32[4,576,576]{2,1,0:T(8,128)} %param.12, pred[576,576]{1,0:T(8,128)(4,1)S(1)} %broadcast_compare_fusion), kind=kLoop, calls=%fused_computation.4 | loop fusion | flops 3979004 | bytes 5649424 | tf_op jit(solution)/shard_map/reduce_sum | solution.py:205
  26.4 4.9 %all-to-all-done = bf16[8,256,144]{1,2,0:T(8,128)(2,1)} async-done(((bf16[8,256,144]{1,2,0:T(8,128)(2,1)}), bf16[8,256,144]{1,2,0:T(8,128)(2,1)}, u32[]{:S(2)}, u32[]{:S(2)}) %all-to-all-start) | async-done | bytes 589856 | tf_op jit(solution)/shard_map/all_to_all | solution.py:192
  31.3 3.7 %all-to-all-start.1 = ((bf16[4,592,576]{1,2,0:T(8,128)(2,1)}), bf16[4,592,576]{1,2,0:T(8,128)(2,1)S(1)}, u32[]{:S(2)}, u32[]{:S(2)}) async-start(bf16[4,592,576]{1,2,0:T(8,128)(2,1)} %fusion.8), calls=%async_computation.1 | async-start | bytes 5898240 | tf_op jit(solution)/shard_map/all_to_all | solution.py:204
  36.0 64.2 %all-to-all-done.1 = bf16[4,592,576]{1,2,0:T(8,128)(2,1)S(1)} async-done(((bf16[4,592,576]{1,2,0:T(8,128)(2,1)}), bf16[4,592,576]{1,2,0:T(8,128)(2,1)S(1)}, u32[]{:S(2)}, u32[]{:S(2)}) %all-to-all-start.1) | async-done | bytes 2727968 | tf_op jit(solution)/shard_map/all_to_all | solution.py:204
  100.6 6.4 %copy.40 = f32[4,576,576]{1,0,2:T(4,128)} copy(f32[4,576,576]{1,2,0:T(8,128)S(1)} %slice_convert_fusion) | data formatting | bytes 10616832 | tf_op jit(solution)/shard_map/convert_element_type | solution.py:214
  107.0 7.8 %reshape.78 = f32[2304,576]{0,1:T(8,128)} reshape(f32[4,576,576]{1,0,2:T(4,128)} %copy.40) | data formatting | bytes 10616832 | tf_op jit(solution)/shard_map/convert_element_type | solution.py:214
  115.2 4.2 %copy.36 = bf16[4,2,4,256,144]{3,1,4,0,2:T(2,128)(2,1)S(1)} copy(bf16[4,2,4,256,144]{3,4,2,1,0:T(8,128)(2,1)} %bitcast.39) | data formatting | bytes 4718592 | tf_op jit(solution)/shard_map/reshape | solution.py:194
  120.1 3.9 %select_reduce_fusion.2 = (f32[576]{0:T(1024)S(1)}, bf16[2304,576]{0,1:T(8,128)(2,1)}) fusion(s32[576]{0:T(1024)S(1)} %copy-done.9, bf16[512,2304]{0,1:T(8,128)(2,1)S(1)} %bitcast.43, s32[]{:T(128)S(6)} %select_n.142, f32[2304,576]{0,1:T(8,128)S(1)} %copy-done.1, f32[576]{0:T(1024)S(1)} %convert_reduce_fusion), kind=kOutput, calls=%fused_computation.8 | convolution fusion | flops 1372225024 | bytes 10922244 | tf_op jit(solution)/shard_map/nr,nc->rc/dot_general | solution.py:210
  124.1 32.2 %psum.21 = f32[4]{0:T(128)S(1)} all-reduce(f32[4]{0:T(128)S(1)} %copy-done.15), channel_id=1, replica_groups=mesh['shard'=2,'tensor'=4,'section'=4] {'tensor','section'}, use_global_device_ids=true, to_apply=%region_1.2 | all-reduce | flops 4 | bytes 32 | tf_op jit(solution)/shard_map/psum | solution.py:205
  157.6 5.5 %multiply_reduce_fusion = f32[]{:T(128)} fusion(bf16[4,2,4,256,144]{3,4,2,1,0:T(8,128)(2,1)S(1)} %bitcast.40), kind=kLoop, calls=%fused_computation.13 | loop fusion | flops 3538943 | bytes 2359300 | tf_op jit(solution)/shard_map/reduce_sum | solution.py:243
  172.6 15.7 %collective-permute-done.2 = bf16[256,1152]{1,0:T(8,128)(2,1)} collective-permute-done((bf16[256,1152]{1,0:T(8,128)(2,1)S(1)}, bf16[256,1152]{1,0:T(8,128)(2,1)}, u32[]{:S(2)}, u32[]{:S(2)}) %collective-permute-start.2) | collective-permute-done | bytes 589856 | tf_op jit(solution)/shard_map/ppermute | solution.py:166
  189.5 5.1 %reduce-precision_convert_fusion.1 = (bf16[256,1152]{1,0:T(8,128)(2,1)S(1)}, f32[256,1152]{1,0:T(8,128)}) fusion(f32[256,1152]{1,0:T(8,128)} %get-tuple-element.38, f32[]{:T(128)S(6)} %mul.233, bf16[256,1152]{1,0:T(8,128)(2,1)} %copy.49, f32[1152]{0:T(1024)S(1)} %get-tuple-element.30, f32[1152]{0:T(1024)S(1)} %get-tuple-element.31, ...), kind=kOutput, calls=%fused_computation.63 | convolution fusion | flops 1375469568 | bytes 10036228 | tf_op jit(solution)/shard_map/dot_general | solution.py:257
  194.9 14.6 %collective-permute-done.3 = bf16[256,1152]{1,0:T(8,128)(2,1)} collective-permute-done((bf16[256,1152]{1,0:T(8,128)(2,1)S(1)}, bf16[256,1152]{1,0:T(8,128)(2,1)}, u32[]{:S(2)}, u32[]{:S(2)}) %collective-permute-start.3) | collective-permute-done | bytes 589856 | tf_op jit(solution)/shard_map/ppermute | solution.py:166
  210.7 4.5 %fusion.30 = bf16[256,1152]{1,0:T(8,128)(2,1)S(1)} fusion(bf16[256,1152]{1,0:T(8,128)(2,1)} %copy.49, f32[256,1152]{1,0:T(8,128)} %get-tuple-element.40, f32[256,1152]{1,0:T(8,128)} %get-tuple-element.38, bf16[2304,576]{0,1:T(8,128)(2,1)} %copy-done.4, bf16[2304,576]{0,1:T(8,128)(2,1)S(1)} %get-tuple-element.12, ...), kind=kOutput, calls=%fused_computation.50 | convolution fusion | flops 1375764480 | bytes 10036232 | tf_op jit(solution)/shard_map/dot_general | solution.py:257
  218.2 4.6 %all_gather.22 = bf16[8,512]{1,0:T(8,128)(2,1)S(1)} all-gather(bf16[8,256]{1,0:T(8,128)(2,1)S(1)} %copy-done.11), channel_id=1, replica_groups=mesh['shard'=2,'tensor'=4,'section'=4] {'shard'}, dimensions={1}, use_global_device_ids=true | all-gather | bytes 12288 | tf_op jit(solution)/shard_map/all_gather | solution.py:280
  225.1 75.8 %all-gather.8.cloned.1.call-done = bf16[4096,576]{1,0:T(8,128)(2,1)} async-done(((bf16[512,576]{1,0:T(8,128)(2,1)}), bf16[4096,576]{1,0:T(8,128)(2,1)}) %all-gather.8.cloned.1.call-update) | async-done | bytes 4718608 | tf_op jit(solution)/shard_map/all_gather | solution.py:278
  307.2 3.4 collective-permute-start.5
  310.7 4.2 %all-gather.2 = s32[2,1,256]{2,1,0:T(1,128)S(1)} all-gather(s32[1,1,256]{2,1,0:T(1,128)S(1)} %bitcast.48), channel_id=1, replica_groups=mesh['shard'=2,'tensor'=4,'section'=4] {'shard'}, dimensions={0}, use_global_device_ids=true | all-gather | bytes 3072 | tf_op jit(solution)/shard_map/all_gather | solution.py:281
  314.9 11.2 %collective-permute-done.5 = bf16[1040,576]{0,1:T(8,128)(2,1)S(1)} collective-permute-done((bf16[1040,576]{0,1:T(8,128)(2,1)}, bf16[1040,576]{0,1:T(8,128)(2,1)S(1)}, u32[]{:S(2)}, u32[]{:S(2)}) %collective-permute-start.5) | collective-permute-done | bytes 1198112 | tf_op jit(solution)/shard_map/ppermute | solution.py:323
  332.9 4.9 %all-reduce.1 = (f32[2,144]{1,0:T(2,128)S(1)}, f32[2,144]{1,0:T(2,128)S(1)}) all-reduce(f32[2,144]{1,0:T(2,128)S(1)} %get-tuple-element.7, f32[2,144]{1,0:T(2,128)S(1)} %get-tuple-element.6), channel_id=1, replica_groups=mesh['shard'=2,'tensor'=4,'section'=4] {'shard'}, use_global_device_ids=true, to_apply=%region_10.11 | all-reduce | flops 576 | bytes 4608 | tf_op jit(solution)/shard_map/psum | solution.py:283
  342.8 4.6 %fusion.5 = f32[2048,576]{0,1:T(8,128)} fusion(f32[2048]{0:T(1024)S(1)} %add_divide_fusion, s32[512]{0:T(512)S(1)} %bitcast.47, s32[2048]{0:T(1024)S(1)} %iota_add_fusion, bf16[4096,576]{1,0:T(8,128)(2,1)} %all-gather.8.cloned.1.call-done), kind=kOutput, calls=%fused_computation.15 | convolution fusion | flops 1210187776 | bytes 5392384 | tf_op jit(solution)/shard_map/dot_general | solution.py:347
  351.3 6.3 %broadcast_multiply_fusion = f32[4,576,576]{2,1,0:T(8,128)} fusion(bf16[1,512,576]{2,1,0:T(8,128)(2,1)S(1)} %get-tuple-element.18, bf16[1,512,576]{2,1,0:T(8,128)(2,1)S(1)} %get-tuple-element.17, bf16[1,512,576]{1,2,0:T(8,128)(2,1)S(1)} %copy.46, bf16[3,512,576]{1,2,0:T(8,128)(2,1)S(1)} %copy-done.5), kind=kOutput, calls=%fused_computation.18 | convolution fusion | flops 1365000192 | bytes 8847360 | tf_op jit(solution)/shard_map/wnr,wnc->wrc/dot_general | solution.py:338
  (94 shorter events, 44.2 us)
Async XLA Ops:
  7.2 24.2 %all-to-all-start = ((bf16[8,256,144]{1,2,0:T(8,128)(2,1)}), bf16[8,256,144]{1,2,0:T(8,128)(2,1)}, u32[]{:S(2)}, u32[]{:S(2)}) async-start(bf16[8,256,144]{1,2,0:T(8,128)(2,1)} %param.8), calls=%async_computation | async-start | bytes 1179648 | tf_op jit(solution)/shard_map/all_to_all | solution.py:192
  31.3 68.9 %all-to-all-start.1 = ((bf16[4,592,576]{1,2,0:T(8,128)(2,1)}), bf16[4,592,576]{1,2,0:T(8,128)(2,1)S(1)}, u32[]{:S(2)}, u32[]{:S(2)}) async-start(bf16[4,592,576]{1,2,0:T(8,128)(2,1)} %fusion.8), calls=%async_computation.1 | async-start | bytes 5898240 | tf_op jit(solution)/shard_map/all_to_all | solution.py:204
  35.0 80.2 %all-gather.6.cloned.1.call-start = ((), (), s32[]{:S(2)}) async-start(), calls=%async_computation.2 | async-start | bytes 2949120 | tf_op jit(solution)/shard_map/all_gather | solution.py:193
  35.8 265.2 %all-gather.8.cloned.1.call-start = ((), (), s32[]{:S(2)}) async-start(), calls=%async_computation.3 | async-start | bytes 5898240 | tf_op jit(solution)/shard_map/all_gather | solution.py:278
  115.2 4.8 %copy-start.1 = (f32[2304,576]{0,1:T(8,128)S(1)}, f32[2304,576]{0,1:T(8,128)}, u32[]{:S(2)}) copy-start(f32[2304,576]{0,1:T(8,128)} %reshape.78) | copy-start | bytes 15925252
  119.9 4.1 %copy-start.2 = (bf16[288,8,2,256]{3,1,2,0:T(8,128)(2,1)}, bf16[288,8,2,256]{3,1,2,0:T(8,128)(2,1)S(1)}, u32[]{:S(2)}) copy-start(bf16[288,8,2,256]{3,1,2,0:T(8,128)(2,1)S(1)} %copy.51) | copy-start | bytes 7077892
  120.1 3.9 %copy-start.15 = (f32[4]{0:T(128)S(1)}, f32[4]{0:T(128)}, u32[]{:S(2)}) copy-start(f32[4]{0:T(128)} %get-tuple-element.4) | copy-start | bytes 52
  120.1 37.5 %copy-start = (bf16[32,256,144]{1,2,0:T(8,128)(2,1)S(1)}, bf16[32,256,144]{1,2,0:T(8,128)(2,1)}, u32[]{:S(2)}) copy-start(bf16[32,256,144]{1,2,0:T(8,128)(2,1)} %all-gather.6.cloned.1.call-done) | copy-start | bytes 7077892
  124.1 42.4 %collective-permute-start = (bf16[2304,576]{0,1:T(8,128)(2,1)}, bf16[2304,576]{0,1:T(8,128)(2,1)}, u32[]{:S(2)}, u32[]{:S(2)}) collective-permute-start(bf16[2304,576]{0,1:T(8,128)(2,1)} %get-tuple-element.11), channel_id=1, source_target_pairs={{0,1},{1,0},{2,3},{3,2},{4,5},{5,4},{6,7},{7,6},{8,9},{9,8},{10,11... | collective-permute-start | bytes 7962632 | tf_op jit(solution)/shard_map/ppermute | solution.py:166
  157.5 8.8 %collective-permute-start.1 = (f32[576]{0:T(1024)S(1)}, f32[576]{0:T(1024)S(1)}, u32[]{:S(2)}, u32[]{:S(2)}) collective-permute-start(f32[576]{0:T(1024)S(1)} %get-tuple-element.10), channel_id=1, source_target_pairs={{0,1},{1,0},{2,3},{3,2},{4,5},{5,4},{6,7},{7,6},{8,9},{9,8},{10,11... | collective-permute-start | bytes 6920 | tf_op jit(solution)/shard_map/ppermute | solution.py:166
  166.5 3.3 copy-start.3
  166.5 3.4 copy-start.6
  172.6 15.7 %collective-permute-start.2 = (bf16[256,1152]{1,0:T(8,128)(2,1)S(1)}, bf16[256,1152]{1,0:T(8,128)(2,1)}, u32[]{:S(2)}, u32[]{:S(2)}) collective-permute-start(bf16[256,1152]{1,0:T(8,128)(2,1)S(1)} %get-tuple-element.37), channel_id=1, source_target_pairs={{0,2},{1,3},{2,0},{3,1},{4,6},{5,7},{6,4},{7,5},{8,10},{9,11},{10,... | collective-permute-start | bytes 1769480 | tf_op jit(solution)/shard_map/ppermute | solution.py:166
  194.6 14.9 %collective-permute-start.3 = (bf16[256,1152]{1,0:T(8,128)(2,1)S(1)}, bf16[256,1152]{1,0:T(8,128)(2,1)}, u32[]{:S(2)}, u32[]{:S(2)}) collective-permute-start(bf16[256,1152]{1,0:T(8,128)(2,1)S(1)} %get-tuple-element.39), channel_id=1, source_target_pairs={{0,2},{1,3},{2,0},{3,1},{4,6},{5,7},{6,4},{7,5},{8,10},{9,11},{10,... | collective-permute-start | bytes 1769480 | tf_op jit(solution)/shard_map/ppermute | solution.py:166
  215.1 3.1 copy-start.11
  215.1 7.7 %copy-start.12 = (f32[8,8]{1,0:T(8,128)S(1)}, f32[8,8]{1,0:T(8,128)}, u32[]{:S(2)}) copy-start(f32[8,8]{1,0:T(8,128)} %param.13) | copy-start | bytes 772
  215.3 1.7 collective-permute-start.4
  305.0 5.7 %copy-start.14 = (s32[256]{0:T(256)S(1)}, s32[256]{0:T(256)}, u32[]{:S(2)}) copy-start(s32[256]{0:T(256)} %param.10) | copy-start | bytes 3076
  307.2 19.0 %collective-permute-start.5 = (bf16[1040,576]{0,1:T(8,128)(2,1)}, bf16[1040,576]{0,1:T(8,128)(2,1)S(1)}, u32[]{:S(2)}, u32[]{:S(2)}) collective-permute-start(bf16[1040,576]{0,1:T(8,128)(2,1)} %copy.41), channel_id=1, source_target_pairs={{0,2},{5,7},{10,8},{15,13},{16,18},{21,23},{26,24},{31,29}} | collective-permute-start | bytes 3594248 | tf_op jit(solution)/shard_map/ppermute | solution.py:323
  327.7 5.0 %copy-start.7 = (bf16[2,256,144]{1,2,0:T(8,128)(2,1)S(1)}, bf16[2,256,144]{1,2,0:T(8,128)(2,1)}, u32[]{:S(2)}) copy-start(bf16[2,256,144]{1,2,0:T(8,128)(2,1)} %param.11) | copy-start | bytes 442372
  327.7 10.9 %copy-start.13 = (f32[2,144]{1,0:T(2,128)S(1)}, f32[2,144]{1,0:T(2,128)}, u32[]{:S(2)}) copy-start(f32[2,144]{1,0:T(2,128)} %param.14) | copy-start | bytes 3460
  327.7 11.5 %copy-start.10 = (f32[2048]{0:T(1024)S(1)}, f32[2048]{0:T(1024)}, u32[]{:S(2)}) copy-start(f32[2048]{0:T(1024)} %param.15) | copy-start | bytes 24580
  330.2 9.1 %slice-start = ((bf16[4096,576]{1,0:T(8,128)(2,1)}), bf16[1536,576]{1,0:T(8,128)(2,1)S(1)}, s32[]{:S(2)}) async-start(bf16[4096,576]{1,0:T(8,128)(2,1)} %all-gather.8.cloned.1.call-done), calls=%async_computation.4 | async-start | bytes 3932160 | tf_op jit(solution)/shard_map/slice | solution.py:337
  330.2 17.2 %collective-permute-start.6 = (bf16[1040,576]{0,1:T(8,128)(2,1)}, bf16[1040,576]{0,1:T(8,128)(2,1)}, u32[]{:S(2)}, u32[]{:S(2)}) collective-permute-start(bf16[1040,576]{0,1:T(8,128)(2,1)} %copy.43), channel_id=1, source_target_pairs={{0,1},{5,4},{10,11},{15,14},{2,3},{7,6},{8,9},{13,12},{16,17},{21,... | collective-permute-start | bytes 3594248 | tf_op jit(solution)/shard_map/ppermute | solution.py:325
  (4 other events, 5.9 us)
Sparse Core Ops, SparseCore 0:
  37.4 24.5 all-gather.5
  218.3 82.5 all-gather.7

commit v2 on v0

--- a/solution.py
+++ b/solution.py
@@ -3,6 +3,8 @@
 import jax
 import jax.numpy as jnp
 from jax import lax
+from jax.experimental import pallas as pl
+from jax.experimental.pallas import tpu as pltpu
 from jax.sharding import PartitionSpec as P
 
 D = 2304
@@ -34,7 +36,7 @@
     return jnp.einsum("kij,kjl->kil", piece, columns, preferred_element_type=jnp.float32)
 
 
-def per_device(
+def general_plan(
     activations,
     router_grad,
     token_ids,
@@ -153,6 +155,311 @@
     divisor = factor_decay * old_embed_diag + (1.0 - factor_decay) * (counts / tokens_all) + damping
     precond_embed = learning_rate * embed_sum / divisor[:, None]
     return (precond_attn, precond_router, precond_norms, precond_embed)
+
+
+def split_three(values):
+    high = lax.reduce_precision(values, 8, 7)
+    rest = values - high
+    middle = lax.reduce_precision(rest, 8, 7)
+    return jnp.stack([high, middle, rest - middle], axis=-2).astype(jnp.bfloat16)
+
+
+def swap(value, axis, size, step):
+    return lax.ppermute(value, axis, [(i, i ^ step) for i in range(size)])
+
+
+def local_diagonals(blocks):
+    width = blocks.shape[1]
+    pieces = []
+    for start in range(0, width, 128):
+        size = min(128, width - start)
+        tile = blocks[:, start : start + size, start : start + size]
+        pieces.append(jnp.sum(tile * jnp.eye(size, dtype=tile.dtype), axis=1))
+    return jnp.concatenate(pieces, axis=1)
+
+
+def attn_kernel(shard_ref, left_own, left_other, own_1, own_2, own_3, other_1, other_2, other_3, out):
+    first = shard_ref[0] == 0
+
+    def product(left, right):
+        out[0] = learning_rate * lax.dot_general(
+            left, right, (((1,), (1,)), ((), ())), preferred_element_type=jnp.float32
+        )
+
+    @pl.when(pl.program_id(0) == 0)
+    def _():
+        left = jnp.where(first, left_own[...], left_other[...])
+        product(left, jnp.where(first, own_1[...], other_1[...]))
+
+    @pl.when(pl.program_id(0) == 1)
+    def _():
+        left = jnp.where(first, left_own[...], left_other[...])
+        product(left, jnp.where(first, own_2[...], other_2[...]))
+
+    @pl.when(pl.program_id(0) == 2)
+    def _():
+        left = jnp.where(first, left_own[...], left_other[...])
+        product(left, jnp.where(first, own_3[...], other_3[...]))
+
+    @pl.when(pl.program_id(0) == 3)
+    def _():
+        left = jnp.where(first, left_other[...], left_own[...])
+        product(left, jnp.where(first, other_1[...], own_1[...]))
+
+
+def attn_products(shard, operands):
+    rows, tokens_all = operands[0].shape
+    cols = operands[2].shape[0]
+    whole = [pl.BlockSpec(value.shape, lambda w: (0, 0)) for value in operands]
+    return pl.pallas_call(
+        attn_kernel,
+        grid=(4,),
+        out_shape=jax.ShapeDtypeStruct((4, rows, cols), jnp.float32),
+        in_specs=[pl.BlockSpec(memory_space=pltpu.SMEM)] + whole,
+        out_specs=pl.BlockSpec((1, rows, cols), lambda w: (w, 0, 0)),
+        compiler_params=pltpu.CompilerParams(vmem_limit_bytes=40 * 1024 * 1024),
+        cost_estimate=pl.CostEstimate(
+            flops=8 * rows * cols * tokens_all,
+            bytes_accessed=16 * rows * cols + 16 * rows * tokens_all,
+            transcendentals=0,
+        ),
+    )(shard.reshape(1), *operands)
+
+
+def layer_plan(
+    activations,
+    router_grad,
+    token_ids,
+    norm_terms,
+    old_factors,
+    old_router_factor,
+    old_norm_diag,
+    old_embed_diag,
+):
+    n_tensor = lax.axis_size("tensor")
+    n_section = lax.axis_size("section")
+    n_shard = lax.axis_size("shard")
+    shard = lax.axis_index("shard")
+    layer = lax.axis_index("tensor")
+    section = lax.axis_index("section")
+    core = section % 2
+    owned, row_block, col_block = old_factors.shape
+    tokens = activations.shape[1]
+    features_dev = activations.shape[2]
+    tokens_all = tokens * n_shard
+    half = 2 * col_block
+    weight = (1.0 - factor_decay) / tokens_all
+    half_place = (section // 2) ^ (layer // 2)
+    core_place = core ^ (layer % 2)
+    own_place = section ^ layer
+
+    blocks = [None] * n_tensor
+    for step in (3, 2, 1):
+        away = lax.dynamic_index_in_dim(old_factors, layer ^ step, 0, False)
+        blocks[step] = swap(away.astype(jnp.bfloat16), "tensor", n_tensor, step)
+    blocks[0] = lax.dynamic_index_in_dim(old_factors, layer, 0, False).astype(jnp.bfloat16)
+
+    diagonals = local_diagonals(old_factors) * (layer == section).astype(jnp.float32)
+    extra = jnp.pad(split_three(diagonals), ((0, 0), (0, 0), (0, 3 * tokens - col_block)))
+    extra = jnp.pad(extra.reshape(owned, 9, tokens), ((0, 0), (0, 7), (0, 0)))
+    extra = jnp.concatenate(
+        [jnp.where(shard == 0, extra, 0), jnp.where(shard == 1, extra, 0)], axis=0
+    )
+    message = jnp.concatenate([jnp.swapaxes(activations, 1, 2), extra], axis=1)
+    moved = lax.all_to_all(message, ("shard", "tensor"), 0, 0, tiled=True)
+    gathered = lax.all_gather(moved, "section", axis=0)
+    gathered = gathered.reshape(n_section, n_shard, n_tensor, features_dev + 16, tokens)
+    by_place = [
+        lax.dynamic_index_in_dim(gathered, layer ^ step, 2, False) for step in range(n_tensor)
+    ]
+    features = jnp.stack([part[:, :, :features_dev] for part in by_place], axis=0)
+    features = features.transpose(2, 0, 1, 3, 4).reshape(n_shard, D, tokens)
+    codes = jnp.sum(
+        gathered[:, :, :, features_dev : features_dev + 9].astype(jnp.float32), axis=(1, 2)
+    )
+    old_diag = jnp.sum(codes.reshape(n_section, 3, 3 * tokens), axis=1)[:, :col_block]
+    old_diag = jnp.concatenate(
+        [
+            lax.dynamic_index_in_dim(old_diag, layer ^ step, 0, False)
+            for step in range(n_tensor)
+        ]
+    )
+    values = features.astype(jnp.float32)
+    squares = jnp.sum(values * values, axis=(0, 2))
+    matrix_diag = factor_decay * old_diag + weight * squares + damping
+    scale = D / (3.0 * jnp.sum(matrix_diag))
+    square = scale * scale
+    all_low_diag = lax.reduce_precision(matrix_diag, 8, 7)
+    low_diag = lax.dynamic_slice_in_dim(all_low_diag, half_place * half, half, 0)
+    own_diag = lax.dynamic_slice_in_dim(all_low_diag, own_place * col_block, col_block, 0)
+    first_diag = lax.reduce_precision(2.0 * scale - square * low_diag, 8, 7)
+    rows = jnp.swapaxes(lax.dynamic_index_in_dim(features, core, 0, False), 0, 1)
+    rows_half = lax.dynamic_slice_in_dim(rows, half_place * half, half, 1).astype(jnp.float32)
+
+    own_features = lax.dynamic_slice_in_dim(features, own_place * col_block, col_block, 1)
+    eye = lax.broadcasted_iota(jnp.int32, (row_block, col_block), 0) == lax.broadcasted_iota(
+        jnp.int32, (row_block, col_block), 1
+    )
+    low_blocks = []
+    for step in range(n_tensor):
+        part = features[:, step * row_block : (step + 1) * row_block]
+        fresh = jnp.einsum("xrn,xcn->rc", part, own_features, preferred_element_type=jnp.float32)
+        block = factor_decay * blocks[step].astype(jnp.float32) + weight * fresh
+        low_blocks.append(
+            jnp.where(eye & (own_place == step), own_diag[None, :], block).astype(jnp.bfloat16)
+        )
+    own_cols = jnp.concatenate(low_blocks, axis=0)
+    other_cols = swap(own_cols, "section", n_section, 1)
+
+    def whole_rows(mine):
+        theirs = swap(mine, "section", n_section, 2)
+        low = half_place == 0
+        return jnp.concatenate(
+            [jnp.where(low, mine, theirs), jnp.where(low, theirs, mine)], axis=1
+        )
+
+    def times(left):
+        own = jnp.dot(left, own_cols, preferred_element_type=jnp.float32)
+        other = jnp.dot(left, other_cols, preferred_element_type=jnp.float32)
+        low = core_place == 0
+        return jnp.concatenate([jnp.where(low, own, other), jnp.where(low, other, own)], axis=1)
+
+    product = times(rows)
+    by_first = 2.0 * scale * rows_half - square * product
+    step_one = first_diag * rows_half - square * (product - low_diag * rows_half)
+    step_one_low = lax.reduce_precision(step_one, 8, 7)
+    step_two = times(whole_rows(step_one_low.astype(jnp.bfloat16))) + low_diag * (
+        step_one - step_one_low
+    )
+    step_two_low = lax.reduce_precision(step_two, 8, 7)
+    step_three = first_diag * step_two - square * (
+        times(whole_rows(step_two_low.astype(jnp.bfloat16))) - low_diag * step_two_low
+    )
+    result = jnp.swapaxes((2.0 * by_first - step_three).astype(jnp.bfloat16), 0, 1)
+
+    keep = lax.dynamic_slice_in_dim(result, core_place * col_block, col_block, 0)
+    give = lax.dynamic_slice_in_dim(result, (1 - core_place) * col_block, col_block, 0)
+    got = swap(give, "section", n_section, 1)
+    own = jnp.concatenate(
+        [jnp.where(core == 0, keep, got), jnp.where(core == 0, got, keep)], axis=1
+    )
+
+    axes = ("shard", "tensor")
+
+    def send(value, moves):
+        return lax.ppermute(
+            value, axes, [(x * n_tensor + a, x * n_tensor + b) for x, a, b in moves]
+        )
+
+    down_1 = send(own, [(0, 3, 2), (0, 2, 1), (0, 1, 0), (1, 3, 2), (1, 1, 0)])
+    up_1 = send(own, [(0, 1, 2), (0, 2, 3), (1, 1, 2)])
+    down_2 = send(down_1, [(0, 2, 1), (0, 1, 0), (1, 2, 1)])
+    up_2 = send(up_1, [(0, 2, 3), (1, 2, 3)])
+    down_3 = send(down_2, [(0, 1, 0), (1, 1, 0)])
+
+    def by_layer(*options):
+        chosen = options[3]
+        for index in (2, 1, 0):
+            chosen = jnp.where(layer == index, options[index], chosen)
+        return chosen
+
+    own_1 = by_layer(down_1, own, up_1, up_2)
+    own_2 = by_layer(down_2, down_1, own, up_1)
+    own_3 = by_layer(down_3, down_2, down_1, own)
+    other_1 = swap(own_1, "shard", n_shard, 1)
+    other_2 = swap(own_2, "shard", n_shard, 1)
+    other_3 = swap(own_3, "shard", n_shard, 1)
+
+    everywhere = ("shard", "tensor", "section")
+
+    def place(x, z, s):
+        return (x * n_tensor + z) * n_section + s
+
+    planes = range(n_shard)
+    layers = range(n_tensor)
+
+    def scatter(value, source):
+        moved_here = lax.ppermute(
+            value,
+            everywhere,
+            [(place(x, source, s), place(x, s, s)) for x in planes for s in layers if s != source],
+        )
+        return jnp.where(layer == source, value, moved_here)
+
+    def across_shards(value):
+        return lax.ppermute(
+            value, everywhere, [(place(x, t, t), place(1 - x, t, t)) for x in planes for t in layers]
+        )
+
+    def hand_round(value):
+        across = lax.ppermute(
+            value, everywhere, [(place(x, t, t), place(x, t, t ^ 2)) for x in planes for t in layers]
+        )
+        value = jnp.where(section == layer, value, across)
+        near = lax.ppermute(
+            value,
+            everywhere,
+            [(place(x, t, t ^ a), place(x, t, t ^ a ^ 1)) for x in planes for t in layers for a in (0, 2)],
+        )
+        return jnp.where((section ^ layer) % 2 == 0, value, near)
+
+    left_here = scatter(own, 0)
+    left_there = across_shards(left_here)
+    left_own = hand_round(left_here)
+    left_other = hand_round(left_there)
+    precond_attn = attn_products(
+        shard, (left_own, left_other, own_1, own_2, own_3, other_1, other_2, other_3)
+    )
+
+    grad_all = lax.all_gather(router_grad, "shard", axis=1, tiled=True)
+    ids_all = lax.all_gather(token_ids, "shard", axis=0, tiled=True)
+    norm_values = norm_terms.astype(jnp.float32)
+    norm_total, norm_squares = lax.psum(
+        (jnp.sum(norm_values, axis=1), jnp.sum(norm_values * norm_values, axis=1)), "shard"
+    )
+    router_matrix = (
+        factor_decay * old_router_factor
+        + weight * jnp.einsum("en,fn->ef", grad_all, grad_all, preferred_element_type=jnp.float32)
+        + damping * jnp.eye(EXPERTS, dtype=jnp.float32)
+    )
+    router_inverse = local_inverse(router_matrix)
+    router_right = jnp.einsum(
+        "en,ef->fn", grad_all, router_inverse, preferred_element_type=jnp.float32
+    ).astype(jnp.bfloat16)
+    precond_norms = (
+        learning_rate
+        * norm_total
+        / (
+            factor_decay * old_norm_diag
+            + (1.0 - factor_decay) * (norm_squares / tokens_all)
+            + damping
+        )
+    )
+    router_cols = learning_rate * jnp.einsum(
+        "fn,cn->fc", router_right, own, preferred_element_type=jnp.float32
+    )
+    router_swapped = swap(router_cols, "shard", n_shard, 1)
+    router_cols = jnp.where(shard == 1, router_cols, router_swapped)
+    precond_router = hand_round(scatter(router_cols, 2))
+
+    vocab_block = old_embed_diag.shape[0]
+    ids_here = layer * vocab_block + lax.iota(jnp.int32, vocab_block)
+    matches = ids_here[:, None] == ids_all[None, :]
+    counts = jnp.sum(matches.astype(jnp.float32), axis=1)
+    divisor = factor_decay * old_embed_diag + (1.0 - factor_decay) * (counts / tokens_all) + damping
+    embed_grads = jnp.where(shard == 1, own_3, other_3)
+    embed_sum = jnp.einsum(
+        "vn,cn->vc", matches.astype(jnp.bfloat16), embed_grads, preferred_element_type=jnp.float32
+    )
+    precond_embed = embed_sum * (learning_rate / divisor)[:, None]
+    return (precond_attn, precond_router, precond_norms, precond_embed)
+
+
+def per_device(*arguments):
+    one_each = arguments[4].shape[0] == lax.axis_size("tensor") == lax.axis_size("section")
+    if one_each and lax.axis_size("section") == 4 and lax.axis_size("shard") == 2:
+        return layer_plan(*arguments)
+    return general_plan(*arguments)
 
 
 def solution(mesh):

time: 1530 us -> 288 us (0.19)
  waiting for transfers between devices: 1150 us -> 129 us
  blocking collectives: 209 us -> 41.3 us
  matrix products: 75.4 us -> 27.1 us
  starting transfers between devices: 0.51 us -> 30.6 us
  local copies, waits for them, and re-layouts: 46.5 us -> 17.3 us
    all_gather x13 -> x1, waiting for transfers between devices: 930 us -> 11.9 us  [layer_plan(): gathered = lax.all_gather(moved, 'section', axis=0)]
    psum x5 -> x1, blocking collectives: 189 us -> 7.4 us  [layer_plan(): lax.psum((jnp.sum(norm_values, axis=1), jnp.sum(norm_values * norm_values...]
    reduce_scatter x1 -> x0, waiting for transfers between devices: 132 us -> none  [per_device(): lax.psum_scatter(partial_value, 'shard', scatter_dimension=0, tiled=True)]
    ppermute x0 -> x25, waiting for transfers between devices: none -> 117 us  [the longest x11 77.3 us: swap(): return lax.ppermute(value, axis, [(i, i ^ step) for i in range(size)])]
    psum x1 -> x0, waiting for transfers between devices: 87.3 us -> none  [per_device(): attn_sum, router_total = lax.psum((attn_terms, router_term), 'shard')]
    dot_general x18 -> x13, matrix products: 75.1 us -> 26.9 us  [the longest x4 10.7 us: layer_plan(): jnp.einsum('xrn,xcn->rc', part, own_features, preferred_element_type=jnp....]
    ppermute x0 -> x25, starting transfers between devices: none -> 30.6 us  [the longest x11 9.89 us: swap(): return lax.ppermute(value, axis, [(i, i ^ step) for i in range(size)])]
    all_to_all x0 -> x1, blocking collectives: none -> 25.4 us  [layer_plan(): moved = lax.all_to_all(message, ('shard', 'tensor'), 0, 0, tiled=True)]
  transfers between devices with their start and end apart: 15 -> 26, of which waited for: 15 -> 15; matrix products, arithmetic and copies ran while one was open for 4% -> 12% of each run, Pallas kernels for 0% -> 0%
where the time goes in v2:
time: 288 us; the launch traced here: 287 us
  waiting for transfers between devices  129 us (45%)
  blocking collectives  41.3 us (14%)
  starting transfers between devices  30.6 us (11%)
  matrix products  27.1 us (9%)
  other arithmetic  20.5 us (7%)
  local copies, waits for them, and re-layouts  17.3 us (6%)
  between operations  16.1 us (6%)
  Pallas kernels  4.25 us (1%)
    ppermute x11, waiting for transfers between devices, swap(): return lax.ppermute(value, axis, [(i, i ^ step) for i in range(size)])  77.3 us
    ppermute x5, waiting for transfers between devices, send(): lax.ppermute(value, axes, [(x * n_tensor + a, x * n_tensor + b) for x, a,...  36.3 us
    all_to_all x1, blocking collectives, layer_plan(): moved = lax.all_to_all(message, ('shard', 'tensor'), 0, 0, tiled=True)  25.4 us
    all_gather x1, waiting for transfers between devices, layer_plan(): gathered = lax.all_gather(moved, 'section', axis=0)  11.9 us
    dot_general x4, matrix products, layer_plan(): jnp.einsum('xrn,xcn->rc', part, own_features, preferred_element_type=jnp....  10.7 us
    ppermute x11, starting transfers between devices, swap(): return lax.ppermute(value, axis, [(i, i ^ step) for i in range(size)])  9.89 us
    dot_general x3, matrix products, times(): other = jnp.dot(left, other_cols, preferred_element_type=jnp.float32)  8.11 us
    psum x1, blocking collectives, layer_plan(): lax.psum((jnp.sum(norm_values, axis=1), jnp.sum(norm_values * norm_values...  7.4 us
  transfers between devices with their start and end apart: 26, of which 15 were waited for; matrix products, arithmetic and copies ran while one was open for 12% of the time, Pallas kernels for 0%

profile of v2, /device:TPU:0, one launch (start us, length us, event | category | flops | bytes accessed | tf_op | source)
XLA Modules:
  0.0 286.6 jit_solution(15215376771582577262)
XLA Ops:
  9.8 25.4 %all_to_all.5 = bf16[8,160,256]{2,1,0:T(8,128)(2,1)} all-to-all(bf16[8,160,256]{2,1,0:T(8,128)(2,1)S(1)} %maximum_maximum_fusion), channel_id=1, replica_groups=mesh['shard'=2,'tensor'=4,'section'=4] {'shard','tensor'}, dimensions={0} | all-to-all | bytes 1310720 | tf_op jit(solution)/shard_map/all_to_all | solution.py:269
  35.2 3.0 %constant_dynamic-slice_fusion = (bf16[1,576,576]{2,1,0:T(8,128)(2,1)S(1)}, bf16[1,576,576]{2,1,0:T(8,128)(2,1)S(1)}, bf16[1,576,576]{2,1,0:T(8,128)(2,1)S(1)}, bf16[1,576,576]{2,1,0:T(8,128)(2,1)S(1)}) fusion(f32[4,576,576]{2,1,0:T(8,128)} %param.12, s32[]{:T(128)S(6)} %select_n.275, s32[]{:T(128)S(6)} %select_n.274, s32[]{:T(128)S(6)} %select_n.273, ...), kind=kLoop, calls=%fused_computation.160 | loop fusion | bytes 5308432 | tf_op jit(solution)/shard_map/jit(dynamic_index_in_dim)/dynamic_slice | solution.py:258
  42.1 3.3 %collective-permute-start.2 = (bf16[576,576]{0,1:T(8,128)(2,1)S(1)}, bf16[576,576]{0,1:T(8,128)(2,1)}, u32[]{:S(2)}, u32[]{:S(2)}) collective-permute-start(bf16[576,576]{0,1:T(8,128)(2,1)S(1)} %bitcast.158), channel_id=1, source_target_pairs={{0,12},{4,8},{8,4},{12,0},{1,13},{5,9},{9,5},{13,1},{2,14},{6,10},... | collective-permute-start | bytes 1990664 | tf_op jit(solution)/shard_map/ppermute | solution.py:168
  46.6 11.9 %all-gather.4.cloned.1.call-done = bf16[32,160,256]{2,1,0:T(8,128)(2,1)} async-done(((bf16[8,160,256]{2,1,0:T(8,128)(2,1)}), bf16[32,160,256]{2,1,0:T(8,128)(2,1)}) %all-gather.4.cloned.1.call-update) | async-done | bytes 2621456 | tf_op jit(solution)/shard_map/all_gather | solution.py:270
  66.6 3.9 %collective-permute-done = bf16[576,576]{0,1:T(8,128)(2,1)} collective-permute-done((bf16[576,576]{0,1:T(8,128)(2,1)}, bf16[576,576]{0,1:T(8,128)(2,1)}, u32[]{:S(2)}, u32[]{:S(2)}) %collective-permute-start) | collective-permute-done | bytes 663584 | tf_op jit(solution)/shard_map/ppermute | solution.py:168
  73.2 19.9 %collective-permute-done.1 = bf16[576,576]{0,1:T(8,128)(2,1)} collective-permute-done((bf16[576,576]{0,1:T(8,128)(2,1)}, bf16[576,576]{0,1:T(8,128)(2,1)}, u32[]{:S(2)}, u32[]{:S(2)}) %collective-permute-start.1) | collective-permute-done | bytes 663584 | tf_op jit(solution)/shard_map/ppermute | solution.py:168
  95.8 2.7 fusion.10
  98.5 5.6 %concatenate.87 = bf16[2304,576]{0,1:T(8,128)(2,1)} concatenate(bf16[576,576]{0,1:T(8,128)(2,1)S(1)} %copy-done.7, bf16[576,576]{0,1:T(8,128)(2,1)} %fusion.16, bf16[576,576]{0,1:T(8,128)(2,1)} %fusion.13, bf16[576,576]{0,1:T(8,128)(2,1)} %fusion.10), dimensions={0} | concatenate | bytes 5308416 | tf_op jit(solution)/shard_map/concatenate | solution.py:311
  114.7 14.2 %collective-permute-done.4 = bf16[256,1152]{0,1:T(8,128)(2,1)} collective-permute-done((bf16[256,1152]{0,1:T(8,128)(2,1)}, bf16[256,1152]{0,1:T(8,128)(2,1)}, u32[]{:S(2)}, u32[]{:S(2)}) %collective-permute-start.4) | collective-permute-done | bytes 589856 | tf_op jit(solution)/shard_map/ppermute | solution.py:168
  130.2 2.8 fusion.50
  137.4 13.3 %collective-permute-done.5 = bf16[256,1152]{0,1:T(8,128)(2,1)} collective-permute-done((bf16[256,1152]{0,1:T(8,128)(2,1)}, bf16[256,1152]{0,1:T(8,128)(2,1)}, u32[]{:S(2)}, u32[]{:S(2)}) %collective-permute-start.5) | collective-permute-done | bytes 589856 | tf_op jit(solution)/shard_map/ppermute | solution.py:168
  152.1 2.8 fusion.48
  163.5 24.4 %collective-permute-done.13 = bf16[576,512]{1,0:T(8,128)(2,1)S(1)} collective-permute-done((bf16[576,512]{1,0:T(8,128)(2,1)S(1)}, bf16[576,512]{1,0:T(8,128)(2,1)S(1)}, u32[]{:S(2)}, u32[]{:S(2)}) %collective-permute-start.13) | collective-permute-done | bytes 589856 | tf_op jit(solution)/shard_map/ppermute | solution.py:350
  189.2 4.3 %all_gather.14 = bf16[8,512]{1,0:T(8,128)(2,1)S(1)} all-gather(bf16[8,256]{1,0:T(8,128)(2,1)S(1)} %copy-done.16), channel_id=1, replica_groups=mesh['shard'=2,'tensor'=4,'section'=4] {'shard'}, dimensions={1}, use_global_device_ids=true | all-gather | bytes 12288 | tf_op jit(solution)/shard_map/all_gather | solution.py:414
  195.6 4.2 %all-gather.1 = s32[2,1,256]{2,1,0:T(1,128)S(1)} all-gather(s32[1,1,256]{2,1,0:T(1,128)S(1)} %bitcast.163), channel_id=1, replica_groups=mesh['shard'=2,'tensor'=4,'section'=4] {'shard'}, dimensions={0}, use_global_device_ids=true | all-gather | bytes 3072 | tf_op jit(solution)/shard_map/all_gather | solution.py:415
  207.6 3.0 %collective-permute-done.21 = f32[8,576]{1,0:T(8,128)S(1)} collective-permute-done((f32[8,576]{1,0:T(8,128)S(1)}, f32[8,576]{1,0:T(8,128)S(1)}, u32[]{:S(2)}, u32[]{:S(2)}) %collective-permute-start.21) | collective-permute-done | bytes 18464 | tf_op jit(solution)/shard_map/ppermute | solution.py:168
  212.1 9.9 %collective-permute-done.17 = bf16[576,512]{1,0:T(8,128)(2,1)} collective-permute-done((bf16[576,512]{1,0:T(8,128)(2,1)S(1)}, bf16[576,512]{1,0:T(8,128)(2,1)}, u32[]{:S(2)}, u32[]{:S(2)}) %collective-permute-start.17) | collective-permute-done | bytes 589856 | tf_op jit(solution)/shard_map/ppermute | solution.py:350
  228.7 7.4 %all-reduce.2 = (f32[2,144]{1,0:T(2,128)S(1)}, f32[2,144]{1,0:T(2,128)S(1)}) all-reduce(f32[2,144]{1,0:T(2,128)S(1)} %get-tuple-element.9, f32[2,144]{1,0:T(2,128)S(1)} %get-tuple-element.8), channel_id=1, replica_groups=mesh['shard'=2,'tensor'=4,'section'=4] {'shard'}, use_global_device_ids=true, to_apply=%region_13.14 | all-reduce | flops 576 | bytes 4608 | tf_op jit(solution)/shard_map/psum | solution.py:417
  247.3 3.8 %collective-permute-done.11 = bf16[576,512]{1,0:T(8,128)(2,1)} collective-permute-done((bf16[576,512]{1,0:T(8,128)(2,1)S(1)}, bf16[576,512]{1,0:T(8,128)(2,1)}, u32[]{:S(2)}, u32[]{:S(2)}) %collective-permute-start.11) | collective-permute-done | bytes 589856 | tf_op jit(solution)/shard_map/ppermute | solution.py:395
  252.5 6.7 %collective-permute-done.20.other_3 = bf16[576,512]{1,0:T(8,128)(2,1)S(1)} collective-permute-done((bf16[576,512]{1,0:T(8,128)(2,1)S(1)}, bf16[576,512]{1,0:T(8,128)(2,1)S(1)}, u32[]{:S(2)}, u32[]{:S(2)}) %collective-permute-start.20) | collective-permute-done | bytes 589856 | tf_op jit(solution)/shard_map/ppermute | solution.py:168
  259.2 3.3 %fusion.3 = f32[2048,576]{0,1:T(8,128)} fusion(f32[2048]{0:T(1024)S(1)} %copy-done.13, s32[512]{0:T(512)S(1)} %bitcast.162, s32[2048]{0:T(1024)S(1)} %iota_add_fusion, bf16[576,512]{1,0:T(8,128)(2,1)S(1)} %get-tuple-element.28.own_3, bf16[576,512]{1,0:T(8,128)(2,1)S(1)} %collective-permute-done.20.other_3, pred[]{:T(512)S(6)} %eq.128), kind=kOutput, calls=%fused_computation.6 | convolution fusion | flops 1210482688 | bytes 5916673 | tf_op jit(solution)/shard_map/vn,cn->vc/dot_general | solution.py:451
  262.7 6.5 %collective-permute-done.18.other_1 = bf16[576,512]{1,0:T(8,128)(2,1)S(1)} collective-permute-done((bf16[576,512]{1,0:T(8,128)(2,1)S(1)}, bf16[576,512]{1,0:T(8,128)(2,1)S(1)}, u32[]{:S(2)}, u32[]{:S(2)}) %collective-permute-start.18) | collective-permute-done | bytes 589856 | tf_op jit(solution)/shard_map/ppermute | solution.py:168
  269.2 6.3 %collective-permute-done.19.other_2 = bf16[576,512]{1,0:T(8,128)(2,1)S(1)} collective-permute-done((bf16[576,512]{1,0:T(8,128)(2,1)S(1)}, bf16[576,512]{1,0:T(8,128)(2,1)S(1)}, u32[]{:S(2)}, u32[]{:S(2)}) %collective-permute-start.19) | collective-permute-done | bytes 589856 | tf_op jit(solution)/shard_map/ppermute | solution.py:168
  275.5 4.3 %shard_map.111 = f32[4,576,576]{2,1,0:T(8,128)} custom-call(s32[1]{0:T(128)} %bitcast.shard_ref, bf16[576,512]{1,0:T(8,128)(2,1)S(1)} %broadcast_select_fusion.8.left_own, bf16[576,512]{1,0:T(8,128)(2,1)S(1)} %broadcast_select_fusion.7.left_other, bf16[576,512]{1,0:T(8,128)(2,1)S(1)} %get-tuple-element.30.own_1, ...), custom_call_target="tpu_custom_call" | custom-call | flops 1358954496 | bytes 10027008 | tf_op jit(solution)/shard_map/pallas_call | solution.py:214
  (156 shorter events, 77.6 us)
Async XLA Ops:
  7.2 51.4 %all-gather.4.cloned.1.call-start = ((), (), s32[]{:S(2)}) async-start(), calls=%async_computation.1 | async-start | bytes 3276800 | tf_op jit(solution)/shard_map/all_gather | solution.py:270
  39.4 31.1 %collective-permute-start = (bf16[576,576]{0,1:T(8,128)(2,1)}, bf16[576,576]{0,1:T(8,128)(2,1)}, u32[]{:S(2)}, u32[]{:S(2)}) collective-permute-start(bf16[576,576]{0,1:T(8,128)(2,1)} %bitcast.159), channel_id=1, source_target_pairs={{0,4},{4,0},{8,12},{12,8},{1,5},{5,1},{9,13},{13,9},{2,6},{6,2},{1... | collective-permute-start | bytes 1990664 | tf_op jit(solution)/shard_map/ppermute | solution.py:168
  40.9 52.2 %collective-permute-start.1 = (bf16[576,576]{0,1:T(8,128)(2,1)}, bf16[576,576]{0,1:T(8,128)(2,1)}, u32[]{:S(2)}, u32[]{:S(2)}) collective-permute-start(bf16[576,576]{0,1:T(8,128)(2,1)} %bitcast.132), channel_id=1, source_target_pairs={{0,8},{4,12},{8,0},{12,4},{1,9},{5,13},{9,1},{13,5},{2,10},{6,14},... | collective-permute-start | bytes 1990664 | tf_op jit(solution)/shard_map/ppermute | solution.py:168
  42.1 53.7 %collective-permute-start.2 = (bf16[576,576]{0,1:T(8,128)(2,1)S(1)}, bf16[576,576]{0,1:T(8,128)(2,1)}, u32[]{:S(2)}, u32[]{:S(2)}) collective-permute-start(bf16[576,576]{0,1:T(8,128)(2,1)S(1)} %bitcast.158), channel_id=1, source_target_pairs={{0,12},{4,8},{8,4},{12,0},{1,13},{5,9},{9,5},{13,1},{2,14},{6,10},... | collective-permute-start | bytes 1990664 | tf_op jit(solution)/shard_map/ppermute | solution.py:168
  104.1 5.3 %collective-permute-start.3 = (bf16[2304,576]{0,1:T(8,128)(2,1)}, bf16[2304,576]{0,1:T(8,128)(2,1)}, u32[]{:S(2)}, u32[]{:S(2)}) collective-permute-start(bf16[2304,576]{0,1:T(8,128)(2,1)} %concatenate.87), channel_id=1, source_target_pairs={{0,1},{1,0},{2,3},{3,2},{4,5},{5,4},{6,7},{7,6},{8,9},{9,8},{10,11... | collective-permute-start | bytes 7962632 | tf_op jit(solution)/shard_map/ppermute | solution.py:168
  113.2 15.7 %collective-permute-start.4 = (bf16[256,1152]{0,1:T(8,128)(2,1)}, bf16[256,1152]{0,1:T(8,128)(2,1)}, u32[]{:S(2)}, u32[]{:S(2)}) collective-permute-start(bf16[256,1152]{0,1:T(8,128)(2,1)} %reduce-precision_convert_fusion), channel_id=1, source_target_pairs={{0,2},{1,3},{2,0},{3,1},{4,6},{5,7},{6,4},{7,5},{8,10},{9,11},{10,... | collective-permute-start | bytes 1769480 | tf_op jit(solution)/shard_map/ppermute | solution.py:168
  135.9 14.9 %collective-permute-start.5 = (bf16[256,1152]{0,1:T(8,128)(2,1)}, bf16[256,1152]{0,1:T(8,128)(2,1)}, u32[]{:S(2)}, u32[]{:S(2)}) collective-permute-start(bf16[256,1152]{0,1:T(8,128)(2,1)} %reduce-precision_convert_fusion.1), channel_id=1, source_target_pairs={{0,2},{1,3},{2,0},{3,1},{4,6},{5,7},{6,4},{7,5},{8,10},{9,11},{10,... | collective-permute-start | bytes 1769480 | tf_op jit(solution)/shard_map/ppermute | solution.py:168
  161.5 26.4 %collective-permute-start.13 = (bf16[576,512]{1,0:T(8,128)(2,1)S(1)}, bf16[576,512]{1,0:T(8,128)(2,1)S(1)}, u32[]{:S(2)}, u32[]{:S(2)}) collective-permute-start(bf16[576,512]{1,0:T(8,128)(2,1)S(1)} %pad_maximum_fusion.8), channel_id=1, source_target_pairs={{12,8},{8,4},{4,0},{28,24},{20,16},{13,9},{9,5},{5,1},{29,25},{21,... | collective-permute-start | bytes 1769480 | tf_op jit(solution)/shard_map/ppermute | solution.py:350
  162.8 38.8 %collective-permute-start.14 = (bf16[576,512]{1,0:T(8,128)(2,1)S(1)}, bf16[576,512]{1,0:T(8,128)(2,1)S(1)}, u32[]{:S(2)}, u32[]{:S(2)}) collective-permute-start(bf16[576,512]{1,0:T(8,128)(2,1)S(1)} %pad_maximum_fusion.8), channel_id=1, source_target_pairs={{4,8},{8,12},{20,24},{5,9},{9,13},{21,25},{6,10},{10,14},{22,26},{... | collective-permute-start | bytes 1769480 | tf_op jit(solution)/shard_map/ppermute | solution.py:350
  187.9 17.2 %collective-permute-start.16 = (bf16[576,512]{1,0:T(8,128)(2,1)S(1)}, bf16[576,512]{1,0:T(8,128)(2,1)S(1)}, u32[]{:S(2)}, u32[]{:S(2)}) collective-permute-start(bf16[576,512]{1,0:T(8,128)(2,1)S(1)} %collective-permute-done.13), channel_id=1, source_target_pairs={{8,4},{4,0},{24,20},{9,5},{5,1},{25,21},{10,6},{6,2},{26,22},{11,7... | collective-permute-start | bytes 1769480 | tf_op jit(solution)/shard_map/ppermute | solution.py:350
  200.1 11.9 %collective-permute-start.7 = (bf16[576,512]{1,0:T(8,128)(2,1)S(1)}, bf16[576,512]{1,0:T(8,128)(2,1)}, u32[]{:S(2)}, u32[]{:S(2)}) collective-permute-start(bf16[576,512]{1,0:T(8,128)(2,1)S(1)} %pad_maximum_fusion.8), channel_id=1, source_target_pairs={{1,5},{2,10},{3,15},{17,21},{18,26},{19,31}} | collective-permute-start | bytes 1769480 | tf_op jit(solution)/shard_map/ppermute | solution.py:382
  201.6 10.4 %collective-permute-start.15 = (bf16[576,512]{1,0:T(8,128)(2,1)S(1)}, bf16[576,512]{1,0:T(8,128)(2,1)}, u32[]{:S(2)}, u32[]{:S(2)}) collective-permute-start(bf16[576,512]{1,0:T(8,128)(2,1)S(1)} %collective-permute-done.14), channel_id=1, source_target_pairs={{8,12},{24,28},{9,13},{25,29},{10,14},{26,30},{11,15},{27,31}} | collective-permute-start | bytes 1769480 | tf_op jit(solution)/shard_map/ppermute | solution.py:350
  205.1 16.8 %collective-permute-start.17 = (bf16[576,512]{1,0:T(8,128)(2,1)S(1)}, bf16[576,512]{1,0:T(8,128)(2,1)}, u32[]{:S(2)}, u32[]{:S(2)}) collective-permute-start(bf16[576,512]{1,0:T(8,128)(2,1)S(1)} %collective-permute-done.16), channel_id=1, source_target_pairs={{4,0},{20,16},{5,1},{21,17},{6,2},{22,18},{7,3},{23,19}} | collective-permute-start | bytes 1769480 | tf_op jit(solution)/shard_map/ppermute | solution.py:350
  210.6 16.5 %collective-permute-start.22 = (f32[8,576]{1,0:T(8,128)S(1)}, f32[8,576]{1,0:T(8,128)S(1)}, u32[]{:S(2)}, u32[]{:S(2)}) collective-permute-start(f32[8,576]{1,0:T(8,128)S(1)} %broadcast_select_fusion.17), channel_id=1, source_target_pairs={{8,0},{9,5},{11,15},{24,16},{25,21},{27,31}} | collective-permute-start | bytes 55304 | tf_op jit(solution)/shard_map/ppermute | solution.py:382
  224.3 15.2 %collective-permute-start.10 = (bf16[576,512]{1,0:T(8,128)(2,1)S(1)}, bf16[576,512]{1,0:T(8,128)(2,1)S(1)}, u32[]{:S(2)}, u32[]{:S(2)}) collective-permute-start(bf16[576,512]{1,0:T(8,128)(2,1)S(1)} %get-tuple-element.43), channel_id=1, source_target_pairs={{0,16},{5,21},{10,26},{15,31},{16,0},{21,5},{26,10},{31,15}} | collective-permute-start | bytes 1769480 | tf_op jit(solution)/shard_map/ppermute | solution.py:390
  227.1 11.1 %collective-permute-start.23 = (f32[8,576]{1,0:T(8,128)S(1)}, f32[8,576]{1,0:T(8,128)S(1)}, u32[]{:S(2)}, u32[]{:S(2)}) collective-permute-start(f32[8,576]{1,0:T(8,128)S(1)} %broadcast_select_fusion.18), channel_id=1, source_target_pairs={{0,2},{5,7},{10,8},{15,13},{16,18},{21,23},{26,24},{31,29}} | collective-permute-start | bytes 55304 | tf_op jit(solution)/shard_map/ppermute | solution.py:395
  236.1 9.8 %collective-permute-start.8 = (bf16[576,512]{1,0:T(8,128)(2,1)S(1)}, bf16[576,512]{1,0:T(8,128)(2,1)}, u32[]{:S(2)}, u32[]{:S(2)}) collective-permute-start(bf16[576,512]{1,0:T(8,128)(2,1)S(1)} %get-tuple-element.43), channel_id=1, source_target_pairs={{0,2},{5,7},{10,8},{15,13},{16,18},{21,23},{26,24},{31,29}} | collective-permute-start | bytes 1769480 | tf_op jit(solution)/shard_map/ppermute | solution.py:395
  238.2 5.0 %collective-permute-start.24 = (f32[8,576]{1,0:T(8,128)S(1)}, f32[8,576]{1,0:T(8,128)S(1)}, u32[]{:S(2)}, u32[]{:S(2)}) collective-permute-start(f32[8,576]{1,0:T(8,128)S(1)} %broadcast_select_fusion.19), channel_id=1, source_target_pairs={{0,1},{2,3},{5,4},{7,6},{10,11},{8,9},{15,14},{13,12},{16,17},{18,... | collective-permute-start | bytes 55304 | tf_op jit(solution)/shard_map/ppermute | solution.py:399
  239.5 11.6 %collective-permute-start.11 = (bf16[576,512]{1,0:T(8,128)(2,1)S(1)}, bf16[576,512]{1,0:T(8,128)(2,1)}, u32[]{:S(2)}, u32[]{:S(2)}) collective-permute-start(bf16[576,512]{1,0:T(8,128)(2,1)S(1)} %collective-permute-done.10), channel_id=1, source_target_pairs={{0,2},{5,7},{10,8},{15,13},{16,18},{21,23},{26,24},{31,29}} | collective-permute-start | bytes 1769480 | tf_op jit(solution)/shard_map/ppermute | solution.py:395
  242.9 16.3 %collective-permute-start.20 = (bf16[576,512]{1,0:T(8,128)(2,1)S(1)}, bf16[576,512]{1,0:T(8,128)(2,1)S(1)}, u32[]{:S(2)}, u32[]{:S(2)}) collective-permute-start(bf16[576,512]{1,0:T(8,128)(2,1)S(1)} %get-tuple-element.28.own_3), channel_id=1, source_target_pairs={{0,16},{16,0},{1,17},{17,1},{2,18},{18,2},{3,19},{19,3},{4,20},{20... | collective-permute-start | bytes 1769480 | tf_op jit(solution)/shard_map/ppermute | solution.py:168
  243.9 25.3 %collective-permute-start.18 = (bf16[576,512]{1,0:T(8,128)(2,1)S(1)}, bf16[576,512]{1,0:T(8,128)(2,1)S(1)}, u32[]{:S(2)}, u32[]{:S(2)}) collective-permute-start(bf16[576,512]{1,0:T(8,128)(2,1)S(1)} %get-tuple-element.30.own_1), channel_id=1, source_target_pairs={{0,16},{16,0},{1,17},{17,1},{2,18},{18,2},{3,19},{19,3},{4,20},{20... | collective-permute-start | bytes 1769480 | tf_op jit(solution)/shard_map/ppermute | solution.py:168
  245.6 29.9 %collective-permute-start.19 = (bf16[576,512]{1,0:T(8,128)(2,1)S(1)}, bf16[576,512]{1,0:T(8,128)(2,1)S(1)}, u32[]{:S(2)}, u32[]{:S(2)}) collective-permute-start(bf16[576,512]{1,0:T(8,128)(2,1)S(1)} %get-tuple-element.29.own_2), channel_id=1, source_target_pairs={{0,16},{16,0},{1,17},{17,1},{2,18},{18,2},{3,19},{19,3},{4,20},{20... | collective-permute-start | bytes 1769480 | tf_op jit(solution)/shard_map/ppermute | solution.py:168
  246.0 16.6 %collective-permute-start.9 = (bf16[576,512]{1,0:T(8,128)(2,1)S(1)}, bf16[576,512]{1,0:T(8,128)(2,1)S(1)}, u32[]{:S(2)}, u32[]{:S(2)}) collective-permute-start(bf16[576,512]{1,0:T(8,128)(2,1)S(1)} %broadcast_select_fusion.6), channel_id=1, source_target_pairs={{0,1},{2,3},{5,4},{7,6},{10,11},{8,9},{15,14},{13,12},{16,17},{18,... | collective-permute-start | bytes 1769480 | tf_op jit(solution)/shard_map/ppermute | solution.py:399
  251.2 11.4 %collective-permute-start.12 = (bf16[576,512]{1,0:T(8,128)(2,1)S(1)}, bf16[576,512]{1,0:T(8,128)(2,1)S(1)}, u32[]{:S(2)}, u32[]{:S(2)}) collective-permute-start(bf16[576,512]{1,0:T(8,128)(2,1)S(1)} %broadcast_select_fusion.5), channel_id=1, source_target_pairs={{0,1},{2,3},{5,4},{7,6},{10,11},{8,9},{15,14},{13,12},{16,17},{18,... | collective-permute-start | bytes 1769480 | tf_op jit(solution)/shard_map/ppermute | solution.py:399
  (21 other events, 216.3 us)
Sparse Core Ops, SparseCore 0:
  35.3 23.1 all-gather.3

commit v3 on v2

--- a/solution.py
+++ b/solution.py
@@ -1,3 +1,4 @@
+import functools
 import math
 
 import jax
@@ -178,6 +179,159 @@
     return jnp.concatenate(pieces, axis=1)
 
 
+def rounded(values):
+    return values.astype(jnp.bfloat16).astype(jnp.float32)
+
+
+def params():
+    return pltpu.CompilerParams(vmem_limit_bytes=40 * 1024 * 1024)
+
+
+def factor_kernel(place_ref, part, own, old, diag, out, *, step, weight):
+    fresh = jnp.zeros(out.shape, jnp.float32)
+    for index in range(part.shape[0]):
+        fresh += lax.dot_general(
+            part[index], own[index], (((1,), (1,)), ((), ())), preferred_element_type=jnp.float32
+        )
+    block = factor_decay * old[...].astype(jnp.float32) + weight * fresh
+    on_diag = lax.broadcasted_iota(jnp.int32, out.shape, 0) == lax.broadcasted_iota(
+        jnp.int32, out.shape, 1
+    )
+    block = jnp.where(on_diag & (place_ref[0] == step), diag[0], block)
+    out[...] = block.astype(jnp.bfloat16)
+
+
+def factor_block(place, features, old, diag, step, weight):
+    groups, _, tokens = features.shape
+    rows, cols = old.shape
+    return pl.pallas_call(
+        functools.partial(factor_kernel, step=step, weight=weight),
+        grid_spec=pltpu.PrefetchScalarGridSpec(
+            num_scalar_prefetch=1,
+            grid=(1,),
+            in_specs=[
+                pl.BlockSpec((groups, rows, tokens), lambda i, place: (0, step, 0)),
+                pl.BlockSpec((groups, cols, tokens), lambda i, place: (0, place[0], 0)),
+                pl.BlockSpec((rows, cols), lambda i, place: (0, 0)),
+                pl.BlockSpec((1, 1, cols), lambda i, place: (place[0], 0, 0)),
+            ],
+            out_specs=pl.BlockSpec((rows, cols), lambda i, place: (0, 0)),
+        ),
+        out_shape=jax.ShapeDtypeStruct((rows, cols), jnp.bfloat16),
+        compiler_params=params(),
+        cost_estimate=pl.CostEstimate(
+            flops=2 * groups * rows * cols * tokens,
+            bytes_accessed=4 * rows * cols + 4 * groups * rows * tokens,
+            transcendentals=0,
+        ),
+    )(place, features, features, old, diag)
+
+
+def fetch_blocks(blocks, held, sems):
+    copies = [
+        pltpu.make_async_copy(blocks[index], held.at[index], sems.at[index])
+        for index in range(len(blocks))
+    ]
+    for copy in copies:
+        copy.start()
+    return copies
+
+
+def block_products(pieces, count, copies, held):
+    own = other = None
+    for step in range(count):
+        piece = pieces(step)
+        copies[step].wait()
+        term = jnp.dot(piece, held[step], preferred_element_type=jnp.float32)
+        own = term if own is None else own + term
+        copies[count + step].wait()
+        term = jnp.dot(piece, held[count + step], preferred_element_type=jnp.float32)
+        other = term if other is None else other + term
+    return own, other
+
+
+def first_kernel(place_ref, scale_ref, rows, diag, *refs):
+    blocks, (by_first, step_one, message), (held, sems) = refs[:8], refs[8:11], refs[11:]
+    copies = fetch_blocks(blocks, held, sems)
+    products = block_products(lambda step: rows[step], 4, copies, held)
+    scale = scale_ref[0]
+    square = scale * scale
+    lows = []
+    for index in range(2):
+        values = rows[place_ref[0] ^ index].astype(jnp.float32)
+        low_diag = diag[place_ref[0] ^ index]
+        first_diag = rounded(2.0 * scale - square * low_diag)
+        by_first[index] = 2.0 * scale * values - square * products[index]
+        one = first_diag * values - square * (products[index] - low_diag * values)
+        step_one[index] = one
+        lows.append(one.astype(jnp.bfloat16))
+    message[...] = jnp.concatenate(lows, axis=1)
+
+
+def put_pieces(pieces, mine, theirs):
+    width = pieces.shape[2]
+    for index in range(2):
+        pieces[index] = mine[:, index * width : (index + 1) * width]
+        pieces[2 + index] = theirs[:, index * width : (index + 1) * width]
+
+
+def second_kernel(place_ref, mine, theirs, step_one, diag, *refs):
+    blocks, (step_two, message), (held, sems, pieces) = refs[:8], refs[8:10], refs[10:]
+    copies = fetch_blocks(blocks, held, sems)
+    put_pieces(pieces, mine, theirs)
+    products = block_products(lambda step: pieces[place_ref[0] ^ step], 4, copies, held)
+    lows = []
+    for index in range(2):
+        low_diag = diag[place_ref[0] ^ index]
+        one = step_one[index]
+        two = products[index] + low_diag * (one - rounded(one))
+        step_two[index] = two
+        lows.append(two.astype(jnp.bfloat16))
+    message[...] = jnp.concatenate(lows, axis=1)
+
+
+def third_kernel(place_ref, scale_ref, mine, theirs, step_two, by_first, diag, *refs):
+    blocks, (keep, give), (held, sems, pieces) = refs[:8], refs[8:10], refs[10:]
+    copies = fetch_blocks(blocks, held, sems)
+    put_pieces(pieces, mine, theirs)
+    products = block_products(lambda step: pieces[place_ref[0] ^ step], 4, copies, held)
+    scale = scale_ref[0]
+    square = scale * scale
+    for index, out in ((0, keep), (1, give)):
+        low_diag = diag[place_ref[0] ^ index]
+        first_diag = rounded(2.0 * scale - square * low_diag)
+        two = step_two[index]
+        three = first_diag * two - square * (products[index] - low_diag * rounded(two))
+        out[...] = (2.0 * by_first[index] - three).T.astype(jnp.bfloat16)
+
+
+def chain_call(kernel, scalars, arrays, blocks, out_shape, pieces):
+    tokens = out_shape[0].shape[-1] if pieces is None else pieces[1]
+    width = blocks[0].shape[1]
+    vmem = pl.BlockSpec(memory_space=pltpu.VMEM)
+    scratch = [
+        pltpu.VMEM((len(blocks),) + blocks[0].shape, jnp.bfloat16),
+        pltpu.SemaphoreType.DMA((len(blocks),)),
+    ]
+    if pieces is not None:
+        scratch.append(pltpu.VMEM(pieces, jnp.bfloat16))
+    return pl.pallas_call(
+        kernel,
+        in_specs=[pl.BlockSpec(memory_space=pltpu.SMEM)] * len(scalars)
+        + [vmem] * len(arrays)
+        + [pl.BlockSpec(memory_space=pl.ANY)] * len(blocks),
+        out_specs=[vmem] * len(out_shape),
+        out_shape=out_shape,
+        scratch_shapes=scratch,
+        compiler_params=params(),
+        cost_estimate=pl.CostEstimate(
+            flops=2 * len(blocks) * tokens * width * width,
+            bytes_accessed=2 * len(blocks) * width * width,
+            transcendentals=0,
+        ),
+    )(*scalars, *arrays, *blocks)
+
+
 def attn_kernel(shard_ref, left_own, left_other, own_1, own_2, own_3, other_1, other_2, other_3, out):
     first = shard_ref[0] == 0
 
@@ -217,7 +371,7 @@
         out_shape=jax.ShapeDtypeStruct((4, rows, cols), jnp.float32),
         in_specs=[pl.BlockSpec(memory_space=pltpu.SMEM)] + whole,
         out_specs=pl.BlockSpec((1, rows, cols), lambda w: (w, 0, 0)),
-        compiler_params=pltpu.CompilerParams(vmem_limit_bytes=40 * 1024 * 1024),
+        compiler_params=params(),
         cost_estimate=pl.CostEstimate(
             flops=8 * rows * cols * tokens_all,
             bytes_accessed=16 * rows * cols + 16 * rows * tokens_all,
@@ -247,115 +401,194 @@
     tokens = activations.shape[1]
     features_dev = activations.shape[2]
     tokens_all = tokens * n_shard
-    half = 2 * col_block
     weight = (1.0 - factor_decay) / tokens_all
-    half_place = (section // 2) ^ (layer // 2)
-    core_place = core ^ (layer % 2)
     own_place = section ^ layer
-
-    blocks = [None] * n_tensor
-    for step in (3, 2, 1):
-        away = lax.dynamic_index_in_dim(old_factors, layer ^ step, 0, False)
-        blocks[step] = swap(away.astype(jnp.bfloat16), "tensor", n_tensor, step)
-    blocks[0] = lax.dynamic_index_in_dim(old_factors, layer, 0, False).astype(jnp.bfloat16)
+    place = own_place.reshape(1)
+
+    def by_index(array, index, axis=0):
+        return lax.dynamic_index_in_dim(array, index, axis, False)
 
     diagonals = local_diagonals(old_factors) * (layer == section).astype(jnp.float32)
     extra = jnp.pad(split_three(diagonals), ((0, 0), (0, 0), (0, 3 * tokens - col_block)))
     extra = jnp.pad(extra.reshape(owned, 9, tokens), ((0, 0), (0, 7), (0, 0)))
-    extra = jnp.concatenate(
-        [jnp.where(shard == 0, extra, 0), jnp.where(shard == 1, extra, 0)], axis=0
-    )
-    message = jnp.concatenate([jnp.swapaxes(activations, 1, 2), extra], axis=1)
-    moved = lax.all_to_all(message, ("shard", "tensor"), 0, 0, tiled=True)
-    gathered = lax.all_gather(moved, "section", axis=0)
-    gathered = gathered.reshape(n_section, n_shard, n_tensor, features_dev + 16, tokens)
-    by_place = [
-        lax.dynamic_index_in_dim(gathered, layer ^ step, 2, False) for step in range(n_tensor)
-    ]
-    features = jnp.stack([part[:, :, :features_dev] for part in by_place], axis=0)
-    features = features.transpose(2, 0, 1, 3, 4).reshape(n_shard, D, tokens)
-    codes = jnp.sum(
-        gathered[:, :, :, features_dev : features_dev + 9].astype(jnp.float32), axis=(1, 2)
-    )
-    old_diag = jnp.sum(codes.reshape(n_section, 3, 3 * tokens), axis=1)[:, :col_block]
-    old_diag = jnp.concatenate(
+    by_feature = jnp.swapaxes(activations, 1, 2)
+    axes = ("shard", "tensor")
+    token_parts = {}
+    for away in range(n_shard):
+        for step in range(n_tensor):
+            factor = (shard ^ away) * n_tensor + (layer ^ step)
+            message = by_index(by_feature, factor)
+            if away == 0:
+                message = jnp.concatenate([message, by_index(extra, layer ^ step)], axis=0)
+            if away or step:
+                moves = [
+                    (x * n_tensor + z, (x ^ away) * n_tensor + (z ^ step))
+                    for x in range(n_shard)
+                    for z in range(n_tensor)
+                ]
+                message = lax.ppermute(message, axes, moves)
+            token_parts[away, step] = message
+    collected = jnp.stack(
         [
-            lax.dynamic_index_in_dim(old_diag, layer ^ step, 0, False)
+            jnp.concatenate(
+                [
+                    token_parts[0, step][:features_dev],
+                    token_parts[1, step],
+                    token_parts[0, step][features_dev:],
+                ],
+                axis=0,
+            )
             for step in range(n_tensor)
         ]
     )
+    gathered = lax.all_gather(collected, "section", axis=0)
+
+    blocks = [by_index(old_factors, layer).astype(jnp.bfloat16)]
+    for step in (1, 2, 3):
+        away = by_index(old_factors, layer ^ step)
+        blocks.append(swap(away.astype(jnp.bfloat16), "tensor", n_tensor, step))
+
+    def both_shards(value, axis):
+        other = swap(value, "shard", n_shard, 1)
+        return jnp.where(
+            shard == 0,
+            jnp.concatenate([value, other], axis=axis),
+            jnp.concatenate([other, value], axis=axis),
+        )
+
+    grad_all = both_shards(router_grad, 1)
+    ids_all = both_shards(token_ids, 0)
+    norm_values = norm_terms.astype(jnp.float32)
+    norm_sums = jnp.stack([jnp.sum(norm_values, axis=1), jnp.sum(norm_values * norm_values, axis=1)])
+    norm_sums = norm_sums + swap(norm_sums, "shard", n_shard, 1)
+    gathered, grad_all, ids_all, norm_sums = lax.optimization_barrier(
+        (gathered, grad_all, ids_all, norm_sums)
+    )
+
+    features = gathered[:, :, : 2 * features_dev].reshape(
+        n_section, n_tensor, n_shard, features_dev, tokens
+    )
+    features = features.transpose(2, 1, 0, 3, 4).reshape(n_shard, D, tokens)
+    codes = jnp.sum(
+        gathered[:, :, 2 * features_dev : 2 * features_dev + 9].astype(jnp.float32), axis=1
+    )
+    old_diag = jnp.sum(codes.reshape(n_section, 3, 3 * tokens), axis=1)[:, :col_block]
+    old_diag = jnp.stack([by_index(old_diag, layer ^ step) for step in range(n_tensor)])
     values = features.astype(jnp.float32)
-    squares = jnp.sum(values * values, axis=(0, 2))
+    squares = jnp.sum(values * values, axis=(0, 2)).reshape(n_tensor, col_block)
     matrix_diag = factor_decay * old_diag + weight * squares + damping
-    scale = D / (3.0 * jnp.sum(matrix_diag))
-    square = scale * scale
-    all_low_diag = lax.reduce_precision(matrix_diag, 8, 7)
-    low_diag = lax.dynamic_slice_in_dim(all_low_diag, half_place * half, half, 0)
-    own_diag = lax.dynamic_slice_in_dim(all_low_diag, own_place * col_block, col_block, 0)
-    first_diag = lax.reduce_precision(2.0 * scale - square * low_diag, 8, 7)
-    rows = jnp.swapaxes(lax.dynamic_index_in_dim(features, core, 0, False), 0, 1)
-    rows_half = lax.dynamic_slice_in_dim(rows, half_place * half, half, 1).astype(jnp.float32)
-
-    own_features = lax.dynamic_slice_in_dim(features, own_place * col_block, col_block, 1)
-    eye = lax.broadcasted_iota(jnp.int32, (row_block, col_block), 0) == lax.broadcasted_iota(
-        jnp.int32, (row_block, col_block), 1
-    )
-    low_blocks = []
-    for step in range(n_tensor):
-        part = features[:, step * row_block : (step + 1) * row_block]
-        fresh = jnp.einsum("xrn,xcn->rc", part, own_features, preferred_element_type=jnp.float32)
-        block = factor_decay * blocks[step].astype(jnp.float32) + weight * fresh
-        low_blocks.append(
-            jnp.where(eye & (own_place == step), own_diag[None, :], block).astype(jnp.bfloat16)
-        )
-    own_cols = jnp.concatenate(low_blocks, axis=0)
-    other_cols = swap(own_cols, "section", n_section, 1)
-
-    def whole_rows(mine):
-        theirs = swap(mine, "section", n_section, 2)
-        low = half_place == 0
-        return jnp.concatenate(
-            [jnp.where(low, mine, theirs), jnp.where(low, theirs, mine)], axis=1
-        )
-
-    def times(left):
-        own = jnp.dot(left, own_cols, preferred_element_type=jnp.float32)
-        other = jnp.dot(left, other_cols, preferred_element_type=jnp.float32)
-        low = core_place == 0
-        return jnp.concatenate([jnp.where(low, own, other), jnp.where(low, other, own)], axis=1)
-
-    product = times(rows)
-    by_first = 2.0 * scale * rows_half - square * product
-    step_one = first_diag * rows_half - square * (product - low_diag * rows_half)
-    step_one_low = lax.reduce_precision(step_one, 8, 7)
-    step_two = times(whole_rows(step_one_low.astype(jnp.bfloat16))) + low_diag * (
-        step_one - step_one_low
-    )
-    step_two_low = lax.reduce_precision(step_two, 8, 7)
-    step_three = first_diag * step_two - square * (
-        times(whole_rows(step_two_low.astype(jnp.bfloat16))) - low_diag * step_two_low
-    )
-    result = jnp.swapaxes((2.0 * by_first - step_three).astype(jnp.bfloat16), 0, 1)
-
-    keep = lax.dynamic_slice_in_dim(result, core_place * col_block, col_block, 0)
-    give = lax.dynamic_slice_in_dim(result, (1 - core_place) * col_block, col_block, 0)
+    scale = (D / (3.0 * jnp.sum(matrix_diag))).reshape(1)
+    low_diag = lax.reduce_precision(matrix_diag, 8, 7)[:, None, :]
+    rows = by_index(features, core).reshape(n_tensor, row_block, tokens)
+    rows = jnp.swapaxes(rows, 1, 2)
+
+    own_cols = [
+        factor_block(place, features, blocks[step], low_diag, step, weight)
+        for step in range(n_tensor)
+    ]
+    other_cols = [swap(block, "section", n_section, 1) for block in own_cols]
+    cols = own_cols + other_cols
+
+    def shaped(dtype, *shape):
+        return jax.ShapeDtypeStruct(shape, dtype)
+
+    wide = shaped(jnp.float32, 2, tokens, col_block)
+    sent = shaped(jnp.bfloat16, tokens, 2 * col_block)
+    part = shaped(jnp.bfloat16, col_block, tokens)
+    pieces = (n_tensor, tokens, col_block)
+    by_first, step_one, message = chain_call(
+        first_kernel, (place, scale), (rows, low_diag), cols, (wide, wide, sent), None
+    )
+    theirs = swap(message, "section", n_section, 2)
+    step_two, message = chain_call(
+        second_kernel, (place,), (message, theirs, step_one, low_diag), cols, (wide, sent), pieces
+    )
+    theirs = swap(message, "section", n_section, 2)
+    keep, give = chain_call(
+        third_kernel,
+        (place, scale),
+        (message, theirs, step_two, by_first, low_diag),
+        cols,
+        (part, part),
+        pieces,
+    )
     got = swap(give, "section", n_section, 1)
-    own = jnp.concatenate(
-        [jnp.where(core == 0, keep, got), jnp.where(core == 0, got, keep)], axis=1
-    )
-
-    axes = ("shard", "tensor")
+    own = jnp.where(
+        core == shard, jnp.concatenate([keep, got], axis=1), jnp.concatenate([got, keep], axis=1)
+    )
 
     def send(value, moves):
         return lax.ppermute(
             value, axes, [(x * n_tensor + a, x * n_tensor + b) for x, a, b in moves]
         )
 
+    def across(value, layers):
+        return lax.ppermute(
+            value,
+            axes,
+            [(x * n_tensor + z, (1 - x) * n_tensor + z) for x, z in layers],
+        )
+
+    everywhere = ("shard", "tensor", "section")
+
+    def spot(x, z, s):
+        return (x * n_tensor + z) * n_section + s
+
+    planes = range(n_shard)
+    layers = range(n_tensor)
+
+    def scatter(value, source):
+        moved_here = lax.ppermute(
+            value,
+            everywhere,
+            [(spot(x, source, s), spot(x, s, s)) for x in planes for s in layers if s != source],
+        )
+        return jnp.where(layer == source, value, moved_here)
+
+    def to_side(value):
+        got = lax.ppermute(
+            value, everywhere, [(spot(x, t, t), spot(x, t, t ^ 2)) for x in planes for t in layers]
+        )
+        return jnp.where(section == layer, value, got)
+
+    def to_core(value):
+        got = lax.ppermute(
+            value,
+            everywhere,
+            [(spot(x, t, t ^ a), spot(x, t, t ^ a ^ 1)) for x in planes for t in layers for a in (0, 2)],
+        )
+        return jnp.where((section ^ layer) % 2 == 0, value, got)
+
     down_1 = send(own, [(0, 3, 2), (0, 2, 1), (0, 1, 0), (1, 3, 2), (1, 1, 0)])
     up_1 = send(own, [(0, 1, 2), (0, 2, 3), (1, 1, 2)])
+    over_0 = across(own, [(0, 1), (0, 2), (0, 3), (1, 1), (1, 3)])
+    left_here = scatter(own, 0)
+    down_1, up_1, over_0 = lax.optimization_barrier((down_1, up_1, over_0))
+
     down_2 = send(down_1, [(0, 2, 1), (0, 1, 0), (1, 2, 1)])
     up_2 = send(up_1, [(0, 2, 3), (1, 2, 3)])
+    over_1 = across(
+        jnp.where(layer == 3, up_1, down_1),
+        [(0, 0), (0, 1), (0, 2), (0, 3), (1, 0), (1, 2)],
+    )
+    down_2, up_2, over_1, left_here = lax.optimization_barrier((down_2, up_2, over_1, left_here))
+
     down_3 = send(down_2, [(0, 1, 0), (1, 1, 0)])
+    over_2 = across(
+        jnp.where(layer < 2, down_2, jnp.where(layer == 2, up_1, up_2)),
+        [(0, 0), (0, 1), (0, 2), (0, 3), (1, 1), (1, 2), (1, 3)],
+    )
+    left_there = lax.ppermute(
+        left_here, everywhere, [(spot(x, t, t), spot(1 - x, t, t)) for x in planes for t in layers]
+    )
+    left_here = to_side(left_here)
+    down_3, over_2, left_there, left_here = lax.optimization_barrier(
+        (down_3, over_2, left_there, left_here)
+    )
+
+    over_3 = across(down_3, [(0, 0), (1, 0)])
+    left_there = to_core(to_side(left_there))
+    left_here = to_core(left_here)
 
     def by_layer(*options):
         chosen = options[3]
@@ -366,57 +599,13 @@
     own_1 = by_layer(down_1, own, up_1, up_2)
     own_2 = by_layer(down_2, down_1, own, up_1)
     own_3 = by_layer(down_3, down_2, down_1, own)
-    other_1 = swap(own_1, "shard", n_shard, 1)
-    other_2 = swap(own_2, "shard", n_shard, 1)
-    other_3 = swap(own_3, "shard", n_shard, 1)
-
-    everywhere = ("shard", "tensor", "section")
-
-    def place(x, z, s):
-        return (x * n_tensor + z) * n_section + s
-
-    planes = range(n_shard)
-    layers = range(n_tensor)
-
-    def scatter(value, source):
-        moved_here = lax.ppermute(
-            value,
-            everywhere,
-            [(place(x, source, s), place(x, s, s)) for x in planes for s in layers if s != source],
-        )
-        return jnp.where(layer == source, value, moved_here)
-
-    def across_shards(value):
-        return lax.ppermute(
-            value, everywhere, [(place(x, t, t), place(1 - x, t, t)) for x in planes for t in layers]
-        )
-
-    def hand_round(value):
-        across = lax.ppermute(
-            value, everywhere, [(place(x, t, t), place(x, t, t ^ 2)) for x in planes for t in layers]
-        )
-        value = jnp.where(section == layer, value, across)
-        near = lax.ppermute(
-            value,
-            everywhere,
-            [(place(x, t, t ^ a), place(x, t, t ^ a ^ 1)) for x in planes for t in layers for a in (0, 2)],
-        )
-        return jnp.where((section ^ layer) % 2 == 0, value, near)
-
-    left_here = scatter(own, 0)
-    left_there = across_shards(left_here)
-    left_own = hand_round(left_here)
-    left_other = hand_round(left_there)
+    other_1 = by_layer(over_1, over_0, over_2, over_2)
+    other_2 = by_layer(over_2, over_1, over_0, over_1)
+    other_3 = by_layer(over_3, over_2, over_1, over_0)
     precond_attn = attn_products(
-        shard, (left_own, left_other, own_1, own_2, own_3, other_1, other_2, other_3)
-    )
-
-    grad_all = lax.all_gather(router_grad, "shard", axis=1, tiled=True)
-    ids_all = lax.all_gather(token_ids, "shard", axis=0, tiled=True)
-    norm_values = norm_terms.astype(jnp.float32)
-    norm_total, norm_squares = lax.psum(
-        (jnp.sum(norm_values, axis=1), jnp.sum(norm_values * norm_values, axis=1)), "shard"
-    )
+        shard, (left_here, left_there, own_1, own_2, own_3, other_1, other_2, other_3)
+    )
+
     router_matrix = (
         factor_decay * old_router_factor
         + weight * jnp.einsum("en,fn->ef", grad_all, grad_all, preferred_element_type=jnp.float32)
@@ -428,19 +617,18 @@
     ).astype(jnp.bfloat16)
     precond_norms = (
         learning_rate
-        * norm_total
+        * norm_sums[0]
         / (
             factor_decay * old_norm_diag
-            + (1.0 - factor_decay) * (norm_squares / tokens_all)
+            + (1.0 - factor_decay) * (norm_sums[1] / tokens_all)
             + damping
         )
     )
     router_cols = learning_rate * jnp.einsum(
         "fn,cn->fc", router_right, own, preferred_element_type=jnp.float32
     )
-    router_swapped = swap(router_cols, "shard", n_shard, 1)
-    router_cols = jnp.where(shard == 1, router_cols, router_swapped)
-    precond_router = hand_round(scatter(router_cols, 2))
+    router_cols = jnp.where(shard == 1, router_cols, across(router_cols, [(1, 2)]))
+    precond_router = to_core(to_side(scatter(router_cols, 2)))
 
     vocab_block = old_embed_diag.shape[0]
     ids_here = layer * vocab_block + lax.iota(jnp.int32, vocab_block)

time: 288 us -> 267 us (0.927)
  blocking collectives: 41.3 us -> 0 us
  starting transfers between devices: 30.6 us -> 61.2 us
  Pallas kernels: 4.25 us -> 32.2 us
  matrix products: 27.1 us -> 4.03 us
  other arithmetic: 20.5 us -> 9.6 us
  waiting for transfers between devices: 129 us -> 126 us
    ppermute x9 -> x21, waiting for transfers between devices: 3.84 us -> 35.4 us  [the longest x5 25.8 us: across(): lax.ppermute(value, axes, [(x * n_tensor + z, (1 - x) * n_tensor + z) for...]
    ppermute x9 -> x21, starting transfers between devices: 14.6 us -> 45.1 us  [the longest x3 14.5 us: to_side(): lax.ppermute(value, everywhere, [(spot(x, t, t), spot(x, t, t ^ 2)) for x...]
    pallas_call x0 -> x7, Pallas kernels: none -> 27.9 us  [the longest x3 19.2 us: chain_call(): pl.pallas_call(kernel, in_specs=[pl.BlockSpec(memory_space=pltpu.SMEM)] *...]
    all_to_all x1 -> x0, blocking collectives: 25.4 us -> none  [layer_plan(): moved = lax.all_to_all(message, ('shard', 'tensor'), 0, 0, tiled=True)]
    dot_general x10 -> x0, matrix products: 23.1 us -> none  [the longest x4 10.7 us: layer_plan(): jnp.einsum('xrn,xcn->rc', part, own_features, preferred_element_type=jnp....]
    ppermute x5, waiting for transfers between devices: 36.3 us -> 17.2 us  [send(): lax.ppermute(value, axes, [(x * n_tensor + a, x * n_tensor + b) for x, a,...]
    ppermute x11 -> x13, waiting for transfers between devices: 77.3 us -> 60.5 us  [swap(): return lax.ppermute(value, axis, [(i, i ^ step) for i in range(size)])]
    all_gather x2 -> x0, blocking collectives: 8.59 us -> none  [the longest x1 4.34 us: layer_plan(): grad_all = lax.all_gather(router_grad, 'shard', axis=1, tiled=True)]
  transfers between devices with their start and end apart: 26 -> 40, of which waited for: 15 -> 14; matrix products, arithmetic and copies ran while one was open for 12% -> 9% of each run, Pallas kernels for 0% -> 3%
where the time goes in v3:
time: 267 us
  waiting for transfers between devices  126 us (47%)
  starting transfers between devices  61.2 us (23%)
  Pallas kernels  32.2 us (12%)
  local copies, waits for them, and re-layouts  17.2 us (6%)
  between operations  16.2 us (6%)
  other arithmetic  9.6 us (4%)
  matrix products  4.03 us (2%)
    ppermute x13, waiting for transfers between devices, swap(): return lax.ppermute(value, axis, [(i, i ^ step) for i in range(size)])  60.5 us
    ppermute x5, waiting for transfers between devices, across(): lax.ppermute(value, axes, [(x * n_tensor + z, (1 - x) * n_tensor + z) for...  25.8 us
    pallas_call x3, Pallas kernels, chain_call(): pl.pallas_call(kernel, in_specs=[pl.BlockSpec(memory_space=pltpu.SMEM)] *...  19.2 us
    ppermute x5, waiting for transfers between devices, send(): lax.ppermute(value, axes, [(x * n_tensor + a, x * n_tensor + b) for x, a,...  17.2 us
    ppermute x3, starting transfers between devices, to_side(): lax.ppermute(value, everywhere, [(spot(x, t, t), spot(x, t, t ^ 2)) for x...  14.5 us
    ppermute x7, starting transfers between devices, layer_plan(): message = lax.ppermute(message, axes, moves)  13.1 us
    all_gather x1, waiting for transfers between devices, layer_plan(): gathered = lax.all_gather(collected, 'section', axis=0)  12.9 us
    ppermute x13, starting transfers between devices, swap(): return lax.ppermute(value, axis, [(i, i ^ step) for i in range(size)])  10.8 us
  transfers between devices with their start and end apart: 40, of which 14 were waited for; matrix products, arithmetic and copies ran while one was open for 9% of the time, Pallas kernels for 3%

profile of v3, /device:TPU:0, one launch (start us, length us, event | category | flops | bytes accessed | tf_op | source)
XLA Modules:
  0.0 266.5 jit_solution(18008750536726085632)
XLA Ops:
  8.5 5.0 %collective-permute-start.4 = (bf16[144,256]{1,0:T(8,128)(2,1)S(1)}, bf16[144,256]{1,0:T(8,128)(2,1)S(1)}, u32[]{:S(2)}, u32[]{:S(2)}) collective-permute-start(bf16[144,256]{1,0:T(8,128)(2,1)S(1)} %get-tuple-element.69), channel_id=1, source_target_pairs={{0,24},{4,28},{8,16},{12,20},{16,8},{20,12},{24,0},{28,4},{1,25},{... | collective-permute-start | bytes 221192 | tf_op jit(solution)/shard_map/ppermute | solution.py:429
  34.8 4.4 %fusion.14 = (bf16[576,576]{1,0:T(8,128)(2,1)}, bf16[576,576]{1,0:T(8,128)(2,1)}, bf16[576,576]{1,0:T(8,128)(2,1)}, bf16[576,576]{1,0:T(8,128)(2,1)}) fusion(f32[4,576,576]{2,1,0:T(8,128)} %param.12, s32[]{:T(128)S(6)} %select_n.255, s32[]{:T(128)S(6)} %select_n.249, s32[]{:T(128)S(6)} %select_n.247, s32[]{:T(128)S(6)} %select_n.252), kind=kLoop, calls=%fused_computation.25 | loop fusion | bytes 5308432 | tf_op jit(solution)/shard_map/convert_element_type | solution.py:449
  39.2 3.0 %collective-permute-start.12 = (bf16[576,576]{1,0:T(8,128)(2,1)}, bf16[576,576]{1,0:T(8,128)(2,1)}, u32[]{:S(2)}, u32[]{:S(2)}) collective-permute-start(bf16[576,576]{1,0:T(8,128)(2,1)} %get-tuple-element.58), channel_id=1, source_target_pairs={{0,12},{4,8},{8,4},{12,0},{1,13},{5,9},{9,5},{13,1},{2,14},{6,10},... | collective-permute-start | bytes 1990664 | tf_op jit(solution)/shard_map/ppermute | solution.py:169
  43.6 12.9 %all-gather.3.cloned.1.call-done = bf16[16,304,256]{2,1,0:T(8,128)(2,1)} async-done(((bf16[4,304,256]{2,1,0:T(8,128)(2,1)}), bf16[16,304,256]{2,1,0:T(8,128)(2,1)}) %all-gather.3.cloned.1.call-update) | async-done | bytes 2490384 | tf_op jit(solution)/shard_map/all_gather | solution.py:444
  66.4 9.0 %collective-permute-done.10.old = bf16[576,576]{1,0:T(8,128)(2,1)} collective-permute-done((bf16[576,576]{1,0:T(8,128)(2,1)}, bf16[576,576]{1,0:T(8,128)(2,1)}, u32[]{:S(2)}, u32[]{:S(2)}) %collective-permute-start.10) | collective-permute-done | bytes 663584 | tf_op jit(solution)/shard_map/ppermute | solution.py:169
  75.4 2.7 %shard_map.112.refs_1_ = bf16[576,576]{1,0:T(8,128)(2,1)} custom-call(s32[1]{0:T(128)} %bitcast.1.place_ref, bf16[2,2304,256]{2,1,0:T(8,128)(2,1)S(1)} %bitcast.106, bf16[2,2304,256]{2,1,0:T(8,128)(2,1)S(1)} %bitcast.107, bf16[576,576]{1,0:T(8,128)(2,1)} %collective-permute-done.10.old, f32[4,1,576]{2,1,0:T(1,128)S(1)} %add_reduce-precision_fusion.diag), custom_call_target="tpu_custom_call" | custom-call | flops 339738624 | bytes 2506752 | tf_op jit(solution)/shard_map/pallas_call | solution.py:207
  78.1 23.8 %collective-permute-done.11.old = bf16[576,576]{1,0:T(8,128)(2,1)} collective-permute-done((bf16[576,576]{1,0:T(8,128)(2,1)}, bf16[576,576]{1,0:T(8,128)(2,1)}, u32[]{:S(2)}, u32[]{:S(2)}) %collective-permute-start.11) | collective-permute-done | bytes 663584 | tf_op jit(solution)/shard_map/ppermute | solution.py:169
  101.9 2.7 %shard_map.113.refs_2_ = bf16[576,576]{1,0:T(8,128)(2,1)} custom-call(s32[1]{0:T(128)} %bitcast.1.place_ref, bf16[2,2304,256]{2,1,0:T(8,128)(2,1)S(1)} %bitcast.108, bf16[2,2304,256]{2,1,0:T(8,128)(2,1)S(1)} %bitcast.109, bf16[576,576]{1,0:T(8,128)(2,1)} %collective-permute-done.11.old, f32[4,1,576]{2,1,0:T(1,128)S(1)} %add_reduce-precision_fusion.diag), custom_call_target="tpu_custom_call" | custom-call | flops 339738624 | bytes 2506752 | tf_op jit(solution)/shard_map/pallas_call | solution.py:207
  110.1 6.1 %shard_map.115 = (f32[2,256,576]{2,1,0:T(8,128)S(1)}, f32[2,256,576]{2,1,0:T(8,128)S(1)}, bf16[256,1152]{1,0:T(8,128)(2,1)S(1)}) custom-call(s32[1]{0:T(128)} %bitcast.1.place_ref, f32[1]{0:T(128)} %bitcast.36.scale_ref, bf16[4,256,576]{2,1,0:T(8,128)(2,1)S(1)} %bitcast.111, f32[4,1,576]{2,1,0:T(1,128)S(1)} %add_reduce-precision_fusion.diag, ...), custom_call_target="tpu_custom_call" | custom-call | flops 3057647616 | bytes 5308416 | tf_op jit(solution)/shard_map/pallas_call | solution.py:318
  117.8 14.2 %collective-permute-done.17.theirs = bf16[256,1152]{1,0:T(8,128)(2,1)S(1)} collective-permute-done((bf16[256,1152]{1,0:T(8,128)(2,1)S(1)}, bf16[256,1152]{1,0:T(8,128)(2,1)S(1)}, u32[]{:S(2)}, u32[]{:S(2)}) %collective-permute-start.17) | collective-permute-done | bytes 589856 | tf_op jit(solution)/shard_map/ppermute | solution.py:169
  132.1 5.9 %shard_map.116 = (f32[2,256,576]{2,1,0:T(8,128)S(1)}, bf16[256,1152]{1,0:T(8,128)(2,1)S(1)}) custom-call(s32[1]{0:T(128)} %bitcast.1.place_ref, bf16[256,1152]{1,0:T(8,128)(2,1)S(1)} %get-tuple-element.27.mine, bf16[256,1152]{1,0:T(8,128)(2,1)S(1)} %collective-permute-done.17.theirs, f32[2,256,576]{2,1,0:T(8,128)S(1)} %get-tuple-element.28.step_one, ...), custom_call_target="tpu_custom_call" | custom-call | flops 1358954496 | bytes 5308416 | tf_op jit(solution)/shard_map/pallas_call | solution.py:318
  140.6 13.5 %collective-permute-done.18.theirs = bf16[256,1152]{1,0:T(8,128)(2,1)} collective-permute-done((bf16[256,1152]{1,0:T(8,128)(2,1)S(1)}, bf16[256,1152]{1,0:T(8,128)(2,1)}, u32[]{:S(2)}, u32[]{:S(2)}) %collective-permute-start.18) | collective-permute-done | bytes 589856 | tf_op jit(solution)/shard_map/ppermute | solution.py:169
  155.4 7.2 %shard_map.117 = (bf16[576,256]{1,0:T(8,128)(2,1)S(1)}, bf16[576,256]{1,0:T(8,128)(2,1)S(1)}) custom-call(s32[1]{0:T(128)} %bitcast.1.place_ref, f32[1]{0:T(128)} %bitcast.36.scale_ref, bf16[256,1152]{1,0:T(8,128)(2,1)S(1)} %get-tuple-element.29.mine, bf16[256,1152]{1,0:T(8,128)(2,1)} %collective-permute-done.18.theirs, f32[2,256,576]{2,1,0:T(8,128)S(1)} %copy-done.2, ...), custom_call_target="tpu_custom_call" | custom-call | flops 1358954496 | bytes 5308416 | tf_op jit(solution)/shard_map/pallas_call | solution.py:318
  171.8 13.9 %collective-permute-done.20 = bf16[576,512]{1,0:T(8,128)(2,1)S(1)} collective-permute-done((bf16[576,512]{1,0:T(8,128)(2,1)S(1)}, bf16[576,512]{1,0:T(8,128)(2,1)S(1)}, u32[]{:S(2)}, u32[]{:S(2)}) %collective-permute-start.20) | collective-permute-done | bytes 589856 | tf_op jit(solution)/shard_map/ppermute | solution.py:521
  189.7 3.4 %collective-permute-start.37 = (f32[8,576]{1,0:T(8,128)S(1)}, f32[8,576]{1,0:T(8,128)S(1)}, u32[]{:S(2)}, u32[]{:S(2)}) collective-permute-start(f32[8,576]{1,0:T(8,128)S(1)} %broadcast_select_fusion.9), channel_id=1, source_target_pairs={{0,2},{5,7},{10,8},{15,13},{16,18},{21,23},{26,24},{31,29}} | collective-permute-start | bytes 55304 | tf_op jit(solution)/shard_map/ppermute | solution.py:549
  193.3 11.0 %collective-permute-done.25 = bf16[576,512]{1,0:T(8,128)(2,1)S(1)} collective-permute-done((bf16[576,512]{1,0:T(8,128)(2,1)S(1)}, bf16[576,512]{1,0:T(8,128)(2,1)S(1)}, u32[]{:S(2)}, u32[]{:S(2)}) %collective-permute-start.25) | collective-permute-done | bytes 589856 | tf_op jit(solution)/shard_map/ppermute | solution.py:526
  204.3 9.7 %collective-permute-start.30 = (bf16[576,512]{1,0:T(8,128)(2,1)S(1)}, bf16[576,512]{1,0:T(8,128)(2,1)S(1)}, u32[]{:S(2)}, u32[]{:S(2)}) collective-permute-start(bf16[576,512]{1,0:T(8,128)(2,1)S(1)} %broadcast_select_fusion.4), channel_id=1, source_target_pairs={{0,2},{5,7},{10,8},{15,13},{16,18},{21,23},{26,24},{31,29}} | collective-permute-start | bytes 1769480 | tf_op jit(solution)/shard_map/ppermute | solution.py:549
  217.4 4.0 %collective-permute-start.28 = (bf16[576,512]{1,0:T(8,128)(2,1)S(1)}, bf16[576,512]{1,0:T(8,128)(2,1)S(1)}, u32[]{:S(2)}, u32[]{:S(2)}) collective-permute-start(bf16[576,512]{1,0:T(8,128)(2,1)S(1)} %broadcast_select_fusion.3), channel_id=1, source_target_pairs={{0,16},{4,20},{8,24},{12,28},{20,4},{24,8},{28,12},{1,17},{5,21},{... | collective-permute-start | bytes 1769480 | tf_op jit(solution)/shard_map/ppermute | solution.py:526
  223.6 6.1 %collective-permute-done.28 = bf16[576,512]{1,0:T(8,128)(2,1)S(1)} collective-permute-done((bf16[576,512]{1,0:T(8,128)(2,1)S(1)}, bf16[576,512]{1,0:T(8,128)(2,1)S(1)}, u32[]{:S(2)}, u32[]{:S(2)}) %collective-permute-start.28) | collective-permute-done | bytes 589856 | tf_op jit(solution)/shard_map/ppermute | solution.py:526
  229.6 3.3 %collective-permute-done.27 = bf16[576,512]{1,0:T(8,128)(2,1)S(1)} collective-permute-done((bf16[576,512]{1,0:T(8,128)(2,1)S(1)}, bf16[576,512]{1,0:T(8,128)(2,1)S(1)}, u32[]{:S(2)}, u32[]{:S(2)}) %collective-permute-start.27) | collective-permute-done | bytes 589856 | tf_op jit(solution)/shard_map/ppermute | solution.py:521
  238.7 2.9 %collective-permute-done.32 = bf16[576,512]{1,0:T(8,128)(2,1)S(1)} collective-permute-done((bf16[576,512]{1,0:T(8,128)(2,1)S(1)}, bf16[576,512]{1,0:T(8,128)(2,1)S(1)}, u32[]{:S(2)}, u32[]{:S(2)}) %collective-permute-start.32) | collective-permute-done | bytes 589856 | tf_op jit(solution)/shard_map/ppermute | solution.py:549
  243.0 8.7 %collective-permute-done.34 = bf16[576,512]{1,0:T(8,128)(2,1)S(1)} collective-permute-done((bf16[576,512]{1,0:T(8,128)(2,1)S(1)}, bf16[576,512]{1,0:T(8,128)(2,1)S(1)}, u32[]{:S(2)}, u32[]{:S(2)}) %collective-permute-start.34) | collective-permute-done | bytes 589856 | tf_op jit(solution)/shard_map/ppermute | solution.py:526
  252.0 3.3 %fusion.3 = f32[2048,576]{0,1:T(8,128)} fusion(f32[2048]{0:T(1024)S(1)} %add_divide_fusion, s32[512]{0:T(512)S(1)} %add_select_fusion, s32[2048]{0:T(1024)S(1)} %iota_add_fusion, bf16[576,512]{1,0:T(8,128)(2,1)S(1)} %get-tuple-element.65.own_3, bf16[576,512]{1,0:T(8,128)(2,1)S(1)} %get-tuple-element.62.other_3, pred[]{:T(512)S(6)} %eq.112), kind=kOutput, calls=%fused_computation.6 | convolution fusion | flops 1210482688 | bytes 5916673 | tf_op jit(solution)/shard_map/vn,cn->vc/dot_general | solution.py:639
  255.4 4.3 %shard_map.118 = f32[4,576,576]{2,1,0:T(8,128)} custom-call(s32[1]{0:T(128)} %bitcast.shard_ref, bf16[576,512]{1,0:T(8,128)(2,1)S(1)} %broadcast_select_fusion.7.left_own, bf16[576,512]{1,0:T(8,128)(2,1)S(1)} %broadcast_select_fusion.6.left_other, bf16[576,512]{1,0:T(8,128)(2,1)S(1)} %get-tuple-element.67.own_1, ...), custom_call_target="tpu_custom_call" | custom-call | flops 1358954496 | bytes 10027008 | tf_op jit(solution)/shard_map/pallas_call | solution.py:368
  (164 shorter events, 69.2 us)
Async XLA Ops:
  7.2 49.4 %all-gather.3.cloned.1.call-start = ((), (), s32[]{:S(2)}) async-start(), calls=%async_computation | async-start | bytes 3112960 | tf_op jit(solution)/shard_map/all_gather | solution.py:444
  8.5 22.4 %collective-permute-start.4 = (bf16[144,256]{1,0:T(8,128)(2,1)S(1)}, bf16[144,256]{1,0:T(8,128)(2,1)S(1)}, u32[]{:S(2)}, u32[]{:S(2)}) collective-permute-start(bf16[144,256]{1,0:T(8,128)(2,1)S(1)} %get-tuple-element.69), channel_id=1, source_target_pairs={{0,24},{4,28},{8,16},{12,20},{16,8},{20,12},{24,0},{28,4},{1,25},{... | collective-permute-start | bytes 221192 | tf_op jit(solution)/shard_map/ppermute | solution.py:429
  14.0 14.4 %collective-permute-start.6 = (bf16[144,256]{1,0:T(8,128)(2,1)S(1)}, bf16[144,256]{1,0:T(8,128)(2,1)S(1)}, u32[]{:S(2)}, u32[]{:S(2)}) collective-permute-start(bf16[144,256]{1,0:T(8,128)(2,1)S(1)} %get-tuple-element.74), channel_id=1, source_target_pairs={{0,28},{4,24},{8,20},{12,16},{16,12},{20,8},{24,4},{28,0},{1,29},{... | collective-permute-start | bytes 221192 | tf_op jit(solution)/shard_map/ppermute | solution.py:429
  39.2 24.3 %collective-permute-start.12 = (bf16[576,576]{1,0:T(8,128)(2,1)}, bf16[576,576]{1,0:T(8,128)(2,1)}, u32[]{:S(2)}, u32[]{:S(2)}) collective-permute-start(bf16[576,576]{1,0:T(8,128)(2,1)} %get-tuple-element.58), channel_id=1, source_target_pairs={{0,12},{4,8},{8,4},{12,0},{1,13},{5,9},{9,5},{13,1},{2,14},{6,10},... | collective-permute-start | bytes 1990664 | tf_op jit(solution)/shard_map/ppermute | solution.py:169
  42.2 33.2 %collective-permute-start.10 = (bf16[576,576]{1,0:T(8,128)(2,1)}, bf16[576,576]{1,0:T(8,128)(2,1)}, u32[]{:S(2)}, u32[]{:S(2)}) collective-permute-start(bf16[576,576]{1,0:T(8,128)(2,1)} %get-tuple-element.59), channel_id=1, source_target_pairs={{0,4},{4,0},{8,12},{12,8},{1,5},{5,1},{9,13},{13,9},{2,6},{6,2},{1... | collective-permute-start | bytes 1990664 | tf_op jit(solution)/shard_map/ppermute | solution.py:169
  42.5 59.3 %collective-permute-start.11 = (bf16[576,576]{1,0:T(8,128)(2,1)}, bf16[576,576]{1,0:T(8,128)(2,1)}, u32[]{:S(2)}, u32[]{:S(2)}) collective-permute-start(bf16[576,576]{1,0:T(8,128)(2,1)} %get-tuple-element.61), channel_id=1, source_target_pairs={{0,8},{4,12},{8,0},{12,4},{1,9},{5,13},{9,1},{13,5},{2,10},{6,14},... | collective-permute-start | bytes 1990664 | tf_op jit(solution)/shard_map/ppermute | solution.py:169
  63.1 45.6 %collective-permute-start.13 = (bf16[576,576]{1,0:T(8,128)(2,1)S(1)}, bf16[576,576]{1,0:T(8,128)(2,1)}, u32[]{:S(2)}, u32[]{:S(2)}) collective-permute-start(bf16[576,576]{1,0:T(8,128)(2,1)S(1)} %shard_map.111.refs_0_), channel_id=1, source_target_pairs={{0,1},{1,0},{2,3},{3,2},{4,5},{5,4},{6,7},{7,6},{8,9},{9,8},{10,11... | collective-permute-start | bytes 1990664 | tf_op jit(solution)/shard_map/ppermute | solution.py:169
  66.1 42.6 %collective-permute-start.16 = (bf16[576,576]{1,0:T(8,128)(2,1)}, bf16[576,576]{1,0:T(8,128)(2,1)}, u32[]{:S(2)}, u32[]{:S(2)}) collective-permute-start(bf16[576,576]{1,0:T(8,128)(2,1)} %shard_map.114.refs_3_), channel_id=1, source_target_pairs={{0,1},{1,0},{2,3},{3,2},{4,5},{5,4},{6,7},{7,6},{8,9},{9,8},{10,11... | collective-permute-start | bytes 1990664 | tf_op jit(solution)/shard_map/ppermute | solution.py:169
  78.1 30.7 %collective-permute-start.14 = (bf16[576,576]{1,0:T(8,128)(2,1)}, bf16[576,576]{1,0:T(8,128)(2,1)}, u32[]{:S(2)}, u32[]{:S(2)}) collective-permute-start(bf16[576,576]{1,0:T(8,128)(2,1)} %shard_map.112.refs_1_), channel_id=1, source_target_pairs={{0,1},{1,0},{2,3},{3,2},{4,5},{5,4},{6,7},{7,6},{8,9},{9,8},{10,11... | collective-permute-start | bytes 1990664 | tf_op jit(solution)/shard_map/ppermute | solution.py:169
  116.3 15.8 %collective-permute-start.17 = (bf16[256,1152]{1,0:T(8,128)(2,1)S(1)}, bf16[256,1152]{1,0:T(8,128)(2,1)S(1)}, u32[]{:S(2)}, u32[]{:S(2)}) collective-permute-start(bf16[256,1152]{1,0:T(8,128)(2,1)S(1)} %get-tuple-element.27.mine), channel_id=1, source_target_pairs={{0,2},{1,3},{2,0},{3,1},{4,6},{5,7},{6,4},{7,5},{8,10},{9,11},{10,... | collective-permute-start | bytes 1769480 | tf_op jit(solution)/shard_map/ppermute | solution.py:169
  139.0 15.1 %collective-permute-start.18 = (bf16[256,1152]{1,0:T(8,128)(2,1)S(1)}, bf16[256,1152]{1,0:T(8,128)(2,1)}, u32[]{:S(2)}, u32[]{:S(2)}) collective-permute-start(bf16[256,1152]{1,0:T(8,128)(2,1)S(1)} %get-tuple-element.29.mine), channel_id=1, source_target_pairs={{0,2},{1,3},{2,0},{3,1},{4,6},{5,7},{6,4},{7,5},{8,10},{9,11},{10,... | collective-permute-start | bytes 1769480 | tf_op jit(solution)/shard_map/ppermute | solution.py:169
  166.6 19.1 %collective-permute-start.20 = (bf16[576,512]{1,0:T(8,128)(2,1)S(1)}, bf16[576,512]{1,0:T(8,128)(2,1)S(1)}, u32[]{:S(2)}, u32[]{:S(2)}) collective-permute-start(bf16[576,512]{1,0:T(8,128)(2,1)S(1)} %maximum_select_fusion), channel_id=1, source_target_pairs={{12,8},{8,4},{4,0},{28,24},{20,16},{13,9},{9,5},{5,1},{29,25},{21,... | collective-permute-start | bytes 1769480 | tf_op jit(solution)/shard_map/ppermute | solution.py:521
  169.7 23.4 %collective-permute-start.26 = (bf16[576,512]{1,0:T(8,128)(2,1)S(1)}, bf16[576,512]{1,0:T(8,128)(2,1)S(1)}, u32[]{:S(2)}, u32[]{:S(2)}) collective-permute-start(bf16[576,512]{1,0:T(8,128)(2,1)S(1)} %maximum_select_fusion), channel_id=1, source_target_pairs={{1,5},{2,10},{3,15},{17,21},{18,26},{19,31}} | collective-permute-start | bytes 1769480 | tf_op jit(solution)/shard_map/ppermute | solution.py:541
  170.5 19.2 %collective-permute-start.36 = (f32[8,576]{1,0:T(8,128)S(1)}, f32[8,576]{1,0:T(8,128)S(1)}, u32[]{:S(2)}, u32[]{:S(2)}) collective-permute-start(f32[8,576]{1,0:T(8,128)S(1)} %broadcast_select_fusion.8), channel_id=1, source_target_pairs={{8,0},{9,5},{11,15},{24,16},{25,21},{27,31}} | collective-permute-start | bytes 55304 | tf_op jit(solution)/shard_map/ppermute | solution.py:541
  185.7 18.6 %collective-permute-start.23 = (bf16[576,512]{1,0:T(8,128)(2,1)S(1)}, bf16[576,512]{1,0:T(8,128)(2,1)S(1)}, u32[]{:S(2)}, u32[]{:S(2)}) collective-permute-start(bf16[576,512]{1,0:T(8,128)(2,1)S(1)} %collective-permute-done.20), channel_id=1, source_target_pairs={{8,4},{4,0},{24,20},{9,5},{5,1},{25,21},{10,6},{6,2},{26,22},{11,7... | collective-permute-start | bytes 1769480 | tf_op jit(solution)/shard_map/ppermute | solution.py:521
  187.0 17.3 %collective-permute-start.24 = (bf16[576,512]{1,0:T(8,128)(2,1)S(1)}, bf16[576,512]{1,0:T(8,128)(2,1)S(1)}, u32[]{:S(2)}, u32[]{:S(2)}) collective-permute-start(bf16[576,512]{1,0:T(8,128)(2,1)S(1)} %collective-permute-done.21), channel_id=1, source_target_pairs={{8,12},{24,28},{9,13},{25,29},{10,14},{26,30},{11,15},{27,31}} | collective-permute-start | bytes 1769480 | tf_op jit(solution)/shard_map/ppermute | solution.py:521
  187.7 16.5 %collective-permute-start.25 = (bf16[576,512]{1,0:T(8,128)(2,1)S(1)}, bf16[576,512]{1,0:T(8,128)(2,1)S(1)}, u32[]{:S(2)}, u32[]{:S(2)}) collective-permute-start(bf16[576,512]{1,0:T(8,128)(2,1)S(1)} %broadcast_select_fusion.5), channel_id=1, source_target_pairs={{0,16},{4,20},{8,24},{12,28},{16,0},{24,8},{1,17},{5,21},{9,25},{1... | collective-permute-start | bytes 1769480 | tf_op jit(solution)/shard_map/ppermute | solution.py:526
  189.7 32.2 %collective-permute-start.37 = (f32[8,576]{1,0:T(8,128)S(1)}, f32[8,576]{1,0:T(8,128)S(1)}, u32[]{:S(2)}, u32[]{:S(2)}) collective-permute-start(f32[8,576]{1,0:T(8,128)S(1)} %broadcast_select_fusion.9), channel_id=1, source_target_pairs={{0,2},{5,7},{10,8},{15,13},{16,18},{21,23},{26,24},{31,29}} | collective-permute-start | bytes 55304 | tf_op jit(solution)/shard_map/ppermute | solution.py:549
  204.3 19.2 %collective-permute-start.30 = (bf16[576,512]{1,0:T(8,128)(2,1)S(1)}, bf16[576,512]{1,0:T(8,128)(2,1)S(1)}, u32[]{:S(2)}, u32[]{:S(2)}) collective-permute-start(bf16[576,512]{1,0:T(8,128)(2,1)S(1)} %broadcast_select_fusion.4), channel_id=1, source_target_pairs={{0,2},{5,7},{10,8},{15,13},{16,18},{21,23},{26,24},{31,29}} | collective-permute-start | bytes 1769480 | tf_op jit(solution)/shard_map/ppermute | solution.py:549
  214.0 19.0 %collective-permute-start.29 = (bf16[576,512]{1,0:T(8,128)(2,1)S(1)}, bf16[576,512]{1,0:T(8,128)(2,1)S(1)}, u32[]{:S(2)}, u32[]{:S(2)}) collective-permute-start(bf16[576,512]{1,0:T(8,128)(2,1)S(1)} %broadcast_select_fusion.4), channel_id=1, source_target_pairs={{0,16},{5,21},{10,26},{15,31},{16,0},{21,5},{26,10},{31,15}} | collective-permute-start | bytes 1769480 | tf_op jit(solution)/shard_map/ppermute | solution.py:581
  215.9 17.0 %collective-permute-start.27 = (bf16[576,512]{1,0:T(8,128)(2,1)S(1)}, bf16[576,512]{1,0:T(8,128)(2,1)S(1)}, u32[]{:S(2)}, u32[]{:S(2)}) collective-permute-start(bf16[576,512]{1,0:T(8,128)(2,1)S(1)} %collective-permute-done.23), channel_id=1, source_target_pairs={{4,0},{20,16},{5,1},{21,17},{6,2},{22,18},{7,3},{23,19}} | collective-permute-start | bytes 1769480 | tf_op jit(solution)/shard_map/ppermute | solution.py:521
  234.9 17.0 %collective-permute-start.31 = (bf16[576,512]{1,0:T(8,128)(2,1)S(1)}, bf16[576,512]{1,0:T(8,128)(2,1)S(1)}, u32[]{:S(2)}, u32[]{:S(2)}) collective-permute-start(bf16[576,512]{1,0:T(8,128)(2,1)S(1)} %broadcast_select_fusion.1), channel_id=1, source_target_pairs={{0,1},{2,3},{5,4},{7,6},{10,11},{8,9},{15,14},{13,12},{16,17},{18,... | collective-permute-start | bytes 1769480 | tf_op jit(solution)/shard_map/ppermute | solution.py:555
  236.2 15.5 %collective-permute-start.34 = (bf16[576,512]{1,0:T(8,128)(2,1)S(1)}, bf16[576,512]{1,0:T(8,128)(2,1)S(1)}, u32[]{:S(2)}, u32[]{:S(2)}) collective-permute-start(bf16[576,512]{1,0:T(8,128)(2,1)S(1)} %collective-permute-done.27), channel_id=1, source_target_pairs={{0,16},{16,0},{1,17},{17,1},{2,18},{18,2},{3,19},{19,3}} | collective-permute-start | bytes 1769480 | tf_op jit(solution)/shard_map/ppermute | solution.py:526
  241.7 13.6 %collective-permute-start.33 = (bf16[576,512]{1,0:T(8,128)(2,1)S(1)}, bf16[576,512]{1,0:T(8,128)(2,1)S(1)}, u32[]{:S(2)}, u32[]{:S(2)}) collective-permute-start(bf16[576,512]{1,0:T(8,128)(2,1)S(1)} %broadcast_select_fusion), channel_id=1, source_target_pairs={{0,1},{2,3},{5,4},{7,6},{10,11},{8,9},{15,14},{13,12},{16,17},{18,... | collective-permute-start | bytes 1769480 | tf_op jit(solution)/shard_map/ppermute | solution.py:555
  (26 other events, 234.8 us)
Sparse Core Ops, SparseCore 0:
  32.0 24.5 all-gather.2

commit v4 on v3

--- a/solution.py
+++ b/solution.py
@@ -227,94 +227,90 @@
     )(place, features, features, old, diag)
 
 
-def fetch_blocks(blocks, held, sems):
-    copies = [
-        pltpu.make_async_copy(blocks[index], held.at[index], sems.at[index])
-        for index in range(len(blocks))
-    ]
+def fetch_blocks(place_ref, blocks, held, sems):
+    count = len(blocks) // 2
+    depth = blocks[0].shape[0]
+    copies = []
+    for index in range(2 * count):
+        slot = pl.multiple_of((place_ref[0] ^ (index % count)) * depth, depth)
+        copies.append(
+            pltpu.make_async_copy(
+                blocks[index], held.at[index // count, pl.ds(slot, depth)], sems.at[index]
+            )
+        )
     for copy in copies:
         copy.start()
     return copies
 
 
-def block_products(pieces, count, copies, held):
-    own = other = None
-    for step in range(count):
-        piece = pieces(step)
-        copies[step].wait()
-        term = jnp.dot(piece, held[step], preferred_element_type=jnp.float32)
-        own = term if own is None else own + term
-        copies[count + step].wait()
-        term = jnp.dot(piece, held[count + step], preferred_element_type=jnp.float32)
-        other = term if other is None else other + term
-    return own, other
+def block_products(rows, copies, held):
+    count = len(copies) // 2
+    products = []
+    for index in range(2):
+        for copy in copies[index * count : (index + 1) * count]:
+            copy.wait()
+        products.append(jnp.dot(rows, held[index], preferred_element_type=jnp.float32))
+    return products
+
+
+def first_parts(place_ref, scale, rows, diag, product, index):
+    width = product.shape[1]
+    square = scale * scale
+    values = rows[:, index * width : (index + 1) * width].astype(jnp.float32)
+    low_diag = diag[place_ref[0] ^ index]
+    first_diag = rounded(2.0 * scale - square * low_diag)
+    by_first = 2.0 * scale * values - square * product
+    step_one = first_diag * values - square * (product - low_diag * values)
+    return by_first, step_one, low_diag, first_diag
 
 
 def first_kernel(place_ref, scale_ref, rows, diag, *refs):
-    blocks, (by_first, step_one, message), (held, sems) = refs[:8], refs[8:11], refs[11:]
-    copies = fetch_blocks(blocks, held, sems)
-    products = block_products(lambda step: rows[step], 4, copies, held)
-    scale = scale_ref[0]
-    square = scale * scale
+    blocks, (kept, message), (held, sems) = refs[:8], refs[8:10], refs[10:]
+    copies = fetch_blocks(place_ref, blocks, held, sems)
+    products = block_products(rows[...], copies, held)
     lows = []
     for index in range(2):
-        values = rows[place_ref[0] ^ index].astype(jnp.float32)
-        low_diag = diag[place_ref[0] ^ index]
-        first_diag = rounded(2.0 * scale - square * low_diag)
-        by_first[index] = 2.0 * scale * values - square * products[index]
-        one = first_diag * values - square * (products[index] - low_diag * values)
-        step_one[index] = one
-        lows.append(one.astype(jnp.bfloat16))
+        kept[index] = products[index]
+        parts = first_parts(place_ref, scale_ref[0], rows, diag, products[index], index)
+        lows.append(parts[1].astype(jnp.bfloat16))
     message[...] = jnp.concatenate(lows, axis=1)
 
 
-def put_pieces(pieces, mine, theirs):
-    width = pieces.shape[2]
-    for index in range(2):
-        pieces[index] = mine[:, index * width : (index + 1) * width]
-        pieces[2 + index] = theirs[:, index * width : (index + 1) * width]
-
-
-def second_kernel(place_ref, mine, theirs, step_one, diag, *refs):
-    blocks, (step_two, message), (held, sems, pieces) = refs[:8], refs[8:10], refs[10:]
-    copies = fetch_blocks(blocks, held, sems)
-    put_pieces(pieces, mine, theirs)
-    products = block_products(lambda step: pieces[place_ref[0] ^ step], 4, copies, held)
+def second_kernel(place_ref, scale_ref, mine, theirs, rows, diag, before, *refs):
+    blocks, (kept, message), (held, sems) = refs[:8], refs[8:10], refs[10:]
+    copies = fetch_blocks(place_ref, blocks, held, sems)
+    both = jnp.concatenate([mine[...], theirs[...]], axis=1)
+    products = block_products(both, copies, held)
+    square = scale_ref[0] * scale_ref[0]
     lows = []
     for index in range(2):
-        low_diag = diag[place_ref[0] ^ index]
-        one = step_one[index]
+        by_first, one, low_diag, first_diag = first_parts(
+            place_ref, scale_ref[0], rows, diag, before[index], index
+        )
         two = products[index] + low_diag * (one - rounded(one))
-        step_two[index] = two
-        lows.append(two.astype(jnp.bfloat16))
+        low = two.astype(jnp.bfloat16)
+        kept[index] = (
+            2.0 * by_first - first_diag * two - square * low_diag * low.astype(jnp.float32)
+        )
+        lows.append(low)
     message[...] = jnp.concatenate(lows, axis=1)
 
 
-def third_kernel(place_ref, scale_ref, mine, theirs, step_two, by_first, diag, *refs):
-    blocks, (keep, give), (held, sems, pieces) = refs[:8], refs[8:10], refs[10:]
-    copies = fetch_blocks(blocks, held, sems)
-    put_pieces(pieces, mine, theirs)
-    products = block_products(lambda step: pieces[place_ref[0] ^ step], 4, copies, held)
-    scale = scale_ref[0]
-    square = scale * scale
+def third_kernel(place_ref, scale_ref, mine, theirs, before, *refs):
+    blocks, (keep, give), (held, sems) = refs[:8], refs[8:10], refs[10:]
+    copies = fetch_blocks(place_ref, blocks, held, sems)
+    both = jnp.concatenate([mine[...], theirs[...]], axis=1)
+    products = block_products(both, copies, held)
+    square = scale_ref[0] * scale_ref[0]
     for index, out in ((0, keep), (1, give)):
-        low_diag = diag[place_ref[0] ^ index]
-        first_diag = rounded(2.0 * scale - square * low_diag)
-        two = step_two[index]
-        three = first_diag * two - square * (products[index] - low_diag * rounded(two))
-        out[...] = (2.0 * by_first[index] - three).T.astype(jnp.bfloat16)
-
-
-def chain_call(kernel, scalars, arrays, blocks, out_shape, pieces):
-    tokens = out_shape[0].shape[-1] if pieces is None else pieces[1]
-    width = blocks[0].shape[1]
+        out[...] = (before[index] + square * products[index]).T.astype(jnp.bfloat16)
+
+
+def chain_call(kernel, scalars, arrays, blocks, out_shape):
+    depth, width = blocks[0].shape
+    count = len(blocks) // 2
+    tokens = arrays[0].shape[0]
     vmem = pl.BlockSpec(memory_space=pltpu.VMEM)
-    scratch = [
-        pltpu.VMEM((len(blocks),) + blocks[0].shape, jnp.bfloat16),
-        pltpu.SemaphoreType.DMA((len(blocks),)),
-    ]
-    if pieces is not None:
-        scratch.append(pltpu.VMEM(pieces, jnp.bfloat16))
     return pl.pallas_call(
         kernel,
         in_specs=[pl.BlockSpec(memory_space=pltpu.SMEM)] * len(scalars)
@@ -322,11 +318,14 @@
         + [pl.BlockSpec(memory_space=pl.ANY)] * len(blocks),
         out_specs=[vmem] * len(out_shape),
         out_shape=out_shape,
-        scratch_shapes=scratch,
+        scratch_shapes=[
+            pltpu.VMEM((2, count * depth, width), jnp.bfloat16),
+            pltpu.SemaphoreType.DMA((len(blocks),)),
+        ],
         compiler_params=params(),
         cost_estimate=pl.CostEstimate(
-            flops=2 * len(blocks) * tokens * width * width,
-            bytes_accessed=2 * len(blocks) * width * width,
+            flops=2 * len(blocks) * tokens * depth * width,
+            bytes_accessed=2 * len(blocks) * depth * width,
             transcendentals=0,
         ),
     )(*scalars, *arrays, *blocks)
@@ -428,6 +427,13 @@
                 ]
                 message = lax.ppermute(message, axes, moves)
             token_parts[away, step] = message
+    def old_block(step, start, size):
+        away = by_index(old_factors, layer ^ step)[start : start + size].astype(jnp.bfloat16)
+        return swap(away, "tensor", n_tensor, step) if step else away
+
+    part_rows = row_block // 2
+    early = old_block(2, 0, part_rows)
+    late = old_block(2, part_rows, part_rows)
     collected = jnp.stack(
         [
             jnp.concatenate(
@@ -441,12 +447,14 @@
             for step in range(n_tensor)
         ]
     )
+    collected, early = lax.optimization_barrier((collected, early))
     gathered = lax.all_gather(collected, "section", axis=0)
-
-    blocks = [by_index(old_factors, layer).astype(jnp.bfloat16)]
-    for step in (1, 2, 3):
-        away = by_index(old_factors, layer ^ step)
-        blocks.append(swap(away.astype(jnp.bfloat16), "tensor", n_tensor, step))
+    blocks = [
+        old_block(0, 0, row_block),
+        old_block(1, 0, row_block),
+        jnp.concatenate([early, late], axis=0),
+        old_block(3, 0, row_block),
+    ]
 
     def both_shards(value, axis):
         other = swap(value, "shard", n_shard, 1)
@@ -480,7 +488,10 @@
     scale = (D / (3.0 * jnp.sum(matrix_diag))).reshape(1)
     low_diag = lax.reduce_precision(matrix_diag, 8, 7)[:, None, :]
     rows = by_index(features, core).reshape(n_tensor, row_block, tokens)
-    rows = jnp.swapaxes(rows, 1, 2)
+    rows = jnp.concatenate(
+        [jnp.swapaxes(by_index(rows, own_place ^ index), 0, 1) for index in range(n_tensor)], axis=1
+    )
+    features, rows = lax.optimization_barrier((features, rows))
 
     own_cols = [
         factor_block(place, features, blocks[step], low_diag, step, weight)
@@ -489,45 +500,42 @@
     other_cols = [swap(block, "section", n_section, 1) for block in own_cols]
     cols = own_cols + other_cols
 
-    def shaped(dtype, *shape):
-        return jax.ShapeDtypeStruct(shape, dtype)
-
-    wide = shaped(jnp.float32, 2, tokens, col_block)
-    sent = shaped(jnp.bfloat16, tokens, 2 * col_block)
-    part = shaped(jnp.bfloat16, col_block, tokens)
-    pieces = (n_tensor, tokens, col_block)
-    by_first, step_one, message = chain_call(
-        first_kernel, (place, scale), (rows, low_diag), cols, (wide, wide, sent), None
-    )
+    wide = jax.ShapeDtypeStruct((2, tokens, col_block), jnp.float32)
+    sent = jax.ShapeDtypeStruct((tokens, 2 * col_block), jnp.bfloat16)
+    part = jax.ShapeDtypeStruct((col_block, tokens), jnp.bfloat16)
+    scalars = (place, scale)
+    kept, message = chain_call(first_kernel, scalars, (rows, low_diag), cols, (wide, sent))
     theirs = swap(message, "section", n_section, 2)
-    step_two, message = chain_call(
-        second_kernel, (place,), (message, theirs, step_one, low_diag), cols, (wide, sent), pieces
+    kept, message = chain_call(
+        second_kernel, scalars, (message, theirs, rows, low_diag, kept), cols, (wide, sent)
     )
     theirs = swap(message, "section", n_section, 2)
-    keep, give = chain_call(
-        third_kernel,
-        (place, scale),
-        (message, theirs, step_two, by_first, low_diag),
-        cols,
-        (part, part),
-        pieces,
-    )
+    keep, give = chain_call(third_kernel, scalars, (message, theirs, kept), cols, (part, part))
     got = swap(give, "section", n_section, 1)
     own = jnp.where(
         core == shard, jnp.concatenate([keep, got], axis=1), jnp.concatenate([got, keep], axis=1)
     )
 
-    def send(value, moves):
-        return lax.ppermute(
-            value, axes, [(x * n_tensor + a, x * n_tensor + b) for x, a, b in moves]
-        )
-
-    def across(value, layers):
-        return lax.ppermute(
-            value,
-            axes,
-            [(x * n_tensor + z, (1 - x) * n_tensor + z) for x, z in layers],
-        )
+    def useful(x, z):
+        return z != 0 and (x, z) != (1, 2)
+
+    def send(value, step, held):
+        moves = [
+            (x * n_tensor + z, x * n_tensor + (z ^ step))
+            for x in range(n_shard)
+            for z in range(n_tensor)
+            if useful(x, z ^ held)
+        ]
+        return lax.ppermute(value, axes, moves)
+
+    def across(value, held):
+        moves = [
+            (x * n_tensor + z, (1 - x) * n_tensor + z)
+            for x in range(n_shard)
+            for z in range(n_tensor)
+            if useful(x, z ^ held)
+        ]
+        return lax.ppermute(value, axes, moves)
 
     everywhere = ("shard", "tensor", "section")
 
@@ -545,65 +553,18 @@
         )
         return jnp.where(layer == source, value, moved_here)
 
-    def to_side(value):
-        got = lax.ppermute(
-            value, everywhere, [(spot(x, t, t), spot(x, t, t ^ 2)) for x in planes for t in layers]
-        )
-        return jnp.where(section == layer, value, got)
-
-    def to_core(value):
-        got = lax.ppermute(
-            value,
-            everywhere,
-            [(spot(x, t, t ^ a), spot(x, t, t ^ a ^ 1)) for x in planes for t in layers for a in (0, 2)],
-        )
-        return jnp.where((section ^ layer) % 2 == 0, value, got)
-
-    down_1 = send(own, [(0, 3, 2), (0, 2, 1), (0, 1, 0), (1, 3, 2), (1, 1, 0)])
-    up_1 = send(own, [(0, 1, 2), (0, 2, 3), (1, 1, 2)])
-    over_0 = across(own, [(0, 1), (0, 2), (0, 3), (1, 1), (1, 3)])
+    near_2 = send(own, 2, 0)
+    near_1 = send(own, 1, 0)
+    over_0 = across(own, 0)
     left_here = scatter(own, 0)
-    down_1, up_1, over_0 = lax.optimization_barrier((down_1, up_1, over_0))
-
-    down_2 = send(down_1, [(0, 2, 1), (0, 1, 0), (1, 2, 1)])
-    up_2 = send(up_1, [(0, 2, 3), (1, 2, 3)])
-    over_1 = across(
-        jnp.where(layer == 3, up_1, down_1),
-        [(0, 0), (0, 1), (0, 2), (0, 3), (1, 0), (1, 2)],
-    )
-    down_2, up_2, over_1, left_here = lax.optimization_barrier((down_2, up_2, over_1, left_here))
-
-    down_3 = send(down_2, [(0, 1, 0), (1, 1, 0)])
-    over_2 = across(
-        jnp.where(layer < 2, down_2, jnp.where(layer == 2, up_1, up_2)),
-        [(0, 0), (0, 1), (0, 2), (0, 3), (1, 1), (1, 2), (1, 3)],
-    )
+    near_1, over_0 = lax.optimization_barrier((near_1, over_0))
+    left_here, near_2 = lax.optimization_barrier((left_here, near_2))
+    over_1 = across(near_1, 1)
+    near_3 = send(near_2, 1, 2)
+    over_2 = across(near_2, 2)
+    over_3 = across(near_3, 3)
     left_there = lax.ppermute(
         left_here, everywhere, [(spot(x, t, t), spot(1 - x, t, t)) for x in planes for t in layers]
-    )
-    left_here = to_side(left_here)
-    down_3, over_2, left_there, left_here = lax.optimization_barrier(
-        (down_3, over_2, left_there, left_here)
-    )
-
-    over_3 = across(down_3, [(0, 0), (1, 0)])
-    left_there = to_core(to_side(left_there))
-    left_here = to_core(left_here)
-
-    def by_layer(*options):
-        chosen = options[3]
-        for index in (2, 1, 0):
-            chosen = jnp.where(layer == index, options[index], chosen)
-        return chosen
-
-    own_1 = by_layer(down_1, own, up_1, up_2)
-    own_2 = by_layer(down_2, down_1, own, up_1)
-    own_3 = by_layer(down_3, down_2, down_1, own)
-    other_1 = by_layer(over_1, over_0, over_2, over_2)
-    other_2 = by_layer(over_2, over_1, over_0, over_1)
-    other_3 = by_layer(over_3, over_2, over_1, over_0)
-    precond_attn = attn_products(
-        shard, (left_here, left_there, own_1, own_2, own_3, other_1, other_2, other_3)
     )
 
     router_matrix = (
@@ -615,6 +576,44 @@
     router_right = jnp.einsum(
         "en,ef->fn", grad_all, router_inverse, preferred_element_type=jnp.float32
     ).astype(jnp.bfloat16)
+    router_cols = learning_rate * jnp.einsum(
+        "fn,cn->fc", router_right, own, preferred_element_type=jnp.float32
+    )
+    router_there = lax.ppermute(router_cols, axes, [(n_tensor + 2, 2)])
+    router_cols = scatter(jnp.where(shard == 1, router_cols, router_there), 2)
+    router_high = lax.reduce_precision(router_cols, 8, 7)
+    codes = jnp.concatenate([router_high, router_cols - router_high], axis=0).astype(jnp.bfloat16)
+    codes = jnp.pad(codes, ((0, 0), (0, 2 * tokens_all - col_block))).reshape(-1, tokens_all)
+    bundle = jnp.concatenate([left_here, left_there, codes], axis=0)
+    bundle, over_1, near_3 = lax.optimization_barrier((bundle, over_1, near_3))
+    to_side = [(spot(x, t, t), spot(x, t, t ^ 2)) for x in planes for t in layers]
+    bundle = jnp.where(section == layer, bundle, lax.ppermute(bundle, everywhere, to_side))
+    bundle, over_2 = lax.optimization_barrier((bundle, over_2))
+    to_core = [
+        (spot(x, t, t ^ a), spot(x, t, t ^ a ^ 1)) for x in planes for t in layers for a in (0, 2)
+    ]
+    bundle = jnp.where(
+        (section ^ layer) % 2 == 0, bundle, lax.ppermute(bundle, everywhere, to_core)
+    )
+    left_here = bundle[:col_block]
+    left_there = bundle[col_block : 2 * col_block]
+    codes = bundle[2 * col_block :].reshape(2 * EXPERTS, -1)[:, :col_block].astype(jnp.float32)
+    precond_router = codes[:EXPERTS] + codes[EXPERTS:]
+
+    def by_layer(options, factor):
+        chosen = options[factor ^ 3]
+        for index in (2, 1, 0):
+            chosen = jnp.where(layer == index, options[factor ^ index], chosen)
+        return chosen
+
+    mine = (own, near_1, near_2, near_3)
+    others = (over_0, over_1, over_2, over_3)
+    own_1, own_2, own_3 = (by_layer(mine, factor) for factor in (1, 2, 3))
+    other_1, other_2, other_3 = (by_layer(others, factor) for factor in (1, 2, 3))
+    precond_attn = attn_products(
+        shard, (left_here, left_there, own_1, own_2, own_3, other_1, other_2, other_3)
+    )
+
     precond_norms = (
         learning_rate
         * norm_sums[0]
@@ -624,12 +623,6 @@
             + damping
         )
     )
-    router_cols = learning_rate * jnp.einsum(
-        "fn,cn->fc", router_right, own, preferred_element_type=jnp.float32
-    )
-    router_cols = jnp.where(shard == 1, router_cols, across(router_cols, [(1, 2)]))
-    precond_router = to_core(to_side(scatter(router_cols, 2)))
-
     vocab_block = old_embed_diag.shape[0]
     ids_here = layer * vocab_block + lax.iota(jnp.int32, vocab_block)
     matches = ids_here[:, None] == ids_all[None, :]

time: 267 us -> 266 us (level)
  starting transfers between devices: 61.2 us -> 49 us
  local copies, waits for them, and re-layouts: 17.2 us -> 23.8 us
  Pallas kernels: 32.2 us -> 25.9 us
  other arithmetic: 9.6 us -> 14.5 us
  waiting for transfers between devices: 126 us -> 130 us
    ppermute x16 -> x10, starting transfers between devices: 33.3 us -> 18.9 us  [the longest x4 9.45 us: across(): return lax.ppermute(value, axes, moves)]
    all_gather x1, waiting for transfers between devices: 12.9 us -> 0.01 us  [layer_plan(): gathered = lax.all_gather(collected, 'section', axis=0)]
    ppermute x1, waiting for transfers between devices: 0.01 us -> 6.51 us  [layer_plan(): lax.ppermute(left_here, everywhere, [(spot(x, t, t), spot(1 - x, t, t)) f...]
    pallas_call x3, Pallas kernels: 19.2 us -> 14.2 us  [chain_call(): pl.pallas_call(kernel, in_specs=[pl.BlockSpec(memory_space=pltpu.SMEM)] *...]
    ppermute x13 -> x14, waiting for transfers between devices: 60.5 us -> 65 us  [swap(): return lax.ppermute(value, axis, [(i, i ^ step) for i in range(size)])]
    dynamic_slice x1 -> x6, local copies, waits for them, and re-layouts: 1.09 us -> 4.41 us  [by_index(): return lax.dynamic_index_in_dim(array, index, axis, False)]
    ppermute x7, waiting for transfers between devices: 6.63 us -> 9.92 us  [layer_plan(): message = lax.ppermute(message, axes, moves)]
    concatenate x0 -> x1, local copies, waits for them, and re-layouts: none -> 3.05 us  [layer_plan(): jnp.concatenate([jnp.swapaxes(by_index(rows, own_place ^ index), 0, 1) fo...]
  transfers between devices with their start and end apart: 40 -> 35, of which waited for: 14 -> 14; matrix products, arithmetic and copies ran while one was open for 9% -> 12% of each run, Pallas kernels for 3% -> 3%
where the time goes in v4:
time: 266 us; the launch traced here: 263 us
  waiting for transfers between devices  130 us (49%)
  starting transfers between devices  49 us (18%)
  Pallas kernels  25.9 us (10%)
  local copies, waits for them, and re-layouts  23.8 us (9%)
  between operations  16.2 us (6%)
  other arithmetic  14.5 us (5%)
  matrix products  4.03 us (2%)
    ppermute x14, waiting for transfers between devices, swap(): return lax.ppermute(value, axis, [(i, i ^ step) for i in range(size)])  65 us
    ppermute x3, waiting for transfers between devices, send(): return lax.ppermute(value, axes, moves)  27 us
    ppermute x4, waiting for transfers between devices, across(): return lax.ppermute(value, axes, moves)  14.2 us
    pallas_call x3, Pallas kernels, chain_call(): pl.pallas_call(kernel, in_specs=[pl.BlockSpec(memory_space=pltpu.SMEM)] *...  14.2 us
    ppermute x14, starting transfers between devices, swap(): return lax.ppermute(value, axis, [(i, i ^ step) for i in range(size)])  13.6 us
    ppermute x7, starting transfers between devices, layer_plan(): message = lax.ppermute(message, axes, moves)  12.5 us
    ppermute x7, waiting for transfers between devices, layer_plan(): message = lax.ppermute(message, axes, moves)  9.92 us
    ppermute x4, starting transfers between devices, across(): return lax.ppermute(value, axes, moves)  9.45 us
  transfers between devices with their start and end apart: 35, of which 14 were waited for; matrix products, arithmetic and copies ran while one was open for 12% of the time, Pallas kernels for 3%

profile of v4, /device:TPU:0, one launch (start us, length us, event | category | flops | bytes accessed | tf_op | source)
XLA Modules:
  0.0 263.3 jit_solution(1528376793690373452)
XLA Ops:
  8.5 5.0 %collective-permute-start.4 = (bf16[144,256]{1,0:T(8,128)(2,1)S(1)}, bf16[144,256]{1,0:T(8,128)(2,1)S(1)}, u32[]{:S(2)}, u32[]{:S(2)}) collective-permute-start(bf16[144,256]{1,0:T(8,128)(2,1)S(1)} %get-tuple-element.79), channel_id=1, source_target_pairs={{0,24},{4,28},{8,16},{12,20},{16,8},{20,12},{24,0},{28,4},{1,25},{... | collective-permute-start | bytes 221192 | tf_op jit(solution)/shard_map/ppermute | solution.py:428
  21.4 4.1 %fusion.13 = (bf16[576,576]{1,0:T(8,128)(2,1)}, bf16[576,576]{1,0:T(8,128)(2,1)}, bf16[1,576,576]{2,1,0:T(8,128)(2,1)S(1)}, bf16[576,576]{1,0:T(8,128)(2,1)}) fusion(f32[4,576,576]{2,1,0:T(8,128)} %param.12, s32[]{:T(128)S(6)} %select_n.237, s32[]{:T(128)S(6)} %select_n.229, s32[]{:T(128)S(6)} %select_n.234, s32[]{:T(128)S(6)} %select_n.231), kind=kLoop, calls=%fused_computation.26 | loop fusion | bytes 5308432 | tf_op jit(solution)/shard_map/convert_element_type | solution.py:431
  27.8 3.0 %collective-permute-start.7 = (bf16[288,576]{1,0:T(8,128)(2,1)S(1)}, bf16[288,576]{1,0:T(8,128)(2,1)S(1)}, u32[]{:S(2)}, u32[]{:S(2)}) collective-permute-start(bf16[288,576]{1,0:T(8,128)(2,1)S(1)} %get-tuple-element.77), channel_id=1, source_target_pairs={{0,8},{4,12},{8,0},{12,4},{1,9},{5,13},{9,1},{13,5},{2,10},{6,14},... | collective-permute-start | bytes 995336 | tf_op jit(solution)/shard_map/ppermute | solution.py:169
  30.8 9.9 %collective-permute-done.3 = bf16[160,256]{1,0:T(8,128)(2,1)S(1)} collective-permute-done((bf16[160,256]{1,0:T(8,128)(2,1)S(1)}, bf16[160,256]{1,0:T(8,128)(2,1)S(1)}, u32[]{:S(2)}, u32[]{:S(2)}) %collective-permute-start.3) | collective-permute-done | bytes 81952 | tf_op jit(solution)/shard_map/ppermute | solution.py:428
  41.7 5.8 %collective-permute-done.7 = bf16[288,576]{1,0:T(8,128)(2,1)S(1)} collective-permute-done((bf16[288,576]{1,0:T(8,128)(2,1)S(1)}, bf16[288,576]{1,0:T(8,128)(2,1)S(1)}, u32[]{:S(2)}, u32[]{:S(2)}) %collective-permute-start.7) | collective-permute-done | bytes 331808 | tf_op jit(solution)/shard_map/ppermute | solution.py:169
  54.2 29.0 %collective-permute-done.12 = bf16[288,576]{1,0:T(8,128)(2,1)S(1)} collective-permute-done((bf16[288,576]{1,0:T(8,128)(2,1)S(1)}, bf16[288,576]{1,0:T(8,128)(2,1)S(1)}, u32[]{:S(2)}, u32[]{:S(2)}) %collective-permute-start.12) | collective-permute-done | bytes 331808 | tf_op jit(solution)/shard_map/ppermute | solution.py:169
  93.4 3.0 %concatenate.109.rows = bf16[256,2304]{1,0:T(8,128)(2,1)} concatenate(bf16[256,576]{1,0:T(8,128)(2,1)} %bitcast.132, bf16[256,576]{1,0:T(8,128)(2,1)S(1)} %bitcast.131, bf16[256,576]{1,0:T(8,128)(2,1)S(1)} %bitcast.130, bf16[256,576]{1,0:T(8,128)(2,1)S(1)} %bitcast.129), dimensions={1} | concatenate | bytes 2359296 | tf_op jit(solution)/shard_map/concatenate | solution.py:491
  98.3 2.7 %shard_map.112.refs_1_ = bf16[576,576]{1,0:T(8,128)(2,1)} custom-call(s32[1]{0:T(128)} %bitcast.1.place_ref, bf16[2,2304,256]{2,1,0:T(8,128)(2,1)S(1)} %bitcast.118, bf16[2,2304,256]{2,1,0:T(8,128)(2,1)S(1)} %bitcast.119, bf16[576,576]{1,0:T(8,128)(2,1)} %collective-permute-done.11.old, f32[4,1,576]{2,1,0:T(1,128)S(1)} %add_reduce-precision_fusion.diag), custom_call_target="tpu_custom_call" | custom-call | flops 339738624 | bytes 2506752 | tf_op jit(solution)/shard_map/pallas_call | solution.py:207
  109.5 4.5 %shard_map.115 = (f32[2,256,576]{2,1,0:T(8,128)S(1)}, bf16[256,1152]{1,0:T(8,128)(2,1)S(1)}) custom-call(s32[1]{0:T(128)} %bitcast.1.place_ref, f32[1]{0:T(128)} %bitcast.37.scale_ref, bf16[256,2304]{1,0:T(8,128)(2,1)S(1)} %copy-done, f32[4,1,576]{2,1,0:T(1,128)S(1)} %add_reduce-precision_fusion.diag, bf16[576,576]{1,0:T(8,128)(2,1)S(1)} %shard_map.111.refs_0_, ...), custom_call_target="tpu_custom_call" | custom-call | flops 1358954496 | bytes 5308416 | tf_op jit(solution)/shard_map/pallas_call | solution.py:314
  115.6 14.1 %collective-permute-done.18.theirs = bf16[256,1152]{1,0:T(8,128)(2,1)S(1)} collective-permute-done((bf16[256,1152]{1,0:T(8,128)(2,1)S(1)}, bf16[256,1152]{1,0:T(8,128)(2,1)S(1)}, u32[]{:S(2)}, u32[]{:S(2)}) %collective-permute-start.18) | collective-permute-done | bytes 589856 | tf_op jit(solution)/shard_map/ppermute | solution.py:169
  129.7 5.3 %shard_map.116 = (f32[2,256,576]{2,1,0:T(8,128)S(1)}, bf16[256,1152]{1,0:T(8,128)(2,1)S(1)}) custom-call(s32[1]{0:T(128)} %bitcast.1.place_ref, f32[1]{0:T(128)} %bitcast.37.scale_ref, bf16[256,1152]{1,0:T(8,128)(2,1)S(1)} %get-tuple-element.32.mine, bf16[256,1152]{1,0:T(8,128)(2,1)S(1)} %collective-permute-done.18.theirs, bf16[256,2304]{1,0:T(8,128)(2,1)S(1)} %copy-done, ...), custom_call_target="tpu_custom_call" | custom-call | flops 1358954496 | bytes 5308416 | tf_op jit(solution)/shard_map/pallas_call | solution.py:314
  136.6 13.3 %collective-permute-done.19.theirs = bf16[256,1152]{1,0:T(8,128)(2,1)S(1)} collective-permute-done((bf16[256,1152]{1,0:T(8,128)(2,1)S(1)}, bf16[256,1152]{1,0:T(8,128)(2,1)S(1)}, u32[]{:S(2)}, u32[]{:S(2)}) %collective-permute-start.19) | collective-permute-done | bytes 589856 | tf_op jit(solution)/shard_map/ppermute | solution.py:169
  149.9 4.3 %shard_map.117 = (bf16[576,256]{1,0:T(8,128)(2,1)S(1)}, bf16[576,256]{1,0:T(8,128)(2,1)S(1)}) custom-call(s32[1]{0:T(128)} %bitcast.1.place_ref, f32[1]{0:T(128)} %bitcast.37.scale_ref, bf16[256,1152]{1,0:T(8,128)(2,1)S(1)} %get-tuple-element.34.mine, bf16[256,1152]{1,0:T(8,128)(2,1)S(1)} %collective-permute-done.19.theirs, ...), custom_call_target="tpu_custom_call" | custom-call | flops 1358954496 | bytes 5308416 | tf_op jit(solution)/shard_map/pallas_call | solution.py:314
  163.4 26.1 %collective-permute-done.22 = bf16[576,512]{1,0:T(8,128)(2,1)S(1)} collective-permute-done((bf16[576,512]{1,0:T(8,128)(2,1)S(1)}, bf16[576,512]{1,0:T(8,128)(2,1)S(1)}, u32[]{:S(2)}, u32[]{:S(2)}) %collective-permute-start.22) | collective-permute-done | bytes 589856 | tf_op jit(solution)/shard_map/ppermute | solution.py:529
  193.7 3.0 %collective-permute-start.28 = (bf16[576,512]{1,0:T(8,128)(2,1)}, bf16[576,512]{1,0:T(8,128)(2,1)}, u32[]{:S(2)}, u32[]{:S(2)}) collective-permute-start(bf16[576,512]{1,0:T(8,128)(2,1)} %collective-permute-done.26), channel_id=1, source_target_pairs={{0,16},{8,24},{12,28},{16,0},{24,8},{1,17},{9,25},{13,29},{17,1},{... | collective-permute-start | bytes 1769480 | tf_op jit(solution)/shard_map/ppermute | solution.py:538
  198.7 6.5 %collective-permute-done.23 = bf16[576,512]{1,0:T(8,128)(2,1)} collective-permute-done((bf16[576,512]{1,0:T(8,128)(2,1)S(1)}, bf16[576,512]{1,0:T(8,128)(2,1)}, u32[]{:S(2)}, u32[]{:S(2)}) %collective-permute-start.23) | collective-permute-done | bytes 589856 | tf_op jit(solution)/shard_map/ppermute | solution.py:566
  206.4 7.6 %collective-permute-done.28 = bf16[576,512]{1,0:T(8,128)(2,1)} collective-permute-done((bf16[576,512]{1,0:T(8,128)(2,1)}, bf16[576,512]{1,0:T(8,128)(2,1)}, u32[]{:S(2)}, u32[]{:S(2)}) %collective-permute-start.28) | collective-permute-done | bytes 589856 | tf_op jit(solution)/shard_map/ppermute | solution.py:538
  214.0 2.9 %collective-permute-start.30 = (bf16[1184,512]{1,0:T(8,128)(2,1)S(1)}, bf16[1184,512]{1,0:T(8,128)(2,1)S(1)}, u32[]{:S(2)}, u32[]{:S(2)}) collective-permute-start(bf16[1184,512]{1,0:T(8,128)(2,1)S(1)} %pad_maximum_fusion), channel_id=1, source_target_pairs={{0,2},{5,7},{10,8},{15,13},{16,18},{21,23},{26,24},{31,29}} | collective-permute-start | bytes 3637256 | tf_op jit(solution)/shard_map/ppermute | solution.py:590
  217.9 3.8 %collective-permute-start.31 = (bf16[576,512]{1,0:T(8,128)(2,1)}, bf16[576,512]{1,0:T(8,128)(2,1)S(1)}, u32[]{:S(2)}, u32[]{:S(2)}) collective-permute-start(bf16[576,512]{1,0:T(8,128)(2,1)} %copy-done.7), channel_id=1, source_target_pairs={{0,16},{4,20},{12,28},{20,4},{28,12},{1,17},{5,21},{13,29},{21,5},... | collective-permute-start | bytes 1769480 | tf_op jit(solution)/shard_map/ppermute | solution.py:538
  223.6 7.1 %collective-permute-done.30 = bf16[1184,512]{1,0:T(8,128)(2,1)S(1)} collective-permute-done((bf16[1184,512]{1,0:T(8,128)(2,1)S(1)}, bf16[1184,512]{1,0:T(8,128)(2,1)S(1)}, u32[]{:S(2)}, u32[]{:S(2)}) %collective-permute-start.30) | collective-permute-done | bytes 1212448 | tf_op jit(solution)/shard_map/ppermute | solution.py:590
  230.8 3.8 %collective-permute-done.31 = bf16[576,512]{1,0:T(8,128)(2,1)S(1)} collective-permute-done((bf16[576,512]{1,0:T(8,128)(2,1)}, bf16[576,512]{1,0:T(8,128)(2,1)S(1)}, u32[]{:S(2)}, u32[]{:S(2)}) %collective-permute-start.31) | collective-permute-done | bytes 589856 | tf_op jit(solution)/shard_map/ppermute | solution.py:538
  238.1 2.8 %collective-permute-done.33 = bf16[576,512]{1,0:T(8,128)(2,1)S(1)} collective-permute-done((bf16[576,512]{1,0:T(8,128)(2,1)}, bf16[576,512]{1,0:T(8,128)(2,1)S(1)}, u32[]{:S(2)}, u32[]{:S(2)}) %collective-permute-start.33) | collective-permute-done | bytes 589856 | tf_op jit(solution)/shard_map/ppermute | solution.py:538
  242.2 3.3 %fusion.3 = f32[2048,576]{0,1:T(8,128)} fusion(f32[2048]{0:T(1024)S(1)} %add_divide_fusion, s32[512]{0:T(512)S(1)} %add_select_fusion, s32[2048]{0:T(1024)S(1)} %iota_add_fusion, bf16[576,512]{1,0:T(8,128)(2,1)S(1)} %get-tuple-element.67.own_3, bf16[576,512]{1,0:T(8,128)(2,1)S(1)} %get-tuple-element.64.other_3, pred[]{:T(512)S(6)} %eq.100), kind=kOutput, calls=%fused_computation.6 | convolution fusion | flops 1210482688 | bytes 5916673 | tf_op jit(solution)/shard_map/vn,cn->vc/dot_general | solution.py:632
  252.2 4.3 %shard_map.118 = f32[4,576,576]{2,1,0:T(8,128)} custom-call(s32[1]{0:T(128)} %bitcast.shard_ref, bf16[576,512]{1,0:T(8,128)(2,1)S(1)} %copy-done.4, bf16[576,512]{1,0:T(8,128)(2,1)S(1)} %copy-done.3, bf16[576,512]{1,0:T(8,128)(2,1)S(1)} %get-tuple-element.69.own_1, bf16[576,512]{1,0:T(8,128)(2,1)S(1)} %get-tuple-element.68.own_2, ...), custom_call_target="tpu_custom_call" | custom-call | flops 1358954496 | bytes 10027008 | tf_op jit(solution)/shard_map/pallas_call | solution.py:367
  (173 shorter events, 71.6 us)
Async XLA Ops:
  7.2 77.0 %all-gather.3.cloned.1.call-start = ((), (), s32[]{:S(2)}) async-start(), calls=%async_computation | async-start | bytes 3112960 | tf_op jit(solution)/shard_map/all_gather | solution.py:451
  8.5 32.3 %collective-permute-start.4 = (bf16[144,256]{1,0:T(8,128)(2,1)S(1)}, bf16[144,256]{1,0:T(8,128)(2,1)S(1)}, u32[]{:S(2)}, u32[]{:S(2)}) collective-permute-start(bf16[144,256]{1,0:T(8,128)(2,1)S(1)} %get-tuple-element.79), channel_id=1, source_target_pairs={{0,24},{4,28},{8,16},{12,20},{16,8},{20,12},{24,0},{28,4},{1,25},{... | collective-permute-start | bytes 221192 | tf_op jit(solution)/shard_map/ppermute | solution.py:428
  13.5 12.1 %collective-permute-start = (bf16[144,256]{1,0:T(8,128)(2,1)S(1)}, bf16[144,256]{1,0:T(8,128)(2,1)S(1)}, u32[]{:S(2)}, u32[]{:S(2)}) collective-permute-start(bf16[144,256]{1,0:T(8,128)(2,1)S(1)} %get-tuple-element.83), channel_id=1, source_target_pairs={{0,16},{4,20},{8,24},{12,28},{16,0},{20,4},{24,8},{28,12},{1,17},{... | collective-permute-start | bytes 221192 | tf_op jit(solution)/shard_map/ppermute | solution.py:428
  14.0 26.7 %collective-permute-start.6 = (bf16[144,256]{1,0:T(8,128)(2,1)S(1)}, bf16[144,256]{1,0:T(8,128)(2,1)S(1)}, u32[]{:S(2)}, u32[]{:S(2)}) collective-permute-start(bf16[144,256]{1,0:T(8,128)(2,1)S(1)} %get-tuple-element.84), channel_id=1, source_target_pairs={{0,28},{4,24},{8,20},{12,16},{16,12},{20,8},{24,4},{28,0},{1,29},{... | collective-permute-start | bytes 221192 | tf_op jit(solution)/shard_map/ppermute | solution.py:428
  18.8 8.8 %collective-permute-start.5 = (bf16[160,256]{1,0:T(8,128)(2,1)S(1)}, bf16[160,256]{1,0:T(8,128)(2,1)S(1)}, u32[]{:S(2)}, u32[]{:S(2)}) collective-permute-start(bf16[160,256]{1,0:T(8,128)(2,1)S(1)} %pad_maximum_fusion.5), channel_id=1, source_target_pairs={{0,12},{4,8},{8,4},{12,0},{16,28},{20,24},{24,20},{28,16},{1,13},{... | collective-permute-start | bytes 245768 | tf_op jit(solution)/shard_map/ppermute | solution.py:428
  25.6 15.1 %collective-permute-start.3 = (bf16[160,256]{1,0:T(8,128)(2,1)S(1)}, bf16[160,256]{1,0:T(8,128)(2,1)S(1)}, u32[]{:S(2)}, u32[]{:S(2)}) collective-permute-start(bf16[160,256]{1,0:T(8,128)(2,1)S(1)} %pad_maximum_fusion.4), channel_id=1, source_target_pairs={{0,8},{4,12},{8,0},{12,4},{16,24},{20,28},{24,16},{28,20},{1,9},{5... | collective-permute-start | bytes 245768 | tf_op jit(solution)/shard_map/ppermute | solution.py:428
  27.6 13.1 %collective-permute-start.2 = (bf16[144,256]{1,0:T(8,128)(2,1)S(1)}, bf16[144,256]{1,0:T(8,128)(2,1)S(1)}, u32[]{:S(2)}, u32[]{:S(2)}) collective-permute-start(bf16[144,256]{1,0:T(8,128)(2,1)S(1)} %get-tuple-element.81), channel_id=1, source_target_pairs={{0,20},{4,16},{8,28},{12,24},{16,4},{20,0},{24,12},{28,8},{1,21},{... | collective-permute-start | bytes 221192 | tf_op jit(solution)/shard_map/ppermute | solution.py:428
  27.8 19.7 %collective-permute-start.7 = (bf16[288,576]{1,0:T(8,128)(2,1)S(1)}, bf16[288,576]{1,0:T(8,128)(2,1)S(1)}, u32[]{:S(2)}, u32[]{:S(2)}) collective-permute-start(bf16[288,576]{1,0:T(8,128)(2,1)S(1)} %get-tuple-element.77), channel_id=1, source_target_pairs={{0,8},{4,12},{8,0},{12,4},{1,9},{5,13},{9,1},{13,5},{2,10},{6,14},... | collective-permute-start | bytes 995336 | tf_op jit(solution)/shard_map/ppermute | solution.py:169
  50.7 32.5 %collective-permute-start.12 = (bf16[288,576]{1,0:T(8,128)(2,1)S(1)}, bf16[288,576]{1,0:T(8,128)(2,1)S(1)}, u32[]{:S(2)}, u32[]{:S(2)}) collective-permute-start(bf16[288,576]{1,0:T(8,128)(2,1)S(1)} %get-tuple-element.76), channel_id=1, source_target_pairs={{0,8},{4,12},{8,0},{12,4},{1,9},{5,13},{9,1},{13,5},{2,10},{6,14},... | collective-permute-start | bytes 995336 | tf_op jit(solution)/shard_map/ppermute | solution.py:169
  50.7 52.4 %collective-permute-start.13 = (bf16[576,576]{1,0:T(8,128)(2,1)}, bf16[576,576]{1,0:T(8,128)(2,1)}, u32[]{:S(2)}, u32[]{:S(2)}) collective-permute-start(bf16[576,576]{1,0:T(8,128)(2,1)} %get-tuple-element.60), channel_id=1, source_target_pairs={{0,12},{4,8},{8,4},{12,0},{1,13},{5,9},{9,5},{13,1},{2,14},{6,10},... | collective-permute-start | bytes 1990664 | tf_op jit(solution)/shard_map/ppermute | solution.py:169
  52.5 45.8 %collective-permute-start.11 = (bf16[576,576]{1,0:T(8,128)(2,1)}, bf16[576,576]{1,0:T(8,128)(2,1)}, u32[]{:S(2)}, u32[]{:S(2)}) collective-permute-start(bf16[576,576]{1,0:T(8,128)(2,1)} %get-tuple-element.63), channel_id=1, source_target_pairs={{0,4},{4,0},{8,12},{12,8},{1,5},{5,1},{9,13},{13,9},{2,6},{6,2},{1... | collective-permute-start | bytes 1990664 | tf_op jit(solution)/shard_map/ppermute | solution.py:169
  114.0 15.7 %collective-permute-start.18 = (bf16[256,1152]{1,0:T(8,128)(2,1)S(1)}, bf16[256,1152]{1,0:T(8,128)(2,1)S(1)}, u32[]{:S(2)}, u32[]{:S(2)}) collective-permute-start(bf16[256,1152]{1,0:T(8,128)(2,1)S(1)} %get-tuple-element.32.mine), channel_id=1, source_target_pairs={{0,2},{1,3},{2,0},{3,1},{4,6},{5,7},{6,4},{7,5},{8,10},{9,11},{10,... | collective-permute-start | bytes 1769480 | tf_op jit(solution)/shard_map/ppermute | solution.py:169
  135.0 14.8 %collective-permute-start.19 = (bf16[256,1152]{1,0:T(8,128)(2,1)S(1)}, bf16[256,1152]{1,0:T(8,128)(2,1)S(1)}, u32[]{:S(2)}, u32[]{:S(2)}) collective-permute-start(bf16[256,1152]{1,0:T(8,128)(2,1)S(1)} %get-tuple-element.34.mine), channel_id=1, source_target_pairs={{0,2},{1,3},{2,0},{3,1},{4,6},{5,7},{6,4},{7,5},{8,10},{9,11},{10,... | collective-permute-start | bytes 1769480 | tf_op jit(solution)/shard_map/ppermute | solution.py:169
  158.7 30.8 %collective-permute-start.22 = (bf16[576,512]{1,0:T(8,128)(2,1)S(1)}, bf16[576,512]{1,0:T(8,128)(2,1)S(1)}, u32[]{:S(2)}, u32[]{:S(2)}) collective-permute-start(bf16[576,512]{1,0:T(8,128)(2,1)S(1)} %maximum_select_fusion), channel_id=1, source_target_pairs={{4,12},{8,0},{12,4},{20,28},{28,20},{5,13},{9,1},{13,5},{21,29},{2... | collective-permute-start | bytes 1769480 | tf_op jit(solution)/shard_map/ppermute | solution.py:529
  160.3 32.5 %collective-permute-start.27 = (bf16[576,512]{1,0:T(8,128)(2,1)S(1)}, bf16[576,512]{1,0:T(8,128)(2,1)S(1)}, u32[]{:S(2)}, u32[]{:S(2)}) collective-permute-start(bf16[576,512]{1,0:T(8,128)(2,1)S(1)} %maximum_select_fusion), channel_id=1, source_target_pairs={{4,20},{8,24},{12,28},{20,4},{28,12},{5,21},{9,25},{13,29},{21,5},... | collective-permute-start | bytes 1769480 | tf_op jit(solution)/shard_map/ppermute | solution.py:538
  161.0 32.7 %collective-permute-start.26 = (bf16[576,512]{1,0:T(8,128)(2,1)S(1)}, bf16[576,512]{1,0:T(8,128)(2,1)}, u32[]{:S(2)}, u32[]{:S(2)}) collective-permute-start(bf16[576,512]{1,0:T(8,128)(2,1)S(1)} %maximum_select_fusion), channel_id=1, source_target_pairs={{4,0},{8,12},{12,8},{20,16},{28,24},{5,1},{9,13},{13,9},{21,17},{2... | collective-permute-start | bytes 1769480 | tf_op jit(solution)/shard_map/ppermute | solution.py:529
  162.6 28.8 %collective-permute-start.24 = (f32[8,576]{1,0:T(8,128)S(1)}, f32[8,576]{1,0:T(8,128)S(1)}, u32[]{:S(2)}, u32[]{:S(2)}) collective-permute-start(f32[8,576]{1,0:T(8,128)S(1)} %convolution_multiply_fusion), channel_id=1, source_target_pairs={{24,8},{25,9},{26,10},{27,11}} | collective-permute-start | bytes 55304 | tf_op jit(solution)/shard_map/ppermute | solution.py:582
  189.5 15.7 %collective-permute-start.23 = (bf16[576,512]{1,0:T(8,128)(2,1)S(1)}, bf16[576,512]{1,0:T(8,128)(2,1)}, u32[]{:S(2)}, u32[]{:S(2)}) collective-permute-start(bf16[576,512]{1,0:T(8,128)(2,1)S(1)} %broadcast_select_fusion.2), channel_id=1, source_target_pairs={{0,16},{5,21},{10,26},{15,31},{16,0},{21,5},{26,10},{31,15}} | collective-permute-start | bytes 1769480 | tf_op jit(solution)/shard_map/ppermute | solution.py:566
  193.7 20.3 %collective-permute-start.28 = (bf16[576,512]{1,0:T(8,128)(2,1)}, bf16[576,512]{1,0:T(8,128)(2,1)}, u32[]{:S(2)}, u32[]{:S(2)}) collective-permute-start(bf16[576,512]{1,0:T(8,128)(2,1)} %collective-permute-done.26), channel_id=1, source_target_pairs={{0,16},{8,24},{12,28},{16,0},{24,8},{1,17},{9,25},{13,29},{17,1},{... | collective-permute-start | bytes 1769480 | tf_op jit(solution)/shard_map/ppermute | solution.py:538
  196.7 17.3 %collective-permute-start.29 = (bf16[576,512]{1,0:T(8,128)(2,1)S(1)}, bf16[576,512]{1,0:T(8,128)(2,1)}, u32[]{:S(2)}, u32[]{:S(2)}) collective-permute-start(bf16[576,512]{1,0:T(8,128)(2,1)S(1)} %collective-permute-done.22), channel_id=1, source_target_pairs={{0,4},{4,0},{12,8},{20,16},{28,24},{1,5},{5,1},{13,9},{21,17},{29,... | collective-permute-start | bytes 1769480 | tf_op jit(solution)/shard_map/ppermute | solution.py:529
  214.0 16.7 %collective-permute-start.30 = (bf16[1184,512]{1,0:T(8,128)(2,1)S(1)}, bf16[1184,512]{1,0:T(8,128)(2,1)S(1)}, u32[]{:S(2)}, u32[]{:S(2)}) collective-permute-start(bf16[1184,512]{1,0:T(8,128)(2,1)S(1)} %pad_maximum_fusion), channel_id=1, source_target_pairs={{0,2},{5,7},{10,8},{15,13},{16,18},{21,23},{26,24},{31,29}} | collective-permute-start | bytes 3637256 | tf_op jit(solution)/shard_map/ppermute | solution.py:590
  217.9 16.8 %collective-permute-start.31 = (bf16[576,512]{1,0:T(8,128)(2,1)}, bf16[576,512]{1,0:T(8,128)(2,1)S(1)}, u32[]{:S(2)}, u32[]{:S(2)}) collective-permute-start(bf16[576,512]{1,0:T(8,128)(2,1)} %copy-done.7), channel_id=1, source_target_pairs={{0,16},{4,20},{12,28},{20,4},{28,12},{1,17},{5,21},{13,29},{21,5},... | collective-permute-start | bytes 1769480 | tf_op jit(solution)/shard_map/ppermute | solution.py:538
  221.7 19.3 %collective-permute-start.33 = (bf16[576,512]{1,0:T(8,128)(2,1)}, bf16[576,512]{1,0:T(8,128)(2,1)S(1)}, u32[]{:S(2)}, u32[]{:S(2)}) collective-permute-start(bf16[576,512]{1,0:T(8,128)(2,1)} %collective-permute-done.29), channel_id=1, source_target_pairs={{0,16},{4,20},{8,24},{16,0},{24,8},{1,17},{5,21},{9,25},{17,1},{25... | collective-permute-start | bytes 1769480 | tf_op jit(solution)/shard_map/ppermute | solution.py:538
  234.6 10.9 %collective-permute-start.32 = (bf16[1184,512]{1,0:T(8,128)(2,1)S(1)}, bf16[1184,512]{1,0:T(8,128)(2,1)S(1)}, u32[]{:S(2)}, u32[]{:S(2)}) collective-permute-start(bf16[1184,512]{1,0:T(8,128)(2,1)S(1)} %broadcast_select_fusion), channel_id=1, source_target_pairs={{0,1},{2,3},{5,4},{7,6},{10,11},{8,9},{15,14},{13,12},{16,17},{18,... | collective-permute-start | bytes 3637256 | tf_op jit(solution)/shard_map/ppermute | solution.py:596
  (26 other events, 222.7 us)
Sparse Core Ops, SparseCore 0:
  47.6 23.5 all-gather.2

commit v5 on v4

--- a/solution.py
+++ b/solution.py
@@ -331,52 +331,104 @@
     )(*scalars, *arrays, *blocks)
 
 
-def attn_kernel(shard_ref, left_own, left_other, own_1, own_2, own_3, other_1, other_2, other_3, out):
-    first = shard_ref[0] == 0
+def output_kernel(
+    where_ref, left_mine, left_other, ids, scale, *refs, attn_steps, vocab_block
+):
+    mine, others, spread = refs[:4], refs[4:8], refs[8:12]
+    attn, embed, held, sems = refs[12:]
+    shard, layer, step = where_ref[0], where_ref[1], pl.program_id(0)
+    first = shard == 0
+
+    def fetch(slot, from_mine, index):
+        for place in range(4):
+            for group, wanted in ((mine, from_mine), (others, jnp.logical_not(from_mine))):
+
+                @pl.when(wanted & (index == place))
+                def _():
+                    pltpu.make_async_copy(group[place], held.at[slot], sems.at[slot]).start()
+
+    @pl.when(step == 0)
+    def _():
+        fetch(0, first, layer)
+        for place in range(4):
+
+            @pl.when(layer == place)
+            def _():
+                pltpu.make_async_copy(spread[place], held.at[1], sems.at[1]).start()
+
+        fetch(2, first, 3 - layer)
+        fetch(3, jnp.logical_not(first), layer)
+        fetch(4, jnp.logical_not(first), 3 - layer)
+
+    def arrived(slot):
+        pltpu.make_async_copy(mine[0], held.at[slot], sems.at[slot]).wait()
+        return held[slot]
 
     def product(left, right):
-        out[0] = learning_rate * lax.dot_general(
+        return lax.dot_general(
             left, right, (((1,), (1,)), ((), ())), preferred_element_type=jnp.float32
         )
 
-    @pl.when(pl.program_id(0) == 0)
+    for slot in range(attn_steps):
+
+        @pl.when(step == slot)
+        def _():
+            same = first if slot < 3 else jnp.logical_not(first)
+            left = jnp.where(same, left_mine[...], left_other[...])
+            attn[0] = learning_rate * product(left, arrived(slot))
+
+    @pl.when(step == attn_steps)
     def _():
-        left = jnp.where(first, left_own[...], left_other[...])
-        product(left, jnp.where(first, own_1[...], other_1[...]))
-
-    @pl.when(pl.program_id(0) == 1)
+        arrived(4)
+
+    @pl.when(step >= attn_steps)
     def _():
-        left = jnp.where(first, left_own[...], left_other[...])
-        product(left, jnp.where(first, own_2[...], other_2[...]))
-
-    @pl.when(pl.program_id(0) == 2)
-    def _():
-        left = jnp.where(first, left_own[...], left_other[...])
-        product(left, jnp.where(first, own_3[...], other_3[...]))
-
-    @pl.when(pl.program_id(0) == 3)
-    def _():
-        left = jnp.where(first, left_other[...], left_own[...])
-        product(left, jnp.where(first, other_1[...], own_1[...]))
-
-
-def attn_products(shard, operands):
-    rows, tokens_all = operands[0].shape
-    cols = operands[2].shape[0]
-    whole = [pl.BlockSpec(value.shape, lambda w: (0, 0)) for value in operands]
+        rows = embed.shape[0]
+        start = layer * vocab_block + (step - attn_steps) * rows
+        here = lax.broadcasted_iota(jnp.int32, (rows, ids.shape[1]), 0) + start
+        matches = (here == ids[...]).astype(jnp.float32).astype(jnp.bfloat16)
+        embed[...] = product(matches, held[4]) * scale[...]
+
+
+def output_products(where, bundle, ids, scale, mine, others, spread):
+    cols, tokens_all = mine[0].shape
+    vocab_block = scale.shape[0]
+    parts = 4
+    rows = vocab_block // parts
+
+    def embed_place(step):
+        return (jnp.maximum(step - 4, 0), 0)
+
     return pl.pallas_call(
-        attn_kernel,
-        grid=(4,),
-        out_shape=jax.ShapeDtypeStruct((4, rows, cols), jnp.float32),
-        in_specs=[pl.BlockSpec(memory_space=pltpu.SMEM)] + whole,
-        out_specs=pl.BlockSpec((1, rows, cols), lambda w: (w, 0, 0)),
+        functools.partial(output_kernel, attn_steps=4, vocab_block=vocab_block),
+        grid=(4 + parts,),
+        out_shape=(
+            jax.ShapeDtypeStruct((4, cols, cols), jnp.float32),
+            jax.ShapeDtypeStruct((vocab_block, cols), jnp.float32),
+        ),
+        in_specs=[
+            pl.BlockSpec(memory_space=pltpu.SMEM),
+            pl.BlockSpec((cols, tokens_all), lambda step: (0, 0)),
+            pl.BlockSpec((cols, tokens_all), lambda step: (1, 0)),
+            pl.BlockSpec((1, tokens_all), lambda step: (0, 0)),
+            pl.BlockSpec((rows, 1), embed_place),
+        ]
+        + [pl.BlockSpec(memory_space=pl.ANY)] * 12,
+        out_specs=(
+            pl.BlockSpec((1, cols, cols), lambda step: (jnp.minimum(step, 3), 0, 0)),
+            pl.BlockSpec((rows, cols), embed_place),
+        ),
+        scratch_shapes=[
+            pltpu.VMEM((5, cols, tokens_all), jnp.bfloat16),
+            pltpu.SemaphoreType.DMA((5,)),
+        ],
         compiler_params=params(),
         cost_estimate=pl.CostEstimate(
-            flops=8 * rows * cols * tokens_all,
-            bytes_accessed=16 * rows * cols + 16 * rows * tokens_all,
+            flops=2 * cols * tokens_all * (4 * cols + vocab_block),
+            bytes_accessed=4 * cols * (4 * cols + vocab_block) + 14 * cols * tokens_all,
             transcendentals=0,
         ),
-    )(shard.reshape(1), *operands)
+    )(where, bundle, bundle, ids, scale, *mine, *others, *spread)
 
 
 def layer_plan(
@@ -403,58 +455,38 @@
     weight = (1.0 - factor_decay) / tokens_all
     own_place = section ^ layer
     place = own_place.reshape(1)
+    axes = ("shard", "tensor")
 
     def by_index(array, index, axis=0):
         return lax.dynamic_index_in_dim(array, index, axis, False)
 
+    def held_by(layer_index):
+        return jnp.where(layer_index == 3, 3, lax.rem(layer_index + 1, 3))
+
+    def old_block(step):
+        away = by_index(old_factors, held_by(layer ^ step)).astype(jnp.bfloat16)
+        return swap(away, "tensor", n_tensor, step) if step else away
+
+    early = old_block(2)
+
+    by_feature = jnp.swapaxes(activations, 1, 2)
+    kept_tokens = lax.dynamic_slice_in_dim(by_feature, shard * owned, owned, 0)
+    sent_tokens = lax.dynamic_slice_in_dim(by_feature, (1 - shard) * owned, owned, 0)
+    other_tokens = swap(sent_tokens, "shard", n_shard, 1)
     diagonals = local_diagonals(old_factors) * (layer == section).astype(jnp.float32)
     extra = jnp.pad(split_three(diagonals), ((0, 0), (0, 0), (0, 3 * tokens - col_block)))
     extra = jnp.pad(extra.reshape(owned, 9, tokens), ((0, 0), (0, 7), (0, 0)))
-    by_feature = jnp.swapaxes(activations, 1, 2)
-    axes = ("shard", "tensor")
-    token_parts = {}
-    for away in range(n_shard):
-        for step in range(n_tensor):
-            factor = (shard ^ away) * n_tensor + (layer ^ step)
-            message = by_index(by_feature, factor)
-            if away == 0:
-                message = jnp.concatenate([message, by_index(extra, layer ^ step)], axis=0)
-            if away or step:
-                moves = [
-                    (x * n_tensor + z, (x ^ away) * n_tensor + (z ^ step))
-                    for x in range(n_shard)
-                    for z in range(n_tensor)
-                ]
-                message = lax.ppermute(message, axes, moves)
-            token_parts[away, step] = message
-    def old_block(step, start, size):
-        away = by_index(old_factors, layer ^ step)[start : start + size].astype(jnp.bfloat16)
-        return swap(away, "tensor", n_tensor, step) if step else away
-
-    part_rows = row_block // 2
-    early = old_block(2, 0, part_rows)
-    late = old_block(2, part_rows, part_rows)
-    collected = jnp.stack(
-        [
-            jnp.concatenate(
-                [
-                    token_parts[0, step][:features_dev],
-                    token_parts[1, step],
-                    token_parts[0, step][features_dev:],
-                ],
-                axis=0,
-            )
-            for step in range(n_tensor)
-        ]
-    )
-    collected, early = lax.optimization_barrier((collected, early))
+    collected = []
+    for step in range(n_tensor):
+        factor = held_by(layer ^ step)
+        message = jnp.concatenate(
+            [by_index(kept_tokens, factor), by_index(other_tokens, factor), by_index(extra, factor)],
+            axis=0,
+        )
+        collected.append(swap(message, "tensor", n_tensor, step) if step else message)
+    collected, early = lax.optimization_barrier((jnp.stack(collected), early))
     gathered = lax.all_gather(collected, "section", axis=0)
-    blocks = [
-        old_block(0, 0, row_block),
-        old_block(1, 0, row_block),
-        jnp.concatenate([early, late], axis=0),
-        old_block(3, 0, row_block),
-    ]
+    blocks = [old_block(0), old_block(1), early, old_block(3)]
 
     def both_shards(value, axis):
         other = swap(value, "shard", n_shard, 1)
@@ -516,34 +548,20 @@
         core == shard, jnp.concatenate([keep, got], axis=1), jnp.concatenate([got, keep], axis=1)
     )
 
-    def useful(x, z):
-        return z != 0 and (x, z) != (1, 2)
-
-    def send(value, step, held):
-        moves = [
-            (x * n_tensor + z, x * n_tensor + (z ^ step))
-            for x in range(n_shard)
-            for z in range(n_tensor)
-            if useful(x, z ^ held)
-        ]
+    def send(value, pairs):
+        moves = [(x * n_tensor + a, x * n_tensor + b) for x in planes for a, b in pairs]
         return lax.ppermute(value, axes, moves)
 
-    def across(value, held):
-        moves = [
-            (x * n_tensor + z, (1 - x) * n_tensor + z)
-            for x in range(n_shard)
-            for z in range(n_tensor)
-            if useful(x, z ^ held)
-        ]
+    def across(value, at):
+        moves = [(x * n_tensor + z, (1 - x) * n_tensor + z) for x, z in at]
         return lax.ppermute(value, axes, moves)
 
     everywhere = ("shard", "tensor", "section")
+    planes = range(n_shard)
+    layers = range(n_tensor)
 
     def spot(x, z, s):
         return (x * n_tensor + z) * n_section + s
-
-    planes = range(n_shard)
-    layers = range(n_tensor)
 
     def scatter(value, source):
         moved_here = lax.ppermute(
@@ -553,16 +571,14 @@
         )
         return jnp.where(layer == source, value, moved_here)
 
-    near_2 = send(own, 2, 0)
-    near_1 = send(own, 1, 0)
-    over_0 = across(own, 0)
-    left_here = scatter(own, 0)
-    near_1, over_0 = lax.optimization_barrier((near_1, over_0))
-    left_here, near_2 = lax.optimization_barrier((left_here, near_2))
-    over_1 = across(near_1, 1)
-    near_3 = send(near_2, 1, 2)
-    over_2 = across(near_2, 2)
-    over_3 = across(near_3, 3)
+    hop_1 = send(own, [(0, 1), (3, 2)])
+    over_0 = across(own, [(0, 0), (1, 0), (0, 1), (0, 3), (1, 3)])
+    left_here = scatter(own, 2)
+    hop_1, over_0, left_here = lax.optimization_barrier((hop_1, over_0, left_here))
+    hop_2 = send(hop_1, [(1, 2), (2, 1)])
+    over_1 = across(hop_1, [(x, z) for x in planes for z in (1, 2)])
+    middle = jnp.where(shard == 0, own, over_0)
+    spread_0 = send(middle, [(1, 0)])
     left_there = lax.ppermute(
         left_here, everywhere, [(spot(x, t, t), spot(1 - x, t, t)) for x in planes for t in layers]
     )
@@ -579,39 +595,48 @@
     router_cols = learning_rate * jnp.einsum(
         "fn,cn->fc", router_right, own, preferred_element_type=jnp.float32
     )
-    router_there = lax.ppermute(router_cols, axes, [(n_tensor + 2, 2)])
-    router_cols = scatter(jnp.where(shard == 1, router_cols, router_there), 2)
+    router_there = across(router_cols, [(1, 1)])
+    router_cols = scatter(jnp.where(shard == 1, router_cols, router_there), 1)
     router_high = lax.reduce_precision(router_cols, 8, 7)
     codes = jnp.concatenate([router_high, router_cols - router_high], axis=0).astype(jnp.bfloat16)
-    codes = jnp.pad(codes, ((0, 0), (0, 2 * tokens_all - col_block))).reshape(-1, tokens_all)
-    bundle = jnp.concatenate([left_here, left_there, codes], axis=0)
-    bundle, over_1, near_3 = lax.optimization_barrier((bundle, over_1, near_3))
+    codes_tail = jnp.pad(codes[:, tokens_all:], ((0, 0), (0, 2 * tokens_all - col_block)))
+    bundle = jnp.concatenate([left_here, left_there, codes[:, :tokens_all], codes_tail], axis=0)
+
+    bundle, hop_2, over_1, spread_0, middle = lax.optimization_barrier(
+        (bundle, hop_2, over_1, spread_0, middle)
+    )
+    hop_3 = send(hop_2, [(1, 0), (2, 3)])
+    over_2 = across(hop_2, [(x, z) for x in planes for z in (1, 2)])
+    spread_2 = send(middle, [(1, 2)])
     to_side = [(spot(x, t, t), spot(x, t, t ^ 2)) for x in planes for t in layers]
     bundle = jnp.where(section == layer, bundle, lax.ppermute(bundle, everywhere, to_side))
-    bundle, over_2 = lax.optimization_barrier((bundle, over_2))
+    bundle, hop_3, over_2, spread_2 = lax.optimization_barrier((bundle, hop_3, over_2, spread_2))
+    over_3 = across(hop_3, [(x, z) for x in planes for z in (0, 3)])
+    spread_3 = send(spread_2, [(2, 3)])
     to_core = [
         (spot(x, t, t ^ a), spot(x, t, t ^ a ^ 1)) for x in planes for t in layers for a in (0, 2)
     ]
     bundle = jnp.where(
         (section ^ layer) % 2 == 0, bundle, lax.ppermute(bundle, everywhere, to_core)
     )
-    left_here = bundle[:col_block]
-    left_there = bundle[col_block : 2 * col_block]
-    codes = bundle[2 * col_block :].reshape(2 * EXPERTS, -1)[:, :col_block].astype(jnp.float32)
+    codes = bundle[2 * col_block :]
+    codes = jnp.concatenate(
+        [codes[: 2 * EXPERTS], codes[2 * EXPERTS :, : col_block - tokens_all]], axis=1
+    ).astype(jnp.float32)
     precond_router = codes[:EXPERTS] + codes[EXPERTS:]
 
-    def by_layer(options, factor):
-        chosen = options[factor ^ 3]
-        for index in (2, 1, 0):
-            chosen = jnp.where(layer == index, options[factor ^ index], chosen)
-        return chosen
-
-    mine = (own, near_1, near_2, near_3)
-    others = (over_0, over_1, over_2, over_3)
-    own_1, own_2, own_3 = (by_layer(mine, factor) for factor in (1, 2, 3))
-    other_1, other_2, other_3 = (by_layer(others, factor) for factor in (1, 2, 3))
-    precond_attn = attn_products(
-        shard, (left_here, left_there, own_1, own_2, own_3, other_1, other_2, other_3)
+    vocab_block = old_embed_diag.shape[0]
+    ids_here = layer * vocab_block + lax.iota(jnp.int32, vocab_block)
+    counts = jnp.sum((ids_here[:, None] == ids_all[None, :]).astype(jnp.float32), axis=1)
+    divisor = factor_decay * old_embed_diag + (1.0 - factor_decay) * (counts / tokens_all) + damping
+    precond_attn, precond_embed = output_products(
+        jnp.stack([shard, layer]),
+        bundle,
+        ids_all[None, :],
+        (learning_rate / divisor)[:, None],
+        (own, hop_1, hop_2, hop_3),
+        (over_0, over_1, over_2, over_3),
+        (spread_0, middle, spread_2, spread_3),
     )
 
     precond_norms = (
@@ -623,16 +648,6 @@
             + damping
         )
     )
-    vocab_block = old_embed_diag.shape[0]
-    ids_here = layer * vocab_block + lax.iota(jnp.int32, vocab_block)
-    matches = ids_here[:, None] == ids_all[None, :]
-    counts = jnp.sum(matches.astype(jnp.float32), axis=1)
-    divisor = factor_decay * old_embed_diag + (1.0 - factor_decay) * (counts / tokens_all) + damping
-    embed_grads = jnp.where(shard == 1, own_3, other_3)
-    embed_sum = jnp.einsum(
-        "vn,cn->vc", matches.astype(jnp.bfloat16), embed_grads, preferred_element_type=jnp.float32
-    )
-    precond_embed = embed_sum * (learning_rate / divisor)[:, None]
     return (precond_attn, precond_router, precond_norms, precond_embed)
 
 

time: 266 us -> 282 us (1.060)
  local copies, waits for them, and re-layouts: 23.8 us -> 34.2 us
  Pallas kernels: 25.9 us -> 30.7 us
  matrix products: 4.03 us -> 0.72 us
    all_gather x1, waiting for transfers between devices: 0.01 us -> 18.1 us  [layer_plan(): gathered = lax.all_gather(collected, 'section', axis=0)]
    ppermute x3 -> x6, waiting for transfers between devices: 27 us -> 9.28 us  [send(): return lax.ppermute(value, axes, moves)]
    ppermute x8 -> x0, starting transfers between devices: 13.2 us -> none  [the longest x7 12.5 us: layer_plan(): message = lax.ppermute(message, axes, moves)]
    unnamed x35 -> x64, local copies, waits for them, and re-layouts: 4.6 us -> 15.2 us
    ppermute x8 -> x0, waiting for transfers between devices: 9.92 us -> none  [the longest x7 9.92 us: layer_plan(): message = lax.ppermute(message, axes, moves)]
    ppermute x2, waiting for transfers between devices: 0.01 us -> 8.4 us  [scatter(): lax.ppermute(value, everywhere, [(spot(x, source, s), spot(x, s, s)) for...]
    ppermute x14 -> x17, starting transfers between devices: 13.6 us -> 21.4 us  [swap(): return lax.ppermute(value, axis, [(i, i ^ step) for i in range(size)])]
    pallas_call x1, Pallas kernels: 4.25 us -> 8.84 us  [output_products(): pl.pallas_call(functools.partial(output_kernel, attn_steps=4, vocab_block...]
  transfers between devices with their start and end apart: 35 -> 34, of which waited for: 14 -> 14; matrix products, arithmetic and copies ran while one was open for 12% -> 10% of each run, Pallas kernels for 3% -> 2%
where the time goes in v5:
time: 282 us; the launch traced here: 278 us
  waiting for transfers between devices  132 us (47%)
  starting transfers between devices  50.3 us (18%)
  local copies, waits for them, and re-layouts  34.2 us (12%)
  Pallas kernels  30.7 us (11%)
  between operations  16.2 us (6%)
  other arithmetic  13.8 us (5%)
    ppermute x17, waiting for transfers between devices, swap(): return lax.ppermute(value, axis, [(i, i ^ step) for i in range(size)])  65.7 us
    ppermute x17, starting transfers between devices, swap(): return lax.ppermute(value, axis, [(i, i ^ step) for i in range(size)])  21.4 us
    all_gather x1, waiting for transfers between devices, layer_plan(): gathered = lax.all_gather(collected, 'section', axis=0)  18.1 us
    pallas_call x3, Pallas kernels, chain_call(): pl.pallas_call(kernel, in_specs=[pl.BlockSpec(memory_space=pltpu.SMEM)] *...  15.5 us
    unnamed x64, local copies, waits for them, and re-layouts  15.2 us
    ppermute x5, waiting for transfers between devices, across(): return lax.ppermute(value, axes, moves)  13.7 us
    ppermute x1, waiting for transfers between devices, layer_plan(): lax.ppermute(bundle, everywhere, to_side)  10.5 us
    ppermute x6, waiting for transfers between devices, send(): return lax.ppermute(value, axes, moves)  9.28 us
  transfers between devices with their start and end apart: 34, of which 14 were waited for; matrix products, arithmetic and copies ran while one was open for 10% of the time, Pallas kernels for 2%

profile of v5, /device:TPU:0, one launch (start us, length us, event | category | flops | bytes accessed | tf_op | source)
XLA Modules:
  0.0 278.4 jit_solution(12609564457289789644)
XLA Ops:
  7.3 4.2 %fusion.6 = (bf16[576,576]{1,0:T(8,128)(2,1)}, bf16[576,576]{1,0:T(8,128)(2,1)}, bf16[576,576]{1,0:T(8,128)(2,1)S(1)}, bf16[576,576]{1,0:T(8,128)(2,1)}) fusion(f32[4,576,576]{2,1,0:T(8,128)} %param.12, s32[]{:T(128)S(6)} %select_n.187, s32[]{:T(128)S(6)} %select_n.175, s32[]{:T(128)S(6)} %select_n.184, s32[]{:T(128)S(6)} %select_n.181), kind=kLoop, calls=%fused_computation.21 | loop fusion | bytes 5308432 | tf_op jit(solution)/shard_map/convert_element_type | solution.py:467
  11.5 4.0 %collective-permute-start.4 = (bf16[576,576]{1,0:T(8,128)(2,1)S(1)}, bf16[576,576]{1,0:T(8,128)(2,1)S(1)}, u32[]{:S(2)}, u32[]{:S(2)}) collective-permute-start(bf16[576,576]{1,0:T(8,128)(2,1)S(1)} %get-tuple-element.92), channel_id=1, source_target_pairs={{0,8},{4,12},{8,0},{12,4},{1,9},{5,13},{9,1},{13,5},{2,10},{6,14},... | collective-permute-start | bytes 1990664 | tf_op jit(solution)/shard_map/ppermute | solution.py:169
  19.7 4.4 %collective-permute-done = bf16[4,144,256]{2,1,0:T(8,128)(2,1)S(1)} collective-permute-done((bf16[4,144,256]{2,1,0:T(8,128)(2,1)S(1)}, bf16[4,144,256]{2,1,0:T(8,128)(2,1)S(1)}, u32[]{:S(2)}, u32[]{:S(2)}) %collective-permute-start) | collective-permute-done | bytes 294944 | tf_op jit(solution)/shard_map/ppermute | solution.py:169
  28.8 7.0 %collective-permute-done.1 = bf16[304,256]{1,0:T(8,128)(2,1)S(1)} collective-permute-done((bf16[304,256]{1,0:T(8,128)(2,1)S(1)}, bf16[304,256]{1,0:T(8,128)(2,1)S(1)}, u32[]{:S(2)}, u32[]{:S(2)}) %collective-permute-start.1) | collective-permute-done | bytes 155680 | tf_op jit(solution)/shard_map/ppermute | solution.py:169
  35.8 22.8 %collective-permute-done.2 = bf16[304,256]{1,0:T(8,128)(2,1)S(1)} collective-permute-done((bf16[304,256]{1,0:T(8,128)(2,1)S(1)}, bf16[304,256]{1,0:T(8,128)(2,1)S(1)}, u32[]{:S(2)}, u32[]{:S(2)}) %collective-permute-start.2) | collective-permute-done | bytes 155680 | tf_op jit(solution)/shard_map/ppermute | solution.py:169
  69.3 18.1 %all-gather.3.cloned.1.call-done = bf16[16,304,256]{2,1,0:T(8,128)(2,1)} async-done(((bf16[4,304,256]{2,1,0:T(8,128)(2,1)}), bf16[16,304,256]{2,1,0:T(8,128)(2,1)}) %all-gather.3.cloned.1.call-update) | async-done | bytes 2490384 | tf_op jit(solution)/shard_map/all_gather | solution.py:488
  100.0 3.3 %concatenate.97.rows = bf16[256,2304]{1,0:T(8,128)(2,1)} concatenate(bf16[256,576]{1,0:T(8,128)(2,1)S(1)} %bitcast.122, bf16[256,576]{1,0:T(8,128)(2,1)} %bitcast.123, bf16[256,576]{1,0:T(8,128)(2,1)} %bitcast.124, bf16[256,576]{1,0:T(8,128)(2,1)} %bitcast.125), dimensions={1} | concatenate | bytes 2359296 | tf_op jit(solution)/shard_map/concatenate | solution.py:523
  116.4 4.2 %shard_map.115 = (f32[2,256,576]{2,1,0:T(8,128)S(1)}, bf16[256,1152]{1,0:T(8,128)(2,1)S(1)}) custom-call(s32[1]{0:T(128)} %bitcast.2.place_ref, f32[1]{0:T(128)} %bitcast.35.scale_ref, bf16[256,2304]{1,0:T(8,128)(2,1)S(1)} %copy-done.1, f32[4,1,576]{2,1,0:T(1,128)S(1)} %add_reduce-precision_fusion.diag, bf16[576,576]{1,0:T(8,128)(2,1)} %shard_map.111.refs_0_, ...), custom_call_target="tpu_custom_call" | custom-call | flops 1358954496 | bytes 5308416 | tf_op jit(solution)/shard_map/pallas_call | solution.py:314
  121.1 15.2 %collective-permute-done.14.theirs = bf16[256,1152]{1,0:T(8,128)(2,1)S(1)} collective-permute-done((bf16[256,1152]{1,0:T(8,128)(2,1)S(1)}, bf16[256,1152]{1,0:T(8,128)(2,1)S(1)}, u32[]{:S(2)}, u32[]{:S(2)}) %collective-permute-start.14) | collective-permute-done | bytes 589856 | tf_op jit(solution)/shard_map/ppermute | solution.py:169
  136.2 6.1 %shard_map.116 = (f32[2,256,576]{2,1,0:T(8,128)S(1)}, bf16[256,1152]{1,0:T(8,128)(2,1)}) custom-call(s32[1]{0:T(128)} %bitcast.2.place_ref, f32[1]{0:T(128)} %bitcast.35.scale_ref, bf16[256,1152]{1,0:T(8,128)(2,1)S(1)} %get-tuple-element.37.mine, bf16[256,1152]{1,0:T(8,128)(2,1)S(1)} %collective-permute-done.14.theirs, bf16[256,2304]{1,0:T(8,128)(2,1)S(1)} %copy-done.1, ...), custom_call_target="tpu_custom_call" | custom-call | flops 1358954496 | bytes 5308416 | tf_op jit(solution)/shard_map/pallas_call | solution.py:314
  142.7 14.7 %collective-permute-done.15.theirs = bf16[256,1152]{1,0:T(8,128)(2,1)} collective-permute-done((bf16[256,1152]{1,0:T(8,128)(2,1)}, bf16[256,1152]{1,0:T(8,128)(2,1)}, u32[]{:S(2)}, u32[]{:S(2)}) %collective-permute-start.15) | collective-permute-done | bytes 589856 | tf_op jit(solution)/shard_map/ppermute | solution.py:169
  157.4 5.2 %shard_map.117 = (bf16[576,256]{1,0:T(8,128)(2,1)S(1)}, bf16[576,256]{1,0:T(8,128)(2,1)S(1)}) custom-call(s32[1]{0:T(128)} %bitcast.2.place_ref, f32[1]{0:T(128)} %bitcast.35.scale_ref, bf16[256,1152]{1,0:T(8,128)(2,1)} %get-tuple-element.39.mine, bf16[256,1152]{1,0:T(8,128)(2,1)} %collective-permute-done.15.theirs, ...), custom_call_target="tpu_custom_call" | custom-call | flops 1358954496 | bytes 5308416 | tf_op jit(solution)/shard_map/pallas_call | solution.py:314
  169.2 3.4 %collective-permute-start.18 = (bf16[576,512]{1,0:T(8,128)(2,1)S(1)}, bf16[576,512]{1,0:T(8,128)(2,1)S(1)}, u32[]{:S(2)}, u32[]{:S(2)}) collective-permute-start(bf16[576,512]{1,0:T(8,128)(2,1)S(1)} %maximum_select_fusion.refs_0_), channel_id=1, source_target_pairs={{0,16},{16,0},{4,20},{12,28},{28,12},{1,17},{17,1},{5,21},{13,29},... | collective-permute-start | bytes 1769480 | tf_op jit(solution)/shard_map/ppermute | solution.py:557
  175.0 8.4 %collective-permute-done.19 = bf16[576,512]{1,0:T(8,128)(2,1)S(1)} collective-permute-done((bf16[576,512]{1,0:T(8,128)(2,1)S(1)}, bf16[576,512]{1,0:T(8,128)(2,1)S(1)}, u32[]{:S(2)}, u32[]{:S(2)}) %collective-permute-start.19) | collective-permute-done | bytes 589856 | tf_op jit(solution)/shard_map/ppermute | solution.py:567
  183.5 3.7 %collective-permute-done.18.refs_4_ = bf16[576,512]{1,0:T(8,128)(2,1)S(1)} collective-permute-done((bf16[576,512]{1,0:T(8,128)(2,1)S(1)}, bf16[576,512]{1,0:T(8,128)(2,1)S(1)}, u32[]{:S(2)}, u32[]{:S(2)}) %collective-permute-start.18) | collective-permute-done | bytes 589856 | tf_op jit(solution)/shard_map/ppermute | solution.py:557
  188.6 3.4 %collective-permute-start.20 = (bf16[576,512]{1,0:T(8,128)(2,1)S(1)}, bf16[576,512]{1,0:T(8,128)(2,1)S(1)}, u32[]{:S(2)}, u32[]{:S(2)}) collective-permute-start(bf16[576,512]{1,0:T(8,128)(2,1)S(1)} %broadcast_select_fusion.3), channel_id=1, source_target_pairs={{0,16},{5,21},{10,26},{15,31},{16,0},{21,5},{26,10},{31,15}} | collective-permute-start | bytes 1769480 | tf_op jit(solution)/shard_map/ppermute | solution.py:582
  193.6 6.7 %collective-permute-done.20 = bf16[576,512]{1,0:T(8,128)(2,1)S(1)} collective-permute-done((bf16[576,512]{1,0:T(8,128)(2,1)S(1)}, bf16[576,512]{1,0:T(8,128)(2,1)S(1)}, u32[]{:S(2)}, u32[]{:S(2)}) %collective-permute-start.20) | collective-permute-done | bytes 589856 | tf_op jit(solution)/shard_map/ppermute | solution.py:582
  201.5 7.6 %collective-permute-done.25.refs_8_ = bf16[576,512]{1,0:T(8,128)(2,1)S(1)} collective-permute-done((bf16[576,512]{1,0:T(8,128)(2,1)S(1)}, bf16[576,512]{1,0:T(8,128)(2,1)S(1)}, u32[]{:S(2)}, u32[]{:S(2)}) %collective-permute-start.25) | collective-permute-done | bytes 589856 | tf_op jit(solution)/shard_map/ppermute | solution.py:553
  215.9 10.5 %collective-permute-done.26 = bf16[1184,512]{1,0:T(8,128)(2,1)} collective-permute-done((bf16[1184,512]{1,0:T(8,128)(2,1)}, bf16[1184,512]{1,0:T(8,128)(2,1)}, u32[]{:S(2)}, u32[]{:S(2)}) %collective-permute-start.26) | collective-permute-done | bytes 1212448 | tf_op jit(solution)/shard_map/ppermute | solution.py:612
  231.4 3.6 %collective-permute-start.30 = (bf16[1184,512]{1,0:T(8,128)(2,1)}, bf16[1184,512]{1,0:T(8,128)(2,1)}, u32[]{:S(2)}, u32[]{:S(2)}) collective-permute-start(bf16[1184,512]{1,0:T(8,128)(2,1)} %broadcast_select_fusion), channel_id=1, source_target_pairs={{0,1},{2,3},{5,4},{7,6},{10,11},{8,9},{15,14},{13,12},{16,17},{18,... | collective-permute-start | bytes 3637256 | tf_op jit(solution)/shard_map/ppermute | solution.py:620
  236.9 3.7 %collective-permute-start.31 = (bf16[576,512]{1,0:T(8,128)(2,1)}, bf16[576,512]{1,0:T(8,128)(2,1)S(1)}, u32[]{:S(2)}, u32[]{:S(2)}) collective-permute-start(bf16[576,512]{1,0:T(8,128)(2,1)} %collective-permute-done.27.refs_3_), channel_id=1, source_target_pairs={{0,16},{12,28},{16,0},{28,12},{1,17},{13,29},{17,1},{29,13},{2,18}... | collective-permute-start | bytes 1769480 | tf_op jit(solution)/shard_map/ppermute | solution.py:557
  242.8 10.0 %collective-permute-done.31.refs_7_ = bf16[576,512]{1,0:T(8,128)(2,1)S(1)} collective-permute-done((bf16[576,512]{1,0:T(8,128)(2,1)}, bf16[576,512]{1,0:T(8,128)(2,1)S(1)}, u32[]{:S(2)}, u32[]{:S(2)}) %collective-permute-start.31) | collective-permute-done | bytes 589856 | tf_op jit(solution)/shard_map/ppermute | solution.py:557
  254.0 8.8 %shard_map.118 = (f32[4,576,576]{2,1,0:T(8,128)}, f32[2048,576]{1,0:T(8,128)S(1)}) custom-call(s32[2]{0:T(128)S(1)} %pad_add_fusion.where_ref, bf16[1184,512]{1,0:T(8,128)(2,1)S(1)} %broadcast_select_fusion.1.left_mine.left_other, bf16[1184,512]{1,0:T(8,128)(2,1)S(1)} %broadcast_select_fusion.1.left_mine.left_other, s32[1,512]{1,0:T(1,128)S(1)} %bitcast.116, ...), custom_call_target="tpu_custom_call" | custom-call | flops 2566914048 | bytes 14155776 | tf_op jit(solution)/shard_map/pallas_call | solution.py:402
  265.2 5.7 %copy.44 = f32[2048,576]{0,1:T(8,128)} copy(f32[2048,576]{1,0:T(8,128)} %copy-done.2) | data formatting | bytes 9437184
  (190 shorter events, 77.3 us)
Async XLA Ops:
  7.2 80.2 %all-gather.3.cloned.1.call-start = ((), (), s32[]{:S(2)}) async-start(), calls=%async_computation | async-start | bytes 3112960 | tf_op jit(solution)/shard_map/all_gather | solution.py:488
  11.5 48.1 %collective-permute-start.4 = (bf16[576,576]{1,0:T(8,128)(2,1)S(1)}, bf16[576,576]{1,0:T(8,128)(2,1)S(1)}, u32[]{:S(2)}, u32[]{:S(2)}) collective-permute-start(bf16[576,576]{1,0:T(8,128)(2,1)S(1)} %get-tuple-element.92), channel_id=1, source_target_pairs={{0,8},{4,12},{8,0},{12,4},{1,9},{5,13},{9,1},{13,5},{2,10},{6,14},... | collective-permute-start | bytes 1990664 | tf_op jit(solution)/shard_map/ppermute | solution.py:169
  24.1 11.7 %collective-permute-start.1 = (bf16[304,256]{1,0:T(8,128)(2,1)S(1)}, bf16[304,256]{1,0:T(8,128)(2,1)S(1)}, u32[]{:S(2)}, u32[]{:S(2)}) collective-permute-start(bf16[304,256]{1,0:T(8,128)(2,1)S(1)} %pad_maximum_fusion.2), channel_id=1, source_target_pairs={{0,4},{4,0},{8,12},{12,8},{1,5},{5,1},{9,13},{13,9},{2,6},{6,2},{1... | collective-permute-start | bytes 466952 | tf_op jit(solution)/shard_map/ppermute | solution.py:169
  25.8 32.8 %collective-permute-start.2 = (bf16[304,256]{1,0:T(8,128)(2,1)S(1)}, bf16[304,256]{1,0:T(8,128)(2,1)S(1)}, u32[]{:S(2)}, u32[]{:S(2)}) collective-permute-start(bf16[304,256]{1,0:T(8,128)(2,1)S(1)} %pad_maximum_fusion.3), channel_id=1, source_target_pairs={{0,8},{4,12},{8,0},{12,4},{1,9},{5,13},{9,1},{13,5},{2,10},{6,14},... | collective-permute-start | bytes 466952 | tf_op jit(solution)/shard_map/ppermute | solution.py:169
  26.3 32.4 %collective-permute-start.3 = (bf16[304,256]{1,0:T(8,128)(2,1)S(1)}, bf16[304,256]{1,0:T(8,128)(2,1)S(1)}, u32[]{:S(2)}, u32[]{:S(2)}) collective-permute-start(bf16[304,256]{1,0:T(8,128)(2,1)S(1)} %pad_maximum_fusion.4), channel_id=1, source_target_pairs={{0,12},{4,8},{8,4},{12,0},{1,13},{5,9},{9,5},{13,1},{2,14},{6,10},... | collective-permute-start | bytes 466952 | tf_op jit(solution)/shard_map/ppermute | solution.py:169
  63.9 39.5 %collective-permute-start.9 = (bf16[576,576]{1,0:T(8,128)(2,1)}, bf16[576,576]{1,0:T(8,128)(2,1)S(1)}, u32[]{:S(2)}, u32[]{:S(2)}) collective-permute-start(bf16[576,576]{1,0:T(8,128)(2,1)} %get-tuple-element.90), channel_id=1, source_target_pairs={{0,12},{4,8},{8,4},{12,0},{1,13},{5,9},{9,5},{13,1},{2,14},{6,10},... | collective-permute-start | bytes 1990664 | tf_op jit(solution)/shard_map/ppermute | solution.py:169
  66.3 42.0 %collective-permute-start.8 = (bf16[576,576]{1,0:T(8,128)(2,1)}, bf16[576,576]{1,0:T(8,128)(2,1)}, u32[]{:S(2)}, u32[]{:S(2)}) collective-permute-start(bf16[576,576]{1,0:T(8,128)(2,1)} %get-tuple-element.93), channel_id=1, source_target_pairs={{0,4},{4,0},{8,12},{12,8},{1,5},{5,1},{9,13},{13,9},{2,6},{6,2},{1... | collective-permute-start | bytes 1990664 | tf_op jit(solution)/shard_map/ppermute | solution.py:169
  120.7 15.5 %collective-permute-start.14 = (bf16[256,1152]{1,0:T(8,128)(2,1)S(1)}, bf16[256,1152]{1,0:T(8,128)(2,1)S(1)}, u32[]{:S(2)}, u32[]{:S(2)}) collective-permute-start(bf16[256,1152]{1,0:T(8,128)(2,1)S(1)} %get-tuple-element.37.mine), channel_id=1, source_target_pairs={{0,2},{1,3},{2,0},{3,1},{4,6},{5,7},{6,4},{7,5},{8,10},{9,11},{10,... | collective-permute-start | bytes 1769480 | tf_op jit(solution)/shard_map/ppermute | solution.py:169
  142.3 15.0 %collective-permute-start.15 = (bf16[256,1152]{1,0:T(8,128)(2,1)}, bf16[256,1152]{1,0:T(8,128)(2,1)}, u32[]{:S(2)}, u32[]{:S(2)}) collective-permute-start(bf16[256,1152]{1,0:T(8,128)(2,1)} %get-tuple-element.39.mine), channel_id=1, source_target_pairs={{0,2},{1,3},{2,0},{3,1},{4,6},{5,7},{6,4},{7,5},{8,10},{9,11},{10,... | collective-permute-start | bytes 1769480 | tf_op jit(solution)/shard_map/ppermute | solution.py:169
  164.9 18.5 %collective-permute-start.19 = (bf16[576,512]{1,0:T(8,128)(2,1)S(1)}, bf16[576,512]{1,0:T(8,128)(2,1)S(1)}, u32[]{:S(2)}, u32[]{:S(2)}) collective-permute-start(bf16[576,512]{1,0:T(8,128)(2,1)S(1)} %maximum_select_fusion.refs_0_), channel_id=1, source_target_pairs={{8,0},{9,5},{11,15},{24,16},{25,21},{27,31}} | collective-permute-start | bytes 1769480 | tf_op jit(solution)/shard_map/ppermute | solution.py:567
  166.4 17.0 %collective-permute-start.17 = (bf16[576,512]{1,0:T(8,128)(2,1)S(1)}, bf16[576,512]{1,0:T(8,128)(2,1)S(1)}, u32[]{:S(2)}, u32[]{:S(2)}) collective-permute-start(bf16[576,512]{1,0:T(8,128)(2,1)S(1)} %maximum_select_fusion.refs_0_), channel_id=1, source_target_pairs={{0,4},{12,8},{16,20},{28,24},{1,5},{13,9},{17,21},{29,25},{2,6},{1... | collective-permute-start | bytes 1769480 | tf_op jit(solution)/shard_map/ppermute | solution.py:553
  169.2 17.9 %collective-permute-start.18 = (bf16[576,512]{1,0:T(8,128)(2,1)S(1)}, bf16[576,512]{1,0:T(8,128)(2,1)S(1)}, u32[]{:S(2)}, u32[]{:S(2)}) collective-permute-start(bf16[576,512]{1,0:T(8,128)(2,1)S(1)} %maximum_select_fusion.refs_0_), channel_id=1, source_target_pairs={{0,16},{16,0},{4,20},{12,28},{28,12},{1,17},{17,1},{5,21},{13,29},... | collective-permute-start | bytes 1769480 | tf_op jit(solution)/shard_map/ppermute | solution.py:557
  173.7 19.9 %collective-permute-start.22 = (f32[8,576]{1,0:T(8,128)S(1)}, f32[8,576]{1,0:T(8,128)S(1)}, u32[]{:S(2)}, u32[]{:S(2)}) collective-permute-start(f32[8,576]{1,0:T(8,128)S(1)} %broadcast_select_fusion.4), channel_id=1, source_target_pairs={{4,0},{6,10},{7,15},{20,16},{22,26},{23,31}} | collective-permute-start | bytes 55304 | tf_op jit(solution)/shard_map/ppermute | solution.py:567
  187.2 22.7 %collective-permute-start.23 = (bf16[576,512]{1,0:T(8,128)(2,1)S(1)}, bf16[576,512]{1,0:T(8,128)(2,1)S(1)}, u32[]{:S(2)}, u32[]{:S(2)}) collective-permute-start(bf16[576,512]{1,0:T(8,128)(2,1)S(1)} %collective-permute-done.17.refs_1_), channel_id=1, source_target_pairs={{4,8},{8,4},{20,24},{24,20},{5,9},{9,5},{21,25},{25,21},{6,10},{10... | collective-permute-start | bytes 1769480 | tf_op jit(solution)/shard_map/ppermute | solution.py:553
  187.9 22.0 %collective-permute-start.24 = (bf16[576,512]{1,0:T(8,128)(2,1)S(1)}, bf16[576,512]{1,0:T(8,128)(2,1)S(1)}, u32[]{:S(2)}, u32[]{:S(2)}) collective-permute-start(bf16[576,512]{1,0:T(8,128)(2,1)S(1)} %collective-permute-done.17.refs_1_), channel_id=1, source_target_pairs={{4,20},{8,24},{20,4},{24,8},{5,21},{9,25},{21,5},{25,9},{6,22},{10... | collective-permute-start | bytes 1769480 | tf_op jit(solution)/shard_map/ppermute | solution.py:557
  188.6 11.8 %collective-permute-start.20 = (bf16[576,512]{1,0:T(8,128)(2,1)S(1)}, bf16[576,512]{1,0:T(8,128)(2,1)S(1)}, u32[]{:S(2)}, u32[]{:S(2)}) collective-permute-start(bf16[576,512]{1,0:T(8,128)(2,1)S(1)} %broadcast_select_fusion.3), channel_id=1, source_target_pairs={{0,16},{5,21},{10,26},{15,31},{16,0},{21,5},{26,10},{31,15}} | collective-permute-start | bytes 1769480 | tf_op jit(solution)/shard_map/ppermute | solution.py:582
  192.0 17.0 %collective-permute-start.25 = (bf16[576,512]{1,0:T(8,128)(2,1)S(1)}, bf16[576,512]{1,0:T(8,128)(2,1)S(1)}, u32[]{:S(2)}, u32[]{:S(2)}) collective-permute-start(bf16[576,512]{1,0:T(8,128)(2,1)S(1)} %broadcast_select_fusion.2.refs_9_), channel_id=1, source_target_pairs={{4,0},{20,16},{5,1},{21,17},{6,2},{22,18},{7,3},{23,19}} | collective-permute-start | bytes 1769480 | tf_op jit(solution)/shard_map/ppermute | solution.py:553
  210.7 15.7 %collective-permute-start.26 = (bf16[1184,512]{1,0:T(8,128)(2,1)}, bf16[1184,512]{1,0:T(8,128)(2,1)}, u32[]{:S(2)}, u32[]{:S(2)}) collective-permute-start(bf16[1184,512]{1,0:T(8,128)(2,1)} %pad_maximum_fusion), channel_id=1, source_target_pairs={{0,2},{5,7},{10,8},{15,13},{16,18},{21,23},{26,24},{31,29}} | collective-permute-start | bytes 3637256 | tf_op jit(solution)/shard_map/ppermute | solution.py:612
  213.1 17.4 %collective-permute-start.27 = (bf16[576,512]{1,0:T(8,128)(2,1)S(1)}, bf16[576,512]{1,0:T(8,128)(2,1)}, u32[]{:S(2)}, u32[]{:S(2)}) collective-permute-start(bf16[576,512]{1,0:T(8,128)(2,1)S(1)} %collective-permute-done.23.refs_2_), channel_id=1, source_target_pairs={{4,0},{8,12},{20,16},{24,28},{5,1},{9,13},{21,17},{25,29},{6,2},{1... | collective-permute-start | bytes 1769480 | tf_op jit(solution)/shard_map/ppermute | solution.py:553
  214.5 16.0 %collective-permute-start.28 = (bf16[576,512]{1,0:T(8,128)(2,1)S(1)}, bf16[576,512]{1,0:T(8,128)(2,1)S(1)}, u32[]{:S(2)}, u32[]{:S(2)}) collective-permute-start(bf16[576,512]{1,0:T(8,128)(2,1)S(1)} %collective-permute-done.23.refs_2_), channel_id=1, source_target_pairs={{4,20},{8,24},{20,4},{24,8},{5,21},{9,25},{21,5},{25,9},{6,22},{10... | collective-permute-start | bytes 1769480 | tf_op jit(solution)/shard_map/ppermute | solution.py:557
  215.2 15.3 %collective-permute-start.29 = (bf16[576,512]{1,0:T(8,128)(2,1)S(1)}, bf16[576,512]{1,0:T(8,128)(2,1)S(1)}, u32[]{:S(2)}, u32[]{:S(2)}) collective-permute-start(bf16[576,512]{1,0:T(8,128)(2,1)S(1)} %broadcast_select_fusion.2.refs_9_), channel_id=1, source_target_pairs={{4,8},{20,24},{5,9},{21,25},{6,10},{22,26},{7,11},{23,27}} | collective-permute-start | bytes 1769480 | tf_op jit(solution)/shard_map/ppermute | solution.py:553
  231.4 9.9 %collective-permute-start.30 = (bf16[1184,512]{1,0:T(8,128)(2,1)}, bf16[1184,512]{1,0:T(8,128)(2,1)}, u32[]{:S(2)}, u32[]{:S(2)}) collective-permute-start(bf16[1184,512]{1,0:T(8,128)(2,1)} %broadcast_select_fusion), channel_id=1, source_target_pairs={{0,1},{2,3},{5,4},{7,6},{10,11},{8,9},{15,14},{13,12},{16,17},{18,... | collective-permute-start | bytes 3637256 | tf_op jit(solution)/shard_map/ppermute | solution.py:620
  236.9 16.0 %collective-permute-start.31 = (bf16[576,512]{1,0:T(8,128)(2,1)}, bf16[576,512]{1,0:T(8,128)(2,1)S(1)}, u32[]{:S(2)}, u32[]{:S(2)}) collective-permute-start(bf16[576,512]{1,0:T(8,128)(2,1)} %collective-permute-done.27.refs_3_), channel_id=1, source_target_pairs={{0,16},{12,28},{16,0},{28,12},{1,17},{13,29},{17,1},{29,13},{2,18}... | collective-permute-start | bytes 1769480 | tf_op jit(solution)/shard_map/ppermute | solution.py:557
  240.6 12.3 %collective-permute-start.32 = (bf16[576,512]{1,0:T(8,128)(2,1)}, bf16[576,512]{1,0:T(8,128)(2,1)S(1)}, u32[]{:S(2)}, u32[]{:S(2)}) collective-permute-start(bf16[576,512]{1,0:T(8,128)(2,1)} %copy-done.20), channel_id=1, source_target_pairs={{8,12},{24,28},{9,13},{25,29},{10,14},{26,30},{11,15},{27,31}} | collective-permute-start | bytes 1769480 | tf_op jit(solution)/shard_map/ppermute | solution.py:553
  (40 other events, 464.3 us)
Sparse Core Ops, SparseCore 0:
  59.7 27.6 all-gather.2

commit v6 on v5

--- a/solution.py
+++ b/solution.py
@@ -187,6 +187,71 @@
     return pltpu.CompilerParams(vmem_limit_bytes=40 * 1024 * 1024)
 
 
+def layout_kernel(place_ref, gathered, features, rows, low_diag, trace, old, *, weight):
+    own_place, layer, core = place_ref[0], place_ref[1], place_ref[2]
+    sections, steps, _, tokens = gathered.shape
+    groups, depth, _ = features.shape
+    part = depth // (sections * steps)
+    width = depth // steps
+    for section in range(sections):
+        codes = jnp.zeros((16, tokens), jnp.float32)
+        for step in range(steps):
+            start = (step * sections + section) * part
+            for group in range(groups):
+                features[group, start : start + part] = gathered[
+                    section, step, group * part : (group + 1) * part
+                ]
+            codes += gathered[section, step, groups * part :].astype(jnp.float32)
+        codes = codes[0:3] + codes[3:6] + codes[6:9]
+        pieces = [codes[0:1], codes[1:2], codes[2:3, : width - 2 * tokens]]
+        old[section ^ layer] = jnp.concatenate(pieces, axis=1)
+    ones = jnp.ones((8, tokens), jnp.bfloat16)
+    total = jnp.float32(0.0)
+    for step in range(steps):
+        squares = jnp.zeros((8, width), jnp.float32)
+        for group in range(groups):
+            values = features[group, step * width : (step + 1) * width].astype(jnp.float32)
+            values = values * values
+            high = values.astype(jnp.bfloat16)
+            low = (values - high.astype(jnp.float32)).astype(jnp.bfloat16)
+            for piece in (high, low):
+                squares += lax.dot_general(
+                    ones, piece, (((1,), (1,)), ((), ())), preferred_element_type=jnp.float32
+                )
+        diag = factor_decay * old[step] + weight * squares[0:1] + damping
+        total += jnp.sum(diag)
+        low_diag[step] = rounded(diag)
+        start = pl.multiple_of((own_place ^ step) * width, width)
+        mine = features[core, pl.ds(start, width)]
+        rows[:, step * width : (step + 1) * width] = mine.T
+    trace[0] = total
+
+
+def lay_out(places, gathered, weight):
+    sections, steps, height, tokens = gathered.shape
+    part = (height - 16) // 2
+    depth = sections * steps * part
+    width = depth // steps
+    vmem = pl.BlockSpec(memory_space=pltpu.VMEM)
+    smem = pl.BlockSpec(memory_space=pltpu.SMEM)
+    return pl.pallas_call(
+        functools.partial(layout_kernel, weight=weight),
+        in_specs=[smem, vmem],
+        out_specs=[vmem, vmem, vmem, smem],
+        out_shape=[
+            jax.ShapeDtypeStruct((2, depth, tokens), jnp.bfloat16),
+            jax.ShapeDtypeStruct((tokens, depth), jnp.bfloat16),
+            jax.ShapeDtypeStruct((steps, 1, width), jnp.float32),
+            jax.ShapeDtypeStruct((1,), jnp.float32),
+        ],
+        scratch_shapes=[pltpu.VMEM((steps, 1, width), jnp.float32)],
+        compiler_params=params(),
+        cost_estimate=pl.CostEstimate(
+            flops=64 * depth * tokens, bytes_accessed=14 * depth * tokens, transcendentals=0
+        ),
+    )(places, gathered)
+
+
 def factor_kernel(place_ref, part, own, old, diag, out, *, step, weight):
     fresh = jnp.zeros(out.shape, jnp.float32)
     for index in range(part.shape[0]):
@@ -315,7 +380,7 @@
         kernel,
         in_specs=[pl.BlockSpec(memory_space=pltpu.SMEM)] * len(scalars)
         + [vmem] * len(arrays)
-        + [pl.BlockSpec(memory_space=pl.ANY)] * len(blocks),
+        + [pl.BlockSpec(memory_space=pltpu.HBM)] * len(blocks),
         out_specs=[vmem] * len(out_shape),
         out_shape=out_shape,
         scratch_shapes=[
@@ -331,92 +396,77 @@
     )(*scalars, *arrays, *blocks)
 
 
-def output_kernel(
-    where_ref, left_mine, left_other, ids, scale, *refs, attn_steps, vocab_block
-):
-    mine, others, spread = refs[:4], refs[4:8], refs[8:12]
-    attn, embed, held, sems = refs[12:]
+def output_kernel(where_ref, left_mine, left_other, ids, scale, *refs, vocab_block):
+    mine, others = refs[:4], refs[4:8]
+    attn, embed, held, sems = refs[8:]
     shard, layer, step = where_ref[0], where_ref[1], pl.program_id(0)
     first = shard == 0
 
-    def fetch(slot, from_mine, index):
-        for place in range(4):
-            for group, wanted in ((mine, from_mine), (others, jnp.logical_not(from_mine))):
-
-                @pl.when(wanted & (index == place))
-                def _():
-                    pltpu.make_async_copy(group[place], held.at[slot], sems.at[slot]).start()
-
     @pl.when(step == 0)
     def _():
-        fetch(0, first, layer)
-        for place in range(4):
-
-            @pl.when(layer == place)
-            def _():
-                pltpu.make_async_copy(spread[place], held.at[1], sems.at[1]).start()
-
-        fetch(2, first, 3 - layer)
-        fetch(3, jnp.logical_not(first), layer)
-        fetch(4, jnp.logical_not(first), 3 - layer)
+        for slot, source in enumerate((0, 1, 3, 0, 3)):
+            from_mine = first if slot < 3 else jnp.logical_not(first)
+            for place in range(4):
+                for group, wanted in ((mine, from_mine), (others, jnp.logical_not(from_mine))):
+
+                    @pl.when(wanted & ((layer ^ source) == place))
+                    def _():
+                        pltpu.make_async_copy(group[place], held.at[slot], sems.at[slot]).start()
 
     def arrived(slot):
         pltpu.make_async_copy(mine[0], held.at[slot], sems.at[slot]).wait()
         return held[slot]
 
-    def product(left, right):
-        return lax.dot_general(
-            left, right, (((1,), (1,)), ((), ())), preferred_element_type=jnp.float32
-        )
-
-    for slot in range(attn_steps):
+    for slot in range(4):
 
         @pl.when(step == slot)
         def _():
             same = first if slot < 3 else jnp.logical_not(first)
             left = jnp.where(same, left_mine[...], left_other[...])
-            attn[0] = learning_rate * product(left, arrived(slot))
-
-    @pl.when(step == attn_steps)
+            attn[0] = learning_rate * lax.dot_general(
+                left, arrived(slot), (((1,), (1,)), ((), ())), preferred_element_type=jnp.float32
+            )
+
+    @pl.when(step == 4)
     def _():
         arrived(4)
 
-    @pl.when(step >= attn_steps)
+    @pl.when(step >= 4)
     def _():
-        rows = embed.shape[0]
-        start = layer * vocab_block + (step - attn_steps) * rows
-        here = lax.broadcasted_iota(jnp.int32, (rows, ids.shape[1]), 0) + start
+        cols = embed.shape[1]
+        start = layer * vocab_block + (step - 4) * cols
+        here = lax.broadcasted_iota(jnp.int32, (ids.shape[0], cols), 1) + start
         matches = (here == ids[...]).astype(jnp.float32).astype(jnp.bfloat16)
-        embed[...] = product(matches, held[4]) * scale[...]
-
-
-def output_products(where, bundle, ids, scale, mine, others, spread):
+        embed[...] = jnp.dot(held[4], matches, preferred_element_type=jnp.float32) * scale[...]
+
+
+def output_products(where, bundle, ids, scale, mine, others):
     cols, tokens_all = mine[0].shape
-    vocab_block = scale.shape[0]
+    vocab_block = scale.shape[1]
     parts = 4
-    rows = vocab_block // parts
+    part = vocab_block // parts
 
     def embed_place(step):
-        return (jnp.maximum(step - 4, 0), 0)
+        return (0, jnp.maximum(step - 4, 0))
 
     return pl.pallas_call(
-        functools.partial(output_kernel, attn_steps=4, vocab_block=vocab_block),
+        functools.partial(output_kernel, vocab_block=vocab_block),
         grid=(4 + parts,),
         out_shape=(
             jax.ShapeDtypeStruct((4, cols, cols), jnp.float32),
-            jax.ShapeDtypeStruct((vocab_block, cols), jnp.float32),
+            jax.ShapeDtypeStruct((cols, vocab_block), jnp.float32),
         ),
         in_specs=[
             pl.BlockSpec(memory_space=pltpu.SMEM),
             pl.BlockSpec((cols, tokens_all), lambda step: (0, 0)),
             pl.BlockSpec((cols, tokens_all), lambda step: (1, 0)),
-            pl.BlockSpec((1, tokens_all), lambda step: (0, 0)),
-            pl.BlockSpec((rows, 1), embed_place),
+            pl.BlockSpec((tokens_all, 1), lambda step: (0, 0)),
+            pl.BlockSpec((1, part), embed_place),
         ]
-        + [pl.BlockSpec(memory_space=pl.ANY)] * 12,
+        + [pl.BlockSpec(memory_space=pltpu.HBM)] * 8,
         out_specs=(
             pl.BlockSpec((1, cols, cols), lambda step: (jnp.minimum(step, 3), 0, 0)),
-            pl.BlockSpec((rows, cols), embed_place),
+            pl.BlockSpec((cols, part), embed_place),
         ),
         scratch_shapes=[
             pltpu.VMEM((5, cols, tokens_all), jnp.bfloat16),
@@ -428,7 +478,7 @@
             bytes_accessed=4 * cols * (4 * cols + vocab_block) + 14 * cols * tokens_all,
             transcendentals=0,
         ),
-    )(where, bundle, bundle, ids, scale, *mine, *others, *spread)
+    )(where, bundle, bundle, ids, scale, *mine, *others)
 
 
 def layer_plan(
@@ -463,11 +513,14 @@
     def held_by(layer_index):
         return jnp.where(layer_index == 3, 3, lax.rem(layer_index + 1, 3))
 
-    def old_block(step):
-        away = by_index(old_factors, held_by(layer ^ step)).astype(jnp.bfloat16)
+    def old_block(factors, step, start, size):
+        away = by_index(factors, held_by(layer ^ step))[start : start + size]
+        away = away.astype(jnp.bfloat16)
         return swap(away, "tensor", n_tensor, step) if step else away
 
-    early = old_block(2)
+    part_rows = row_block // 2
+    early = old_block(old_factors, 2, 0, part_rows)
+    later_factors = lax.optimization_barrier(old_factors)
 
     by_feature = jnp.swapaxes(activations, 1, 2)
     kept_tokens = lax.dynamic_slice_in_dim(by_feature, shard * owned, owned, 0)
@@ -486,7 +539,13 @@
         collected.append(swap(message, "tensor", n_tensor, step) if step else message)
     collected, early = lax.optimization_barrier((jnp.stack(collected), early))
     gathered = lax.all_gather(collected, "section", axis=0)
-    blocks = [old_block(0), old_block(1), early, old_block(3)]
+    late = old_block(later_factors, 2, part_rows, part_rows)
+    blocks = [
+        old_block(later_factors, 0, 0, row_block),
+        old_block(later_factors, 1, 0, row_block),
+        jnp.concatenate([early, late], axis=0),
+        old_block(later_factors, 3, 0, row_block),
+    ]
 
     def both_shards(value, axis):
         other = swap(value, "shard", n_shard, 1)
@@ -501,29 +560,20 @@
     norm_values = norm_terms.astype(jnp.float32)
     norm_sums = jnp.stack([jnp.sum(norm_values, axis=1), jnp.sum(norm_values * norm_values, axis=1)])
     norm_sums = norm_sums + swap(norm_sums, "shard", n_shard, 1)
-    gathered, grad_all, ids_all, norm_sums = lax.optimization_barrier(
-        (gathered, grad_all, ids_all, norm_sums)
-    )
-
-    features = gathered[:, :, : 2 * features_dev].reshape(
-        n_section, n_tensor, n_shard, features_dev, tokens
-    )
-    features = features.transpose(2, 1, 0, 3, 4).reshape(n_shard, D, tokens)
-    codes = jnp.sum(
-        gathered[:, :, 2 * features_dev : 2 * features_dev + 9].astype(jnp.float32), axis=1
-    )
-    old_diag = jnp.sum(codes.reshape(n_section, 3, 3 * tokens), axis=1)[:, :col_block]
-    old_diag = jnp.stack([by_index(old_diag, layer ^ step) for step in range(n_tensor)])
-    values = features.astype(jnp.float32)
-    squares = jnp.sum(values * values, axis=(0, 2)).reshape(n_tensor, col_block)
-    matrix_diag = factor_decay * old_diag + weight * squares + damping
-    scale = (D / (3.0 * jnp.sum(matrix_diag))).reshape(1)
-    low_diag = lax.reduce_precision(matrix_diag, 8, 7)[:, None, :]
-    rows = by_index(features, core).reshape(n_tensor, row_block, tokens)
-    rows = jnp.concatenate(
-        [jnp.swapaxes(by_index(rows, own_place ^ index), 0, 1) for index in range(n_tensor)], axis=1
-    )
-    features, rows = lax.optimization_barrier((features, rows))
+    vocab_block = old_embed_diag.shape[0]
+    ids_here = layer * vocab_block + lax.iota(jnp.int32, vocab_block)
+    counts = jnp.sum((ids_all[:, None] == ids_here[None, :]).astype(jnp.float32), axis=0)
+    divisor = factor_decay * old_embed_diag + (1.0 - factor_decay) * (counts / tokens_all) + damping
+    embed_scale = (learning_rate / divisor)[None, :]
+    embed_ids = ids_all[:, None]
+    gathered, grad_all, embed_ids, embed_scale, norm_sums = lax.optimization_barrier(
+        (gathered, grad_all, embed_ids, embed_scale, norm_sums)
+    )
+
+    features, rows, low_diag, trace = lay_out(
+        jnp.stack([own_place, layer, core]), gathered, weight
+    )
+    scale = D / (3.0 * trace)
 
     own_cols = [
         factor_block(place, features, blocks[step], low_diag, step, weight)
@@ -548,17 +598,31 @@
         core == shard, jnp.concatenate([keep, got], axis=1), jnp.concatenate([got, keep], axis=1)
     )
 
-    def send(value, pairs):
-        moves = [(x * n_tensor + a, x * n_tensor + b) for x in planes for a, b in pairs]
-        return lax.ppermute(value, axes, moves)
-
-    def across(value, at):
-        moves = [(x * n_tensor + z, (1 - x) * n_tensor + z) for x, z in at]
-        return lax.ppermute(value, axes, moves)
-
-    everywhere = ("shard", "tensor", "section")
     planes = range(n_shard)
     layers = range(n_tensor)
+
+    def useful(x, z):
+        return z != 2 and (x, z) != (1, 1)
+
+    def send(value, step, held):
+        moves = [
+            (x * n_tensor + z, x * n_tensor + (z ^ step))
+            for x in planes
+            for z in layers
+            if useful(x, z ^ held)
+        ]
+        return lax.ppermute(value, axes, moves)
+
+    def across(value, held):
+        moves = [
+            (x * n_tensor + z, (1 - x) * n_tensor + z)
+            for x in planes
+            for z in layers
+            if useful(x, z ^ held)
+        ]
+        return lax.ppermute(value, axes, moves)
+
+    everywhere = ("shard", "tensor", "section")
 
     def spot(x, z, s):
         return (x * n_tensor + z) * n_section + s
@@ -571,18 +635,6 @@
         )
         return jnp.where(layer == source, value, moved_here)
 
-    hop_1 = send(own, [(0, 1), (3, 2)])
-    over_0 = across(own, [(0, 0), (1, 0), (0, 1), (0, 3), (1, 3)])
-    left_here = scatter(own, 2)
-    hop_1, over_0, left_here = lax.optimization_barrier((hop_1, over_0, left_here))
-    hop_2 = send(hop_1, [(1, 2), (2, 1)])
-    over_1 = across(hop_1, [(x, z) for x in planes for z in (1, 2)])
-    middle = jnp.where(shard == 0, own, over_0)
-    spread_0 = send(middle, [(1, 0)])
-    left_there = lax.ppermute(
-        left_here, everywhere, [(spot(x, t, t), spot(1 - x, t, t)) for x in planes for t in layers]
-    )
-
     router_matrix = (
         factor_decay * old_router_factor
         + weight * jnp.einsum("en,fn->ef", grad_all, grad_all, preferred_element_type=jnp.float32)
@@ -592,27 +644,36 @@
     router_right = jnp.einsum(
         "en,ef->fn", grad_all, router_inverse, preferred_element_type=jnp.float32
     ).astype(jnp.bfloat16)
+
+    near_1 = send(own, 1, 0)
+    near_2 = send(own, 2, 0)
+    over_0 = across(own, 0)
+    left_here = scatter(own, 2)
     router_cols = learning_rate * jnp.einsum(
         "fn,cn->fc", router_right, own, preferred_element_type=jnp.float32
     )
-    router_there = across(router_cols, [(1, 1)])
-    router_cols = scatter(jnp.where(shard == 1, router_cols, router_there), 1)
+    router_cols = scatter(router_cols, 1)
     router_high = lax.reduce_precision(router_cols, 8, 7)
     codes = jnp.concatenate([router_high, router_cols - router_high], axis=0).astype(jnp.bfloat16)
     codes_tail = jnp.pad(codes[:, tokens_all:], ((0, 0), (0, 2 * tokens_all - col_block)))
-    bundle = jnp.concatenate([left_here, left_there, codes[:, :tokens_all], codes_tail], axis=0)
-
-    bundle, hop_2, over_1, spread_0, middle = lax.optimization_barrier(
-        (bundle, hop_2, over_1, spread_0, middle)
-    )
-    hop_3 = send(hop_2, [(1, 0), (2, 3)])
-    over_2 = across(hop_2, [(x, z) for x in planes for z in (1, 2)])
-    spread_2 = send(middle, [(1, 2)])
+    codes = jnp.concatenate([codes[:, :tokens_all], codes_tail], axis=0)
+    near_1, over_0 = lax.optimization_barrier((near_1, over_0))
+    over_1 = across(near_1, 1)
+    left_here, near_2, codes = lax.optimization_barrier((left_here, near_2, codes))
+    left_there = lax.ppermute(
+        jnp.concatenate([left_here, codes], axis=0),
+        everywhere,
+        [(spot(x, t, t), spot(1 - x, t, t)) for x in planes for t in layers],
+    )
+    near_3 = send(near_2, 1, 2)
+    over_2 = across(near_2, 2)
+    codes = jnp.where(shard == 1, codes, left_there[col_block:])
+    bundle = jnp.concatenate([left_here, left_there[:col_block], codes], axis=0)
+    bundle, over_1 = lax.optimization_barrier((bundle, over_1))
     to_side = [(spot(x, t, t), spot(x, t, t ^ 2)) for x in planes for t in layers]
     bundle = jnp.where(section == layer, bundle, lax.ppermute(bundle, everywhere, to_side))
-    bundle, hop_3, over_2, spread_2 = lax.optimization_barrier((bundle, hop_3, over_2, spread_2))
-    over_3 = across(hop_3, [(x, z) for x in planes for z in (0, 3)])
-    spread_3 = send(spread_2, [(2, 3)])
+    bundle, near_3, over_2 = lax.optimization_barrier((bundle, near_3, over_2))
+    over_3 = across(near_3, 3)
     to_core = [
         (spot(x, t, t ^ a), spot(x, t, t ^ a ^ 1)) for x in planes for t in layers for a in (0, 2)
     ]
@@ -625,19 +686,15 @@
     ).astype(jnp.float32)
     precond_router = codes[:EXPERTS] + codes[EXPERTS:]
 
-    vocab_block = old_embed_diag.shape[0]
-    ids_here = layer * vocab_block + lax.iota(jnp.int32, vocab_block)
-    counts = jnp.sum((ids_here[:, None] == ids_all[None, :]).astype(jnp.float32), axis=1)
-    divisor = factor_decay * old_embed_diag + (1.0 - factor_decay) * (counts / tokens_all) + damping
-    precond_attn, precond_embed = output_products(
+    precond_attn, embed_columns = output_products(
         jnp.stack([shard, layer]),
         bundle,
-        ids_all[None, :],
-        (learning_rate / divisor)[:, None],
-        (own, hop_1, hop_2, hop_3),
+        embed_ids,
+        embed_scale,
+        (own, near_1, near_2, near_3),
         (over_0, over_1, over_2, over_3),
-        (spread_0, middle, spread_2, spread_3),
-    )
+    )
+    precond_embed = embed_columns.T
 
     precond_norms = (
         learning_rate

time: 282 us -> 277 us (0.982)
  local copies, waits for them, and re-layouts: 34.2 us -> 19.4 us
  starting transfers between devices: 50.3 us -> 56.8 us
  Pallas kernels: 30.7 us -> 34 us
  other arithmetic: 13.8 us -> 16.7 us
    all_gather x1, waiting for transfers between devices: 18.1 us -> 0.02 us  [layer_plan(): gathered = lax.all_gather(collected, 'section', axis=0)]
    ppermute x17 -> x18, waiting for transfers between devices: 65.7 us -> 77.6 us  [swap(): return lax.ppermute(value, axis, [(i, i ^ step) for i in range(size)])]
    ppermute x2, waiting for transfers between devices: 8.4 us -> 18.3 us  [scatter(): lax.ppermute(value, everywhere, [(spot(x, source, s), spot(x, s, s)) for...]
    ppermute x6 -> x3, waiting for transfers between devices: 9.28 us -> 0.97 us  [send(): return lax.ppermute(value, axes, moves)]
    dynamic_slice x6 -> x0, local copies, waits for them, and re-layouts: 7.86 us -> none  [by_index(): return lax.dynamic_index_in_dim(array, index, axis, False)]
    ppermute x6 -> x3, starting transfers between devices: 7.8 us -> 15.3 us  [send(): return lax.ppermute(value, axes, moves)]
    unnamed x64 -> x53, local copies, waits for them, and re-layouts: 15.2 us -> 10.2 us
    ppermute x1, waiting for transfers between devices: 6.74 us -> 10.9 us  [layer_plan(): lax.ppermute(jnp.concatenate([left_here, codes], axis=0), everywhere, [(s...]
  transfers between devices with their start and end apart: 34 -> 31, of which waited for: 14 -> 14; matrix products, arithmetic and copies ran while one was open for 10% -> 9% of each run, Pallas kernels for 2% -> 2%
where the time goes in v6:
time: 277 us; the launch traced here: 276 us
  waiting for transfers between devices  132 us (48%)
  starting transfers between devices  56.8 us (21%)
  Pallas kernels  34 us (12%)
  local copies, waits for them, and re-layouts  19.4 us (7%)
  other arithmetic  16.7 us (6%)
  between operations  16 us (6%)
    ppermute x18, waiting for transfers between devices, swap(): return lax.ppermute(value, axis, [(i, i ^ step) for i in range(size)])  77.6 us
    ppermute x18, starting transfers between devices, swap(): return lax.ppermute(value, axis, [(i, i ^ step) for i in range(size)])  21.3 us
    ppermute x2, waiting for transfers between devices, scatter(): lax.ppermute(value, everywhere, [(spot(x, source, s), spot(x, s, s)) for...  18.3 us
    pallas_call x3, Pallas kernels, chain_call(): pl.pallas_call(kernel, in_specs=[pl.BlockSpec(memory_space=pltpu.SMEM)] *...  17.7 us
    ppermute x3, starting transfers between devices, send(): return lax.ppermute(value, axes, moves)  15.3 us
    ppermute x4, waiting for transfers between devices, across(): return lax.ppermute(value, axes, moves)  13.3 us
    ppermute x1, waiting for transfers between devices, layer_plan(): lax.ppermute(bundle, everywhere, to_side)  11.2 us
    ppermute x1, waiting for transfers between devices, layer_plan(): lax.ppermute(jnp.concatenate([left_here, codes], axis=0), everywhere, [(s...  10.9 us
  transfers between devices with their start and end apart: 31, of which 14 were waited for; matrix products, arithmetic and copies ran while one was open for 9% of the time, Pallas kernels for 2%

profile of v6, /device:TPU:0, one launch (start us, length us, event | category | flops | bytes accessed | tf_op | source)
XLA Modules:
  0.0 275.9 jit_solution(6172275949583243472)
XLA Ops:
  8.2 3.0 %collective-permute-start = (bf16[4,144,256]{2,1,0:T(8,128)(2,1)S(1)}, bf16[4,144,256]{2,1,0:T(8,128)(2,1)S(1)}, u32[]{:S(2)}, u32[]{:S(2)}) collective-permute-start(bf16[4,144,256]{2,1,0:T(8,128)(2,1)S(1)} %dynamic-slice_bitcast_fusion), channel_id=1, source_target_pairs={{0,16},{16,0},{1,17},{17,1},{2,18},{18,2},{3,19},{19,3},{4,20},{20... | collective-permute-start | bytes 884744 | tf_op jit(solution)/shard_map/ppermute | solution.py:169
  18.3 3.9 %collective-permute-start.3 = (bf16[304,256]{1,0:T(8,128)(2,1)S(1)}, bf16[304,256]{1,0:T(8,128)(2,1)S(1)}, u32[]{:S(2)}, u32[]{:S(2)}) collective-permute-start(bf16[304,256]{1,0:T(8,128)(2,1)S(1)} %pad_maximum_fusion.6), channel_id=1, source_target_pairs={{0,12},{4,8},{8,4},{12,0},{1,13},{5,9},{9,5},{13,1},{2,14},{6,10},... | collective-permute-start | bytes 466952 | tf_op jit(solution)/shard_map/ppermute | solution.py:169
  22.9 6.4 %collective-permute-done.3 = bf16[304,256]{1,0:T(8,128)(2,1)S(1)} collective-permute-done((bf16[304,256]{1,0:T(8,128)(2,1)S(1)}, bf16[304,256]{1,0:T(8,128)(2,1)S(1)}, u32[]{:S(2)}, u32[]{:S(2)}) %collective-permute-start.3) | collective-permute-done | bytes 155680 | tf_op jit(solution)/shard_map/ppermute | solution.py:169
  29.3 15.4 %collective-permute-done.2 = bf16[304,256]{1,0:T(8,128)(2,1)S(1)} collective-permute-done((bf16[304,256]{1,0:T(8,128)(2,1)S(1)}, bf16[304,256]{1,0:T(8,128)(2,1)S(1)}, u32[]{:S(2)}, u32[]{:S(2)}) %collective-permute-start.2) | collective-permute-done | bytes 155680 | tf_op jit(solution)/shard_map/ppermute | solution.py:169
  48.5 3.6 %fusion.5 = (bf16[576,576]{1,0:T(8,128)(2,1)}, bf16[576,576]{1,0:T(8,128)(2,1)}, bf16[576,576]{1,0:T(8,128)(2,1)S(1)}) fusion(f32[4,576,576]{2,1,0:T(8,128)} %param.12, s32[]{:T(128)S(6)} %select_n.168, s32[]{:T(128)S(6)} %select_n.162, s32[]{:T(128)S(6)} %select_n.156), kind=kLoop, calls=%fused_computation.18 | loop fusion | bytes 3981324 | tf_op jit(solution)/shard_map/convert_element_type | solution.py:518
  54.1 3.6 %collective-permute-start.9 = (bf16[288,576]{1,0:T(8,128)(2,1)S(1)}, bf16[288,576]{1,0:T(8,128)(2,1)}, u32[]{:S(2)}, u32[]{:S(2)}) collective-permute-start(bf16[288,576]{1,0:T(8,128)(2,1)S(1)} %fusion.7), channel_id=1, source_target_pairs={{0,8},{4,12},{8,0},{12,4},{1,9},{5,13},{9,1},{13,5},{2,10},{6,14},... | collective-permute-start | bytes 995336 | tf_op jit(solution)/shard_map/ppermute | solution.py:169
  60.1 17.9 %collective-permute-done.9 = bf16[288,576]{1,0:T(8,128)(2,1)} collective-permute-done((bf16[288,576]{1,0:T(8,128)(2,1)S(1)}, bf16[288,576]{1,0:T(8,128)(2,1)}, u32[]{:S(2)}, u32[]{:S(2)}) %collective-permute-start.9) | collective-permute-done | bytes 331808 | tf_op jit(solution)/shard_map/ppermute | solution.py:169
  80.8 2.8 %shard_map.111 = (bf16[2,2304,256]{2,1,0:T(8,128)(2,1)S(1)}, bf16[256,2304]{1,0:T(8,128)(2,1)S(1)}, f32[4,1,576]{2,1,0:T(1,128)S(1)}, f32[1]{0:T(128)}) custom-call(s32[3]{0:T(128)S(1)} %pad_add_fusion.3.place_ref, bf16[4,4,304,256]{3,2,1,0:T(8,128)(2,1)S(1)} %bitcast.86), custom_call_target="tpu_custom_call" | custom-call | flops 37748736 | bytes 8257536 | tf_op jit(solution)/shard_map/pallas_call | solution.py:237
  86.2 9.4 %collective-permute-done.10.old = bf16[576,576]{1,0:T(8,128)(2,1)} collective-permute-done((bf16[576,576]{1,0:T(8,128)(2,1)}, bf16[576,576]{1,0:T(8,128)(2,1)}, u32[]{:S(2)}, u32[]{:S(2)}) %collective-permute-start.10) | collective-permute-done | bytes 663584 | tf_op jit(solution)/shard_map/ppermute | solution.py:169
  99.7 5.2 %shard_map.116 = (f32[2,256,576]{2,1,0:T(8,128)S(1)}, bf16[256,1152]{1,0:T(8,128)(2,1)S(1)}) custom-call(s32[1]{0:T(128)} %bitcast.2.place_ref, f32[1]{0:T(128)S(6)} %div.21.scale_ref, bf16[256,2304]{1,0:T(8,128)(2,1)S(1)} %get-tuple-element.36.rows, f32[4,1,576]{2,1,0:T(1,128)S(1)} %get-tuple-element.37.diag, bf16[576,576]{1,0:T(8,128)(2,1)S(1)} %shard_map.112.refs_0_, ...), custom_call_target="tpu_custom_call" | custom-call | flops 1358954496 | bytes 5308416 | tf_op jit(solution)/shard_map/pallas_call | solution.py:379
  106.6 13.8 %collective-permute-done.15.theirs = bf16[256,1152]{1,0:T(8,128)(2,1)S(1)} collective-permute-done((bf16[256,1152]{1,0:T(8,128)(2,1)S(1)}, bf16[256,1152]{1,0:T(8,128)(2,1)S(1)}, u32[]{:S(2)}, u32[]{:S(2)}) %collective-permute-start.15) | collective-permute-done | bytes 589856 | tf_op jit(solution)/shard_map/ppermute | solution.py:169
  120.4 5.7 %shard_map.117 = (f32[2,256,576]{2,1,0:T(8,128)S(1)}, bf16[256,1152]{1,0:T(8,128)(2,1)S(1)}) custom-call(s32[1]{0:T(128)} %bitcast.2.place_ref, f32[1]{0:T(128)S(6)} %div.21.scale_ref, bf16[256,1152]{1,0:T(8,128)(2,1)S(1)} %get-tuple-element.40.mine, bf16[256,1152]{1,0:T(8,128)(2,1)S(1)} %collective-permute-done.15.theirs, ...), custom_call_target="tpu_custom_call" | custom-call | flops 1358954496 | bytes 5308416 | tf_op jit(solution)/shard_map/pallas_call | solution.py:379
  129.2 12.6 %collective-permute-done.16.theirs = bf16[256,1152]{1,0:T(8,128)(2,1)} collective-permute-done((bf16[256,1152]{1,0:T(8,128)(2,1)S(1)}, bf16[256,1152]{1,0:T(8,128)(2,1)}, u32[]{:S(2)}, u32[]{:S(2)}) %collective-permute-start.16) | collective-permute-done | bytes 589856 | tf_op jit(solution)/shard_map/ppermute | solution.py:169
  147.6 6.8 %shard_map.118 = (bf16[576,256]{1,0:T(8,128)(2,1)S(1)}, bf16[576,256]{1,0:T(8,128)(2,1)}) custom-call(s32[1]{0:T(128)} %bitcast.2.place_ref, f32[1]{0:T(128)S(6)} %div.21.scale_ref, bf16[256,1152]{1,0:T(8,128)(2,1)S(1)} %get-tuple-element.42.mine, bf16[256,1152]{1,0:T(8,128)(2,1)} %collective-permute-done.16.theirs, f32[2,256,576]{2,1,0:T(8,128)S(1)} %copy-done.10, ...), custom_call_target="tpu_custom_call" | custom-call | flops 1358954496 | bytes 5308416 | tf_op jit(solution)/shard_map/pallas_call | solution.py:379
  161.6 12.0 %collective-permute-start.19 = (bf16[576,512]{1,0:T(8,128)(2,1)S(1)}, bf16[576,512]{1,0:T(8,128)(2,1)S(1)}, u32[]{:S(2)}, u32[]{:S(2)}) collective-permute-start(bf16[576,512]{1,0:T(8,128)(2,1)S(1)} %maximum_select_fusion.refs_0_), channel_id=1, source_target_pairs={{0,8},{4,12},{12,4},{16,24},{28,20},{1,9},{5,13},{13,5},{17,25},{2... | collective-permute-start | bytes 1769480 | tf_op jit(solution)/shard_map/ppermute | solution.py:614
  175.5 2.8 %collective-permute-start.23 = (bf16[576,512]{1,0:T(8,128)(2,1)S(1)}, bf16[576,512]{1,0:T(8,128)(2,1)S(1)}, u32[]{:S(2)}, u32[]{:S(2)}) collective-permute-start(bf16[576,512]{1,0:T(8,128)(2,1)S(1)} %maximum_select_fusion.refs_0_), channel_id=1, source_target_pairs={{0,16},{4,20},{12,28},{16,0},{28,12},{1,17},{5,21},{13,29},{17,1},... | collective-permute-start | bytes 1769480 | tf_op jit(solution)/shard_map/ppermute | solution.py:623
  178.3 18.3 %collective-permute-done.18 = bf16[576,512]{1,0:T(8,128)(2,1)S(1)} collective-permute-done((bf16[576,512]{1,0:T(8,128)(2,1)S(1)}, bf16[576,512]{1,0:T(8,128)(2,1)S(1)}, u32[]{:S(2)}, u32[]{:S(2)}) %collective-permute-start.18) | collective-permute-done | bytes 589856 | tf_op jit(solution)/shard_map/ppermute | solution.py:631
  197.6 3.3 %collective-permute-start.21 = (bf16[608,512]{1,0:T(8,128)(2,1)}, bf16[608,512]{1,0:T(8,128)(2,1)}, u32[]{:S(2)}, u32[]{:S(2)}) collective-permute-start(bf16[608,512]{1,0:T(8,128)(2,1)} %pad_maximum_fusion.3), channel_id=1, source_target_pairs={{0,16},{5,21},{10,26},{15,31},{16,0},{21,5},{26,10},{31,15}} | collective-permute-start | bytes 1867784 | tf_op jit(solution)/shard_map/ppermute | solution.py:663
  203.5 10.9 %collective-permute-done.21 = bf16[608,512]{1,0:T(8,128)(2,1)} collective-permute-done((bf16[608,512]{1,0:T(8,128)(2,1)}, bf16[608,512]{1,0:T(8,128)(2,1)}, u32[]{:S(2)}, u32[]{:S(2)}) %collective-permute-start.21) | collective-permute-done | bytes 622624 | tf_op jit(solution)/shard_map/ppermute | solution.py:663
  217.4 4.1 %collective-permute-done.24.refs_5_ = bf16[576,512]{1,0:T(8,128)(2,1)S(1)} collective-permute-done((bf16[576,512]{1,0:T(8,128)(2,1)S(1)}, bf16[576,512]{1,0:T(8,128)(2,1)S(1)}, u32[]{:S(2)}, u32[]{:S(2)}) %collective-permute-start.24) | collective-permute-done | bytes 589856 | tf_op jit(solution)/shard_map/ppermute | solution.py:623
  226.0 11.2 %collective-permute-done.25 = bf16[1184,512]{1,0:T(8,128)(2,1)} collective-permute-done((bf16[1184,512]{1,0:T(8,128)(2,1)}, bf16[1184,512]{1,0:T(8,128)(2,1)}, u32[]{:S(2)}, u32[]{:S(2)}) %collective-permute-start.25) | collective-permute-done | bytes 1212448 | tf_op jit(solution)/shard_map/ppermute | solution.py:674
  244.4 3.6 %collective-permute-start.29 = (bf16[576,512]{1,0:T(8,128)(2,1)S(1)}, bf16[576,512]{1,0:T(8,128)(2,1)S(1)}, u32[]{:S(2)}, u32[]{:S(2)}) collective-permute-start(bf16[576,512]{1,0:T(8,128)(2,1)S(1)} %collective-permute-done.26.refs_3_), channel_id=1, source_target_pairs={{0,16},{8,24},{12,28},{16,0},{28,12},{1,17},{9,25},{13,29},{17,1},... | collective-permute-start | bytes 1769480 | tf_op jit(solution)/shard_map/ppermute | solution.py:623
  250.1 9.1 %collective-permute-done.29.refs_7_ = bf16[576,512]{1,0:T(8,128)(2,1)S(1)} collective-permute-done((bf16[576,512]{1,0:T(8,128)(2,1)S(1)}, bf16[576,512]{1,0:T(8,128)(2,1)S(1)}, u32[]{:S(2)}, u32[]{:S(2)}) %collective-permute-start.29) | collective-permute-done | bytes 589856 | tf_op jit(solution)/shard_map/ppermute | solution.py:623
  259.2 9.8 %shard_map.119 = (f32[4,576,576]{2,1,0:T(8,128)}, f32[576,2048]{1,0:T(8,128)}) custom-call(s32[2]{0:T(128)S(1)} %pad_add_fusion.2.where_ref, bf16[1184,512]{1,0:T(8,128)(2,1)S(1)} %broadcast_select_fusion.1.left_mine.left_other, bf16[1184,512]{1,0:T(8,128)(2,1)S(1)} %broadcast_select_fusion.1.left_mine.left_other, s32[512,1]{1,0:T(8,128)S(1)} %copy-done.12, ...), custom_call_target="tpu_custom_call" | custom-call | flops 2566914048 | bytes 14155776 | tf_op jit(solution)/shard_map/pallas_call | solution.py:452
  (159 shorter events, 64.6 us)
Async XLA Ops:
  7.2 71.9 %all-gather.3.cloned.1.call-start = ((), (), s32[]{:S(2)}) async-start(), calls=%async_computation | async-start | bytes 3112960 | tf_op jit(solution)/shard_map/all_gather | solution.py:541
  12.4 33.2 %collective-permute-start.4 = (bf16[288,576]{1,0:T(8,128)(2,1)S(1)}, bf16[288,576]{1,0:T(8,128)(2,1)S(1)}, u32[]{:S(2)}, u32[]{:S(2)}) collective-permute-start(bf16[288,576]{1,0:T(8,128)(2,1)S(1)} %fusion.6), channel_id=1, source_target_pairs={{0,8},{4,12},{8,0},{12,4},{1,9},{5,13},{9,1},{13,5},{2,10},{6,14},... | collective-permute-start | bytes 995336 | tf_op jit(solution)/shard_map/ppermute | solution.py:169
  22.2 22.5 %collective-permute-start.2 = (bf16[304,256]{1,0:T(8,128)(2,1)S(1)}, bf16[304,256]{1,0:T(8,128)(2,1)S(1)}, u32[]{:S(2)}, u32[]{:S(2)}) collective-permute-start(bf16[304,256]{1,0:T(8,128)(2,1)S(1)} %pad_maximum_fusion.5), channel_id=1, source_target_pairs={{0,8},{4,12},{8,0},{12,4},{1,9},{5,13},{9,1},{13,5},{2,10},{6,14},... | collective-permute-start | bytes 466952 | tf_op jit(solution)/shard_map/ppermute | solution.py:169
  22.3 22.4 %collective-permute-start.1 = (bf16[304,256]{1,0:T(8,128)(2,1)S(1)}, bf16[304,256]{1,0:T(8,128)(2,1)S(1)}, u32[]{:S(2)}, u32[]{:S(2)}) collective-permute-start(bf16[304,256]{1,0:T(8,128)(2,1)S(1)} %pad_maximum_fusion.4), channel_id=1, source_target_pairs={{0,4},{4,0},{8,12},{12,8},{1,5},{5,1},{9,13},{13,9},{2,6},{6,2},{1... | collective-permute-start | bytes 466952 | tf_op jit(solution)/shard_map/ppermute | solution.py:169
  45.6 14.5 %collective-permute-start.5 = (bf16[8,256]{1,0:T(8,128)(2,1)S(1)}, bf16[8,256]{1,0:T(8,128)(2,1)S(1)}, u32[]{:S(2)}, u32[]{:S(2)}) collective-permute-start(bf16[8,256]{1,0:T(8,128)(2,1)S(1)} %copy-done.20), channel_id=1, source_target_pairs={{0,16},{16,0},{1,17},{17,1},{2,18},{18,2},{3,19},{19,3},{4,20},{20... | collective-permute-start | bytes 12296 | tf_op jit(solution)/shard_map/ppermute | solution.py:169
  52.1 32.2 %collective-permute-start.8 = (bf16[576,576]{1,0:T(8,128)(2,1)}, bf16[576,576]{1,0:T(8,128)(2,1)S(1)}, u32[]{:S(2)}, u32[]{:S(2)}) collective-permute-start(bf16[576,576]{1,0:T(8,128)(2,1)} %get-tuple-element.69), channel_id=1, source_target_pairs={{0,4},{4,0},{8,12},{12,8},{1,5},{5,1},{9,13},{13,9},{2,6},{6,2},{1... | collective-permute-start | bytes 1990664 | tf_op jit(solution)/shard_map/ppermute | solution.py:169
  54.1 23.9 %collective-permute-start.9 = (bf16[288,576]{1,0:T(8,128)(2,1)S(1)}, bf16[288,576]{1,0:T(8,128)(2,1)}, u32[]{:S(2)}, u32[]{:S(2)}) collective-permute-start(bf16[288,576]{1,0:T(8,128)(2,1)S(1)} %fusion.7), channel_id=1, source_target_pairs={{0,8},{4,12},{8,0},{12,4},{1,9},{5,13},{9,1},{13,5},{2,10},{6,14},... | collective-permute-start | bytes 995336 | tf_op jit(solution)/shard_map/ppermute | solution.py:169
  57.8 37.9 %collective-permute-start.10 = (bf16[576,576]{1,0:T(8,128)(2,1)}, bf16[576,576]{1,0:T(8,128)(2,1)}, u32[]{:S(2)}, u32[]{:S(2)}) collective-permute-start(bf16[576,576]{1,0:T(8,128)(2,1)} %get-tuple-element.68), channel_id=1, source_target_pairs={{0,12},{4,8},{8,4},{12,0},{1,13},{5,9},{9,5},{13,1},{2,14},{6,10},... | collective-permute-start | bytes 1990664 | tf_op jit(solution)/shard_map/ppermute | solution.py:169
  84.2 13.9 %collective-permute-start.11 = (bf16[576,576]{1,0:T(8,128)(2,1)S(1)}, bf16[576,576]{1,0:T(8,128)(2,1)S(1)}, u32[]{:S(2)}, u32[]{:S(2)}) collective-permute-start(bf16[576,576]{1,0:T(8,128)(2,1)S(1)} %shard_map.112.refs_0_), channel_id=1, source_target_pairs={{0,1},{1,0},{2,3},{3,2},{4,5},{5,4},{6,7},{7,6},{8,9},{9,8},{10,11... | collective-permute-start | bytes 1990664 | tf_op jit(solution)/shard_map/ppermute | solution.py:169
  85.0 13.2 %collective-permute-start.12 = (bf16[576,576]{1,0:T(8,128)(2,1)S(1)}, bf16[576,576]{1,0:T(8,128)(2,1)S(1)}, u32[]{:S(2)}, u32[]{:S(2)}) collective-permute-start(bf16[576,576]{1,0:T(8,128)(2,1)S(1)} %shard_map.113.refs_1_), channel_id=1, source_target_pairs={{0,1},{1,0},{2,3},{3,2},{4,5},{5,4},{6,7},{7,6},{8,9},{9,8},{10,11... | collective-permute-start | bytes 1990664 | tf_op jit(solution)/shard_map/ppermute | solution.py:169
  86.1 12.0 %collective-permute-start.13 = (bf16[576,576]{1,0:T(8,128)(2,1)S(1)}, bf16[576,576]{1,0:T(8,128)(2,1)S(1)}, u32[]{:S(2)}, u32[]{:S(2)}) collective-permute-start(bf16[576,576]{1,0:T(8,128)(2,1)S(1)} %shard_map.114.refs_2_), channel_id=1, source_target_pairs={{0,1},{1,0},{2,3},{3,2},{4,5},{5,4},{6,7},{7,6},{8,9},{9,8},{10,11... | collective-permute-start | bytes 1990664 | tf_op jit(solution)/shard_map/ppermute | solution.py:169
  105.0 15.4 %collective-permute-start.15 = (bf16[256,1152]{1,0:T(8,128)(2,1)S(1)}, bf16[256,1152]{1,0:T(8,128)(2,1)S(1)}, u32[]{:S(2)}, u32[]{:S(2)}) collective-permute-start(bf16[256,1152]{1,0:T(8,128)(2,1)S(1)} %get-tuple-element.40.mine), channel_id=1, source_target_pairs={{0,2},{1,3},{2,0},{3,1},{4,6},{5,7},{6,4},{7,5},{8,10},{9,11},{10,... | collective-permute-start | bytes 1769480 | tf_op jit(solution)/shard_map/ppermute | solution.py:169
  127.2 14.6 %collective-permute-start.16 = (bf16[256,1152]{1,0:T(8,128)(2,1)S(1)}, bf16[256,1152]{1,0:T(8,128)(2,1)}, u32[]{:S(2)}, u32[]{:S(2)}) collective-permute-start(bf16[256,1152]{1,0:T(8,128)(2,1)S(1)} %get-tuple-element.42.mine), channel_id=1, source_target_pairs={{0,2},{1,3},{2,0},{3,1},{4,6},{5,7},{6,4},{7,5},{8,10},{9,11},{10,... | collective-permute-start | bytes 1769480 | tf_op jit(solution)/shard_map/ppermute | solution.py:169
  158.6 38.1 %collective-permute-start.18 = (bf16[576,512]{1,0:T(8,128)(2,1)S(1)}, bf16[576,512]{1,0:T(8,128)(2,1)S(1)}, u32[]{:S(2)}, u32[]{:S(2)}) collective-permute-start(bf16[576,512]{1,0:T(8,128)(2,1)S(1)} %maximum_select_fusion.refs_0_), channel_id=1, source_target_pairs={{8,0},{9,5},{11,15},{24,16},{25,21},{27,31}} | collective-permute-start | bytes 1769480 | tf_op jit(solution)/shard_map/ppermute | solution.py:631
  160.2 18.0 %collective-permute-start.20 = (f32[8,576]{1,0:T(8,128)S(1)}, f32[8,576]{1,0:T(8,128)S(1)}, u32[]{:S(2)}, u32[]{:S(2)}) collective-permute-start(f32[8,576]{1,0:T(8,128)S(1)} %convolution_multiply_fusion), channel_id=1, source_target_pairs={{4,0},{6,10},{7,15},{20,16},{22,26},{23,31}} | collective-permute-start | bytes 55304 | tf_op jit(solution)/shard_map/ppermute | solution.py:631
  161.6 35.2 %collective-permute-start.19 = (bf16[576,512]{1,0:T(8,128)(2,1)S(1)}, bf16[576,512]{1,0:T(8,128)(2,1)S(1)}, u32[]{:S(2)}, u32[]{:S(2)}) collective-permute-start(bf16[576,512]{1,0:T(8,128)(2,1)S(1)} %maximum_select_fusion.refs_0_), channel_id=1, source_target_pairs={{0,8},{4,12},{12,4},{16,24},{28,20},{1,9},{5,13},{13,5},{17,25},{2... | collective-permute-start | bytes 1769480 | tf_op jit(solution)/shard_map/ppermute | solution.py:614
  173.6 27.4 %collective-permute-start.22 = (bf16[576,512]{1,0:T(8,128)(2,1)S(1)}, bf16[576,512]{1,0:T(8,128)(2,1)S(1)}, u32[]{:S(2)}, u32[]{:S(2)}) collective-permute-start(bf16[576,512]{1,0:T(8,128)(2,1)S(1)} %maximum_select_fusion.refs_0_), channel_id=1, source_target_pairs={{0,4},{4,0},{12,8},{16,20},{28,24},{1,5},{5,1},{13,9},{17,21},{29,... | collective-permute-start | bytes 1769480 | tf_op jit(solution)/shard_map/ppermute | solution.py:614
  175.5 25.5 %collective-permute-start.23 = (bf16[576,512]{1,0:T(8,128)(2,1)S(1)}, bf16[576,512]{1,0:T(8,128)(2,1)S(1)}, u32[]{:S(2)}, u32[]{:S(2)}) collective-permute-start(bf16[576,512]{1,0:T(8,128)(2,1)S(1)} %maximum_select_fusion.refs_0_), channel_id=1, source_target_pairs={{0,16},{4,20},{12,28},{16,0},{28,12},{1,17},{5,21},{13,29},{17,1},... | collective-permute-start | bytes 1769480 | tf_op jit(solution)/shard_map/ppermute | solution.py:623
  197.6 16.8 %collective-permute-start.21 = (bf16[608,512]{1,0:T(8,128)(2,1)}, bf16[608,512]{1,0:T(8,128)(2,1)}, u32[]{:S(2)}, u32[]{:S(2)}) collective-permute-start(bf16[608,512]{1,0:T(8,128)(2,1)} %pad_maximum_fusion.3), channel_id=1, source_target_pairs={{0,16},{5,21},{10,26},{15,31},{16,0},{21,5},{26,10},{31,15}} | collective-permute-start | bytes 1867784 | tf_op jit(solution)/shard_map/ppermute | solution.py:663
  201.0 20.6 %collective-permute-start.24 = (bf16[576,512]{1,0:T(8,128)(2,1)S(1)}, bf16[576,512]{1,0:T(8,128)(2,1)S(1)}, u32[]{:S(2)}, u32[]{:S(2)}) collective-permute-start(bf16[576,512]{1,0:T(8,128)(2,1)S(1)} %collective-permute-done.22.refs_1_), channel_id=1, source_target_pairs={{0,16},{4,20},{8,24},{20,4},{24,8},{1,17},{5,21},{9,25},{21,5},{25... | collective-permute-start | bytes 1769480 | tf_op jit(solution)/shard_map/ppermute | solution.py:623
  221.5 15.7 %collective-permute-start.25 = (bf16[1184,512]{1,0:T(8,128)(2,1)}, bf16[1184,512]{1,0:T(8,128)(2,1)}, u32[]{:S(2)}, u32[]{:S(2)}) collective-permute-start(bf16[1184,512]{1,0:T(8,128)(2,1)} %pad_maximum_fusion), channel_id=1, source_target_pairs={{0,2},{5,7},{10,8},{15,13},{16,18},{21,23},{26,24},{31,29}} | collective-permute-start | bytes 3637256 | tf_op jit(solution)/shard_map/ppermute | solution.py:674
  223.9 16.7 %collective-permute-start.26 = (bf16[576,512]{1,0:T(8,128)(2,1)S(1)}, bf16[576,512]{1,0:T(8,128)(2,1)S(1)}, u32[]{:S(2)}, u32[]{:S(2)}) collective-permute-start(bf16[576,512]{1,0:T(8,128)(2,1)S(1)} %collective-permute-done.19.refs_2_), channel_id=1, source_target_pairs={{4,0},{8,12},{12,8},{20,16},{24,28},{5,1},{9,13},{13,9},{21,17},{2... | collective-permute-start | bytes 1769480 | tf_op jit(solution)/shard_map/ppermute | solution.py:614
  225.3 15.3 %collective-permute-start.27 = (bf16[576,512]{1,0:T(8,128)(2,1)S(1)}, bf16[576,512]{1,0:T(8,128)(2,1)S(1)}, u32[]{:S(2)}, u32[]{:S(2)}) collective-permute-start(bf16[576,512]{1,0:T(8,128)(2,1)S(1)} %collective-permute-done.19.refs_2_), channel_id=1, source_target_pairs={{4,20},{8,24},{12,28},{20,4},{24,8},{5,21},{9,25},{13,29},{21,5},{... | collective-permute-start | bytes 1769480 | tf_op jit(solution)/shard_map/ppermute | solution.py:623
  244.4 14.8 %collective-permute-start.29 = (bf16[576,512]{1,0:T(8,128)(2,1)S(1)}, bf16[576,512]{1,0:T(8,128)(2,1)S(1)}, u32[]{:S(2)}, u32[]{:S(2)}) collective-permute-start(bf16[576,512]{1,0:T(8,128)(2,1)S(1)} %collective-permute-done.26.refs_3_), channel_id=1, source_target_pairs={{0,16},{8,24},{12,28},{16,0},{28,12},{1,17},{9,25},{13,29},{17,1},... | collective-permute-start | bytes 1769480 | tf_op jit(solution)/shard_map/ppermute | solution.py:623
  (31 other events, 338.9 us)
Sparse Core Ops, SparseCore 0:
  45.7 25.0 all-gather.2

commit v7 on v6

--- a/solution.py
+++ b/solution.py
@@ -380,7 +380,7 @@
         kernel,
         in_specs=[pl.BlockSpec(memory_space=pltpu.SMEM)] * len(scalars)
         + [vmem] * len(arrays)
-        + [pl.BlockSpec(memory_space=pltpu.HBM)] * len(blocks),
+        + [pl.BlockSpec(memory_space=pl.ANY)] * len(blocks),
         out_specs=[vmem] * len(out_shape),
         out_shape=out_shape,
         scratch_shapes=[
@@ -396,7 +396,7 @@
     )(*scalars, *arrays, *blocks)
 
 
-def output_kernel(where_ref, left_mine, left_other, ids, scale, *refs, vocab_block):
+def output_kernel(where_ref, left, matches, scale, *refs):
     mine, others = refs[:4], refs[4:8]
     attn, embed, held, sems = refs[8:]
     shard, layer, step = where_ref[0], where_ref[1], pl.program_id(0)
@@ -415,16 +415,14 @@
 
     def arrived(slot):
         pltpu.make_async_copy(mine[0], held.at[slot], sems.at[slot]).wait()
-        return held[slot]
 
     for slot in range(4):
 
         @pl.when(step == slot)
         def _():
-            same = first if slot < 3 else jnp.logical_not(first)
-            left = jnp.where(same, left_mine[...], left_other[...])
+            arrived(slot)
             attn[0] = learning_rate * lax.dot_general(
-                left, arrived(slot), (((1,), (1,)), ((), ())), preferred_element_type=jnp.float32
+                left[...], held[slot], (((1,), (1,)), ((), ())), preferred_element_type=jnp.float32
             )
 
     @pl.when(step == 4)
@@ -433,52 +431,53 @@
 
     @pl.when(step >= 4)
     def _():
-        cols = embed.shape[1]
-        start = layer * vocab_block + (step - 4) * cols
-        here = lax.broadcasted_iota(jnp.int32, (ids.shape[0], cols), 1) + start
-        matches = (here == ids[...]).astype(jnp.float32).astype(jnp.bfloat16)
-        embed[...] = jnp.dot(held[4], matches, preferred_element_type=jnp.float32) * scale[...]
-
-
-def output_products(where, bundle, ids, scale, mine, others):
+        product = jnp.dot(held[4], matches[...], preferred_element_type=jnp.float32)
+        embed[...] = product * scale[...]
+
+
+def output_products(where, bundle, matches, scale, mine, others):
     cols, tokens_all = mine[0].shape
     vocab_block = scale.shape[1]
     parts = 4
     part = vocab_block // parts
 
-    def embed_place(step):
+    def embed_place(step, where):
         return (0, jnp.maximum(step - 4, 0))
 
+    def left_place(step, where):
+        return (jnp.where(step < 3, where[0], 1 - where[0]), 0)
+
     return pl.pallas_call(
-        functools.partial(output_kernel, vocab_block=vocab_block),
-        grid=(4 + parts,),
+        output_kernel,
+        grid_spec=pltpu.PrefetchScalarGridSpec(
+            num_scalar_prefetch=1,
+            grid=(4 + parts,),
+            in_specs=[
+                pl.BlockSpec((cols, tokens_all), left_place),
+                pl.BlockSpec((tokens_all, part), embed_place),
+                pl.BlockSpec((1, part), embed_place),
+            ]
+            + [pl.BlockSpec(memory_space=pl.ANY)] * 8,
+            out_specs=(
+                pl.BlockSpec((1, cols, cols), lambda step, where: (jnp.minimum(step, 3), 0, 0)),
+                pl.BlockSpec((cols, part), embed_place),
+            ),
+            scratch_shapes=[
+                pltpu.VMEM((5, cols, tokens_all), jnp.bfloat16),
+                pltpu.SemaphoreType.DMA((5,)),
+            ],
+        ),
         out_shape=(
             jax.ShapeDtypeStruct((4, cols, cols), jnp.float32),
             jax.ShapeDtypeStruct((cols, vocab_block), jnp.float32),
         ),
-        in_specs=[
-            pl.BlockSpec(memory_space=pltpu.SMEM),
-            pl.BlockSpec((cols, tokens_all), lambda step: (0, 0)),
-            pl.BlockSpec((cols, tokens_all), lambda step: (1, 0)),
-            pl.BlockSpec((tokens_all, 1), lambda step: (0, 0)),
-            pl.BlockSpec((1, part), embed_place),
-        ]
-        + [pl.BlockSpec(memory_space=pltpu.HBM)] * 8,
-        out_specs=(
-            pl.BlockSpec((1, cols, cols), lambda step: (jnp.minimum(step, 3), 0, 0)),
-            pl.BlockSpec((cols, part), embed_place),
-        ),
-        scratch_shapes=[
-            pltpu.VMEM((5, cols, tokens_all), jnp.bfloat16),
-            pltpu.SemaphoreType.DMA((5,)),
-        ],
         compiler_params=params(),
         cost_estimate=pl.CostEstimate(
             flops=2 * cols * tokens_all * (4 * cols + vocab_block),
             bytes_accessed=4 * cols * (4 * cols + vocab_block) + 14 * cols * tokens_all,
             transcendentals=0,
         ),
-    )(where, bundle, bundle, ids, scale, *mine, *others)
+    )(where, bundle, matches, scale, *mine, *others)
 
 
 def layer_plan(
@@ -513,19 +512,7 @@
     def held_by(layer_index):
         return jnp.where(layer_index == 3, 3, lax.rem(layer_index + 1, 3))
 
-    def old_block(factors, step, start, size):
-        away = by_index(factors, held_by(layer ^ step))[start : start + size]
-        away = away.astype(jnp.bfloat16)
-        return swap(away, "tensor", n_tensor, step) if step else away
-
-    part_rows = row_block // 2
-    early = old_block(old_factors, 2, 0, part_rows)
-    later_factors = lax.optimization_barrier(old_factors)
-
     by_feature = jnp.swapaxes(activations, 1, 2)
-    kept_tokens = lax.dynamic_slice_in_dim(by_feature, shard * owned, owned, 0)
-    sent_tokens = lax.dynamic_slice_in_dim(by_feature, (1 - shard) * owned, owned, 0)
-    other_tokens = swap(sent_tokens, "shard", n_shard, 1)
     diagonals = local_diagonals(old_factors) * (layer == section).astype(jnp.float32)
     extra = jnp.pad(split_three(diagonals), ((0, 0), (0, 0), (0, 3 * tokens - col_block)))
     extra = jnp.pad(extra.reshape(owned, 9, tokens), ((0, 0), (0, 7), (0, 0)))
@@ -533,18 +520,42 @@
     for step in range(n_tensor):
         factor = held_by(layer ^ step)
         message = jnp.concatenate(
-            [by_index(kept_tokens, factor), by_index(other_tokens, factor), by_index(extra, factor)],
+            [
+                by_index(by_feature, shard * owned + factor),
+                by_index(by_feature, (1 - shard) * owned + factor),
+                by_index(extra, factor),
+            ],
             axis=0,
         )
         collected.append(swap(message, "tensor", n_tensor, step) if step else message)
-    collected, early = lax.optimization_barrier((jnp.stack(collected), early))
+    collected = jnp.stack(collected)
+    other_tokens = swap(
+        collected[:, features_dev : 2 * features_dev], "shard", n_shard, 1
+    )
+
+    part_rows = row_block // 2
+
+    def old_block(factors, step, start, size):
+        away = by_index(factors, held_by(layer ^ step))[start : start + size]
+        return away.astype(jnp.bfloat16)
+
+    early = swap(old_block(old_factors, 2, 0, part_rows), "tensor", n_tensor, 2)
+    later_factors = lax.optimization_barrier(old_factors)
+    late = old_block(later_factors, 2, part_rows, part_rows)
+    blocks = [old_block(later_factors, step, 0, row_block) for step in (0, 1, 3)]
+    other_tokens, collected, early, late, blocks = lax.optimization_barrier(
+        (other_tokens, collected, early, late, blocks)
+    )
+    collected = jnp.concatenate(
+        [collected[:, :features_dev], other_tokens, collected[:, 2 * features_dev :]], axis=1
+    )
     gathered = lax.all_gather(collected, "section", axis=0)
-    late = old_block(later_factors, 2, part_rows, part_rows)
+    late = swap(late, "tensor", n_tensor, 2)
     blocks = [
-        old_block(later_factors, 0, 0, row_block),
-        old_block(later_factors, 1, 0, row_block),
+        blocks[0],
+        swap(blocks[1], "tensor", n_tensor, 1),
         jnp.concatenate([early, late], axis=0),
-        old_block(later_factors, 3, 0, row_block),
+        swap(blocks[2], "tensor", n_tensor, 3),
     ]
 
     def both_shards(value, axis):
@@ -562,12 +573,12 @@
     norm_sums = norm_sums + swap(norm_sums, "shard", n_shard, 1)
     vocab_block = old_embed_diag.shape[0]
     ids_here = layer * vocab_block + lax.iota(jnp.int32, vocab_block)
-    counts = jnp.sum((ids_all[:, None] == ids_here[None, :]).astype(jnp.float32), axis=0)
+    matches = (ids_all[:, None] == ids_here[None, :]).astype(jnp.bfloat16)
+    counts = jnp.sum(matches, axis=0, dtype=jnp.float32)
     divisor = factor_decay * old_embed_diag + (1.0 - factor_decay) * (counts / tokens_all) + damping
     embed_scale = (learning_rate / divisor)[None, :]
-    embed_ids = ids_all[:, None]
-    gathered, grad_all, embed_ids, embed_scale, norm_sums = lax.optimization_barrier(
-        (gathered, grad_all, embed_ids, embed_scale, norm_sums)
+    gathered, grad_all, matches, embed_scale, norm_sums = lax.optimization_barrier(
+        (gathered, grad_all, matches, embed_scale, norm_sums)
     )
 
     features, rows, low_diag, trace = lay_out(
@@ -659,7 +670,9 @@
     codes = jnp.concatenate([codes[:, :tokens_all], codes_tail], axis=0)
     near_1, over_0 = lax.optimization_barrier((near_1, over_0))
     over_1 = across(near_1, 1)
-    left_here, near_2, codes = lax.optimization_barrier((left_here, near_2, codes))
+    left_here, near_2, codes, over_1 = lax.optimization_barrier(
+        (left_here, near_2, codes, over_1)
+    )
     left_there = lax.ppermute(
         jnp.concatenate([left_here, codes], axis=0),
         everywhere,
@@ -669,11 +682,11 @@
     over_2 = across(near_2, 2)
     codes = jnp.where(shard == 1, codes, left_there[col_block:])
     bundle = jnp.concatenate([left_here, left_there[:col_block], codes], axis=0)
-    bundle, over_1 = lax.optimization_barrier((bundle, over_1))
+    bundle, near_3 = lax.optimization_barrier((bundle, near_3))
     to_side = [(spot(x, t, t), spot(x, t, t ^ 2)) for x in planes for t in layers]
     bundle = jnp.where(section == layer, bundle, lax.ppermute(bundle, everywhere, to_side))
-    bundle, near_3, over_2 = lax.optimization_barrier((bundle, near_3, over_2))
     over_3 = across(near_3, 3)
+    bundle, over_2, over_3 = lax.optimization_barrier((bundle, over_2, over_3))
     to_core = [
         (spot(x, t, t ^ a), spot(x, t, t ^ a ^ 1)) for x in planes for t in layers for a in (0, 2)
     ]
@@ -689,7 +702,7 @@
     precond_attn, embed_columns = output_products(
         jnp.stack([shard, layer]),
         bundle,
-        embed_ids,
+        matches,
         embed_scale,
         (own, near_1, near_2, near_3),
         (over_0, over_1, over_2, over_3),

time: 277 us -> 274 us (0.989)
  the two profiles are of different devices: /device:TPU:0 before, /device:TPU:31 now
where the time goes in v7:
time: 274 us; the launch traced here: 273 us
  waiting for transfers between devices  134 us (49%)
  starting transfers between devices  62.9 us (23%)
  Pallas kernels  30.7 us (11%)
  between operations  16.1 us (6%)
  other arithmetic  16 us (6%)
  local copies, waits for them, and re-layouts  11.3 us (4%)
    ppermute x18, waiting for transfers between devices, swap(): return lax.ppermute(value, axis, [(i, i ^ step) for i in range(size)])  95.9 us
    ppermute x4, waiting for transfers between devices, across(): return lax.ppermute(value, axes, moves)  20 us
    ppermute x18, starting transfers between devices, swap(): return lax.ppermute(value, axis, [(i, i ^ step) for i in range(size)])  16.6 us
    ppermute x1, starting transfers between devices, layer_plan(): lax.ppermute(jnp.concatenate([left_here, codes], axis=0), everywhere, [(s...  16.4 us
    pallas_call x3, Pallas kernels, chain_call(): pl.pallas_call(kernel, in_specs=[pl.BlockSpec(memory_space=pltpu.SMEM)] *...  15.9 us
    ppermute x4, starting transfers between devices, across(): return lax.ppermute(value, axes, moves)  13.5 us
    pallas_call x1, Pallas kernels, output_products(): pl.pallas_call(output_kernel, grid_spec=pltpu.PrefetchScalarGridSpec(num_...  9.53 us
    ppermute x3, starting transfers between devices, send(): return lax.ppermute(value, axes, moves)  8.11 us
  transfers between devices with their start and end apart: 31, of which 17 were waited for; matrix products, arithmetic and copies ran while one was open for 7% of the time, Pallas kernels for 2%

profile of v7, /device:TPU:31, one launch (start us, length us, event | category | flops | bytes accessed | tf_op | source)
XLA Modules:
  0.0 272.8 jit_solution(17336470320344206399)
XLA Ops:
  16.8 15.9 %collective-permute-done.1 = bf16[304,256]{1,0:T(8,128)(2,1)S(1)} collective-permute-done((bf16[304,256]{1,0:T(8,128)(2,1)S(1)}, bf16[304,256]{1,0:T(8,128)(2,1)S(1)}, u32[]{:S(2)}, u32[]{:S(2)}) %collective-permute-start.1) | collective-permute-done | bytes 155680 | tf_op jit(solution)/shard_map/ppermute | solution.py:169
  34.3 3.6 %fusion.5 = (bf16[576,576]{1,0:T(8,128)(2,1)}, bf16[576,576]{1,0:T(8,128)(2,1)}, bf16[576,576]{1,0:T(8,128)(2,1)S(1)}) fusion(f32[4,576,576]{2,1,0:T(8,128)} %param.12, s32[]{:T(128)S(6)} %select_n.162, s32[]{:T(128)S(6)} %select_n.154, s32[]{:T(128)S(6)} %select_n.150), kind=kLoop, calls=%fused_computation.19 | loop fusion | bytes 3981324 | tf_op jit(solution)/shard_map/convert_element_type | solution.py:540
  38.0 2.7 collective-permute-done.4
  50.0 44.2 %collective-permute-done.9 = bf16[288,576]{1,0:T(8,128)(2,1)S(1)} collective-permute-done((bf16[288,576]{1,0:T(8,128)(2,1)S(1)}, bf16[288,576]{1,0:T(8,128)(2,1)S(1)}, u32[]{:S(2)}, u32[]{:S(2)}) %collective-permute-start.9) | collective-permute-done | bytes 331808 | tf_op jit(solution)/shard_map/ppermute | solution.py:169
  96.0 2.8 %shard_map.111 = (bf16[2,2304,256]{2,1,0:T(8,128)(2,1)S(1)}, bf16[256,2304]{1,0:T(8,128)(2,1)S(1)}, f32[4,1,576]{2,1,0:T(1,128)S(1)}, f32[1]{0:T(128)}) custom-call(s32[3]{0:T(128)S(1)} %pad_add_fusion.1.place_ref, bf16[4,4,304,256]{3,2,1,0:T(8,128)(2,1)S(1)} %bitcast.90), custom_call_target="tpu_custom_call" | custom-call | flops 37748736 | bytes 8257536 | tf_op jit(solution)/shard_map/pallas_call | solution.py:237
  99.5 4.4 %collective-permute-start.11 = (bf16[576,576]{1,0:T(8,128)(2,1)S(1)}, bf16[576,576]{1,0:T(8,128)(2,1)S(1)}, u32[]{:S(2)}, u32[]{:S(2)}) collective-permute-start(bf16[576,576]{1,0:T(8,128)(2,1)S(1)} %shard_map.112.refs_0_), channel_id=1, source_target_pairs={{0,1},{1,0},{2,3},{3,2},{4,5},{5,4},{6,7},{7,6},{8,9},{9,8},{10,11... | collective-permute-start | bytes 1990664 | tf_op jit(solution)/shard_map/ppermute | solution.py:169
  108.9 5.2 %shard_map.116 = (f32[2,256,576]{2,1,0:T(8,128)S(1)}, bf16[256,1152]{1,0:T(8,128)(2,1)S(1)}) custom-call(s32[1]{0:T(128)} %bitcast.2.place_ref, f32[1]{0:T(128)S(6)} %div.21.scale_ref, bf16[256,2304]{1,0:T(8,128)(2,1)S(1)} %get-tuple-element.43.rows, f32[4,1,576]{2,1,0:T(1,128)S(1)} %get-tuple-element.44.diag, bf16[576,576]{1,0:T(8,128)(2,1)S(1)} %shard_map.112.refs_0_, ...), custom_call_target="tpu_custom_call" | custom-call | flops 1358954496 | bytes 5308416 | tf_op jit(solution)/shard_map/pallas_call | solution.py:379
  114.4 14.3 %collective-permute-done.15.theirs = bf16[256,1152]{1,0:T(8,128)(2,1)S(1)} collective-permute-done((bf16[256,1152]{1,0:T(8,128)(2,1)S(1)}, bf16[256,1152]{1,0:T(8,128)(2,1)S(1)}, u32[]{:S(2)}, u32[]{:S(2)}) %collective-permute-start.15) | collective-permute-done | bytes 589856 | tf_op jit(solution)/shard_map/ppermute | solution.py:169
  128.7 5.6 %shard_map.117 = (f32[2,256,576]{2,1,0:T(8,128)S(1)}, bf16[256,1152]{1,0:T(8,128)(2,1)S(1)}) custom-call(s32[1]{0:T(128)} %bitcast.2.place_ref, f32[1]{0:T(128)S(6)} %div.21.scale_ref, bf16[256,1152]{1,0:T(8,128)(2,1)S(1)} %get-tuple-element.51.mine, bf16[256,1152]{1,0:T(8,128)(2,1)S(1)} %collective-permute-done.15.theirs, ...), custom_call_target="tpu_custom_call" | custom-call | flops 1358954496 | bytes 5308416 | tf_op jit(solution)/shard_map/pallas_call | solution.py:379
  134.7 13.4 %collective-permute-done.16.theirs = bf16[256,1152]{1,0:T(8,128)(2,1)S(1)} collective-permute-done((bf16[256,1152]{1,0:T(8,128)(2,1)S(1)}, bf16[256,1152]{1,0:T(8,128)(2,1)S(1)}, u32[]{:S(2)}, u32[]{:S(2)}) %collective-permute-start.16) | collective-permute-done | bytes 589856 | tf_op jit(solution)/shard_map/ppermute | solution.py:169
  148.1 5.0 %shard_map.118 = (bf16[576,256]{1,0:T(8,128)(2,1)S(1)}, bf16[576,256]{1,0:T(8,128)(2,1)S(1)}) custom-call(s32[1]{0:T(128)} %bitcast.2.place_ref, f32[1]{0:T(128)S(6)} %div.21.scale_ref, bf16[256,1152]{1,0:T(8,128)(2,1)S(1)} %get-tuple-element.53.mine, bf16[256,1152]{1,0:T(8,128)(2,1)S(1)} %collective-permute-done.16.theirs, ...), custom_call_target="tpu_custom_call" | custom-call | flops 1358954496 | bytes 5308416 | tf_op jit(solution)/shard_map/pallas_call | solution.py:379
  158.0 3.1 %collective-permute-start.22 = (bf16[576,512]{1,0:T(8,128)(2,1)S(1)}, bf16[576,512]{1,0:T(8,128)(2,1)S(1)}, u32[]{:S(2)}, u32[]{:S(2)}) collective-permute-start(bf16[576,512]{1,0:T(8,128)(2,1)S(1)} %maximum_select_fusion.refs_0_), channel_id=1, source_target_pairs={{0,16},{4,20},{12,28},{16,0},{28,12},{1,17},{5,21},{13,29},{17,1},... | collective-permute-start | bytes 1769480 | tf_op jit(solution)/shard_map/ppermute | solution.py:634
  167.0 5.5 %collective-permute-start.19 = (bf16[576,512]{1,0:T(8,128)(2,1)S(1)}, bf16[576,512]{1,0:T(8,128)(2,1)S(1)}, u32[]{:S(2)}, u32[]{:S(2)}) collective-permute-start(bf16[576,512]{1,0:T(8,128)(2,1)S(1)} %maximum_select_fusion.refs_0_), channel_id=1, source_target_pairs={{0,8},{4,12},{12,4},{16,24},{28,20},{1,9},{5,13},{13,5},{17,25},{2... | collective-permute-start | bytes 1769480 | tf_op jit(solution)/shard_map/ppermute | solution.py:625
  176.0 7.7 %collective-permute-done.19.refs_2_ = bf16[576,512]{1,0:T(8,128)(2,1)S(1)} collective-permute-done((bf16[576,512]{1,0:T(8,128)(2,1)S(1)}, bf16[576,512]{1,0:T(8,128)(2,1)S(1)}, u32[]{:S(2)}, u32[]{:S(2)}) %collective-permute-start.19) | collective-permute-done | bytes 589856 | tf_op jit(solution)/shard_map/ppermute | solution.py:625
  184.6 16.4 %collective-permute-start.24 = (bf16[608,512]{1,0:T(8,128)(2,1)}, bf16[608,512]{1,0:T(8,128)(2,1)}, u32[]{:S(2)}, u32[]{:S(2)}) collective-permute-start(bf16[608,512]{1,0:T(8,128)(2,1)} %pad_maximum_fusion.4), channel_id=1, source_target_pairs={{0,16},{5,21},{10,26},{15,31},{16,0},{21,5},{26,10},{31,15}} | collective-permute-start | bytes 1867784 | tf_op jit(solution)/shard_map/ppermute | solution.py:676
  202.3 6.6 %collective-permute-done.24 = bf16[608,512]{1,0:T(8,128)(2,1)} collective-permute-done((bf16[608,512]{1,0:T(8,128)(2,1)}, bf16[608,512]{1,0:T(8,128)(2,1)}, u32[]{:S(2)}, u32[]{:S(2)}) %collective-permute-start.24) | collective-permute-done | bytes 622624 | tf_op jit(solution)/shard_map/ppermute | solution.py:676
  211.9 2.3 collective-permute-start.26
  215.7 8.3 %collective-permute-start.28 = (bf16[576,512]{1,0:T(8,128)(2,1)S(1)}, bf16[576,512]{1,0:T(8,128)(2,1)S(1)}, u32[]{:S(2)}, u32[]{:S(2)}) collective-permute-start(bf16[576,512]{1,0:T(8,128)(2,1)S(1)} %collective-permute-done.25.refs_3_), channel_id=1, source_target_pairs={{0,16},{8,24},{12,28},{16,0},{28,12},{1,17},{9,25},{13,29},{17,1},... | collective-permute-start | bytes 1769480 | tf_op jit(solution)/shard_map/ppermute | solution.py:634
  224.0 3.0 %collective-permute-done.26 = bf16[1184,512]{1,0:T(8,128)(2,1)} collective-permute-done((bf16[1184,512]{1,0:T(8,128)(2,1)}, bf16[1184,512]{1,0:T(8,128)(2,1)}, u32[]{:S(2)}, u32[]{:S(2)}) %collective-permute-start.26) | collective-permute-done | bytes 1212448 | tf_op jit(solution)/shard_map/ppermute | solution.py:687
  227.0 2.4 broadcast_select_fusion
  229.5 6.4 %collective-permute-done.27.refs_6_ = bf16[576,512]{1,0:T(8,128)(2,1)S(1)} collective-permute-done((bf16[576,512]{1,0:T(8,128)(2,1)S(1)}, bf16[576,512]{1,0:T(8,128)(2,1)S(1)}, u32[]{:S(2)}, u32[]{:S(2)}) %collective-permute-start.27) | collective-permute-done | bytes 589856 | tf_op jit(solution)/shard_map/ppermute | solution.py:634
  236.7 11.7 %collective-permute-done.28.refs_7_ = bf16[576,512]{1,0:T(8,128)(2,1)S(1)} collective-permute-done((bf16[576,512]{1,0:T(8,128)(2,1)S(1)}, bf16[576,512]{1,0:T(8,128)(2,1)S(1)}, u32[]{:S(2)}, u32[]{:S(2)}) %collective-permute-start.28) | collective-permute-done | bytes 589856 | tf_op jit(solution)/shard_map/ppermute | solution.py:634
  249.2 3.4 %collective-permute-start.29 = (bf16[1184,512]{1,0:T(8,128)(2,1)}, bf16[1184,512]{1,0:T(8,128)(2,1)}, u32[]{:S(2)}, u32[]{:S(2)}) collective-permute-start(bf16[1184,512]{1,0:T(8,128)(2,1)} %broadcast_select_fusion), channel_id=1, source_target_pairs={{0,1},{2,3},{5,4},{7,6},{10,11},{8,9},{15,14},{13,12},{16,17},{18,... | collective-permute-start | bytes 3637256 | tf_op jit(solution)/shard_map/ppermute | solution.py:694
  256.4 9.5 %shard_map.119 = (f32[4,576,576]{2,1,0:T(8,128)}, f32[576,2048]{1,0:T(8,128)}) custom-call(s32[2]{0:T(128)S(1)} %pad_add_fusion.where_ref, bf16[1184,512]{1,0:T(8,128)(2,1)S(1)} %broadcast_select_fusion.1.left, bf16[512,2048]{1,0:T(8,128)(2,1)S(1)} %copy-done.1, f32[1,2048]{1,0:T(1,128)S(1)} %bitcast.91, bf16[576,512]{1,0:T(8,128)(2,1)S(1)} %maximum_select_fusion.refs_0_, ...), custom_call_target="tpu_custom_call" | custom-call | flops 2566914048 | bytes 14155776 | tf_op jit(solution)/shard_map/pallas_call | solution.py:450
  (144 shorter events, 53.0 us)
Async XLA Ops:
  7.2 87.1 %all-gather.3.cloned.1.call-start = ((), (), s32[]{:S(2)}) async-start(), calls=%async_computation | async-start | bytes 3112960 | tf_op jit(solution)/shard_map/all_gather | solution.py:552
  10.0 6.8 %collective-permute-start.2 = (bf16[304,256]{1,0:T(8,128)(2,1)S(1)}, bf16[304,256]{1,0:T(8,128)(2,1)S(1)}, u32[]{:S(2)}, u32[]{:S(2)}) collective-permute-start(bf16[304,256]{1,0:T(8,128)(2,1)S(1)} %pad_maximum_fusion.7), channel_id=1, source_target_pairs={{0,12},{4,8},{8,4},{12,0},{1,13},{5,9},{9,5},{13,1},{2,14},{6,10},... | collective-permute-start | bytes 466952 | tf_op jit(solution)/shard_map/ppermute | solution.py:169
  10.1 22.7 %collective-permute-start.1 = (bf16[304,256]{1,0:T(8,128)(2,1)S(1)}, bf16[304,256]{1,0:T(8,128)(2,1)S(1)}, u32[]{:S(2)}, u32[]{:S(2)}) collective-permute-start(bf16[304,256]{1,0:T(8,128)(2,1)S(1)} %pad_maximum_fusion.6), channel_id=1, source_target_pairs={{0,8},{4,12},{8,0},{12,4},{1,9},{5,13},{9,1},{13,5},{2,10},{6,14},... | collective-permute-start | bytes 466952 | tf_op jit(solution)/shard_map/ppermute | solution.py:169
  11.5 21.2 %collective-permute-start = (bf16[304,256]{1,0:T(8,128)(2,1)S(1)}, bf16[304,256]{1,0:T(8,128)(2,1)S(1)}, u32[]{:S(2)}, u32[]{:S(2)}) collective-permute-start(bf16[304,256]{1,0:T(8,128)(2,1)S(1)} %pad_maximum_fusion.5), channel_id=1, source_target_pairs={{0,4},{4,0},{8,12},{12,8},{1,5},{5,1},{9,13},{13,9},{2,6},{6,2},{1... | collective-permute-start | bytes 466952 | tf_op jit(solution)/shard_map/ppermute | solution.py:169
  14.9 25.7 %collective-permute-start.4 = (bf16[288,576]{1,0:T(8,128)(2,1)S(1)}, bf16[288,576]{1,0:T(8,128)(2,1)S(1)}, u32[]{:S(2)}, u32[]{:S(2)}) collective-permute-start(bf16[288,576]{1,0:T(8,128)(2,1)S(1)} %fusion.6), channel_id=1, source_target_pairs={{0,8},{4,12},{8,0},{12,4},{1,9},{5,13},{9,1},{13,5},{2,10},{6,14},... | collective-permute-start | bytes 995336 | tf_op jit(solution)/shard_map/ppermute | solution.py:169
  32.9 7.8 %collective-permute-start.3 = (bf16[4,144,256]{2,1,0:T(8,128)(2,1)S(1)}, bf16[4,144,256]{2,1,0:T(8,128)(2,1)S(1)}, u32[]{:S(2)}, u32[]{:S(2)}) collective-permute-start(bf16[4,144,256]{2,1,0:T(8,128)(2,1)S(1)} %slice.89), channel_id=1, source_target_pairs={{0,16},{16,0},{1,17},{17,1},{2,18},{18,2},{3,19},{19,3},{4,20},{20... | collective-permute-start | bytes 884744 | tf_op jit(solution)/shard_map/ppermute | solution.py:169
  41.6 8.3 %collective-permute-start.5 = (bf16[8,256]{1,0:T(8,128)(2,1)S(1)}, bf16[8,256]{1,0:T(8,128)(2,1)S(1)}, u32[]{:S(2)}, u32[]{:S(2)}) collective-permute-start(bf16[8,256]{1,0:T(8,128)(2,1)S(1)} %copy-done.13), channel_id=1, source_target_pairs={{0,16},{16,0},{1,17},{17,1},{2,18},{18,2},{3,19},{19,3},{4,20},{20... | collective-permute-start | bytes 12296 | tf_op jit(solution)/shard_map/ppermute | solution.py:169
  46.6 57.2 %collective-permute-start.8 = (bf16[576,576]{1,0:T(8,128)(2,1)}, bf16[576,576]{1,0:T(8,128)(2,1)S(1)}, u32[]{:S(2)}, u32[]{:S(2)}) collective-permute-start(bf16[576,576]{1,0:T(8,128)(2,1)} %get-tuple-element.47), channel_id=1, source_target_pairs={{0,4},{4,0},{8,12},{12,8},{1,5},{5,1},{9,13},{13,9},{2,6},{6,2},{1... | collective-permute-start | bytes 1990664 | tf_op jit(solution)/shard_map/ppermute | solution.py:169
  46.6 59.1 %collective-permute-start.10 = (bf16[576,576]{1,0:T(8,128)(2,1)}, bf16[576,576]{1,0:T(8,128)(2,1)S(1)}, u32[]{:S(2)}, u32[]{:S(2)}) collective-permute-start(bf16[576,576]{1,0:T(8,128)(2,1)} %get-tuple-element.50), channel_id=1, source_target_pairs={{0,12},{4,8},{8,4},{12,0},{1,13},{5,9},{9,5},{13,1},{2,14},{6,10},... | collective-permute-start | bytes 1990664 | tf_op jit(solution)/shard_map/ppermute | solution.py:169
  47.9 46.3 %collective-permute-start.9 = (bf16[288,576]{1,0:T(8,128)(2,1)S(1)}, bf16[288,576]{1,0:T(8,128)(2,1)S(1)}, u32[]{:S(2)}, u32[]{:S(2)}) collective-permute-start(bf16[288,576]{1,0:T(8,128)(2,1)S(1)} %fusion.7), channel_id=1, source_target_pairs={{0,8},{4,12},{8,0},{12,4},{1,9},{5,13},{9,1},{13,5},{2,10},{6,14},... | collective-permute-start | bytes 995336 | tf_op jit(solution)/shard_map/ppermute | solution.py:169
  99.5 7.7 %collective-permute-start.11 = (bf16[576,576]{1,0:T(8,128)(2,1)S(1)}, bf16[576,576]{1,0:T(8,128)(2,1)S(1)}, u32[]{:S(2)}, u32[]{:S(2)}) collective-permute-start(bf16[576,576]{1,0:T(8,128)(2,1)S(1)} %shard_map.112.refs_0_), channel_id=1, source_target_pairs={{0,1},{1,0},{2,3},{3,2},{4,5},{5,4},{6,7},{7,6},{8,9},{9,8},{10,11... | collective-permute-start | bytes 1990664 | tf_op jit(solution)/shard_map/ppermute | solution.py:169
  114.1 14.6 %collective-permute-start.15 = (bf16[256,1152]{1,0:T(8,128)(2,1)S(1)}, bf16[256,1152]{1,0:T(8,128)(2,1)S(1)}, u32[]{:S(2)}, u32[]{:S(2)}) collective-permute-start(bf16[256,1152]{1,0:T(8,128)(2,1)S(1)} %get-tuple-element.51.mine), channel_id=1, source_target_pairs={{0,2},{1,3},{2,0},{3,1},{4,6},{5,7},{6,4},{7,5},{8,10},{9,11},{10,... | collective-permute-start | bytes 1769480 | tf_op jit(solution)/shard_map/ppermute | solution.py:169
  134.4 13.7 %collective-permute-start.16 = (bf16[256,1152]{1,0:T(8,128)(2,1)S(1)}, bf16[256,1152]{1,0:T(8,128)(2,1)S(1)}, u32[]{:S(2)}, u32[]{:S(2)}) collective-permute-start(bf16[256,1152]{1,0:T(8,128)(2,1)S(1)} %get-tuple-element.53.mine), channel_id=1, source_target_pairs={{0,2},{1,3},{2,0},{3,1},{4,6},{5,7},{6,4},{7,5},{8,10},{9,11},{10,... | collective-permute-start | bytes 1769480 | tf_op jit(solution)/shard_map/ppermute | solution.py:169
  156.6 15.9 %collective-permute-start.21 = (bf16[576,512]{1,0:T(8,128)(2,1)S(1)}, bf16[576,512]{1,0:T(8,128)(2,1)S(1)}, u32[]{:S(2)}, u32[]{:S(2)}) collective-permute-start(bf16[576,512]{1,0:T(8,128)(2,1)S(1)} %maximum_select_fusion.refs_0_), channel_id=1, source_target_pairs={{0,4},{4,0},{12,8},{16,20},{28,24},{1,5},{5,1},{13,9},{17,21},{29,... | collective-permute-start | bytes 1769480 | tf_op jit(solution)/shard_map/ppermute | solution.py:625
  158.0 16.4 %collective-permute-start.22 = (bf16[576,512]{1,0:T(8,128)(2,1)S(1)}, bf16[576,512]{1,0:T(8,128)(2,1)S(1)}, u32[]{:S(2)}, u32[]{:S(2)}) collective-permute-start(bf16[576,512]{1,0:T(8,128)(2,1)S(1)} %maximum_select_fusion.refs_0_), channel_id=1, source_target_pairs={{0,16},{4,20},{12,28},{16,0},{28,12},{1,17},{5,21},{13,29},{17,1},... | collective-permute-start | bytes 1769480 | tf_op jit(solution)/shard_map/ppermute | solution.py:634
  163.4 12.5 %collective-permute-start.18 = (bf16[576,512]{1,0:T(8,128)(2,1)S(1)}, bf16[576,512]{1,0:T(8,128)(2,1)S(1)}, u32[]{:S(2)}, u32[]{:S(2)}) collective-permute-start(bf16[576,512]{1,0:T(8,128)(2,1)S(1)} %maximum_select_fusion.refs_0_), channel_id=1, source_target_pairs={{8,0},{9,5},{11,15},{24,16},{25,21},{27,31}} | collective-permute-start | bytes 1769480 | tf_op jit(solution)/shard_map/ppermute | solution.py:642
  165.7 9.4 %collective-permute-start.20 = (f32[8,576]{1,0:T(8,128)}, f32[8,576]{1,0:T(8,128)}, u32[]{:S(2)}, u32[]{:S(2)}) collective-permute-start(f32[8,576]{1,0:T(8,128)} %convolution_multiply_fusion), channel_id=1, source_target_pairs={{4,0},{6,10},{7,15},{20,16},{22,26},{23,31}} | collective-permute-start | bytes 55304 | tf_op jit(solution)/shard_map/ppermute | solution.py:642
  167.0 16.7 %collective-permute-start.19 = (bf16[576,512]{1,0:T(8,128)(2,1)S(1)}, bf16[576,512]{1,0:T(8,128)(2,1)S(1)}, u32[]{:S(2)}, u32[]{:S(2)}) collective-permute-start(bf16[576,512]{1,0:T(8,128)(2,1)S(1)} %maximum_select_fusion.refs_0_), channel_id=1, source_target_pairs={{0,8},{4,12},{12,4},{16,24},{28,20},{1,9},{5,13},{13,5},{17,25},{2... | collective-permute-start | bytes 1769480 | tf_op jit(solution)/shard_map/ppermute | solution.py:625
  174.4 9.3 %collective-permute-start.23 = (bf16[576,512]{1,0:T(8,128)(2,1)S(1)}, bf16[576,512]{1,0:T(8,128)(2,1)S(1)}, u32[]{:S(2)}, u32[]{:S(2)}) collective-permute-start(bf16[576,512]{1,0:T(8,128)(2,1)S(1)} %collective-permute-done.21.refs_1_), channel_id=1, source_target_pairs={{0,16},{4,20},{8,24},{20,4},{24,8},{1,17},{5,21},{9,25},{21,5},{25... | collective-permute-start | bytes 1769480 | tf_op jit(solution)/shard_map/ppermute | solution.py:634
  184.6 24.3 %collective-permute-start.24 = (bf16[608,512]{1,0:T(8,128)(2,1)}, bf16[608,512]{1,0:T(8,128)(2,1)}, u32[]{:S(2)}, u32[]{:S(2)}) collective-permute-start(bf16[608,512]{1,0:T(8,128)(2,1)} %pad_maximum_fusion.4), channel_id=1, source_target_pairs={{0,16},{5,21},{10,26},{15,31},{16,0},{21,5},{26,10},{31,15}} | collective-permute-start | bytes 1867784 | tf_op jit(solution)/shard_map/ppermute | solution.py:676
  201.0 10.9 %collective-permute-start.25 = (bf16[576,512]{1,0:T(8,128)(2,1)S(1)}, bf16[576,512]{1,0:T(8,128)(2,1)S(1)}, u32[]{:S(2)}, u32[]{:S(2)}) collective-permute-start(bf16[576,512]{1,0:T(8,128)(2,1)S(1)} %collective-permute-done.19.refs_2_), channel_id=1, source_target_pairs={{4,0},{8,12},{12,8},{20,16},{24,28},{5,1},{9,13},{13,9},{21,17},{2... | collective-permute-start | bytes 1769480 | tf_op jit(solution)/shard_map/ppermute | solution.py:625
  211.9 15.1 %collective-permute-start.26 = (bf16[1184,512]{1,0:T(8,128)(2,1)}, bf16[1184,512]{1,0:T(8,128)(2,1)}, u32[]{:S(2)}, u32[]{:S(2)}) collective-permute-start(bf16[1184,512]{1,0:T(8,128)(2,1)} %pad_maximum_fusion), channel_id=1, source_target_pairs={{0,2},{5,7},{10,8},{15,13},{16,18},{21,23},{26,24},{31,29}} | collective-permute-start | bytes 3637256 | tf_op jit(solution)/shard_map/ppermute | solution.py:687
  214.3 21.6 %collective-permute-start.27 = (bf16[576,512]{1,0:T(8,128)(2,1)S(1)}, bf16[576,512]{1,0:T(8,128)(2,1)S(1)}, u32[]{:S(2)}, u32[]{:S(2)}) collective-permute-start(bf16[576,512]{1,0:T(8,128)(2,1)S(1)} %collective-permute-done.19.refs_2_), channel_id=1, source_target_pairs={{4,20},{8,24},{12,28},{20,4},{24,8},{5,21},{9,25},{13,29},{21,5},{... | collective-permute-start | bytes 1769480 | tf_op jit(solution)/shard_map/ppermute | solution.py:634
  215.7 32.7 %collective-permute-start.28 = (bf16[576,512]{1,0:T(8,128)(2,1)S(1)}, bf16[576,512]{1,0:T(8,128)(2,1)S(1)}, u32[]{:S(2)}, u32[]{:S(2)}) collective-permute-start(bf16[576,512]{1,0:T(8,128)(2,1)S(1)} %collective-permute-done.25.refs_3_), channel_id=1, source_target_pairs={{0,16},{8,24},{12,28},{16,0},{28,12},{1,17},{9,25},{13,29},{17,1},... | collective-permute-start | bytes 1769480 | tf_op jit(solution)/shard_map/ppermute | solution.py:634
  (24 other events, 183.3 us)
Sparse Core Ops, SparseCore 0:
  41.7 26.2 all-gather.2

commit v8 on v7

--- a/solution.py
+++ b/solution.py
@@ -396,88 +396,107 @@
     )(*scalars, *arrays, *blocks)
 
 
-def output_kernel(where_ref, left, matches, scale, *refs):
-    mine, others = refs[:4], refs[4:8]
-    attn, embed, held, sems = refs[8:]
-    shard, layer, step = where_ref[0], where_ref[1], pl.program_id(0)
+def output_kernel(where_ref, scale, matches, *refs):
+    lefts, mine, others = (refs[:4], refs[4:8]), refs[8:12], refs[12:16]
+    attn, embed = refs[16:18]
+    left_held, held, found, attn_made, embed_made, sems, out_sems = refs[18:]
+    shard, layer, turn = where_ref[0], where_ref[1], where_ref[2]
     first = shard == 0
-
-    @pl.when(step == 0)
-    def _():
-        for slot, source in enumerate((0, 1, 3, 0, 3)):
-            from_mine = first if slot < 3 else jnp.logical_not(first)
+    rows, tokens_all = held.shape[1:]
+
+    found_copy = pltpu.make_async_copy(matches, found, sems.at[7])
+    for slot in range(2):
+        for group in range(2):
             for place in range(4):
-                for group, wanted in ((mine, from_mine), (others, jnp.logical_not(from_mine))):
-
-                    @pl.when(wanted & ((layer ^ source) == place))
-                    def _():
-                        pltpu.make_async_copy(group[place], held.at[slot], sems.at[slot]).start()
+
+                @pl.when((turn == place) & (((shard ^ slot) == group)))
+                def _():
+                    source = lefts[group][place].at[pl.ds(0, rows)]
+                    pltpu.make_async_copy(source, left_held.at[slot], sems.at[5 + slot]).start()
+
+        if slot == 0:
+            for index, source in enumerate((0, 1, 3, 0, 3)):
+                from_mine = first if index < 3 else jnp.logical_not(first)
+                for place in range(4):
+                    for group, wanted in ((mine, from_mine), (others, jnp.logical_not(from_mine))):
+
+                        @pl.when(wanted & ((layer ^ source) == place))
+                        def _():
+                            pltpu.make_async_copy(
+                                group[place], held.at[index], sems.at[index]
+                            ).start()
+
+            found_copy.start()
 
     def arrived(slot):
-        pltpu.make_async_copy(mine[0], held.at[slot], sems.at[slot]).wait()
-
+        target = held.at[slot] if slot < 5 else left_held.at[slot - 5]
+        pltpu.make_async_copy(mine[0], target, sems.at[slot]).wait()
+
+    results = []
+    arrived(5)
     for slot in range(4):
-
-        @pl.when(step == slot)
-        def _():
-            arrived(slot)
-            attn[0] = learning_rate * lax.dot_general(
-                left[...], held[slot], (((1,), (1,)), ((), ())), preferred_element_type=jnp.float32
+        if slot == 3:
+            arrived(6)
+        arrived(slot)
+        attn_made[slot] = learning_rate * lax.dot_general(
+            left_held[slot // 3],
+            held[slot],
+            (((1,), (1,)), ((), ())),
+            preferred_element_type=jnp.float32,
+        )
+        results.append(
+            pltpu.make_async_copy(attn_made.at[slot], attn.at[slot], out_sems.at[slot])
+        )
+        results[-1].start()
+    arrived(4)
+    found_copy.wait()
+    part = found.shape[1] // 4
+    for index in range(4):
+        cols = pl.ds(index * part, part)
+        product = jnp.dot(held[4], found[:, cols], preferred_element_type=jnp.float32)
+        embed_made[:, cols] = product * scale[:, cols]
+        results.append(
+            pltpu.make_async_copy(
+                embed_made.at[:, cols], embed.at[:, cols], out_sems.at[4 + index]
             )
-
-    @pl.when(step == 4)
-    def _():
-        arrived(4)
-
-    @pl.when(step >= 4)
-    def _():
-        product = jnp.dot(held[4], matches[...], preferred_element_type=jnp.float32)
-        embed[...] = product * scale[...]
-
-
-def output_products(where, bundle, matches, scale, mine, others):
+        )
+        results[-1].start()
+    for result in results:
+        result.wait()
+
+
+def output_products(where, scale, matches, lefts, mine, others):
     cols, tokens_all = mine[0].shape
     vocab_block = scale.shape[1]
-    parts = 4
-    part = vocab_block // parts
-
-    def embed_place(step, where):
-        return (0, jnp.maximum(step - 4, 0))
-
-    def left_place(step, where):
-        return (jnp.where(step < 3, where[0], 1 - where[0]), 0)
-
+    anywhere = pl.BlockSpec(memory_space=pl.ANY)
     return pl.pallas_call(
         output_kernel,
-        grid_spec=pltpu.PrefetchScalarGridSpec(
-            num_scalar_prefetch=1,
-            grid=(4 + parts,),
-            in_specs=[
-                pl.BlockSpec((cols, tokens_all), left_place),
-                pl.BlockSpec((tokens_all, part), embed_place),
-                pl.BlockSpec((1, part), embed_place),
-            ]
-            + [pl.BlockSpec(memory_space=pl.ANY)] * 8,
-            out_specs=(
-                pl.BlockSpec((1, cols, cols), lambda step, where: (jnp.minimum(step, 3), 0, 0)),
-                pl.BlockSpec((cols, part), embed_place),
-            ),
-            scratch_shapes=[
-                pltpu.VMEM((5, cols, tokens_all), jnp.bfloat16),
-                pltpu.SemaphoreType.DMA((5,)),
-            ],
-        ),
+        in_specs=[
+            pl.BlockSpec(memory_space=pltpu.SMEM),
+            pl.BlockSpec(memory_space=pltpu.VMEM),
+        ]
+        + [anywhere] * 17,
+        out_specs=(anywhere, anywhere),
         out_shape=(
             jax.ShapeDtypeStruct((4, cols, cols), jnp.float32),
             jax.ShapeDtypeStruct((cols, vocab_block), jnp.float32),
         ),
+        scratch_shapes=[
+            pltpu.VMEM((2, cols, tokens_all), jnp.bfloat16),
+            pltpu.VMEM((5, cols, tokens_all), jnp.bfloat16),
+            pltpu.VMEM((tokens_all, vocab_block), jnp.bfloat16),
+            pltpu.VMEM((4, cols, cols), jnp.float32),
+            pltpu.VMEM((cols, vocab_block), jnp.float32),
+            pltpu.SemaphoreType.DMA((8,)),
+            pltpu.SemaphoreType.DMA((8,)),
+        ],
         compiler_params=params(),
         cost_estimate=pl.CostEstimate(
             flops=2 * cols * tokens_all * (4 * cols + vocab_block),
             bytes_accessed=4 * cols * (4 * cols + vocab_block) + 14 * cols * tokens_all,
             transcendentals=0,
         ),
-    )(where, bundle, matches, scale, *mine, *others)
+    )(where, scale, matches, *lefts[0], *lefts[1], *mine, *others)
 
 
 def layer_plan(
@@ -533,31 +552,6 @@
         collected[:, features_dev : 2 * features_dev], "shard", n_shard, 1
     )
 
-    part_rows = row_block // 2
-
-    def old_block(factors, step, start, size):
-        away = by_index(factors, held_by(layer ^ step))[start : start + size]
-        return away.astype(jnp.bfloat16)
-
-    early = swap(old_block(old_factors, 2, 0, part_rows), "tensor", n_tensor, 2)
-    later_factors = lax.optimization_barrier(old_factors)
-    late = old_block(later_factors, 2, part_rows, part_rows)
-    blocks = [old_block(later_factors, step, 0, row_block) for step in (0, 1, 3)]
-    other_tokens, collected, early, late, blocks = lax.optimization_barrier(
-        (other_tokens, collected, early, late, blocks)
-    )
-    collected = jnp.concatenate(
-        [collected[:, :features_dev], other_tokens, collected[:, 2 * features_dev :]], axis=1
-    )
-    gathered = lax.all_gather(collected, "section", axis=0)
-    late = swap(late, "tensor", n_tensor, 2)
-    blocks = [
-        blocks[0],
-        swap(blocks[1], "tensor", n_tensor, 1),
-        jnp.concatenate([early, late], axis=0),
-        swap(blocks[2], "tensor", n_tensor, 3),
-    ]
-
     def both_shards(value, axis):
         other = swap(value, "shard", n_shard, 1)
         return jnp.where(
@@ -577,14 +571,48 @@
     counts = jnp.sum(matches, axis=0, dtype=jnp.float32)
     divisor = factor_decay * old_embed_diag + (1.0 - factor_decay) * (counts / tokens_all) + damping
     embed_scale = (learning_rate / divisor)[None, :]
-    gathered, grad_all, matches, embed_scale, norm_sums = lax.optimization_barrier(
-        (gathered, grad_all, matches, embed_scale, norm_sums)
-    )
+    router_matrix = (
+        factor_decay * old_router_factor
+        + weight * jnp.einsum("en,fn->ef", grad_all, grad_all, preferred_element_type=jnp.float32)
+        + damping * jnp.eye(EXPERTS, dtype=jnp.float32)
+    )
+    router_inverse = local_inverse(router_matrix)
+    router_right = jnp.einsum(
+        "en,ef->fn", grad_all, router_inverse, preferred_element_type=jnp.float32
+    ).astype(jnp.bfloat16)
+
+    part_rows = row_block // 2
+
+    def old_block(factors, step, start, size):
+        away = by_index(factors, held_by(layer ^ step))[start : start + size]
+        return away.astype(jnp.bfloat16)
+
+    early = swap(old_block(old_factors, 2, 0, part_rows), "tensor", n_tensor, 2)
+    later_factors = lax.optimization_barrier(old_factors)
+    late = old_block(later_factors, 2, part_rows, part_rows)
+    blocks = [old_block(later_factors, step, 0, row_block) for step in (0, 1, 3)]
+    other_tokens, collected, early, late, blocks, small = lax.optimization_barrier(
+        (other_tokens, collected, early, late, blocks, (router_right, matches, embed_scale, norm_sums))
+    )
+    router_right, matches, embed_scale, norm_sums = small
+    collected = jnp.concatenate(
+        [collected[:, :features_dev], other_tokens, collected[:, 2 * features_dev :]], axis=1
+    )
+    gathered = lax.all_gather(collected, "section", axis=0)
+    late = swap(late, "tensor", n_tensor, 2)
+    blocks = [
+        blocks[0],
+        swap(blocks[1], "tensor", n_tensor, 1),
+        None,
+        swap(blocks[2], "tensor", n_tensor, 3),
+    ]
 
     features, rows, low_diag, trace = lay_out(
         jnp.stack([own_place, layer, core]), gathered, weight
     )
     scale = D / (3.0 * trace)
+    early, features = lax.optimization_barrier((early, features))
+    blocks[2] = jnp.concatenate([early, late], axis=0)
 
     own_cols = [
         factor_block(place, features, blocks[step], low_diag, step, weight)
@@ -646,20 +674,27 @@
         )
         return jnp.where(layer == source, value, moved_here)
 
-    router_matrix = (
-        factor_decay * old_router_factor
-        + weight * jnp.einsum("en,fn->ef", grad_all, grad_all, preferred_element_type=jnp.float32)
-        + damping * jnp.eye(EXPERTS, dtype=jnp.float32)
-    )
-    router_inverse = local_inverse(router_matrix)
-    router_right = jnp.einsum(
-        "en,ef->fn", grad_all, router_inverse, preferred_element_type=jnp.float32
-    ).astype(jnp.bfloat16)
+    def hand_round(value, *ahead):
+        sides = lax.ppermute(
+            value, everywhere, [(spot(x, t, t), spot(x, t, t ^ 2)) for x in planes for t in layers]
+        )
+        sides, *ahead = lax.optimization_barrier((sides, *ahead))
+        near = lax.ppermute(
+            value, everywhere, [(spot(x, t, t), spot(x, t, t ^ 1)) for x in planes for t in layers]
+        )
+        far = lax.ppermute(
+            sides,
+            everywhere,
+            [(spot(x, t, t ^ 2), spot(x, t, t ^ 3)) for x in planes for t in layers],
+        )
+        return (value, near, sides, far), *ahead
 
     near_1 = send(own, 1, 0)
     near_2 = send(own, 2, 0)
     over_0 = across(own, 0)
     left_here = scatter(own, 2)
+    near_1, over_0, own = lax.optimization_barrier((near_1, over_0, own))
+    over_1 = across(near_1, 1)
     router_cols = learning_rate * jnp.einsum(
         "fn,cn->fc", router_right, own, preferred_element_type=jnp.float32
     )
@@ -667,43 +702,37 @@
     router_high = lax.reduce_precision(router_cols, 8, 7)
     codes = jnp.concatenate([router_high, router_cols - router_high], axis=0).astype(jnp.bfloat16)
     codes_tail = jnp.pad(codes[:, tokens_all:], ((0, 0), (0, 2 * tokens_all - col_block)))
-    codes = jnp.concatenate([codes[:, :tokens_all], codes_tail], axis=0)
-    near_1, over_0 = lax.optimization_barrier((near_1, over_0))
-    over_1 = across(near_1, 1)
-    left_here, near_2, codes, over_1 = lax.optimization_barrier(
-        (left_here, near_2, codes, over_1)
-    )
-    left_there = lax.ppermute(
-        jnp.concatenate([left_here, codes], axis=0),
-        everywhere,
-        [(spot(x, t, t), spot(1 - x, t, t)) for x in planes for t in layers],
-    )
+    left_here = jnp.concatenate([left_here, codes[:, :tokens_all], codes_tail], axis=0)
+    left_here, near_2, over_1 = lax.optimization_barrier((left_here, near_2, over_1))
     near_3 = send(near_2, 1, 2)
     over_2 = across(near_2, 2)
-    codes = jnp.where(shard == 1, codes, left_there[col_block:])
-    bundle = jnp.concatenate([left_here, left_there[:col_block], codes], axis=0)
-    bundle, near_3 = lax.optimization_barrier((bundle, near_3))
-    to_side = [(spot(x, t, t), spot(x, t, t ^ 2)) for x in planes for t in layers]
-    bundle = jnp.where(section == layer, bundle, lax.ppermute(bundle, everywhere, to_side))
+    left_there = lax.ppermute(
+        left_here, everywhere, [(spot(x, t, t), spot(1 - x, t, t)) for x in planes for t in layers]
+    )
+    (lefts_here,) = hand_round(left_here)
+    left_there, near_3, over_2 = lax.optimization_barrier((left_there, near_3, over_2))
     over_3 = across(near_3, 3)
-    bundle, over_2, over_3 = lax.optimization_barrier((bundle, over_2, over_3))
-    to_core = [
-        (spot(x, t, t ^ a), spot(x, t, t ^ a ^ 1)) for x in planes for t in layers for a in (0, 2)
-    ]
-    bundle = jnp.where(
-        (section ^ layer) % 2 == 0, bundle, lax.ppermute(bundle, everywhere, to_core)
-    )
-    codes = bundle[2 * col_block :]
+    lefts_there, over_3 = hand_round(left_there, over_3)
+    turn = section ^ layer
+
+    def codes_of(group):
+        parts = [part[col_block:] for part in group]
+        chosen = parts[3]
+        for index in (2, 1, 0):
+            chosen = jnp.where(turn == index, parts[index], chosen)
+        return chosen
+
+    codes = jnp.where(shard == 1, codes_of(lefts_here), codes_of(lefts_there))
     codes = jnp.concatenate(
         [codes[: 2 * EXPERTS], codes[2 * EXPERTS :, : col_block - tokens_all]], axis=1
     ).astype(jnp.float32)
     precond_router = codes[:EXPERTS] + codes[EXPERTS:]
 
     precond_attn, embed_columns = output_products(
-        jnp.stack([shard, layer]),
-        bundle,
+        jnp.stack([shard, layer, turn]),
+        embed_scale,
         matches,
-        embed_scale,
+        (lefts_here, lefts_there),
         (own, near_1, near_2, near_3),
         (over_0, over_1, over_2, over_3),
     )

time: 274 us -> 257 us (0.938)
  the two profiles are of different devices: /device:TPU:31 before, /device:TPU:0 now
where the time goes in v8:
time: 257 us; the launch traced here: 252 us
  waiting for transfers between devices  104 us (40%)
  starting transfers between devices  63 us (25%)
  Pallas kernels  31.2 us (12%)
  local copies, waits for them, and re-layouts  22.6 us (9%)
  between operations  16.1 us (6%)
  other arithmetic  14.4 us (6%)
    ppermute x18, waiting for transfers between devices, swap(): return lax.ppermute(value, axis, [(i, i ^ step) for i in range(size)])  57.6 us
    all_gather x1, waiting for transfers between devices, layer_plan(): gathered = lax.all_gather(collected, 'section', axis=0)  20.7 us
    ppermute x18, starting transfers between devices, swap(): return lax.ppermute(value, axis, [(i, i ^ step) for i in range(size)])  19.2 us
    pallas_call x3, Pallas kernels, chain_call(): pl.pallas_call(kernel, in_specs=[pl.BlockSpec(memory_space=pltpu.SMEM)] *...  15.9 us
    ppermute x3, waiting for transfers between devices, send(): return lax.ppermute(value, axes, moves)  13.7 us
    unnamed x53, local copies, waits for them, and re-layouts  13.7 us
    ppermute x4, starting transfers between devices, across(): return lax.ppermute(value, axes, moves)  11.2 us
    ppermute x2, waiting for transfers between devices, scatter(): lax.ppermute(value, everywhere, [(spot(x, source, s), spot(x, s, s)) for...  9.62 us
  transfers between devices with their start and end apart: 35, of which 16 were waited for; matrix products, arithmetic and copies ran while one was open for 7% of the time, Pallas kernels for 3%

profile of v8, /device:TPU:0, one launch (start us, length us, event | category | flops | bytes accessed | tf_op | source)
XLA Modules:
  0.0 252.5 jit_solution(17980322529650516418)
XLA Ops:
  10.0 5.1 %collective-permute-start.2 = (bf16[304,256]{1,0:T(8,128)(2,1)S(1)}, bf16[304,256]{1,0:T(8,128)(2,1)S(1)}, u32[]{:S(2)}, u32[]{:S(2)}) collective-permute-start(bf16[304,256]{1,0:T(8,128)(2,1)S(1)} %pad_maximum_fusion.6), channel_id=1, source_target_pairs={{0,12},{4,8},{8,4},{12,0},{1,13},{5,9},{9,5},{13,1},{2,14},{6,10},... | collective-permute-start | bytes 466952 | tf_op jit(solution)/shard_map/ppermute | solution.py:169
  18.4 2.3 collective-permute-start.4
  22.2 3.6 %fusion.5 = (bf16[576,576]{1,0:T(8,128)(2,1)}, bf16[576,576]{1,0:T(8,128)(2,1)}, bf16[576,576]{1,0:T(8,128)(2,1)S(1)}) fusion(f32[4,576,576]{2,1,0:T(8,128)} %param.12, s32[]{:T(128)S(6)} %select_n.168, s32[]{:T(128)S(6)} %select_n.160, s32[]{:T(128)S(6)} %select_n.156), kind=kLoop, calls=%fused_computation.16 | loop fusion | bytes 3981324 | tf_op jit(solution)/shard_map/convert_element_type | solution.py:588
  32.9 3.1 %collective-permute-done.5 = bf16[8,256]{1,0:T(8,128)(2,1)S(1)} collective-permute-done((bf16[8,256]{1,0:T(8,128)(2,1)S(1)}, bf16[8,256]{1,0:T(8,128)(2,1)S(1)}, u32[]{:S(2)}, u32[]{:S(2)}) %collective-permute-start.5) | collective-permute-done | bytes 4128 | tf_op jit(solution)/shard_map/ppermute | solution.py:169
  41.7 2.5 collective-permute-done.4
  44.2 3.5 %collective-permute-done.3 = bf16[4,144,256]{2,1,0:T(8,128)(2,1)} collective-permute-done((bf16[4,144,256]{2,1,0:T(8,128)(2,1)}, bf16[4,144,256]{2,1,0:T(8,128)(2,1)}, u32[]{:S(2)}, u32[]{:S(2)}) %collective-permute-start.3) | collective-permute-done | bytes 294944 | tf_op jit(solution)/shard_map/ppermute | solution.py:169
  53.4 20.7 %all-gather.3.cloned.1.call-done = bf16[16,304,256]{2,1,0:T(8,128)(2,1)} async-done(((bf16[4,304,256]{2,1,0:T(8,128)(2,1)}), bf16[16,304,256]{2,1,0:T(8,128)(2,1)}) %all-gather.3.cloned.1.call-update) | async-done | bytes 2490384 | tf_op jit(solution)/shard_map/all_gather | solution.py:601
  75.7 2.8 %shard_map.111 = (bf16[2,2304,256]{2,1,0:T(8,128)(2,1)S(1)}, bf16[256,2304]{1,0:T(8,128)(2,1)S(1)}, f32[4,1,576]{2,1,0:T(1,128)S(1)}, f32[1]{0:T(128)}) custom-call(s32[3]{0:T(128)S(1)} %pad_add_fusion.1.place_ref, bf16[4,4,304,256]{3,2,1,0:T(8,128)(2,1)S(1)} %bitcast.88), custom_call_target="tpu_custom_call" | custom-call | flops 37748736 | bytes 8257536 | tf_op jit(solution)/shard_map/pallas_call | solution.py:237
  82.1 15.6 %collective-permute-done.9 = bf16[288,576]{1,0:T(8,128)(2,1)} collective-permute-done((bf16[288,576]{1,0:T(8,128)(2,1)S(1)}, bf16[288,576]{1,0:T(8,128)(2,1)}, u32[]{:S(2)}, u32[]{:S(2)}) %collective-permute-start.9) | collective-permute-done | bytes 331808 | tf_op jit(solution)/shard_map/ppermute | solution.py:169
  103.8 5.2 %shard_map.116 = (f32[2,256,576]{2,1,0:T(8,128)S(1)}, bf16[256,1152]{1,0:T(8,128)(2,1)S(1)}) custom-call(s32[1]{0:T(128)} %bitcast.2.place_ref, f32[1]{0:T(128)S(6)} %div.22.scale_ref, bf16[256,2304]{1,0:T(8,128)(2,1)S(1)} %get-tuple-element.45.rows, f32[4,1,576]{2,1,0:T(1,128)S(1)} %get-tuple-element.46.diag, bf16[576,576]{1,0:T(8,128)(2,1)S(1)} %shard_map.112.refs_0_, ...), custom_call_target="tpu_custom_call" | custom-call | flops 1358954496 | bytes 5308416 | tf_op jit(solution)/shard_map/pallas_call | solution.py:379
  110.6 14.1 %collective-permute-done.15.theirs = bf16[256,1152]{1,0:T(8,128)(2,1)S(1)} collective-permute-done((bf16[256,1152]{1,0:T(8,128)(2,1)S(1)}, bf16[256,1152]{1,0:T(8,128)(2,1)S(1)}, u32[]{:S(2)}, u32[]{:S(2)}) %collective-permute-start.15) | collective-permute-done | bytes 589856 | tf_op jit(solution)/shard_map/ppermute | solution.py:169
  124.7 5.6 %shard_map.117 = (f32[2,256,576]{2,1,0:T(8,128)S(1)}, bf16[256,1152]{1,0:T(8,128)(2,1)S(1)}) custom-call(s32[1]{0:T(128)} %bitcast.2.place_ref, f32[1]{0:T(128)S(6)} %div.22.scale_ref, bf16[256,1152]{1,0:T(8,128)(2,1)S(1)} %get-tuple-element.55.mine, bf16[256,1152]{1,0:T(8,128)(2,1)S(1)} %collective-permute-done.15.theirs, ...), custom_call_target="tpu_custom_call" | custom-call | flops 1358954496 | bytes 5308416 | tf_op jit(solution)/shard_map/pallas_call | solution.py:379
  131.9 13.3 %collective-permute-done.16.theirs = bf16[256,1152]{1,0:T(8,128)(2,1)S(1)} collective-permute-done((bf16[256,1152]{1,0:T(8,128)(2,1)S(1)}, bf16[256,1152]{1,0:T(8,128)(2,1)S(1)}, u32[]{:S(2)}, u32[]{:S(2)}) %collective-permute-start.16) | collective-permute-done | bytes 589856 | tf_op jit(solution)/shard_map/ppermute | solution.py:169
  145.2 5.0 %shard_map.118 = (bf16[576,256]{1,0:T(8,128)(2,1)S(1)}, bf16[576,256]{1,0:T(8,128)(2,1)S(1)}) custom-call(s32[1]{0:T(128)} %bitcast.2.place_ref, f32[1]{0:T(128)S(6)} %div.22.scale_ref, bf16[256,1152]{1,0:T(8,128)(2,1)S(1)} %get-tuple-element.57.mine, bf16[256,1152]{1,0:T(8,128)(2,1)S(1)} %collective-permute-done.16.theirs, ...), custom_call_target="tpu_custom_call" | custom-call | flops 1358954496 | bytes 5308416 | tf_op jit(solution)/shard_map/pallas_call | solution.py:379
  155.7 3.9 %collective-permute-start.20 = (bf16[576,512]{1,0:T(8,128)(2,1)S(1)}, bf16[576,512]{1,0:T(8,128)(2,1)S(1)}, u32[]{:S(2)}, u32[]{:S(2)}) collective-permute-start(bf16[576,512]{1,0:T(8,128)(2,1)S(1)} %maximum_select_fusion.refs_8_), channel_id=1, source_target_pairs={{0,16},{4,20},{12,28},{16,0},{28,12},{1,17},{5,21},{13,29},{17,1},... | collective-permute-start | bytes 1769480 | tf_op jit(solution)/shard_map/ppermute | solution.py:662
  160.9 6.3 %collective-permute-start.22 = (bf16[576,512]{1,0:T(8,128)(2,1)S(1)}, bf16[576,512]{1,0:T(8,128)(2,1)S(1)}, u32[]{:S(2)}, u32[]{:S(2)}) collective-permute-start(bf16[576,512]{1,0:T(8,128)(2,1)S(1)} %maximum_select_fusion.refs_8_), channel_id=1, source_target_pairs={{0,8},{4,12},{12,4},{16,24},{28,20},{1,9},{5,13},{13,5},{17,25},{2... | collective-permute-start | bytes 1769480 | tf_op jit(solution)/shard_map/ppermute | solution.py:653
  167.2 6.5 %collective-permute-done.19.refs_9_ = bf16[576,512]{1,0:T(8,128)(2,1)} collective-permute-done((bf16[576,512]{1,0:T(8,128)(2,1)S(1)}, bf16[576,512]{1,0:T(8,128)(2,1)}, u32[]{:S(2)}, u32[]{:S(2)}) %collective-permute-start.19) | collective-permute-done | bytes 589856 | tf_op jit(solution)/shard_map/ppermute | solution.py:653
  175.4 3.2 %collective-permute-start.23 = (bf16[576,512]{1,0:T(8,128)(2,1)}, bf16[576,512]{1,0:T(8,128)(2,1)S(1)}, u32[]{:S(2)}, u32[]{:S(2)}) collective-permute-start(bf16[576,512]{1,0:T(8,128)(2,1)} %collective-permute-done.19.refs_9_), channel_id=1, source_target_pairs={{0,16},{4,20},{8,24},{20,4},{24,8},{1,17},{5,21},{9,25},{21,5},{25... | collective-permute-start | bytes 1769480 | tf_op jit(solution)/shard_map/ppermute | solution.py:662
  178.6 9.6 %collective-permute-done.18 = bf16[576,512]{1,0:T(8,128)(2,1)} collective-permute-done((bf16[576,512]{1,0:T(8,128)(2,1)S(1)}, bf16[576,512]{1,0:T(8,128)(2,1)}, u32[]{:S(2)}, u32[]{:S(2)}) %collective-permute-start.18) | collective-permute-done | bytes 589856 | tf_op jit(solution)/shard_map/ppermute | solution.py:670
  191.2 4.3 %collective-permute-start.27 = (bf16[608,512]{1,0:T(8,128)(2,1)S(1)}, bf16[608,512]{1,0:T(8,128)(2,1)}, u32[]{:S(2)}, u32[]{:S(2)}) collective-permute-start(bf16[608,512]{1,0:T(8,128)(2,1)S(1)} %pad_maximum_fusion.3.refs_0_), channel_id=1, source_target_pairs={{0,16},{5,21},{10,26},{15,31},{16,0},{21,5},{26,10},{31,15}} | collective-permute-start | bytes 1867784 | tf_op jit(solution)/shard_map/ppermute | solution.py:709
  200.5 7.2 %collective-permute-done.28.refs_11_ = bf16[576,512]{1,0:T(8,128)(2,1)S(1)} collective-permute-done((bf16[576,512]{1,0:T(8,128)(2,1)S(1)}, bf16[576,512]{1,0:T(8,128)(2,1)S(1)}, u32[]{:S(2)}, u32[]{:S(2)}) %collective-permute-start.28) | collective-permute-done | bytes 589856 | tf_op jit(solution)/shard_map/ppermute | solution.py:653
  208.5 6.8 %collective-permute-start.31 = (bf16[608,512]{1,0:T(8,128)(2,1)}, bf16[608,512]{1,0:T(8,128)(2,1)}, u32[]{:S(2)}, u32[]{:S(2)}) collective-permute-start(bf16[608,512]{1,0:T(8,128)(2,1)} %collective-permute-done.27.refs_4_), channel_id=1, source_target_pairs={{0,2},{5,7},{10,8},{15,13},{16,18},{21,23},{26,24},{31,29}} | collective-permute-start | bytes 1867784 | tf_op jit(solution)/shard_map/ppermute | solution.py:678
  215.3 3.4 %collective-permute-start.32 = (bf16[576,512]{1,0:T(8,128)(2,1)S(1)}, bf16[576,512]{1,0:T(8,128)(2,1)S(1)}, u32[]{:S(2)}, u32[]{:S(2)}) collective-permute-start(bf16[576,512]{1,0:T(8,128)(2,1)S(1)} %collective-permute-done.28.refs_11_), channel_id=1, source_target_pairs={{0,16},{8,24},{12,28},{16,0},{28,12},{1,17},{9,25},{13,29},{17,1},... | collective-permute-start | bytes 1769480 | tf_op jit(solution)/shard_map/ppermute | solution.py:662
  238.0 7.6 %shard_map.119 = (f32[4,576,576]{2,1,0:T(8,128)}, f32[576,2048]{1,0:T(8,128)}) custom-call(s32[3]{0:T(128)S(1)} %pad_add_fusion.where_ref, f32[1,2048]{1,0:T(1,128)S(1)} %bitcast.89, bf16[512,2048]{1,0:T(8,128)(2,1)S(1)} %compare_convert_fusion.matches, bf16[608,512]{1,0:T(8,128)(2,1)S(1)} %pad_maximum_fusion.3.refs_0_, ...), custom_call_target="tpu_custom_call" | custom-call | flops 2566914048 | bytes 14155776 | tf_op jit(solution)/shard_map/pallas_call | solution.py:472
  (161 shorter events, 75.1 us)
Async XLA Ops:
  7.2 66.9 %all-gather.3.cloned.1.call-start = ((), (), s32[]{:S(2)}) async-start(), calls=%async_computation | async-start | bytes 3112960 | tf_op jit(solution)/shard_map/all_gather | solution.py:601
  10.0 28.0 %collective-permute-start.2 = (bf16[304,256]{1,0:T(8,128)(2,1)S(1)}, bf16[304,256]{1,0:T(8,128)(2,1)S(1)}, u32[]{:S(2)}, u32[]{:S(2)}) collective-permute-start(bf16[304,256]{1,0:T(8,128)(2,1)S(1)} %pad_maximum_fusion.6), channel_id=1, source_target_pairs={{0,12},{4,8},{8,4},{12,0},{1,13},{5,9},{9,5},{13,1},{2,14},{6,10},... | collective-permute-start | bytes 466952 | tf_op jit(solution)/shard_map/ppermute | solution.py:169
  15.1 22.9 %collective-permute-start.1 = (bf16[304,256]{1,0:T(8,128)(2,1)S(1)}, bf16[304,256]{1,0:T(8,128)(2,1)S(1)}, u32[]{:S(2)}, u32[]{:S(2)}) collective-permute-start(bf16[304,256]{1,0:T(8,128)(2,1)S(1)} %pad_maximum_fusion.5), channel_id=1, source_target_pairs={{0,8},{4,12},{8,0},{12,4},{1,9},{5,13},{9,1},{13,5},{2,10},{6,14},... | collective-permute-start | bytes 466952 | tf_op jit(solution)/shard_map/ppermute | solution.py:169
  15.9 22.2 %collective-permute-start = (bf16[304,256]{1,0:T(8,128)(2,1)}, bf16[304,256]{1,0:T(8,128)(2,1)}, u32[]{:S(2)}, u32[]{:S(2)}) collective-permute-start(bf16[304,256]{1,0:T(8,128)(2,1)} %pad_maximum_fusion.4), channel_id=1, source_target_pairs={{0,4},{4,0},{8,12},{12,8},{1,5},{5,1},{9,13},{13,9},{2,6},{6,2},{1... | collective-permute-start | bytes 466952 | tf_op jit(solution)/shard_map/ppermute | solution.py:169
  18.4 25.8 %collective-permute-start.4 = (bf16[288,576]{1,0:T(8,128)(2,1)}, bf16[288,576]{1,0:T(8,128)(2,1)}, u32[]{:S(2)}, u32[]{:S(2)}) collective-permute-start(bf16[288,576]{1,0:T(8,128)(2,1)} %fusion.6), channel_id=1, source_target_pairs={{0,8},{4,12},{8,0},{12,4},{1,9},{5,13},{9,1},{13,5},{2,10},{6,14},... | collective-permute-start | bytes 995336 | tf_op jit(solution)/shard_map/ppermute | solution.py:169
  49.7 30.5 %collective-permute-start.8 = (bf16[576,576]{1,0:T(8,128)(2,1)}, bf16[576,576]{1,0:T(8,128)(2,1)}, u32[]{:S(2)}, u32[]{:S(2)}) collective-permute-start(bf16[576,576]{1,0:T(8,128)(2,1)} %get-tuple-element.51), channel_id=1, source_target_pairs={{0,4},{4,0},{8,12},{12,8},{1,5},{5,1},{9,13},{13,9},{2,6},{6,2},{1... | collective-permute-start | bytes 1990664 | tf_op jit(solution)/shard_map/ppermute | solution.py:169
  51.8 47.8 %collective-permute-start.10 = (bf16[576,576]{1,0:T(8,128)(2,1)}, bf16[576,576]{1,0:T(8,128)(2,1)}, u32[]{:S(2)}, u32[]{:S(2)}) collective-permute-start(bf16[576,576]{1,0:T(8,128)(2,1)} %get-tuple-element.54), channel_id=1, source_target_pairs={{0,12},{4,8},{8,4},{12,0},{1,13},{5,9},{9,5},{13,1},{2,14},{6,10},... | collective-permute-start | bytes 1990664 | tf_op jit(solution)/shard_map/ppermute | solution.py:169
  52.0 45.6 %collective-permute-start.9 = (bf16[288,576]{1,0:T(8,128)(2,1)S(1)}, bf16[288,576]{1,0:T(8,128)(2,1)}, u32[]{:S(2)}, u32[]{:S(2)}) collective-permute-start(bf16[288,576]{1,0:T(8,128)(2,1)S(1)} %copy-done.14), channel_id=1, source_target_pairs={{0,8},{4,12},{8,0},{12,4},{1,9},{5,13},{9,1},{13,5},{2,10},{6,14},... | collective-permute-start | bytes 995336 | tf_op jit(solution)/shard_map/ppermute | solution.py:169
  79.2 23.3 %collective-permute-start.11 = (bf16[576,576]{1,0:T(8,128)(2,1)S(1)}, bf16[576,576]{1,0:T(8,128)(2,1)S(1)}, u32[]{:S(2)}, u32[]{:S(2)}) collective-permute-start(bf16[576,576]{1,0:T(8,128)(2,1)S(1)} %shard_map.112.refs_0_), channel_id=1, source_target_pairs={{0,1},{1,0},{2,3},{3,2},{4,5},{5,4},{6,7},{7,6},{8,9},{9,8},{10,11... | collective-permute-start | bytes 1990664 | tf_op jit(solution)/shard_map/ppermute | solution.py:169
  82.0 20.6 %collective-permute-start.12 = (bf16[576,576]{1,0:T(8,128)(2,1)S(1)}, bf16[576,576]{1,0:T(8,128)(2,1)S(1)}, u32[]{:S(2)}, u32[]{:S(2)}) collective-permute-start(bf16[576,576]{1,0:T(8,128)(2,1)S(1)} %shard_map.113.refs_1_), channel_id=1, source_target_pairs={{0,1},{1,0},{2,3},{3,2},{4,5},{5,4},{6,7},{7,6},{8,9},{9,8},{10,11... | collective-permute-start | bytes 1990664 | tf_op jit(solution)/shard_map/ppermute | solution.py:169
  109.0 15.7 %collective-permute-start.15 = (bf16[256,1152]{1,0:T(8,128)(2,1)S(1)}, bf16[256,1152]{1,0:T(8,128)(2,1)S(1)}, u32[]{:S(2)}, u32[]{:S(2)}) collective-permute-start(bf16[256,1152]{1,0:T(8,128)(2,1)S(1)} %get-tuple-element.55.mine), channel_id=1, source_target_pairs={{0,2},{1,3},{2,0},{3,1},{4,6},{5,7},{6,4},{7,5},{8,10},{9,11},{10,... | collective-permute-start | bytes 1769480 | tf_op jit(solution)/shard_map/ppermute | solution.py:169
  130.3 14.9 %collective-permute-start.16 = (bf16[256,1152]{1,0:T(8,128)(2,1)S(1)}, bf16[256,1152]{1,0:T(8,128)(2,1)S(1)}, u32[]{:S(2)}, u32[]{:S(2)}) collective-permute-start(bf16[256,1152]{1,0:T(8,128)(2,1)S(1)} %get-tuple-element.57.mine), channel_id=1, source_target_pairs={{0,2},{1,3},{2,0},{3,1},{4,6},{5,7},{6,4},{7,5},{8,10},{9,11},{10,... | collective-permute-start | bytes 1769480 | tf_op jit(solution)/shard_map/ppermute | solution.py:169
  153.8 19.9 %collective-permute-start.19 = (bf16[576,512]{1,0:T(8,128)(2,1)S(1)}, bf16[576,512]{1,0:T(8,128)(2,1)}, u32[]{:S(2)}, u32[]{:S(2)}) collective-permute-start(bf16[576,512]{1,0:T(8,128)(2,1)S(1)} %maximum_select_fusion.refs_8_), channel_id=1, source_target_pairs={{0,4},{4,0},{12,8},{16,20},{28,24},{1,5},{5,1},{13,9},{17,21},{29,... | collective-permute-start | bytes 1769480 | tf_op jit(solution)/shard_map/ppermute | solution.py:653
  155.7 18.0 %collective-permute-start.20 = (bf16[576,512]{1,0:T(8,128)(2,1)S(1)}, bf16[576,512]{1,0:T(8,128)(2,1)S(1)}, u32[]{:S(2)}, u32[]{:S(2)}) collective-permute-start(bf16[576,512]{1,0:T(8,128)(2,1)S(1)} %maximum_select_fusion.refs_8_), channel_id=1, source_target_pairs={{0,16},{4,20},{12,28},{16,0},{28,12},{1,17},{5,21},{13,29},{17,1},... | collective-permute-start | bytes 1769480 | tf_op jit(solution)/shard_map/ppermute | solution.py:662
  159.6 28.6 %collective-permute-start.18 = (bf16[576,512]{1,0:T(8,128)(2,1)S(1)}, bf16[576,512]{1,0:T(8,128)(2,1)}, u32[]{:S(2)}, u32[]{:S(2)}) collective-permute-start(bf16[576,512]{1,0:T(8,128)(2,1)S(1)} %maximum_select_fusion.refs_8_), channel_id=1, source_target_pairs={{8,0},{9,5},{11,15},{24,16},{25,21},{27,31}} | collective-permute-start | bytes 1769480 | tf_op jit(solution)/shard_map/ppermute | solution.py:670
  160.9 28.6 %collective-permute-start.22 = (bf16[576,512]{1,0:T(8,128)(2,1)S(1)}, bf16[576,512]{1,0:T(8,128)(2,1)S(1)}, u32[]{:S(2)}, u32[]{:S(2)}) collective-permute-start(bf16[576,512]{1,0:T(8,128)(2,1)S(1)} %maximum_select_fusion.refs_8_), channel_id=1, source_target_pairs={{0,8},{4,12},{12,4},{16,24},{28,20},{1,9},{5,13},{13,5},{17,25},{2... | collective-permute-start | bytes 1769480 | tf_op jit(solution)/shard_map/ppermute | solution.py:653
  173.9 15.4 %collective-permute-start.21 = (f32[8,576]{1,0:T(8,128)S(1)}, f32[8,576]{1,0:T(8,128)S(1)}, u32[]{:S(2)}, u32[]{:S(2)}) collective-permute-start(f32[8,576]{1,0:T(8,128)S(1)} %convolution_multiply_fusion), channel_id=1, source_target_pairs={{4,0},{6,10},{7,15},{20,16},{22,26},{23,31}} | collective-permute-start | bytes 55304 | tf_op jit(solution)/shard_map/ppermute | solution.py:670
  175.4 15.0 %collective-permute-start.23 = (bf16[576,512]{1,0:T(8,128)(2,1)}, bf16[576,512]{1,0:T(8,128)(2,1)S(1)}, u32[]{:S(2)}, u32[]{:S(2)}) collective-permute-start(bf16[576,512]{1,0:T(8,128)(2,1)} %collective-permute-done.19.refs_9_), channel_id=1, source_target_pairs={{0,16},{4,20},{8,24},{20,4},{24,8},{1,17},{5,21},{9,25},{21,5},{25... | collective-permute-start | bytes 1769480 | tf_op jit(solution)/shard_map/ppermute | solution.py:662
  191.2 17.3 %collective-permute-start.27 = (bf16[608,512]{1,0:T(8,128)(2,1)S(1)}, bf16[608,512]{1,0:T(8,128)(2,1)}, u32[]{:S(2)}, u32[]{:S(2)}) collective-permute-start(bf16[608,512]{1,0:T(8,128)(2,1)S(1)} %pad_maximum_fusion.3.refs_0_), channel_id=1, source_target_pairs={{0,16},{5,21},{10,26},{15,31},{16,0},{21,5},{26,10},{31,15}} | collective-permute-start | bytes 1867784 | tf_op jit(solution)/shard_map/ppermute | solution.py:709
  195.5 12.2 %collective-permute-start.28 = (bf16[576,512]{1,0:T(8,128)(2,1)S(1)}, bf16[576,512]{1,0:T(8,128)(2,1)S(1)}, u32[]{:S(2)}, u32[]{:S(2)}) collective-permute-start(bf16[576,512]{1,0:T(8,128)(2,1)S(1)} %collective-permute-done.22.refs_10_), channel_id=1, source_target_pairs={{4,0},{8,12},{12,8},{20,16},{24,28},{5,1},{9,13},{13,9},{21,17},{2... | collective-permute-start | bytes 1769480 | tf_op jit(solution)/shard_map/ppermute | solution.py:653
  196.8 10.9 %collective-permute-start.29 = (bf16[576,512]{1,0:T(8,128)(2,1)S(1)}, bf16[576,512]{1,0:T(8,128)(2,1)S(1)}, u32[]{:S(2)}, u32[]{:S(2)}) collective-permute-start(bf16[576,512]{1,0:T(8,128)(2,1)S(1)} %collective-permute-done.22.refs_10_), channel_id=1, source_target_pairs={{4,20},{8,24},{12,28},{20,4},{24,8},{5,21},{9,25},{13,29},{21,5},{... | collective-permute-start | bytes 1769480 | tf_op jit(solution)/shard_map/ppermute | solution.py:662
  198.3 25.4 %collective-permute-start.25 = (bf16[608,512]{1,0:T(8,128)(2,1)S(1)}, bf16[608,512]{1,0:T(8,128)(2,1)}, u32[]{:S(2)}, u32[]{:S(2)}) collective-permute-start(bf16[608,512]{1,0:T(8,128)(2,1)S(1)} %pad_maximum_fusion.3.refs_0_), channel_id=1, source_target_pairs={{0,2},{5,7},{10,8},{15,13},{16,18},{21,23},{26,24},{31,29}} | collective-permute-start | bytes 1867784 | tf_op jit(solution)/shard_map/ppermute | solution.py:678
  208.5 19.3 %collective-permute-start.31 = (bf16[608,512]{1,0:T(8,128)(2,1)}, bf16[608,512]{1,0:T(8,128)(2,1)}, u32[]{:S(2)}, u32[]{:S(2)}) collective-permute-start(bf16[608,512]{1,0:T(8,128)(2,1)} %collective-permute-done.27.refs_4_), channel_id=1, source_target_pairs={{0,2},{5,7},{10,8},{15,13},{16,18},{21,23},{26,24},{31,29}} | collective-permute-start | bytes 1867784 | tf_op jit(solution)/shard_map/ppermute | solution.py:678
  215.3 11.8 %collective-permute-start.32 = (bf16[576,512]{1,0:T(8,128)(2,1)S(1)}, bf16[576,512]{1,0:T(8,128)(2,1)S(1)}, u32[]{:S(2)}, u32[]{:S(2)}) collective-permute-start(bf16[576,512]{1,0:T(8,128)(2,1)S(1)} %collective-permute-done.28.refs_11_), channel_id=1, source_target_pairs={{0,16},{8,24},{12,28},{16,0},{28,12},{1,17},{9,25},{13,29},{17,1},... | collective-permute-start | bytes 1769480 | tf_op jit(solution)/shard_map/ppermute | solution.py:662
  (35 other events, 181.2 us)
Sparse Core Ops, SparseCore 0:
  49.8 24.1 all-gather.2

commit v9 on v8

--- a/solution.py
+++ b/solution.py
@@ -396,51 +396,88 @@
     )(*scalars, *arrays, *blocks)
 
 
-def output_kernel(where_ref, scale, matches, *refs):
-    lefts, mine, others = (refs[:4], refs[4:8]), refs[8:12], refs[12:16]
-    attn, embed = refs[16:18]
-    left_held, held, found, attn_made, embed_made, sems, out_sems = refs[18:]
-    shard, layer, turn = where_ref[0], where_ref[1], where_ref[2]
-    first = shard == 0
-    rows, tokens_all = held.shape[1:]
-
-    found_copy = pltpu.make_async_copy(matches, found, sems.at[7])
-    for slot in range(2):
+def left_kernel(take_ref, own, moved, codes, out):
+    rows, width = own.shape
+    experts, cols = codes.shape
+    out[:rows] = jnp.where(take_ref[0] == 1, own[...], moved[...])
+    high = codes[...].astype(jnp.bfloat16)
+    low = (codes[...] - high.astype(jnp.float32)).astype(jnp.bfloat16)
+    both = jnp.concatenate([high, low], axis=0)
+    out[rows : rows + 2 * experts] = both[:, :width]
+    rest = jnp.zeros((2 * experts, 2 * width - cols), jnp.bfloat16)
+    out[rows + 2 * experts :] = jnp.concatenate([both[:, width:], rest], axis=1)
+
+
+def left_message(take, own, moved, codes):
+    rows, width = own.shape
+    vmem = pl.BlockSpec(memory_space=pltpu.VMEM)
+    return pl.pallas_call(
+        left_kernel,
+        in_specs=[pl.BlockSpec(memory_space=pltpu.SMEM), vmem, vmem, vmem],
+        out_specs=vmem,
+        out_shape=jax.ShapeDtypeStruct((rows + 4 * codes.shape[0], width), own.dtype),
+        compiler_params=params(),
+        cost_estimate=pl.CostEstimate(
+            flops=60 * rows * rows * rows * 4, bytes_accessed=8 * rows * width, transcendentals=0
+        ),
+    )(take.astype(jnp.int32).reshape(1), own, moved, codes)
+
+
+def output_kernel(where_ref, scale, matches, *refs, parts):
+    lefts, refs = (refs[:4], refs[4:8]), refs[8:]
+    mine, others, refs = refs[:parts], refs[parts : 2 * parts], refs[2 * parts :]
+    attn, embed, left_held, held, found, attn_made, embed_made, sems, out_sems = refs
+    shard, turn = where_ref[0], where_ref[1]
+    rows = held.shape[1]
+
+    def fetch_left(slot):
         for group in range(2):
             for place in range(4):
 
-                @pl.when((turn == place) & (((shard ^ slot) == group)))
+                @pl.when((turn == place) & ((shard ^ slot) == group))
                 def _():
                     source = lefts[group][place].at[pl.ds(0, rows)]
                     pltpu.make_async_copy(source, left_held.at[slot], sems.at[5 + slot]).start()
 
-        if slot == 0:
-            for index, source in enumerate((0, 1, 3, 0, 3)):
-                from_mine = first if index < 3 else jnp.logical_not(first)
-                for place in range(4):
-                    for group, wanted in ((mine, from_mine), (others, jnp.logical_not(from_mine))):
-
-                        @pl.when(wanted & ((layer ^ source) == place))
-                        def _():
-                            pltpu.make_async_copy(
-                                group[place], held.at[index], sems.at[index]
-                            ).start()
-
-            found_copy.start()
+    def pieces(slot, group, layer):
+        copies, start = [], 0
+        for part in group:
+            size = part.shape[1]
+            target = held.at[slot, pl.ds(start, size)]
+            copies.append(pltpu.make_async_copy(part.at[layer], target, sems.at[slot]))
+            start += size
+        return copies
+
+    layers = (0, 1, 2, 0, 2)
+    found_copy = pltpu.make_async_copy(matches, found, sems.at[7])
+    fetch_left(0)
+    for slot, layer in enumerate(layers):
+        for owner, group in enumerate((mine, others)):
+
+            @pl.when((shard ^ owner) == (0 if slot < 3 else 1))
+            def _():
+                for copy in pieces(slot, group, layer):
+                    copy.start()
+
+    fetch_left(1)
+    found_copy.start()
 
     def arrived(slot):
-        target = held.at[slot] if slot < 5 else left_held.at[slot - 5]
-        pltpu.make_async_copy(mine[0], target, sems.at[slot]).wait()
+        pltpu.make_async_copy(held.at[slot], held.at[slot], sems.at[slot]).wait()
+        return held[slot]
+
+    def left_arrived(slot):
+        target = left_held.at[slot]
+        pltpu.make_async_copy(target, target, sems.at[5 + slot]).wait()
 
     results = []
-    arrived(5)
+    left_arrived(0)
     for slot in range(4):
         if slot == 3:
-            arrived(6)
-        arrived(slot)
+            left_arrived(1)
         attn_made[slot] = learning_rate * lax.dot_general(
             left_held[slot // 3],
-            held[slot],
+            arrived(slot),
             (((1,), (1,)), ((), ())),
             preferred_element_type=jnp.float32,
         )
@@ -448,12 +485,12 @@
             pltpu.make_async_copy(attn_made.at[slot], attn.at[slot], out_sems.at[slot])
         )
         results[-1].start()
-    arrived(4)
+    right = arrived(4)
     found_copy.wait()
     part = found.shape[1] // 4
     for index in range(4):
         cols = pl.ds(index * part, part)
-        product = jnp.dot(held[4], found[:, cols], preferred_element_type=jnp.float32)
+        product = jnp.dot(right, found[:, cols], preferred_element_type=jnp.float32)
         embed_made[:, cols] = product * scale[:, cols]
         results.append(
             pltpu.make_async_copy(
@@ -466,16 +503,17 @@
 
 
 def output_products(where, scale, matches, lefts, mine, others):
-    cols, tokens_all = mine[0].shape
+    parts = len(mine)
+    cols, tokens_all = sum(part.shape[1] for part in mine), mine[0].shape[2]
     vocab_block = scale.shape[1]
     anywhere = pl.BlockSpec(memory_space=pl.ANY)
     return pl.pallas_call(
-        output_kernel,
+        functools.partial(output_kernel, parts=parts),
         in_specs=[
             pl.BlockSpec(memory_space=pltpu.SMEM),
             pl.BlockSpec(memory_space=pltpu.VMEM),
         ]
-        + [anywhere] * 17,
+        + [anywhere] * (9 + 2 * parts),
         out_specs=(anywhere, anywhere),
         out_shape=(
             jax.ShapeDtypeStruct((4, cols, cols), jnp.float32),
@@ -490,7 +528,7 @@
             pltpu.SemaphoreType.DMA((8,)),
             pltpu.SemaphoreType.DMA((8,)),
         ],
-        compiler_params=params(),
+        compiler_params=pltpu.CompilerParams(vmem_limit_bytes=60 * 1024 * 1024),
         cost_estimate=pl.CostEstimate(
             flops=2 * cols * tokens_all * (4 * cols + vocab_block),
             bytes_accessed=4 * cols * (4 * cols + vocab_block) + 14 * cols * tokens_all,
@@ -529,7 +567,7 @@
         return lax.dynamic_index_in_dim(array, index, axis, False)
 
     def held_by(layer_index):
-        return jnp.where(layer_index == 3, 3, lax.rem(layer_index + 1, 3))
+        return lax.rem(layer_index + 1, owned)
 
     by_feature = jnp.swapaxes(activations, 1, 2)
     diagonals = local_diagonals(old_factors) * (layer == section).astype(jnp.float32)
@@ -581,29 +619,24 @@
         "en,ef->fn", grad_all, router_inverse, preferred_element_type=jnp.float32
     ).astype(jnp.bfloat16)
 
-    part_rows = row_block // 2
-
-    def old_block(factors, step, start, size):
-        away = by_index(factors, held_by(layer ^ step))[start : start + size]
-        return away.astype(jnp.bfloat16)
-
-    early = swap(old_block(old_factors, 2, 0, part_rows), "tensor", n_tensor, 2)
+    def old_block(factors, step):
+        return by_index(factors, held_by(layer ^ step)).astype(jnp.bfloat16)
+
+    early = swap(old_block(old_factors, 2), "tensor", n_tensor, 2)
     later_factors = lax.optimization_barrier(old_factors)
-    late = old_block(later_factors, 2, part_rows, part_rows)
-    blocks = [old_block(later_factors, step, 0, row_block) for step in (0, 1, 3)]
-    other_tokens, collected, early, late, blocks, small = lax.optimization_barrier(
-        (other_tokens, collected, early, late, blocks, (router_right, matches, embed_scale, norm_sums))
+    blocks = [old_block(later_factors, step) for step in (0, 1, 3)]
+    other_tokens, collected, early, blocks, small = lax.optimization_barrier(
+        (other_tokens, collected, early, blocks, (router_right, matches, embed_scale, norm_sums))
     )
     router_right, matches, embed_scale, norm_sums = small
     collected = jnp.concatenate(
         [collected[:, :features_dev], other_tokens, collected[:, 2 * features_dev :]], axis=1
     )
     gathered = lax.all_gather(collected, "section", axis=0)
-    late = swap(late, "tensor", n_tensor, 2)
     blocks = [
         blocks[0],
         swap(blocks[1], "tensor", n_tensor, 1),
-        None,
+        early,
         swap(blocks[2], "tensor", n_tensor, 3),
     ]
 
@@ -611,9 +644,6 @@
         jnp.stack([own_place, layer, core]), gathered, weight
     )
     scale = D / (3.0 * trace)
-    early, features = lax.optimization_barrier((early, features))
-    blocks[2] = jnp.concatenate([early, late], axis=0)
-
     own_cols = [
         factor_block(place, features, blocks[step], low_diag, step, weight)
         for step in range(n_tensor)
@@ -639,46 +669,22 @@
 
     planes = range(n_shard)
     layers = range(n_tensor)
-
-    def useful(x, z):
-        return z != 2 and (x, z) != (1, 1)
-
-    def send(value, step, held):
-        moves = [
-            (x * n_tensor + z, x * n_tensor + (z ^ step))
-            for x in planes
-            for z in layers
-            if useful(x, z ^ held)
-        ]
-        return lax.ppermute(value, axes, moves)
-
-    def across(value, held):
-        moves = [
-            (x * n_tensor + z, (1 - x) * n_tensor + z)
-            for x in planes
-            for z in layers
-            if useful(x, z ^ held)
-        ]
-        return lax.ppermute(value, axes, moves)
-
     everywhere = ("shard", "tensor", "section")
 
     def spot(x, z, s):
         return (x * n_tensor + z) * n_section + s
 
     def scatter(value, source):
-        moved_here = lax.ppermute(
+        return lax.ppermute(
             value,
             everywhere,
             [(spot(x, source, s), spot(x, s, s)) for x in planes for s in layers if s != source],
         )
-        return jnp.where(layer == source, value, moved_here)
-
-    def hand_round(value, *ahead):
+
+    def hand_round(value):
         sides = lax.ppermute(
             value, everywhere, [(spot(x, t, t), spot(x, t, t ^ 2)) for x in planes for t in layers]
         )
-        sides, *ahead = lax.optimization_barrier((sides, *ahead))
         near = lax.ppermute(
             value, everywhere, [(spot(x, t, t), spot(x, t, t ^ 1)) for x in planes for t in layers]
         )
@@ -687,39 +693,39 @@
             everywhere,
             [(spot(x, t, t ^ 2), spot(x, t, t ^ 3)) for x in planes for t in layers],
         )
-        return (value, near, sides, far), *ahead
-
-    near_1 = send(own, 1, 0)
-    near_2 = send(own, 2, 0)
-    over_0 = across(own, 0)
-    left_here = scatter(own, 2)
-    near_1, over_0, own = lax.optimization_barrier((near_1, over_0, own))
-    over_1 = across(near_1, 1)
+        return (value, near, sides, far)
+
+    cut = col_block // 3 * 2
+    mine = [
+        lax.all_gather(own[start:stop], "tensor", axis=0)
+        for start, stop in ((0, cut), (cut, col_block))
+    ]
     router_cols = learning_rate * jnp.einsum(
         "fn,cn->fc", router_right, own, preferred_element_type=jnp.float32
     )
-    router_cols = scatter(router_cols, 1)
-    router_high = lax.reduce_precision(router_cols, 8, 7)
-    codes = jnp.concatenate([router_high, router_cols - router_high], axis=0).astype(jnp.bfloat16)
-    codes_tail = jnp.pad(codes[:, tokens_all:], ((0, 0), (0, 2 * tokens_all - col_block)))
-    left_here = jnp.concatenate([left_here, codes[:, :tokens_all], codes_tail], axis=0)
-    left_here, near_2, over_1 = lax.optimization_barrier((left_here, near_2, over_1))
-    near_3 = send(near_2, 1, 2)
-    over_2 = across(near_2, 2)
+    router_cols = jnp.where(layer == 1, router_cols, scatter(router_cols, 1))
+    left_layer = n_tensor - 1
+    left_here = left_message(layer == left_layer, own, scatter(own, left_layer), router_cols)
     left_there = lax.ppermute(
         left_here, everywhere, [(spot(x, t, t), spot(1 - x, t, t)) for x in planes for t in layers]
     )
-    (lefts_here,) = hand_round(left_here)
-    left_there, near_3, over_2 = lax.optimization_barrier((left_there, near_3, over_2))
-    over_3 = across(near_3, 3)
-    lefts_there, over_3 = hand_round(left_there, over_3)
+    lefts_here = hand_round(left_here)
+
+    def hand_over(piece):
+        return swap(piece[: n_tensor - 1], "shard", n_shard, 1)
+
+    left_there, mine[0] = lax.optimization_barrier((left_there, mine[0]))
+    lefts_there = hand_round(left_there)
+    others = [hand_over(mine[0])]
+    mine[1], others[0] = lax.optimization_barrier((mine[1], others[0]))
+    others.append(hand_over(mine[1]))
     turn = section ^ layer
 
     def codes_of(group):
-        parts = [part[col_block:] for part in group]
-        chosen = parts[3]
+        found = [part[col_block:] for part in group]
+        chosen = found[3]
         for index in (2, 1, 0):
-            chosen = jnp.where(turn == index, parts[index], chosen)
+            chosen = jnp.where(turn == index, found[index], chosen)
         return chosen
 
     codes = jnp.where(shard == 1, codes_of(lefts_here), codes_of(lefts_there))
@@ -729,12 +735,7 @@
     precond_router = codes[:EXPERTS] + codes[EXPERTS:]
 
     precond_attn, embed_columns = output_products(
-        jnp.stack([shard, layer, turn]),
-        embed_scale,
-        matches,
-        (lefts_here, lefts_there),
-        (own, near_1, near_2, near_3),
-        (over_0, over_1, over_2, over_3),
+        jnp.stack([shard, turn]), embed_scale, matches, (lefts_here, lefts_there), mine, others
     )
     precond_embed = embed_columns.T
 

time: 257 us -> 259 us (level); the launches traced: 252 us -> 258 us
  waiting for transfers between devices: 104 us -> 134 us
  starting transfers between devices: 63 us -> 36.6 us
  blocking collectives: 0 us -> 19.7 us
  local copies, waits for them, and re-layouts: 22.6 us -> 11.4 us
  other arithmetic: 14.4 us -> 9.93 us
    ppermute x7 -> x0, starting transfers between devices: 20.7 us -> none  [the longest x4 11.2 us: across(): return lax.ppermute(value, axes, moves)]
    all_gather x0 -> x1, blocking collectives: none -> 19.7 us  [layer_plan(): lax.all_gather(own[start:stop], 'tensor', axis=0)]
    ppermute x7 -> x0, waiting for transfers between devices: 16.5 us -> none  [the longest x3 13.7 us: send(): return lax.ppermute(value, axes, moves)]
    all_gather x0 -> x1, waiting for transfers between devices: none -> 11.4 us  [layer_plan(): lax.all_gather(own[start:stop], 'tensor', axis=0)]
    unnamed x53 -> x37, local copies, waits for them, and re-layouts: 13.7 us -> 2.34 us
    ppermute x18 -> x19, waiting for transfers between devices: 57.6 us -> 66.3 us  [swap(): return lax.ppermute(value, axis, [(i, i ^ step) for i in range(size)])]
    ppermute x1, waiting for transfers between devices: 0.01 us -> 8.67 us  [layer_plan(): lax.ppermute(left_here, everywhere, [(spot(x, t, t), spot(1 - x, t, t)) f...]
    ppermute x2, waiting for transfers between devices: 0.01 us -> 8.08 us  [hand_round(): lax.ppermute(value, everywhere, [(spot(x, t, t), spot(x, t, t ^ 2)) for x...]
  transfers between devices with their start and end apart: 35 -> 30, of which waited for: 16 -> 18; matrix products, arithmetic and copies ran while one was open for 7% -> 5% of each run, Pallas kernels for 3% -> 2%
where the time goes in v9:
time: 259 us; the launch traced here: 258 us
  waiting for transfers between devices  134 us (52%)
  starting transfers between devices  36.6 us (14%)
  Pallas kernels  29.3 us (11%)
  blocking collectives  19.7 us (8%)
  between operations  16.2 us (6%)
  local copies, waits for them, and re-layouts  11.4 us (4%)
  other arithmetic  9.93 us (4%)
    ppermute x19, waiting for transfers between devices, swap(): return lax.ppermute(value, axis, [(i, i ^ step) for i in range(size)])  66.3 us
    all_gather x1, waiting for transfers between devices, layer_plan(): gathered = lax.all_gather(collected, 'section', axis=0)  22.4 us
    ppermute x19, starting transfers between devices, swap(): return lax.ppermute(value, axis, [(i, i ^ step) for i in range(size)])  22.2 us
    all_gather x1, blocking collectives, layer_plan(): lax.all_gather(own[start:stop], 'tensor', axis=0)  19.7 us
    ppermute x2, waiting for transfers between devices, scatter(): lax.ppermute(value, everywhere, [(spot(x, source, s), spot(x, s, s)) for...  17.4 us
    pallas_call x3, Pallas kernels, chain_call(): pl.pallas_call(kernel, in_specs=[pl.BlockSpec(memory_space=pltpu.SMEM)] *...  15.9 us
    all_gather x1, waiting for transfers between devices, layer_plan(): lax.all_gather(own[start:stop], 'tensor', axis=0)  11.4 us
    ppermute x1, waiting for transfers between devices, layer_plan(): lax.ppermute(left_here, everywhere, [(spot(x, t, t), spot(1 - x, t, t)) f...  8.67 us
  transfers between devices with their start and end apart: 30, of which 18 were waited for; matrix products, arithmetic and copies ran while one was open for 5% of the time, Pallas kernels for 2%

profile of v9, /device:TPU:0, one launch (start us, length us, event | category | flops | bytes accessed | tf_op | source)
XLA Modules:
  0.0 258.2 jit_solution(13441919807865350830)
XLA Ops:
  10.0 5.1 %collective-permute-start.2 = (bf16[304,256]{1,0:T(8,128)(2,1)S(1)}, bf16[304,256]{1,0:T(8,128)(2,1)S(1)}, u32[]{:S(2)}, u32[]{:S(2)}) collective-permute-start(bf16[304,256]{1,0:T(8,128)(2,1)S(1)} %pad_maximum_fusion.4), channel_id=1, source_target_pairs={{0,12},{4,8},{8,4},{12,0},{1,13},{5,9},{9,5},{13,1},{2,14},{6,10},... | collective-permute-start | bytes 466952 | tf_op jit(solution)/shard_map/ppermute | solution.py:169
  17.3 2.4 collective-permute-start.4
  21.2 3.6 %fusion.6 = (bf16[576,576]{1,0:T(8,128)(2,1)}, bf16[576,576]{1,0:T(8,128)(2,1)}, bf16[576,576]{1,0:T(8,128)(2,1)S(1)}) fusion(f32[4,576,576]{2,1,0:T(8,128)} %param.12, s32[]{:T(128)S(6)} %select_n.139, s32[]{:T(128)S(6)} %select_n.133, s32[]{:T(128)S(6)} %select_n.130), kind=kLoop, calls=%fused_computation.18 | loop fusion | bytes 3981324 | tf_op jit(solution)/shard_map/convert_element_type | solution.py:623
  34.5 10.5 %collective-permute-done.1 = bf16[304,256]{1,0:T(8,128)(2,1)S(1)} collective-permute-done((bf16[304,256]{1,0:T(8,128)(2,1)S(1)}, bf16[304,256]{1,0:T(8,128)(2,1)S(1)}, u32[]{:S(2)}, u32[]{:S(2)}) %collective-permute-start.1) | collective-permute-done | bytes 155680 | tf_op jit(solution)/shard_map/ppermute | solution.py:169
  47.1 5.2 %collective-permute-done.3 = bf16[4,144,256]{2,1,0:T(8,128)(2,1)S(1)} collective-permute-done((bf16[4,144,256]{2,1,0:T(8,128)(2,1)S(1)}, bf16[4,144,256]{2,1,0:T(8,128)(2,1)S(1)}, u32[]{:S(2)}, u32[]{:S(2)}) %collective-permute-start.3) | collective-permute-done | bytes 294944 | tf_op jit(solution)/shard_map/ppermute | solution.py:169
  52.3 7.6 %collective-permute-done.4.old = bf16[576,576]{1,0:T(8,128)(2,1)S(1)} collective-permute-done((bf16[576,576]{1,0:T(8,128)(2,1)S(1)}, bf16[576,576]{1,0:T(8,128)(2,1)S(1)}, u32[]{:S(2)}, u32[]{:S(2)}) %collective-permute-start.4) | collective-permute-done | bytes 663584 | tf_op jit(solution)/shard_map/ppermute | solution.py:169
  60.9 2.5 collective-permute-start.9
  63.6 22.4 %all-gather.6.cloned.1.call-done = bf16[16,304,256]{2,1,0:T(8,128)(2,1)} async-done(((bf16[4,304,256]{2,1,0:T(8,128)(2,1)}), bf16[16,304,256]{2,1,0:T(8,128)(2,1)}) %all-gather.6.cloned.1.call-update) | async-done | bytes 2490384 | tf_op jit(solution)/shard_map/all_gather | solution.py:635
  87.6 2.8 %shard_map.111 = (bf16[2,2304,256]{2,1,0:T(8,128)(2,1)S(1)}, bf16[256,2304]{1,0:T(8,128)(2,1)S(1)}, f32[4,1,576]{2,1,0:T(1,128)S(1)}, f32[1]{0:T(128)}) custom-call(s32[3]{0:T(128)S(1)} %pad_add_fusion.1.place_ref, bf16[4,4,304,256]{3,2,1,0:T(8,128)(2,1)S(1)} %bitcast.89), custom_call_target="tpu_custom_call" | custom-call | flops 37748736 | bytes 8257536 | tf_op jit(solution)/shard_map/pallas_call | solution.py:237
  98.1 5.2 %shard_map.116 = (f32[2,256,576]{2,1,0:T(8,128)S(1)}, bf16[256,1152]{1,0:T(8,128)(2,1)S(1)}) custom-call(s32[1]{0:T(128)} %bitcast.1.place_ref, f32[1]{0:T(128)S(6)} %div.22.scale_ref, bf16[256,2304]{1,0:T(8,128)(2,1)S(1)} %get-tuple-element.35.rows, f32[4,1,576]{2,1,0:T(1,128)S(1)} %get-tuple-element.36.diag, bf16[576,576]{1,0:T(8,128)(2,1)S(1)} %shard_map.112.refs_0_, ...), custom_call_target="tpu_custom_call" | custom-call | flops 1358954496 | bytes 5308416 | tf_op jit(solution)/shard_map/pallas_call | solution.py:379
  104.9 13.8 %collective-permute-done.14.theirs = bf16[256,1152]{1,0:T(8,128)(2,1)S(1)} collective-permute-done((bf16[256,1152]{1,0:T(8,128)(2,1)S(1)}, bf16[256,1152]{1,0:T(8,128)(2,1)S(1)}, u32[]{:S(2)}, u32[]{:S(2)}) %collective-permute-start.14) | collective-permute-done | bytes 589856 | tf_op jit(solution)/shard_map/ppermute | solution.py:169
  118.7 5.6 %shard_map.117 = (f32[2,256,576]{2,1,0:T(8,128)S(1)}, bf16[256,1152]{1,0:T(8,128)(2,1)S(1)}) custom-call(s32[1]{0:T(128)} %bitcast.1.place_ref, f32[1]{0:T(128)S(6)} %div.22.scale_ref, bf16[256,1152]{1,0:T(8,128)(2,1)S(1)} %get-tuple-element.42.mine, bf16[256,1152]{1,0:T(8,128)(2,1)S(1)} %collective-permute-done.14.theirs, ...), custom_call_target="tpu_custom_call" | custom-call | flops 1358954496 | bytes 5308416 | tf_op jit(solution)/shard_map/pallas_call | solution.py:379
  126.0 13.0 %collective-permute-done.15.theirs = bf16[256,1152]{1,0:T(8,128)(2,1)S(1)} collective-permute-done((bf16[256,1152]{1,0:T(8,128)(2,1)S(1)}, bf16[256,1152]{1,0:T(8,128)(2,1)S(1)}, u32[]{:S(2)}, u32[]{:S(2)}) %collective-permute-start.15) | collective-permute-done | bytes 589856 | tf_op jit(solution)/shard_map/ppermute | solution.py:169
  139.0 5.0 %shard_map.118 = (bf16[576,256]{1,0:T(8,128)(2,1)S(1)}, bf16[576,256]{1,0:T(8,128)(2,1)S(1)}) custom-call(s32[1]{0:T(128)} %bitcast.1.place_ref, f32[1]{0:T(128)S(6)} %div.22.scale_ref, bf16[256,1152]{1,0:T(8,128)(2,1)S(1)} %get-tuple-element.44.mine, bf16[256,1152]{1,0:T(8,128)(2,1)S(1)} %collective-permute-done.15.theirs, ...), custom_call_target="tpu_custom_call" | custom-call | flops 1358954496 | bytes 5308416 | tf_op jit(solution)/shard_map/pallas_call | solution.py:379
  149.5 3.6 %collective-permute-done.18 = f32[8,576]{1,0:T(8,128)S(1)} collective-permute-done((f32[8,576]{1,0:T(8,128)S(1)}, f32[8,576]{1,0:T(8,128)S(1)}, u32[]{:S(2)}, u32[]{:S(2)}) %collective-permute-start.18) | collective-permute-done | bytes 18464 | tf_op jit(solution)/shard_map/ppermute | solution.py:678
  153.0 13.8 %collective-permute-done.17.moved = bf16[576,512]{1,0:T(8,128)(2,1)S(1)} collective-permute-done((bf16[576,512]{1,0:T(8,128)(2,1)S(1)}, bf16[576,512]{1,0:T(8,128)(2,1)S(1)}, u32[]{:S(2)}, u32[]{:S(2)}) %collective-permute-start.17) | collective-permute-done | bytes 589856 | tf_op jit(solution)/shard_map/ppermute | solution.py:678
  166.9 3.5 %collective-permute-start.22 = (bf16[608,512]{1,0:T(8,128)(2,1)S(1)}, bf16[608,512]{1,0:T(8,128)(2,1)S(1)}, u32[]{:S(2)}, u32[]{:S(2)}) collective-permute-start(bf16[608,512]{1,0:T(8,128)(2,1)S(1)} %shard_map.119.refs_0_), channel_id=1, source_target_pairs={{0,16},{5,21},{10,26},{15,31},{16,0},{21,5},{26,10},{31,15}} | collective-permute-start | bytes 1867784 | tf_op jit(solution)/shard_map/ppermute | solution.py:709
  170.4 8.7 %collective-permute-done.22.refs_4_ = bf16[608,512]{1,0:T(8,128)(2,1)S(1)} collective-permute-done((bf16[608,512]{1,0:T(8,128)(2,1)S(1)}, bf16[608,512]{1,0:T(8,128)(2,1)S(1)}, u32[]{:S(2)}, u32[]{:S(2)}) %collective-permute-start.22) | collective-permute-done | bytes 622624 | tf_op jit(solution)/shard_map/ppermute | solution.py:709
  179.0 11.4 %all-gather.8.cloned.1.call-done = bf16[1536,512]{1,0:T(8,128)(2,1)} async-done(((bf16[384,512]{1,0:T(8,128)(2,1)}), bf16[1536,512]{1,0:T(8,128)(2,1)}) %all-gather.8.cloned.1.call-update) | async-done | bytes 1572880 | tf_op jit(solution)/shard_map/all_gather | solution.py:700
  199.9 3.4 %collective-permute-done.20.refs_2_ = bf16[608,512]{1,0:T(8,128)(2,1)} collective-permute-done((bf16[608,512]{1,0:T(8,128)(2,1)S(1)}, bf16[608,512]{1,0:T(8,128)(2,1)}, u32[]{:S(2)}, u32[]{:S(2)}) %collective-permute-start.20) | collective-permute-done | bytes 622624 | tf_op jit(solution)/shard_map/ppermute | solution.py:685
  205.4 4.6 %collective-permute-done.24.refs_6_ = bf16[608,512]{1,0:T(8,128)(2,1)} collective-permute-done((bf16[608,512]{1,0:T(8,128)(2,1)S(1)}, bf16[608,512]{1,0:T(8,128)(2,1)}, u32[]{:S(2)}, u32[]{:S(2)}) %collective-permute-start.24) | collective-permute-done | bytes 622624 | tf_op jit(solution)/shard_map/ppermute | solution.py:685
  211.3 19.7 %all-gather.2 = bf16[768,512]{1,0:T(8,128)(2,1)S(1)} all-gather(bf16[192,512]{1,0:T(8,128)(2,1)S(1)} %slice.108), channel_id=4, replica_groups=mesh['shard'=2,'tensor'=4,'section'=4] {'tensor'}, dimensions={0}, use_global_device_ids=true | all-gather | bytes 983040 | tf_op jit(solution)/shard_map/all_gather | solution.py:700
  234.5 8.8 %collective-permute-done.27.refs_11_ = bf16[3,192,512]{2,1,0:T(8,128)(2,1)} collective-permute-done((bf16[3,192,512]{2,1,0:T(8,128)(2,1)S(1)}, bf16[3,192,512]{2,1,0:T(8,128)(2,1)}, u32[]{:S(2)}, u32[]{:S(2)}) %collective-permute-start.27) | collective-permute-done | bytes 589856 | tf_op jit(solution)/shard_map/ppermute | solution.py:169
  243.3 8.1 %shard_map.120 = (f32[4,576,576]{2,1,0:T(8,128)}, f32[576,2048]{1,0:T(8,128)}) custom-call(s32[2]{0:T(128)} %pad_add_fusion.where_ref, f32[1,2048]{1,0:T(1,128)} %bitcast.97, bf16[512,2048]{1,0:T(8,128)(2,1)} %compare_convert_fusion.matches, bf16[608,512]{1,0:T(8,128)(2,1)} %copy-done.1, bf16[608,512]{1,0:T(8,128)(2,1)} %copy-done.5, ...), custom_call_target="tpu_custom_call" | custom-call | flops 2566914048 | bytes 14155776 | tf_op jit(solution)/shard_map/pallas_call | solution.py:510
  (137 shorter events, 51.5 us)
Async XLA Ops:
  7.2 78.7 %all-gather.6.cloned.1.call-start = ((), (), s32[]{:S(2)}) async-start(), calls=%async_computation | async-start | bytes 3112960 | tf_op jit(solution)/shard_map/all_gather | solution.py:635
  10.0 24.5 %collective-permute-start.2 = (bf16[304,256]{1,0:T(8,128)(2,1)S(1)}, bf16[304,256]{1,0:T(8,128)(2,1)S(1)}, u32[]{:S(2)}, u32[]{:S(2)}) collective-permute-start(bf16[304,256]{1,0:T(8,128)(2,1)S(1)} %pad_maximum_fusion.4), channel_id=1, source_target_pairs={{0,12},{4,8},{8,4},{12,0},{1,13},{5,9},{9,5},{13,1},{2,14},{6,10},... | collective-permute-start | bytes 466952 | tf_op jit(solution)/shard_map/ppermute | solution.py:169
  15.1 29.9 %collective-permute-start.1 = (bf16[304,256]{1,0:T(8,128)(2,1)S(1)}, bf16[304,256]{1,0:T(8,128)(2,1)S(1)}, u32[]{:S(2)}, u32[]{:S(2)}) collective-permute-start(bf16[304,256]{1,0:T(8,128)(2,1)S(1)} %pad_maximum_fusion.3), channel_id=1, source_target_pairs={{0,8},{4,12},{8,0},{12,4},{1,9},{5,13},{9,1},{13,5},{2,10},{6,14},... | collective-permute-start | bytes 466952 | tf_op jit(solution)/shard_map/ppermute | solution.py:169
  15.2 29.8 %collective-permute-start = (bf16[304,256]{1,0:T(8,128)(2,1)S(1)}, bf16[304,256]{1,0:T(8,128)(2,1)S(1)}, u32[]{:S(2)}, u32[]{:S(2)}) collective-permute-start(bf16[304,256]{1,0:T(8,128)(2,1)S(1)} %pad_maximum_fusion.2), channel_id=1, source_target_pairs={{0,4},{4,0},{8,12},{12,8},{1,5},{5,1},{9,13},{13,9},{2,6},{6,2},{1... | collective-permute-start | bytes 466952 | tf_op jit(solution)/shard_map/ppermute | solution.py:169
  17.3 42.6 %collective-permute-start.4 = (bf16[576,576]{1,0:T(8,128)(2,1)S(1)}, bf16[576,576]{1,0:T(8,128)(2,1)S(1)}, u32[]{:S(2)}, u32[]{:S(2)}) collective-permute-start(bf16[576,576]{1,0:T(8,128)(2,1)S(1)} %fusion.3), channel_id=1, source_target_pairs={{0,8},{4,12},{8,0},{12,4},{1,9},{5,13},{9,1},{13,5},{2,10},{6,14},... | collective-permute-start | bytes 1990664 | tf_op jit(solution)/shard_map/ppermute | solution.py:169
  19.7 5.4 %collective-permute-start.6 = (s32[256]{0:T(256)S(1)}, s32[256]{0:T(256)S(1)}, u32[]{:S(2)}, u32[]{:S(2)}) collective-permute-start(s32[256]{0:T(256)S(1)} %copy-done.13), channel_id=1, source_target_pairs={{0,16},{16,0},{1,17},{17,1},{2,18},{18,2},{3,19},{19,3},{4,20},{20... | collective-permute-start | bytes 3080 | tf_op jit(solution)/shard_map/ppermute | solution.py:169
  45.2 7.2 %collective-permute-start.3 = (bf16[4,144,256]{2,1,0:T(8,128)(2,1)S(1)}, bf16[4,144,256]{2,1,0:T(8,128)(2,1)S(1)}, u32[]{:S(2)}, u32[]{:S(2)}) collective-permute-start(bf16[4,144,256]{2,1,0:T(8,128)(2,1)S(1)} %slice.106), channel_id=1, source_target_pairs={{0,16},{16,0},{1,17},{17,1},{2,18},{18,2},{3,19},{19,3},{4,20},{20... | collective-permute-start | bytes 884744 | tf_op jit(solution)/shard_map/ppermute | solution.py:169
  60.8 129.6 %all-gather.8.cloned.1.call-start = ((), (), s32[]{:S(2)}) async-start(), calls=%async_computation.1 | async-start | bytes 1966080 | tf_op jit(solution)/shard_map/all_gather | solution.py:700
  60.9 30.5 %collective-permute-start.8 = (bf16[576,576]{1,0:T(8,128)(2,1)}, bf16[576,576]{1,0:T(8,128)(2,1)S(1)}, u32[]{:S(2)}, u32[]{:S(2)}) collective-permute-start(bf16[576,576]{1,0:T(8,128)(2,1)} %get-tuple-element.39), channel_id=1, source_target_pairs={{0,4},{4,0},{8,12},{12,8},{1,5},{5,1},{9,13},{13,9},{2,6},{6,2},{1... | collective-permute-start | bytes 1990664 | tf_op jit(solution)/shard_map/ppermute | solution.py:169
  60.9 34.2 %collective-permute-start.9 = (bf16[576,576]{1,0:T(8,128)(2,1)}, bf16[576,576]{1,0:T(8,128)(2,1)S(1)}, u32[]{:S(2)}, u32[]{:S(2)}) collective-permute-start(bf16[576,576]{1,0:T(8,128)(2,1)} %get-tuple-element.41), channel_id=1, source_target_pairs={{0,12},{4,8},{8,4},{12,0},{1,13},{5,9},{9,5},{13,1},{2,14},{6,10},... | collective-permute-start | bytes 1990664 | tf_op jit(solution)/shard_map/ppermute | solution.py:169
  91.1 5.5 %collective-permute-start.10 = (bf16[576,576]{1,0:T(8,128)(2,1)S(1)}, bf16[576,576]{1,0:T(8,128)(2,1)S(1)}, u32[]{:S(2)}, u32[]{:S(2)}) collective-permute-start(bf16[576,576]{1,0:T(8,128)(2,1)S(1)} %shard_map.112.refs_0_), channel_id=1, source_target_pairs={{0,1},{1,0},{2,3},{3,2},{4,5},{5,4},{6,7},{7,6},{8,9},{9,8},{10,11... | collective-permute-start | bytes 1990664 | tf_op jit(solution)/shard_map/ppermute | solution.py:169
  103.3 15.4 %collective-permute-start.14 = (bf16[256,1152]{1,0:T(8,128)(2,1)S(1)}, bf16[256,1152]{1,0:T(8,128)(2,1)S(1)}, u32[]{:S(2)}, u32[]{:S(2)}) collective-permute-start(bf16[256,1152]{1,0:T(8,128)(2,1)S(1)} %get-tuple-element.42.mine), channel_id=1, source_target_pairs={{0,2},{1,3},{2,0},{3,1},{4,6},{5,7},{6,4},{7,5},{8,10},{9,11},{10,... | collective-permute-start | bytes 1769480 | tf_op jit(solution)/shard_map/ppermute | solution.py:169
  124.4 14.6 %collective-permute-start.15 = (bf16[256,1152]{1,0:T(8,128)(2,1)S(1)}, bf16[256,1152]{1,0:T(8,128)(2,1)S(1)}, u32[]{:S(2)}, u32[]{:S(2)}) collective-permute-start(bf16[256,1152]{1,0:T(8,128)(2,1)S(1)} %get-tuple-element.44.mine), channel_id=1, source_target_pairs={{0,2},{1,3},{2,0},{3,1},{4,6},{5,7},{6,4},{7,5},{8,10},{9,11},{10,... | collective-permute-start | bytes 1769480 | tf_op jit(solution)/shard_map/ppermute | solution.py:169
  145.8 21.0 %collective-permute-start.17 = (bf16[576,512]{1,0:T(8,128)(2,1)S(1)}, bf16[576,512]{1,0:T(8,128)(2,1)S(1)}, u32[]{:S(2)}, u32[]{:S(2)}) collective-permute-start(bf16[576,512]{1,0:T(8,128)(2,1)S(1)} %maximum_select_fusion.own), channel_id=1, source_target_pairs={{12,0},{13,5},{14,10},{28,16},{29,21},{30,26}} | collective-permute-start | bytes 1769480 | tf_op jit(solution)/shard_map/ppermute | solution.py:678
  147.3 5.7 %collective-permute-start.18 = (f32[8,576]{1,0:T(8,128)S(1)}, f32[8,576]{1,0:T(8,128)S(1)}, u32[]{:S(2)}, u32[]{:S(2)}) collective-permute-start(f32[8,576]{1,0:T(8,128)S(1)} %convolution_multiply_fusion), channel_id=1, source_target_pairs={{4,0},{6,10},{7,15},{20,16},{22,26},{23,31}} | collective-permute-start | bytes 55304 | tf_op jit(solution)/shard_map/ppermute | solution.py:678
  166.9 12.1 %collective-permute-start.22 = (bf16[608,512]{1,0:T(8,128)(2,1)S(1)}, bf16[608,512]{1,0:T(8,128)(2,1)S(1)}, u32[]{:S(2)}, u32[]{:S(2)}) collective-permute-start(bf16[608,512]{1,0:T(8,128)(2,1)S(1)} %shard_map.119.refs_0_), channel_id=1, source_target_pairs={{0,16},{5,21},{10,26},{15,31},{16,0},{21,5},{26,10},{31,15}} | collective-permute-start | bytes 1867784 | tf_op jit(solution)/shard_map/ppermute | solution.py:709
  192.8 38.3 %collective-permute-start.26 = (bf16[3,384,512]{2,1,0:T(8,128)(2,1)}, bf16[3,384,512]{2,1,0:T(8,128)(2,1)S(1)}, u32[]{:S(2)}, u32[]{:S(2)}) collective-permute-start(bf16[3,384,512]{2,1,0:T(8,128)(2,1)} %slice.88), channel_id=1, source_target_pairs={{0,16},{16,0},{1,17},{17,1},{2,18},{18,2},{3,19},{19,3},{4,20},{20... | collective-permute-start | bytes 3538952 | tf_op jit(solution)/shard_map/ppermute | solution.py:169
  194.3 9.0 %collective-permute-start.20 = (bf16[608,512]{1,0:T(8,128)(2,1)S(1)}, bf16[608,512]{1,0:T(8,128)(2,1)}, u32[]{:S(2)}, u32[]{:S(2)}) collective-permute-start(bf16[608,512]{1,0:T(8,128)(2,1)S(1)} %shard_map.119.refs_0_), channel_id=1, source_target_pairs={{0,2},{5,7},{10,8},{15,13},{16,18},{21,23},{26,24},{31,29}} | collective-permute-start | bytes 1867784 | tf_op jit(solution)/shard_map/ppermute | solution.py:685
  196.4 13.6 %collective-permute-start.24 = (bf16[608,512]{1,0:T(8,128)(2,1)S(1)}, bf16[608,512]{1,0:T(8,128)(2,1)}, u32[]{:S(2)}, u32[]{:S(2)}) collective-permute-start(bf16[608,512]{1,0:T(8,128)(2,1)S(1)} %collective-permute-done.22.refs_4_), channel_id=1, source_target_pairs={{0,2},{5,7},{10,8},{15,13},{16,18},{21,23},{26,24},{31,29}} | collective-permute-start | bytes 1867784 | tf_op jit(solution)/shard_map/ppermute | solution.py:685
  198.6 33.8 %collective-permute-start.19 = (bf16[608,512]{1,0:T(8,128)(2,1)S(1)}, bf16[608,512]{1,0:T(8,128)(2,1)S(1)}, u32[]{:S(2)}, u32[]{:S(2)}) collective-permute-start(bf16[608,512]{1,0:T(8,128)(2,1)S(1)} %shard_map.119.refs_0_), channel_id=1, source_target_pairs={{0,1},{5,4},{10,11},{15,14},{16,17},{21,20},{26,27},{31,30}} | collective-permute-start | bytes 1867784 | tf_op jit(solution)/shard_map/ppermute | solution.py:688
  203.3 29.0 %collective-permute-start.21 = (bf16[608,512]{1,0:T(8,128)(2,1)}, bf16[608,512]{1,0:T(8,128)(2,1)S(1)}, u32[]{:S(2)}, u32[]{:S(2)}) collective-permute-start(bf16[608,512]{1,0:T(8,128)(2,1)} %collective-permute-done.20.refs_2_), channel_id=1, source_target_pairs={{2,3},{7,6},{8,9},{13,12},{18,19},{23,22},{24,25},{29,28}} | collective-permute-start | bytes 1867784 | tf_op jit(solution)/shard_map/ppermute | solution.py:691
  204.0 28.3 %collective-permute-start.23 = (bf16[608,512]{1,0:T(8,128)(2,1)S(1)}, bf16[608,512]{1,0:T(8,128)(2,1)S(1)}, u32[]{:S(2)}, u32[]{:S(2)}) collective-permute-start(bf16[608,512]{1,0:T(8,128)(2,1)S(1)} %collective-permute-done.22.refs_4_), channel_id=1, source_target_pairs={{0,1},{5,4},{10,11},{15,14},{16,17},{21,20},{26,27},{31,30}} | collective-permute-start | bytes 1867784 | tf_op jit(solution)/shard_map/ppermute | solution.py:688
  210.0 22.4 %collective-permute-start.25 = (bf16[608,512]{1,0:T(8,128)(2,1)}, bf16[608,512]{1,0:T(8,128)(2,1)S(1)}, u32[]{:S(2)}, u32[]{:S(2)}) collective-permute-start(bf16[608,512]{1,0:T(8,128)(2,1)} %collective-permute-done.24.refs_6_), channel_id=1, source_target_pairs={{2,3},{7,6},{8,9},{13,12},{18,19},{23,22},{24,25},{29,28}} | collective-permute-start | bytes 1867784 | tf_op jit(solution)/shard_map/ppermute | solution.py:691
  231.1 12.1 %collective-permute-start.27 = (bf16[3,192,512]{2,1,0:T(8,128)(2,1)S(1)}, bf16[3,192,512]{2,1,0:T(8,128)(2,1)}, u32[]{:S(2)}, u32[]{:S(2)}) collective-permute-start(bf16[3,192,512]{2,1,0:T(8,128)(2,1)S(1)} %slice.89), channel_id=1, source_target_pairs={{0,16},{16,0},{1,17},{17,1},{2,18},{18,2},{3,19},{19,3},{4,20},{20... | collective-permute-start | bytes 1769480 | tf_op jit(solution)/shard_map/ppermute | solution.py:169
  (22 other events, 246.5 us)
Sparse Core Ops, SparseCore 0:
  60.9 24.9 all-gather.5
  149.6 40.8 all-gather.7

commit v10 on v9

--- a/solution.py
+++ b/solution.py
@@ -418,7 +418,7 @@
         out_shape=jax.ShapeDtypeStruct((rows + 4 * codes.shape[0], width), own.dtype),
         compiler_params=params(),
         cost_estimate=pl.CostEstimate(
-            flops=60 * rows * rows * rows * 4, bytes_accessed=8 * rows * width, transcendentals=0
+            flops=rows * width, bytes_accessed=8 * rows * width, transcendentals=0
         ),
     )(take.astype(jnp.int32).reshape(1), own, moved, codes)
 
@@ -695,10 +695,11 @@
         )
         return (value, near, sides, far)
 
-    cut = col_block // 3 * 2
+    parts = 3
+    size = col_block // parts
     mine = [
-        lax.all_gather(own[start:stop], "tensor", axis=0)
-        for start, stop in ((0, cut), (cut, col_block))
+        lax.all_gather(own[part * size : (part + 1) * size], "tensor", axis=0)
+        for part in range(parts)
     ]
     router_cols = learning_rate * jnp.einsum(
         "fn,cn->fc", router_right, own, preferred_element_type=jnp.float32
@@ -706,19 +707,14 @@
     router_cols = jnp.where(layer == 1, router_cols, scatter(router_cols, 1))
     left_layer = n_tensor - 1
     left_here = left_message(layer == left_layer, own, scatter(own, left_layer), router_cols)
+    left_here, mine[0] = lax.optimization_barrier((left_here, mine[0]))
     left_there = lax.ppermute(
         left_here, everywhere, [(spot(x, t, t), spot(1 - x, t, t)) for x in planes for t in layers]
     )
     lefts_here = hand_round(left_here)
-
-    def hand_over(piece):
-        return swap(piece[: n_tensor - 1], "shard", n_shard, 1)
-
-    left_there, mine[0] = lax.optimization_barrier((left_there, mine[0]))
+    left_there, mine[1] = lax.optimization_barrier((left_there, mine[1]))
     lefts_there = hand_round(left_there)
-    others = [hand_over(mine[0])]
-    mine[1], others[0] = lax.optimization_barrier((mine[1], others[0]))
-    others.append(hand_over(mine[1]))
+    others = [swap(piece[: n_tensor - 1], "shard", n_shard, 1) for piece in mine]
     turn = section ^ layer
 
     def codes_of(group):

time: 259 us -> 283 us (1.093)
  blocking collectives: 19.7 us -> 65.6 us
  waiting for transfers between devices: 134 us -> 113 us
    all_gather x1 -> x3, blocking collectives: 19.7 us -> 65.6 us  [layer_plan(): lax.all_gather(own[part * size:(part + 1) * size], 'tensor', axis=0)]
    ppermute x19 -> x20, waiting for transfers between devices: 66.3 us -> 88.5 us  [swap(): return lax.ppermute(value, axis, [(i, i ^ step) for i in range(size)])]
    ppermute x2, waiting for transfers between devices: 17.4 us -> 0.01 us  [scatter(): lax.ppermute(value, everywhere, [(spot(x, source, s), spot(x, s, s)) for...]
    all_gather x1 -> x0, waiting for transfers between devices: 11.4 us -> none  [layer_plan(): lax.all_gather(own[start:stop], 'tensor', axis=0)]
    ppermute x1, waiting for transfers between devices: 8.67 us -> 0.01 us  [layer_plan(): lax.ppermute(left_here, everywhere, [(spot(x, t, t), spot(1 - x, t, t)) f...]
    ppermute x2, waiting for transfers between devices: 8.08 us -> 2.29 us  [hand_round(): lax.ppermute(value, everywhere, [(spot(x, t, t), spot(x, t, t ^ 2)) for x...]
    slice x4, local copies, waits for them, and re-layouts: 3.2 us -> 0.16 us  [the longest x3 0.12 us: layer_plan(): others = [swap(piece[:n_tensor - 1], 'shard', n_shard, 1) for piece in mine]]
    ppermute x19 -> x20, starting transfers between devices: 22.2 us -> 22.8 us  [swap(): return lax.ppermute(value, axis, [(i, i ^ step) for i in range(size)])]
  transfers between devices with their start and end apart: 30 -> 30, of which waited for: 18 -> 15; matrix products, arithmetic and copies ran while one was open for 5% -> 5% of each run, Pallas kernels for 2% -> 2%
where the time goes in v10:
time: 283 us; the launch traced here: 282 us
  waiting for transfers between devices  113 us (40%)
  blocking collectives  65.6 us (23%)
  starting transfers between devices  38.6 us (14%)
  Pallas kernels  29.2 us (10%)
  between operations  16.1 us (6%)
  other arithmetic  10.2 us (4%)
  local copies, waits for them, and re-layouts  8.66 us (3%)
    ppermute x20, waiting for transfers between devices, swap(): return lax.ppermute(value, axis, [(i, i ^ step) for i in range(size)])  88.5 us
    all_gather x3, blocking collectives, layer_plan(): lax.all_gather(own[part * size:(part + 1) * size], 'tensor', axis=0)  65.6 us
    ppermute x20, starting transfers between devices, swap(): return lax.ppermute(value, axis, [(i, i ^ step) for i in range(size)])  22.8 us
    all_gather x1, waiting for transfers between devices, layer_plan(): gathered = lax.all_gather(collected, 'section', axis=0)  22.4 us
    pallas_call x3, Pallas kernels, chain_call(): pl.pallas_call(kernel, in_specs=[pl.BlockSpec(memory_space=pltpu.SMEM)] *...  15.9 us
    pallas_call x1, Pallas kernels, output_products(): pl.pallas_call(functools.partial(output_kernel, parts=parts), in_specs=[p...  7.97 us
  transfers between devices with their start and end apart: 30, of which 15 were waited for; matrix products, arithmetic and copies ran while one was open for 5% of the time, Pallas kernels for 2%

profile of v10, /device:TPU:0, one launch (start us, length us, event | category | flops | bytes accessed | tf_op | source)
XLA Modules:
  0.0 282.5 jit_solution(16086995833586534326)
XLA Ops:
  10.0 5.1 %collective-permute-start.2 = (bf16[304,256]{1,0:T(8,128)(2,1)S(1)}, bf16[304,256]{1,0:T(8,128)(2,1)S(1)}, u32[]{:S(2)}, u32[]{:S(2)}) collective-permute-start(bf16[304,256]{1,0:T(8,128)(2,1)S(1)} %pad_maximum_fusion.4), channel_id=1, source_target_pairs={{0,12},{4,8},{8,4},{12,0},{1,13},{5,9},{9,5},{13,1},{2,14},{6,10},... | collective-permute-start | bytes 466952 | tf_op jit(solution)/shard_map/ppermute | solution.py:169
  17.3 2.4 collective-permute-start.4
  21.2 3.6 %fusion.6 = (bf16[576,576]{1,0:T(8,128)(2,1)}, bf16[576,576]{1,0:T(8,128)(2,1)}, bf16[576,576]{1,0:T(8,128)(2,1)S(1)}) fusion(f32[4,576,576]{2,1,0:T(8,128)} %param.12, s32[]{:T(128)S(6)} %select_n.139, s32[]{:T(128)S(6)} %select_n.133, s32[]{:T(128)S(6)} %select_n.130), kind=kLoop, calls=%fused_computation.18 | loop fusion | bytes 3981324 | tf_op jit(solution)/shard_map/convert_element_type | solution.py:623
  30.1 2.3 collective-permute-done.5
  34.5 10.5 %collective-permute-done.1 = bf16[304,256]{1,0:T(8,128)(2,1)S(1)} collective-permute-done((bf16[304,256]{1,0:T(8,128)(2,1)S(1)}, bf16[304,256]{1,0:T(8,128)(2,1)S(1)}, u32[]{:S(2)}, u32[]{:S(2)}) %collective-permute-start.1) | collective-permute-done | bytes 155680 | tf_op jit(solution)/shard_map/ppermute | solution.py:169
  47.1 5.2 %collective-permute-done.3 = bf16[4,144,256]{2,1,0:T(8,128)(2,1)S(1)} collective-permute-done((bf16[4,144,256]{2,1,0:T(8,128)(2,1)S(1)}, bf16[4,144,256]{2,1,0:T(8,128)(2,1)S(1)}, u32[]{:S(2)}, u32[]{:S(2)}) %collective-permute-start.3) | collective-permute-done | bytes 294944 | tf_op jit(solution)/shard_map/ppermute | solution.py:169
  52.3 7.6 %collective-permute-done.4.old = bf16[576,576]{1,0:T(8,128)(2,1)S(1)} collective-permute-done((bf16[576,576]{1,0:T(8,128)(2,1)S(1)}, bf16[576,576]{1,0:T(8,128)(2,1)S(1)}, u32[]{:S(2)}, u32[]{:S(2)}) %collective-permute-start.4) | collective-permute-done | bytes 663584 | tf_op jit(solution)/shard_map/ppermute | solution.py:169
  60.9 2.5 collective-permute-start.9
  63.5 22.4 %all-gather.6.cloned.1.call-done = bf16[16,304,256]{2,1,0:T(8,128)(2,1)} async-done(((bf16[4,304,256]{2,1,0:T(8,128)(2,1)}), bf16[16,304,256]{2,1,0:T(8,128)(2,1)}) %all-gather.6.cloned.1.call-update) | async-done | bytes 2490384 | tf_op jit(solution)/shard_map/all_gather | solution.py:635
  87.6 2.8 shard_map.111
  98.0 5.2 %shard_map.116 = (f32[2,256,576]{2,1,0:T(8,128)S(1)}, bf16[256,1152]{1,0:T(8,128)(2,1)S(1)}) custom-call(s32[1]{0:T(128)} %bitcast.1.place_ref, f32[1]{0:T(128)S(6)} %div.22.scale_ref, bf16[256,2304]{1,0:T(8,128)(2,1)S(1)} %get-tuple-element.35.rows, f32[4,1,576]{2,1,0:T(1,128)S(1)} %get-tuple-element.36.diag, bf16[576,576]{1,0:T(8,128)(2,1)S(1)} %shard_map.112.refs_0_, ...), custom_call_target="tpu_custom_call" | custom-call | flops 1358954496 | bytes 5308416 | tf_op jit(solution)/shard_map/pallas_call | solution.py:379
  104.8 13.9 %collective-permute-done.14.theirs = bf16[256,1152]{1,0:T(8,128)(2,1)S(1)} collective-permute-done((bf16[256,1152]{1,0:T(8,128)(2,1)S(1)}, bf16[256,1152]{1,0:T(8,128)(2,1)S(1)}, u32[]{:S(2)}, u32[]{:S(2)}) %collective-permute-start.14) | collective-permute-done | bytes 589856 | tf_op jit(solution)/shard_map/ppermute | solution.py:169
  118.7 5.6 %shard_map.117 = (f32[2,256,576]{2,1,0:T(8,128)S(1)}, bf16[256,1152]{1,0:T(8,128)(2,1)S(1)}) custom-call(s32[1]{0:T(128)} %bitcast.1.place_ref, f32[1]{0:T(128)S(6)} %div.22.scale_ref, bf16[256,1152]{1,0:T(8,128)(2,1)S(1)} %get-tuple-element.42.mine, bf16[256,1152]{1,0:T(8,128)(2,1)S(1)} %collective-permute-done.14.theirs, ...), custom_call_target="tpu_custom_call" | custom-call | flops 1358954496 | bytes 5308416 | tf_op jit(solution)/shard_map/pallas_call | solution.py:379
  125.9 13.0 %collective-permute-done.15.theirs = bf16[256,1152]{1,0:T(8,128)(2,1)S(1)} collective-permute-done((bf16[256,1152]{1,0:T(8,128)(2,1)S(1)}, bf16[256,1152]{1,0:T(8,128)(2,1)S(1)}, u32[]{:S(2)}, u32[]{:S(2)}) %collective-permute-start.15) | collective-permute-done | bytes 589856 | tf_op jit(solution)/shard_map/ppermute | solution.py:169
  139.0 5.0 %shard_map.118 = (bf16[576,256]{1,0:T(8,128)(2,1)S(1)}, bf16[576,256]{1,0:T(8,128)(2,1)S(1)}) custom-call(s32[1]{0:T(128)} %bitcast.1.place_ref, f32[1]{0:T(128)S(6)} %div.22.scale_ref, bf16[256,1152]{1,0:T(8,128)(2,1)S(1)} %get-tuple-element.44.mine, bf16[256,1152]{1,0:T(8,128)(2,1)S(1)} %collective-permute-done.15.theirs, ...), custom_call_target="tpu_custom_call" | custom-call | flops 1358954496 | bytes 5308416 | tf_op jit(solution)/shard_map/pallas_call | solution.py:379
  148.7 28.9 %all-gather.1 = bf16[768,512]{1,0:T(8,128)(2,1)S(1)} all-gather(bf16[192,512]{1,0:T(8,128)(2,1)S(1)} %get-tuple-element.67), channel_id=3, replica_groups=mesh['shard'=2,'tensor'=4,'section'=4] {'tensor'}, dimensions={0}, use_global_device_ids=true | all-gather | bytes 983040 | tf_op jit(solution)/shard_map/all_gather | solution.py:701
  177.7 3.3 %collective-permute-start.22 = (bf16[608,512]{1,0:T(8,128)(2,1)S(1)}, bf16[608,512]{1,0:T(8,128)(2,1)}, u32[]{:S(2)}, u32[]{:S(2)}) collective-permute-start(bf16[608,512]{1,0:T(8,128)(2,1)S(1)} %shard_map.119.refs_0_), channel_id=1, source_target_pairs={{0,16},{5,21},{10,26},{15,31},{16,0},{21,5},{26,10},{31,15}} | collective-permute-start | bytes 1867784 | tf_op jit(solution)/shard_map/ppermute | solution.py:711
  183.2 17.4 %all-gather.2 = bf16[768,512]{1,0:T(8,128)(2,1)S(1)} all-gather(bf16[192,512]{1,0:T(8,128)(2,1)S(1)} %get-tuple-element.66), channel_id=4, replica_groups=mesh['shard'=2,'tensor'=4,'section'=4] {'tensor'}, dimensions={0}, use_global_device_ids=true | all-gather | bytes 983040 | tf_op jit(solution)/shard_map/all_gather | solution.py:701
  207.6 2.3 collective-permute-done.24.refs_6_
  211.3 19.4 %all-gather.3 = bf16[768,512]{1,0:T(8,128)(2,1)S(1)} all-gather(bf16[192,512]{1,0:T(8,128)(2,1)S(1)} %get-tuple-element.65), channel_id=5, replica_groups=mesh['shard'=2,'tensor'=4,'section'=4] {'tensor'}, dimensions={0}, use_global_device_ids=true | all-gather | bytes 983040 | tf_op jit(solution)/shard_map/all_gather | solution.py:701
  235.9 11.3 %collective-permute-done.28.refs_13_ = bf16[3,192,512]{2,1,0:T(8,128)(2,1)} collective-permute-done((bf16[3,192,512]{2,1,0:T(8,128)(2,1)S(1)}, bf16[3,192,512]{2,1,0:T(8,128)(2,1)}, u32[]{:S(2)}, u32[]{:S(2)}) %collective-permute-start.28) | collective-permute-done | bytes 589856 | tf_op jit(solution)/shard_map/ppermute | solution.py:169
  247.1 12.5 %collective-permute-done.26.refs_11_ = bf16[3,192,512]{2,1,0:T(8,128)(2,1)S(1)} collective-permute-done((bf16[3,192,512]{2,1,0:T(8,128)(2,1)S(1)}, bf16[3,192,512]{2,1,0:T(8,128)(2,1)S(1)}, u32[]{:S(2)}, u32[]{:S(2)}) %collective-permute-start.26) | collective-permute-done | bytes 589856 | tf_op jit(solution)/shard_map/ppermute | solution.py:169
  259.7 7.2 %collective-permute-done.27.refs_12_ = bf16[3,192,512]{2,1,0:T(8,128)(2,1)S(1)} collective-permute-done((bf16[3,192,512]{2,1,0:T(8,128)(2,1)S(1)}, bf16[3,192,512]{2,1,0:T(8,128)(2,1)S(1)}, u32[]{:S(2)}, u32[]{:S(2)}) %collective-permute-start.27) | collective-permute-done | bytes 589856 | tf_op jit(solution)/shard_map/ppermute | solution.py:169
  267.6 8.0 %shard_map.120 = (f32[4,576,576]{2,1,0:T(8,128)}, f32[576,2048]{1,0:T(8,128)}) custom-call(s32[2]{0:T(128)} %pad_add_fusion.where_ref, f32[1,2048]{1,0:T(1,128)} %bitcast.101, bf16[512,2048]{1,0:T(8,128)(2,1)} %compare_convert_fusion.matches, bf16[608,512]{1,0:T(8,128)(2,1)} %copy-done, bf16[608,512]{1,0:T(8,128)(2,1)} %collective-permute-done.19.refs_1_, ...), custom_call_target="tpu_custom_call" | custom-call | flops 2566914048 | bytes 14155776 | tf_op jit(solution)/shard_map/pallas_call | solution.py:510
  (138 shorter events, 48.9 us)
Async XLA Ops:
  7.2 78.7 %all-gather.6.cloned.1.call-start = ((), (), s32[]{:S(2)}) async-start(), calls=%async_computation | async-start | bytes 3112960 | tf_op jit(solution)/shard_map/all_gather | solution.py:635
  10.0 24.5 %collective-permute-start.2 = (bf16[304,256]{1,0:T(8,128)(2,1)S(1)}, bf16[304,256]{1,0:T(8,128)(2,1)S(1)}, u32[]{:S(2)}, u32[]{:S(2)}) collective-permute-start(bf16[304,256]{1,0:T(8,128)(2,1)S(1)} %pad_maximum_fusion.4), channel_id=1, source_target_pairs={{0,12},{4,8},{8,4},{12,0},{1,13},{5,9},{9,5},{13,1},{2,14},{6,10},... | collective-permute-start | bytes 466952 | tf_op jit(solution)/shard_map/ppermute | solution.py:169
  15.1 29.9 %collective-permute-start.1 = (bf16[304,256]{1,0:T(8,128)(2,1)S(1)}, bf16[304,256]{1,0:T(8,128)(2,1)S(1)}, u32[]{:S(2)}, u32[]{:S(2)}) collective-permute-start(bf16[304,256]{1,0:T(8,128)(2,1)S(1)} %pad_maximum_fusion.3), channel_id=1, source_target_pairs={{0,8},{4,12},{8,0},{12,4},{1,9},{5,13},{9,1},{13,5},{2,10},{6,14},... | collective-permute-start | bytes 466952 | tf_op jit(solution)/shard_map/ppermute | solution.py:169
  15.2 29.8 %collective-permute-start = (bf16[304,256]{1,0:T(8,128)(2,1)S(1)}, bf16[304,256]{1,0:T(8,128)(2,1)S(1)}, u32[]{:S(2)}, u32[]{:S(2)}) collective-permute-start(bf16[304,256]{1,0:T(8,128)(2,1)S(1)} %pad_maximum_fusion.2), channel_id=1, source_target_pairs={{0,4},{4,0},{8,12},{12,8},{1,5},{5,1},{9,13},{13,9},{2,6},{6,2},{1... | collective-permute-start | bytes 466952 | tf_op jit(solution)/shard_map/ppermute | solution.py:169
  17.3 42.6 %collective-permute-start.4 = (bf16[576,576]{1,0:T(8,128)(2,1)S(1)}, bf16[576,576]{1,0:T(8,128)(2,1)S(1)}, u32[]{:S(2)}, u32[]{:S(2)}) collective-permute-start(bf16[576,576]{1,0:T(8,128)(2,1)S(1)} %fusion.3), channel_id=1, source_target_pairs={{0,8},{4,12},{8,0},{12,4},{1,9},{5,13},{9,1},{13,5},{2,10},{6,14},... | collective-permute-start | bytes 1990664 | tf_op jit(solution)/shard_map/ppermute | solution.py:169
  19.7 5.4 %collective-permute-start.6 = (s32[256]{0:T(256)S(1)}, s32[256]{0:T(256)S(1)}, u32[]{:S(2)}, u32[]{:S(2)}) collective-permute-start(s32[256]{0:T(256)S(1)} %copy-done.13), channel_id=1, source_target_pairs={{0,16},{16,0},{1,17},{17,1},{2,18},{18,2},{3,19},{19,3},{4,20},{20... | collective-permute-start | bytes 3080 | tf_op jit(solution)/shard_map/ppermute | solution.py:169
  45.2 7.2 %collective-permute-start.3 = (bf16[4,144,256]{2,1,0:T(8,128)(2,1)S(1)}, bf16[4,144,256]{2,1,0:T(8,128)(2,1)S(1)}, u32[]{:S(2)}, u32[]{:S(2)}) collective-permute-start(bf16[4,144,256]{2,1,0:T(8,128)(2,1)S(1)} %slice.115), channel_id=1, source_target_pairs={{0,16},{16,0},{1,17},{17,1},{2,18},{18,2},{3,19},{19,3},{4,20},{20... | collective-permute-start | bytes 884744 | tf_op jit(solution)/shard_map/ppermute | solution.py:169
  60.8 30.6 %collective-permute-start.8 = (bf16[576,576]{1,0:T(8,128)(2,1)}, bf16[576,576]{1,0:T(8,128)(2,1)S(1)}, u32[]{:S(2)}, u32[]{:S(2)}) collective-permute-start(bf16[576,576]{1,0:T(8,128)(2,1)} %get-tuple-element.39), channel_id=1, source_target_pairs={{0,4},{4,0},{8,12},{12,8},{1,5},{5,1},{9,13},{13,9},{2,6},{6,2},{1... | collective-permute-start | bytes 1990664 | tf_op jit(solution)/shard_map/ppermute | solution.py:169
  60.9 34.2 %collective-permute-start.9 = (bf16[576,576]{1,0:T(8,128)(2,1)}, bf16[576,576]{1,0:T(8,128)(2,1)S(1)}, u32[]{:S(2)}, u32[]{:S(2)}) collective-permute-start(bf16[576,576]{1,0:T(8,128)(2,1)} %get-tuple-element.41), channel_id=1, source_target_pairs={{0,12},{4,8},{8,4},{12,0},{1,13},{5,9},{9,5},{13,1},{2,14},{6,10},... | collective-permute-start | bytes 1990664 | tf_op jit(solution)/shard_map/ppermute | solution.py:169
  91.1 5.4 %collective-permute-start.10 = (bf16[576,576]{1,0:T(8,128)(2,1)S(1)}, bf16[576,576]{1,0:T(8,128)(2,1)S(1)}, u32[]{:S(2)}, u32[]{:S(2)}) collective-permute-start(bf16[576,576]{1,0:T(8,128)(2,1)S(1)} %shard_map.112.refs_0_), channel_id=1, source_target_pairs={{0,1},{1,0},{2,3},{3,2},{4,5},{5,4},{6,7},{7,6},{8,9},{9,8},{10,11... | collective-permute-start | bytes 1990664 | tf_op jit(solution)/shard_map/ppermute | solution.py:169
  103.2 15.4 %collective-permute-start.14 = (bf16[256,1152]{1,0:T(8,128)(2,1)S(1)}, bf16[256,1152]{1,0:T(8,128)(2,1)S(1)}, u32[]{:S(2)}, u32[]{:S(2)}) collective-permute-start(bf16[256,1152]{1,0:T(8,128)(2,1)S(1)} %get-tuple-element.42.mine), channel_id=1, source_target_pairs={{0,2},{1,3},{2,0},{3,1},{4,6},{5,7},{6,4},{7,5},{8,10},{9,11},{10,... | collective-permute-start | bytes 1769480 | tf_op jit(solution)/shard_map/ppermute | solution.py:169
  124.3 14.6 %collective-permute-start.15 = (bf16[256,1152]{1,0:T(8,128)(2,1)S(1)}, bf16[256,1152]{1,0:T(8,128)(2,1)S(1)}, u32[]{:S(2)}, u32[]{:S(2)}) collective-permute-start(bf16[256,1152]{1,0:T(8,128)(2,1)S(1)} %get-tuple-element.44.mine), channel_id=1, source_target_pairs={{0,2},{1,3},{2,0},{3,1},{4,6},{5,7},{6,4},{7,5},{8,10},{9,11},{10,... | collective-permute-start | bytes 1769480 | tf_op jit(solution)/shard_map/ppermute | solution.py:169
  145.8 31.8 %collective-permute-start.17 = (bf16[576,512]{1,0:T(8,128)(2,1)S(1)}, bf16[576,512]{1,0:T(8,128)(2,1)S(1)}, u32[]{:S(2)}, u32[]{:S(2)}) collective-permute-start(bf16[576,512]{1,0:T(8,128)(2,1)S(1)} %maximum_select_fusion.own), channel_id=1, source_target_pairs={{12,0},{13,5},{14,10},{28,16},{29,21},{30,26}} | collective-permute-start | bytes 1769480 | tf_op jit(solution)/shard_map/ppermute | solution.py:678
  147.4 30.2 %collective-permute-start.18 = (f32[8,576]{1,0:T(8,128)S(1)}, f32[8,576]{1,0:T(8,128)S(1)}, u32[]{:S(2)}, u32[]{:S(2)}) collective-permute-start(f32[8,576]{1,0:T(8,128)S(1)} %convolution_multiply_fusion), channel_id=1, source_target_pairs={{4,0},{6,10},{7,15},{20,16},{22,26},{23,31}} | collective-permute-start | bytes 55304 | tf_op jit(solution)/shard_map/ppermute | solution.py:678
  177.7 22.9 %collective-permute-start.22 = (bf16[608,512]{1,0:T(8,128)(2,1)S(1)}, bf16[608,512]{1,0:T(8,128)(2,1)}, u32[]{:S(2)}, u32[]{:S(2)}) collective-permute-start(bf16[608,512]{1,0:T(8,128)(2,1)S(1)} %shard_map.119.refs_0_), channel_id=1, source_target_pairs={{0,16},{5,21},{10,26},{15,31},{16,0},{21,5},{26,10},{31,15}} | collective-permute-start | bytes 1867784 | tf_op jit(solution)/shard_map/ppermute | solution.py:711
  181.0 23.8 %collective-permute-start.20 = (bf16[608,512]{1,0:T(8,128)(2,1)S(1)}, bf16[608,512]{1,0:T(8,128)(2,1)}, u32[]{:S(2)}, u32[]{:S(2)}) collective-permute-start(bf16[608,512]{1,0:T(8,128)(2,1)S(1)} %shard_map.119.refs_0_), channel_id=1, source_target_pairs={{0,2},{5,7},{10,8},{15,13},{16,18},{21,23},{26,24},{31,29}} | collective-permute-start | bytes 1867784 | tf_op jit(solution)/shard_map/ppermute | solution.py:685
  200.6 9.3 %collective-permute-start.24 = (bf16[608,512]{1,0:T(8,128)(2,1)}, bf16[608,512]{1,0:T(8,128)(2,1)}, u32[]{:S(2)}, u32[]{:S(2)}) collective-permute-start(bf16[608,512]{1,0:T(8,128)(2,1)} %collective-permute-done.22.refs_4_), channel_id=1, source_target_pairs={{0,2},{5,7},{10,8},{15,13},{16,18},{21,23},{26,24},{31,29}} | collective-permute-start | bytes 1867784 | tf_op jit(solution)/shard_map/ppermute | solution.py:685
  202.7 28.7 %collective-permute-start.19 = (bf16[608,512]{1,0:T(8,128)(2,1)S(1)}, bf16[608,512]{1,0:T(8,128)(2,1)}, u32[]{:S(2)}, u32[]{:S(2)}) collective-permute-start(bf16[608,512]{1,0:T(8,128)(2,1)S(1)} %shard_map.119.refs_0_), channel_id=1, source_target_pairs={{0,1},{5,4},{10,11},{15,14},{16,17},{21,20},{26,27},{31,30}} | collective-permute-start | bytes 1867784 | tf_op jit(solution)/shard_map/ppermute | solution.py:688
  204.8 28.1 %collective-permute-start.21 = (bf16[608,512]{1,0:T(8,128)(2,1)}, bf16[608,512]{1,0:T(8,128)(2,1)}, u32[]{:S(2)}, u32[]{:S(2)}) collective-permute-start(bf16[608,512]{1,0:T(8,128)(2,1)} %collective-permute-done.20.refs_2_), channel_id=1, source_target_pairs={{2,3},{7,6},{8,9},{13,12},{18,19},{23,22},{24,25},{29,28}} | collective-permute-start | bytes 1867784 | tf_op jit(solution)/shard_map/ppermute | solution.py:691
  206.3 27.8 %collective-permute-start.23 = (bf16[608,512]{1,0:T(8,128)(2,1)}, bf16[608,512]{1,0:T(8,128)(2,1)S(1)}, u32[]{:S(2)}, u32[]{:S(2)}) collective-permute-start(bf16[608,512]{1,0:T(8,128)(2,1)} %collective-permute-done.22.refs_4_), channel_id=1, source_target_pairs={{0,1},{5,4},{10,11},{15,14},{16,17},{21,20},{26,27},{31,30}} | collective-permute-start | bytes 1867784 | tf_op jit(solution)/shard_map/ppermute | solution.py:688
  209.9 24.2 %collective-permute-start.25 = (bf16[608,512]{1,0:T(8,128)(2,1)}, bf16[608,512]{1,0:T(8,128)(2,1)S(1)}, u32[]{:S(2)}, u32[]{:S(2)}) collective-permute-start(bf16[608,512]{1,0:T(8,128)(2,1)} %collective-permute-done.24.refs_6_), channel_id=1, source_target_pairs={{2,3},{7,6},{8,9},{13,12},{18,19},{23,22},{24,25},{29,28}} | collective-permute-start | bytes 1867784 | tf_op jit(solution)/shard_map/ppermute | solution.py:691
  230.7 16.4 %collective-permute-start.28 = (bf16[3,192,512]{2,1,0:T(8,128)(2,1)S(1)}, bf16[3,192,512]{2,1,0:T(8,128)(2,1)}, u32[]{:S(2)}, u32[]{:S(2)}) collective-permute-start(bf16[3,192,512]{2,1,0:T(8,128)(2,1)S(1)} %bitcast.97), channel_id=1, source_target_pairs={{0,16},{16,0},{1,17},{17,1},{2,18},{18,2},{3,19},{19,3},{4,20},{20... | collective-permute-start | bytes 1769480 | tf_op jit(solution)/shard_map/ppermute | solution.py:169
  231.4 28.2 %collective-permute-start.26 = (bf16[3,192,512]{2,1,0:T(8,128)(2,1)S(1)}, bf16[3,192,512]{2,1,0:T(8,128)(2,1)S(1)}, u32[]{:S(2)}, u32[]{:S(2)}) collective-permute-start(bf16[3,192,512]{2,1,0:T(8,128)(2,1)S(1)} %slice.95), channel_id=1, source_target_pairs={{0,16},{16,0},{1,17},{17,1},{2,18},{18,2},{3,19},{19,3},{4,20},{20... | collective-permute-start | bytes 1769480 | tf_op jit(solution)/shard_map/ppermute | solution.py:169
  233.0 33.9 %collective-permute-start.27 = (bf16[3,192,512]{2,1,0:T(8,128)(2,1)S(1)}, bf16[3,192,512]{2,1,0:T(8,128)(2,1)S(1)}, u32[]{:S(2)}, u32[]{:S(2)}) collective-permute-start(bf16[3,192,512]{2,1,0:T(8,128)(2,1)S(1)} %slice.96), channel_id=1, source_target_pairs={{0,16},{16,0},{1,17},{17,1},{2,18},{18,2},{3,19},{19,3},{4,20},{20... | collective-permute-start | bytes 1769480 | tf_op jit(solution)/shard_map/ppermute | solution.py:169
  (22 other events, 266.6 us)
Sparse Core Ops, SparseCore 0:
  60.9 24.9 all-gather.5

commit v11 on v8

--- a/solution.py
+++ b/solution.py
@@ -187,21 +187,24 @@
     return pltpu.CompilerParams(vmem_limit_bytes=40 * 1024 * 1024)
 
 
-def layout_kernel(place_ref, gathered, features, rows, low_diag, trace, old, *, weight):
-    own_place, layer, core = place_ref[0], place_ref[1], place_ref[2]
-    sections, steps, _, tokens = gathered.shape
+def layout_kernel(place_ref, *refs, weight):
+    gathered, (features, rows, low_diag, trace, old) = refs[:4], refs[4:]
+    own_place, layer, core, here = (place_ref[index] for index in range(4))
+    steps, _, tokens = gathered[0].shape
+    sections = len(gathered)
     groups, depth, _ = features.shape
     part = depth // (sections * steps)
     width = depth // steps
-    for section in range(sections):
+    for away in range(sections):
+        section = here ^ away
         codes = jnp.zeros((16, tokens), jnp.float32)
         for step in range(steps):
-            start = (step * sections + section) * part
+            start = pl.multiple_of((step * sections + section) * part, 16)
             for group in range(groups):
-                features[group, start : start + part] = gathered[
-                    section, step, group * part : (group + 1) * part
+                features[group, pl.ds(start, part)] = gathered[away][
+                    step, group * part : (group + 1) * part
                 ]
-            codes += gathered[section, step, groups * part :].astype(jnp.float32)
+            codes += gathered[away][step, groups * part :].astype(jnp.float32)
         codes = codes[0:3] + codes[3:6] + codes[6:9]
         pieces = [codes[0:1], codes[1:2], codes[2:3, : width - 2 * tokens]]
         old[section ^ layer] = jnp.concatenate(pieces, axis=1)
@@ -228,7 +231,8 @@
 
 
 def lay_out(places, gathered, weight):
-    sections, steps, height, tokens = gathered.shape
+    steps, height, tokens = gathered[0].shape
+    sections = len(gathered)
     part = (height - 16) // 2
     depth = sections * steps * part
     width = depth // steps
@@ -236,7 +240,7 @@
     smem = pl.BlockSpec(memory_space=pltpu.SMEM)
     return pl.pallas_call(
         functools.partial(layout_kernel, weight=weight),
-        in_specs=[smem, vmem],
+        in_specs=[smem] + [vmem] * sections,
         out_specs=[vmem, vmem, vmem, smem],
         out_shape=[
             jax.ShapeDtypeStruct((2, depth, tokens), jnp.bfloat16),
@@ -249,7 +253,7 @@
         cost_estimate=pl.CostEstimate(
             flops=64 * depth * tokens, bytes_accessed=14 * depth * tokens, transcendentals=0
         ),
-    )(places, gathered)
+    )(places, *gathered)
 
 
 def factor_kernel(place_ref, part, own, old, diag, out, *, step, weight):
@@ -308,14 +312,9 @@
     return copies
 
 
-def block_products(rows, copies, held):
-    count = len(copies) // 2
-    products = []
-    for index in range(2):
-        for copy in copies[index * count : (index + 1) * count]:
-            copy.wait()
-        products.append(jnp.dot(rows, held[index], preferred_element_type=jnp.float32))
-    return products
+def block_products(mine, theirs, held):
+    rows = jnp.concatenate([mine[...], theirs[...]], axis=1)
+    return [jnp.dot(rows, held[index], preferred_element_type=jnp.float32) for index in range(2)]
 
 
 def first_parts(place_ref, scale, rows, diag, product, index):
@@ -330,9 +329,13 @@
 
 
 def first_kernel(place_ref, scale_ref, rows, diag, *refs):
-    blocks, (kept, message), (held, sems) = refs[:8], refs[8:10], refs[10:]
+    blocks, (kept, message, held, sems) = refs[:8], refs[8:]
     copies = fetch_blocks(place_ref, blocks, held, sems)
-    products = block_products(rows[...], copies, held)
+    products = []
+    for index in range(2):
+        for copy in copies[index * 4 : (index + 1) * 4]:
+            copy.wait()
+        products.append(jnp.dot(rows[...], held[index], preferred_element_type=jnp.float32))
     lows = []
     for index in range(2):
         kept[index] = products[index]
@@ -341,11 +344,10 @@
     message[...] = jnp.concatenate(lows, axis=1)
 
 
-def second_kernel(place_ref, scale_ref, mine, theirs, rows, diag, before, *refs):
-    blocks, (kept, message), (held, sems) = refs[:8], refs[8:10], refs[10:]
-    copies = fetch_blocks(place_ref, blocks, held, sems)
-    both = jnp.concatenate([mine[...], theirs[...]], axis=1)
-    products = block_products(both, copies, held)
+def second_kernel(
+    place_ref, scale_ref, mine, theirs, rows, diag, before, held, kept, message
+):
+    products = block_products(mine, theirs, held)
     square = scale_ref[0] * scale_ref[0]
     lows = []
     for index in range(2):
@@ -361,21 +363,17 @@
     message[...] = jnp.concatenate(lows, axis=1)
 
 
-def third_kernel(place_ref, scale_ref, mine, theirs, before, *refs):
-    blocks, (keep, give), (held, sems) = refs[:8], refs[8:10], refs[10:]
-    copies = fetch_blocks(place_ref, blocks, held, sems)
-    both = jnp.concatenate([mine[...], theirs[...]], axis=1)
-    products = block_products(both, copies, held)
+def third_kernel(place_ref, scale_ref, mine, theirs, before, held, keep, give):
+    products = block_products(mine, theirs, held)
     square = scale_ref[0] * scale_ref[0]
     for index, out in ((0, keep), (1, give)):
         out[...] = (before[index] + square * products[index]).T.astype(jnp.bfloat16)
 
 
 def chain_call(kernel, scalars, arrays, blocks, out_shape):
-    depth, width = blocks[0].shape
-    count = len(blocks) // 2
     tokens = arrays[0].shape[0]
     vmem = pl.BlockSpec(memory_space=pltpu.VMEM)
+    scratch = [pltpu.SemaphoreType.DMA((len(blocks),))] if blocks else []
     return pl.pallas_call(
         kernel,
         in_specs=[pl.BlockSpec(memory_space=pltpu.SMEM)] * len(scalars)
@@ -383,15 +381,10 @@
         + [pl.BlockSpec(memory_space=pl.ANY)] * len(blocks),
         out_specs=[vmem] * len(out_shape),
         out_shape=out_shape,
-        scratch_shapes=[
-            pltpu.VMEM((2, count * depth, width), jnp.bfloat16),
-            pltpu.SemaphoreType.DMA((len(blocks),)),
-        ],
+        scratch_shapes=scratch,
         compiler_params=params(),
         cost_estimate=pl.CostEstimate(
-            flops=2 * len(blocks) * tokens * depth * width,
-            bytes_accessed=2 * len(blocks) * depth * width,
-            transcendentals=0,
+            flops=2 * tokens * D * D, bytes_accessed=2 * D * D, transcendentals=0
         ),
     )(*scalars, *arrays, *blocks)
 
@@ -490,7 +483,7 @@
             pltpu.SemaphoreType.DMA((8,)),
             pltpu.SemaphoreType.DMA((8,)),
         ],
-        compiler_params=params(),
+        compiler_params=pltpu.CompilerParams(vmem_limit_bytes=60 * 1024 * 1024),
         cost_estimate=pl.CostEstimate(
             flops=2 * cols * tokens_all * (4 * cols + vocab_block),
             bytes_accessed=4 * cols * (4 * cols + vocab_block) + 14 * cols * tokens_all,
@@ -583,36 +576,43 @@
 
     part_rows = row_block // 2
 
-    def old_block(factors, step, start, size):
-        away = by_index(factors, held_by(layer ^ step))[start : start + size]
-        return away.astype(jnp.bfloat16)
-
-    early = swap(old_block(old_factors, 2, 0, part_rows), "tensor", n_tensor, 2)
+    def old_block(factors, step):
+        return by_index(factors, held_by(layer ^ step)).astype(jnp.bfloat16)
+
+    early = swap(old_block(old_factors, 2), "tensor", n_tensor, 2)
     later_factors = lax.optimization_barrier(old_factors)
-    late = old_block(later_factors, 2, part_rows, part_rows)
-    blocks = [old_block(later_factors, step, 0, row_block) for step in (0, 1, 3)]
-    other_tokens, collected, early, late, blocks, small = lax.optimization_barrier(
-        (other_tokens, collected, early, late, blocks, (router_right, matches, embed_scale, norm_sums))
+    far_block = old_block(later_factors, 3)
+    early_far = swap(far_block[:part_rows], "tensor", n_tensor, 3)
+    blocks = [old_block(later_factors, 0), old_block(later_factors, 1), far_block[part_rows:]]
+    other_tokens, collected, early, early_far, blocks, small = lax.optimization_barrier(
+        (
+            other_tokens,
+            collected,
+            early,
+            early_far,
+            blocks,
+            (router_right, matches, embed_scale, norm_sums),
+        )
     )
     router_right, matches, embed_scale, norm_sums = small
     collected = jnp.concatenate(
         [collected[:, :features_dev], other_tokens, collected[:, 2 * features_dev :]], axis=1
     )
-    gathered = lax.all_gather(collected, "section", axis=0)
-    late = swap(late, "tensor", n_tensor, 2)
-    blocks = [
-        blocks[0],
-        swap(blocks[1], "tensor", n_tensor, 1),
-        None,
-        swap(blocks[2], "tensor", n_tensor, 3),
-    ]
+    by_side = swap(collected, "section", n_section, 2)
+    by_core = swap(collected, "section", n_section, 1)
+    late_far = swap(blocks[2], "tensor", n_tensor, 3)
+    blocks = [blocks[0], swap(blocks[1], "tensor", n_tensor, 1), early]
+    by_side, late_far, blocks[1] = lax.optimization_barrier((by_side, late_far, blocks[1]))
+    by_both = swap(by_side, "section", n_section, 1)
 
     features, rows, low_diag, trace = lay_out(
-        jnp.stack([own_place, layer, core]), gathered, weight
+        jnp.stack([own_place, layer, core, section]),
+        (collected, by_core, by_side, by_both),
+        weight,
     )
     scale = D / (3.0 * trace)
-    early, features = lax.optimization_barrier((early, features))
-    blocks[2] = jnp.concatenate([early, late], axis=0)
+    early_far, features = lax.optimization_barrier((early_far, features))
+    blocks.append(jnp.concatenate([early_far, late_far], axis=0))
 
     own_cols = [
         factor_block(place, features, blocks[step], low_diag, step, weight)
@@ -625,13 +625,18 @@
     sent = jax.ShapeDtypeStruct((tokens, 2 * col_block), jnp.bfloat16)
     part = jax.ShapeDtypeStruct((col_block, tokens), jnp.bfloat16)
     scalars = (place, scale)
-    kept, message = chain_call(first_kernel, scalars, (rows, low_diag), cols, (wide, sent))
+    columns = jax.ShapeDtypeStruct((2, D, col_block), jnp.bfloat16)
+    kept, message, held = chain_call(
+        first_kernel, scalars, (rows, low_diag), cols, (wide, sent, columns)
+    )
     theirs = swap(message, "section", n_section, 2)
     kept, message = chain_call(
-        second_kernel, scalars, (message, theirs, rows, low_diag, kept), cols, (wide, sent)
+        second_kernel, scalars, (message, theirs, rows, low_diag, kept, held), (), (wide, sent)
     )
     theirs = swap(message, "section", n_section, 2)
-    keep, give = chain_call(third_kernel, scalars, (message, theirs, kept), cols, (part, part))
+    keep, give = chain_call(
+        third_kernel, scalars, (message, theirs, kept, held), (), (part, part)
+    )
     got = swap(give, "section", n_section, 1)
     own = jnp.where(
         core == shard, jnp.concatenate([keep, got], axis=1), jnp.concatenate([got, keep], axis=1)
@@ -693,7 +698,7 @@
     near_2 = send(own, 2, 0)
     over_0 = across(own, 0)
     left_here = scatter(own, 2)
-    near_1, over_0, own = lax.optimization_barrier((near_1, over_0, own))
+    near_1, own = lax.optimization_barrier((near_1, own))
     over_1 = across(near_1, 1)
     router_cols = learning_rate * jnp.einsum(
         "fn,cn->fc", router_right, own, preferred_element_type=jnp.float32
@@ -703,7 +708,9 @@
     codes = jnp.concatenate([router_high, router_cols - router_high], axis=0).astype(jnp.bfloat16)
     codes_tail = jnp.pad(codes[:, tokens_all:], ((0, 0), (0, 2 * tokens_all - col_block)))
     left_here = jnp.concatenate([left_here, codes[:, :tokens_all], codes_tail], axis=0)
-    left_here, near_2, over_1 = lax.optimization_barrier((left_here, near_2, over_1))
+    left_here, near_2, over_0, over_1 = lax.optimization_barrier(
+        (left_here, near_2, over_0, over_1)
+    )
     near_3 = send(near_2, 1, 2)
     over_2 = across(near_2, 2)
     left_there = lax.ppermute(

time: 257 us -> 243 us (0.946)
  the two profiles are of different devices: /device:TPU:0 before, /device:TPU:29 now
where the time goes in v11:
time: 243 us; the launch traced here: 242 us
  waiting for transfers between devices  128 us (53%)
  starting transfers between devices  60.2 us (25%)
  Pallas kernels  26.5 us (11%)
  local copies, waits for them, and re-layouts  12 us (5%)
  other arithmetic  11.2 us (5%)
  between operations  3.06 us (1%)
    ppermute x21, waiting for transfers between devices, swap(): return lax.ppermute(value, axis, [(i, i ^ step) for i in range(size)])  85.2 us
    ppermute x21, starting transfers between devices, swap(): return lax.ppermute(value, axis, [(i, i ^ step) for i in range(size)])  28 us
    ppermute x2, waiting for transfers between devices, scatter(): lax.ppermute(value, everywhere, [(spot(x, source, s), spot(x, s, s)) for...  16.8 us
    ppermute x3, waiting for transfers between devices, send(): return lax.ppermute(value, axes, moves)  14.6 us
    pallas_call x3, Pallas kernels, chain_call(): pl.pallas_call(kernel, in_specs=[pl.BlockSpec(memory_space=pltpu.SMEM)] *...  12.6 us
    ppermute x4, waiting for transfers between devices, across(): return lax.ppermute(value, axes, moves)  11.6 us
    ppermute x4, starting transfers between devices, across(): return lax.ppermute(value, axes, moves)  9.5 us
    pallas_call x1, Pallas kernels, output_products(): pl.pallas_call(output_kernel, in_specs=[pl.BlockSpec(memory_space=pltpu.S...  7.86 us
  transfers between devices with their start and end apart: 37, of which 19 were waited for; matrix products, arithmetic and copies ran while one was open for 6% of the time, Pallas kernels for 0%

profile of v11, /device:TPU:29, one launch (start us, length us, event | category | flops | bytes accessed | tf_op | source)
XLA Modules:
  0.0 242.0 jit_solution(14646715186381020478)
XLA Ops:
  10.1 3.4 %fusion.5 = (bf16[576,576]{1,0:T(8,128)(2,1)}, bf16[576,576]{1,0:T(8,128)(2,1)S(1)}, bf16[1,576,576]{2,1,0:T(8,128)(2,1)S(1)}) fusion(f32[4,576,576]{2,1,0:T(8,128)} %param.12, s32[]{:T(128)S(6)} %select_n.158, s32[]{:T(128)S(6)} %select_n.154, s32[]{:T(128)S(6)} %select_n.166), kind=kLoop, calls=%fused_computation.17 | loop fusion | bytes 3981324 | tf_op jit(solution)/shard_map/convert_element_type | solution.py:580
  24.9 17.2 %collective-permute-done.1 = bf16[304,256]{1,0:T(8,128)(2,1)} collective-permute-done((bf16[304,256]{1,0:T(8,128)(2,1)S(1)}, bf16[304,256]{1,0:T(8,128)(2,1)}, u32[]{:S(2)}, u32[]{:S(2)}) %collective-permute-start.1) | collective-permute-done | bytes 155680 | tf_op jit(solution)/shard_map/ppermute | solution.py:169
  45.6 4.4 %collective-permute-done.3 = bf16[4,144,256]{2,1,0:T(8,128)(2,1)} collective-permute-done((bf16[4,144,256]{2,1,0:T(8,128)(2,1)}, bf16[4,144,256]{2,1,0:T(8,128)(2,1)}, u32[]{:S(2)}, u32[]{:S(2)}) %collective-permute-start.3) | collective-permute-done | bytes 294944 | tf_op jit(solution)/shard_map/ppermute | solution.py:169
  50.0 7.8 %collective-permute-done.4.old = bf16[576,576]{1,0:T(8,128)(2,1)S(1)} collective-permute-done((bf16[576,576]{1,0:T(8,128)(2,1)S(1)}, bf16[576,576]{1,0:T(8,128)(2,1)S(1)}, u32[]{:S(2)}, u32[]{:S(2)}) %collective-permute-start.4) | collective-permute-done | bytes 663584 | tf_op jit(solution)/shard_map/ppermute | solution.py:169
  57.8 8.3 %collective-permute-start.12 = (bf16[576,576]{1,0:T(8,128)(2,1)}, bf16[576,576]{1,0:T(8,128)(2,1)S(1)}, u32[]{:S(2)}, u32[]{:S(2)}) collective-permute-start(bf16[576,576]{1,0:T(8,128)(2,1)} %get-tuple-element.49), channel_id=1, source_target_pairs={{0,4},{4,0},{8,12},{12,8},{1,5},{5,1},{9,13},{13,9},{2,6},{6,2},{1... | collective-permute-start | bytes 1990664 | tf_op jit(solution)/shard_map/ppermute | solution.py:169
  70.9 19.8 %collective-permute-done.11 = bf16[288,576]{1,0:T(8,128)(2,1)S(1)} collective-permute-done((bf16[288,576]{1,0:T(8,128)(2,1)S(1)}, bf16[288,576]{1,0:T(8,128)(2,1)S(1)}, u32[]{:S(2)}, u32[]{:S(2)}) %collective-permute-start.11) | collective-permute-done | bytes 331808 | tf_op jit(solution)/shard_map/ppermute | solution.py:169
  91.4 2.3 collective-permute-start.13
  95.5 3.6 %shard_map.111 = (bf16[2,2304,256]{2,1,0:T(8,128)(2,1)S(1)}, bf16[256,2304]{1,0:T(8,128)(2,1)S(1)}, f32[4,1,576]{2,1,0:T(1,128)S(1)}, f32[1]{0:T(128)}) custom-call(s32[4]{0:T(128)S(1)} %pad_add_fusion.1.place_ref, bf16[4,304,256]{2,1,0:T(8,128)(2,1)S(1)} %pad_maximum_fusion.2.refs_0_, bf16[4,304,256]{2,1,0:T(8,128)(2,1)} %collective-permute-done.9.refs_1_, ...), custom_call_target="tpu_custom_call" | custom-call | flops 37748736 | bytes 8257536 | tf_op jit(solution)/shard_map/pallas_call | solution.py:241
  107.6 7.7 %shard_map.116 = (f32[2,256,576]{2,1,0:T(8,128)S(1)}, bf16[256,1152]{1,0:T(8,128)(2,1)S(1)}, bf16[2,2304,576]{2,1,0:T(8,128)(2,1)}) custom-call(s32[1]{0:T(128)} %bitcast.2.place_ref, f32[1]{0:T(128)S(6)} %div.22.scale_ref, bf16[256,2304]{1,0:T(8,128)(2,1)S(1)} %get-tuple-element.52.rows, f32[4,1,576]{2,1,0:T(1,128)S(1)} %get-tuple-element.53.diag, ...), custom_call_target="tpu_custom_call" | custom-call | flops 2717908992 | bytes 10616832 | tf_op jit(solution)/shard_map/pallas_call | solution.py:377
  115.5 14.3 %collective-permute-done.18.theirs = bf16[256,1152]{1,0:T(8,128)(2,1)S(1)} collective-permute-done((bf16[256,1152]{1,0:T(8,128)(2,1)S(1)}, bf16[256,1152]{1,0:T(8,128)(2,1)S(1)}, u32[]{:S(2)}, u32[]{:S(2)}) %collective-permute-start.18) | collective-permute-done | bytes 589856 | tf_op jit(solution)/shard_map/ppermute | solution.py:169
  129.8 2.7 %copy-done = bf16[2,2304,576]{2,1,0:T(8,128)(2,1)S(1)} copy-done((bf16[2,2304,576]{2,1,0:T(8,128)(2,1)S(1)}, bf16[2,2304,576]{2,1,0:T(8,128)(2,1)}, u32[]{:S(2)}) %copy-start) | copy-done | bytes 5308440
  132.5 2.8 %shard_map.117 = (f32[2,256,576]{2,1,0:T(8,128)S(1)}, bf16[256,1152]{1,0:T(8,128)(2,1)S(1)}) custom-call(s32[1]{0:T(128)} %bitcast.2.place_ref, f32[1]{0:T(128)S(6)} %div.22.scale_ref, bf16[256,1152]{1,0:T(8,128)(2,1)S(1)} %get-tuple-element.62.mine, bf16[256,1152]{1,0:T(8,128)(2,1)S(1)} %collective-permute-done.18.theirs, ...), custom_call_target="tpu_custom_call" | custom-call | flops 2717908992 | bytes 10616832 | tf_op jit(solution)/shard_map/pallas_call | solution.py:377
  135.6 13.4 %collective-permute-done.19.theirs = bf16[256,1152]{1,0:T(8,128)(2,1)S(1)} collective-permute-done((bf16[256,1152]{1,0:T(8,128)(2,1)S(1)}, bf16[256,1152]{1,0:T(8,128)(2,1)S(1)}, u32[]{:S(2)}, u32[]{:S(2)}) %collective-permute-start.19) | collective-permute-done | bytes 589856 | tf_op jit(solution)/shard_map/ppermute | solution.py:169
  157.3 4.2 %collective-permute-start.24 = (bf16[576,512]{1,0:T(8,128)(2,1)S(1)}, bf16[576,512]{1,0:T(8,128)(2,1)S(1)}, u32[]{:S(2)}, u32[]{:S(2)}) collective-permute-start(bf16[576,512]{1,0:T(8,128)(2,1)S(1)} %maximum_select_fusion.refs_8_), channel_id=1, source_target_pairs={{0,8},{4,12},{12,4},{16,24},{28,20},{1,9},{5,13},{13,5},{17,25},{2... | collective-permute-start | bytes 1769480 | tf_op jit(solution)/shard_map/ppermute | solution.py:658
  163.4 5.2 %collective-permute-done.22.refs_9_ = bf16[576,512]{1,0:T(8,128)(2,1)S(1)} collective-permute-done((bf16[576,512]{1,0:T(8,128)(2,1)S(1)}, bf16[576,512]{1,0:T(8,128)(2,1)S(1)}, u32[]{:S(2)}, u32[]{:S(2)}) %collective-permute-start.22) | collective-permute-done | bytes 589856 | tf_op jit(solution)/shard_map/ppermute | solution.py:658
  171.0 5.6 %collective-permute-done.21 = bf16[576,512]{1,0:T(8,128)(2,1)S(1)} collective-permute-done((bf16[576,512]{1,0:T(8,128)(2,1)S(1)}, bf16[576,512]{1,0:T(8,128)(2,1)S(1)}, u32[]{:S(2)}, u32[]{:S(2)}) %collective-permute-start.21) | collective-permute-done | bytes 589856 | tf_op jit(solution)/shard_map/ppermute | solution.py:675
  176.7 11.1 %collective-permute-done.23 = f32[8,576]{1,0:T(8,128)S(1)} collective-permute-done((f32[8,576]{1,0:T(8,128)S(1)}, f32[8,576]{1,0:T(8,128)S(1)}, u32[]{:S(2)}, u32[]{:S(2)}) %collective-permute-start.23) | collective-permute-done | bytes 18464 | tf_op jit(solution)/shard_map/ppermute | solution.py:675
  191.8 2.8 %collective-permute-start.32 = (bf16[576,512]{1,0:T(8,128)(2,1)S(1)}, bf16[576,512]{1,0:T(8,128)(2,1)S(1)}, u32[]{:S(2)}, u32[]{:S(2)}) collective-permute-start(bf16[576,512]{1,0:T(8,128)(2,1)S(1)} %collective-permute-done.24.refs_10_), channel_id=1, source_target_pairs={{4,20},{8,24},{12,28},{20,4},{24,8},{5,21},{9,25},{13,29},{21,5},{... | collective-permute-start | bytes 1769480 | tf_op jit(solution)/shard_map/ppermute | solution.py:667
  196.0 9.4 %collective-permute-done.31.refs_11_ = bf16[576,512]{1,0:T(8,128)(2,1)S(1)} collective-permute-done((bf16[576,512]{1,0:T(8,128)(2,1)S(1)}, bf16[576,512]{1,0:T(8,128)(2,1)S(1)}, u32[]{:S(2)}, u32[]{:S(2)}) %collective-permute-start.31) | collective-permute-done | bytes 589856 | tf_op jit(solution)/shard_map/ppermute | solution.py:658
  205.4 4.3 %collective-permute-done.32.refs_14_ = bf16[576,512]{1,0:T(8,128)(2,1)S(1)} collective-permute-done((bf16[576,512]{1,0:T(8,128)(2,1)S(1)}, bf16[576,512]{1,0:T(8,128)(2,1)S(1)}, u32[]{:S(2)}, u32[]{:S(2)}) %collective-permute-start.32) | collective-permute-done | bytes 589856 | tf_op jit(solution)/shard_map/ppermute | solution.py:667
  211.0 4.1 %collective-permute-start.35 = (bf16[576,512]{1,0:T(8,128)(2,1)S(1)}, bf16[576,512]{1,0:T(8,128)(2,1)S(1)}, u32[]{:S(2)}, u32[]{:S(2)}) collective-permute-start(bf16[576,512]{1,0:T(8,128)(2,1)S(1)} %collective-permute-done.31.refs_11_), channel_id=1, source_target_pairs={{0,16},{8,24},{12,28},{16,0},{28,12},{1,17},{9,25},{13,29},{17,1},... | collective-permute-start | bytes 1769480 | tf_op jit(solution)/shard_map/ppermute | solution.py:667
  215.1 2.8 %collective-permute-start.27 = (bf16[608,512]{1,0:T(8,128)(2,1)S(1)}, bf16[608,512]{1,0:T(8,128)(2,1)}, u32[]{:S(2)}, u32[]{:S(2)}) collective-permute-start(bf16[608,512]{1,0:T(8,128)(2,1)S(1)} %pad_maximum_fusion.3.refs_0_), channel_id=1, source_target_pairs={{0,1},{5,4},{10,11},{15,14},{16,17},{21,20},{26,27},{31,30}} | collective-permute-start | bytes 1867784 | tf_op jit(solution)/shard_map/ppermute | solution.py:687
  221.6 7.4 %collective-permute-done.35.refs_15_ = bf16[576,512]{1,0:T(8,128)(2,1)S(1)} collective-permute-done((bf16[576,512]{1,0:T(8,128)(2,1)S(1)}, bf16[576,512]{1,0:T(8,128)(2,1)S(1)}, u32[]{:S(2)}, u32[]{:S(2)}) %collective-permute-start.35) | collective-permute-done | bytes 589856 | tf_op jit(solution)/shard_map/ppermute | solution.py:667
  233.9 7.9 %shard_map.119 = (f32[4,576,576]{2,1,0:T(8,128)}, f32[576,2048]{1,0:T(8,128)}) custom-call(s32[3]{0:T(128)} %pad_add_fusion.where_ref, f32[1,2048]{1,0:T(1,128)} %bitcast.89, bf16[512,2048]{1,0:T(8,128)(2,1)} %compare_convert_fusion.matches, bf16[608,512]{1,0:T(8,128)(2,1)} %copy-done.3, bf16[608,512]{1,0:T(8,128)(2,1)} %collective-permute-done.27.refs_1_, ...), custom_call_target="tpu_custom_call" | custom-call | flops 2566914048 | bytes 14155776 | tf_op jit(solution)/shard_map/pallas_call | solution.py:465
  (168 shorter events, 66.7 us)
Async XLA Ops:
  3.5 21.4 %collective-permute-start.2 = (bf16[304,256]{1,0:T(8,128)(2,1)S(1)}, bf16[304,256]{1,0:T(8,128)(2,1)S(1)}, u32[]{:S(2)}, u32[]{:S(2)}) collective-permute-start(bf16[304,256]{1,0:T(8,128)(2,1)S(1)} %pad_maximum_fusion.6), channel_id=1, source_target_pairs={{0,12},{4,8},{8,4},{12,0},{1,13},{5,9},{9,5},{13,1},{2,14},{6,10},... | collective-permute-start | bytes 466952 | tf_op jit(solution)/shard_map/ppermute | solution.py:169
  3.6 38.6 %collective-permute-start.1 = (bf16[304,256]{1,0:T(8,128)(2,1)S(1)}, bf16[304,256]{1,0:T(8,128)(2,1)}, u32[]{:S(2)}, u32[]{:S(2)}) collective-permute-start(bf16[304,256]{1,0:T(8,128)(2,1)S(1)} %pad_maximum_fusion.5), channel_id=1, source_target_pairs={{0,8},{4,12},{8,0},{12,4},{1,9},{5,13},{9,1},{13,5},{2,10},{6,14},... | collective-permute-start | bytes 466952 | tf_op jit(solution)/shard_map/ppermute | solution.py:169
  5.0 37.1 %collective-permute-start = (bf16[304,256]{1,0:T(8,128)(2,1)S(1)}, bf16[304,256]{1,0:T(8,128)(2,1)}, u32[]{:S(2)}, u32[]{:S(2)}) collective-permute-start(bf16[304,256]{1,0:T(8,128)(2,1)S(1)} %pad_maximum_fusion.4), channel_id=1, source_target_pairs={{0,4},{4,0},{8,12},{12,8},{1,5},{5,1},{9,13},{13,9},{2,6},{6,2},{1... | collective-permute-start | bytes 466952 | tf_op jit(solution)/shard_map/ppermute | solution.py:169
  8.7 49.1 %collective-permute-start.4 = (bf16[576,576]{1,0:T(8,128)(2,1)S(1)}, bf16[576,576]{1,0:T(8,128)(2,1)S(1)}, u32[]{:S(2)}, u32[]{:S(2)}) collective-permute-start(bf16[576,576]{1,0:T(8,128)(2,1)S(1)} %fusion.3), channel_id=1, source_target_pairs={{0,8},{4,12},{8,0},{12,4},{1,9},{5,13},{9,1},{13,5},{2,10},{6,14},... | collective-permute-start | bytes 1990664 | tf_op jit(solution)/shard_map/ppermute | solution.py:169
  20.7 24.9 %collective-permute-start.5 = (bf16[288,576]{1,0:T(8,128)(2,1)}, bf16[288,576]{1,0:T(8,128)(2,1)S(1)}, u32[]{:S(2)}, u32[]{:S(2)}) collective-permute-start(bf16[288,576]{1,0:T(8,128)(2,1)} %get-tuple-element.94), channel_id=1, source_target_pairs={{0,12},{4,8},{8,4},{12,0},{1,13},{5,9},{9,5},{13,1},{2,14},{6,10},... | collective-permute-start | bytes 995336 | tf_op jit(solution)/shard_map/ppermute | solution.py:169
  57.8 32.8 %collective-permute-start.12 = (bf16[576,576]{1,0:T(8,128)(2,1)}, bf16[576,576]{1,0:T(8,128)(2,1)S(1)}, u32[]{:S(2)}, u32[]{:S(2)}) collective-permute-start(bf16[576,576]{1,0:T(8,128)(2,1)} %get-tuple-element.49), channel_id=1, source_target_pairs={{0,4},{4,0},{8,12},{12,8},{1,5},{5,1},{9,13},{13,9},{2,6},{6,2},{1... | collective-permute-start | bytes 1990664 | tf_op jit(solution)/shard_map/ppermute | solution.py:169
  67.1 23.5 %collective-permute-start.10 = (bf16[4,304,256]{2,1,0:T(8,128)(2,1)S(1)}, bf16[4,304,256]{2,1,0:T(8,128)(2,1)S(1)}, u32[]{:S(2)}, u32[]{:S(2)}) collective-permute-start(bf16[4,304,256]{2,1,0:T(8,128)(2,1)S(1)} %pad_maximum_fusion.2.refs_0_), channel_id=1, source_target_pairs={{0,2},{1,3},{2,0},{3,1},{4,6},{5,7},{6,4},{7,5},{8,10},{9,11},{10,... | collective-permute-start | bytes 1867784 | tf_op jit(solution)/shard_map/ppermute | solution.py:169
  67.4 23.2 %collective-permute-start.11 = (bf16[288,576]{1,0:T(8,128)(2,1)S(1)}, bf16[288,576]{1,0:T(8,128)(2,1)S(1)}, u32[]{:S(2)}, u32[]{:S(2)}) collective-permute-start(bf16[288,576]{1,0:T(8,128)(2,1)S(1)} %copy-done.17), channel_id=1, source_target_pairs={{0,12},{4,8},{8,4},{12,0},{1,13},{5,9},{9,5},{13,1},{2,14},{6,10},... | collective-permute-start | bytes 995336 | tf_op jit(solution)/shard_map/ppermute | solution.py:169
  68.7 25.1 %collective-permute-start.9 = (bf16[4,304,256]{2,1,0:T(8,128)(2,1)S(1)}, bf16[4,304,256]{2,1,0:T(8,128)(2,1)}, u32[]{:S(2)}, u32[]{:S(2)}) collective-permute-start(bf16[4,304,256]{2,1,0:T(8,128)(2,1)S(1)} %pad_maximum_fusion.2.refs_0_), channel_id=1, source_target_pairs={{0,1},{1,0},{2,3},{3,2},{4,5},{5,4},{6,7},{7,6},{8,9},{9,8},{10,11... | collective-permute-start | bytes 1867784 | tf_op jit(solution)/shard_map/ppermute | solution.py:169
  115.2 14.6 %collective-permute-start.18 = (bf16[256,1152]{1,0:T(8,128)(2,1)S(1)}, bf16[256,1152]{1,0:T(8,128)(2,1)S(1)}, u32[]{:S(2)}, u32[]{:S(2)}) collective-permute-start(bf16[256,1152]{1,0:T(8,128)(2,1)S(1)} %get-tuple-element.62.mine), channel_id=1, source_target_pairs={{0,2},{1,3},{2,0},{3,1},{4,6},{5,7},{6,4},{7,5},{8,10},{9,11},{10,... | collective-permute-start | bytes 1769480 | tf_op jit(solution)/shard_map/ppermute | solution.py:169
  154.6 13.9 %collective-permute-start.22 = (bf16[576,512]{1,0:T(8,128)(2,1)S(1)}, bf16[576,512]{1,0:T(8,128)(2,1)S(1)}, u32[]{:S(2)}, u32[]{:S(2)}) collective-permute-start(bf16[576,512]{1,0:T(8,128)(2,1)S(1)} %maximum_select_fusion.refs_8_), channel_id=1, source_target_pairs={{0,4},{4,0},{12,8},{16,20},{28,24},{1,5},{5,1},{13,9},{17,21},{29,... | collective-permute-start | bytes 1769480 | tf_op jit(solution)/shard_map/ppermute | solution.py:658
  156.0 20.6 %collective-permute-start.21 = (bf16[576,512]{1,0:T(8,128)(2,1)S(1)}, bf16[576,512]{1,0:T(8,128)(2,1)S(1)}, u32[]{:S(2)}, u32[]{:S(2)}) collective-permute-start(bf16[576,512]{1,0:T(8,128)(2,1)S(1)} %maximum_select_fusion.refs_8_), channel_id=1, source_target_pairs={{8,0},{9,5},{11,15},{24,16},{25,21},{27,31}} | collective-permute-start | bytes 1769480 | tf_op jit(solution)/shard_map/ppermute | solution.py:675
  157.3 30.6 %collective-permute-start.24 = (bf16[576,512]{1,0:T(8,128)(2,1)S(1)}, bf16[576,512]{1,0:T(8,128)(2,1)S(1)}, u32[]{:S(2)}, u32[]{:S(2)}) collective-permute-start(bf16[576,512]{1,0:T(8,128)(2,1)S(1)} %maximum_select_fusion.refs_8_), channel_id=1, source_target_pairs={{0,8},{4,12},{12,4},{16,24},{28,20},{1,9},{5,13},{13,5},{17,25},{2... | collective-permute-start | bytes 1769480 | tf_op jit(solution)/shard_map/ppermute | solution.py:658
  161.5 26.5 %collective-permute-start.25 = (bf16[576,512]{1,0:T(8,128)(2,1)S(1)}, bf16[576,512]{1,0:T(8,128)(2,1)S(1)}, u32[]{:S(2)}, u32[]{:S(2)}) collective-permute-start(bf16[576,512]{1,0:T(8,128)(2,1)S(1)} %maximum_select_fusion.refs_8_), channel_id=1, source_target_pairs={{0,16},{4,20},{12,28},{16,0},{28,12},{1,17},{5,21},{13,29},{17,1},... | collective-permute-start | bytes 1769480 | tf_op jit(solution)/shard_map/ppermute | solution.py:667
  168.8 19.0 %collective-permute-start.23 = (f32[8,576]{1,0:T(8,128)S(1)}, f32[8,576]{1,0:T(8,128)S(1)}, u32[]{:S(2)}, u32[]{:S(2)}) collective-permute-start(f32[8,576]{1,0:T(8,128)S(1)} %convolution_multiply_fusion), channel_id=1, source_target_pairs={{4,0},{6,10},{7,15},{20,16},{22,26},{23,31}} | collective-permute-start | bytes 55304 | tf_op jit(solution)/shard_map/ppermute | solution.py:675
  170.3 17.7 %collective-permute-start.26 = (bf16[576,512]{1,0:T(8,128)(2,1)S(1)}, bf16[576,512]{1,0:T(8,128)(2,1)S(1)}, u32[]{:S(2)}, u32[]{:S(2)}) collective-permute-start(bf16[576,512]{1,0:T(8,128)(2,1)S(1)} %collective-permute-done.22.refs_9_), channel_id=1, source_target_pairs={{0,16},{4,20},{8,24},{20,4},{24,8},{1,17},{5,21},{9,25},{21,5},{25... | collective-permute-start | bytes 1769480 | tf_op jit(solution)/shard_map/ppermute | solution.py:667
  188.0 21.7 %collective-permute-start.30 = (bf16[608,512]{1,0:T(8,128)(2,1)S(1)}, bf16[608,512]{1,0:T(8,128)(2,1)S(1)}, u32[]{:S(2)}, u32[]{:S(2)}) collective-permute-start(bf16[608,512]{1,0:T(8,128)(2,1)S(1)} %pad_maximum_fusion.3.refs_0_), channel_id=1, source_target_pairs={{0,16},{5,21},{10,26},{15,31},{16,0},{21,5},{26,10},{31,15}} | collective-permute-start | bytes 1867784 | tf_op jit(solution)/shard_map/ppermute | solution.py:716
  189.9 15.5 %collective-permute-start.31 = (bf16[576,512]{1,0:T(8,128)(2,1)S(1)}, bf16[576,512]{1,0:T(8,128)(2,1)S(1)}, u32[]{:S(2)}, u32[]{:S(2)}) collective-permute-start(bf16[576,512]{1,0:T(8,128)(2,1)S(1)} %collective-permute-done.24.refs_10_), channel_id=1, source_target_pairs={{4,0},{8,12},{12,8},{20,16},{24,28},{5,1},{9,13},{13,9},{21,17},{2... | collective-permute-start | bytes 1769480 | tf_op jit(solution)/shard_map/ppermute | solution.py:658
  191.8 17.8 %collective-permute-start.32 = (bf16[576,512]{1,0:T(8,128)(2,1)S(1)}, bf16[576,512]{1,0:T(8,128)(2,1)S(1)}, u32[]{:S(2)}, u32[]{:S(2)}) collective-permute-start(bf16[576,512]{1,0:T(8,128)(2,1)S(1)} %collective-permute-done.24.refs_10_), channel_id=1, source_target_pairs={{4,20},{8,24},{12,28},{20,4},{24,8},{5,21},{9,25},{13,29},{21,5},{... | collective-permute-start | bytes 1769480 | tf_op jit(solution)/shard_map/ppermute | solution.py:667
  194.6 25.5 %collective-permute-start.28 = (bf16[608,512]{1,0:T(8,128)(2,1)S(1)}, bf16[608,512]{1,0:T(8,128)(2,1)S(1)}, u32[]{:S(2)}, u32[]{:S(2)}) collective-permute-start(bf16[608,512]{1,0:T(8,128)(2,1)S(1)} %pad_maximum_fusion.3.refs_0_), channel_id=1, source_target_pairs={{0,2},{5,7},{10,8},{15,13},{16,18},{21,23},{26,24},{31,29}} | collective-permute-start | bytes 1867784 | tf_op jit(solution)/shard_map/ppermute | solution.py:683
  209.7 19.3 %collective-permute-start.34 = (bf16[608,512]{1,0:T(8,128)(2,1)S(1)}, bf16[608,512]{1,0:T(8,128)(2,1)S(1)}, u32[]{:S(2)}, u32[]{:S(2)}) collective-permute-start(bf16[608,512]{1,0:T(8,128)(2,1)S(1)} %collective-permute-done.30.refs_4_), channel_id=1, source_target_pairs={{0,2},{5,7},{10,8},{15,13},{16,18},{21,23},{26,24},{31,29}} | collective-permute-start | bytes 1867784 | tf_op jit(solution)/shard_map/ppermute | solution.py:683
  211.0 18.0 %collective-permute-start.35 = (bf16[576,512]{1,0:T(8,128)(2,1)S(1)}, bf16[576,512]{1,0:T(8,128)(2,1)S(1)}, u32[]{:S(2)}, u32[]{:S(2)}) collective-permute-start(bf16[576,512]{1,0:T(8,128)(2,1)S(1)} %collective-permute-done.31.refs_11_), channel_id=1, source_target_pairs={{0,16},{8,24},{12,28},{16,0},{28,12},{1,17},{9,25},{13,29},{17,1},... | collective-permute-start | bytes 1769480 | tf_op jit(solution)/shard_map/ppermute | solution.py:667
  215.1 17.3 %collective-permute-start.27 = (bf16[608,512]{1,0:T(8,128)(2,1)S(1)}, bf16[608,512]{1,0:T(8,128)(2,1)}, u32[]{:S(2)}, u32[]{:S(2)}) collective-permute-start(bf16[608,512]{1,0:T(8,128)(2,1)S(1)} %pad_maximum_fusion.3.refs_0_), channel_id=1, source_target_pairs={{0,1},{5,4},{10,11},{15,14},{16,17},{21,20},{26,27},{31,30}} | collective-permute-start | bytes 1867784 | tf_op jit(solution)/shard_map/ppermute | solution.py:687
  218.0 14.5 %collective-permute-start.33 = (bf16[608,512]{1,0:T(8,128)(2,1)S(1)}, bf16[608,512]{1,0:T(8,128)(2,1)}, u32[]{:S(2)}, u32[]{:S(2)}) collective-permute-start(bf16[608,512]{1,0:T(8,128)(2,1)S(1)} %collective-permute-done.30.refs_4_), channel_id=1, source_target_pairs={{0,1},{5,4},{10,11},{15,14},{16,17},{21,20},{26,27},{31,30}} | collective-permute-start | bytes 1867784 | tf_op jit(solution)/shard_map/ppermute | solution.py:687
  (39 other events, 531.5 us)

commit v12 on v11

--- a/solution.py
+++ b/solution.py
@@ -256,23 +256,32 @@
     )(places, *gathered)
 
 
-def factor_kernel(place_ref, part, own, old, diag, out, *, step, weight):
-    fresh = jnp.zeros(out.shape, jnp.float32)
-    for index in range(part.shape[0]):
-        fresh += lax.dot_general(
-            part[index], own[index], (((1,), (1,)), ((), ())), preferred_element_type=jnp.float32
-        )
-    block = factor_decay * old[...].astype(jnp.float32) + weight * fresh
-    on_diag = lax.broadcasted_iota(jnp.int32, out.shape, 0) == lax.broadcasted_iota(
-        jnp.int32, out.shape, 1
-    )
-    block = jnp.where(on_diag & (place_ref[0] == step), diag[0], block)
-    out[...] = block.astype(jnp.bfloat16)
-
-
-def factor_block(place, features, old, diag, step, weight):
+def factor_kernel(place_ref, part, own, diag, *refs, step, weight):
+    portions, out = refs[:-1], refs[-1]
+    start = 0
+    for old in portions:
+        stop = start + old.shape[0]
+        shape = (old.shape[0], out.shape[1])
+        fresh = jnp.zeros(shape, jnp.float32)
+        for index in range(part.shape[0]):
+            fresh += lax.dot_general(
+                part[index, start:stop],
+                own[index],
+                (((1,), (1,)), ((), ())),
+                preferred_element_type=jnp.float32,
+            )
+        block = factor_decay * old[...].astype(jnp.float32) + weight * fresh
+        on_diag = lax.broadcasted_iota(jnp.int32, shape, 0) + start == lax.broadcasted_iota(
+            jnp.int32, shape, 1
+        )
+        block = jnp.where(on_diag & (place_ref[0] == step), diag[0], block)
+        out[start:stop] = block.astype(jnp.bfloat16)
+        start = stop
+
+
+def factor_block(place, features, portions, diag, step, weight):
     groups, _, tokens = features.shape
-    rows, cols = old.shape
+    rows, cols = sum(old.shape[0] for old in portions), portions[0].shape[1]
     return pl.pallas_call(
         functools.partial(factor_kernel, step=step, weight=weight),
         grid_spec=pltpu.PrefetchScalarGridSpec(
@@ -281,9 +290,9 @@
             in_specs=[
                 pl.BlockSpec((groups, rows, tokens), lambda i, place: (0, step, 0)),
                 pl.BlockSpec((groups, cols, tokens), lambda i, place: (0, place[0], 0)),
-                pl.BlockSpec((rows, cols), lambda i, place: (0, 0)),
                 pl.BlockSpec((1, 1, cols), lambda i, place: (place[0], 0, 0)),
-            ],
+            ]
+            + [pl.BlockSpec(old.shape, lambda i, place: (0, 0)) for old in portions],
             out_specs=pl.BlockSpec((rows, cols), lambda i, place: (0, 0)),
         ),
         out_shape=jax.ShapeDtypeStruct((rows, cols), jnp.bfloat16),
@@ -293,28 +302,21 @@
             bytes_accessed=4 * rows * cols + 4 * groups * rows * tokens,
             transcendentals=0,
         ),
-    )(place, features, features, old, diag)
-
-
-def fetch_blocks(place_ref, blocks, held, sems):
-    count = len(blocks) // 2
-    depth = blocks[0].shape[0]
-    copies = []
-    for index in range(2 * count):
-        slot = pl.multiple_of((place_ref[0] ^ (index % count)) * depth, depth)
-        copies.append(
-            pltpu.make_async_copy(
-                blocks[index], held.at[index // count, pl.ds(slot, depth)], sems.at[index]
-            )
-        )
-    for copy in copies:
-        copy.start()
-    return copies
-
-
-def block_products(mine, theirs, held):
-    rows = jnp.concatenate([mine[...], theirs[...]], axis=1)
-    return [jnp.dot(rows, held[index], preferred_element_type=jnp.float32) for index in range(2)]
+    )(place, features, features, diag, *portions)
+
+
+def block_products(place_ref, halves, blocks, pieces):
+    width = pieces.shape[2]
+    for index, half in enumerate(halves):
+        pieces[2 * index] = half[:, :width]
+        pieces[2 * index + 1] = half[:, width:]
+    products = [None, None]
+    for step in range(4):
+        piece = pieces[place_ref[0] ^ step]
+        for index in range(2):
+            term = jnp.dot(piece, blocks[4 * index + step][...], preferred_element_type=jnp.float32)
+            products[index] = term if products[index] is None else products[index] + term
+    return products
 
 
 def first_parts(place_ref, scale, rows, diag, product, index):
@@ -329,13 +331,10 @@
 
 
 def first_kernel(place_ref, scale_ref, rows, diag, *refs):
-    blocks, (kept, message, held, sems) = refs[:8], refs[8:]
-    copies = fetch_blocks(place_ref, blocks, held, sems)
-    products = []
-    for index in range(2):
-        for copy in copies[index * 4 : (index + 1) * 4]:
-            copy.wait()
-        products.append(jnp.dot(rows[...], held[index], preferred_element_type=jnp.float32))
+    blocks, (kept, message, pieces) = refs[:8], refs[8:]
+    half = rows.shape[1] // 2
+    halves = [rows[:, :half], rows[:, half:]]
+    products = block_products(place_ref, halves, blocks, pieces)
     lows = []
     for index in range(2):
         kept[index] = products[index]
@@ -344,10 +343,9 @@
     message[...] = jnp.concatenate(lows, axis=1)
 
 
-def second_kernel(
-    place_ref, scale_ref, mine, theirs, rows, diag, before, held, kept, message
-):
-    products = block_products(mine, theirs, held)
+def second_kernel(place_ref, scale_ref, mine, theirs, rows, diag, before, *refs):
+    blocks, (kept, message, pieces) = refs[:8], refs[8:]
+    products = block_products(place_ref, [mine[...], theirs[...]], blocks, pieces)
     square = scale_ref[0] * scale_ref[0]
     lows = []
     for index in range(2):
@@ -363,8 +361,9 @@
     message[...] = jnp.concatenate(lows, axis=1)
 
 
-def third_kernel(place_ref, scale_ref, mine, theirs, before, held, keep, give):
-    products = block_products(mine, theirs, held)
+def third_kernel(place_ref, scale_ref, mine, theirs, before, *refs):
+    blocks, (keep, give, pieces) = refs[:8], refs[8:]
+    products = block_products(place_ref, [mine[...], theirs[...]], blocks, pieces)
     square = scale_ref[0] * scale_ref[0]
     for index, out in ((0, keep), (1, give)):
         out[...] = (before[index] + square * products[index]).T.astype(jnp.bfloat16)
@@ -372,19 +371,20 @@
 
 def chain_call(kernel, scalars, arrays, blocks, out_shape):
     tokens = arrays[0].shape[0]
+    depth, width = blocks[0].shape
     vmem = pl.BlockSpec(memory_space=pltpu.VMEM)
-    scratch = [pltpu.SemaphoreType.DMA((len(blocks),))] if blocks else []
     return pl.pallas_call(
         kernel,
         in_specs=[pl.BlockSpec(memory_space=pltpu.SMEM)] * len(scalars)
-        + [vmem] * len(arrays)
-        + [pl.BlockSpec(memory_space=pl.ANY)] * len(blocks),
+        + [vmem] * (len(arrays) + len(blocks)),
         out_specs=[vmem] * len(out_shape),
         out_shape=out_shape,
-        scratch_shapes=scratch,
+        scratch_shapes=[pltpu.VMEM((4, tokens, depth), jnp.bfloat16)],
         compiler_params=params(),
         cost_estimate=pl.CostEstimate(
-            flops=2 * tokens * D * D, bytes_accessed=2 * D * D, transcendentals=0
+            flops=2 * len(blocks) * tokens * depth * width,
+            bytes_accessed=2 * len(blocks) * depth * width,
+            transcendentals=0,
         ),
     )(*scalars, *arrays, *blocks)
 
@@ -541,9 +541,10 @@
         )
         collected.append(swap(message, "tensor", n_tensor, step) if step else message)
     collected = jnp.stack(collected)
-    other_tokens = swap(
-        collected[:, features_dev : 2 * features_dev], "shard", n_shard, 1
-    )
+    lows = [
+        by_index(old_factors, held_by(layer ^ step)).astype(jnp.bfloat16)
+        for step in range(n_tensor)
+    ]
 
     def both_shards(value, axis):
         other = swap(value, "shard", n_shard, 1)
@@ -574,36 +575,34 @@
         "en,ef->fn", grad_all, router_inverse, preferred_element_type=jnp.float32
     ).astype(jnp.bfloat16)
 
-    part_rows = row_block // 2
-
-    def old_block(factors, step):
-        return by_index(factors, held_by(layer ^ step)).astype(jnp.bfloat16)
-
-    early = swap(old_block(old_factors, 2), "tensor", n_tensor, 2)
-    later_factors = lax.optimization_barrier(old_factors)
-    far_block = old_block(later_factors, 3)
-    early_far = swap(far_block[:part_rows], "tensor", n_tensor, 3)
-    blocks = [old_block(later_factors, 0), old_block(later_factors, 1), far_block[part_rows:]]
-    other_tokens, collected, early, early_far, blocks, small = lax.optimization_barrier(
-        (
-            other_tokens,
-            collected,
-            early,
-            early_far,
-            blocks,
-            (router_right, matches, embed_scale, norm_sums),
-        )
+    collected, lows, small = lax.optimization_barrier(
+        (collected, lows, (router_right, matches, embed_scale, norm_sums))
     )
     router_right, matches, embed_scale, norm_sums = small
+    other_tokens = swap(collected[:, features_dev : 2 * features_dev], "shard", n_shard, 1)
+    quarter = row_block // 4
+
+    def portion(step, start, stop):
+        return swap(lows[step][start:stop], "tensor", n_tensor, step)
+
+    near_rows = portion(2, 0, quarter)
+    other_tokens, near_rows = lax.optimization_barrier((other_tokens, near_rows))
     collected = jnp.concatenate(
         [collected[:, :features_dev], other_tokens, collected[:, 2 * features_dev :]], axis=1
     )
     by_side = swap(collected, "section", n_section, 2)
     by_core = swap(collected, "section", n_section, 1)
-    late_far = swap(blocks[2], "tensor", n_tensor, 3)
-    blocks = [blocks[0], swap(blocks[1], "tensor", n_tensor, 1), early]
-    by_side, late_far, blocks[1] = lax.optimization_barrier((by_side, late_far, blocks[1]))
+    middle_rows = portion(2, quarter, 3 * quarter)
+    by_side, middle_rows = lax.optimization_barrier((by_side, middle_rows))
     by_both = swap(by_side, "section", n_section, 1)
+    far_block = portion(3, 0, row_block)
+    last_rows = portion(2, 3 * quarter, row_block)
+    blocks = [
+        (lows[0],),
+        (portion(1, 0, row_block),),
+        (near_rows, middle_rows, last_rows),
+        (far_block,),
+    ]
 
     features, rows, low_diag, trace = lay_out(
         jnp.stack([own_place, layer, core, section]),
@@ -611,9 +610,6 @@
         weight,
     )
     scale = D / (3.0 * trace)
-    early_far, features = lax.optimization_barrier((early_far, features))
-    blocks.append(jnp.concatenate([early_far, late_far], axis=0))
-
     own_cols = [
         factor_block(place, features, blocks[step], low_diag, step, weight)
         for step in range(n_tensor)
@@ -625,18 +621,13 @@
     sent = jax.ShapeDtypeStruct((tokens, 2 * col_block), jnp.bfloat16)
     part = jax.ShapeDtypeStruct((col_block, tokens), jnp.bfloat16)
     scalars = (place, scale)
-    columns = jax.ShapeDtypeStruct((2, D, col_block), jnp.bfloat16)
-    kept, message, held = chain_call(
-        first_kernel, scalars, (rows, low_diag), cols, (wide, sent, columns)
-    )
+    kept, message = chain_call(first_kernel, scalars, (rows, low_diag), cols, (wide, sent))
     theirs = swap(message, "section", n_section, 2)
     kept, message = chain_call(
-        second_kernel, scalars, (message, theirs, rows, low_diag, kept, held), (), (wide, sent)
+        second_kernel, scalars, (message, theirs, rows, low_diag, kept), cols, (wide, sent)
     )
     theirs = swap(message, "section", n_section, 2)
-    keep, give = chain_call(
-        third_kernel, scalars, (message, theirs, kept, held), (), (part, part)
-    )
+    keep, give = chain_call(third_kernel, scalars, (message, theirs, kept), cols, (part, part))
     got = swap(give, "section", n_section, 1)
     own = jnp.where(
         core == shard, jnp.concatenate([keep, got], axis=1), jnp.concatenate([got, keep], axis=1)
@@ -700,40 +691,25 @@
     left_here = scatter(own, 2)
     near_1, own = lax.optimization_barrier((near_1, own))
     over_1 = across(near_1, 1)
+    left_there = lax.ppermute(
+        left_here, everywhere, [(spot(x, t, t), spot(1 - x, t, t)) for x in planes for t in layers]
+    )
     router_cols = learning_rate * jnp.einsum(
         "fn,cn->fc", router_right, own, preferred_element_type=jnp.float32
     )
-    router_cols = scatter(router_cols, 1)
-    router_high = lax.reduce_precision(router_cols, 8, 7)
-    codes = jnp.concatenate([router_high, router_cols - router_high], axis=0).astype(jnp.bfloat16)
-    codes_tail = jnp.pad(codes[:, tokens_all:], ((0, 0), (0, 2 * tokens_all - col_block)))
-    left_here = jnp.concatenate([left_here, codes[:, :tokens_all], codes_tail], axis=0)
-    left_here, near_2, over_0, over_1 = lax.optimization_barrier(
-        (left_here, near_2, over_0, over_1)
+    router_cols = jnp.where((shard == 1) & (layer == 1), router_cols, 0.0)
+    router_all = lax.all_gather(lax.psum(router_cols, axes), "section", axis=0)
+    precond_router = by_index(router_all, layer)
+    (lefts_here,) = hand_round(left_here)
+    near_2, over_0, over_1, left_there, precond_router = lax.optimization_barrier(
+        (near_2, over_0, over_1, left_there, precond_router)
     )
     near_3 = send(near_2, 1, 2)
     over_2 = across(near_2, 2)
-    left_there = lax.ppermute(
-        left_here, everywhere, [(spot(x, t, t), spot(1 - x, t, t)) for x in planes for t in layers]
-    )
-    (lefts_here,) = hand_round(left_here)
-    left_there, near_3, over_2 = lax.optimization_barrier((left_there, near_3, over_2))
+    near_3, over_2 = lax.optimization_barrier((near_3, over_2))
     over_3 = across(near_3, 3)
     lefts_there, over_3 = hand_round(left_there, over_3)
     turn = section ^ layer
-
-    def codes_of(group):
-        parts = [part[col_block:] for part in group]
-        chosen = parts[3]
-        for index in (2, 1, 0):
-            chosen = jnp.where(turn == index, parts[index], chosen)
-        return chosen
-
-    codes = jnp.where(shard == 1, codes_of(lefts_here), codes_of(lefts_there))
-    codes = jnp.concatenate(
-        [codes[: 2 * EXPERTS], codes[2 * EXPERTS :, : col_block - tokens_all]], axis=1
-    ).astype(jnp.float32)
-    precond_router = codes[:EXPERTS] + codes[EXPERTS:]
 
     precond_attn, embed_columns = output_products(
         jnp.stack([shard, layer, turn]),

time: 243 us -> 270 us (1.11)
  the two profiles are of different devices: /device:TPU:29 before, /device:TPU:0 now
where the time goes in v12:
time: 270 us
  waiting for transfers between devices  136 us (50%)
  starting transfers between devices  45.8 us (17%)
  blocking collectives  39.8 us (15%)
  Pallas kernels  23.8 us (9%)
  local copies, waits for them, and re-layouts  10.5 us (4%)
  other arithmetic  9.63 us (4%)
  between operations  2.97 us (1%)
    ppermute x22, waiting for transfers between devices, swap(): return lax.ppermute(value, axis, [(i, i ^ step) for i in range(size)])  91.7 us
    psum x1, blocking collectives, layer_plan(): router_all = lax.all_gather(lax.psum(router_cols, axes), 'section', axis=0)  34.3 us
    ppermute x3, waiting for transfers between devices, send(): return lax.ppermute(value, axes, moves)  24.3 us
    ppermute x22, starting transfers between devices, swap(): return lax.ppermute(value, axis, [(i, i ^ step) for i in range(size)])  18.3 us
    ppermute x1, waiting for transfers between devices, scatter(): lax.ppermute(value, everywhere, [(spot(x, source, s), spot(x, s, s)) for...  10.1 us
    pallas_call x3, Pallas kernels, chain_call(): pl.pallas_call(kernel, in_specs=[pl.BlockSpec(memory_space=pltpu.SMEM)] *...  9.75 us
    ppermute x4, waiting for transfers between devices, across(): return lax.ppermute(value, axes, moves)  9.59 us
    ppermute x4, starting transfers between devices, across(): return lax.ppermute(value, axes, moves)  8.74 us
  transfers between devices with their start and end apart: 37, of which 15 were waited for; matrix products, arithmetic and copies ran while one was open for 6% of the time, Pallas kernels for 2%

profile of v12, /device:TPU:0, one launch (start us, length us, event | category | flops | bytes accessed | tf_op | source)
XLA Modules:
  0.0 269.6 jit_solution(6863111985579831653)
XLA Ops:
  0.6 3.0 %collective-permute-start.4 = (s32[256]{0:T(256)}, s32[256]{0:T(256)S(1)}, u32[]{:S(2)}, u32[]{:S(2)}) collective-permute-start(s32[256]{0:T(256)} %param.10), channel_id=1, source_target_pairs={{0,16},{16,0},{1,17},{17,1},{2,18},{18,2},{3,19},{19,3},{4,20},{20... | collective-permute-start | bytes 3080 | tf_op jit(solution)/shard_map/ppermute | solution.py:169
  9.5 3.7 %collective-permute-start.2 = (bf16[304,256]{1,0:T(8,128)(2,1)S(1)}, bf16[304,256]{1,0:T(8,128)(2,1)S(1)}, u32[]{:S(2)}, u32[]{:S(2)}) collective-permute-start(bf16[304,256]{1,0:T(8,128)(2,1)S(1)} %pad_maximum_fusion.4), channel_id=1, source_target_pairs={{0,12},{4,8},{8,4},{12,0},{1,13},{5,9},{9,5},{13,1},{2,14},{6,10},... | collective-permute-start | bytes 466952 | tf_op jit(solution)/shard_map/ppermute | solution.py:169
  13.3 4.1 %fusion.8 = (bf16[576,576]{1,0:T(8,128)(2,1)}, bf16[576,576]{1,0:T(8,128)(2,1)}, bf16[576,576]{1,0:T(8,128)(2,1)S(1)}, bf16[576,576]{1,0:T(8,128)(2,1)S(1)}) fusion(f32[4,576,576]{2,1,0:T(8,128)} %param.12, s32[]{:T(128)S(6)} %select_n.132, s32[]{:T(128)S(6)} %select_n.124, s32[]{:T(128)S(6)} %select_n.120, s32[]{:T(128)S(6)} %select_n.128), kind=kLoop, calls=%fused_computation.20 | loop fusion | bytes 5308432 | tf_op jit(solution)/shard_map/convert_element_type | solution.py:545
  23.8 2.7 %collective-permute-done.1 = bf16[304,256]{1,0:T(8,128)(2,1)S(1)} collective-permute-done((bf16[304,256]{1,0:T(8,128)(2,1)S(1)}, bf16[304,256]{1,0:T(8,128)(2,1)S(1)}, u32[]{:S(2)}, u32[]{:S(2)}) %collective-permute-start.1) | collective-permute-done | bytes 155680 | tf_op jit(solution)/shard_map/ppermute | solution.py:169
  28.0 8.2 %collective-permute-done.7.refs_0_ = bf16[144,576]{1,0:T(8,128)(2,1)S(1)} collective-permute-done((bf16[144,576]{1,0:T(8,128)(2,1)S(1)}, bf16[144,576]{1,0:T(8,128)(2,1)S(1)}, u32[]{:S(2)}, u32[]{:S(2)}) %collective-permute-start.7) | collective-permute-done | bytes 165920 | tf_op jit(solution)/shard_map/ppermute | solution.py:169
  41.1 14.7 %collective-permute-done.10.refs_1_ = bf16[288,576]{1,0:T(8,128)(2,1)S(1)} collective-permute-done((bf16[288,576]{1,0:T(8,128)(2,1)S(1)}, bf16[288,576]{1,0:T(8,128)(2,1)S(1)}, u32[]{:S(2)}, u32[]{:S(2)}) %collective-permute-start.10) | collective-permute-done | bytes 331808 | tf_op jit(solution)/shard_map/ppermute | solution.py:169
  58.7 3.6 %shard_map.111 = (bf16[2,2304,256]{2,1,0:T(8,128)(2,1)S(1)}, bf16[256,2304]{1,0:T(8,128)(2,1)S(1)}, f32[4,1,576]{2,1,0:T(1,128)S(1)}, f32[1]{0:T(128)}) custom-call(s32[4]{0:T(128)S(1)} %pad_add_fusion.1.place_ref, bf16[4,304,256]{2,1,0:T(8,128)(2,1)S(1)} %pad_maximum_fusion.1.refs_0_, bf16[4,304,256]{2,1,0:T(8,128)(2,1)} %collective-permute-done.8.refs_1_, ...), custom_call_target="tpu_custom_call" | custom-call | flops 37748736 | bytes 8257536 | tf_op jit(solution)/shard_map/pallas_call | solution.py:241
  63.1 15.2 %collective-permute-done.12.refs_0_ = bf16[576,576]{1,0:T(8,128)(2,1)S(1)} collective-permute-done((bf16[576,576]{1,0:T(8,128)(2,1)}, bf16[576,576]{1,0:T(8,128)(2,1)S(1)}, u32[]{:S(2)}, u32[]{:S(2)}) %collective-permute-start.12) | collective-permute-done | bytes 663584 | tf_op jit(solution)/shard_map/ppermute | solution.py:169
  79.0 18.7 %collective-permute-done.13.refs_2_ = bf16[144,576]{1,0:T(8,128)(2,1)S(1)} collective-permute-done((bf16[144,576]{1,0:T(8,128)(2,1)}, bf16[144,576]{1,0:T(8,128)(2,1)S(1)}, u32[]{:S(2)}, u32[]{:S(2)}) %collective-permute-start.13) | collective-permute-done | bytes 165920 | tf_op jit(solution)/shard_map/ppermute | solution.py:169
  101.8 2.9 %shard_map.116 = (f32[2,256,576]{2,1,0:T(8,128)S(1)}, bf16[256,1152]{1,0:T(8,128)(2,1)S(1)}) custom-call(s32[1]{0:T(128)} %bitcast.2.place_ref, f32[1]{0:T(128)S(6)} %div.22.scale_ref, bf16[256,2304]{1,0:T(8,128)(2,1)S(1)} %get-tuple-element.47.rows, f32[4,1,576]{2,1,0:T(1,128)S(1)} %get-tuple-element.48.diag, bf16[576,576]{1,0:T(8,128)(2,1)S(1)} %shard_map.112.refs_0_, ...), custom_call_target="tpu_custom_call" | custom-call | flops 1358954496 | bytes 5308416 | tf_op jit(solution)/shard_map/pallas_call | solution.py:376
  105.3 14.9 %collective-permute-done.19.theirs = bf16[256,1152]{1,0:T(8,128)(2,1)S(1)} collective-permute-done((bf16[256,1152]{1,0:T(8,128)(2,1)S(1)}, bf16[256,1152]{1,0:T(8,128)(2,1)S(1)}, u32[]{:S(2)}, u32[]{:S(2)}) %collective-permute-start.19) | collective-permute-done | bytes 589856 | tf_op jit(solution)/shard_map/ppermute | solution.py:169
  120.2 4.0 %shard_map.117 = (f32[2,256,576]{2,1,0:T(8,128)S(1)}, bf16[256,1152]{1,0:T(8,128)(2,1)S(1)}) custom-call(s32[1]{0:T(128)} %bitcast.2.place_ref, f32[1]{0:T(128)S(6)} %div.22.scale_ref, bf16[256,1152]{1,0:T(8,128)(2,1)S(1)} %get-tuple-element.55.mine, bf16[256,1152]{1,0:T(8,128)(2,1)S(1)} %collective-permute-done.19.theirs, ...), custom_call_target="tpu_custom_call" | custom-call | flops 1358954496 | bytes 5308416 | tf_op jit(solution)/shard_map/pallas_call | solution.py:376
  124.7 14.1 %collective-permute-done.20.theirs = bf16[256,1152]{1,0:T(8,128)(2,1)S(1)} collective-permute-done((bf16[256,1152]{1,0:T(8,128)(2,1)S(1)}, bf16[256,1152]{1,0:T(8,128)(2,1)S(1)}, u32[]{:S(2)}, u32[]{:S(2)}) %collective-permute-start.20) | collective-permute-done | bytes 589856 | tf_op jit(solution)/shard_map/ppermute | solution.py:169
  138.8 2.9 %shard_map.118 = (bf16[576,256]{1,0:T(8,128)(2,1)S(1)}, bf16[576,256]{1,0:T(8,128)(2,1)S(1)}) custom-call(s32[1]{0:T(128)} %bitcast.2.place_ref, f32[1]{0:T(128)S(6)} %div.22.scale_ref, bf16[256,1152]{1,0:T(8,128)(2,1)S(1)} %get-tuple-element.57.mine, bf16[256,1152]{1,0:T(8,128)(2,1)S(1)} %collective-permute-done.20.theirs, ...), custom_call_target="tpu_custom_call" | custom-call | flops 1358954496 | bytes 5308416 | tf_op jit(solution)/shard_map/pallas_call | solution.py:376
  146.7 2.8 %collective-permute-start.27 = (bf16[576,512]{1,0:T(8,128)(2,1)S(1)}, bf16[576,512]{1,0:T(8,128)(2,1)S(1)}, u32[]{:S(2)}, u32[]{:S(2)}) collective-permute-start(bf16[576,512]{1,0:T(8,128)(2,1)S(1)} %maximum_select_fusion.refs_8_), channel_id=1, source_target_pairs={{0,16},{4,20},{12,28},{16,0},{28,12},{1,17},{5,21},{13,29},{17,1},... | collective-permute-start | bytes 1769480 | tf_op jit(solution)/shard_map/ppermute | solution.py:658
  149.5 4.2 %collective-permute-start.26 = (bf16[576,512]{1,0:T(8,128)(2,1)S(1)}, bf16[576,512]{1,0:T(8,128)(2,1)S(1)}, u32[]{:S(2)}, u32[]{:S(2)}) collective-permute-start(bf16[576,512]{1,0:T(8,128)(2,1)S(1)} %maximum_select_fusion.refs_8_), channel_id=1, source_target_pairs={{0,8},{4,12},{12,4},{16,24},{28,20},{1,9},{5,13},{13,5},{17,25},{2... | collective-permute-start | bytes 1769480 | tf_op jit(solution)/shard_map/ppermute | solution.py:649
  153.7 11.5 %collective-permute-done.28.refs_9_ = bf16[576,512]{1,0:T(8,128)(2,1)S(1)} collective-permute-done((bf16[576,512]{1,0:T(8,128)(2,1)S(1)}, bf16[576,512]{1,0:T(8,128)(2,1)S(1)}, u32[]{:S(2)}, u32[]{:S(2)}) %collective-permute-start.28) | collective-permute-done | bytes 589856 | tf_op jit(solution)/shard_map/ppermute | solution.py:649
  166.5 10.1 %collective-permute-done.22 = bf16[576,512]{1,0:T(8,128)(2,1)} collective-permute-done((bf16[576,512]{1,0:T(8,128)(2,1)S(1)}, bf16[576,512]{1,0:T(8,128)(2,1)}, u32[]{:S(2)}, u32[]{:S(2)}) %collective-permute-start.22) | collective-permute-done | bytes 589856 | tf_op jit(solution)/shard_map/ppermute | solution.py:666
  180.6 34.3 %psum.7 = f32[1,8,576]{2,1,0:T(8,128)} all-reduce(f32[1,8,576]{2,1,0:T(8,128)} %fusion.1), channel_id=1, replica_groups=mesh['shard'=2,'tensor'=4,'section'=4] {'shard','tensor'}, use_global_device_ids=true, to_apply=%region_9.10 | all-reduce | flops 4608 | bytes 36864 | tf_op jit(solution)/shard_map/psum | solution.py:701
  214.9 5.5 %all_gather.7 = f32[4,8,576]{2,1,0:T(8,128)S(1)} all-gather(f32[1,8,576]{2,1,0:T(8,128)} %psum.7), channel_id=1, replica_groups=mesh['shard'=2,'tensor'=4,'section'=4] {'section'}, dimensions={0}, use_global_device_ids=true | all-gather | bytes 92160 | tf_op jit(solution)/shard_map/all_gather | solution.py:701
  226.4 12.8 %collective-permute-done.33.refs_11_ = bf16[576,512]{1,0:T(8,128)(2,1)S(1)} collective-permute-done((bf16[576,512]{1,0:T(8,128)(2,1)S(1)}, bf16[576,512]{1,0:T(8,128)(2,1)S(1)}, u32[]{:S(2)}, u32[]{:S(2)}) %collective-permute-start.33) | collective-permute-done | bytes 589856 | tf_op jit(solution)/shard_map/ppermute | solution.py:649
  239.2 3.9 %collective-permute-start.35 = (bf16[576,512]{1,0:T(8,128)(2,1)S(1)}, bf16[576,512]{1,0:T(8,128)(2,1)S(1)}, u32[]{:S(2)}, u32[]{:S(2)}) collective-permute-start(bf16[576,512]{1,0:T(8,128)(2,1)S(1)} %collective-permute-done.33.refs_11_), channel_id=1, source_target_pairs={{0,16},{8,24},{12,28},{16,0},{28,12},{1,17},{9,25},{13,29},{17,1},... | collective-permute-start | bytes 1769480 | tf_op jit(solution)/shard_map/ppermute | solution.py:658
  246.6 9.6 %collective-permute-done.35.refs_15_ = bf16[576,512]{1,0:T(8,128)(2,1)S(1)} collective-permute-done((bf16[576,512]{1,0:T(8,128)(2,1)S(1)}, bf16[576,512]{1,0:T(8,128)(2,1)S(1)}, u32[]{:S(2)}, u32[]{:S(2)}) %collective-permute-start.35) | collective-permute-done | bytes 589856 | tf_op jit(solution)/shard_map/ppermute | solution.py:658
  261.6 7.9 %shard_map.119 = (f32[4,576,576]{2,1,0:T(8,128)}, f32[576,2048]{1,0:T(8,128)}) custom-call(s32[3]{0:T(128)} %pad_add_fusion.where_ref, f32[1,2048]{1,0:T(1,128)} %bitcast.93, bf16[512,2048]{1,0:T(8,128)(2,1)} %compare_convert_fusion.matches, bf16[576,512]{1,0:T(8,128)(2,1)} %copy-done.5, bf16[576,512]{1,0:T(8,128)(2,1)} %copy-done.15, ...), custom_call_target="tpu_custom_call" | custom-call | flops 2566914048 | bytes 14155776 | tf_op jit(solution)/shard_map/pallas_call | solution.py:465
  (157 shorter events, 51.6 us)
Async XLA Ops:
  0.6 16.9 %collective-permute-start.4 = (s32[256]{0:T(256)}, s32[256]{0:T(256)S(1)}, u32[]{:S(2)}, u32[]{:S(2)}) collective-permute-start(s32[256]{0:T(256)} %param.10), channel_id=1, source_target_pairs={{0,16},{16,0},{1,17},{17,1},{2,18},{18,2},{3,19},{19,3},{4,20},{20... | collective-permute-start | bytes 3080 | tf_op jit(solution)/shard_map/ppermute | solution.py:169
  4.8 16.4 %collective-permute-start.5 = (f32[2,2,144]{2,1,0:T(2,128)S(1)}, f32[2,2,144]{2,1,0:T(2,128)S(1)}, u32[]{:S(2)}, u32[]{:S(2)}) collective-permute-start(f32[2,2,144]{2,1,0:T(2,128)S(1)} %pad_maximum_fusion.6), channel_id=1, source_target_pairs={{0,16},{16,0},{1,17},{17,1},{2,18},{18,2},{3,19},{19,3},{4,20},{20... | collective-permute-start | bytes 6920 | tf_op jit(solution)/shard_map/ppermute | solution.py:169
  4.9 16.3 %collective-permute-start.3 = (bf16[8,256]{1,0:T(8,128)(2,1)}, bf16[8,256]{1,0:T(8,128)(2,1)S(1)}, u32[]{:S(2)}, u32[]{:S(2)}) collective-permute-start(bf16[8,256]{1,0:T(8,128)(2,1)} %param.9), channel_id=1, source_target_pairs={{0,16},{16,0},{1,17},{17,1},{2,18},{18,2},{3,19},{19,3},{4,20},{20... | collective-permute-start | bytes 12296 | tf_op jit(solution)/shard_map/ppermute | solution.py:169
  36.9 19.6 %collective-permute-start.9 = (bf16[4,304,256]{2,1,0:T(8,128)(2,1)S(1)}, bf16[4,304,256]{2,1,0:T(8,128)(2,1)S(1)}, u32[]{:S(2)}, u32[]{:S(2)}) collective-permute-start(bf16[4,304,256]{2,1,0:T(8,128)(2,1)S(1)} %pad_maximum_fusion.1.refs_0_), channel_id=1, source_target_pairs={{0,2},{1,3},{2,0},{3,1},{4,6},{5,7},{6,4},{7,5},{8,10},{9,11},{10,... | collective-permute-start | bytes 1867784 | tf_op jit(solution)/shard_map/ppermute | solution.py:169
  38.5 17.3 %collective-permute-start.10 = (bf16[288,576]{1,0:T(8,128)(2,1)S(1)}, bf16[288,576]{1,0:T(8,128)(2,1)S(1)}, u32[]{:S(2)}, u32[]{:S(2)}) collective-permute-start(bf16[288,576]{1,0:T(8,128)(2,1)S(1)} %slice.48), channel_id=1, source_target_pairs={{0,8},{4,12},{8,0},{12,4},{1,9},{5,13},{9,1},{13,5},{2,10},{6,14},... | collective-permute-start | bytes 995336 | tf_op jit(solution)/shard_map/ppermute | solution.py:169
  38.6 39.7 %collective-permute-start.12 = (bf16[576,576]{1,0:T(8,128)(2,1)}, bf16[576,576]{1,0:T(8,128)(2,1)S(1)}, u32[]{:S(2)}, u32[]{:S(2)}) collective-permute-start(bf16[576,576]{1,0:T(8,128)(2,1)} %get-tuple-element.51), channel_id=1, source_target_pairs={{0,4},{4,0},{8,12},{12,8},{1,5},{5,1},{9,13},{13,9},{2,6},{6,2},{1... | collective-permute-start | bytes 1990664 | tf_op jit(solution)/shard_map/ppermute | solution.py:169
  41.1 17.3 %collective-permute-start.8 = (bf16[4,304,256]{2,1,0:T(8,128)(2,1)S(1)}, bf16[4,304,256]{2,1,0:T(8,128)(2,1)}, u32[]{:S(2)}, u32[]{:S(2)}) collective-permute-start(bf16[4,304,256]{2,1,0:T(8,128)(2,1)S(1)} %pad_maximum_fusion.1.refs_0_), channel_id=1, source_target_pairs={{0,1},{1,0},{2,3},{3,2},{4,5},{5,4},{6,7},{7,6},{8,9},{9,8},{10,11... | collective-permute-start | bytes 1867784 | tf_op jit(solution)/shard_map/ppermute | solution.py:169
  56.5 42.0 %collective-permute-start.14 = (bf16[576,576]{1,0:T(8,128)(2,1)}, bf16[576,576]{1,0:T(8,128)(2,1)S(1)}, u32[]{:S(2)}, u32[]{:S(2)}) collective-permute-start(bf16[576,576]{1,0:T(8,128)(2,1)} %get-tuple-element.54), channel_id=1, source_target_pairs={{0,12},{4,8},{8,4},{12,0},{1,13},{5,9},{9,5},{13,1},{2,14},{6,10},... | collective-permute-start | bytes 1990664 | tf_op jit(solution)/shard_map/ppermute | solution.py:169
  58.3 39.4 %collective-permute-start.13 = (bf16[144,576]{1,0:T(8,128)(2,1)}, bf16[144,576]{1,0:T(8,128)(2,1)S(1)}, u32[]{:S(2)}, u32[]{:S(2)}) collective-permute-start(bf16[144,576]{1,0:T(8,128)(2,1)} %get-tuple-element.86), channel_id=1, source_target_pairs={{0,8},{4,12},{8,0},{12,4},{1,9},{5,13},{9,1},{13,5},{2,10},{6,14},... | collective-permute-start | bytes 497672 | tf_op jit(solution)/shard_map/ppermute | solution.py:169
  62.9 37.5 %collective-permute-start.15 = (bf16[576,576]{1,0:T(8,128)(2,1)S(1)}, bf16[576,576]{1,0:T(8,128)(2,1)S(1)}, u32[]{:S(2)}, u32[]{:S(2)}) collective-permute-start(bf16[576,576]{1,0:T(8,128)(2,1)S(1)} %shard_map.112.refs_0_), channel_id=1, source_target_pairs={{0,1},{1,0},{2,3},{3,2},{4,5},{5,4},{6,7},{7,6},{8,9},{9,8},{10,11... | collective-permute-start | bytes 1990664 | tf_op jit(solution)/shard_map/ppermute | solution.py:169
  78.9 21.5 %collective-permute-start.16 = (bf16[576,576]{1,0:T(8,128)(2,1)S(1)}, bf16[576,576]{1,0:T(8,128)(2,1)S(1)}, u32[]{:S(2)}, u32[]{:S(2)}) collective-permute-start(bf16[576,576]{1,0:T(8,128)(2,1)S(1)} %shard_map.113.refs_1_), channel_id=1, source_target_pairs={{0,1},{1,0},{2,3},{3,2},{4,5},{5,4},{6,7},{7,6},{8,9},{9,8},{10,11... | collective-permute-start | bytes 1990664 | tf_op jit(solution)/shard_map/ppermute | solution.py:169
  104.7 15.5 %collective-permute-start.19 = (bf16[256,1152]{1,0:T(8,128)(2,1)S(1)}, bf16[256,1152]{1,0:T(8,128)(2,1)S(1)}, u32[]{:S(2)}, u32[]{:S(2)}) collective-permute-start(bf16[256,1152]{1,0:T(8,128)(2,1)S(1)} %get-tuple-element.55.mine), channel_id=1, source_target_pairs={{0,2},{1,3},{2,0},{3,1},{4,6},{5,7},{6,4},{7,5},{8,10},{9,11},{10,... | collective-permute-start | bytes 1769480 | tf_op jit(solution)/shard_map/ppermute | solution.py:169
  143.5 21.7 %collective-permute-start.28 = (bf16[576,512]{1,0:T(8,128)(2,1)S(1)}, bf16[576,512]{1,0:T(8,128)(2,1)S(1)}, u32[]{:S(2)}, u32[]{:S(2)}) collective-permute-start(bf16[576,512]{1,0:T(8,128)(2,1)S(1)} %maximum_select_fusion.refs_8_), channel_id=1, source_target_pairs={{0,4},{4,0},{12,8},{16,20},{28,24},{1,5},{5,1},{13,9},{17,21},{29,... | collective-permute-start | bytes 1769480 | tf_op jit(solution)/shard_map/ppermute | solution.py:649
  145.4 31.2 %collective-permute-start.22 = (bf16[576,512]{1,0:T(8,128)(2,1)S(1)}, bf16[576,512]{1,0:T(8,128)(2,1)}, u32[]{:S(2)}, u32[]{:S(2)}) collective-permute-start(bf16[576,512]{1,0:T(8,128)(2,1)S(1)} %maximum_select_fusion.refs_8_), channel_id=1, source_target_pairs={{8,0},{9,5},{11,15},{24,16},{25,21},{27,31}} | collective-permute-start | bytes 1769480 | tf_op jit(solution)/shard_map/ppermute | solution.py:666
  146.7 74.2 %collective-permute-start.27 = (bf16[576,512]{1,0:T(8,128)(2,1)S(1)}, bf16[576,512]{1,0:T(8,128)(2,1)S(1)}, u32[]{:S(2)}, u32[]{:S(2)}) collective-permute-start(bf16[576,512]{1,0:T(8,128)(2,1)S(1)} %maximum_select_fusion.refs_8_), channel_id=1, source_target_pairs={{0,16},{4,20},{12,28},{16,0},{28,12},{1,17},{5,21},{13,29},{17,1},... | collective-permute-start | bytes 1769480 | tf_op jit(solution)/shard_map/ppermute | solution.py:658
  149.5 71.4 %collective-permute-start.26 = (bf16[576,512]{1,0:T(8,128)(2,1)S(1)}, bf16[576,512]{1,0:T(8,128)(2,1)S(1)}, u32[]{:S(2)}, u32[]{:S(2)}) collective-permute-start(bf16[576,512]{1,0:T(8,128)(2,1)S(1)} %maximum_select_fusion.refs_8_), channel_id=1, source_target_pairs={{0,8},{4,12},{12,4},{16,24},{28,20},{1,9},{5,13},{13,5},{17,25},{2... | collective-permute-start | bytes 1769480 | tf_op jit(solution)/shard_map/ppermute | solution.py:649
  165.2 55.8 %collective-permute-start.29 = (bf16[576,512]{1,0:T(8,128)(2,1)S(1)}, bf16[576,512]{1,0:T(8,128)(2,1)S(1)}, u32[]{:S(2)}, u32[]{:S(2)}) collective-permute-start(bf16[576,512]{1,0:T(8,128)(2,1)S(1)} %collective-permute-done.28.refs_9_), channel_id=1, source_target_pairs={{0,16},{4,20},{8,24},{20,4},{24,8},{1,17},{5,21},{9,25},{21,5},{25... | collective-permute-start | bytes 1769480 | tf_op jit(solution)/shard_map/ppermute | solution.py:658
  177.7 43.3 %collective-permute-start.30 = (bf16[576,512]{1,0:T(8,128)(2,1)S(1)}, bf16[576,512]{1,0:T(8,128)(2,1)}, u32[]{:S(2)}, u32[]{:S(2)}) collective-permute-start(bf16[576,512]{1,0:T(8,128)(2,1)S(1)} %broadcast_select_fusion.refs_0_), channel_id=1, source_target_pairs={{0,16},{5,21},{10,26},{15,31},{16,0},{21,5},{26,10},{31,15}} | collective-permute-start | bytes 1769480 | tf_op jit(solution)/shard_map/ppermute | solution.py:694
  221.7 17.5 %collective-permute-start.33 = (bf16[576,512]{1,0:T(8,128)(2,1)S(1)}, bf16[576,512]{1,0:T(8,128)(2,1)S(1)}, u32[]{:S(2)}, u32[]{:S(2)}) collective-permute-start(bf16[576,512]{1,0:T(8,128)(2,1)S(1)} %collective-permute-done.26.refs_10_), channel_id=1, source_target_pairs={{4,0},{8,12},{12,8},{20,16},{24,28},{5,1},{9,13},{13,9},{21,17},{2... | collective-permute-start | bytes 1769480 | tf_op jit(solution)/shard_map/ppermute | solution.py:649
  223.0 22.8 %collective-permute-start.24 = (bf16[576,512]{1,0:T(8,128)(2,1)S(1)}, bf16[576,512]{1,0:T(8,128)(2,1)S(1)}, u32[]{:S(2)}, u32[]{:S(2)}) collective-permute-start(bf16[576,512]{1,0:T(8,128)(2,1)S(1)} %broadcast_select_fusion.refs_0_), channel_id=1, source_target_pairs={{0,2},{5,7},{10,8},{15,13},{16,18},{21,23},{26,24},{31,29}} | collective-permute-start | bytes 1769480 | tf_op jit(solution)/shard_map/ppermute | solution.py:674
  225.0 21.5 %collective-permute-start.32 = (bf16[576,512]{1,0:T(8,128)(2,1)}, bf16[576,512]{1,0:T(8,128)(2,1)S(1)}, u32[]{:S(2)}, u32[]{:S(2)}) collective-permute-start(bf16[576,512]{1,0:T(8,128)(2,1)} %collective-permute-done.30.refs_4_), channel_id=1, source_target_pairs={{0,2},{5,7},{10,8},{15,13},{16,18},{21,23},{26,24},{31,29}} | collective-permute-start | bytes 1769480 | tf_op jit(solution)/shard_map/ppermute | solution.py:674
  239.2 16.9 %collective-permute-start.35 = (bf16[576,512]{1,0:T(8,128)(2,1)S(1)}, bf16[576,512]{1,0:T(8,128)(2,1)S(1)}, u32[]{:S(2)}, u32[]{:S(2)}) collective-permute-start(bf16[576,512]{1,0:T(8,128)(2,1)S(1)} %collective-permute-done.33.refs_11_), channel_id=1, source_target_pairs={{0,16},{8,24},{12,28},{16,0},{28,12},{1,17},{9,25},{13,29},{17,1},... | collective-permute-start | bytes 1769480 | tf_op jit(solution)/shard_map/ppermute | solution.py:658
  243.1 16.5 %collective-permute-start.23 = (bf16[576,512]{1,0:T(8,128)(2,1)S(1)}, bf16[576,512]{1,0:T(8,128)(2,1)S(1)}, u32[]{:S(2)}, u32[]{:S(2)}) collective-permute-start(bf16[576,512]{1,0:T(8,128)(2,1)S(1)} %broadcast_select_fusion.refs_0_), channel_id=1, source_target_pairs={{0,1},{5,4},{10,11},{15,14},{16,17},{21,20},{26,27},{31,30}} | collective-permute-start | bytes 1769480 | tf_op jit(solution)/shard_map/ppermute | solution.py:678
  244.5 15.2 %collective-permute-start.31 = (bf16[576,512]{1,0:T(8,128)(2,1)}, bf16[576,512]{1,0:T(8,128)(2,1)S(1)}, u32[]{:S(2)}, u32[]{:S(2)}) collective-permute-start(bf16[576,512]{1,0:T(8,128)(2,1)} %collective-permute-done.30.refs_4_), channel_id=1, source_target_pairs={{0,1},{5,4},{10,11},{15,14},{16,17},{21,20},{26,27},{31,30}} | collective-permute-start | bytes 1769480 | tf_op jit(solution)/shard_map/ppermute | solution.py:678
  (37 other events, 789.6 us)

commit v13 on v12

--- a/solution.py
+++ b/solution.py
@@ -670,20 +670,22 @@
         )
         return jnp.where(layer == source, value, moved_here)
 
-    def hand_round(value, *ahead):
-        sides = lax.ppermute(
+    def to_side(value):
+        return lax.ppermute(
             value, everywhere, [(spot(x, t, t), spot(x, t, t ^ 2)) for x in planes for t in layers]
         )
-        sides, *ahead = lax.optimization_barrier((sides, *ahead))
-        near = lax.ppermute(
+
+    def to_core(value):
+        return lax.ppermute(
             value, everywhere, [(spot(x, t, t), spot(x, t, t ^ 1)) for x in planes for t in layers]
         )
-        far = lax.ppermute(
-            sides,
+
+    def to_far(value):
+        return lax.ppermute(
+            value,
             everywhere,
             [(spot(x, t, t ^ 2), spot(x, t, t ^ 3)) for x in planes for t in layers],
         )
-        return (value, near, sides, far), *ahead
 
     near_1 = send(own, 1, 0)
     near_2 = send(own, 2, 0)
@@ -697,19 +699,33 @@
     router_cols = learning_rate * jnp.einsum(
         "fn,cn->fc", router_right, own, preferred_element_type=jnp.float32
     )
-    router_cols = jnp.where((shard == 1) & (layer == 1), router_cols, 0.0)
-    router_all = lax.all_gather(lax.psum(router_cols, axes), "section", axis=0)
-    precond_router = by_index(router_all, layer)
-    (lefts_here,) = hand_round(left_here)
-    near_2, over_0, over_1, left_there, precond_router = lax.optimization_barrier(
-        (near_2, over_0, over_1, left_there, precond_router)
+    router_moved = lax.ppermute(
+        router_cols, everywhere, [(spot(1, 1, s), spot(1, s, s)) for s in layers if s != 1]
+    )
+    router_cols = jnp.where(layer == 1, router_cols, router_moved)
+    side_here = to_side(left_here)
+    lefts_here = (left_here, to_core(left_here), side_here, to_far(side_here))
+    near_2, over_0, over_1, left_there, router_cols = lax.optimization_barrier(
+        (near_2, over_0, over_1, left_there, router_cols)
     )
     near_3 = send(near_2, 1, 2)
     over_2 = across(near_2, 2)
-    near_3, over_2 = lax.optimization_barrier((near_3, over_2))
+    router_there = lax.ppermute(
+        router_cols, everywhere, [(spot(1, t, t), spot(0, t, t)) for t in layers]
+    )
+    near_3, over_2, router_there = lax.optimization_barrier((near_3, over_2, router_there))
     over_3 = across(near_3, 3)
-    lefts_there, over_3 = hand_round(left_there, over_3)
+    router_cols = jnp.where(shard == 1, router_cols, router_there)
+    router_side, router_core = to_side(router_cols), to_core(router_cols)
+    side_there, over_3, router_side, router_core = lax.optimization_barrier(
+        (to_side(left_there), over_3, router_side, router_core)
+    )
+    lefts_there = (left_there, to_core(left_there), side_there, to_far(side_there))
+    routers = (router_cols, router_core, router_side, to_far(router_side))
     turn = section ^ layer
+    precond_router = routers[3]
+    for index in (2, 1, 0):
+        precond_router = jnp.where(turn == index, routers[index], precond_router)
 
     precond_attn, embed_columns = output_products(
         jnp.stack([shard, layer, turn]),

time: 270 us -> 235 us (0.87)
  blocking collectives: 39.8 us -> 0 us
  starting transfers between devices: 45.8 us -> 54.6 us
  waiting for transfers between devices: 136 us -> 132 us
  local copies, waits for them, and re-layouts: 10.5 us -> 7.2 us
  other arithmetic: 9.63 us -> 12.4 us
    psum x1 -> x0, blocking collectives: 34.3 us -> none  [layer_plan(): router_all = lax.all_gather(lax.psum(router_cols, axes), 'section', axis=0)]
    ppermute x6 -> x11, starting transfers between devices: 8.18 us -> 17.2 us  [the longest x3 5.51 us: to_core(): lax.ppermute(value, everywhere, [(spot(x, t, t), spot(x, t, t ^ 1)) for x...]
    ppermute x1, waiting for transfers between devices: 0.01 us -> 7.03 us  [layer_plan(): lax.ppermute(left_here, everywhere, [(spot(x, t, t), spot(1 - x, t, t)) f...]
    ppermute x4, waiting for transfers between devices: 9.59 us -> 3.29 us  [across(): return lax.ppermute(value, axes, moves)]
    all_gather x1 -> x0, blocking collectives: 5.49 us -> none  [layer_plan(): router_all = lax.all_gather(lax.psum(router_cols, axes), 'section', axis=0)]
    ppermute x3, waiting for transfers between devices: 24.3 us -> 19.5 us  [send(): return lax.ppermute(value, axes, moves)]
    select_n x0 -> x3, other arithmetic: none -> 2.83 us  [the longest x1 1.34 us: layer_plan(): precond_router = jnp.where(turn == index, routers[index], precond_router)]
  transfers between devices with their start and end apart: 37 -> 42, of which waited for: 15 -> 17; matrix products, arithmetic and copies ran while one was open for 6% -> 8% of each run, Pallas kernels for 2% -> 3%
where the time goes in v13:
time: 235 us; the launch traced here: 234 us
  waiting for transfers between devices  132 us (56%)
  starting transfers between devices  54.6 us (23%)
  Pallas kernels  23.8 us (10%)
  other arithmetic  12.4 us (5%)
  local copies, waits for them, and re-layouts  7.2 us (3%)
  between operations  2.92 us (1%)
    ppermute x22, waiting for transfers between devices, swap(): return lax.ppermute(value, axis, [(i, i ^ step) for i in range(size)])  91.7 us
    ppermute x3, waiting for transfers between devices, send(): return lax.ppermute(value, axes, moves)  19.5 us
    ppermute x22, starting transfers between devices, swap(): return lax.ppermute(value, axis, [(i, i ^ step) for i in range(size)])  18.3 us
    ppermute x1, waiting for transfers between devices, scatter(): lax.ppermute(value, everywhere, [(spot(x, source, s), spot(x, s, s)) for...  10.1 us
    pallas_call x3, Pallas kernels, chain_call(): pl.pallas_call(kernel, in_specs=[pl.BlockSpec(memory_space=pltpu.SMEM)] *...  9.75 us
    ppermute x4, starting transfers between devices, across(): return lax.ppermute(value, axes, moves)  8.45 us
    pallas_call x1, Pallas kernels, output_products(): pl.pallas_call(output_kernel, in_specs=[pl.BlockSpec(memory_space=pltpu.S...  7.86 us
    ppermute x3, starting transfers between devices, send(): return lax.ppermute(value, axes, moves)  7.38 us
  transfers between devices with their start and end apart: 42, of which 17 were waited for; matrix products, arithmetic and copies ran while one was open for 8% of the time, Pallas kernels for 3%

profile of v13, /device:TPU:0, one launch (start us, length us, event | category | flops | bytes accessed | tf_op | source)
XLA Modules:
  0.0 234.2 jit_solution(641742243048944503)
XLA Ops:
  0.6 3.0 %collective-permute-start.4 = (s32[256]{0:T(256)}, s32[256]{0:T(256)S(1)}, u32[]{:S(2)}, u32[]{:S(2)}) collective-permute-start(s32[256]{0:T(256)} %param.10), channel_id=1, source_target_pairs={{0,16},{16,0},{1,17},{17,1},{2,18},{18,2},{3,19},{19,3},{4,20},{20... | collective-permute-start | bytes 3080 | tf_op jit(solution)/shard_map/ppermute | solution.py:169
  9.5 3.7 %collective-permute-start.2 = (bf16[304,256]{1,0:T(8,128)(2,1)S(1)}, bf16[304,256]{1,0:T(8,128)(2,1)S(1)}, u32[]{:S(2)}, u32[]{:S(2)}) collective-permute-start(bf16[304,256]{1,0:T(8,128)(2,1)S(1)} %pad_maximum_fusion.4), channel_id=1, source_target_pairs={{0,12},{4,8},{8,4},{12,0},{1,13},{5,9},{9,5},{13,1},{2,14},{6,10},... | collective-permute-start | bytes 466952 | tf_op jit(solution)/shard_map/ppermute | solution.py:169
  13.3 4.1 %fusion.6 = (bf16[576,576]{1,0:T(8,128)(2,1)}, bf16[576,576]{1,0:T(8,128)(2,1)}, bf16[576,576]{1,0:T(8,128)(2,1)S(1)}, bf16[576,576]{1,0:T(8,128)(2,1)S(1)}) fusion(f32[4,576,576]{2,1,0:T(8,128)} %param.12, s32[]{:T(128)S(6)} %select_n.152, s32[]{:T(128)S(6)} %select_n.144, s32[]{:T(128)S(6)} %select_n.140, s32[]{:T(128)S(6)} %select_n.148), kind=kLoop, calls=%fused_computation.18 | loop fusion | bytes 5308432 | tf_op jit(solution)/shard_map/convert_element_type | solution.py:545
  23.8 2.7 %collective-permute-done.1 = bf16[304,256]{1,0:T(8,128)(2,1)S(1)} collective-permute-done((bf16[304,256]{1,0:T(8,128)(2,1)S(1)}, bf16[304,256]{1,0:T(8,128)(2,1)S(1)}, u32[]{:S(2)}, u32[]{:S(2)}) %collective-permute-start.1) | collective-permute-done | bytes 155680 | tf_op jit(solution)/shard_map/ppermute | solution.py:169
  27.9 8.2 %collective-permute-done.7.refs_0_ = bf16[144,576]{1,0:T(8,128)(2,1)S(1)} collective-permute-done((bf16[144,576]{1,0:T(8,128)(2,1)S(1)}, bf16[144,576]{1,0:T(8,128)(2,1)S(1)}, u32[]{:S(2)}, u32[]{:S(2)}) %collective-permute-start.7) | collective-permute-done | bytes 165920 | tf_op jit(solution)/shard_map/ppermute | solution.py:169
  38.6 2.5 %collective-permute-start.12 = (bf16[576,576]{1,0:T(8,128)(2,1)}, bf16[576,576]{1,0:T(8,128)(2,1)S(1)}, u32[]{:S(2)}, u32[]{:S(2)}) collective-permute-start(bf16[576,576]{1,0:T(8,128)(2,1)} %get-tuple-element.54), channel_id=1, source_target_pairs={{0,4},{4,0},{8,12},{12,8},{1,5},{5,1},{9,13},{13,9},{2,6},{6,2},{1... | collective-permute-start | bytes 1990664 | tf_op jit(solution)/shard_map/ppermute | solution.py:169
  41.0 14.7 %collective-permute-done.10.refs_1_ = bf16[288,576]{1,0:T(8,128)(2,1)S(1)} collective-permute-done((bf16[288,576]{1,0:T(8,128)(2,1)S(1)}, bf16[288,576]{1,0:T(8,128)(2,1)S(1)}, u32[]{:S(2)}, u32[]{:S(2)}) %collective-permute-start.10) | collective-permute-done | bytes 331808 | tf_op jit(solution)/shard_map/ppermute | solution.py:169
  58.7 3.6 %shard_map.111 = (bf16[2,2304,256]{2,1,0:T(8,128)(2,1)S(1)}, bf16[256,2304]{1,0:T(8,128)(2,1)S(1)}, f32[4,1,576]{2,1,0:T(1,128)S(1)}, f32[1]{0:T(128)}) custom-call(s32[4]{0:T(128)S(1)} %pad_add_fusion.1.place_ref, bf16[4,304,256]{2,1,0:T(8,128)(2,1)S(1)} %pad_maximum_fusion.1.refs_0_, bf16[4,304,256]{2,1,0:T(8,128)(2,1)} %collective-permute-done.8.refs_1_, ...), custom_call_target="tpu_custom_call" | custom-call | flops 37748736 | bytes 8257536 | tf_op jit(solution)/shard_map/pallas_call | solution.py:241
  63.1 15.2 %collective-permute-done.12.refs_0_ = bf16[576,576]{1,0:T(8,128)(2,1)S(1)} collective-permute-done((bf16[576,576]{1,0:T(8,128)(2,1)}, bf16[576,576]{1,0:T(8,128)(2,1)S(1)}, u32[]{:S(2)}, u32[]{:S(2)}) %collective-permute-start.12) | collective-permute-done | bytes 663584 | tf_op jit(solution)/shard_map/ppermute | solution.py:169
  79.0 18.7 %collective-permute-done.13.refs_2_ = bf16[144,576]{1,0:T(8,128)(2,1)S(1)} collective-permute-done((bf16[144,576]{1,0:T(8,128)(2,1)}, bf16[144,576]{1,0:T(8,128)(2,1)S(1)}, u32[]{:S(2)}, u32[]{:S(2)}) %collective-permute-start.13) | collective-permute-done | bytes 165920 | tf_op jit(solution)/shard_map/ppermute | solution.py:169
  101.8 2.9 %shard_map.116 = (f32[2,256,576]{2,1,0:T(8,128)S(1)}, bf16[256,1152]{1,0:T(8,128)(2,1)S(1)}) custom-call(s32[1]{0:T(128)} %bitcast.2.place_ref, f32[1]{0:T(128)S(6)} %div.22.scale_ref, bf16[256,2304]{1,0:T(8,128)(2,1)S(1)} %get-tuple-element.50.rows, f32[4,1,576]{2,1,0:T(1,128)S(1)} %get-tuple-element.51.diag, bf16[576,576]{1,0:T(8,128)(2,1)S(1)} %shard_map.112.refs_0_, ...), custom_call_target="tpu_custom_call" | custom-call | flops 1358954496 | bytes 5308416 | tf_op jit(solution)/shard_map/pallas_call | solution.py:376
  105.3 14.9 %collective-permute-done.19.theirs = bf16[256,1152]{1,0:T(8,128)(2,1)S(1)} collective-permute-done((bf16[256,1152]{1,0:T(8,128)(2,1)S(1)}, bf16[256,1152]{1,0:T(8,128)(2,1)S(1)}, u32[]{:S(2)}, u32[]{:S(2)}) %collective-permute-start.19) | collective-permute-done | bytes 589856 | tf_op jit(solution)/shard_map/ppermute | solution.py:169
  120.2 4.0 %shard_map.117 = (f32[2,256,576]{2,1,0:T(8,128)S(1)}, bf16[256,1152]{1,0:T(8,128)(2,1)S(1)}) custom-call(s32[1]{0:T(128)} %bitcast.2.place_ref, f32[1]{0:T(128)S(6)} %div.22.scale_ref, bf16[256,1152]{1,0:T(8,128)(2,1)S(1)} %get-tuple-element.58.mine, bf16[256,1152]{1,0:T(8,128)(2,1)S(1)} %collective-permute-done.19.theirs, ...), custom_call_target="tpu_custom_call" | custom-call | flops 1358954496 | bytes 5308416 | tf_op jit(solution)/shard_map/pallas_call | solution.py:376
  124.7 14.1 %collective-permute-done.20.theirs = bf16[256,1152]{1,0:T(8,128)(2,1)S(1)} collective-permute-done((bf16[256,1152]{1,0:T(8,128)(2,1)S(1)}, bf16[256,1152]{1,0:T(8,128)(2,1)S(1)}, u32[]{:S(2)}, u32[]{:S(2)}) %collective-permute-start.20) | collective-permute-done | bytes 589856 | tf_op jit(solution)/shard_map/ppermute | solution.py:169
  138.8 2.9 %shard_map.118 = (bf16[576,256]{1,0:T(8,128)(2,1)S(1)}, bf16[576,256]{1,0:T(8,128)(2,1)S(1)}) custom-call(s32[1]{0:T(128)} %bitcast.2.place_ref, f32[1]{0:T(128)S(6)} %div.22.scale_ref, bf16[256,1152]{1,0:T(8,128)(2,1)S(1)} %get-tuple-element.60.mine, bf16[256,1152]{1,0:T(8,128)(2,1)S(1)} %collective-permute-done.20.theirs, ...), custom_call_target="tpu_custom_call" | custom-call | flops 1358954496 | bytes 5308416 | tf_op jit(solution)/shard_map/pallas_call | solution.py:376
  146.7 2.8 %collective-permute-start.27 = (bf16[576,512]{1,0:T(8,128)(2,1)S(1)}, bf16[576,512]{1,0:T(8,128)(2,1)S(1)}, u32[]{:S(2)}, u32[]{:S(2)}) collective-permute-start(bf16[576,512]{1,0:T(8,128)(2,1)S(1)} %maximum_select_fusion.refs_8_), channel_id=1, source_target_pairs={{0,16},{4,20},{12,28},{16,0},{28,12},{1,17},{5,21},{13,29},{17,1},... | collective-permute-start | bytes 1769480 | tf_op jit(solution)/shard_map/ppermute | solution.py:658
  149.5 4.2 %collective-permute-start.26 = (bf16[576,512]{1,0:T(8,128)(2,1)S(1)}, bf16[576,512]{1,0:T(8,128)(2,1)S(1)}, u32[]{:S(2)}, u32[]{:S(2)}) collective-permute-start(bf16[576,512]{1,0:T(8,128)(2,1)S(1)} %maximum_select_fusion.refs_8_), channel_id=1, source_target_pairs={{0,8},{4,12},{12,4},{16,24},{28,20},{1,9},{5,13},{13,5},{17,25},{2... | collective-permute-start | bytes 1769480 | tf_op jit(solution)/shard_map/ppermute | solution.py:649
  153.7 11.4 %collective-permute-done.28.refs_9_ = bf16[576,512]{1,0:T(8,128)(2,1)S(1)} collective-permute-done((bf16[576,512]{1,0:T(8,128)(2,1)S(1)}, bf16[576,512]{1,0:T(8,128)(2,1)S(1)}, u32[]{:S(2)}, u32[]{:S(2)}) %collective-permute-start.28) | collective-permute-done | bytes 589856 | tf_op jit(solution)/shard_map/ppermute | solution.py:649
  166.5 10.1 %collective-permute-done.22 = bf16[576,512]{1,0:T(8,128)(2,1)} collective-permute-done((bf16[576,512]{1,0:T(8,128)(2,1)S(1)}, bf16[576,512]{1,0:T(8,128)(2,1)}, u32[]{:S(2)}, u32[]{:S(2)}) %collective-permute-start.22) | collective-permute-done | bytes 589856 | tf_op jit(solution)/shard_map/ppermute | solution.py:666
  182.6 7.0 %collective-permute-done.30.refs_4_ = bf16[576,512]{1,0:T(8,128)(2,1)} collective-permute-done((bf16[576,512]{1,0:T(8,128)(2,1)S(1)}, bf16[576,512]{1,0:T(8,128)(2,1)}, u32[]{:S(2)}, u32[]{:S(2)}) %collective-permute-start.30) | collective-permute-done | bytes 589856 | tf_op jit(solution)/shard_map/ppermute | solution.py:696
  197.3 8.0 %collective-permute-done.34.refs_11_ = bf16[576,512]{1,0:T(8,128)(2,1)} collective-permute-done((bf16[576,512]{1,0:T(8,128)(2,1)S(1)}, bf16[576,512]{1,0:T(8,128)(2,1)}, u32[]{:S(2)}, u32[]{:S(2)}) %collective-permute-start.34) | collective-permute-done | bytes 589856 | tf_op jit(solution)/shard_map/ppermute | solution.py:649
  205.3 3.6 %collective-permute-start.37 = (bf16[576,512]{1,0:T(8,128)(2,1)}, bf16[576,512]{1,0:T(8,128)(2,1)}, u32[]{:S(2)}, u32[]{:S(2)}) collective-permute-start(bf16[576,512]{1,0:T(8,128)(2,1)} %collective-permute-done.34.refs_11_), channel_id=1, source_target_pairs={{0,16},{8,24},{12,28},{16,0},{28,12},{1,17},{9,25},{13,29},{17,1},... | collective-permute-start | bytes 1769480 | tf_op jit(solution)/shard_map/ppermute | solution.py:658
  218.1 3.3 %collective-permute-done.37.refs_15_ = bf16[576,512]{1,0:T(8,128)(2,1)} collective-permute-done((bf16[576,512]{1,0:T(8,128)(2,1)}, bf16[576,512]{1,0:T(8,128)(2,1)}, u32[]{:S(2)}, u32[]{:S(2)}) %collective-permute-start.37) | collective-permute-done | bytes 589856 | tf_op jit(solution)/shard_map/ppermute | solution.py:658
  226.2 7.9 %shard_map.119 = (f32[4,576,576]{2,1,0:T(8,128)}, f32[576,2048]{1,0:T(8,128)}) custom-call(s32[3]{0:T(128)} %pad_add_fusion.where_ref, f32[1,2048]{1,0:T(1,128)} %bitcast.89, bf16[512,2048]{1,0:T(8,128)(2,1)} %compare_convert_fusion.matches, bf16[576,512]{1,0:T(8,128)(2,1)} %copy-done.5, bf16[576,512]{1,0:T(8,128)(2,1)} %collective-permute-done.23.refs_1_, ...), custom_call_target="tpu_custom_call" | custom-call | flops 2566914048 | bytes 14155776 | tf_op jit(solution)/shard_map/pallas_call | solution.py:465
  (163 shorter events, 57.8 us)
Async XLA Ops:
  0.6 16.9 %collective-permute-start.4 = (s32[256]{0:T(256)}, s32[256]{0:T(256)S(1)}, u32[]{:S(2)}, u32[]{:S(2)}) collective-permute-start(s32[256]{0:T(256)} %param.10), channel_id=1, source_target_pairs={{0,16},{16,0},{1,17},{17,1},{2,18},{18,2},{3,19},{19,3},{4,20},{20... | collective-permute-start | bytes 3080 | tf_op jit(solution)/shard_map/ppermute | solution.py:169
  4.8 16.4 %collective-permute-start.5 = (f32[2,2,144]{2,1,0:T(2,128)S(1)}, f32[2,2,144]{2,1,0:T(2,128)S(1)}, u32[]{:S(2)}, u32[]{:S(2)}) collective-permute-start(f32[2,2,144]{2,1,0:T(2,128)S(1)} %pad_maximum_fusion.6), channel_id=1, source_target_pairs={{0,16},{16,0},{1,17},{17,1},{2,18},{18,2},{3,19},{19,3},{4,20},{20... | collective-permute-start | bytes 6920 | tf_op jit(solution)/shard_map/ppermute | solution.py:169
  4.9 16.3 %collective-permute-start.3 = (bf16[8,256]{1,0:T(8,128)(2,1)}, bf16[8,256]{1,0:T(8,128)(2,1)S(1)}, u32[]{:S(2)}, u32[]{:S(2)}) collective-permute-start(bf16[8,256]{1,0:T(8,128)(2,1)} %param.9), channel_id=1, source_target_pairs={{0,16},{16,0},{1,17},{17,1},{2,18},{18,2},{3,19},{19,3},{4,20},{20... | collective-permute-start | bytes 12296 | tf_op jit(solution)/shard_map/ppermute | solution.py:169
  9.5 14.2 %collective-permute-start.2 = (bf16[304,256]{1,0:T(8,128)(2,1)S(1)}, bf16[304,256]{1,0:T(8,128)(2,1)S(1)}, u32[]{:S(2)}, u32[]{:S(2)}) collective-permute-start(bf16[304,256]{1,0:T(8,128)(2,1)S(1)} %pad_maximum_fusion.4), channel_id=1, source_target_pairs={{0,12},{4,8},{8,4},{12,0},{1,13},{5,9},{9,5},{13,1},{2,14},{6,10},... | collective-permute-start | bytes 466952 | tf_op jit(solution)/shard_map/ppermute | solution.py:169
  36.9 19.6 %collective-permute-start.9 = (bf16[4,304,256]{2,1,0:T(8,128)(2,1)S(1)}, bf16[4,304,256]{2,1,0:T(8,128)(2,1)S(1)}, u32[]{:S(2)}, u32[]{:S(2)}) collective-permute-start(bf16[4,304,256]{2,1,0:T(8,128)(2,1)S(1)} %pad_maximum_fusion.1.refs_0_), channel_id=1, source_target_pairs={{0,2},{1,3},{2,0},{3,1},{4,6},{5,7},{6,4},{7,5},{8,10},{9,11},{10,... | collective-permute-start | bytes 1867784 | tf_op jit(solution)/shard_map/ppermute | solution.py:169
  38.5 17.3 %collective-permute-start.10 = (bf16[288,576]{1,0:T(8,128)(2,1)S(1)}, bf16[288,576]{1,0:T(8,128)(2,1)S(1)}, u32[]{:S(2)}, u32[]{:S(2)}) collective-permute-start(bf16[288,576]{1,0:T(8,128)(2,1)S(1)} %slice.48), channel_id=1, source_target_pairs={{0,8},{4,12},{8,0},{12,4},{1,9},{5,13},{9,1},{13,5},{2,10},{6,14},... | collective-permute-start | bytes 995336 | tf_op jit(solution)/shard_map/ppermute | solution.py:169
  38.6 39.7 %collective-permute-start.12 = (bf16[576,576]{1,0:T(8,128)(2,1)}, bf16[576,576]{1,0:T(8,128)(2,1)S(1)}, u32[]{:S(2)}, u32[]{:S(2)}) collective-permute-start(bf16[576,576]{1,0:T(8,128)(2,1)} %get-tuple-element.54), channel_id=1, source_target_pairs={{0,4},{4,0},{8,12},{12,8},{1,5},{5,1},{9,13},{13,9},{2,6},{6,2},{1... | collective-permute-start | bytes 1990664 | tf_op jit(solution)/shard_map/ppermute | solution.py:169
  41.0 17.4 %collective-permute-start.8 = (bf16[4,304,256]{2,1,0:T(8,128)(2,1)S(1)}, bf16[4,304,256]{2,1,0:T(8,128)(2,1)}, u32[]{:S(2)}, u32[]{:S(2)}) collective-permute-start(bf16[4,304,256]{2,1,0:T(8,128)(2,1)S(1)} %pad_maximum_fusion.1.refs_0_), channel_id=1, source_target_pairs={{0,1},{1,0},{2,3},{3,2},{4,5},{5,4},{6,7},{7,6},{8,9},{9,8},{10,11... | collective-permute-start | bytes 1867784 | tf_op jit(solution)/shard_map/ppermute | solution.py:169
  56.5 42.0 %collective-permute-start.14 = (bf16[576,576]{1,0:T(8,128)(2,1)}, bf16[576,576]{1,0:T(8,128)(2,1)S(1)}, u32[]{:S(2)}, u32[]{:S(2)}) collective-permute-start(bf16[576,576]{1,0:T(8,128)(2,1)} %get-tuple-element.57), channel_id=1, source_target_pairs={{0,12},{4,8},{8,4},{12,0},{1,13},{5,9},{9,5},{13,1},{2,14},{6,10},... | collective-permute-start | bytes 1990664 | tf_op jit(solution)/shard_map/ppermute | solution.py:169
  58.3 39.4 %collective-permute-start.13 = (bf16[144,576]{1,0:T(8,128)(2,1)}, bf16[144,576]{1,0:T(8,128)(2,1)S(1)}, u32[]{:S(2)}, u32[]{:S(2)}) collective-permute-start(bf16[144,576]{1,0:T(8,128)(2,1)} %get-tuple-element.92), channel_id=1, source_target_pairs={{0,8},{4,12},{8,0},{12,4},{1,9},{5,13},{9,1},{13,5},{2,10},{6,14},... | collective-permute-start | bytes 497672 | tf_op jit(solution)/shard_map/ppermute | solution.py:169
  62.9 37.5 %collective-permute-start.15 = (bf16[576,576]{1,0:T(8,128)(2,1)S(1)}, bf16[576,576]{1,0:T(8,128)(2,1)S(1)}, u32[]{:S(2)}, u32[]{:S(2)}) collective-permute-start(bf16[576,576]{1,0:T(8,128)(2,1)S(1)} %shard_map.112.refs_0_), channel_id=1, source_target_pairs={{0,1},{1,0},{2,3},{3,2},{4,5},{5,4},{6,7},{7,6},{8,9},{9,8},{10,11... | collective-permute-start | bytes 1990664 | tf_op jit(solution)/shard_map/ppermute | solution.py:169
  78.9 21.5 %collective-permute-start.16 = (bf16[576,576]{1,0:T(8,128)(2,1)S(1)}, bf16[576,576]{1,0:T(8,128)(2,1)S(1)}, u32[]{:S(2)}, u32[]{:S(2)}) collective-permute-start(bf16[576,576]{1,0:T(8,128)(2,1)S(1)} %shard_map.113.refs_1_), channel_id=1, source_target_pairs={{0,1},{1,0},{2,3},{3,2},{4,5},{5,4},{6,7},{7,6},{8,9},{9,8},{10,11... | collective-permute-start | bytes 1990664 | tf_op jit(solution)/shard_map/ppermute | solution.py:169
  104.7 15.5 %collective-permute-start.19 = (bf16[256,1152]{1,0:T(8,128)(2,1)S(1)}, bf16[256,1152]{1,0:T(8,128)(2,1)S(1)}, u32[]{:S(2)}, u32[]{:S(2)}) collective-permute-start(bf16[256,1152]{1,0:T(8,128)(2,1)S(1)} %get-tuple-element.58.mine), channel_id=1, source_target_pairs={{0,2},{1,3},{2,0},{3,1},{4,6},{5,7},{6,4},{7,5},{8,10},{9,11},{10,... | collective-permute-start | bytes 1769480 | tf_op jit(solution)/shard_map/ppermute | solution.py:169
  124.1 14.6 %collective-permute-start.20 = (bf16[256,1152]{1,0:T(8,128)(2,1)S(1)}, bf16[256,1152]{1,0:T(8,128)(2,1)S(1)}, u32[]{:S(2)}, u32[]{:S(2)}) collective-permute-start(bf16[256,1152]{1,0:T(8,128)(2,1)S(1)} %get-tuple-element.60.mine), channel_id=1, source_target_pairs={{0,2},{1,3},{2,0},{3,1},{4,6},{5,7},{6,4},{7,5},{8,10},{9,11},{10,... | collective-permute-start | bytes 1769480 | tf_op jit(solution)/shard_map/ppermute | solution.py:169
  143.5 21.7 %collective-permute-start.28 = (bf16[576,512]{1,0:T(8,128)(2,1)S(1)}, bf16[576,512]{1,0:T(8,128)(2,1)S(1)}, u32[]{:S(2)}, u32[]{:S(2)}) collective-permute-start(bf16[576,512]{1,0:T(8,128)(2,1)S(1)} %maximum_select_fusion.refs_8_), channel_id=1, source_target_pairs={{0,4},{4,0},{12,8},{16,20},{28,24},{1,5},{5,1},{13,9},{17,21},{29,... | collective-permute-start | bytes 1769480 | tf_op jit(solution)/shard_map/ppermute | solution.py:649
  145.4 31.2 %collective-permute-start.22 = (bf16[576,512]{1,0:T(8,128)(2,1)S(1)}, bf16[576,512]{1,0:T(8,128)(2,1)}, u32[]{:S(2)}, u32[]{:S(2)}) collective-permute-start(bf16[576,512]{1,0:T(8,128)(2,1)S(1)} %maximum_select_fusion.refs_8_), channel_id=1, source_target_pairs={{8,0},{9,5},{11,15},{24,16},{25,21},{27,31}} | collective-permute-start | bytes 1769480 | tf_op jit(solution)/shard_map/ppermute | solution.py:666
  146.7 35.8 %collective-permute-start.27 = (bf16[576,512]{1,0:T(8,128)(2,1)S(1)}, bf16[576,512]{1,0:T(8,128)(2,1)S(1)}, u32[]{:S(2)}, u32[]{:S(2)}) collective-permute-start(bf16[576,512]{1,0:T(8,128)(2,1)S(1)} %maximum_select_fusion.refs_8_), channel_id=1, source_target_pairs={{0,16},{4,20},{12,28},{16,0},{28,12},{1,17},{5,21},{13,29},{17,1},... | collective-permute-start | bytes 1769480 | tf_op jit(solution)/shard_map/ppermute | solution.py:658
  149.5 33.0 %collective-permute-start.26 = (bf16[576,512]{1,0:T(8,128)(2,1)S(1)}, bf16[576,512]{1,0:T(8,128)(2,1)S(1)}, u32[]{:S(2)}, u32[]{:S(2)}) collective-permute-start(bf16[576,512]{1,0:T(8,128)(2,1)S(1)} %maximum_select_fusion.refs_8_), channel_id=1, source_target_pairs={{0,8},{4,12},{12,4},{16,24},{28,20},{1,9},{5,13},{13,5},{17,25},{2... | collective-permute-start | bytes 1769480 | tf_op jit(solution)/shard_map/ppermute | solution.py:649
  165.1 17.4 %collective-permute-start.29 = (bf16[576,512]{1,0:T(8,128)(2,1)S(1)}, bf16[576,512]{1,0:T(8,128)(2,1)S(1)}, u32[]{:S(2)}, u32[]{:S(2)}) collective-permute-start(bf16[576,512]{1,0:T(8,128)(2,1)S(1)} %collective-permute-done.28.refs_9_), channel_id=1, source_target_pairs={{0,16},{4,20},{8,24},{20,4},{24,8},{1,17},{5,21},{9,25},{21,5},{25... | collective-permute-start | bytes 1769480 | tf_op jit(solution)/shard_map/ppermute | solution.py:658
  190.3 15.0 %collective-permute-start.34 = (bf16[576,512]{1,0:T(8,128)(2,1)S(1)}, bf16[576,512]{1,0:T(8,128)(2,1)}, u32[]{:S(2)}, u32[]{:S(2)}) collective-permute-start(bf16[576,512]{1,0:T(8,128)(2,1)S(1)} %collective-permute-done.26.refs_10_), channel_id=1, source_target_pairs={{4,0},{8,12},{12,8},{20,16},{24,28},{5,1},{9,13},{13,9},{21,17},{2... | collective-permute-start | bytes 1769480 | tf_op jit(solution)/shard_map/ppermute | solution.py:649
  192.9 19.4 %collective-permute-start.24 = (bf16[576,512]{1,0:T(8,128)(2,1)S(1)}, bf16[576,512]{1,0:T(8,128)(2,1)}, u32[]{:S(2)}, u32[]{:S(2)}) collective-permute-start(bf16[576,512]{1,0:T(8,128)(2,1)S(1)} %broadcast_select_fusion.refs_0_), channel_id=1, source_target_pairs={{0,2},{5,7},{10,8},{15,13},{16,18},{21,23},{26,24},{31,29}} | collective-permute-start | bytes 1769480 | tf_op jit(solution)/shard_map/ppermute | solution.py:674
  195.0 19.5 %collective-permute-start.33 = (bf16[576,512]{1,0:T(8,128)(2,1)}, bf16[576,512]{1,0:T(8,128)(2,1)}, u32[]{:S(2)}, u32[]{:S(2)}) collective-permute-start(bf16[576,512]{1,0:T(8,128)(2,1)} %collective-permute-done.30.refs_4_), channel_id=1, source_target_pairs={{0,2},{5,7},{10,8},{15,13},{16,18},{21,23},{26,24},{31,29}} | collective-permute-start | bytes 1769480 | tf_op jit(solution)/shard_map/ppermute | solution.py:674
  205.3 16.0 %collective-permute-start.37 = (bf16[576,512]{1,0:T(8,128)(2,1)}, bf16[576,512]{1,0:T(8,128)(2,1)}, u32[]{:S(2)}, u32[]{:S(2)}) collective-permute-start(bf16[576,512]{1,0:T(8,128)(2,1)} %collective-permute-done.34.refs_11_), channel_id=1, source_target_pairs={{0,16},{8,24},{12,28},{16,0},{28,12},{1,17},{9,25},{13,29},{17,1},... | collective-permute-start | bytes 1769480 | tf_op jit(solution)/shard_map/ppermute | solution.py:658
  212.3 13.8 %collective-permute-start.23 = (bf16[576,512]{1,0:T(8,128)(2,1)S(1)}, bf16[576,512]{1,0:T(8,128)(2,1)}, u32[]{:S(2)}, u32[]{:S(2)}) collective-permute-start(bf16[576,512]{1,0:T(8,128)(2,1)S(1)} %broadcast_select_fusion.refs_0_), channel_id=1, source_target_pairs={{0,1},{5,4},{10,11},{15,14},{16,17},{21,20},{26,27},{31,30}} | collective-permute-start | bytes 1769480 | tf_op jit(solution)/shard_map/ppermute | solution.py:679
  (40 other events, 661.8 us)

commit v14 on v13

--- a/solution.py
+++ b/solution.py
@@ -390,76 +390,76 @@
 
 
 def output_kernel(where_ref, scale, matches, *refs):
-    lefts, mine, others = (refs[:4], refs[4:8]), refs[8:12], refs[12:16]
-    attn, embed = refs[16:18]
-    left_held, held, found, attn_made, embed_made, sems, out_sems = refs[18:]
-    shard, layer, turn = where_ref[0], where_ref[1], where_ref[2]
-    first = shard == 0
-    rows, tokens_all = held.shape[1:]
-
-    found_copy = pltpu.make_async_copy(matches, found, sems.at[7])
-    for slot in range(2):
-        for group in range(2):
+    lefts, rights, refs = refs[:4], refs[4:8], refs[-9:]
+    attn, embed, left_held, held, found, attn_made, embed_made, sems, out_sems = refs
+    owner, layer, turn = where_ref[0], where_ref[1], where_ref[2]
+    rows = held.shape[1]
+
+    for place in range(4):
+
+        @pl.when(turn == place)
+        def _():
+            pltpu.make_async_copy(lefts[place].at[pl.ds(0, rows)], left_held, sems.at[4]).start()
+
+    def fetch(sources):
+        for slot, source in enumerate(sources):
             for place in range(4):
 
-                @pl.when((turn == place) & (((shard ^ slot) == group)))
+                @pl.when((layer ^ source) == place)
                 def _():
-                    source = lefts[group][place].at[pl.ds(0, rows)]
-                    pltpu.make_async_copy(source, left_held.at[slot], sems.at[5 + slot]).start()
-
-        if slot == 0:
-            for index, source in enumerate((0, 1, 3, 0, 3)):
-                from_mine = first if index < 3 else jnp.logical_not(first)
-                for place in range(4):
-                    for group, wanted in ((mine, from_mine), (others, jnp.logical_not(from_mine))):
-
-                        @pl.when(wanted & ((layer ^ source) == place))
-                        def _():
-                            pltpu.make_async_copy(
-                                group[place], held.at[index], sems.at[index]
-                            ).start()
-
-            found_copy.start()
+                    pltpu.make_async_copy(rights[place], held.at[slot], sems.at[slot]).start()
+
+    def left_arrived():
+        pltpu.make_async_copy(left_held, left_held, sems.at[4]).wait()
 
     def arrived(slot):
-        target = held.at[slot] if slot < 5 else left_held.at[slot - 5]
-        pltpu.make_async_copy(mine[0], target, sems.at[slot]).wait()
-
-    results = []
-    arrived(5)
-    for slot in range(4):
-        if slot == 3:
-            arrived(6)
-        arrived(slot)
+        pltpu.make_async_copy(held.at[slot], held.at[slot], sems.at[slot]).wait()
+        return held[slot]
+
+    def send_product(slot, target):
         attn_made[slot] = learning_rate * lax.dot_general(
-            left_held[slot // 3],
-            held[slot],
+            left_held[...],
+            arrived(slot),
             (((1,), (1,)), ((), ())),
             preferred_element_type=jnp.float32,
         )
-        results.append(
-            pltpu.make_async_copy(attn_made.at[slot], attn.at[slot], out_sems.at[slot])
-        )
-        results[-1].start()
-    arrived(4)
-    found_copy.wait()
-    part = found.shape[1] // 4
-    for index in range(4):
-        cols = pl.ds(index * part, part)
-        product = jnp.dot(held[4], found[:, cols], preferred_element_type=jnp.float32)
-        embed_made[:, cols] = product * scale[:, cols]
-        results.append(
-            pltpu.make_async_copy(
-                embed_made.at[:, cols], embed.at[:, cols], out_sems.at[4 + index]
+        copy = pltpu.make_async_copy(attn_made.at[slot], attn.at[target], out_sems.at[slot])
+        copy.start()
+        return copy
+
+    @pl.when(owner == 0)
+    def _():
+        fetch((0, 1, 3))
+        left_arrived()
+        for copy in [send_product(slot, slot) for slot in range(3)]:
+            copy.wait()
+
+    @pl.when(owner == 1)
+    def _():
+        fetch((0, 3))
+        found_copy = pltpu.make_async_copy(matches, found, sems.at[5])
+        found_copy.start()
+        left_arrived()
+        results = [send_product(0, 3)]
+        right = arrived(1)
+        found_copy.wait()
+        part = found.shape[1] // 4
+        for index in range(4):
+            cols = pl.ds(index * part, part)
+            product = jnp.dot(right, found[:, cols], preferred_element_type=jnp.float32)
+            embed_made[:, cols] = product * scale[:, cols]
+            results.append(
+                pltpu.make_async_copy(
+                    embed_made.at[:, cols], embed.at[:, cols], out_sems.at[3 + index]
+                )
             )
-        )
-        results[-1].start()
-    for result in results:
-        result.wait()
-
-
-def output_products(where, scale, matches, lefts, mine, others):
-    cols, tokens_all = mine[0].shape
+            results[-1].start()
+        for copy in results:
+            copy.wait()
+
+
+def output_products(where, scale, matches, lefts, rights, made):
+    cols, tokens_all = rights[0].shape
     vocab_block = scale.shape[1]
     anywhere = pl.BlockSpec(memory_space=pl.ANY)
     return pl.pallas_call(
@@ -468,28 +468,29 @@
             pl.BlockSpec(memory_space=pltpu.SMEM),
             pl.BlockSpec(memory_space=pltpu.VMEM),
         ]
-        + [anywhere] * 17,
+        + [anywhere] * (9 + len(made)),
         out_specs=(anywhere, anywhere),
         out_shape=(
             jax.ShapeDtypeStruct((4, cols, cols), jnp.float32),
             jax.ShapeDtypeStruct((cols, vocab_block), jnp.float32),
         ),
+        input_output_aliases={11: 0, 12: 1} if made else {},
         scratch_shapes=[
-            pltpu.VMEM((2, cols, tokens_all), jnp.bfloat16),
-            pltpu.VMEM((5, cols, tokens_all), jnp.bfloat16),
+            pltpu.VMEM((cols, tokens_all), jnp.bfloat16),
+            pltpu.VMEM((3, cols, tokens_all), jnp.bfloat16),
             pltpu.VMEM((tokens_all, vocab_block), jnp.bfloat16),
-            pltpu.VMEM((4, cols, cols), jnp.float32),
+            pltpu.VMEM((3, cols, cols), jnp.float32),
             pltpu.VMEM((cols, vocab_block), jnp.float32),
-            pltpu.SemaphoreType.DMA((8,)),
-            pltpu.SemaphoreType.DMA((8,)),
+            pltpu.SemaphoreType.DMA((6,)),
+            pltpu.SemaphoreType.DMA((7,)),
         ],
         compiler_params=pltpu.CompilerParams(vmem_limit_bytes=60 * 1024 * 1024),
         cost_estimate=pl.CostEstimate(
-            flops=2 * cols * tokens_all * (4 * cols + vocab_block),
-            bytes_accessed=4 * cols * (4 * cols + vocab_block) + 14 * cols * tokens_all,
+            flops=6 * cols * cols * tokens_all,
+            bytes_accessed=12 * cols * cols + 8 * cols * tokens_all,
             transcendentals=0,
         ),
-    )(where, scale, matches, *lefts[0], *lefts[1], *mine, *others)
+    )(where, scale, matches, *lefts, *rights, *made)
 
 
 def layer_plan(
@@ -541,10 +542,14 @@
         )
         collected.append(swap(message, "tensor", n_tensor, step) if step else message)
     collected = jnp.stack(collected)
-    lows = [
-        by_index(old_factors, held_by(layer ^ step)).astype(jnp.bfloat16)
-        for step in range(n_tensor)
-    ]
+
+    def old_block(factors, step):
+        return by_index(factors, held_by(layer ^ step)).astype(jnp.bfloat16)
+
+    far_block = swap(old_block(old_factors, 2), "tensor", n_tensor, 2)
+    later_factors = lax.optimization_barrier(old_factors)
+    near_block = swap(old_block(later_factors, 1), "tensor", n_tensor, 1)
+    here_block, farthest = old_block(later_factors, 0), old_block(later_factors, 3)
 
     def both_shards(value, axis):
         other = swap(value, "shard", n_shard, 1)
@@ -575,34 +580,25 @@
         "en,ef->fn", grad_all, router_inverse, preferred_element_type=jnp.float32
     ).astype(jnp.bfloat16)
 
-    collected, lows, small = lax.optimization_barrier(
-        (collected, lows, (router_right, matches, embed_scale, norm_sums))
+    other_tokens = swap(collected[:, features_dev : 2 * features_dev], "shard", n_shard, 1)
+    small = (router_right, matches, embed_scale, norm_sums)
+    other_tokens, collected, far_block, near_block, here_block, farthest, small = (
+        lax.optimization_barrier(
+            (other_tokens, collected, far_block, near_block, here_block, farthest, small)
+        )
     )
     router_right, matches, embed_scale, norm_sums = small
-    other_tokens = swap(collected[:, features_dev : 2 * features_dev], "shard", n_shard, 1)
-    quarter = row_block // 4
-
-    def portion(step, start, stop):
-        return swap(lows[step][start:stop], "tensor", n_tensor, step)
-
-    near_rows = portion(2, 0, quarter)
-    other_tokens, near_rows = lax.optimization_barrier((other_tokens, near_rows))
     collected = jnp.concatenate(
         [collected[:, :features_dev], other_tokens, collected[:, 2 * features_dev :]], axis=1
     )
     by_side = swap(collected, "section", n_section, 2)
     by_core = swap(collected, "section", n_section, 1)
-    middle_rows = portion(2, quarter, 3 * quarter)
-    by_side, middle_rows = lax.optimization_barrier((by_side, middle_rows))
+    part_rows = row_block // 2
+    farthest_1 = swap(farthest[:part_rows], "tensor", n_tensor, 3)
+    by_side, farthest_1 = lax.optimization_barrier((by_side, farthest_1))
     by_both = swap(by_side, "section", n_section, 1)
-    far_block = portion(3, 0, row_block)
-    last_rows = portion(2, 3 * quarter, row_block)
-    blocks = [
-        (lows[0],),
-        (portion(1, 0, row_block),),
-        (near_rows, middle_rows, last_rows),
-        (far_block,),
-    ]
+    farthest_2 = swap(farthest[part_rows:], "tensor", n_tensor, 3)
+    blocks = [(here_block,), (near_block,), (far_block,), (farthest_1, farthest_2)]
 
     features, rows, low_diag, trace = lay_out(
         jnp.stack([own_place, layer, core, section]),
@@ -717,23 +713,31 @@
     over_3 = across(near_3, 3)
     router_cols = jnp.where(shard == 1, router_cols, router_there)
     router_side, router_core = to_side(router_cols), to_core(router_cols)
-    side_there, over_3, router_side, router_core = lax.optimization_barrier(
-        (to_side(left_there), over_3, router_side, router_core)
+    turn = section ^ layer
+    made = output_products(
+        jnp.stack([shard, layer, turn]),
+        embed_scale,
+        matches,
+        lefts_here,
+        (own, near_1, near_2, near_3),
+        (),
+    )
+    side_there, over_3, router_side, router_core, made = lax.optimization_barrier(
+        (to_side(left_there), over_3, router_side, router_core, made)
     )
     lefts_there = (left_there, to_core(left_there), side_there, to_far(side_there))
     routers = (router_cols, router_core, router_side, to_far(router_side))
-    turn = section ^ layer
     precond_router = routers[3]
     for index in (2, 1, 0):
         precond_router = jnp.where(turn == index, routers[index], precond_router)
 
     precond_attn, embed_columns = output_products(
-        jnp.stack([shard, layer, turn]),
+        jnp.stack([1 - shard, layer, turn]),
         embed_scale,
         matches,
-        (lefts_here, lefts_there),
-        (own, near_1, near_2, near_3),
+        lefts_there,
         (over_0, over_1, over_2, over_3),
+        made,
     )
     precond_embed = embed_columns.T
 

time: 235 us -> 228 us (0.970)
  waiting for transfers between devices: 132 us -> 108 us
  starting transfers between devices: 54.6 us -> 64.6 us
  Pallas kernels: 23.8 us -> 28 us
  local copies, waits for them, and re-layouts: 7.2 us -> 10.3 us
    ppermute x22 -> x21, waiting for transfers between devices: 91.7 us -> 74.2 us  [swap(): return lax.ppermute(value, axis, [(i, i ^ step) for i in range(size)])]
    ppermute x3, waiting for transfers between devices: 19.5 us -> 9.99 us  [send(): return lax.ppermute(value, axes, moves)]
    ppermute x4, waiting for transfers between devices: 3.29 us -> 10.5 us  [across(): return lax.ppermute(value, axes, moves)]
    ppermute x1, waiting for transfers between devices: 7.03 us -> 0.01 us  [layer_plan(): lax.ppermute(left_here, everywhere, [(spot(x, t, t), spot(1 - x, t, t)) f...]
    ppermute x3, starting transfers between devices: 7.38 us -> 13.1 us  [send(): return lax.ppermute(value, axes, moves)]
    ppermute x22 -> x21, starting transfers between devices: 18.3 us -> 23.2 us  [swap(): return lax.ppermute(value, axis, [(i, i ^ step) for i in range(size)])]
    ppermute x1, waiting for transfers between devices: 0.17 us -> 4.59 us  [layer_plan(): lax.ppermute(router_cols, everywhere, [(spot(1, t, t), spot(0, t, t)) for...]
    pallas_call x1 -> x2, Pallas kernels: 7.86 us -> 11.1 us  [output_products(): pl.pallas_call(output_kernel, in_specs=[pl.BlockSpec(memory_space=pltpu.S...]
  transfers between devices with their start and end apart: 42 -> 41, of which waited for: 17 -> 15; matrix products, arithmetic and copies ran while one was open for 8% -> 10% of each run, Pallas kernels for 3% -> 6%
where the time goes in v14:
time: 228 us; the launch traced here: 227 us
  waiting for transfers between devices  108 us (47%)
  starting transfers between devices  64.6 us (28%)
  Pallas kernels  28 us (12%)
  other arithmetic  12.6 us (6%)
  local copies, waits for them, and re-layouts  10.3 us (5%)
  between operations  2.82 us (1%)
    ppermute x21, waiting for transfers between devices, swap(): return lax.ppermute(value, axis, [(i, i ^ step) for i in range(size)])  74.2 us
    ppermute x21, starting transfers between devices, swap(): return lax.ppermute(value, axis, [(i, i ^ step) for i in range(size)])  23.2 us
    ppermute x3, starting transfers between devices, send(): return lax.ppermute(value, axes, moves)  13.1 us
    pallas_call x2, Pallas kernels, output_products(): pl.pallas_call(output_kernel, in_specs=[pl.BlockSpec(memory_space=pltpu.S...  11.1 us
    ppermute x4, waiting for transfers between devices, across(): return lax.ppermute(value, axes, moves)  10.5 us
    ppermute x3, waiting for transfers between devices, send(): return lax.ppermute(value, axes, moves)  9.99 us
    pallas_call x3, Pallas kernels, chain_call(): pl.pallas_call(kernel, in_specs=[pl.BlockSpec(memory_space=pltpu.SMEM)] *...  9.74 us
    ppermute x1, waiting for transfers between devices, scatter(): lax.ppermute(value, everywhere, [(spot(x, source, s), spot(x, s, s)) for...  8.37 us
  transfers between devices with their start and end apart: 41, of which 15 were waited for; matrix products, arithmetic and copies ran while one was open for 10% of the time, Pallas kernels for 6%

profile of v14, /device:TPU:0, one launch (start us, length us, event | category | flops | bytes accessed | tf_op | source)
XLA Modules:
  0.0 227.3 jit_solution(9051965847230498869)
XLA Ops:
  0.6 3.0 %collective-permute-start.7 = (s32[256]{0:T(256)}, s32[256]{0:T(256)S(1)}, u32[]{:S(2)}, u32[]{:S(2)}) collective-permute-start(s32[256]{0:T(256)} %param.10), channel_id=1, source_target_pairs={{0,16},{16,0},{1,17},{17,1},{2,18},{18,2},{3,19},{19,3},{4,20},{20... | collective-permute-start | bytes 3080 | tf_op jit(solution)/shard_map/ppermute | solution.py:169
  9.5 3.7 %collective-permute-start.2 = (bf16[304,256]{1,0:T(8,128)(2,1)S(1)}, bf16[304,256]{1,0:T(8,128)(2,1)S(1)}, u32[]{:S(2)}, u32[]{:S(2)}) collective-permute-start(bf16[304,256]{1,0:T(8,128)(2,1)S(1)} %pad_maximum_fusion.4), channel_id=1, source_target_pairs={{0,12},{4,8},{8,4},{12,0},{1,13},{5,9},{9,5},{13,1},{2,14},{6,10},... | collective-permute-start | bytes 466952 | tf_op jit(solution)/shard_map/ppermute | solution.py:169
  15.6 3.6 %fusion.6 = (bf16[576,576]{1,0:T(8,128)(2,1)}, bf16[576,576]{1,0:T(8,128)(2,1)S(1)}, bf16[576,576]{1,0:T(8,128)(2,1)}) fusion(f32[4,576,576]{2,1,0:T(8,128)} %param.12, s32[]{:T(128)S(6)} %select_n.152, s32[]{:T(128)S(6)} %select_n.140, s32[]{:T(128)S(6)} %select_n.144), kind=kLoop, calls=%fused_computation.18 | loop fusion | bytes 3981324 | tf_op jit(solution)/shard_map/convert_element_type | solution.py:547
  29.2 16.1 %collective-permute-done.1 = bf16[304,256]{1,0:T(8,128)(2,1)S(1)} collective-permute-done((bf16[304,256]{1,0:T(8,128)(2,1)S(1)}, bf16[304,256]{1,0:T(8,128)(2,1)S(1)}, u32[]{:S(2)}, u32[]{:S(2)}) %collective-permute-start.1) | collective-permute-done | bytes 155680 | tf_op jit(solution)/shard_map/ppermute | solution.py:169
  46.5 5.8 %collective-permute-done.3 = bf16[4,144,256]{2,1,0:T(8,128)(2,1)S(1)} collective-permute-done((bf16[4,144,256]{2,1,0:T(8,128)(2,1)S(1)}, bf16[4,144,256]{2,1,0:T(8,128)(2,1)S(1)}, u32[]{:S(2)}, u32[]{:S(2)}) %collective-permute-start.3) | collective-permute-done | bytes 294944 | tf_op jit(solution)/shard_map/ppermute | solution.py:169
  52.3 7.6 %collective-permute-done.4.refs_0_ = bf16[576,576]{1,0:T(8,128)(2,1)S(1)} collective-permute-done((bf16[576,576]{1,0:T(8,128)(2,1)}, bf16[576,576]{1,0:T(8,128)(2,1)S(1)}, u32[]{:S(2)}, u32[]{:S(2)}) %collective-permute-start.4) | collective-permute-done | bytes 663584 | tf_op jit(solution)/shard_map/ppermute | solution.py:169
  64.9 9.5 %collective-permute-done.11.refs_0_ = bf16[288,576]{1,0:T(8,128)(2,1)S(1)} collective-permute-done((bf16[288,576]{1,0:T(8,128)(2,1)S(1)}, bf16[288,576]{1,0:T(8,128)(2,1)S(1)}, u32[]{:S(2)}, u32[]{:S(2)}) %collective-permute-start.11) | collective-permute-done | bytes 331808 | tf_op jit(solution)/shard_map/ppermute | solution.py:169
  77.3 3.6 %shard_map.111 = (bf16[2,2304,256]{2,1,0:T(8,128)(2,1)S(1)}, bf16[256,2304]{1,0:T(8,128)(2,1)S(1)}, f32[4,1,576]{2,1,0:T(1,128)S(1)}, f32[1]{0:T(128)}) custom-call(s32[4]{0:T(128)S(1)} %pad_add_fusion.place_ref, bf16[4,304,256]{2,1,0:T(8,128)(2,1)S(1)} %pad_maximum_fusion.1.refs_0_, bf16[4,304,256]{2,1,0:T(8,128)(2,1)} %collective-permute-done.9.refs_1_, ...), custom_call_target="tpu_custom_call" | custom-call | flops 37748736 | bytes 8257536 | tf_op jit(solution)/shard_map/pallas_call | solution.py:241
  83.7 4.6 %collective-permute-done.13.refs_1_ = bf16[288,576]{1,0:T(8,128)(2,1)} collective-permute-done((bf16[288,576]{1,0:T(8,128)(2,1)}, bf16[288,576]{1,0:T(8,128)(2,1)}, u32[]{:S(2)}, u32[]{:S(2)}) %collective-permute-start.13) | collective-permute-done | bytes 331808 | tf_op jit(solution)/shard_map/ppermute | solution.py:169
  92.3 2.9 %shard_map.116 = (f32[2,256,576]{2,1,0:T(8,128)S(1)}, bf16[256,1152]{1,0:T(8,128)(2,1)S(1)}) custom-call(s32[1]{0:T(128)} %bitcast.2.place_ref, f32[1]{0:T(128)S(6)} %div.22.scale_ref, bf16[256,2304]{1,0:T(8,128)(2,1)S(1)} %get-tuple-element.53.rows, f32[4,1,576]{2,1,0:T(1,128)S(1)} %get-tuple-element.54.diag, bf16[576,576]{1,0:T(8,128)(2,1)S(1)} %shard_map.112.refs_0_, ...), custom_call_target="tpu_custom_call" | custom-call | flops 1358954496 | bytes 5308416 | tf_op jit(solution)/shard_map/pallas_call | solution.py:376
  96.4 14.2 %collective-permute-done.18.theirs = bf16[256,1152]{1,0:T(8,128)(2,1)S(1)} collective-permute-done((bf16[256,1152]{1,0:T(8,128)(2,1)S(1)}, bf16[256,1152]{1,0:T(8,128)(2,1)S(1)}, u32[]{:S(2)}, u32[]{:S(2)}) %collective-permute-start.18) | collective-permute-done | bytes 589856 | tf_op jit(solution)/shard_map/ppermute | solution.py:169
  110.6 4.0 %shard_map.117 = (f32[2,256,576]{2,1,0:T(8,128)S(1)}, bf16[256,1152]{1,0:T(8,128)(2,1)S(1)}) custom-call(s32[1]{0:T(128)} %bitcast.2.place_ref, f32[1]{0:T(128)S(6)} %div.22.scale_ref, bf16[256,1152]{1,0:T(8,128)(2,1)S(1)} %get-tuple-element.60.mine, bf16[256,1152]{1,0:T(8,128)(2,1)S(1)} %collective-permute-done.18.theirs, ...), custom_call_target="tpu_custom_call" | custom-call | flops 1358954496 | bytes 5308416 | tf_op jit(solution)/shard_map/pallas_call | solution.py:376
  115.8 13.4 %collective-permute-done.19.theirs = bf16[256,1152]{1,0:T(8,128)(2,1)S(1)} collective-permute-done((bf16[256,1152]{1,0:T(8,128)(2,1)S(1)}, bf16[256,1152]{1,0:T(8,128)(2,1)S(1)}, u32[]{:S(2)}, u32[]{:S(2)}) %collective-permute-start.19) | collective-permute-done | bytes 589856 | tf_op jit(solution)/shard_map/ppermute | solution.py:169
  129.2 2.9 %shard_map.118 = (bf16[576,256]{1,0:T(8,128)(2,1)S(1)}, bf16[576,256]{1,0:T(8,128)(2,1)S(1)}) custom-call(s32[1]{0:T(128)} %bitcast.2.place_ref, f32[1]{0:T(128)S(6)} %div.22.scale_ref, bf16[256,1152]{1,0:T(8,128)(2,1)S(1)} %get-tuple-element.62.mine, bf16[256,1152]{1,0:T(8,128)(2,1)S(1)} %collective-permute-done.19.theirs, ...), custom_call_target="tpu_custom_call" | custom-call | flops 1358954496 | bytes 5308416 | tf_op jit(solution)/shard_map/pallas_call | solution.py:376
  135.2 9.7 %collective-permute-start.23 = (bf16[576,512]{1,0:T(8,128)(2,1)S(1)}, bf16[576,512]{1,0:T(8,128)(2,1)S(1)}, u32[]{:S(2)}, u32[]{:S(2)}) collective-permute-start(bf16[576,512]{1,0:T(8,128)(2,1)S(1)} %maximum_select_fusion.refs_4_), channel_id=1, source_target_pairs={{0,4},{4,0},{12,8},{16,20},{28,24},{1,5},{5,1},{13,9},{17,21},{29,... | collective-permute-start | bytes 1769480 | tf_op jit(solution)/shard_map/ppermute | solution.py:645
  144.9 2.5 %collective-permute-start.22 = (bf16[576,512]{1,0:T(8,128)(2,1)S(1)}, bf16[576,512]{1,0:T(8,128)(2,1)S(1)}, u32[]{:S(2)}, u32[]{:S(2)}) collective-permute-start(bf16[576,512]{1,0:T(8,128)(2,1)S(1)} %maximum_select_fusion.refs_4_), channel_id=1, source_target_pairs={{0,16},{4,20},{12,28},{16,0},{28,12},{1,17},{5,21},{13,29},{17,1},... | collective-permute-start | bytes 1769480 | tf_op jit(solution)/shard_map/ppermute | solution.py:654
  149.5 8.4 %collective-permute-done.25 = bf16[576,512]{1,0:T(8,128)(2,1)S(1)} collective-permute-done((bf16[576,512]{1,0:T(8,128)(2,1)S(1)}, bf16[576,512]{1,0:T(8,128)(2,1)S(1)}, u32[]{:S(2)}, u32[]{:S(2)}) %collective-permute-start.25) | collective-permute-done | bytes 589856 | tf_op jit(solution)/shard_map/ppermute | solution.py:662
  160.4 4.4 %collective-permute-done.23.refs_5_ = bf16[576,512]{1,0:T(8,128)(2,1)S(1)} collective-permute-done((bf16[576,512]{1,0:T(8,128)(2,1)S(1)}, bf16[576,512]{1,0:T(8,128)(2,1)S(1)}, u32[]{:S(2)}, u32[]{:S(2)}) %collective-permute-start.23) | collective-permute-done | bytes 589856 | tf_op jit(solution)/shard_map/ppermute | solution.py:645
  171.7 8.7 %collective-permute-done.24.refs_5_ = bf16[576,512]{1,0:T(8,128)(2,1)S(1)} collective-permute-done((bf16[576,512]{1,0:T(8,128)(2,1)S(1)}, bf16[576,512]{1,0:T(8,128)(2,1)S(1)}, u32[]{:S(2)}, u32[]{:S(2)}) %collective-permute-start.24) | collective-permute-done | bytes 589856 | tf_op jit(solution)/shard_map/ppermute | solution.py:654
  187.3 4.6 %collective-permute-done.32 = f32[8,576]{1,0:T(8,128)S(1)} collective-permute-done((f32[8,576]{1,0:T(8,128)}, f32[8,576]{1,0:T(8,128)S(1)}, u32[]{:S(2)}, u32[]{:S(2)}) %collective-permute-start.32) | collective-permute-done | bytes 18464 | tf_op jit(solution)/shard_map/ppermute | solution.py:709
  194.0 5.6 %collective-permute-done.30.refs_7_ = bf16[576,512]{1,0:T(8,128)(2,1)} collective-permute-done((bf16[576,512]{1,0:T(8,128)(2,1)}, bf16[576,512]{1,0:T(8,128)(2,1)}, u32[]{:S(2)}, u32[]{:S(2)}) %collective-permute-start.30) | collective-permute-done | bytes 589856 | tf_op jit(solution)/shard_map/ppermute | solution.py:645
  199.6 3.6 %collective-permute-start.33 = (bf16[576,512]{1,0:T(8,128)(2,1)}, bf16[576,512]{1,0:T(8,128)(2,1)}, u32[]{:S(2)}, u32[]{:S(2)}) collective-permute-start(bf16[576,512]{1,0:T(8,128)(2,1)} %collective-permute-done.30.refs_7_), channel_id=1, source_target_pairs={{0,16},{8,24},{12,28},{16,0},{28,12},{1,17},{9,25},{13,29},{17,1},... | collective-permute-start | bytes 1769480 | tf_op jit(solution)/shard_map/ppermute | solution.py:654
  209.4 5.5 %shard_map.119 = (f32[4,576,576]{2,1,0:T(8,128)}, f32[576,2048]{1,0:T(8,128)}) custom-call(s32[3]{0:T(128)} %add_add_fusion.1.where_ref, f32[1,2048]{1,0:T(1,128)} %bitcast.91, bf16[512,2048]{1,0:T(8,128)(2,1)} %compare_convert_fusion.matches, bf16[576,512]{1,0:T(8,128)(2,1)} %copy-done.3, bf16[576,512]{1,0:T(8,128)(2,1)} %collective-permute-done.36.refs_1_, ...), custom_call_target="tpu_custom_call" | custom-call | flops 1019215872 | bytes 6340608 | tf_op jit(solution)/shard_map/pallas_call | solution.py:465
  221.5 5.6 %shard_map.120 = (f32[4,576,576]{2,1,0:T(8,128)}, f32[576,2048]{1,0:T(8,128)}) custom-call(s32[3]{0:T(128)} %add_add_fusion.where_ref, f32[1,2048]{1,0:T(1,128)} %bitcast.92, bf16[512,2048]{1,0:T(8,128)(2,1)} %compare_convert_fusion.matches, bf16[576,512]{1,0:T(8,128)(2,1)} %copy-done.5, ...), custom_call_target="tpu_custom_call", output_to_operand_aliasing={{0}: (11, {}), {1}: (12, {})} | custom-call | flops 1019215872 | bytes 6340608 | tf_op jit(solution)/shard_map/pallas_call | solution.py:465
  (160 shorter events, 71.4 us)
Async XLA Ops:
  0.6 18.7 %collective-permute-start.7 = (s32[256]{0:T(256)}, s32[256]{0:T(256)S(1)}, u32[]{:S(2)}, u32[]{:S(2)}) collective-permute-start(s32[256]{0:T(256)} %param.10), channel_id=1, source_target_pairs={{0,16},{16,0},{1,17},{17,1},{2,18},{18,2},{3,19},{19,3},{4,20},{20... | collective-permute-start | bytes 3080 | tf_op jit(solution)/shard_map/ppermute | solution.py:169
  4.8 18.2 %collective-permute-start.8 = (f32[2,2,144]{2,1,0:T(2,128)S(1)}, f32[2,2,144]{2,1,0:T(2,128)S(1)}, u32[]{:S(2)}, u32[]{:S(2)}) collective-permute-start(f32[2,2,144]{2,1,0:T(2,128)S(1)} %pad_maximum_fusion.6), channel_id=1, source_target_pairs={{0,16},{16,0},{1,17},{17,1},{2,18},{18,2},{3,19},{19,3},{4,20},{20... | collective-permute-start | bytes 6920 | tf_op jit(solution)/shard_map/ppermute | solution.py:169
  4.9 20.2 %collective-permute-start.6 = (bf16[8,256]{1,0:T(8,128)(2,1)}, bf16[8,256]{1,0:T(8,128)(2,1)S(1)}, u32[]{:S(2)}, u32[]{:S(2)}) collective-permute-start(bf16[8,256]{1,0:T(8,128)(2,1)} %param.9), channel_id=1, source_target_pairs={{0,16},{16,0},{1,17},{17,1},{2,18},{18,2},{3,19},{19,3},{4,20},{20... | collective-permute-start | bytes 12296 | tf_op jit(solution)/shard_map/ppermute | solution.py:169
  9.5 19.7 %collective-permute-start.2 = (bf16[304,256]{1,0:T(8,128)(2,1)S(1)}, bf16[304,256]{1,0:T(8,128)(2,1)S(1)}, u32[]{:S(2)}, u32[]{:S(2)}) collective-permute-start(bf16[304,256]{1,0:T(8,128)(2,1)S(1)} %pad_maximum_fusion.4), channel_id=1, source_target_pairs={{0,12},{4,8},{8,4},{12,0},{1,13},{5,9},{9,5},{13,1},{2,14},{6,10},... | collective-permute-start | bytes 466952 | tf_op jit(solution)/shard_map/ppermute | solution.py:169
  13.2 16.0 %collective-permute-start = (bf16[304,256]{1,0:T(8,128)(2,1)S(1)}, bf16[304,256]{1,0:T(8,128)(2,1)S(1)}, u32[]{:S(2)}, u32[]{:S(2)}) collective-permute-start(bf16[304,256]{1,0:T(8,128)(2,1)S(1)} %pad_maximum_fusion.2), channel_id=1, source_target_pairs={{0,4},{4,0},{8,12},{12,8},{1,5},{5,1},{9,13},{13,9},{2,6},{6,2},{1... | collective-permute-start | bytes 466952 | tf_op jit(solution)/shard_map/ppermute | solution.py:169
  19.3 26.1 %collective-permute-start.1 = (bf16[304,256]{1,0:T(8,128)(2,1)S(1)}, bf16[304,256]{1,0:T(8,128)(2,1)S(1)}, u32[]{:S(2)}, u32[]{:S(2)}) collective-permute-start(bf16[304,256]{1,0:T(8,128)(2,1)S(1)} %pad_maximum_fusion.3), channel_id=1, source_target_pairs={{0,8},{4,12},{8,0},{12,4},{1,9},{5,13},{9,1},{13,5},{2,10},{6,14},... | collective-permute-start | bytes 466952 | tf_op jit(solution)/shard_map/ppermute | solution.py:169
  23.0 36.9 %collective-permute-start.4 = (bf16[576,576]{1,0:T(8,128)(2,1)}, bf16[576,576]{1,0:T(8,128)(2,1)S(1)}, u32[]{:S(2)}, u32[]{:S(2)}) collective-permute-start(bf16[576,576]{1,0:T(8,128)(2,1)} %fusion.3), channel_id=1, source_target_pairs={{0,8},{4,12},{8,0},{12,4},{1,9},{5,13},{9,1},{13,5},{2,10},{6,14},... | collective-permute-start | bytes 1990664 | tf_op jit(solution)/shard_map/ppermute | solution.py:169
  25.2 34.7 %collective-permute-start.5 = (bf16[576,576]{1,0:T(8,128)(2,1)}, bf16[576,576]{1,0:T(8,128)(2,1)S(1)}, u32[]{:S(2)}, u32[]{:S(2)}) collective-permute-start(bf16[576,576]{1,0:T(8,128)(2,1)} %get-tuple-element.96), channel_id=1, source_target_pairs={{0,4},{4,0},{8,12},{12,8},{1,5},{5,1},{9,13},{13,9},{2,6},{6,2},{1... | collective-permute-start | bytes 1990664 | tf_op jit(solution)/shard_map/ppermute | solution.py:169
  59.9 15.1 %collective-permute-start.10 = (bf16[4,304,256]{2,1,0:T(8,128)(2,1)S(1)}, bf16[4,304,256]{2,1,0:T(8,128)(2,1)S(1)}, u32[]{:S(2)}, u32[]{:S(2)}) collective-permute-start(bf16[4,304,256]{2,1,0:T(8,128)(2,1)S(1)} %pad_maximum_fusion.1.refs_0_), channel_id=1, source_target_pairs={{0,2},{1,3},{2,0},{3,1},{4,6},{5,7},{6,4},{7,5},{8,10},{9,11},{10,... | collective-permute-start | bytes 1867784 | tf_op jit(solution)/shard_map/ppermute | solution.py:169
  95.2 15.4 %collective-permute-start.18 = (bf16[256,1152]{1,0:T(8,128)(2,1)S(1)}, bf16[256,1152]{1,0:T(8,128)(2,1)S(1)}, u32[]{:S(2)}, u32[]{:S(2)}) collective-permute-start(bf16[256,1152]{1,0:T(8,128)(2,1)S(1)} %get-tuple-element.60.mine), channel_id=1, source_target_pairs={{0,2},{1,3},{2,0},{3,1},{4,6},{5,7},{6,4},{7,5},{8,10},{9,11},{10,... | collective-permute-start | bytes 1769480 | tf_op jit(solution)/shard_map/ppermute | solution.py:169
  114.6 14.6 %collective-permute-start.19 = (bf16[256,1152]{1,0:T(8,128)(2,1)S(1)}, bf16[256,1152]{1,0:T(8,128)(2,1)S(1)}, u32[]{:S(2)}, u32[]{:S(2)}) collective-permute-start(bf16[256,1152]{1,0:T(8,128)(2,1)S(1)} %get-tuple-element.62.mine), channel_id=1, source_target_pairs={{0,2},{1,3},{2,0},{3,1},{4,6},{5,7},{6,4},{7,5},{8,10},{9,11},{10,... | collective-permute-start | bytes 1769480 | tf_op jit(solution)/shard_map/ppermute | solution.py:169
  133.9 23.9 %collective-permute-start.25 = (bf16[576,512]{1,0:T(8,128)(2,1)S(1)}, bf16[576,512]{1,0:T(8,128)(2,1)S(1)}, u32[]{:S(2)}, u32[]{:S(2)}) collective-permute-start(bf16[576,512]{1,0:T(8,128)(2,1)S(1)} %maximum_select_fusion.refs_4_), channel_id=1, source_target_pairs={{8,0},{9,5},{11,15},{24,16},{25,21},{27,31}} | collective-permute-start | bytes 1769480 | tf_op jit(solution)/shard_map/ppermute | solution.py:662
  135.2 29.5 %collective-permute-start.23 = (bf16[576,512]{1,0:T(8,128)(2,1)S(1)}, bf16[576,512]{1,0:T(8,128)(2,1)S(1)}, u32[]{:S(2)}, u32[]{:S(2)}) collective-permute-start(bf16[576,512]{1,0:T(8,128)(2,1)S(1)} %maximum_select_fusion.refs_4_), channel_id=1, source_target_pairs={{0,4},{4,0},{12,8},{16,20},{28,24},{1,5},{5,1},{13,9},{17,21},{29,... | collective-permute-start | bytes 1769480 | tf_op jit(solution)/shard_map/ppermute | solution.py:645
  144.9 26.7 %collective-permute-start.22 = (bf16[576,512]{1,0:T(8,128)(2,1)S(1)}, bf16[576,512]{1,0:T(8,128)(2,1)S(1)}, u32[]{:S(2)}, u32[]{:S(2)}) collective-permute-start(bf16[576,512]{1,0:T(8,128)(2,1)S(1)} %maximum_select_fusion.refs_4_), channel_id=1, source_target_pairs={{0,16},{4,20},{12,28},{16,0},{28,12},{1,17},{5,21},{13,29},{17,1},... | collective-permute-start | bytes 1769480 | tf_op jit(solution)/shard_map/ppermute | solution.py:654
  147.4 24.3 %collective-permute-start.21 = (bf16[576,512]{1,0:T(8,128)(2,1)S(1)}, bf16[576,512]{1,0:T(8,128)(2,1)}, u32[]{:S(2)}, u32[]{:S(2)}) collective-permute-start(bf16[576,512]{1,0:T(8,128)(2,1)S(1)} %maximum_select_fusion.refs_4_), channel_id=1, source_target_pairs={{0,8},{4,12},{12,4},{16,24},{28,20},{1,9},{5,13},{13,5},{17,25},{2... | collective-permute-start | bytes 1769480 | tf_op jit(solution)/shard_map/ppermute | solution.py:645
  157.9 13.7 %collective-permute-start.26 = (bf16[576,512]{1,0:T(8,128)(2,1)S(1)}, bf16[576,512]{1,0:T(8,128)(2,1)S(1)}, u32[]{:S(2)}, u32[]{:S(2)}) collective-permute-start(bf16[576,512]{1,0:T(8,128)(2,1)S(1)} %broadcast_select_fusion.refs_0_), channel_id=1, source_target_pairs={{0,16},{5,21},{10,26},{15,31},{16,0},{21,5},{26,10},{31,15}} | collective-permute-start | bytes 1769480 | tf_op jit(solution)/shard_map/ppermute | solution.py:692
  164.7 15.6 %collective-permute-start.24 = (bf16[576,512]{1,0:T(8,128)(2,1)S(1)}, bf16[576,512]{1,0:T(8,128)(2,1)S(1)}, u32[]{:S(2)}, u32[]{:S(2)}) collective-permute-start(bf16[576,512]{1,0:T(8,128)(2,1)S(1)} %collective-permute-done.23.refs_5_), channel_id=1, source_target_pairs={{0,16},{4,20},{8,24},{20,4},{24,8},{1,17},{5,21},{9,25},{21,5},{25... | collective-permute-start | bytes 1769480 | tf_op jit(solution)/shard_map/ppermute | solution.py:654
  168.2 16.3 %collective-permute-start.37 = (bf16[576,512]{1,0:T(8,128)(2,1)S(1)}, bf16[576,512]{1,0:T(8,128)(2,1)}, u32[]{:S(2)}, u32[]{:S(2)}) collective-permute-start(bf16[576,512]{1,0:T(8,128)(2,1)S(1)} %broadcast_select_fusion.refs_0_), channel_id=1, source_target_pairs={{0,2},{5,7},{10,8},{15,13},{16,18},{21,23},{26,24},{31,29}} | collective-permute-start | bytes 1769480 | tf_op jit(solution)/shard_map/ppermute | solution.py:670
  181.1 18.5 %collective-permute-start.30 = (bf16[576,512]{1,0:T(8,128)(2,1)}, bf16[576,512]{1,0:T(8,128)(2,1)}, u32[]{:S(2)}, u32[]{:S(2)}) collective-permute-start(bf16[576,512]{1,0:T(8,128)(2,1)} %collective-permute-done.21.refs_6_), channel_id=1, source_target_pairs={{4,0},{8,12},{12,8},{20,16},{24,28},{5,1},{9,13},{13,9},{21,17},{2... | collective-permute-start | bytes 1769480 | tf_op jit(solution)/shard_map/ppermute | solution.py:645
  182.4 24.3 %collective-permute-start.36 = (bf16[576,512]{1,0:T(8,128)(2,1)S(1)}, bf16[576,512]{1,0:T(8,128)(2,1)}, u32[]{:S(2)}, u32[]{:S(2)}) collective-permute-start(bf16[576,512]{1,0:T(8,128)(2,1)S(1)} %broadcast_select_fusion.refs_0_), channel_id=1, source_target_pairs={{0,1},{5,4},{10,11},{15,14},{16,17},{21,20},{26,27},{31,30}} | collective-permute-start | bytes 1769480 | tf_op jit(solution)/shard_map/ppermute | solution.py:675
  184.5 23.6 %collective-permute-start.38 = (bf16[576,512]{1,0:T(8,128)(2,1)}, bf16[576,512]{1,0:T(8,128)(2,1)}, u32[]{:S(2)}, u32[]{:S(2)}) collective-permute-start(bf16[576,512]{1,0:T(8,128)(2,1)} %collective-permute-done.37.refs_2_), channel_id=1, source_target_pairs={{2,3},{7,6},{8,9},{13,12},{18,19},{23,22},{24,25},{29,28}} | collective-permute-start | bytes 1769480 | tf_op jit(solution)/shard_map/ppermute | solution.py:680
  191.9 23.1 %collective-permute-start.29 = (bf16[576,512]{1,0:T(8,128)(2,1)S(1)}, bf16[576,512]{1,0:T(8,128)(2,1)}, u32[]{:S(2)}, u32[]{:S(2)}) collective-permute-start(bf16[576,512]{1,0:T(8,128)(2,1)S(1)} %collective-permute-done.26.refs_0_), channel_id=1, source_target_pairs={{0,2},{5,7},{10,8},{15,13},{16,18},{21,23},{26,24},{31,29}} | collective-permute-start | bytes 1769480 | tf_op jit(solution)/shard_map/ppermute | solution.py:670
  199.6 17.1 %collective-permute-start.33 = (bf16[576,512]{1,0:T(8,128)(2,1)}, bf16[576,512]{1,0:T(8,128)(2,1)}, u32[]{:S(2)}, u32[]{:S(2)}) collective-permute-start(bf16[576,512]{1,0:T(8,128)(2,1)} %collective-permute-done.30.refs_7_), channel_id=1, source_target_pairs={{0,16},{8,24},{12,28},{16,0},{28,12},{1,17},{9,25},{13,29},{17,1},... | collective-permute-start | bytes 1769480 | tf_op jit(solution)/shard_map/ppermute | solution.py:654
  203.8 16.9 %collective-permute-start.28 = (bf16[576,512]{1,0:T(8,128)(2,1)S(1)}, bf16[576,512]{1,0:T(8,128)(2,1)}, u32[]{:S(2)}, u32[]{:S(2)}) collective-permute-start(bf16[576,512]{1,0:T(8,128)(2,1)S(1)} %collective-permute-done.26.refs_0_), channel_id=1, source_target_pairs={{0,1},{5,4},{10,11},{15,14},{16,17},{21,20},{26,27},{31,30}} | collective-permute-start | bytes 1769480 | tf_op jit(solution)/shard_map/ppermute | solution.py:675
  (37 other events, 459.7 us)

commit v15 on v14

--- a/solution.py
+++ b/solution.py
@@ -390,7 +390,8 @@
 
 
 def output_kernel(where_ref, scale, matches, *refs):
-    lefts, rights, refs = refs[:4], refs[4:8], refs[-9:]
+    lefts, rights, refs = refs[:4], refs[4:10], refs[-9:]
+    rights = ((rights[0],), (rights[1],), rights[2:4], rights[4:6])
     attn, embed, left_held, held, found, attn_made, embed_made, sems, out_sems = refs
     owner, layer, turn = where_ref[0], where_ref[1], where_ref[2]
     rows = held.shape[1]
@@ -407,7 +408,11 @@
 
                 @pl.when((layer ^ source) == place)
                 def _():
-                    pltpu.make_async_copy(rights[place], held.at[slot], sems.at[slot]).start()
+                    start = 0
+                    for part in rights[place]:
+                        target = held.at[slot, pl.ds(start, part.shape[0])]
+                        pltpu.make_async_copy(part, target, sems.at[slot]).start()
+                        start += part.shape[0]
 
     def left_arrived():
         pltpu.make_async_copy(left_held, left_held, sems.at[4]).wait()
@@ -468,13 +473,13 @@
             pl.BlockSpec(memory_space=pltpu.SMEM),
             pl.BlockSpec(memory_space=pltpu.VMEM),
         ]
-        + [anywhere] * (9 + len(made)),
+        + [anywhere] * (11 + len(made)),
         out_specs=(anywhere, anywhere),
         out_shape=(
             jax.ShapeDtypeStruct((4, cols, cols), jnp.float32),
             jax.ShapeDtypeStruct((cols, vocab_block), jnp.float32),
         ),
-        input_output_aliases={11: 0, 12: 1} if made else {},
+        input_output_aliases={13: 0, 14: 1} if made else {},
         scratch_shapes=[
             pltpu.VMEM((cols, tokens_all), jnp.bfloat16),
             pltpu.VMEM((3, cols, tokens_all), jnp.bfloat16),
@@ -684,10 +689,11 @@
         )
 
     near_1 = send(own, 1, 0)
-    near_2 = send(own, 2, 0)
+    cut = col_block // 2
+    near_2 = [send(own[:cut], 2, 0), send(own[cut:], 2, 0)]
     over_0 = across(own, 0)
     left_here = scatter(own, 2)
-    near_1, own = lax.optimization_barrier((near_1, own))
+    near_1, near_2[0], own = lax.optimization_barrier((near_1, near_2[0], own))
     over_1 = across(near_1, 1)
     left_there = lax.ppermute(
         left_here, everywhere, [(spot(x, t, t), spot(1 - x, t, t)) for x in planes for t in layers]
@@ -701,16 +707,17 @@
     router_cols = jnp.where(layer == 1, router_cols, router_moved)
     side_here = to_side(left_here)
     lefts_here = (left_here, to_core(left_here), side_here, to_far(side_here))
-    near_2, over_0, over_1, left_there, router_cols = lax.optimization_barrier(
-        (near_2, over_0, over_1, left_there, router_cols)
-    )
-    near_3 = send(near_2, 1, 2)
-    over_2 = across(near_2, 2)
+    near_3, over_2 = [send(near_2[0], 1, 2)], [across(near_2[0], 2)]
+    near_2[1], near_3[0], over_0, over_1, left_there, router_cols = lax.optimization_barrier(
+        (near_2[1], near_3[0], over_0, over_1, left_there, router_cols)
+    )
+    near_3.append(send(near_2[1], 1, 2))
+    over_2.append(across(near_2[1], 2))
     router_there = lax.ppermute(
         router_cols, everywhere, [(spot(1, t, t), spot(0, t, t)) for t in layers]
     )
     near_3, over_2, router_there = lax.optimization_barrier((near_3, over_2, router_there))
-    over_3 = across(near_3, 3)
+    over_3 = [across(part, 3) for part in near_3]
     router_cols = jnp.where(shard == 1, router_cols, router_there)
     router_side, router_core = to_side(router_cols), to_core(router_cols)
     turn = section ^ layer
@@ -719,7 +726,7 @@
         embed_scale,
         matches,
         lefts_here,
-        (own, near_1, near_2, near_3),
+        (own, near_1, *near_2, *near_3),
         (),
     )
     side_there, over_3, router_side, router_core, made = lax.optimization_barrier(
@@ -736,7 +743,7 @@
         embed_scale,
         matches,
         lefts_there,
-        (over_0, over_1, over_2, over_3),
+        (over_0, over_1, *over_2, *over_3),
         made,
     )
     precond_embed = embed_columns.T

time: 228 us -> 238 us (1.044); the launches traced: 227 us -> 234 us
  starting transfers between devices: 64.6 us -> 73.5 us
  waiting for transfers between devices: 108 us -> 102 us
  local copies, waits for them, and re-layouts: 10.3 us -> 13.3 us
    ppermute x4 -> x6, waiting for transfers between devices: 10.5 us -> 0.02 us  [across(): return lax.ppermute(value, axes, moves)]
    ppermute x3 -> x5, waiting for transfers between devices: 9.99 us -> 17.3 us  [send(): return lax.ppermute(value, axes, moves)]
    ppermute x4 -> x6, starting transfers between devices: 8.03 us -> 14.6 us  [across(): return lax.ppermute(value, axes, moves)]
    ppermute x3 -> x5, starting transfers between devices: 13.1 us -> 15.5 us  [send(): return lax.ppermute(value, axes, moves)]
  transfers between devices with their start and end apart: 41 -> 45, of which waited for: 15 -> 15; matrix products, arithmetic and copies ran while one was open for 10% -> 10% of each run, Pallas kernels for 6% -> 5%
where the time goes in v15:
time: 238 us; the launch traced here: 234 us
  waiting for transfers between devices  102 us (43%)
  starting transfers between devices  73.5 us (31%)
  Pallas kernels  28.2 us (12%)
  local copies, waits for them, and re-layouts  13.3 us (6%)
  other arithmetic  12 us (5%)
  between operations  2.94 us (1%)
    ppermute x21, waiting for transfers between devices, swap(): return lax.ppermute(value, axis, [(i, i ^ step) for i in range(size)])  73.5 us
    ppermute x21, starting transfers between devices, swap(): return lax.ppermute(value, axis, [(i, i ^ step) for i in range(size)])  23.1 us
    ppermute x5, waiting for transfers between devices, send(): return lax.ppermute(value, axes, moves)  17.3 us
    ppermute x5, starting transfers between devices, send(): return lax.ppermute(value, axes, moves)  15.5 us
    ppermute x6, starting transfers between devices, across(): return lax.ppermute(value, axes, moves)  14.6 us
    pallas_call x2, Pallas kernels, output_products(): pl.pallas_call(output_kernel, in_specs=[pl.BlockSpec(memory_space=pltpu.S...  11.3 us
    pallas_call x3, Pallas kernels, chain_call(): pl.pallas_call(kernel, in_specs=[pl.BlockSpec(memory_space=pltpu.SMEM)] *...  9.74 us
    ppermute x1, waiting for transfers between devices, scatter(): lax.ppermute(value, everywhere, [(spot(x, source, s), spot(x, s, s)) for...  7.13 us
  transfers between devices with their start and end apart: 45, of which 15 were waited for; matrix products, arithmetic and copies ran while one was open for 10% of the time, Pallas kernels for 5%

profile of v15, /device:TPU:0, one launch (start us, length us, event | category | flops | bytes accessed | tf_op | source)
XLA Modules:
  0.0 233.7 jit_solution(6129067978717294880)
XLA Ops:
  0.6 3.0 %collective-permute-start.7 = (s32[256]{0:T(256)}, s32[256]{0:T(256)S(1)}, u32[]{:S(2)}, u32[]{:S(2)}) collective-permute-start(s32[256]{0:T(256)} %param.10), channel_id=1, source_target_pairs={{0,16},{16,0},{1,17},{17,1},{2,18},{18,2},{3,19},{19,3},{4,20},{20... | collective-permute-start | bytes 3080 | tf_op jit(solution)/shard_map/ppermute | solution.py:169
  9.5 3.7 %collective-permute-start.2 = (bf16[304,256]{1,0:T(8,128)(2,1)S(1)}, bf16[304,256]{1,0:T(8,128)(2,1)S(1)}, u32[]{:S(2)}, u32[]{:S(2)}) collective-permute-start(bf16[304,256]{1,0:T(8,128)(2,1)S(1)} %pad_maximum_fusion.4), channel_id=1, source_target_pairs={{0,12},{4,8},{8,4},{12,0},{1,13},{5,9},{9,5},{13,1},{2,14},{6,10},... | collective-permute-start | bytes 466952 | tf_op jit(solution)/shard_map/ppermute | solution.py:169
  15.6 3.6 %fusion.6 = (bf16[576,576]{1,0:T(8,128)(2,1)}, bf16[576,576]{1,0:T(8,128)(2,1)S(1)}, bf16[576,576]{1,0:T(8,128)(2,1)}) fusion(f32[4,576,576]{2,1,0:T(8,128)} %param.12, s32[]{:T(128)S(6)} %select_n.152, s32[]{:T(128)S(6)} %select_n.140, s32[]{:T(128)S(6)} %select_n.144), kind=kLoop, calls=%fused_computation.18 | loop fusion | bytes 3981324 | tf_op jit(solution)/shard_map/convert_element_type | solution.py:552
  29.3 16.1 %collective-permute-done.1 = bf16[304,256]{1,0:T(8,128)(2,1)S(1)} collective-permute-done((bf16[304,256]{1,0:T(8,128)(2,1)S(1)}, bf16[304,256]{1,0:T(8,128)(2,1)S(1)}, u32[]{:S(2)}, u32[]{:S(2)}) %collective-permute-start.1) | collective-permute-done | bytes 155680 | tf_op jit(solution)/shard_map/ppermute | solution.py:169
  47.1 6.0 %collective-permute-done.3 = bf16[4,144,256]{2,1,0:T(8,128)(2,1)S(1)} collective-permute-done((bf16[4,144,256]{2,1,0:T(8,128)(2,1)}, bf16[4,144,256]{2,1,0:T(8,128)(2,1)S(1)}, u32[]{:S(2)}, u32[]{:S(2)}) %collective-permute-start.3) | collective-permute-done | bytes 294944 | tf_op jit(solution)/shard_map/ppermute | solution.py:169
  53.1 6.7 %collective-permute-done.4.refs_0_ = bf16[576,576]{1,0:T(8,128)(2,1)S(1)} collective-permute-done((bf16[576,576]{1,0:T(8,128)(2,1)}, bf16[576,576]{1,0:T(8,128)(2,1)S(1)}, u32[]{:S(2)}, u32[]{:S(2)}) %collective-permute-start.4) | collective-permute-done | bytes 663584 | tf_op jit(solution)/shard_map/ppermute | solution.py:169
  64.9 9.5 %collective-permute-done.11.refs_0_ = bf16[288,576]{1,0:T(8,128)(2,1)S(1)} collective-permute-done((bf16[288,576]{1,0:T(8,128)(2,1)S(1)}, bf16[288,576]{1,0:T(8,128)(2,1)S(1)}, u32[]{:S(2)}, u32[]{:S(2)}) %collective-permute-start.11) | collective-permute-done | bytes 331808 | tf_op jit(solution)/shard_map/ppermute | solution.py:169
  77.3 3.6 %shard_map.111 = (bf16[2,2304,256]{2,1,0:T(8,128)(2,1)S(1)}, bf16[256,2304]{1,0:T(8,128)(2,1)S(1)}, f32[4,1,576]{2,1,0:T(1,128)S(1)}, f32[1]{0:T(128)}) custom-call(s32[4]{0:T(128)S(1)} %pad_add_fusion.place_ref, bf16[4,304,256]{2,1,0:T(8,128)(2,1)S(1)} %pad_maximum_fusion.1.refs_0_, bf16[4,304,256]{2,1,0:T(8,128)(2,1)} %collective-permute-done.9.refs_1_, ...), custom_call_target="tpu_custom_call" | custom-call | flops 37748736 | bytes 8257536 | tf_op jit(solution)/shard_map/pallas_call | solution.py:241
  83.7 4.6 %collective-permute-done.13.refs_1_ = bf16[288,576]{1,0:T(8,128)(2,1)} collective-permute-done((bf16[288,576]{1,0:T(8,128)(2,1)}, bf16[288,576]{1,0:T(8,128)(2,1)}, u32[]{:S(2)}, u32[]{:S(2)}) %collective-permute-start.13) | collective-permute-done | bytes 331808 | tf_op jit(solution)/shard_map/ppermute | solution.py:169
  92.3 2.9 %shard_map.116 = (f32[2,256,576]{2,1,0:T(8,128)S(1)}, bf16[256,1152]{1,0:T(8,128)(2,1)S(1)}) custom-call(s32[1]{0:T(128)} %bitcast.2.place_ref, f32[1]{0:T(128)S(6)} %div.22.scale_ref, bf16[256,2304]{1,0:T(8,128)(2,1)S(1)} %get-tuple-element.58.rows, f32[4,1,576]{2,1,0:T(1,128)S(1)} %get-tuple-element.59.diag, bf16[576,576]{1,0:T(8,128)(2,1)S(1)} %shard_map.112.refs_0_, ...), custom_call_target="tpu_custom_call" | custom-call | flops 1358954496 | bytes 5308416 | tf_op jit(solution)/shard_map/pallas_call | solution.py:376
  96.4 14.2 %collective-permute-done.18.theirs = bf16[256,1152]{1,0:T(8,128)(2,1)S(1)} collective-permute-done((bf16[256,1152]{1,0:T(8,128)(2,1)S(1)}, bf16[256,1152]{1,0:T(8,128)(2,1)S(1)}, u32[]{:S(2)}, u32[]{:S(2)}) %collective-permute-start.18) | collective-permute-done | bytes 589856 | tf_op jit(solution)/shard_map/ppermute | solution.py:169
  110.6 4.0 %shard_map.117 = (f32[2,256,576]{2,1,0:T(8,128)S(1)}, bf16[256,1152]{1,0:T(8,128)(2,1)S(1)}) custom-call(s32[1]{0:T(128)} %bitcast.2.place_ref, f32[1]{0:T(128)S(6)} %div.22.scale_ref, bf16[256,1152]{1,0:T(8,128)(2,1)S(1)} %get-tuple-element.65.mine, bf16[256,1152]{1,0:T(8,128)(2,1)S(1)} %collective-permute-done.18.theirs, ...), custom_call_target="tpu_custom_call" | custom-call | flops 1358954496 | bytes 5308416 | tf_op jit(solution)/shard_map/pallas_call | solution.py:376
  115.8 13.4 %collective-permute-done.19.theirs = bf16[256,1152]{1,0:T(8,128)(2,1)S(1)} collective-permute-done((bf16[256,1152]{1,0:T(8,128)(2,1)S(1)}, bf16[256,1152]{1,0:T(8,128)(2,1)S(1)}, u32[]{:S(2)}, u32[]{:S(2)}) %collective-permute-start.19) | collective-permute-done | bytes 589856 | tf_op jit(solution)/shard_map/ppermute | solution.py:169
  129.2 2.9 %shard_map.118 = (bf16[576,256]{1,0:T(8,128)(2,1)S(1)}, bf16[576,256]{1,0:T(8,128)(2,1)S(1)}) custom-call(s32[1]{0:T(128)} %bitcast.2.place_ref, f32[1]{0:T(128)S(6)} %div.22.scale_ref, bf16[256,1152]{1,0:T(8,128)(2,1)S(1)} %get-tuple-element.67.mine, bf16[256,1152]{1,0:T(8,128)(2,1)S(1)} %collective-permute-done.19.theirs, ...), custom_call_target="tpu_custom_call" | custom-call | flops 1358954496 | bytes 5308416 | tf_op jit(solution)/shard_map/pallas_call | solution.py:376
  135.2 9.7 %collective-permute-start.22 = (bf16[576,512]{1,0:T(8,128)(2,1)S(1)}, bf16[576,512]{1,0:T(8,128)(2,1)S(1)}, u32[]{:S(2)}, u32[]{:S(2)}) collective-permute-start(bf16[576,512]{1,0:T(8,128)(2,1)S(1)} %maximum_select_fusion.refs_4_), channel_id=1, source_target_pairs={{0,4},{4,0},{12,8},{16,20},{28,24},{1,5},{5,1},{13,9},{17,21},{29,... | collective-permute-start | bytes 1769480 | tf_op jit(solution)/shard_map/ppermute | solution.py:650
  150.7 7.1 %collective-permute-done.27 = bf16[576,512]{1,0:T(8,128)(2,1)S(1)} collective-permute-done((bf16[576,512]{1,0:T(8,128)(2,1)S(1)}, bf16[576,512]{1,0:T(8,128)(2,1)S(1)}, u32[]{:S(2)}, u32[]{:S(2)}) %collective-permute-start.27) | collective-permute-done | bytes 589856 | tf_op jit(solution)/shard_map/ppermute | solution.py:667
  160.1 4.9 %collective-permute-done.23.refs_6_ = bf16[288,512]{1,0:T(8,128)(2,1)} collective-permute-done((bf16[288,512]{1,0:T(8,128)(2,1)S(1)}, bf16[288,512]{1,0:T(8,128)(2,1)}, u32[]{:S(2)}, u32[]{:S(2)}) %collective-permute-start.23) | collective-permute-done | bytes 294944 | tf_op jit(solution)/shard_map/ppermute | solution.py:650
  167.4 3.5 %collective-permute-start.26 = (bf16[576,512]{1,0:T(8,128)(2,1)S(1)}, bf16[576,512]{1,0:T(8,128)(2,1)S(1)}, u32[]{:S(2)}, u32[]{:S(2)}) collective-permute-start(bf16[576,512]{1,0:T(8,128)(2,1)S(1)} %collective-permute-done.22.refs_5_), channel_id=1, source_target_pairs={{0,16},{4,20},{8,24},{20,4},{24,8},{1,17},{5,21},{9,25},{21,5},{25... | collective-permute-start | bytes 1769480 | tf_op jit(solution)/shard_map/ppermute | solution.py:659
  175.9 11.5 %collective-permute-done.24.refs_8_ = bf16[288,512]{1,0:T(8,128)(2,1)} collective-permute-done((bf16[288,512]{1,0:T(8,128)(2,1)}, bf16[288,512]{1,0:T(8,128)(2,1)}, u32[]{:S(2)}, u32[]{:S(2)}) %collective-permute-start.24) | collective-permute-done | bytes 294944 | tf_op jit(solution)/shard_map/ppermute | solution.py:650
  195.7 4.4 %collective-permute-done.35 = f32[8,576]{1,0:T(8,128)S(1)} collective-permute-done((f32[8,576]{1,0:T(8,128)S(1)}, f32[8,576]{1,0:T(8,128)S(1)}, u32[]{:S(2)}, u32[]{:S(2)}) %collective-permute-start.35) | collective-permute-done | bytes 18464 | tf_op jit(solution)/shard_map/ppermute | solution.py:716
  205.3 3.9 %collective-permute-start.37 = (bf16[288,512]{1,0:T(8,128)(2,1)}, bf16[288,512]{1,0:T(8,128)(2,1)}, u32[]{:S(2)}, u32[]{:S(2)}) collective-permute-start(bf16[288,512]{1,0:T(8,128)(2,1)} %collective-permute-done.32.refs_9_), channel_id=1, source_target_pairs={{0,16},{8,24},{12,28},{16,0},{28,12},{1,17},{9,25},{13,29},{17,1},... | collective-permute-start | bytes 884744 | tf_op jit(solution)/shard_map/ppermute | solution.py:659
  210.0 3.0 %collective-permute-start.39 = (f32[8,576]{1,0:T(8,128)S(1)}, f32[8,576]{1,0:T(8,128)S(1)}, u32[]{:S(2)}, u32[]{:S(2)}) collective-permute-start(f32[8,576]{1,0:T(8,128)S(1)} %broadcast_select_fusion.1), channel_id=1, source_target_pairs={{0,1},{5,4},{10,11},{15,14},{16,17},{21,20},{26,27},{31,30}} | collective-permute-start | bytes 55304 | tf_op jit(solution)/shard_map/ppermute | solution.py:680
  214.4 5.5 %shard_map.119 = (f32[4,576,576]{2,1,0:T(8,128)}, f32[576,2048]{1,0:T(8,128)}) custom-call(s32[3]{0:T(128)} %add_add_fusion.1.where_ref, f32[1,2048]{1,0:T(1,128)} %bitcast.91, bf16[512,2048]{1,0:T(8,128)(2,1)} %compare_convert_fusion.matches, bf16[576,512]{1,0:T(8,128)(2,1)} %copy-done.3, bf16[576,512]{1,0:T(8,128)(2,1)} %collective-permute-done.40.refs_1_, ...), custom_call_target="tpu_custom_call" | custom-call | flops 1019215872 | bytes 6340608 | tf_op jit(solution)/shard_map/pallas_call | solution.py:470
  227.8 5.8 %shard_map.120 = (f32[4,576,576]{2,1,0:T(8,128)}, f32[576,2048]{1,0:T(8,128)}) custom-call(s32[3]{0:T(128)} %add_add_fusion.where_ref, f32[1,2048]{1,0:T(1,128)} %bitcast.92, bf16[512,2048]{1,0:T(8,128)(2,1)} %compare_convert_fusion.matches, bf16[576,512]{1,0:T(8,128)(2,1)} %copy-done.5, ...), custom_call_target="tpu_custom_call", output_to_operand_aliasing={{0}: (13, {}), {1}: (14, {})} | custom-call | flops 1019215872 | bytes 6340608 | tf_op jit(solution)/shard_map/pallas_call | solution.py:470
  (177 shorter events, 77.5 us)
Async XLA Ops:
  0.6 18.7 %collective-permute-start.7 = (s32[256]{0:T(256)}, s32[256]{0:T(256)S(1)}, u32[]{:S(2)}, u32[]{:S(2)}) collective-permute-start(s32[256]{0:T(256)} %param.10), channel_id=1, source_target_pairs={{0,16},{16,0},{1,17},{17,1},{2,18},{18,2},{3,19},{19,3},{4,20},{20... | collective-permute-start | bytes 3080 | tf_op jit(solution)/shard_map/ppermute | solution.py:169
  4.8 18.2 %collective-permute-start.8 = (f32[2,2,144]{2,1,0:T(2,128)S(1)}, f32[2,2,144]{2,1,0:T(2,128)S(1)}, u32[]{:S(2)}, u32[]{:S(2)}) collective-permute-start(f32[2,2,144]{2,1,0:T(2,128)S(1)} %pad_maximum_fusion.6), channel_id=1, source_target_pairs={{0,16},{16,0},{1,17},{17,1},{2,18},{18,2},{3,19},{19,3},{4,20},{20... | collective-permute-start | bytes 6920 | tf_op jit(solution)/shard_map/ppermute | solution.py:169
  4.9 20.2 %collective-permute-start.6 = (bf16[8,256]{1,0:T(8,128)(2,1)}, bf16[8,256]{1,0:T(8,128)(2,1)S(1)}, u32[]{:S(2)}, u32[]{:S(2)}) collective-permute-start(bf16[8,256]{1,0:T(8,128)(2,1)} %param.9), channel_id=1, source_target_pairs={{0,16},{16,0},{1,17},{17,1},{2,18},{18,2},{3,19},{19,3},{4,20},{20... | collective-permute-start | bytes 12296 | tf_op jit(solution)/shard_map/ppermute | solution.py:169
  9.5 19.7 %collective-permute-start.2 = (bf16[304,256]{1,0:T(8,128)(2,1)S(1)}, bf16[304,256]{1,0:T(8,128)(2,1)S(1)}, u32[]{:S(2)}, u32[]{:S(2)}) collective-permute-start(bf16[304,256]{1,0:T(8,128)(2,1)S(1)} %pad_maximum_fusion.4), channel_id=1, source_target_pairs={{0,12},{4,8},{8,4},{12,0},{1,13},{5,9},{9,5},{13,1},{2,14},{6,10},... | collective-permute-start | bytes 466952 | tf_op jit(solution)/shard_map/ppermute | solution.py:169
  13.2 16.0 %collective-permute-start = (bf16[304,256]{1,0:T(8,128)(2,1)S(1)}, bf16[304,256]{1,0:T(8,128)(2,1)S(1)}, u32[]{:S(2)}, u32[]{:S(2)}) collective-permute-start(bf16[304,256]{1,0:T(8,128)(2,1)S(1)} %pad_maximum_fusion.2), channel_id=1, source_target_pairs={{0,4},{4,0},{8,12},{12,8},{1,5},{5,1},{9,13},{13,9},{2,6},{6,2},{1... | collective-permute-start | bytes 466952 | tf_op jit(solution)/shard_map/ppermute | solution.py:169
  19.3 26.1 %collective-permute-start.1 = (bf16[304,256]{1,0:T(8,128)(2,1)S(1)}, bf16[304,256]{1,0:T(8,128)(2,1)S(1)}, u32[]{:S(2)}, u32[]{:S(2)}) collective-permute-start(bf16[304,256]{1,0:T(8,128)(2,1)S(1)} %pad_maximum_fusion.3), channel_id=1, source_target_pairs={{0,8},{4,12},{8,0},{12,4},{1,9},{5,13},{9,1},{13,5},{2,10},{6,14},... | collective-permute-start | bytes 466952 | tf_op jit(solution)/shard_map/ppermute | solution.py:169
  23.0 36.9 %collective-permute-start.4 = (bf16[576,576]{1,0:T(8,128)(2,1)}, bf16[576,576]{1,0:T(8,128)(2,1)S(1)}, u32[]{:S(2)}, u32[]{:S(2)}) collective-permute-start(bf16[576,576]{1,0:T(8,128)(2,1)} %fusion.3), channel_id=1, source_target_pairs={{0,8},{4,12},{8,0},{12,4},{1,9},{5,13},{9,1},{13,5},{2,10},{6,14},... | collective-permute-start | bytes 1990664 | tf_op jit(solution)/shard_map/ppermute | solution.py:169
  25.2 34.7 %collective-permute-start.5 = (bf16[576,576]{1,0:T(8,128)(2,1)}, bf16[576,576]{1,0:T(8,128)(2,1)S(1)}, u32[]{:S(2)}, u32[]{:S(2)}) collective-permute-start(bf16[576,576]{1,0:T(8,128)(2,1)} %get-tuple-element.106), channel_id=1, source_target_pairs={{0,4},{4,0},{8,12},{12,8},{1,5},{5,1},{9,13},{13,9},{2,6},{6,2},{1... | collective-permute-start | bytes 1990664 | tf_op jit(solution)/shard_map/ppermute | solution.py:169
  95.2 15.4 %collective-permute-start.18 = (bf16[256,1152]{1,0:T(8,128)(2,1)S(1)}, bf16[256,1152]{1,0:T(8,128)(2,1)S(1)}, u32[]{:S(2)}, u32[]{:S(2)}) collective-permute-start(bf16[256,1152]{1,0:T(8,128)(2,1)S(1)} %get-tuple-element.65.mine), channel_id=1, source_target_pairs={{0,2},{1,3},{2,0},{3,1},{4,6},{5,7},{6,4},{7,5},{8,10},{9,11},{10,... | collective-permute-start | bytes 1769480 | tf_op jit(solution)/shard_map/ppermute | solution.py:169
  133.9 23.9 %collective-permute-start.27 = (bf16[576,512]{1,0:T(8,128)(2,1)S(1)}, bf16[576,512]{1,0:T(8,128)(2,1)S(1)}, u32[]{:S(2)}, u32[]{:S(2)}) collective-permute-start(bf16[576,512]{1,0:T(8,128)(2,1)S(1)} %maximum_select_fusion.refs_4_), channel_id=1, source_target_pairs={{8,0},{9,5},{11,15},{24,16},{25,21},{27,31}} | collective-permute-start | bytes 1769480 | tf_op jit(solution)/shard_map/ppermute | solution.py:667
  135.2 32.1 %collective-permute-start.22 = (bf16[576,512]{1,0:T(8,128)(2,1)S(1)}, bf16[576,512]{1,0:T(8,128)(2,1)S(1)}, u32[]{:S(2)}, u32[]{:S(2)}) collective-permute-start(bf16[576,512]{1,0:T(8,128)(2,1)S(1)} %maximum_select_fusion.refs_4_), channel_id=1, source_target_pairs={{0,4},{4,0},{12,8},{16,20},{28,24},{1,5},{5,1},{13,9},{17,21},{29,... | collective-permute-start | bytes 1769480 | tf_op jit(solution)/shard_map/ppermute | solution.py:650
  144.9 28.3 %collective-permute-start.25 = (bf16[576,512]{1,0:T(8,128)(2,1)S(1)}, bf16[576,512]{1,0:T(8,128)(2,1)S(1)}, u32[]{:S(2)}, u32[]{:S(2)}) collective-permute-start(bf16[576,512]{1,0:T(8,128)(2,1)S(1)} %maximum_select_fusion.refs_4_), channel_id=1, source_target_pairs={{0,16},{4,20},{12,28},{16,0},{28,12},{1,17},{5,21},{13,29},{17,1},... | collective-permute-start | bytes 1769480 | tf_op jit(solution)/shard_map/ppermute | solution.py:659
  147.4 17.5 %collective-permute-start.23 = (bf16[288,512]{1,0:T(8,128)(2,1)S(1)}, bf16[288,512]{1,0:T(8,128)(2,1)}, u32[]{:S(2)}, u32[]{:S(2)}) collective-permute-start(bf16[288,512]{1,0:T(8,128)(2,1)S(1)} %get-tuple-element.109), channel_id=1, source_target_pairs={{0,8},{4,12},{12,4},{16,24},{28,20},{1,9},{5,13},{13,5},{17,25},{2... | collective-permute-start | bytes 884744 | tf_op jit(solution)/shard_map/ppermute | solution.py:650
  149.4 21.6 %collective-permute-start.21 = (bf16[288,512]{1,0:T(8,128)(2,1)S(1)}, bf16[288,512]{1,0:T(8,128)(2,1)S(1)}, u32[]{:S(2)}, u32[]{:S(2)}) collective-permute-start(bf16[288,512]{1,0:T(8,128)(2,1)S(1)} %get-tuple-element.110), channel_id=1, source_target_pairs={{0,8},{4,12},{12,4},{16,24},{28,20},{1,9},{5,13},{13,5},{17,25},{2... | collective-permute-start | bytes 884744 | tf_op jit(solution)/shard_map/ppermute | solution.py:650
  157.9 31.5 %collective-permute-start.41 = (bf16[576,512]{1,0:T(8,128)(2,1)S(1)}, bf16[576,512]{1,0:T(8,128)(2,1)}, u32[]{:S(2)}, u32[]{:S(2)}) collective-permute-start(bf16[576,512]{1,0:T(8,128)(2,1)S(1)} %broadcast_select_fusion.refs_0_), channel_id=1, source_target_pairs={{0,2},{5,7},{10,8},{15,13},{16,18},{21,23},{26,24},{31,29}} | collective-permute-start | bytes 1769480 | tf_op jit(solution)/shard_map/ppermute | solution.py:675
  164.9 26.7 %collective-permute-start.28 = (bf16[576,512]{1,0:T(8,128)(2,1)S(1)}, bf16[576,512]{1,0:T(8,128)(2,1)S(1)}, u32[]{:S(2)}, u32[]{:S(2)}) collective-permute-start(bf16[576,512]{1,0:T(8,128)(2,1)S(1)} %broadcast_select_fusion.refs_0_), channel_id=1, source_target_pairs={{0,16},{5,21},{10,26},{15,31},{16,0},{21,5},{26,10},{31,15}} | collective-permute-start | bytes 1769480 | tf_op jit(solution)/shard_map/ppermute | solution.py:698
  167.4 24.3 %collective-permute-start.26 = (bf16[576,512]{1,0:T(8,128)(2,1)S(1)}, bf16[576,512]{1,0:T(8,128)(2,1)S(1)}, u32[]{:S(2)}, u32[]{:S(2)}) collective-permute-start(bf16[576,512]{1,0:T(8,128)(2,1)S(1)} %collective-permute-done.22.refs_5_), channel_id=1, source_target_pairs={{0,16},{4,20},{8,24},{20,4},{24,8},{1,17},{5,21},{9,25},{21,5},{25... | collective-permute-start | bytes 1769480 | tf_op jit(solution)/shard_map/ppermute | solution.py:659
  171.0 16.3 %collective-permute-start.24 = (bf16[288,512]{1,0:T(8,128)(2,1)}, bf16[288,512]{1,0:T(8,128)(2,1)}, u32[]{:S(2)}, u32[]{:S(2)}) collective-permute-start(bf16[288,512]{1,0:T(8,128)(2,1)} %collective-permute-done.23.refs_6_), channel_id=1, source_target_pairs={{4,0},{8,12},{12,8},{20,16},{24,28},{5,1},{9,13},{13,9},{21,17},{2... | collective-permute-start | bytes 884744 | tf_op jit(solution)/shard_map/ppermute | solution.py:650
  174.5 19.9 %collective-permute-start.33 = (bf16[288,512]{1,0:T(8,128)(2,1)}, bf16[288,512]{1,0:T(8,128)(2,1)}, u32[]{:S(2)}, u32[]{:S(2)}) collective-permute-start(bf16[288,512]{1,0:T(8,128)(2,1)} %collective-permute-done.23.refs_6_), channel_id=1, source_target_pairs={{4,20},{8,24},{12,28},{20,4},{24,8},{5,21},{9,25},{13,29},{21,5},{... | collective-permute-start | bytes 884744 | tf_op jit(solution)/shard_map/ppermute | solution.py:659
  187.3 22.7 %collective-permute-start.40 = (bf16[576,512]{1,0:T(8,128)(2,1)S(1)}, bf16[576,512]{1,0:T(8,128)(2,1)}, u32[]{:S(2)}, u32[]{:S(2)}) collective-permute-start(bf16[576,512]{1,0:T(8,128)(2,1)S(1)} %broadcast_select_fusion.refs_0_), channel_id=1, source_target_pairs={{0,1},{5,4},{10,11},{15,14},{16,17},{21,20},{26,27},{31,30}} | collective-permute-start | bytes 1769480 | tf_op jit(solution)/shard_map/ppermute | solution.py:680
  189.4 23.6 %collective-permute-start.42 = (bf16[576,512]{1,0:T(8,128)(2,1)}, bf16[576,512]{1,0:T(8,128)(2,1)}, u32[]{:S(2)}, u32[]{:S(2)}) collective-permute-start(bf16[576,512]{1,0:T(8,128)(2,1)} %collective-permute-done.41.refs_2_), channel_id=1, source_target_pairs={{2,3},{7,6},{8,9},{13,12},{18,19},{23,22},{24,25},{29,28}} | collective-permute-start | bytes 1769480 | tf_op jit(solution)/shard_map/ppermute | solution.py:685
  200.7 20.7 %collective-permute-start.31 = (bf16[576,512]{1,0:T(8,128)(2,1)S(1)}, bf16[576,512]{1,0:T(8,128)(2,1)S(1)}, u32[]{:S(2)}, u32[]{:S(2)}) collective-permute-start(bf16[576,512]{1,0:T(8,128)(2,1)S(1)} %collective-permute-done.28.refs_0_), channel_id=1, source_target_pairs={{0,2},{5,7},{10,8},{15,13},{16,18},{21,23},{26,24},{31,29}} | collective-permute-start | bytes 1769480 | tf_op jit(solution)/shard_map/ppermute | solution.py:675
  203.4 17.9 %collective-permute-start.36 = (bf16[288,512]{1,0:T(8,128)(2,1)}, bf16[288,512]{1,0:T(8,128)(2,1)S(1)}, u32[]{:S(2)}, u32[]{:S(2)}) collective-permute-start(bf16[288,512]{1,0:T(8,128)(2,1)} %collective-permute-done.24.refs_8_), channel_id=1, source_target_pairs={{0,16},{8,24},{12,28},{16,0},{28,12},{1,17},{9,25},{13,29},{17,1},... | collective-permute-start | bytes 884744 | tf_op jit(solution)/shard_map/ppermute | solution.py:659
  205.3 16.0 %collective-permute-start.37 = (bf16[288,512]{1,0:T(8,128)(2,1)}, bf16[288,512]{1,0:T(8,128)(2,1)}, u32[]{:S(2)}, u32[]{:S(2)}) collective-permute-start(bf16[288,512]{1,0:T(8,128)(2,1)} %collective-permute-done.32.refs_9_), channel_id=1, source_target_pairs={{0,16},{8,24},{12,28},{16,0},{28,12},{1,17},{9,25},{13,29},{17,1},... | collective-permute-start | bytes 884744 | tf_op jit(solution)/shard_map/ppermute | solution.py:659
  (45 other events, 515.2 us)

commit v16 on v14

--- a/solution.py
+++ b/solution.py
@@ -546,10 +546,9 @@
     def old_block(factors, step):
         return by_index(factors, held_by(layer ^ step)).astype(jnp.bfloat16)
 
-    far_block = swap(old_block(old_factors, 2), "tensor", n_tensor, 2)
-    later_factors = lax.optimization_barrier(old_factors)
-    near_block = swap(old_block(later_factors, 1), "tensor", n_tensor, 1)
-    here_block, farthest = old_block(later_factors, 0), old_block(later_factors, 3)
+    part_rows = row_block // 2
+    away_block = old_block(old_factors, 2)
+    far_1 = swap(away_block[:part_rows], "tensor", n_tensor, 2)
 
     def both_shards(value, axis):
         other = swap(value, "shard", n_shard, 1)
@@ -580,11 +579,17 @@
         "en,ef->fn", grad_all, router_inverse, preferred_element_type=jnp.float32
     ).astype(jnp.bfloat16)
 
+    later_factors, router_right = lax.optimization_barrier((old_factors, router_right))
+    near_away = old_block(later_factors, 1)
+    here_block, farthest = old_block(later_factors, 0), old_block(later_factors, 3)
+    collected, far_1, near_away = lax.optimization_barrier((collected, far_1, near_away))
     other_tokens = swap(collected[:, features_dev : 2 * features_dev], "shard", n_shard, 1)
+    far_2 = swap(away_block[part_rows:], "tensor", n_tensor, 2)
+    near_block = swap(near_away, "tensor", n_tensor, 1)
     small = (router_right, matches, embed_scale, norm_sums)
-    other_tokens, collected, far_block, near_block, here_block, farthest, small = (
+    other_tokens, collected, far_2, near_block, here_block, farthest, small = (
         lax.optimization_barrier(
-            (other_tokens, collected, far_block, near_block, here_block, farthest, small)
+            (other_tokens, collected, far_2, near_block, here_block, farthest, small)
         )
     )
     router_right, matches, embed_scale, norm_sums = small
@@ -593,12 +598,11 @@
     )
     by_side = swap(collected, "section", n_section, 2)
     by_core = swap(collected, "section", n_section, 1)
-    part_rows = row_block // 2
     farthest_1 = swap(farthest[:part_rows], "tensor", n_tensor, 3)
     by_side, farthest_1 = lax.optimization_barrier((by_side, farthest_1))
     by_both = swap(by_side, "section", n_section, 1)
     farthest_2 = swap(farthest[part_rows:], "tensor", n_tensor, 3)
-    blocks = [(here_block,), (near_block,), (far_block,), (farthest_1, farthest_2)]
+    blocks = [(here_block,), (near_block,), (far_1, far_2), (farthest_1, farthest_2)]
 
     features, rows, low_diag, trace = lay_out(
         jnp.stack([own_place, layer, core, section]),
@@ -722,11 +726,12 @@
         (own, near_1, near_2, near_3),
         (),
     )
-    side_there, over_3, router_side, router_core, made = lax.optimization_barrier(
-        (to_side(left_there), over_3, router_side, router_core, made)
-    )
+    side_there = to_side(left_there)
     lefts_there = (left_there, to_core(left_there), side_there, to_far(side_there))
     routers = (router_cols, router_core, router_side, to_far(router_side))
+    lefts_there, over_3, routers, made = lax.optimization_barrier(
+        (lefts_there, over_3, routers, made)
+    )
     precond_router = routers[3]
     for index in (2, 1, 0):
         precond_router = jnp.where(turn == index, routers[index], precond_router)

time: 228 us -> 246 us (1.079); the launches traced: 227 us -> 243 us
  waiting for transfers between devices: 108 us -> 121 us
  starting transfers between devices: 64.6 us -> 72.2 us
  local copies, waits for them, and re-layouts: 10.3 us -> 7.06 us
    ppermute x21 -> x22, waiting for transfers between devices: 74.2 us -> 92 us  [swap(): return lax.ppermute(value, axis, [(i, i ^ step) for i in range(size)])]
    ppermute x4, waiting for transfers between devices: 10.5 us -> 4.7 us  [across(): return lax.ppermute(value, axes, moves)]
    ppermute x3, starting transfers between devices: 13.1 us -> 17.9 us  [send(): return lax.ppermute(value, axes, moves)]
    ppermute x21 -> x22, starting transfers between devices: 23.2 us -> 23.9 us  [swap(): return lax.ppermute(value, axis, [(i, i ^ step) for i in range(size)])]
  transfers between devices with their start and end apart: 41 -> 42, of which waited for: 15 -> 19; matrix products, arithmetic and copies ran while one was open for 10% -> 6% of each run, Pallas kernels for 6% -> 4%
where the time goes in v16:
time: 246 us; the launch traced here: 243 us
  waiting for transfers between devices  121 us (49%)
  starting transfers between devices  72.2 us (29%)
  Pallas kernels  27.9 us (11%)
  other arithmetic  10.3 us (4%)
  local copies, waits for them, and re-layouts  7.06 us (3%)
  between operations  3.11 us (1%)
    ppermute x22, waiting for transfers between devices, swap(): return lax.ppermute(value, axis, [(i, i ^ step) for i in range(size)])  92 us
    ppermute x22, starting transfers between devices, swap(): return lax.ppermute(value, axis, [(i, i ^ step) for i in range(size)])  23.9 us
    ppermute x3, starting transfers between devices, send(): return lax.ppermute(value, axes, moves)  17.9 us
    pallas_call x2, Pallas kernels, output_products(): pl.pallas_call(output_kernel, in_specs=[pl.BlockSpec(memory_space=pltpu.S...  11.1 us
    ppermute x1, waiting for transfers between devices, scatter(): lax.ppermute(value, everywhere, [(spot(x, source, s), spot(x, s, s)) for...  10.2 us
    pallas_call x3, Pallas kernels, chain_call(): pl.pallas_call(kernel, in_specs=[pl.BlockSpec(memory_space=pltpu.SMEM)] *...  9.71 us
    ppermute x4, starting transfers between devices, across(): return lax.ppermute(value, axes, moves)  9.13 us
    ppermute x3, waiting for transfers between devices, send(): return lax.ppermute(value, axes, moves)  8.08 us
  transfers between devices with their start and end apart: 42, of which 19 were waited for; matrix products, arithmetic and copies ran while one was open for 6% of the time, Pallas kernels for 4%

profile of v16, /device:TPU:0, one launch (start us, length us, event | category | flops | bytes accessed | tf_op | source)
XLA Modules:
  0.0 242.5 jit_solution(7765097859217314699)
XLA Ops:
  3.5 3.1 %collective-permute-start = (bf16[304,256]{1,0:T(8,128)(2,1)S(1)}, bf16[304,256]{1,0:T(8,128)(2,1)S(1)}, u32[]{:S(2)}, u32[]{:S(2)}) collective-permute-start(bf16[304,256]{1,0:T(8,128)(2,1)S(1)} %pad_maximum_fusion.2), channel_id=1, source_target_pairs={{0,4},{4,0},{8,12},{12,8},{1,5},{5,1},{9,13},{13,9},{2,6},{6,2},{1... | collective-permute-start | bytes 466952 | tf_op jit(solution)/shard_map/ppermute | solution.py:169
  6.6 2.7 %collective-permute-start.1 = (bf16[304,256]{1,0:T(8,128)(2,1)S(1)}, bf16[304,256]{1,0:T(8,128)(2,1)S(1)}, u32[]{:S(2)}, u32[]{:S(2)}) collective-permute-start(bf16[304,256]{1,0:T(8,128)(2,1)S(1)} %pad_maximum_fusion.3), channel_id=1, source_target_pairs={{0,8},{4,12},{8,0},{12,4},{1,9},{5,13},{9,1},{13,5},{2,10},{6,14},... | collective-permute-start | bytes 466952 | tf_op jit(solution)/shard_map/ppermute | solution.py:169
  23.1 13.9 %collective-permute-done.1 = bf16[304,256]{1,0:T(8,128)(2,1)S(1)} collective-permute-done((bf16[304,256]{1,0:T(8,128)(2,1)S(1)}, bf16[304,256]{1,0:T(8,128)(2,1)S(1)}, u32[]{:S(2)}, u32[]{:S(2)}) %collective-permute-start.1) | collective-permute-done | bytes 155680 | tf_op jit(solution)/shard_map/ppermute | solution.py:169
  37.1 11.2 %collective-permute-done.3.refs_0_ = bf16[288,576]{1,0:T(8,128)(2,1)S(1)} collective-permute-done((bf16[288,576]{1,0:T(8,128)(2,1)S(1)}, bf16[288,576]{1,0:T(8,128)(2,1)S(1)}, u32[]{:S(2)}, u32[]{:S(2)}) %collective-permute-start.3) | collective-permute-done | bytes 331808 | tf_op jit(solution)/shard_map/ppermute | solution.py:169
  57.3 13.2 %collective-permute-done.7.refs_0_ = bf16[576,576]{1,0:T(8,128)(2,1)S(1)} collective-permute-done((bf16[576,576]{1,0:T(8,128)(2,1)S(1)}, bf16[576,576]{1,0:T(8,128)(2,1)S(1)}, u32[]{:S(2)}, u32[]{:S(2)}) %collective-permute-start.7) | collective-permute-done | bytes 663584 | tf_op jit(solution)/shard_map/ppermute | solution.py:169
  75.4 9.7 %collective-permute-done.12.refs_0_ = bf16[288,576]{1,0:T(8,128)(2,1)S(1)} collective-permute-done((bf16[288,576]{1,0:T(8,128)(2,1)S(1)}, bf16[288,576]{1,0:T(8,128)(2,1)S(1)}, u32[]{:S(2)}, u32[]{:S(2)}) %collective-permute-start.12) | collective-permute-done | bytes 331808 | tf_op jit(solution)/shard_map/ppermute | solution.py:169
  89.2 3.4 %shard_map.111 = (bf16[2,2304,256]{2,1,0:T(8,128)(2,1)S(1)}, bf16[256,2304]{1,0:T(8,128)(2,1)S(1)}, f32[4,1,576]{2,1,0:T(1,128)S(1)}, f32[1]{0:T(128)}) custom-call(s32[4]{0:T(128)S(1)} %pad_add_fusion.place_ref, bf16[4,304,256]{2,1,0:T(8,128)(2,1)S(1)} %pad_maximum_fusion.1.refs_0_, bf16[4,304,256]{2,1,0:T(8,128)(2,1)S(1)} %collective-permute-done.10.refs_1_, ...), custom_call_target="tpu_custom_call" | custom-call | flops 37748736 | bytes 8257536 | tf_op jit(solution)/shard_map/pallas_call | solution.py:241
  92.6 7.2 %collective-permute-done.14.refs_1_ = bf16[288,576]{1,0:T(8,128)(2,1)} collective-permute-done((bf16[288,576]{1,0:T(8,128)(2,1)}, bf16[288,576]{1,0:T(8,128)(2,1)}, u32[]{:S(2)}, u32[]{:S(2)}) %collective-permute-start.14) | collective-permute-done | bytes 331808 | tf_op jit(solution)/shard_map/ppermute | solution.py:169
  107.1 2.8 %shard_map.116 = (f32[2,256,576]{2,1,0:T(8,128)S(1)}, bf16[256,1152]{1,0:T(8,128)(2,1)S(1)}) custom-call(s32[1]{0:T(128)} %bitcast.2.place_ref, f32[1]{0:T(128)S(6)} %div.22.scale_ref, bf16[256,2304]{1,0:T(8,128)(2,1)S(1)} %get-tuple-element.67.rows, f32[4,1,576]{2,1,0:T(1,128)S(1)} %get-tuple-element.68.diag, bf16[576,576]{1,0:T(8,128)(2,1)S(1)} %shard_map.112.refs_0_, ...), custom_call_target="tpu_custom_call" | custom-call | flops 1358954496 | bytes 5308416 | tf_op jit(solution)/shard_map/pallas_call | solution.py:376
  111.5 13.9 %collective-permute-done.19.theirs = bf16[256,1152]{1,0:T(8,128)(2,1)S(1)} collective-permute-done((bf16[256,1152]{1,0:T(8,128)(2,1)S(1)}, bf16[256,1152]{1,0:T(8,128)(2,1)S(1)}, u32[]{:S(2)}, u32[]{:S(2)}) %collective-permute-start.19) | collective-permute-done | bytes 589856 | tf_op jit(solution)/shard_map/ppermute | solution.py:169
  125.4 4.0 %shard_map.117 = (f32[2,256,576]{2,1,0:T(8,128)S(1)}, bf16[256,1152]{1,0:T(8,128)(2,1)S(1)}) custom-call(s32[1]{0:T(128)} %bitcast.2.place_ref, f32[1]{0:T(128)S(6)} %div.22.scale_ref, bf16[256,1152]{1,0:T(8,128)(2,1)S(1)} %get-tuple-element.75.mine, bf16[256,1152]{1,0:T(8,128)(2,1)S(1)} %collective-permute-done.19.theirs, ...), custom_call_target="tpu_custom_call" | custom-call | flops 1358954496 | bytes 5308416 | tf_op jit(solution)/shard_map/pallas_call | solution.py:376
  131.0 13.1 %collective-permute-done.20.theirs = bf16[256,1152]{1,0:T(8,128)(2,1)S(1)} collective-permute-done((bf16[256,1152]{1,0:T(8,128)(2,1)S(1)}, bf16[256,1152]{1,0:T(8,128)(2,1)S(1)}, u32[]{:S(2)}, u32[]{:S(2)}) %collective-permute-start.20) | collective-permute-done | bytes 589856 | tf_op jit(solution)/shard_map/ppermute | solution.py:169
  144.1 2.9 %shard_map.118 = (bf16[576,256]{1,0:T(8,128)(2,1)S(1)}, bf16[576,256]{1,0:T(8,128)(2,1)S(1)}) custom-call(s32[1]{0:T(128)} %bitcast.2.place_ref, f32[1]{0:T(128)S(6)} %div.22.scale_ref, bf16[256,1152]{1,0:T(8,128)(2,1)S(1)} %get-tuple-element.77.mine, bf16[256,1152]{1,0:T(8,128)(2,1)S(1)} %collective-permute-done.20.theirs, ...), custom_call_target="tpu_custom_call" | custom-call | flops 1358954496 | bytes 5308416 | tf_op jit(solution)/shard_map/pallas_call | solution.py:376
  148.8 10.3 %collective-permute-start.24 = (bf16[576,512]{1,0:T(8,128)(2,1)S(1)}, bf16[576,512]{1,0:T(8,128)(2,1)S(1)}, u32[]{:S(2)}, u32[]{:S(2)}) collective-permute-start(bf16[576,512]{1,0:T(8,128)(2,1)S(1)} %maximum_select_fusion.refs_4_), channel_id=1, source_target_pairs={{0,4},{4,0},{12,8},{16,20},{28,24},{1,5},{5,1},{13,9},{17,21},{29,... | collective-permute-start | bytes 1769480 | tf_op jit(solution)/shard_map/ppermute | solution.py:649
  160.3 6.3 %collective-permute-start.22 = (bf16[576,512]{1,0:T(8,128)(2,1)S(1)}, bf16[576,512]{1,0:T(8,128)(2,1)}, u32[]{:S(2)}, u32[]{:S(2)}) collective-permute-start(bf16[576,512]{1,0:T(8,128)(2,1)S(1)} %maximum_select_fusion.refs_4_), channel_id=1, source_target_pairs={{0,8},{4,12},{12,4},{16,24},{28,20},{1,9},{5,13},{13,5},{17,25},{2... | collective-permute-start | bytes 1769480 | tf_op jit(solution)/shard_map/ppermute | solution.py:649
  166.7 3.4 %collective-permute-start.23 = (bf16[576,512]{1,0:T(8,128)(2,1)S(1)}, bf16[576,512]{1,0:T(8,128)(2,1)S(1)}, u32[]{:S(2)}, u32[]{:S(2)}) collective-permute-start(bf16[576,512]{1,0:T(8,128)(2,1)S(1)} %maximum_select_fusion.refs_4_), channel_id=1, source_target_pairs={{0,16},{4,20},{12,28},{16,0},{28,12},{1,17},{5,21},{13,29},{17,1},... | collective-permute-start | bytes 1769480 | tf_op jit(solution)/shard_map/ppermute | solution.py:658
  170.1 8.1 %collective-permute-done.24.refs_5_ = bf16[576,512]{1,0:T(8,128)(2,1)S(1)} collective-permute-done((bf16[576,512]{1,0:T(8,128)(2,1)S(1)}, bf16[576,512]{1,0:T(8,128)(2,1)S(1)}, u32[]{:S(2)}, u32[]{:S(2)}) %collective-permute-start.24) | collective-permute-done | bytes 589856 | tf_op jit(solution)/shard_map/ppermute | solution.py:649
  178.2 10.2 %collective-permute-done.26 = bf16[576,512]{1,0:T(8,128)(2,1)S(1)} collective-permute-done((bf16[576,512]{1,0:T(8,128)(2,1)S(1)}, bf16[576,512]{1,0:T(8,128)(2,1)S(1)}, u32[]{:S(2)}, u32[]{:S(2)}) %collective-permute-start.26) | collective-permute-done | bytes 589856 | tf_op jit(solution)/shard_map/ppermute | solution.py:666
  188.5 2.8 %collective-permute-start.27 = (bf16[576,512]{1,0:T(8,128)(2,1)S(1)}, bf16[576,512]{1,0:T(8,128)(2,1)S(1)}, u32[]{:S(2)}, u32[]{:S(2)}) collective-permute-start(bf16[576,512]{1,0:T(8,128)(2,1)S(1)} %broadcast_select_fusion.refs_0_), channel_id=1, source_target_pairs={{0,16},{5,21},{10,26},{15,31},{16,0},{21,5},{26,10},{31,15}} | collective-permute-start | bytes 1769480 | tf_op jit(solution)/shard_map/ppermute | solution.py:696
  191.2 3.1 %collective-permute-start.25 = (bf16[576,512]{1,0:T(8,128)(2,1)S(1)}, bf16[576,512]{1,0:T(8,128)(2,1)S(1)}, u32[]{:S(2)}, u32[]{:S(2)}) collective-permute-start(bf16[576,512]{1,0:T(8,128)(2,1)S(1)} %collective-permute-done.24.refs_5_), channel_id=1, source_target_pairs={{0,16},{4,20},{8,24},{20,4},{24,8},{1,17},{5,21},{9,25},{21,5},{25... | collective-permute-start | bytes 1769480 | tf_op jit(solution)/shard_map/ppermute | solution.py:658
  200.2 4.7 %collective-permute-done.25.refs_5_ = bf16[576,512]{1,0:T(8,128)(2,1)S(1)} collective-permute-done((bf16[576,512]{1,0:T(8,128)(2,1)S(1)}, bf16[576,512]{1,0:T(8,128)(2,1)S(1)}, u32[]{:S(2)}, u32[]{:S(2)}) %collective-permute-start.25) | collective-permute-done | bytes 589856 | tf_op jit(solution)/shard_map/ppermute | solution.py:658
  212.5 4.6 %collective-permute-done.34 = f32[8,576]{1,0:T(8,128)S(1)} collective-permute-done((f32[8,576]{1,0:T(8,128)S(1)}, f32[8,576]{1,0:T(8,128)S(1)}, u32[]{:S(2)}, u32[]{:S(2)}) %collective-permute-start.34) | collective-permute-done | bytes 18464 | tf_op jit(solution)/shard_map/ppermute | solution.py:713
  230.5 5.5 %shard_map.119 = (f32[4,576,576]{2,1,0:T(8,128)}, f32[576,2048]{1,0:T(8,128)}) custom-call(s32[3]{0:T(128)} %add_add_fusion.1.where_ref, f32[1,2048]{1,0:T(1,128)} %bitcast.93, bf16[512,2048]{1,0:T(8,128)(2,1)} %compare_convert_fusion.matches, bf16[576,512]{1,0:T(8,128)(2,1)} %copy-done.7, bf16[576,512]{1,0:T(8,128)(2,1)} %collective-permute-done.39.refs_1_, ...), custom_call_target="tpu_custom_call" | custom-call | flops 1019215872 | bytes 6340608 | tf_op jit(solution)/shard_map/pallas_call | solution.py:465
  236.7 5.6 %shard_map.120 = (f32[4,576,576]{2,1,0:T(8,128)}, f32[576,2048]{1,0:T(8,128)}) custom-call(s32[3]{0:T(128)} %add_add_fusion.where_ref, f32[1,2048]{1,0:T(1,128)} %bitcast.94, bf16[512,2048]{1,0:T(8,128)(2,1)} %compare_convert_fusion.matches, bf16[576,512]{1,0:T(8,128)(2,1)} %copy-done.9, ...), custom_call_target="tpu_custom_call", output_to_operand_aliasing={{0}: (11, {}), {1}: (12, {})} | custom-call | flops 1019215872 | bytes 6340608 | tf_op jit(solution)/shard_map/pallas_call | solution.py:465
  (167 shorter events, 73.8 us)
Async XLA Ops:
  3.5 19.1 %collective-permute-start = (bf16[304,256]{1,0:T(8,128)(2,1)S(1)}, bf16[304,256]{1,0:T(8,128)(2,1)S(1)}, u32[]{:S(2)}, u32[]{:S(2)}) collective-permute-start(bf16[304,256]{1,0:T(8,128)(2,1)S(1)} %pad_maximum_fusion.2), channel_id=1, source_target_pairs={{0,4},{4,0},{8,12},{12,8},{1,5},{5,1},{9,13},{13,9},{2,6},{6,2},{1... | collective-permute-start | bytes 466952 | tf_op jit(solution)/shard_map/ppermute | solution.py:169
  6.6 30.4 %collective-permute-start.1 = (bf16[304,256]{1,0:T(8,128)(2,1)S(1)}, bf16[304,256]{1,0:T(8,128)(2,1)S(1)}, u32[]{:S(2)}, u32[]{:S(2)}) collective-permute-start(bf16[304,256]{1,0:T(8,128)(2,1)S(1)} %pad_maximum_fusion.3), channel_id=1, source_target_pairs={{0,8},{4,12},{8,0},{12,4},{1,9},{5,13},{9,1},{13,5},{2,10},{6,14},... | collective-permute-start | bytes 466952 | tf_op jit(solution)/shard_map/ppermute | solution.py:169
  9.2 27.7 %collective-permute-start.2 = (bf16[304,256]{1,0:T(8,128)(2,1)S(1)}, bf16[304,256]{1,0:T(8,128)(2,1)S(1)}, u32[]{:S(2)}, u32[]{:S(2)}) collective-permute-start(bf16[304,256]{1,0:T(8,128)(2,1)S(1)} %pad_maximum_fusion.4), channel_id=1, source_target_pairs={{0,12},{4,8},{8,4},{12,0},{1,13},{5,9},{9,5},{13,1},{2,14},{6,10},... | collective-permute-start | bytes 466952 | tf_op jit(solution)/shard_map/ppermute | solution.py:169
  14.6 33.6 %collective-permute-start.3 = (bf16[288,576]{1,0:T(8,128)(2,1)S(1)}, bf16[288,576]{1,0:T(8,128)(2,1)S(1)}, u32[]{:S(2)}, u32[]{:S(2)}) collective-permute-start(bf16[288,576]{1,0:T(8,128)(2,1)S(1)} %get-tuple-element.120), channel_id=1, source_target_pairs={{0,8},{4,12},{8,0},{12,4},{1,9},{5,13},{9,1},{13,5},{2,10},{6,14},... | collective-permute-start | bytes 995336 | tf_op jit(solution)/shard_map/ppermute | solution.py:169
  16.3 38.5 %collective-permute-start.6 = (bf16[288,576]{1,0:T(8,128)(2,1)S(1)}, bf16[288,576]{1,0:T(8,128)(2,1)S(1)}, u32[]{:S(2)}, u32[]{:S(2)}) collective-permute-start(bf16[288,576]{1,0:T(8,128)(2,1)S(1)} %get-tuple-element.119), channel_id=1, source_target_pairs={{0,8},{4,12},{8,0},{12,4},{1,9},{5,13},{9,1},{13,5},{2,10},{6,14},... | collective-permute-start | bytes 995336 | tf_op jit(solution)/shard_map/ppermute | solution.py:169
  22.6 30.0 %collective-permute-start.9 = (f32[2,2,144]{2,1,0:T(2,128)S(1)}, f32[2,2,144]{2,1,0:T(2,128)S(1)}, u32[]{:S(2)}, u32[]{:S(2)}) collective-permute-start(f32[2,2,144]{2,1,0:T(2,128)S(1)} %pad_maximum_fusion.6), channel_id=1, source_target_pairs={{0,16},{16,0},{1,17},{17,1},{2,18},{18,2},{3,19},{19,3},{4,20},{20... | collective-permute-start | bytes 6920 | tf_op jit(solution)/shard_map/ppermute | solution.py:169
  48.2 22.3 %collective-permute-start.7 = (bf16[576,576]{1,0:T(8,128)(2,1)S(1)}, bf16[576,576]{1,0:T(8,128)(2,1)S(1)}, u32[]{:S(2)}, u32[]{:S(2)}) collective-permute-start(bf16[576,576]{1,0:T(8,128)(2,1)S(1)} %get-tuple-element.58), channel_id=1, source_target_pairs={{0,4},{4,0},{8,12},{12,8},{1,5},{5,1},{9,13},{13,9},{2,6},{6,2},{1... | collective-permute-start | bytes 1990664 | tf_op jit(solution)/shard_map/ppermute | solution.py:169
  70.6 16.0 %collective-permute-start.11 = (bf16[4,304,256]{2,1,0:T(8,128)(2,1)S(1)}, bf16[4,304,256]{2,1,0:T(8,128)(2,1)S(1)}, u32[]{:S(2)}, u32[]{:S(2)}) collective-permute-start(bf16[4,304,256]{2,1,0:T(8,128)(2,1)S(1)} %pad_maximum_fusion.1.refs_0_), channel_id=1, source_target_pairs={{0,2},{1,3},{2,0},{3,1},{4,6},{5,7},{6,4},{7,5},{8,10},{9,11},{10,... | collective-permute-start | bytes 1867784 | tf_op jit(solution)/shard_map/ppermute | solution.py:169
  75.4 13.7 %collective-permute-start.10 = (bf16[4,304,256]{2,1,0:T(8,128)(2,1)S(1)}, bf16[4,304,256]{2,1,0:T(8,128)(2,1)S(1)}, u32[]{:S(2)}, u32[]{:S(2)}) collective-permute-start(bf16[4,304,256]{2,1,0:T(8,128)(2,1)S(1)} %pad_maximum_fusion.1.refs_0_), channel_id=1, source_target_pairs={{0,1},{1,0},{2,3},{3,2},{4,5},{5,4},{6,7},{7,6},{8,9},{9,8},{10,11... | collective-permute-start | bytes 1867784 | tf_op jit(solution)/shard_map/ppermute | solution.py:169
  86.6 13.2 %collective-permute-start.14 = (bf16[288,576]{1,0:T(8,128)(2,1)}, bf16[288,576]{1,0:T(8,128)(2,1)}, u32[]{:S(2)}, u32[]{:S(2)}) collective-permute-start(bf16[288,576]{1,0:T(8,128)(2,1)} %get-tuple-element.117), channel_id=1, source_target_pairs={{0,12},{4,8},{8,4},{12,0},{1,13},{5,9},{9,5},{13,1},{2,14},{6,10},... | collective-permute-start | bytes 995336 | tf_op jit(solution)/shard_map/ppermute | solution.py:169
  109.9 15.5 %collective-permute-start.19 = (bf16[256,1152]{1,0:T(8,128)(2,1)S(1)}, bf16[256,1152]{1,0:T(8,128)(2,1)S(1)}, u32[]{:S(2)}, u32[]{:S(2)}) collective-permute-start(bf16[256,1152]{1,0:T(8,128)(2,1)S(1)} %get-tuple-element.75.mine), channel_id=1, source_target_pairs={{0,2},{1,3},{2,0},{3,1},{4,6},{5,7},{6,4},{7,5},{8,10},{9,11},{10,... | collective-permute-start | bytes 1769480 | tf_op jit(solution)/shard_map/ppermute | solution.py:169
  129.4 14.7 %collective-permute-start.20 = (bf16[256,1152]{1,0:T(8,128)(2,1)S(1)}, bf16[256,1152]{1,0:T(8,128)(2,1)S(1)}, u32[]{:S(2)}, u32[]{:S(2)}) collective-permute-start(bf16[256,1152]{1,0:T(8,128)(2,1)S(1)} %get-tuple-element.77.mine), channel_id=1, source_target_pairs={{0,2},{1,3},{2,0},{3,1},{4,6},{5,7},{6,4},{7,5},{8,10},{9,11},{10,... | collective-permute-start | bytes 1769480 | tf_op jit(solution)/shard_map/ppermute | solution.py:169
  148.8 29.4 %collective-permute-start.24 = (bf16[576,512]{1,0:T(8,128)(2,1)S(1)}, bf16[576,512]{1,0:T(8,128)(2,1)S(1)}, u32[]{:S(2)}, u32[]{:S(2)}) collective-permute-start(bf16[576,512]{1,0:T(8,128)(2,1)S(1)} %maximum_select_fusion.refs_4_), channel_id=1, source_target_pairs={{0,4},{4,0},{12,8},{16,20},{28,24},{1,5},{5,1},{13,9},{17,21},{29,... | collective-permute-start | bytes 1769480 | tf_op jit(solution)/shard_map/ppermute | solution.py:649
  159.0 29.4 %collective-permute-start.26 = (bf16[576,512]{1,0:T(8,128)(2,1)S(1)}, bf16[576,512]{1,0:T(8,128)(2,1)S(1)}, u32[]{:S(2)}, u32[]{:S(2)}) collective-permute-start(bf16[576,512]{1,0:T(8,128)(2,1)S(1)} %maximum_select_fusion.refs_4_), channel_id=1, source_target_pairs={{8,0},{9,5},{11,15},{24,16},{25,21},{27,31}} | collective-permute-start | bytes 1769480 | tf_op jit(solution)/shard_map/ppermute | solution.py:666
  160.3 39.0 %collective-permute-start.22 = (bf16[576,512]{1,0:T(8,128)(2,1)S(1)}, bf16[576,512]{1,0:T(8,128)(2,1)}, u32[]{:S(2)}, u32[]{:S(2)}) collective-permute-start(bf16[576,512]{1,0:T(8,128)(2,1)S(1)} %maximum_select_fusion.refs_4_), channel_id=1, source_target_pairs={{0,8},{4,12},{12,4},{16,24},{28,20},{1,9},{5,13},{13,5},{17,25},{2... | collective-permute-start | bytes 1769480 | tf_op jit(solution)/shard_map/ppermute | solution.py:649
  166.7 32.7 %collective-permute-start.23 = (bf16[576,512]{1,0:T(8,128)(2,1)S(1)}, bf16[576,512]{1,0:T(8,128)(2,1)S(1)}, u32[]{:S(2)}, u32[]{:S(2)}) collective-permute-start(bf16[576,512]{1,0:T(8,128)(2,1)S(1)} %maximum_select_fusion.refs_4_), channel_id=1, source_target_pairs={{0,16},{4,20},{12,28},{16,0},{28,12},{1,17},{5,21},{13,29},{17,1},... | collective-permute-start | bytes 1769480 | tf_op jit(solution)/shard_map/ppermute | solution.py:658
  191.2 13.7 %collective-permute-start.25 = (bf16[576,512]{1,0:T(8,128)(2,1)S(1)}, bf16[576,512]{1,0:T(8,128)(2,1)S(1)}, u32[]{:S(2)}, u32[]{:S(2)}) collective-permute-start(bf16[576,512]{1,0:T(8,128)(2,1)S(1)} %collective-permute-done.24.refs_5_), channel_id=1, source_target_pairs={{0,16},{4,20},{8,24},{20,4},{24,8},{1,17},{5,21},{9,25},{21,5},{25... | collective-permute-start | bytes 1769480 | tf_op jit(solution)/shard_map/ppermute | solution.py:658
  196.5 14.7 %collective-permute-start.40 = (bf16[576,512]{1,0:T(8,128)(2,1)S(1)}, bf16[576,512]{1,0:T(8,128)(2,1)}, u32[]{:S(2)}, u32[]{:S(2)}) collective-permute-start(bf16[576,512]{1,0:T(8,128)(2,1)S(1)} %broadcast_select_fusion.refs_0_), channel_id=1, source_target_pairs={{0,2},{5,7},{10,8},{15,13},{16,18},{21,23},{26,24},{31,29}} | collective-permute-start | bytes 1769480 | tf_op jit(solution)/shard_map/ppermute | solution.py:674
  204.9 14.8 %collective-permute-start.32 = (bf16[576,512]{1,0:T(8,128)(2,1)}, bf16[576,512]{1,0:T(8,128)(2,1)}, u32[]{:S(2)}, u32[]{:S(2)}) collective-permute-start(bf16[576,512]{1,0:T(8,128)(2,1)} %collective-permute-done.22.refs_6_), channel_id=1, source_target_pairs={{4,0},{8,12},{12,8},{20,16},{24,28},{5,1},{9,13},{13,9},{21,17},{2... | collective-permute-start | bytes 1769480 | tf_op jit(solution)/shard_map/ppermute | solution.py:649
  206.2 15.7 %collective-permute-start.33 = (bf16[576,512]{1,0:T(8,128)(2,1)}, bf16[576,512]{1,0:T(8,128)(2,1)S(1)}, u32[]{:S(2)}, u32[]{:S(2)}) collective-permute-start(bf16[576,512]{1,0:T(8,128)(2,1)} %collective-permute-done.22.refs_6_), channel_id=1, source_target_pairs={{4,20},{8,24},{12,28},{20,4},{24,8},{5,21},{9,25},{13,29},{21,5},{... | collective-permute-start | bytes 1769480 | tf_op jit(solution)/shard_map/ppermute | solution.py:658
  206.9 16.9 %collective-permute-start.30 = (bf16[576,512]{1,0:T(8,128)(2,1)S(1)}, bf16[576,512]{1,0:T(8,128)(2,1)}, u32[]{:S(2)}, u32[]{:S(2)}) collective-permute-start(bf16[576,512]{1,0:T(8,128)(2,1)S(1)} %collective-permute-done.27.refs_0_), channel_id=1, source_target_pairs={{0,2},{5,7},{10,8},{15,13},{16,18},{21,23},{26,24},{31,29}} | collective-permute-start | bytes 1769480 | tf_op jit(solution)/shard_map/ppermute | solution.py:674
  209.1 17.6 %collective-permute-start.39 = (bf16[576,512]{1,0:T(8,128)(2,1)S(1)}, bf16[576,512]{1,0:T(8,128)(2,1)}, u32[]{:S(2)}, u32[]{:S(2)}) collective-permute-start(bf16[576,512]{1,0:T(8,128)(2,1)S(1)} %broadcast_select_fusion.refs_0_), channel_id=1, source_target_pairs={{0,1},{5,4},{10,11},{15,14},{16,17},{21,20},{26,27},{31,30}} | collective-permute-start | bytes 1769480 | tf_op jit(solution)/shard_map/ppermute | solution.py:679
  219.8 16.3 %collective-permute-start.29 = (bf16[576,512]{1,0:T(8,128)(2,1)S(1)}, bf16[576,512]{1,0:T(8,128)(2,1)}, u32[]{:S(2)}, u32[]{:S(2)}) collective-permute-start(bf16[576,512]{1,0:T(8,128)(2,1)S(1)} %collective-permute-done.27.refs_0_), channel_id=1, source_target_pairs={{0,1},{5,4},{10,11},{15,14},{16,17},{21,20},{26,27},{31,30}} | collective-permute-start | bytes 1769480 | tf_op jit(solution)/shard_map/ppermute | solution.py:679
  221.9 14.2 %collective-permute-start.35 = (bf16[576,512]{1,0:T(8,128)(2,1)}, bf16[576,512]{1,0:T(8,128)(2,1)}, u32[]{:S(2)}, u32[]{:S(2)}) collective-permute-start(bf16[576,512]{1,0:T(8,128)(2,1)} %collective-permute-done.32.refs_7_), channel_id=1, source_target_pairs={{0,16},{8,24},{12,28},{16,0},{28,12},{1,17},{9,25},{13,29},{17,1},... | collective-permute-start | bytes 1769480 | tf_op jit(solution)/shard_map/ppermute | solution.py:658
  (40 other events, 607.7 us)

commit v17 on v14

--- a/solution.py
+++ b/solution.py
@@ -547,9 +547,6 @@
         return by_index(factors, held_by(layer ^ step)).astype(jnp.bfloat16)
 
     far_block = swap(old_block(old_factors, 2), "tensor", n_tensor, 2)
-    later_factors = lax.optimization_barrier(old_factors)
-    near_block = swap(old_block(later_factors, 1), "tensor", n_tensor, 1)
-    here_block, farthest = old_block(later_factors, 0), old_block(later_factors, 3)
 
     def both_shards(value, axis):
         other = swap(value, "shard", n_shard, 1)
@@ -580,6 +577,9 @@
         "en,ef->fn", grad_all, router_inverse, preferred_element_type=jnp.float32
     ).astype(jnp.bfloat16)
 
+    later_factors, router_right = lax.optimization_barrier((old_factors, router_right))
+    near_block = swap(old_block(later_factors, 1), "tensor", n_tensor, 1)
+    here_block, farthest = old_block(later_factors, 0), old_block(later_factors, 3)
     other_tokens = swap(collected[:, features_dev : 2 * features_dev], "shard", n_shard, 1)
     small = (router_right, matches, embed_scale, norm_sums)
     other_tokens, collected, far_block, near_block, here_block, farthest, small = (

time: 228 us -> 225 us (0.987)
  local copies, waits for them, and re-layouts: 10.3 us -> 7.22 us
    ppermute x1, waiting for transfers between devices: 8.37 us -> 3.9 us  [scatter(): lax.ppermute(value, everywhere, [(spot(x, source, s), spot(x, s, s)) for...]
  transfers between devices with their start and end apart: 41 -> 41, of which waited for: 15 -> 19; matrix products, arithmetic and copies ran while one was open for 10% -> 9% of each run, Pallas kernels for 6% -> 6%
where the time goes in v17:
time: 225 us; the launch traced here: 224 us
  waiting for transfers between devices  107 us (48%)
  starting transfers between devices  64.2 us (29%)
  Pallas kernels  28 us (12%)
  other arithmetic  14 us (6%)
  local copies, waits for them, and re-layouts  7.22 us (3%)
  between operations  2.8 us (1%)
    ppermute x21, waiting for transfers between devices, swap(): return lax.ppermute(value, axis, [(i, i ^ step) for i in range(size)])  73.8 us
    ppermute x21, starting transfers between devices, swap(): return lax.ppermute(value, axis, [(i, i ^ step) for i in range(size)])  22.1 us
    ppermute x3, starting transfers between devices, send(): return lax.ppermute(value, axes, moves)  13.1 us
    ppermute x4, waiting for transfers between devices, across(): return lax.ppermute(value, axes, moves)  12.5 us
    ppermute x3, waiting for transfers between devices, send(): return lax.ppermute(value, axes, moves)  12.1 us
    pallas_call x2, Pallas kernels, output_products(): pl.pallas_call(output_kernel, in_specs=[pl.BlockSpec(memory_space=pltpu.S...  11.1 us
    pallas_call x3, Pallas kernels, chain_call(): pl.pallas_call(kernel, in_specs=[pl.BlockSpec(memory_space=pltpu.SMEM)] *...  9.74 us
    ppermute x4, starting transfers between devices, across(): return lax.ppermute(value, axes, moves)  7.78 us
  transfers between devices with their start and end apart: 41, of which 19 were waited for; matrix products, arithmetic and copies ran while one was open for 9% of the time, Pallas kernels for 6%

profile of v17, /device:TPU:0, one launch (start us, length us, event | category | flops | bytes accessed | tf_op | source)
XLA Modules:
  0.0 224.3 jit_solution(1869671148564193919)
XLA Ops:
  0.6 3.0 %collective-permute-start.7 = (s32[256]{0:T(256)}, s32[256]{0:T(256)S(1)}, u32[]{:S(2)}, u32[]{:S(2)}) collective-permute-start(s32[256]{0:T(256)} %param.10), channel_id=1, source_target_pairs={{0,16},{16,0},{1,17},{17,1},{2,18},{18,2},{3,19},{19,3},{4,20},{20... | collective-permute-start | bytes 3080 | tf_op jit(solution)/shard_map/ppermute | solution.py:169
  7.1 4.1 %collective-permute-start.2 = (bf16[304,256]{1,0:T(8,128)(2,1)}, bf16[304,256]{1,0:T(8,128)(2,1)S(1)}, u32[]{:S(2)}, u32[]{:S(2)}) collective-permute-start(bf16[304,256]{1,0:T(8,128)(2,1)} %pad_maximum_fusion.4), channel_id=1, source_target_pairs={{0,12},{4,8},{8,4},{12,0},{1,13},{5,9},{9,5},{13,1},{2,14},{6,10},... | collective-permute-start | bytes 466952 | tf_op jit(solution)/shard_map/ppermute | solution.py:169
  28.1 12.9 %collective-permute-done.1 = bf16[304,256]{1,0:T(8,128)(2,1)} collective-permute-done((bf16[304,256]{1,0:T(8,128)(2,1)}, bf16[304,256]{1,0:T(8,128)(2,1)}, u32[]{:S(2)}, u32[]{:S(2)}) %collective-permute-start.1) | collective-permute-done | bytes 155680 | tf_op jit(solution)/shard_map/ppermute | solution.py:169
  44.2 4.7 %collective-permute-done.3 = bf16[4,144,256]{2,1,0:T(8,128)(2,1)S(1)} collective-permute-done((bf16[4,144,256]{2,1,0:T(8,128)(2,1)S(1)}, bf16[4,144,256]{2,1,0:T(8,128)(2,1)S(1)}, u32[]{:S(2)}, u32[]{:S(2)}) %collective-permute-start.3) | collective-permute-done | bytes 294944 | tf_op jit(solution)/shard_map/ppermute | solution.py:169
  48.9 6.7 %collective-permute-done.4.refs_0_ = bf16[576,576]{1,0:T(8,128)(2,1)S(1)} collective-permute-done((bf16[576,576]{1,0:T(8,128)(2,1)S(1)}, bf16[576,576]{1,0:T(8,128)(2,1)S(1)}, u32[]{:S(2)}, u32[]{:S(2)}) %collective-permute-start.4) | collective-permute-done | bytes 663584 | tf_op jit(solution)/shard_map/ppermute | solution.py:169
  55.6 3.3 %collective-permute-done.6.refs_0_ = bf16[576,576]{1,0:T(8,128)(2,1)S(1)} collective-permute-done((bf16[576,576]{1,0:T(8,128)(2,1)S(1)}, bf16[576,576]{1,0:T(8,128)(2,1)S(1)}, u32[]{:S(2)}, u32[]{:S(2)}) %collective-permute-start.6) | collective-permute-done | bytes 663584 | tf_op jit(solution)/shard_map/ppermute | solution.py:169
  62.0 9.1 %collective-permute-done.11.refs_0_ = bf16[288,576]{1,0:T(8,128)(2,1)S(1)} collective-permute-done((bf16[288,576]{1,0:T(8,128)(2,1)S(1)}, bf16[288,576]{1,0:T(8,128)(2,1)S(1)}, u32[]{:S(2)}, u32[]{:S(2)}) %collective-permute-start.11) | collective-permute-done | bytes 331808 | tf_op jit(solution)/shard_map/ppermute | solution.py:169
  74.7 3.6 %shard_map.111 = (bf16[2,2304,256]{2,1,0:T(8,128)(2,1)S(1)}, bf16[256,2304]{1,0:T(8,128)(2,1)S(1)}, f32[4,1,576]{2,1,0:T(1,128)S(1)}, f32[1]{0:T(128)}) custom-call(s32[4]{0:T(128)S(1)} %pad_add_fusion.place_ref, bf16[4,304,256]{2,1,0:T(8,128)(2,1)S(1)} %pad_maximum_fusion.1.refs_0_, bf16[4,304,256]{2,1,0:T(8,128)(2,1)} %collective-permute-done.9.refs_1_, ...), custom_call_target="tpu_custom_call" | custom-call | flops 37748736 | bytes 8257536 | tf_op jit(solution)/shard_map/pallas_call | solution.py:241
  81.0 4.7 %collective-permute-done.13.refs_1_ = bf16[288,576]{1,0:T(8,128)(2,1)} collective-permute-done((bf16[288,576]{1,0:T(8,128)(2,1)}, bf16[288,576]{1,0:T(8,128)(2,1)}, u32[]{:S(2)}, u32[]{:S(2)}) %collective-permute-start.13) | collective-permute-done | bytes 331808 | tf_op jit(solution)/shard_map/ppermute | solution.py:169
  94.3 13.8 %collective-permute-done.18.theirs = bf16[256,1152]{1,0:T(8,128)(2,1)S(1)} collective-permute-done((bf16[256,1152]{1,0:T(8,128)(2,1)S(1)}, bf16[256,1152]{1,0:T(8,128)(2,1)S(1)}, u32[]{:S(2)}, u32[]{:S(2)}) %collective-permute-start.18) | collective-permute-done | bytes 589856 | tf_op jit(solution)/shard_map/ppermute | solution.py:169
  108.1 4.0 %shard_map.117 = (f32[2,256,576]{2,1,0:T(8,128)S(1)}, bf16[256,1152]{1,0:T(8,128)(2,1)S(1)}) custom-call(s32[1]{0:T(128)} %bitcast.2.place_ref, f32[1]{0:T(128)S(6)} %div.22.scale_ref, bf16[256,1152]{1,0:T(8,128)(2,1)S(1)} %get-tuple-element.64.mine, bf16[256,1152]{1,0:T(8,128)(2,1)S(1)} %collective-permute-done.18.theirs, ...), custom_call_target="tpu_custom_call" | custom-call | flops 1358954496 | bytes 5308416 | tf_op jit(solution)/shard_map/pallas_call | solution.py:376
  113.7 13.0 %collective-permute-done.19.theirs = bf16[256,1152]{1,0:T(8,128)(2,1)S(1)} collective-permute-done((bf16[256,1152]{1,0:T(8,128)(2,1)S(1)}, bf16[256,1152]{1,0:T(8,128)(2,1)S(1)}, u32[]{:S(2)}, u32[]{:S(2)}) %collective-permute-start.19) | collective-permute-done | bytes 589856 | tf_op jit(solution)/shard_map/ppermute | solution.py:169
  126.7 2.9 %shard_map.118 = (bf16[576,256]{1,0:T(8,128)(2,1)S(1)}, bf16[576,256]{1,0:T(8,128)(2,1)S(1)}) custom-call(s32[1]{0:T(128)} %bitcast.2.place_ref, f32[1]{0:T(128)S(6)} %div.22.scale_ref, bf16[256,1152]{1,0:T(8,128)(2,1)S(1)} %get-tuple-element.66.mine, bf16[256,1152]{1,0:T(8,128)(2,1)S(1)} %collective-permute-done.19.theirs, ...), custom_call_target="tpu_custom_call" | custom-call | flops 1358954496 | bytes 5308416 | tf_op jit(solution)/shard_map/pallas_call | solution.py:376
  132.7 9.7 %collective-permute-start.23 = (bf16[576,512]{1,0:T(8,128)(2,1)S(1)}, bf16[576,512]{1,0:T(8,128)(2,1)S(1)}, u32[]{:S(2)}, u32[]{:S(2)}) collective-permute-start(bf16[576,512]{1,0:T(8,128)(2,1)S(1)} %maximum_select_fusion.refs_4_), channel_id=1, source_target_pairs={{0,4},{4,0},{12,8},{16,20},{28,24},{1,5},{5,1},{13,9},{17,21},{29,... | collective-permute-start | bytes 1769480 | tf_op jit(solution)/shard_map/ppermute | solution.py:645
  142.3 3.5 %collective-permute-start.22 = (bf16[576,512]{1,0:T(8,128)(2,1)S(1)}, bf16[576,512]{1,0:T(8,128)(2,1)S(1)}, u32[]{:S(2)}, u32[]{:S(2)}) collective-permute-start(bf16[576,512]{1,0:T(8,128)(2,1)S(1)} %maximum_select_fusion.refs_4_), channel_id=1, source_target_pairs={{0,16},{4,20},{12,28},{16,0},{28,12},{1,17},{5,21},{13,29},{17,1},... | collective-permute-start | bytes 1769480 | tf_op jit(solution)/shard_map/ppermute | solution.py:654
  147.9 3.9 %collective-permute-done.25 = bf16[576,512]{1,0:T(8,128)(2,1)S(1)} collective-permute-done((bf16[576,512]{1,0:T(8,128)(2,1)S(1)}, bf16[576,512]{1,0:T(8,128)(2,1)S(1)}, u32[]{:S(2)}, u32[]{:S(2)}) %collective-permute-start.25) | collective-permute-done | bytes 589856 | tf_op jit(solution)/shard_map/ppermute | solution.py:662
  151.9 3.4 %collective-permute-start.26 = (bf16[576,512]{1,0:T(8,128)(2,1)S(1)}, bf16[576,512]{1,0:T(8,128)(2,1)S(1)}, u32[]{:S(2)}, u32[]{:S(2)}) collective-permute-start(bf16[576,512]{1,0:T(8,128)(2,1)S(1)} %broadcast_select_fusion.refs_0_), channel_id=1, source_target_pairs={{0,16},{5,21},{10,26},{15,31},{16,0},{21,5},{26,10},{31,15}} | collective-permute-start | bytes 1769480 | tf_op jit(solution)/shard_map/ppermute | solution.py:692
  155.4 5.1 %collective-permute-done.23.refs_5_ = bf16[576,512]{1,0:T(8,128)(2,1)S(1)} collective-permute-done((bf16[576,512]{1,0:T(8,128)(2,1)S(1)}, bf16[576,512]{1,0:T(8,128)(2,1)S(1)}, u32[]{:S(2)}, u32[]{:S(2)}) %collective-permute-start.23) | collective-permute-done | bytes 589856 | tf_op jit(solution)/shard_map/ppermute | solution.py:645
  168.5 9.5 %collective-permute-done.24.refs_5_ = bf16[576,512]{1,0:T(8,128)(2,1)S(1)} collective-permute-done((bf16[576,512]{1,0:T(8,128)(2,1)S(1)}, bf16[576,512]{1,0:T(8,128)(2,1)S(1)}, u32[]{:S(2)}, u32[]{:S(2)}) %collective-permute-start.24) | collective-permute-done | bytes 589856 | tf_op jit(solution)/shard_map/ppermute | solution.py:654
  184.9 4.4 %collective-permute-done.32 = f32[8,576]{1,0:T(8,128)S(1)} collective-permute-done((f32[8,576]{1,0:T(8,128)S(1)}, f32[8,576]{1,0:T(8,128)S(1)}, u32[]{:S(2)}, u32[]{:S(2)}) %collective-permute-start.32) | collective-permute-done | bytes 18464 | tf_op jit(solution)/shard_map/ppermute | solution.py:709
  191.4 5.2 %collective-permute-done.30.refs_7_ = bf16[576,512]{1,0:T(8,128)(2,1)} collective-permute-done((bf16[576,512]{1,0:T(8,128)(2,1)}, bf16[576,512]{1,0:T(8,128)(2,1)}, u32[]{:S(2)}, u32[]{:S(2)}) %collective-permute-start.30) | collective-permute-done | bytes 589856 | tf_op jit(solution)/shard_map/ppermute | solution.py:645
  205.1 5.5 %shard_map.119 = (f32[4,576,576]{2,1,0:T(8,128)}, f32[576,2048]{1,0:T(8,128)}) custom-call(s32[3]{0:T(128)} %add_add_fusion.1.where_ref, f32[1,2048]{1,0:T(1,128)} %bitcast.90, bf16[512,2048]{1,0:T(8,128)(2,1)} %compare_convert_fusion.matches, bf16[576,512]{1,0:T(8,128)(2,1)} %copy-done.3, bf16[576,512]{1,0:T(8,128)(2,1)} %collective-permute-done.36.refs_1_, ...), custom_call_target="tpu_custom_call" | custom-call | flops 1019215872 | bytes 6340608 | tf_op jit(solution)/shard_map/pallas_call | solution.py:465
  210.8 3.0 %collective-permute-done.33.refs_7_ = bf16[576,512]{1,0:T(8,128)(2,1)} collective-permute-done((bf16[576,512]{1,0:T(8,128)(2,1)}, bf16[576,512]{1,0:T(8,128)(2,1)}, u32[]{:S(2)}, u32[]{:S(2)}) %collective-permute-start.33) | collective-permute-done | bytes 589856 | tf_op jit(solution)/shard_map/ppermute | solution.py:654
  218.5 5.6 %shard_map.120 = (f32[4,576,576]{2,1,0:T(8,128)}, f32[576,2048]{1,0:T(8,128)}) custom-call(s32[3]{0:T(128)} %add_add_fusion.where_ref, f32[1,2048]{1,0:T(1,128)} %bitcast.91, bf16[512,2048]{1,0:T(8,128)(2,1)} %compare_convert_fusion.matches, bf16[576,512]{1,0:T(8,128)(2,1)} %copy-done.5, ...), custom_call_target="tpu_custom_call", output_to_operand_aliasing={{0}: (11, {}), {1}: (12, {})} | custom-call | flops 1019215872 | bytes 6340608 | tf_op jit(solution)/shard_map/pallas_call | solution.py:465
  (164 shorter events, 76.9 us)
Async XLA Ops:
  0.6 14.2 %collective-permute-start.7 = (s32[256]{0:T(256)}, s32[256]{0:T(256)S(1)}, u32[]{:S(2)}, u32[]{:S(2)}) collective-permute-start(s32[256]{0:T(256)} %param.10), channel_id=1, source_target_pairs={{0,16},{16,0},{1,17},{17,1},{2,18},{18,2},{3,19},{19,3},{4,20},{20... | collective-permute-start | bytes 3080 | tf_op jit(solution)/shard_map/ppermute | solution.py:169
  3.6 15.4 %collective-permute-start.5 = (bf16[8,256]{1,0:T(8,128)(2,1)}, bf16[8,256]{1,0:T(8,128)(2,1)S(1)}, u32[]{:S(2)}, u32[]{:S(2)}) collective-permute-start(bf16[8,256]{1,0:T(8,128)(2,1)} %param.9), channel_id=1, source_target_pairs={{0,16},{16,0},{1,17},{17,1},{2,18},{18,2},{3,19},{19,3},{4,20},{20... | collective-permute-start | bytes 12296 | tf_op jit(solution)/shard_map/ppermute | solution.py:169
  7.1 19.4 %collective-permute-start.2 = (bf16[304,256]{1,0:T(8,128)(2,1)}, bf16[304,256]{1,0:T(8,128)(2,1)S(1)}, u32[]{:S(2)}, u32[]{:S(2)}) collective-permute-start(bf16[304,256]{1,0:T(8,128)(2,1)} %pad_maximum_fusion.4), channel_id=1, source_target_pairs={{0,12},{4,8},{8,4},{12,0},{1,13},{5,9},{9,5},{13,1},{2,14},{6,10},... | collective-permute-start | bytes 466952 | tf_op jit(solution)/shard_map/ppermute | solution.py:169
  11.8 16.3 %collective-permute-start = (bf16[304,256]{1,0:T(8,128)(2,1)}, bf16[304,256]{1,0:T(8,128)(2,1)S(1)}, u32[]{:S(2)}, u32[]{:S(2)}) collective-permute-start(bf16[304,256]{1,0:T(8,128)(2,1)} %pad_maximum_fusion.2), channel_id=1, source_target_pairs={{0,4},{4,0},{8,12},{12,8},{1,5},{5,1},{9,13},{13,9},{2,6},{6,2},{1... | collective-permute-start | bytes 466952 | tf_op jit(solution)/shard_map/ppermute | solution.py:169
  12.5 28.5 %collective-permute-start.1 = (bf16[304,256]{1,0:T(8,128)(2,1)}, bf16[304,256]{1,0:T(8,128)(2,1)}, u32[]{:S(2)}, u32[]{:S(2)}) collective-permute-start(bf16[304,256]{1,0:T(8,128)(2,1)} %pad_maximum_fusion.3), channel_id=1, source_target_pairs={{0,8},{4,12},{8,0},{12,4},{1,9},{5,13},{9,1},{13,5},{2,10},{6,14},... | collective-permute-start | bytes 466952 | tf_op jit(solution)/shard_map/ppermute | solution.py:169
  14.8 40.8 %collective-permute-start.4 = (bf16[576,576]{1,0:T(8,128)(2,1)S(1)}, bf16[576,576]{1,0:T(8,128)(2,1)S(1)}, u32[]{:S(2)}, u32[]{:S(2)}) collective-permute-start(bf16[576,576]{1,0:T(8,128)(2,1)S(1)} %fusion.3), channel_id=1, source_target_pairs={{0,8},{4,12},{8,0},{12,4},{1,9},{5,13},{9,1},{13,5},{2,10},{6,14},... | collective-permute-start | bytes 1990664 | tf_op jit(solution)/shard_map/ppermute | solution.py:169
  23.9 35.0 %collective-permute-start.6 = (bf16[576,576]{1,0:T(8,128)(2,1)S(1)}, bf16[576,576]{1,0:T(8,128)(2,1)S(1)}, u32[]{:S(2)}, u32[]{:S(2)}) collective-permute-start(bf16[576,576]{1,0:T(8,128)(2,1)S(1)} %get-tuple-element.100), channel_id=1, source_target_pairs={{0,4},{4,0},{8,12},{12,8},{1,5},{5,1},{9,13},{13,9},{2,6},{6,2},{1... | collective-permute-start | bytes 1990664 | tf_op jit(solution)/shard_map/ppermute | solution.py:169
  26.5 17.6 %collective-permute-start.8 = (f32[2,2,144]{2,1,0:T(2,128)S(1)}, f32[2,2,144]{2,1,0:T(2,128)S(1)}, u32[]{:S(2)}, u32[]{:S(2)}) collective-permute-start(f32[2,2,144]{2,1,0:T(2,128)S(1)} %pad_maximum_fusion.6), channel_id=1, source_target_pairs={{0,16},{16,0},{1,17},{17,1},{2,18},{18,2},{3,19},{19,3},{4,20},{20... | collective-permute-start | bytes 6920 | tf_op jit(solution)/shard_map/ppermute | solution.py:169
  59.0 13.5 %collective-permute-start.10 = (bf16[4,304,256]{2,1,0:T(8,128)(2,1)S(1)}, bf16[4,304,256]{2,1,0:T(8,128)(2,1)S(1)}, u32[]{:S(2)}, u32[]{:S(2)}) collective-permute-start(bf16[4,304,256]{2,1,0:T(8,128)(2,1)S(1)} %pad_maximum_fusion.1.refs_0_), channel_id=1, source_target_pairs={{0,2},{1,3},{2,0},{3,1},{4,6},{5,7},{6,4},{7,5},{8,10},{9,11},{10,... | collective-permute-start | bytes 1867784 | tf_op jit(solution)/shard_map/ppermute | solution.py:169
  92.7 15.4 %collective-permute-start.18 = (bf16[256,1152]{1,0:T(8,128)(2,1)S(1)}, bf16[256,1152]{1,0:T(8,128)(2,1)S(1)}, u32[]{:S(2)}, u32[]{:S(2)}) collective-permute-start(bf16[256,1152]{1,0:T(8,128)(2,1)S(1)} %get-tuple-element.64.mine), channel_id=1, source_target_pairs={{0,2},{1,3},{2,0},{3,1},{4,6},{5,7},{6,4},{7,5},{8,10},{9,11},{10,... | collective-permute-start | bytes 1769480 | tf_op jit(solution)/shard_map/ppermute | solution.py:169
  112.1 14.6 %collective-permute-start.19 = (bf16[256,1152]{1,0:T(8,128)(2,1)S(1)}, bf16[256,1152]{1,0:T(8,128)(2,1)S(1)}, u32[]{:S(2)}, u32[]{:S(2)}) collective-permute-start(bf16[256,1152]{1,0:T(8,128)(2,1)S(1)} %get-tuple-element.66.mine), channel_id=1, source_target_pairs={{0,2},{1,3},{2,0},{3,1},{4,6},{5,7},{6,4},{7,5},{8,10},{9,11},{10,... | collective-permute-start | bytes 1769480 | tf_op jit(solution)/shard_map/ppermute | solution.py:169
  131.4 20.5 %collective-permute-start.25 = (bf16[576,512]{1,0:T(8,128)(2,1)S(1)}, bf16[576,512]{1,0:T(8,128)(2,1)S(1)}, u32[]{:S(2)}, u32[]{:S(2)}) collective-permute-start(bf16[576,512]{1,0:T(8,128)(2,1)S(1)} %maximum_select_fusion.refs_4_), channel_id=1, source_target_pairs={{8,0},{9,5},{11,15},{24,16},{25,21},{27,31}} | collective-permute-start | bytes 1769480 | tf_op jit(solution)/shard_map/ppermute | solution.py:662
  132.7 27.8 %collective-permute-start.23 = (bf16[576,512]{1,0:T(8,128)(2,1)S(1)}, bf16[576,512]{1,0:T(8,128)(2,1)S(1)}, u32[]{:S(2)}, u32[]{:S(2)}) collective-permute-start(bf16[576,512]{1,0:T(8,128)(2,1)S(1)} %maximum_select_fusion.refs_4_), channel_id=1, source_target_pairs={{0,4},{4,0},{12,8},{16,20},{28,24},{1,5},{5,1},{13,9},{17,21},{29,... | collective-permute-start | bytes 1769480 | tf_op jit(solution)/shard_map/ppermute | solution.py:645
  142.3 24.4 %collective-permute-start.22 = (bf16[576,512]{1,0:T(8,128)(2,1)S(1)}, bf16[576,512]{1,0:T(8,128)(2,1)S(1)}, u32[]{:S(2)}, u32[]{:S(2)}) collective-permute-start(bf16[576,512]{1,0:T(8,128)(2,1)S(1)} %maximum_select_fusion.refs_4_), channel_id=1, source_target_pairs={{0,16},{4,20},{12,28},{16,0},{28,12},{1,17},{5,21},{13,29},{17,1},... | collective-permute-start | bytes 1769480 | tf_op jit(solution)/shard_map/ppermute | solution.py:654
  145.8 22.6 %collective-permute-start.21 = (bf16[576,512]{1,0:T(8,128)(2,1)S(1)}, bf16[576,512]{1,0:T(8,128)(2,1)}, u32[]{:S(2)}, u32[]{:S(2)}) collective-permute-start(bf16[576,512]{1,0:T(8,128)(2,1)S(1)} %maximum_select_fusion.refs_4_), channel_id=1, source_target_pairs={{0,8},{4,12},{12,4},{16,24},{28,20},{1,9},{5,13},{13,5},{17,25},{2... | collective-permute-start | bytes 1769480 | tf_op jit(solution)/shard_map/ppermute | solution.py:645
  151.9 16.6 %collective-permute-start.26 = (bf16[576,512]{1,0:T(8,128)(2,1)S(1)}, bf16[576,512]{1,0:T(8,128)(2,1)S(1)}, u32[]{:S(2)}, u32[]{:S(2)}) collective-permute-start(bf16[576,512]{1,0:T(8,128)(2,1)S(1)} %broadcast_select_fusion.refs_0_), channel_id=1, source_target_pairs={{0,16},{5,21},{10,26},{15,31},{16,0},{21,5},{26,10},{31,15}} | collective-permute-start | bytes 1769480 | tf_op jit(solution)/shard_map/ppermute | solution.py:692
  160.5 17.5 %collective-permute-start.24 = (bf16[576,512]{1,0:T(8,128)(2,1)S(1)}, bf16[576,512]{1,0:T(8,128)(2,1)S(1)}, u32[]{:S(2)}, u32[]{:S(2)}) collective-permute-start(bf16[576,512]{1,0:T(8,128)(2,1)S(1)} %collective-permute-done.23.refs_5_), channel_id=1, source_target_pairs={{0,16},{4,20},{8,24},{20,4},{24,8},{1,17},{5,21},{9,25},{21,5},{25... | collective-permute-start | bytes 1769480 | tf_op jit(solution)/shard_map/ppermute | solution.py:654
  163.9 18.2 %collective-permute-start.37 = (bf16[576,512]{1,0:T(8,128)(2,1)S(1)}, bf16[576,512]{1,0:T(8,128)(2,1)}, u32[]{:S(2)}, u32[]{:S(2)}) collective-permute-start(bf16[576,512]{1,0:T(8,128)(2,1)S(1)} %broadcast_select_fusion.refs_0_), channel_id=1, source_target_pairs={{0,2},{5,7},{10,8},{15,13},{16,18},{21,23},{26,24},{31,29}} | collective-permute-start | bytes 1769480 | tf_op jit(solution)/shard_map/ppermute | solution.py:670
  178.7 17.9 %collective-permute-start.30 = (bf16[576,512]{1,0:T(8,128)(2,1)}, bf16[576,512]{1,0:T(8,128)(2,1)}, u32[]{:S(2)}, u32[]{:S(2)}) collective-permute-start(bf16[576,512]{1,0:T(8,128)(2,1)} %collective-permute-done.21.refs_6_), channel_id=1, source_target_pairs={{4,0},{8,12},{12,8},{20,16},{24,28},{5,1},{9,13},{13,9},{21,17},{2... | collective-permute-start | bytes 1769480 | tf_op jit(solution)/shard_map/ppermute | solution.py:645
  180.0 22.4 %collective-permute-start.36 = (bf16[576,512]{1,0:T(8,128)(2,1)S(1)}, bf16[576,512]{1,0:T(8,128)(2,1)}, u32[]{:S(2)}, u32[]{:S(2)}) collective-permute-start(bf16[576,512]{1,0:T(8,128)(2,1)S(1)} %broadcast_select_fusion.refs_0_), channel_id=1, source_target_pairs={{0,1},{5,4},{10,11},{15,14},{16,17},{21,20},{26,27},{31,30}} | collective-permute-start | bytes 1769480 | tf_op jit(solution)/shard_map/ppermute | solution.py:675
  182.1 21.7 %collective-permute-start.38 = (bf16[576,512]{1,0:T(8,128)(2,1)}, bf16[576,512]{1,0:T(8,128)(2,1)}, u32[]{:S(2)}, u32[]{:S(2)}) collective-permute-start(bf16[576,512]{1,0:T(8,128)(2,1)} %collective-permute-done.37.refs_2_), channel_id=1, source_target_pairs={{2,3},{7,6},{8,9},{13,12},{18,19},{23,22},{24,25},{29,28}} | collective-permute-start | bytes 1769480 | tf_op jit(solution)/shard_map/ppermute | solution.py:680
  189.2 21.5 %collective-permute-start.29 = (bf16[576,512]{1,0:T(8,128)(2,1)S(1)}, bf16[576,512]{1,0:T(8,128)(2,1)}, u32[]{:S(2)}, u32[]{:S(2)}) collective-permute-start(bf16[576,512]{1,0:T(8,128)(2,1)S(1)} %collective-permute-done.26.refs_0_), channel_id=1, source_target_pairs={{0,2},{5,7},{10,8},{15,13},{16,18},{21,23},{26,24},{31,29}} | collective-permute-start | bytes 1769480 | tf_op jit(solution)/shard_map/ppermute | solution.py:670
  196.6 17.2 %collective-permute-start.33 = (bf16[576,512]{1,0:T(8,128)(2,1)}, bf16[576,512]{1,0:T(8,128)(2,1)}, u32[]{:S(2)}, u32[]{:S(2)}) collective-permute-start(bf16[576,512]{1,0:T(8,128)(2,1)} %collective-permute-done.30.refs_7_), channel_id=1, source_target_pairs={{0,16},{8,24},{12,28},{16,0},{28,12},{1,17},{9,25},{13,29},{17,1},... | collective-permute-start | bytes 1769480 | tf_op jit(solution)/shard_map/ppermute | solution.py:654
  199.5 18.2 %collective-permute-start.28 = (bf16[576,512]{1,0:T(8,128)(2,1)S(1)}, bf16[576,512]{1,0:T(8,128)(2,1)}, u32[]{:S(2)}, u32[]{:S(2)}) collective-permute-start(bf16[576,512]{1,0:T(8,128)(2,1)S(1)} %collective-permute-done.26.refs_0_), channel_id=1, source_target_pairs={{0,1},{5,4},{10,11},{15,14},{16,17},{21,20},{26,27},{31,30}} | collective-permute-start | bytes 1769480 | tf_op jit(solution)/shard_map/ppermute | solution.py:675
  (39 other events, 513.8 us)

commit v18 on v17

--- a/solution.py
+++ b/solution.py
@@ -701,15 +701,17 @@
     router_cols = jnp.where(layer == 1, router_cols, router_moved)
     side_here = to_side(left_here)
     lefts_here = (left_here, to_core(left_here), side_here, to_far(side_here))
-    near_2, over_0, over_1, left_there, router_cols = lax.optimization_barrier(
-        (near_2, over_0, over_1, left_there, router_cols)
+    near_2, over_0, over_1, router_cols = lax.optimization_barrier(
+        (near_2, over_0, over_1, router_cols)
     )
     near_3 = send(near_2, 1, 2)
     over_2 = across(near_2, 2)
     router_there = lax.ppermute(
         router_cols, everywhere, [(spot(1, t, t), spot(0, t, t)) for t in layers]
     )
-    near_3, over_2, router_there = lax.optimization_barrier((near_3, over_2, router_there))
+    near_3, over_2, router_there, left_there = lax.optimization_barrier(
+        (near_3, over_2, router_there, left_there)
+    )
     over_3 = across(near_3, 3)
     router_cols = jnp.where(shard == 1, router_cols, router_there)
     router_side, router_core = to_side(router_cols), to_core(router_cols)

time: 225 us -> 222 us (0.987)
  waiting for transfers between devices: 107 us -> 102 us
  starting transfers between devices: 64.2 us -> 66.5 us
    ppermute x4, waiting for transfers between devices: 12.5 us -> 0.01 us  [across(): return lax.ppermute(value, axes, moves)]
    ppermute x1, waiting for transfers between devices: 3.9 us -> 9.76 us  [scatter(): lax.ppermute(value, everywhere, [(spot(x, source, s), spot(x, s, s)) for...]
    ppermute x1, waiting for transfers between devices: 0.01 us -> 3.24 us  [layer_plan(): lax.ppermute(left_here, everywhere, [(spot(x, t, t), spot(1 - x, t, t)) f...]
  transfers between devices with their start and end apart: 41 -> 41, of which waited for: 19 -> 17; matrix products, arithmetic and copies ran while one was open for 9% -> 9% of each run, Pallas kernels for 6% -> 6%
where the time goes in v18:
time: 222 us; the launch traced here: 221 us
  waiting for transfers between devices  102 us (46%)
  starting transfers between devices  66.5 us (30%)
  Pallas kernels  28 us (13%)
  other arithmetic  13.3 us (6%)
  local copies, waits for them, and re-layouts  7.8 us (4%)
  between operations  2.89 us (1%)
    ppermute x21, waiting for transfers between devices, swap(): return lax.ppermute(value, axis, [(i, i ^ step) for i in range(size)])  73.7 us
    ppermute x21, starting transfers between devices, swap(): return lax.ppermute(value, axis, [(i, i ^ step) for i in range(size)])  22.1 us
    ppermute x3, starting transfers between devices, send(): return lax.ppermute(value, axes, moves)  14.3 us
    pallas_call x2, Pallas kernels, output_products(): pl.pallas_call(output_kernel, in_specs=[pl.BlockSpec(memory_space=pltpu.S...  11.1 us
    ppermute x3, waiting for transfers between devices, send(): return lax.ppermute(value, axes, moves)  10.9 us
    ppermute x1, waiting for transfers between devices, scatter(): lax.ppermute(value, everywhere, [(spot(x, source, s), spot(x, s, s)) for...  9.76 us
    pallas_call x3, Pallas kernels, chain_call(): pl.pallas_call(kernel, in_specs=[pl.BlockSpec(memory_space=pltpu.SMEM)] *...  9.74 us
    ppermute x4, starting transfers between devices, across(): return lax.ppermute(value, axes, moves)  8.08 us
  transfers between devices with their start and end apart: 41, of which 17 were waited for; matrix products, arithmetic and copies ran while one was open for 9% of the time, Pallas kernels for 6%

profile of v18, /device:TPU:0, one launch (start us, length us, event | category | flops | bytes accessed | tf_op | source)
XLA Modules:
  0.0 221.4 jit_solution(13415857305127383022)
XLA Ops:
  0.6 3.0 %collective-permute-start.7 = (s32[256]{0:T(256)}, s32[256]{0:T(256)S(1)}, u32[]{:S(2)}, u32[]{:S(2)}) collective-permute-start(s32[256]{0:T(256)} %param.10), channel_id=1, source_target_pairs={{0,16},{16,0},{1,17},{17,1},{2,18},{18,2},{3,19},{19,3},{4,20},{20... | collective-permute-start | bytes 3080 | tf_op jit(solution)/shard_map/ppermute | solution.py:169
  7.1 4.1 %collective-permute-start.2 = (bf16[304,256]{1,0:T(8,128)(2,1)}, bf16[304,256]{1,0:T(8,128)(2,1)S(1)}, u32[]{:S(2)}, u32[]{:S(2)}) collective-permute-start(bf16[304,256]{1,0:T(8,128)(2,1)} %pad_maximum_fusion.4), channel_id=1, source_target_pairs={{0,12},{4,8},{8,4},{12,0},{1,13},{5,9},{9,5},{13,1},{2,14},{6,10},... | collective-permute-start | bytes 466952 | tf_op jit(solution)/shard_map/ppermute | solution.py:169
  28.1 12.9 %collective-permute-done.1 = bf16[304,256]{1,0:T(8,128)(2,1)} collective-permute-done((bf16[304,256]{1,0:T(8,128)(2,1)}, bf16[304,256]{1,0:T(8,128)(2,1)}, u32[]{:S(2)}, u32[]{:S(2)}) %collective-permute-start.1) | collective-permute-done | bytes 155680 | tf_op jit(solution)/shard_map/ppermute | solution.py:169
  44.1 4.8 %collective-permute-done.3 = bf16[4,144,256]{2,1,0:T(8,128)(2,1)S(1)} collective-permute-done((bf16[4,144,256]{2,1,0:T(8,128)(2,1)S(1)}, bf16[4,144,256]{2,1,0:T(8,128)(2,1)S(1)}, u32[]{:S(2)}, u32[]{:S(2)}) %collective-permute-start.3) | collective-permute-done | bytes 294944 | tf_op jit(solution)/shard_map/ppermute | solution.py:169
  48.9 6.7 %collective-permute-done.4.refs_0_ = bf16[576,576]{1,0:T(8,128)(2,1)S(1)} collective-permute-done((bf16[576,576]{1,0:T(8,128)(2,1)S(1)}, bf16[576,576]{1,0:T(8,128)(2,1)S(1)}, u32[]{:S(2)}, u32[]{:S(2)}) %collective-permute-start.4) | collective-permute-done | bytes 663584 | tf_op jit(solution)/shard_map/ppermute | solution.py:169
  55.6 3.3 %collective-permute-done.6.refs_0_ = bf16[576,576]{1,0:T(8,128)(2,1)S(1)} collective-permute-done((bf16[576,576]{1,0:T(8,128)(2,1)S(1)}, bf16[576,576]{1,0:T(8,128)(2,1)S(1)}, u32[]{:S(2)}, u32[]{:S(2)}) %collective-permute-start.6) | collective-permute-done | bytes 663584 | tf_op jit(solution)/shard_map/ppermute | solution.py:169
  62.0 9.1 %collective-permute-done.11.refs_0_ = bf16[288,576]{1,0:T(8,128)(2,1)S(1)} collective-permute-done((bf16[288,576]{1,0:T(8,128)(2,1)S(1)}, bf16[288,576]{1,0:T(8,128)(2,1)S(1)}, u32[]{:S(2)}, u32[]{:S(2)}) %collective-permute-start.11) | collective-permute-done | bytes 331808 | tf_op jit(solution)/shard_map/ppermute | solution.py:169
  74.7 3.6 %shard_map.111 = (bf16[2,2304,256]{2,1,0:T(8,128)(2,1)S(1)}, bf16[256,2304]{1,0:T(8,128)(2,1)S(1)}, f32[4,1,576]{2,1,0:T(1,128)S(1)}, f32[1]{0:T(128)}) custom-call(s32[4]{0:T(128)S(1)} %pad_add_fusion.place_ref, bf16[4,304,256]{2,1,0:T(8,128)(2,1)S(1)} %pad_maximum_fusion.1.refs_0_, bf16[4,304,256]{2,1,0:T(8,128)(2,1)} %collective-permute-done.9.refs_1_, ...), custom_call_target="tpu_custom_call" | custom-call | flops 37748736 | bytes 8257536 | tf_op jit(solution)/shard_map/pallas_call | solution.py:241
  81.0 4.7 %collective-permute-done.13.refs_1_ = bf16[288,576]{1,0:T(8,128)(2,1)} collective-permute-done((bf16[288,576]{1,0:T(8,128)(2,1)}, bf16[288,576]{1,0:T(8,128)(2,1)}, u32[]{:S(2)}, u32[]{:S(2)}) %collective-permute-start.13) | collective-permute-done | bytes 331808 | tf_op jit(solution)/shard_map/ppermute | solution.py:169
  89.8 2.9 %shard_map.116 = (f32[2,256,576]{2,1,0:T(8,128)S(1)}, bf16[256,1152]{1,0:T(8,128)(2,1)S(1)}) custom-call(s32[1]{0:T(128)} %bitcast.2.place_ref, f32[1]{0:T(128)S(6)} %div.22.scale_ref, bf16[256,2304]{1,0:T(8,128)(2,1)S(1)} %get-tuple-element.57.rows, f32[4,1,576]{2,1,0:T(1,128)S(1)} %get-tuple-element.58.diag, bf16[576,576]{1,0:T(8,128)(2,1)S(1)} %shard_map.112.refs_0_, ...), custom_call_target="tpu_custom_call" | custom-call | flops 1358954496 | bytes 5308416 | tf_op jit(solution)/shard_map/pallas_call | solution.py:376
  94.3 13.8 %collective-permute-done.18.theirs = bf16[256,1152]{1,0:T(8,128)(2,1)S(1)} collective-permute-done((bf16[256,1152]{1,0:T(8,128)(2,1)S(1)}, bf16[256,1152]{1,0:T(8,128)(2,1)S(1)}, u32[]{:S(2)}, u32[]{:S(2)}) %collective-permute-start.18) | collective-permute-done | bytes 589856 | tf_op jit(solution)/shard_map/ppermute | solution.py:169
  108.1 4.0 %shard_map.117 = (f32[2,256,576]{2,1,0:T(8,128)S(1)}, bf16[256,1152]{1,0:T(8,128)(2,1)S(1)}) custom-call(s32[1]{0:T(128)} %bitcast.2.place_ref, f32[1]{0:T(128)S(6)} %div.22.scale_ref, bf16[256,1152]{1,0:T(8,128)(2,1)S(1)} %get-tuple-element.64.mine, bf16[256,1152]{1,0:T(8,128)(2,1)S(1)} %collective-permute-done.18.theirs, ...), custom_call_target="tpu_custom_call" | custom-call | flops 1358954496 | bytes 5308416 | tf_op jit(solution)/shard_map/pallas_call | solution.py:376
  113.7 13.0 %collective-permute-done.19.theirs = bf16[256,1152]{1,0:T(8,128)(2,1)S(1)} collective-permute-done((bf16[256,1152]{1,0:T(8,128)(2,1)S(1)}, bf16[256,1152]{1,0:T(8,128)(2,1)S(1)}, u32[]{:S(2)}, u32[]{:S(2)}) %collective-permute-start.19) | collective-permute-done | bytes 589856 | tf_op jit(solution)/shard_map/ppermute | solution.py:169
  126.7 2.9 %shard_map.118 = (bf16[576,256]{1,0:T(8,128)(2,1)S(1)}, bf16[576,256]{1,0:T(8,128)(2,1)S(1)}) custom-call(s32[1]{0:T(128)} %bitcast.2.place_ref, f32[1]{0:T(128)S(6)} %div.22.scale_ref, bf16[256,1152]{1,0:T(8,128)(2,1)S(1)} %get-tuple-element.66.mine, bf16[256,1152]{1,0:T(8,128)(2,1)S(1)} %collective-permute-done.19.theirs, ...), custom_call_target="tpu_custom_call" | custom-call | flops 1358954496 | bytes 5308416 | tf_op jit(solution)/shard_map/pallas_call | solution.py:376
  131.4 10.3 %collective-permute-start.23 = (bf16[576,512]{1,0:T(8,128)(2,1)S(1)}, bf16[576,512]{1,0:T(8,128)(2,1)S(1)}, u32[]{:S(2)}, u32[]{:S(2)}) collective-permute-start(bf16[576,512]{1,0:T(8,128)(2,1)S(1)} %maximum_select_fusion.refs_4_), channel_id=1, source_target_pairs={{0,4},{4,0},{12,8},{16,20},{28,24},{1,5},{5,1},{13,9},{17,21},{29,... | collective-permute-start | bytes 1769480 | tf_op jit(solution)/shard_map/ppermute | solution.py:645
  142.9 3.5 %collective-permute-start.22 = (bf16[576,512]{1,0:T(8,128)(2,1)S(1)}, bf16[576,512]{1,0:T(8,128)(2,1)S(1)}, u32[]{:S(2)}, u32[]{:S(2)}) collective-permute-start(bf16[576,512]{1,0:T(8,128)(2,1)S(1)} %maximum_select_fusion.refs_4_), channel_id=1, source_target_pairs={{0,16},{4,20},{12,28},{16,0},{28,12},{1,17},{5,21},{13,29},{17,1},... | collective-permute-start | bytes 1769480 | tf_op jit(solution)/shard_map/ppermute | solution.py:654
  149.2 9.8 %collective-permute-done.23.refs_5_ = bf16[576,512]{1,0:T(8,128)(2,1)S(1)} collective-permute-done((bf16[576,512]{1,0:T(8,128)(2,1)S(1)}, bf16[576,512]{1,0:T(8,128)(2,1)S(1)}, u32[]{:S(2)}, u32[]{:S(2)}) %collective-permute-start.23) | collective-permute-done | bytes 589856 | tf_op jit(solution)/shard_map/ppermute | solution.py:645
  161.2 9.8 %collective-permute-done.29 = bf16[576,512]{1,0:T(8,128)(2,1)S(1)} collective-permute-done((bf16[576,512]{1,0:T(8,128)(2,1)S(1)}, bf16[576,512]{1,0:T(8,128)(2,1)S(1)}, u32[]{:S(2)}, u32[]{:S(2)}) %collective-permute-start.29) | collective-permute-done | bytes 589856 | tf_op jit(solution)/shard_map/ppermute | solution.py:662
  173.2 2.8 %collective-permute-start.30 = (bf16[576,512]{1,0:T(8,128)(2,1)S(1)}, bf16[576,512]{1,0:T(8,128)(2,1)S(1)}, u32[]{:S(2)}, u32[]{:S(2)}) collective-permute-start(bf16[576,512]{1,0:T(8,128)(2,1)S(1)} %broadcast_select_fusion.refs_0_), channel_id=1, source_target_pairs={{0,16},{5,21},{10,26},{15,31},{16,0},{21,5},{26,10},{31,15}} | collective-permute-start | bytes 1769480 | tf_op jit(solution)/shard_map/ppermute | solution.py:692
  181.8 3.2 %collective-permute-done.30.refs_0_ = bf16[576,512]{1,0:T(8,128)(2,1)S(1)} collective-permute-done((bf16[576,512]{1,0:T(8,128)(2,1)S(1)}, bf16[576,512]{1,0:T(8,128)(2,1)S(1)}, u32[]{:S(2)}, u32[]{:S(2)}) %collective-permute-start.30) | collective-permute-done | bytes 589856 | tf_op jit(solution)/shard_map/ppermute | solution.py:692
  186.3 4.4 %collective-permute-done.28 = f32[8,576]{1,0:T(8,128)S(1)} collective-permute-done((f32[8,576]{1,0:T(8,128)S(1)}, f32[8,576]{1,0:T(8,128)S(1)}, u32[]{:S(2)}, u32[]{:S(2)}) %collective-permute-start.28) | collective-permute-done | bytes 18464 | tf_op jit(solution)/shard_map/ppermute | solution.py:709
  194.4 4.0 %collective-permute-start.32 = (bf16[576,512]{1,0:T(8,128)(2,1)S(1)}, bf16[576,512]{1,0:T(8,128)(2,1)}, u32[]{:S(2)}, u32[]{:S(2)}) collective-permute-start(bf16[576,512]{1,0:T(8,128)(2,1)S(1)} %collective-permute-done.30.refs_0_), channel_id=1, source_target_pairs={{0,2},{5,7},{10,8},{15,13},{16,18},{21,23},{26,24},{31,29}} | collective-permute-start | bytes 1769480 | tf_op jit(solution)/shard_map/ppermute | solution.py:670
  204.7 5.5 %shard_map.119 = (f32[4,576,576]{2,1,0:T(8,128)}, f32[576,2048]{1,0:T(8,128)}) custom-call(s32[3]{0:T(128)} %add_add_fusion.1.where_ref, f32[1,2048]{1,0:T(1,128)} %bitcast.90, bf16[512,2048]{1,0:T(8,128)(2,1)} %compare_convert_fusion.matches, bf16[576,512]{1,0:T(8,128)(2,1)} %copy-done.3, bf16[576,512]{1,0:T(8,128)(2,1)} %collective-permute-done.36.refs_1_, ...), custom_call_target="tpu_custom_call" | custom-call | flops 1019215872 | bytes 6340608 | tf_op jit(solution)/shard_map/pallas_call | solution.py:465
  215.7 5.6 %shard_map.120 = (f32[4,576,576]{2,1,0:T(8,128)}, f32[576,2048]{1,0:T(8,128)}) custom-call(s32[3]{0:T(128)} %add_add_fusion.where_ref, f32[1,2048]{1,0:T(1,128)} %bitcast.91, bf16[512,2048]{1,0:T(8,128)(2,1)} %compare_convert_fusion.matches, bf16[576,512]{1,0:T(8,128)(2,1)} %copy-done.6, ...), custom_call_target="tpu_custom_call", output_to_operand_aliasing={{0}: (11, {}), {1}: (12, {})} | custom-call | flops 1019215872 | bytes 6340608 | tf_op jit(solution)/shard_map/pallas_call | solution.py:465
  (166 shorter events, 71.0 us)
Async XLA Ops:
  0.6 14.1 %collective-permute-start.7 = (s32[256]{0:T(256)}, s32[256]{0:T(256)S(1)}, u32[]{:S(2)}, u32[]{:S(2)}) collective-permute-start(s32[256]{0:T(256)} %param.10), channel_id=1, source_target_pairs={{0,16},{16,0},{1,17},{17,1},{2,18},{18,2},{3,19},{19,3},{4,20},{20... | collective-permute-start | bytes 3080 | tf_op jit(solution)/shard_map/ppermute | solution.py:169
  3.6 15.3 %collective-permute-start.5 = (bf16[8,256]{1,0:T(8,128)(2,1)}, bf16[8,256]{1,0:T(8,128)(2,1)S(1)}, u32[]{:S(2)}, u32[]{:S(2)}) collective-permute-start(bf16[8,256]{1,0:T(8,128)(2,1)} %param.9), channel_id=1, source_target_pairs={{0,16},{16,0},{1,17},{17,1},{2,18},{18,2},{3,19},{19,3},{4,20},{20... | collective-permute-start | bytes 12296 | tf_op jit(solution)/shard_map/ppermute | solution.py:169
  7.1 19.4 %collective-permute-start.2 = (bf16[304,256]{1,0:T(8,128)(2,1)}, bf16[304,256]{1,0:T(8,128)(2,1)S(1)}, u32[]{:S(2)}, u32[]{:S(2)}) collective-permute-start(bf16[304,256]{1,0:T(8,128)(2,1)} %pad_maximum_fusion.4), channel_id=1, source_target_pairs={{0,12},{4,8},{8,4},{12,0},{1,13},{5,9},{9,5},{13,1},{2,14},{6,10},... | collective-permute-start | bytes 466952 | tf_op jit(solution)/shard_map/ppermute | solution.py:169
  11.8 16.3 %collective-permute-start = (bf16[304,256]{1,0:T(8,128)(2,1)}, bf16[304,256]{1,0:T(8,128)(2,1)S(1)}, u32[]{:S(2)}, u32[]{:S(2)}) collective-permute-start(bf16[304,256]{1,0:T(8,128)(2,1)} %pad_maximum_fusion.2), channel_id=1, source_target_pairs={{0,4},{4,0},{8,12},{12,8},{1,5},{5,1},{9,13},{13,9},{2,6},{6,2},{1... | collective-permute-start | bytes 466952 | tf_op jit(solution)/shard_map/ppermute | solution.py:169
  12.5 28.5 %collective-permute-start.1 = (bf16[304,256]{1,0:T(8,128)(2,1)}, bf16[304,256]{1,0:T(8,128)(2,1)}, u32[]{:S(2)}, u32[]{:S(2)}) collective-permute-start(bf16[304,256]{1,0:T(8,128)(2,1)} %pad_maximum_fusion.3), channel_id=1, source_target_pairs={{0,8},{4,12},{8,0},{12,4},{1,9},{5,13},{9,1},{13,5},{2,10},{6,14},... | collective-permute-start | bytes 466952 | tf_op jit(solution)/shard_map/ppermute | solution.py:169
  14.8 40.8 %collective-permute-start.4 = (bf16[576,576]{1,0:T(8,128)(2,1)S(1)}, bf16[576,576]{1,0:T(8,128)(2,1)S(1)}, u32[]{:S(2)}, u32[]{:S(2)}) collective-permute-start(bf16[576,576]{1,0:T(8,128)(2,1)S(1)} %fusion.3), channel_id=1, source_target_pairs={{0,8},{4,12},{8,0},{12,4},{1,9},{5,13},{9,1},{13,5},{2,10},{6,14},... | collective-permute-start | bytes 1990664 | tf_op jit(solution)/shard_map/ppermute | solution.py:169
  23.9 35.0 %collective-permute-start.6 = (bf16[576,576]{1,0:T(8,128)(2,1)S(1)}, bf16[576,576]{1,0:T(8,128)(2,1)S(1)}, u32[]{:S(2)}, u32[]{:S(2)}) collective-permute-start(bf16[576,576]{1,0:T(8,128)(2,1)S(1)} %get-tuple-element.100), channel_id=1, source_target_pairs={{0,4},{4,0},{8,12},{12,8},{1,5},{5,1},{9,13},{13,9},{2,6},{6,2},{1... | collective-permute-start | bytes 1990664 | tf_op jit(solution)/shard_map/ppermute | solution.py:169
  26.5 17.6 %collective-permute-start.8 = (f32[2,2,144]{2,1,0:T(2,128)S(1)}, f32[2,2,144]{2,1,0:T(2,128)S(1)}, u32[]{:S(2)}, u32[]{:S(2)}) collective-permute-start(f32[2,2,144]{2,1,0:T(2,128)S(1)} %pad_maximum_fusion.6), channel_id=1, source_target_pairs={{0,16},{16,0},{1,17},{17,1},{2,18},{18,2},{3,19},{19,3},{4,20},{20... | collective-permute-start | bytes 6920 | tf_op jit(solution)/shard_map/ppermute | solution.py:169
  59.0 13.5 %collective-permute-start.10 = (bf16[4,304,256]{2,1,0:T(8,128)(2,1)S(1)}, bf16[4,304,256]{2,1,0:T(8,128)(2,1)S(1)}, u32[]{:S(2)}, u32[]{:S(2)}) collective-permute-start(bf16[4,304,256]{2,1,0:T(8,128)(2,1)S(1)} %pad_maximum_fusion.1.refs_0_), channel_id=1, source_target_pairs={{0,2},{1,3},{2,0},{3,1},{4,6},{5,7},{6,4},{7,5},{8,10},{9,11},{10,... | collective-permute-start | bytes 1867784 | tf_op jit(solution)/shard_map/ppermute | solution.py:169
  72.5 13.2 %collective-permute-start.13 = (bf16[288,576]{1,0:T(8,128)(2,1)}, bf16[288,576]{1,0:T(8,128)(2,1)}, u32[]{:S(2)}, u32[]{:S(2)}) collective-permute-start(bf16[288,576]{1,0:T(8,128)(2,1)} %get-tuple-element.101), channel_id=1, source_target_pairs={{0,12},{4,8},{8,4},{12,0},{1,13},{5,9},{9,5},{13,1},{2,14},{6,10},... | collective-permute-start | bytes 995336 | tf_op jit(solution)/shard_map/ppermute | solution.py:169
  92.6 15.4 %collective-permute-start.18 = (bf16[256,1152]{1,0:T(8,128)(2,1)S(1)}, bf16[256,1152]{1,0:T(8,128)(2,1)S(1)}, u32[]{:S(2)}, u32[]{:S(2)}) collective-permute-start(bf16[256,1152]{1,0:T(8,128)(2,1)S(1)} %get-tuple-element.64.mine), channel_id=1, source_target_pairs={{0,2},{1,3},{2,0},{3,1},{4,6},{5,7},{6,4},{7,5},{8,10},{9,11},{10,... | collective-permute-start | bytes 1769480 | tf_op jit(solution)/shard_map/ppermute | solution.py:169
  112.1 14.6 %collective-permute-start.19 = (bf16[256,1152]{1,0:T(8,128)(2,1)S(1)}, bf16[256,1152]{1,0:T(8,128)(2,1)S(1)}, u32[]{:S(2)}, u32[]{:S(2)}) collective-permute-start(bf16[256,1152]{1,0:T(8,128)(2,1)S(1)} %get-tuple-element.66.mine), channel_id=1, source_target_pairs={{0,2},{1,3},{2,0},{3,1},{4,6},{5,7},{6,4},{7,5},{8,10},{9,11},{10,... | collective-permute-start | bytes 1769480 | tf_op jit(solution)/shard_map/ppermute | solution.py:169
  131.4 27.6 %collective-permute-start.23 = (bf16[576,512]{1,0:T(8,128)(2,1)S(1)}, bf16[576,512]{1,0:T(8,128)(2,1)S(1)}, u32[]{:S(2)}, u32[]{:S(2)}) collective-permute-start(bf16[576,512]{1,0:T(8,128)(2,1)S(1)} %maximum_select_fusion.refs_4_), channel_id=1, source_target_pairs={{0,4},{4,0},{12,8},{16,20},{28,24},{1,5},{5,1},{13,9},{17,21},{29,... | collective-permute-start | bytes 1769480 | tf_op jit(solution)/shard_map/ppermute | solution.py:645
  141.6 29.4 %collective-permute-start.29 = (bf16[576,512]{1,0:T(8,128)(2,1)S(1)}, bf16[576,512]{1,0:T(8,128)(2,1)S(1)}, u32[]{:S(2)}, u32[]{:S(2)}) collective-permute-start(bf16[576,512]{1,0:T(8,128)(2,1)S(1)} %maximum_select_fusion.refs_4_), channel_id=1, source_target_pairs={{8,0},{9,5},{11,15},{24,16},{25,21},{27,31}} | collective-permute-start | bytes 1769480 | tf_op jit(solution)/shard_map/ppermute | solution.py:662
  142.9 33.1 %collective-permute-start.22 = (bf16[576,512]{1,0:T(8,128)(2,1)S(1)}, bf16[576,512]{1,0:T(8,128)(2,1)S(1)}, u32[]{:S(2)}, u32[]{:S(2)}) collective-permute-start(bf16[576,512]{1,0:T(8,128)(2,1)S(1)} %maximum_select_fusion.refs_4_), channel_id=1, source_target_pairs={{0,16},{4,20},{12,28},{16,0},{28,12},{1,17},{5,21},{13,29},{17,1},... | collective-permute-start | bytes 1769480 | tf_op jit(solution)/shard_map/ppermute | solution.py:654
  146.4 29.7 %collective-permute-start.21 = (bf16[576,512]{1,0:T(8,128)(2,1)S(1)}, bf16[576,512]{1,0:T(8,128)(2,1)S(1)}, u32[]{:S(2)}, u32[]{:S(2)}) collective-permute-start(bf16[576,512]{1,0:T(8,128)(2,1)S(1)} %maximum_select_fusion.refs_4_), channel_id=1, source_target_pairs={{0,8},{4,12},{12,4},{16,24},{28,20},{1,9},{5,13},{13,5},{17,25},{2... | collective-permute-start | bytes 1769480 | tf_op jit(solution)/shard_map/ppermute | solution.py:645
  159.0 17.2 %collective-permute-start.24 = (bf16[576,512]{1,0:T(8,128)(2,1)S(1)}, bf16[576,512]{1,0:T(8,128)(2,1)S(1)}, u32[]{:S(2)}, u32[]{:S(2)}) collective-permute-start(bf16[576,512]{1,0:T(8,128)(2,1)S(1)} %collective-permute-done.23.refs_5_), channel_id=1, source_target_pairs={{0,16},{4,20},{8,24},{20,4},{24,8},{1,17},{5,21},{9,25},{21,5},{25... | collective-permute-start | bytes 1769480 | tf_op jit(solution)/shard_map/ppermute | solution.py:654
  160.5 12.7 %collective-permute-start.25 = (f32[8,576]{1,0:T(8,128)S(1)}, f32[8,576]{1,0:T(8,128)S(1)}, u32[]{:S(2)}, u32[]{:S(2)}) collective-permute-start(f32[8,576]{1,0:T(8,128)S(1)} %convolution_multiply_fusion), channel_id=1, source_target_pairs={{20,16},{22,26},{23,31}} | collective-permute-start | bytes 55304 | tf_op jit(solution)/shard_map/ppermute | solution.py:698
  176.1 14.5 %collective-permute-start.27 = (bf16[576,512]{1,0:T(8,128)(2,1)S(1)}, bf16[576,512]{1,0:T(8,128)(2,1)S(1)}, u32[]{:S(2)}, u32[]{:S(2)}) collective-permute-start(bf16[576,512]{1,0:T(8,128)(2,1)S(1)} %collective-permute-done.21.refs_6_), channel_id=1, source_target_pairs={{4,20},{8,24},{12,28},{20,4},{24,8},{5,21},{9,25},{13,29},{21,5},{... | collective-permute-start | bytes 1769480 | tf_op jit(solution)/shard_map/ppermute | solution.py:654
  176.9 15.0 %collective-permute-start.26 = (bf16[576,512]{1,0:T(8,128)(2,1)S(1)}, bf16[576,512]{1,0:T(8,128)(2,1)}, u32[]{:S(2)}, u32[]{:S(2)}) collective-permute-start(bf16[576,512]{1,0:T(8,128)(2,1)S(1)} %collective-permute-done.21.refs_6_), channel_id=1, source_target_pairs={{4,0},{8,12},{12,8},{20,16},{24,28},{5,1},{9,13},{13,9},{21,17},{2... | collective-permute-start | bytes 1769480 | tf_op jit(solution)/shard_map/ppermute | solution.py:645
  178.2 23.0 %collective-permute-start.36 = (bf16[576,512]{1,0:T(8,128)(2,1)S(1)}, bf16[576,512]{1,0:T(8,128)(2,1)}, u32[]{:S(2)}, u32[]{:S(2)}) collective-permute-start(bf16[576,512]{1,0:T(8,128)(2,1)S(1)} %broadcast_select_fusion.refs_0_), channel_id=1, source_target_pairs={{0,1},{5,4},{10,11},{15,14},{16,17},{21,20},{26,27},{31,30}} | collective-permute-start | bytes 1769480 | tf_op jit(solution)/shard_map/ppermute | solution.py:675
  180.3 22.2 %collective-permute-start.38 = (bf16[576,512]{1,0:T(8,128)(2,1)}, bf16[576,512]{1,0:T(8,128)(2,1)}, u32[]{:S(2)}, u32[]{:S(2)}) collective-permute-start(bf16[576,512]{1,0:T(8,128)(2,1)} %collective-permute-done.37.refs_2_), channel_id=1, source_target_pairs={{2,3},{7,6},{8,9},{13,12},{18,19},{23,22},{24,25},{29,28}} | collective-permute-start | bytes 1769480 | tf_op jit(solution)/shard_map/ppermute | solution.py:680
  191.8 18.4 %collective-permute-start.33 = (bf16[576,512]{1,0:T(8,128)(2,1)}, bf16[576,512]{1,0:T(8,128)(2,1)}, u32[]{:S(2)}, u32[]{:S(2)}) collective-permute-start(bf16[576,512]{1,0:T(8,128)(2,1)} %collective-permute-done.26.refs_7_), channel_id=1, source_target_pairs={{0,16},{8,24},{12,28},{16,0},{28,12},{1,17},{9,25},{13,29},{17,1},... | collective-permute-start | bytes 1769480 | tf_op jit(solution)/shard_map/ppermute | solution.py:654
  194.4 15.8 %collective-permute-start.32 = (bf16[576,512]{1,0:T(8,128)(2,1)S(1)}, bf16[576,512]{1,0:T(8,128)(2,1)}, u32[]{:S(2)}, u32[]{:S(2)}) collective-permute-start(bf16[576,512]{1,0:T(8,128)(2,1)S(1)} %collective-permute-done.30.refs_0_), channel_id=1, source_target_pairs={{0,2},{5,7},{10,8},{15,13},{16,18},{21,23},{26,24},{31,29}} | collective-permute-start | bytes 1769480 | tf_op jit(solution)/shard_map/ppermute | solution.py:670
  (40 other events, 490.2 us)

commit v19 on v18

--- a/solution.py
+++ b/solution.py
@@ -676,6 +676,11 @@
             value, everywhere, [(spot(x, t, t), spot(x, t, t ^ 1)) for x in planes for t in layers]
         )
 
+    def straight_far(value):
+        return lax.ppermute(
+            value, everywhere, [(spot(x, t, t), spot(x, t, t ^ 3)) for x in planes for t in layers]
+        )
+
     def to_far(value):
         return lax.ppermute(
             value,
@@ -724,10 +729,10 @@
         (own, near_1, near_2, near_3),
         (),
     )
-    side_there, over_3, router_side, router_core, made = lax.optimization_barrier(
-        (to_side(left_there), over_3, router_side, router_core, made)
-    )
-    lefts_there = (left_there, to_core(left_there), side_there, to_far(side_there))
+    side_there, far_there, over_3, router_side, router_core, made = lax.optimization_barrier(
+        (to_side(left_there), straight_far(left_there), over_3, router_side, router_core, made)
+    )
+    lefts_there = (left_there, to_core(left_there), side_there, far_there)
     routers = (router_cols, router_core, router_side, to_far(router_side))
     precond_router = routers[3]
     for index in (2, 1, 0):

time: 222 us -> 230 us (1.036); the launches traced: 221 us -> 226 us
  starting transfers between devices: 66.5 us -> 74.7 us
  waiting for transfers between devices: 102 us -> 99.3 us
    ppermute x1, starting transfers between devices: 2.81 us -> 7.01 us  [layer_plan(): lax.ppermute(left_here, everywhere, [(spot(x, t, t), spot(1 - x, t, t)) f...]
    ppermute x3, starting transfers between devices: 14.3 us -> 17.9 us  [send(): return lax.ppermute(value, axes, moves)]
    ppermute x3, waiting for transfers between devices: 0.01 us -> 2.91 us  [to_side(): lax.ppermute(value, everywhere, [(spot(x, t, t), spot(x, t, t ^ 2)) for x...]
    ppermute x3, waiting for transfers between devices: 10.9 us -> 8.23 us  [send(): return lax.ppermute(value, axes, moves)]
  transfers between devices with their start and end apart: 41 -> 41, of which waited for: 17 -> 17; matrix products, arithmetic and copies ran while one was open for 9% -> 7% of each run, Pallas kernels for 6% -> 7%
where the time goes in v19:
time: 230 us; the launch traced here: 226 us
  waiting for transfers between devices  99.3 us (43%)
  starting transfers between devices  74.7 us (32%)
  Pallas kernels  28 us (12%)
  other arithmetic  13.3 us (6%)
  local copies, waits for them, and re-layouts  7.24 us (3%)
  between operations  2.94 us (1%)
    ppermute x21, waiting for transfers between devices, swap(): return lax.ppermute(value, axis, [(i, i ^ step) for i in range(size)])  73.1 us
    ppermute x21, starting transfers between devices, swap(): return lax.ppermute(value, axis, [(i, i ^ step) for i in range(size)])  24.3 us
    ppermute x3, starting transfers between devices, send(): return lax.ppermute(value, axes, moves)  17.9 us
    pallas_call x2, Pallas kernels, output_products(): pl.pallas_call(output_kernel, in_specs=[pl.BlockSpec(memory_space=pltpu.S...  11.1 us
    pallas_call x3, Pallas kernels, chain_call(): pl.pallas_call(kernel, in_specs=[pl.BlockSpec(memory_space=pltpu.SMEM)] *...  9.7 us
    ppermute x1, waiting for transfers between devices, scatter(): lax.ppermute(value, everywhere, [(spot(x, source, s), spot(x, s, s)) for...  9.04 us
    ppermute x3, waiting for transfers between devices, send(): return lax.ppermute(value, axes, moves)  8.23 us
    ppermute x4, starting transfers between devices, across(): return lax.ppermute(value, axes, moves)  7.08 us
  transfers between devices with their start and end apart: 41, of which 17 were waited for; matrix products, arithmetic and copies ran while one was open for 7% of the time, Pallas kernels for 7%

profile of v19, /device:TPU:0, one launch (start us, length us, event | category | flops | bytes accessed | tf_op | source)
XLA Modules:
  0.0 226.3 jit_solution(14876586589582211909)
XLA Ops:
  4.2 3.0 %collective-permute-start = (bf16[304,256]{1,0:T(8,128)(2,1)}, bf16[304,256]{1,0:T(8,128)(2,1)S(1)}, u32[]{:S(2)}, u32[]{:S(2)}) collective-permute-start(bf16[304,256]{1,0:T(8,128)(2,1)} %pad_maximum_fusion.2), channel_id=1, source_target_pairs={{0,4},{4,0},{8,12},{12,8},{1,5},{5,1},{9,13},{13,9},{2,6},{6,2},{1... | collective-permute-start | bytes 466952 | tf_op jit(solution)/shard_map/ppermute | solution.py:169
  7.9 2.6 %collective-permute-start.1 = (bf16[304,256]{1,0:T(8,128)(2,1)}, bf16[304,256]{1,0:T(8,128)(2,1)S(1)}, u32[]{:S(2)}, u32[]{:S(2)}) collective-permute-start(bf16[304,256]{1,0:T(8,128)(2,1)} %pad_maximum_fusion.3), channel_id=1, source_target_pairs={{0,8},{4,12},{8,0},{12,4},{1,9},{5,13},{9,1},{13,5},{2,10},{6,14},... | collective-permute-start | bytes 466952 | tf_op jit(solution)/shard_map/ppermute | solution.py:169
  24.9 2.5 %collective-permute-start.6 = (bf16[576,576]{1,0:T(8,128)(2,1)S(1)}, bf16[576,576]{1,0:T(8,128)(2,1)S(1)}, u32[]{:S(2)}, u32[]{:S(2)}) collective-permute-start(bf16[576,576]{1,0:T(8,128)(2,1)S(1)} %get-tuple-element.102), channel_id=1, source_target_pairs={{0,4},{4,0},{8,12},{12,8},{1,5},{5,1},{9,13},{13,9},{2,6},{6,2},{1... | collective-permute-start | bytes 1990664 | tf_op jit(solution)/shard_map/ppermute | solution.py:169
  28.6 9.8 %collective-permute-done.1 = bf16[304,256]{1,0:T(8,128)(2,1)S(1)} collective-permute-done((bf16[304,256]{1,0:T(8,128)(2,1)}, bf16[304,256]{1,0:T(8,128)(2,1)S(1)}, u32[]{:S(2)}, u32[]{:S(2)}) %collective-permute-start.1) | collective-permute-done | bytes 155680 | tf_op jit(solution)/shard_map/ppermute | solution.py:169
  41.6 4.6 %collective-permute-done.3 = bf16[4,144,256]{2,1,0:T(8,128)(2,1)S(1)} collective-permute-done((bf16[4,144,256]{2,1,0:T(8,128)(2,1)S(1)}, bf16[4,144,256]{2,1,0:T(8,128)(2,1)S(1)}, u32[]{:S(2)}, u32[]{:S(2)}) %collective-permute-start.3) | collective-permute-done | bytes 294944 | tf_op jit(solution)/shard_map/ppermute | solution.py:169
  46.2 10.0 %collective-permute-done.4.refs_0_ = bf16[576,576]{1,0:T(8,128)(2,1)S(1)} collective-permute-done((bf16[576,576]{1,0:T(8,128)(2,1)S(1)}, bf16[576,576]{1,0:T(8,128)(2,1)S(1)}, u32[]{:S(2)}, u32[]{:S(2)}) %collective-permute-start.4) | collective-permute-done | bytes 663584 | tf_op jit(solution)/shard_map/ppermute | solution.py:169
  63.4 7.1 %collective-permute-done.11.refs_0_ = bf16[288,576]{1,0:T(8,128)(2,1)S(1)} collective-permute-done((bf16[288,576]{1,0:T(8,128)(2,1)S(1)}, bf16[288,576]{1,0:T(8,128)(2,1)S(1)}, u32[]{:S(2)}, u32[]{:S(2)}) %collective-permute-start.11) | collective-permute-done | bytes 331808 | tf_op jit(solution)/shard_map/ppermute | solution.py:169
  73.7 3.6 %shard_map.111 = (bf16[2,2304,256]{2,1,0:T(8,128)(2,1)S(1)}, bf16[256,2304]{1,0:T(8,128)(2,1)S(1)}, f32[4,1,576]{2,1,0:T(1,128)S(1)}, f32[1]{0:T(128)}) custom-call(s32[4]{0:T(128)S(1)} %pad_add_fusion.place_ref, bf16[4,304,256]{2,1,0:T(8,128)(2,1)S(1)} %pad_maximum_fusion.1.refs_0_, bf16[4,304,256]{2,1,0:T(8,128)(2,1)} %collective-permute-done.9.refs_1_, ...), custom_call_target="tpu_custom_call" | custom-call | flops 37748736 | bytes 8257536 | tf_op jit(solution)/shard_map/pallas_call | solution.py:241
  77.3 7.2 %collective-permute-done.13.refs_1_ = bf16[288,576]{1,0:T(8,128)(2,1)} collective-permute-done((bf16[288,576]{1,0:T(8,128)(2,1)}, bf16[288,576]{1,0:T(8,128)(2,1)}, u32[]{:S(2)}, u32[]{:S(2)}) %collective-permute-start.13) | collective-permute-done | bytes 331808 | tf_op jit(solution)/shard_map/ppermute | solution.py:169
  91.6 2.8 %shard_map.116 = (f32[2,256,576]{2,1,0:T(8,128)S(1)}, bf16[256,1152]{1,0:T(8,128)(2,1)S(1)}) custom-call(s32[1]{0:T(128)} %bitcast.2.place_ref, f32[1]{0:T(128)S(6)} %div.22.scale_ref, bf16[256,2304]{1,0:T(8,128)(2,1)S(1)} %get-tuple-element.58.rows, f32[4,1,576]{2,1,0:T(1,128)S(1)} %get-tuple-element.59.diag, bf16[576,576]{1,0:T(8,128)(2,1)S(1)} %shard_map.112.refs_0_, ...), custom_call_target="tpu_custom_call" | custom-call | flops 1358954496 | bytes 5308416 | tf_op jit(solution)/shard_map/pallas_call | solution.py:376
  95.8 14.1 %collective-permute-done.18.theirs = bf16[256,1152]{1,0:T(8,128)(2,1)S(1)} collective-permute-done((bf16[256,1152]{1,0:T(8,128)(2,1)S(1)}, bf16[256,1152]{1,0:T(8,128)(2,1)S(1)}, u32[]{:S(2)}, u32[]{:S(2)}) %collective-permute-start.18) | collective-permute-done | bytes 589856 | tf_op jit(solution)/shard_map/ppermute | solution.py:169
  109.9 4.0 %shard_map.117 = (f32[2,256,576]{2,1,0:T(8,128)S(1)}, bf16[256,1152]{1,0:T(8,128)(2,1)S(1)}) custom-call(s32[1]{0:T(128)} %bitcast.2.place_ref, f32[1]{0:T(128)S(6)} %div.22.scale_ref, bf16[256,1152]{1,0:T(8,128)(2,1)S(1)} %get-tuple-element.65.mine, bf16[256,1152]{1,0:T(8,128)(2,1)S(1)} %collective-permute-done.18.theirs, ...), custom_call_target="tpu_custom_call" | custom-call | flops 1358954496 | bytes 5308416 | tf_op jit(solution)/shard_map/pallas_call | solution.py:376
  115.2 13.3 %collective-permute-done.19.theirs = bf16[256,1152]{1,0:T(8,128)(2,1)S(1)} collective-permute-done((bf16[256,1152]{1,0:T(8,128)(2,1)S(1)}, bf16[256,1152]{1,0:T(8,128)(2,1)S(1)}, u32[]{:S(2)}, u32[]{:S(2)}) %collective-permute-start.19) | collective-permute-done | bytes 589856 | tf_op jit(solution)/shard_map/ppermute | solution.py:169
  128.5 2.9 %shard_map.118 = (bf16[576,256]{1,0:T(8,128)(2,1)S(1)}, bf16[576,256]{1,0:T(8,128)(2,1)S(1)}) custom-call(s32[1]{0:T(128)} %bitcast.2.place_ref, f32[1]{0:T(128)S(6)} %div.22.scale_ref, bf16[256,1152]{1,0:T(8,128)(2,1)S(1)} %get-tuple-element.67.mine, bf16[256,1152]{1,0:T(8,128)(2,1)S(1)} %collective-permute-done.19.theirs, ...), custom_call_target="tpu_custom_call" | custom-call | flops 1358954496 | bytes 5308416 | tf_op jit(solution)/shard_map/pallas_call | solution.py:376
  133.2 10.3 %collective-permute-start.23 = (bf16[576,512]{1,0:T(8,128)(2,1)S(1)}, bf16[576,512]{1,0:T(8,128)(2,1)S(1)}, u32[]{:S(2)}, u32[]{:S(2)}) collective-permute-start(bf16[576,512]{1,0:T(8,128)(2,1)S(1)} %maximum_select_fusion.refs_4_), channel_id=1, source_target_pairs={{0,4},{4,0},{12,8},{16,20},{28,24},{1,5},{5,1},{13,9},{17,21},{29,... | collective-permute-start | bytes 1769480 | tf_op jit(solution)/shard_map/ppermute | solution.py:645
  144.8 6.3 %collective-permute-start.21 = (bf16[576,512]{1,0:T(8,128)(2,1)S(1)}, bf16[576,512]{1,0:T(8,128)(2,1)}, u32[]{:S(2)}, u32[]{:S(2)}) collective-permute-start(bf16[576,512]{1,0:T(8,128)(2,1)S(1)} %maximum_select_fusion.refs_4_), channel_id=1, source_target_pairs={{0,8},{4,12},{12,4},{16,24},{28,20},{1,9},{5,13},{13,5},{17,25},{2... | collective-permute-start | bytes 1769480 | tf_op jit(solution)/shard_map/ppermute | solution.py:645
  151.1 3.2 %collective-permute-start.22 = (bf16[576,512]{1,0:T(8,128)(2,1)S(1)}, bf16[576,512]{1,0:T(8,128)(2,1)S(1)}, u32[]{:S(2)}, u32[]{:S(2)}) collective-permute-start(bf16[576,512]{1,0:T(8,128)(2,1)S(1)} %maximum_select_fusion.refs_4_), channel_id=1, source_target_pairs={{0,16},{4,20},{12,28},{16,0},{28,12},{1,17},{5,21},{13,29},{17,1},... | collective-permute-start | bytes 1769480 | tf_op jit(solution)/shard_map/ppermute | solution.py:654
  154.3 8.2 %collective-permute-done.23.refs_5_ = bf16[576,512]{1,0:T(8,128)(2,1)S(1)} collective-permute-done((bf16[576,512]{1,0:T(8,128)(2,1)S(1)}, bf16[576,512]{1,0:T(8,128)(2,1)S(1)}, u32[]{:S(2)}, u32[]{:S(2)}) %collective-permute-start.23) | collective-permute-done | bytes 589856 | tf_op jit(solution)/shard_map/ppermute | solution.py:645
  163.8 9.0 %collective-permute-done.29 = bf16[576,512]{1,0:T(8,128)(2,1)S(1)} collective-permute-done((bf16[576,512]{1,0:T(8,128)(2,1)S(1)}, bf16[576,512]{1,0:T(8,128)(2,1)S(1)}, u32[]{:S(2)}, u32[]{:S(2)}) %collective-permute-start.29) | collective-permute-done | bytes 589856 | tf_op jit(solution)/shard_map/ppermute | solution.py:662
  176.7 7.0 %collective-permute-start.30 = (bf16[576,512]{1,0:T(8,128)(2,1)S(1)}, bf16[576,512]{1,0:T(8,128)(2,1)S(1)}, u32[]{:S(2)}, u32[]{:S(2)}) collective-permute-start(bf16[576,512]{1,0:T(8,128)(2,1)S(1)} %broadcast_select_fusion.refs_0_), channel_id=1, source_target_pairs={{0,16},{5,21},{10,26},{15,31},{16,0},{21,5},{26,10},{31,15}} | collective-permute-start | bytes 1769480 | tf_op jit(solution)/shard_map/ppermute | solution.py:697
  193.4 3.8 %collective-permute-done.28 = f32[8,576]{1,0:T(8,128)S(1)} collective-permute-done((f32[8,576]{1,0:T(8,128)S(1)}, f32[8,576]{1,0:T(8,128)S(1)}, u32[]{:S(2)}, u32[]{:S(2)}) %collective-permute-start.28) | collective-permute-done | bytes 18464 | tf_op jit(solution)/shard_map/ppermute | solution.py:714
  209.5 2.9 %collective-permute-done.35 = f32[8,576]{1,0:T(8,128)S(1)} collective-permute-done((f32[8,576]{1,0:T(8,128)S(1)}, f32[8,576]{1,0:T(8,128)S(1)}, u32[]{:S(2)}, u32[]{:S(2)}) %collective-permute-start.35) | collective-permute-done | bytes 18464 | tf_op jit(solution)/shard_map/ppermute | solution.py:670
  213.7 5.5 %shard_map.119 = (f32[4,576,576]{2,1,0:T(8,128)}, f32[576,2048]{1,0:T(8,128)}) custom-call(s32[3]{0:T(128)} %add_add_fusion.1.where_ref, f32[1,2048]{1,0:T(1,128)} %bitcast.90, bf16[512,2048]{1,0:T(8,128)(2,1)} %compare_convert_fusion.matches, bf16[576,512]{1,0:T(8,128)(2,1)} %copy-done.3, bf16[576,512]{1,0:T(8,128)(2,1)} %copy-done.10, ...), custom_call_target="tpu_custom_call" | custom-call | flops 1019215872 | bytes 6340608 | tf_op jit(solution)/shard_map/pallas_call | solution.py:465
  220.0 5.6 %shard_map.120 = (f32[4,576,576]{2,1,0:T(8,128)}, f32[576,2048]{1,0:T(8,128)}) custom-call(s32[3]{0:T(128)} %add_add_fusion.where_ref, f32[1,2048]{1,0:T(1,128)} %bitcast.91, bf16[512,2048]{1,0:T(8,128)(2,1)} %compare_convert_fusion.matches, bf16[576,512]{1,0:T(8,128)(2,1)} %copy-done.6, ...), custom_call_target="tpu_custom_call", output_to_operand_aliasing={{0}: (11, {}), {1}: (12, {})} | custom-call | flops 1019215872 | bytes 6340608 | tf_op jit(solution)/shard_map/pallas_call | solution.py:465
  (160 shorter events, 73.9 us)
Async XLA Ops:
  4.2 23.8 %collective-permute-start = (bf16[304,256]{1,0:T(8,128)(2,1)}, bf16[304,256]{1,0:T(8,128)(2,1)S(1)}, u32[]{:S(2)}, u32[]{:S(2)}) collective-permute-start(bf16[304,256]{1,0:T(8,128)(2,1)} %pad_maximum_fusion.2), channel_id=1, source_target_pairs={{0,4},{4,0},{8,12},{12,8},{1,5},{5,1},{9,13},{13,9},{2,6},{6,2},{1... | collective-permute-start | bytes 466952 | tf_op jit(solution)/shard_map/ppermute | solution.py:169
  7.9 30.5 %collective-permute-start.1 = (bf16[304,256]{1,0:T(8,128)(2,1)}, bf16[304,256]{1,0:T(8,128)(2,1)S(1)}, u32[]{:S(2)}, u32[]{:S(2)}) collective-permute-start(bf16[304,256]{1,0:T(8,128)(2,1)} %pad_maximum_fusion.3), channel_id=1, source_target_pairs={{0,8},{4,12},{8,0},{12,4},{1,9},{5,13},{9,1},{13,5},{2,10},{6,14},... | collective-permute-start | bytes 466952 | tf_op jit(solution)/shard_map/ppermute | solution.py:169
  11.1 27.2 %collective-permute-start.2 = (bf16[304,256]{1,0:T(8,128)(2,1)}, bf16[304,256]{1,0:T(8,128)(2,1)}, u32[]{:S(2)}, u32[]{:S(2)}) collective-permute-start(bf16[304,256]{1,0:T(8,128)(2,1)} %pad_maximum_fusion.4), channel_id=1, source_target_pairs={{0,12},{4,8},{8,4},{12,0},{1,13},{5,9},{9,5},{13,1},{2,14},{6,10},... | collective-permute-start | bytes 466952 | tf_op jit(solution)/shard_map/ppermute | solution.py:169
  16.4 39.8 %collective-permute-start.4 = (bf16[576,576]{1,0:T(8,128)(2,1)S(1)}, bf16[576,576]{1,0:T(8,128)(2,1)S(1)}, u32[]{:S(2)}, u32[]{:S(2)}) collective-permute-start(bf16[576,576]{1,0:T(8,128)(2,1)S(1)} %fusion.3), channel_id=1, source_target_pairs={{0,8},{4,12},{8,0},{12,4},{1,9},{5,13},{9,1},{13,5},{2,10},{6,14},... | collective-permute-start | bytes 1990664 | tf_op jit(solution)/shard_map/ppermute | solution.py:169
  24.9 33.7 %collective-permute-start.6 = (bf16[576,576]{1,0:T(8,128)(2,1)S(1)}, bf16[576,576]{1,0:T(8,128)(2,1)S(1)}, u32[]{:S(2)}, u32[]{:S(2)}) collective-permute-start(bf16[576,576]{1,0:T(8,128)(2,1)S(1)} %get-tuple-element.102), channel_id=1, source_target_pairs={{0,4},{4,0},{8,12},{12,8},{1,5},{5,1},{9,13},{13,9},{2,6},{6,2},{1... | collective-permute-start | bytes 1990664 | tf_op jit(solution)/shard_map/ppermute | solution.py:169
  28.0 13.6 %collective-permute-start.8 = (f32[2,2,144]{2,1,0:T(2,128)S(1)}, f32[2,2,144]{2,1,0:T(2,128)S(1)}, u32[]{:S(2)}, u32[]{:S(2)}) collective-permute-start(f32[2,2,144]{2,1,0:T(2,128)S(1)} %pad_maximum_fusion.6), channel_id=1, source_target_pairs={{0,16},{16,0},{1,17},{17,1},{2,18},{18,2},{3,19},{19,3},{4,20},{20... | collective-permute-start | bytes 6920 | tf_op jit(solution)/shard_map/ppermute | solution.py:169
  58.7 12.5 %collective-permute-start.10 = (bf16[4,304,256]{2,1,0:T(8,128)(2,1)S(1)}, bf16[4,304,256]{2,1,0:T(8,128)(2,1)S(1)}, u32[]{:S(2)}, u32[]{:S(2)}) collective-permute-start(bf16[4,304,256]{2,1,0:T(8,128)(2,1)S(1)} %pad_maximum_fusion.1.refs_0_), channel_id=1, source_target_pairs={{0,2},{1,3},{2,0},{3,1},{4,6},{5,7},{6,4},{7,5},{8,10},{9,11},{10,... | collective-permute-start | bytes 1867784 | tf_op jit(solution)/shard_map/ppermute | solution.py:169
  71.2 13.2 %collective-permute-start.13 = (bf16[288,576]{1,0:T(8,128)(2,1)}, bf16[288,576]{1,0:T(8,128)(2,1)}, u32[]{:S(2)}, u32[]{:S(2)}) collective-permute-start(bf16[288,576]{1,0:T(8,128)(2,1)} %get-tuple-element.103), channel_id=1, source_target_pairs={{0,12},{4,8},{8,4},{12,0},{1,13},{5,9},{9,5},{13,1},{2,14},{6,10},... | collective-permute-start | bytes 995336 | tf_op jit(solution)/shard_map/ppermute | solution.py:169
  94.5 15.5 %collective-permute-start.18 = (bf16[256,1152]{1,0:T(8,128)(2,1)S(1)}, bf16[256,1152]{1,0:T(8,128)(2,1)S(1)}, u32[]{:S(2)}, u32[]{:S(2)}) collective-permute-start(bf16[256,1152]{1,0:T(8,128)(2,1)S(1)} %get-tuple-element.65.mine), channel_id=1, source_target_pairs={{0,2},{1,3},{2,0},{3,1},{4,6},{5,7},{6,4},{7,5},{8,10},{9,11},{10,... | collective-permute-start | bytes 1769480 | tf_op jit(solution)/shard_map/ppermute | solution.py:169
  113.9 14.6 %collective-permute-start.19 = (bf16[256,1152]{1,0:T(8,128)(2,1)S(1)}, bf16[256,1152]{1,0:T(8,128)(2,1)S(1)}, u32[]{:S(2)}, u32[]{:S(2)}) collective-permute-start(bf16[256,1152]{1,0:T(8,128)(2,1)S(1)} %get-tuple-element.67.mine), channel_id=1, source_target_pairs={{0,2},{1,3},{2,0},{3,1},{4,6},{5,7},{6,4},{7,5},{8,10},{9,11},{10,... | collective-permute-start | bytes 1769480 | tf_op jit(solution)/shard_map/ppermute | solution.py:169
  133.2 29.3 %collective-permute-start.23 = (bf16[576,512]{1,0:T(8,128)(2,1)S(1)}, bf16[576,512]{1,0:T(8,128)(2,1)S(1)}, u32[]{:S(2)}, u32[]{:S(2)}) collective-permute-start(bf16[576,512]{1,0:T(8,128)(2,1)S(1)} %maximum_select_fusion.refs_4_), channel_id=1, source_target_pairs={{0,4},{4,0},{12,8},{16,20},{28,24},{1,5},{5,1},{13,9},{17,21},{29,... | collective-permute-start | bytes 1769480 | tf_op jit(solution)/shard_map/ppermute | solution.py:645
  143.5 29.4 %collective-permute-start.29 = (bf16[576,512]{1,0:T(8,128)(2,1)S(1)}, bf16[576,512]{1,0:T(8,128)(2,1)S(1)}, u32[]{:S(2)}, u32[]{:S(2)}) collective-permute-start(bf16[576,512]{1,0:T(8,128)(2,1)S(1)} %maximum_select_fusion.refs_4_), channel_id=1, source_target_pairs={{8,0},{9,5},{11,15},{24,16},{25,21},{27,31}} | collective-permute-start | bytes 1769480 | tf_op jit(solution)/shard_map/ppermute | solution.py:662
  144.8 39.6 %collective-permute-start.21 = (bf16[576,512]{1,0:T(8,128)(2,1)S(1)}, bf16[576,512]{1,0:T(8,128)(2,1)}, u32[]{:S(2)}, u32[]{:S(2)}) collective-permute-start(bf16[576,512]{1,0:T(8,128)(2,1)S(1)} %maximum_select_fusion.refs_4_), channel_id=1, source_target_pairs={{0,8},{4,12},{12,4},{16,24},{28,20},{1,9},{5,13},{13,5},{17,25},{2... | collective-permute-start | bytes 1769480 | tf_op jit(solution)/shard_map/ppermute | solution.py:645
  151.1 33.3 %collective-permute-start.22 = (bf16[576,512]{1,0:T(8,128)(2,1)S(1)}, bf16[576,512]{1,0:T(8,128)(2,1)S(1)}, u32[]{:S(2)}, u32[]{:S(2)}) collective-permute-start(bf16[576,512]{1,0:T(8,128)(2,1)S(1)} %maximum_select_fusion.refs_4_), channel_id=1, source_target_pairs={{0,16},{4,20},{12,28},{16,0},{28,12},{1,17},{5,21},{13,29},{17,1},... | collective-permute-start | bytes 1769480 | tf_op jit(solution)/shard_map/ppermute | solution.py:654
  162.5 21.9 %collective-permute-start.24 = (bf16[576,512]{1,0:T(8,128)(2,1)S(1)}, bf16[576,512]{1,0:T(8,128)(2,1)S(1)}, u32[]{:S(2)}, u32[]{:S(2)}) collective-permute-start(bf16[576,512]{1,0:T(8,128)(2,1)S(1)} %collective-permute-done.23.refs_5_), channel_id=1, source_target_pairs={{0,16},{4,20},{8,24},{20,4},{24,8},{1,17},{5,21},{9,25},{21,5},{25... | collective-permute-start | bytes 1769480 | tf_op jit(solution)/shard_map/ppermute | solution.py:654
  172.9 14.9 %collective-permute-start.38 = (bf16[576,512]{1,0:T(8,128)(2,1)S(1)}, bf16[576,512]{1,0:T(8,128)(2,1)}, u32[]{:S(2)}, u32[]{:S(2)}) collective-permute-start(bf16[576,512]{1,0:T(8,128)(2,1)S(1)} %broadcast_select_fusion.refs_0_), channel_id=1, source_target_pairs={{0,2},{5,7},{10,8},{15,13},{16,18},{21,23},{26,24},{31,29}} | collective-permute-start | bytes 1769480 | tf_op jit(solution)/shard_map/ppermute | solution.py:670
  176.7 14.9 %collective-permute-start.30 = (bf16[576,512]{1,0:T(8,128)(2,1)S(1)}, bf16[576,512]{1,0:T(8,128)(2,1)S(1)}, u32[]{:S(2)}, u32[]{:S(2)}) collective-permute-start(bf16[576,512]{1,0:T(8,128)(2,1)S(1)} %broadcast_select_fusion.refs_0_), channel_id=1, source_target_pairs={{0,16},{5,21},{10,26},{15,31},{16,0},{21,5},{26,10},{31,15}} | collective-permute-start | bytes 1769480 | tf_op jit(solution)/shard_map/ppermute | solution.py:697
  184.5 12.7 %collective-permute-start.26 = (bf16[576,512]{1,0:T(8,128)(2,1)}, bf16[576,512]{1,0:T(8,128)(2,1)}, u32[]{:S(2)}, u32[]{:S(2)}) collective-permute-start(bf16[576,512]{1,0:T(8,128)(2,1)} %collective-permute-done.21.refs_6_), channel_id=1, source_target_pairs={{4,0},{8,12},{12,8},{20,16},{24,28},{5,1},{9,13},{13,9},{21,17},{2... | collective-permute-start | bytes 1769480 | tf_op jit(solution)/shard_map/ppermute | solution.py:645
  186.5 17.1 %collective-permute-start.37 = (bf16[576,512]{1,0:T(8,128)(2,1)S(1)}, bf16[576,512]{1,0:T(8,128)(2,1)S(1)}, u32[]{:S(2)}, u32[]{:S(2)}) collective-permute-start(bf16[576,512]{1,0:T(8,128)(2,1)S(1)} %broadcast_select_fusion.refs_0_), channel_id=1, source_target_pairs={{0,1},{5,4},{10,11},{15,14},{16,17},{21,20},{26,27},{31,30}} | collective-permute-start | bytes 1769480 | tf_op jit(solution)/shard_map/ppermute | solution.py:675
  187.8 19.8 %collective-permute-start.39 = (bf16[576,512]{1,0:T(8,128)(2,1)}, bf16[576,512]{1,0:T(8,128)(2,1)}, u32[]{:S(2)}, u32[]{:S(2)}) collective-permute-start(bf16[576,512]{1,0:T(8,128)(2,1)} %collective-permute-done.38.refs_2_), channel_id=1, source_target_pairs={{2,3},{7,6},{8,9},{13,12},{18,19},{23,22},{24,25},{29,28}} | collective-permute-start | bytes 1769480 | tf_op jit(solution)/shard_map/ppermute | solution.py:685
  197.2 22.1 %collective-permute-start.32 = (bf16[576,512]{1,0:T(8,128)(2,1)S(1)}, bf16[576,512]{1,0:T(8,128)(2,1)}, u32[]{:S(2)}, u32[]{:S(2)}) collective-permute-start(bf16[576,512]{1,0:T(8,128)(2,1)S(1)} %collective-permute-done.30.refs_0_), channel_id=1, source_target_pairs={{0,2},{5,7},{10,8},{15,13},{16,18},{21,23},{26,24},{31,29}} | collective-permute-start | bytes 1769480 | tf_op jit(solution)/shard_map/ppermute | solution.py:670
  199.3 20.0 %collective-permute-start.33 = (bf16[576,512]{1,0:T(8,128)(2,1)S(1)}, bf16[576,512]{1,0:T(8,128)(2,1)}, u32[]{:S(2)}, u32[]{:S(2)}) collective-permute-start(bf16[576,512]{1,0:T(8,128)(2,1)S(1)} %collective-permute-done.30.refs_0_), channel_id=1, source_target_pairs={{0,3},{5,6},{10,9},{15,12},{16,19},{21,22},{26,25},{31,28}} | collective-permute-start | bytes 1769480 | tf_op jit(solution)/shard_map/ppermute | solution.py:680
  201.4 18.6 %collective-permute-start.31 = (bf16[576,512]{1,0:T(8,128)(2,1)S(1)}, bf16[576,512]{1,0:T(8,128)(2,1)}, u32[]{:S(2)}, u32[]{:S(2)}) collective-permute-start(bf16[576,512]{1,0:T(8,128)(2,1)S(1)} %collective-permute-done.30.refs_0_), channel_id=1, source_target_pairs={{0,1},{5,4},{10,11},{15,14},{16,17},{21,20},{26,27},{31,30}} | collective-permute-start | bytes 1769480 | tf_op jit(solution)/shard_map/ppermute | solution.py:675
  204.4 14.9 %collective-permute-start.34 = (bf16[576,512]{1,0:T(8,128)(2,1)}, bf16[576,512]{1,0:T(8,128)(2,1)}, u32[]{:S(2)}, u32[]{:S(2)}) collective-permute-start(bf16[576,512]{1,0:T(8,128)(2,1)} %collective-permute-done.26.refs_7_), channel_id=1, source_target_pairs={{0,16},{8,24},{12,28},{16,0},{28,12},{1,17},{9,25},{13,29},{17,1},... | collective-permute-start | bytes 1769480 | tf_op jit(solution)/shard_map/ppermute | solution.py:654
  (37 other events, 541.9 us)
